TPU v7x, 32 devices: a whole 2x2x4 slice. The times are simulated.
32 devices in a mesh: seq: 16 (over z, x, core), rep: 2 (over y).
Axes of the slice: x: 2, y: 2, z: 4, core: 2. Of those that a mesh axis runs over, the one named last changes fastest.
Arguments:
- acts: bfloat16 [8192, 6144], P(('seq', 'rep')), may hold values from -6 to 6
- grad_logits: bfloat16 [8192, 128], P(('seq', 'rep')), may hold values from -0.017944336 to 0.017944336
- master: float32 [6144, 128], P('seq'), may hold values from -0.078125 to 0.078125
- moment_one: float32 [6144, 128], P('seq'), may hold values from -3 to 3
- moment_two: float32 [6144, 128], P('seq'), may hold values from 0.05 to 2
- step_count: int32 [1], replicated, may hold values from 1 to 40
Outputs:
- master_new: float32 [6144, 128], P('seq')
- moment_one_new: float32 [6144, 128], P('seq')
- moment_two_new: float32 [6144, 128], P('seq')
- logits_new: bfloat16 [8192, 128], P(('seq', 'rep'))
All inputs are finite; a program needn't handle non-finite values.
Results may differ from a plain program's by a relative error of at most 0.0024.
The roundings to bfloat16 on the way count: a program that leaves them out, or rounds other values in their place, can miss the bound.
Values may be sent and summed in bfloat16 or wider, within the bound.
No kernel may reach another device: no remote copies, remote signals or barrier semaphores. Data moves between devices by JAX's collectives and lax.ppermute only.
A program may use at most 64 MiB of HBM per device.

v0:
```python
import jax
import jax.numpy as jnp
from jax import lax
from jax.sharding import PartitionSpec as P


def per_device(acts, grad_logits, master, moment_one, moment_two, step_count):
    columns = acts
    product = lax.dot_general(
        columns, grad_logits, (((0,), (0,)), ((), ())), preferred_element_type=jnp.float32
    )
    rounded = lax.optimization_barrier(product.astype(jnp.bfloat16))
    row_grad = lax.psum_scatter(rounded.astype(jnp.float32), "seq", scatter_dimension=0, tiled=True)
    grad = lax.psum(row_grad, "rep")
    count = step_count[0].astype(jnp.float32)
    beta_one = 0.9
    beta_two = 0.95
    first = beta_one * moment_one + (1.0 - beta_one) * grad
    second = beta_two * moment_two + (1.0 - beta_two) * grad * grad
    first_hat = first / (1.0 - jnp.power(beta_one, count))
    second_hat = second / (1.0 - jnp.power(beta_two, count))
    updated = master - 0.01 * (first_hat / (jnp.sqrt(second_hat) + 1e-08) + 0.1 * master)
    weight_new = updated.astype(jnp.bfloat16)
    columns = acts
    logits = jnp.dot(
        columns,
        lax.all_gather(weight_new, "seq", axis=0, tiled=True),
        preferred_element_type=jnp.float32,
    )
    return (updated, first, second, logits.astype(jnp.bfloat16))


def solution(mesh):
    in_specs = (
        P(("seq", "rep"), None),
        P(("seq", "rep"), None),
        P("seq", None),
        P("seq", None),
        P("seq", None),
        P(),
    )
    out_specs = (P("seq", None), P("seq", None), P("seq", None), P(("seq", "rep"), None))
    return jax.shard_map(
        per_device, mesh=mesh, in_specs=in_specs, out_specs=out_specs, check_vma=False
    )
```

profile of v0, /device:TPU:0, one launch (start us, length us, event | category | flops | bytes accessed | tf_op | source)
XLA Modules:
  0.0 157.3 jit_solution(12849079662112145761)
XLA Ops:
  7.2 0.0 copy-start
  7.2 0.0 reduce-scatter.2.cloned.1.call-start
  7.2 1.8 %copy-done = bf16[256,6144]{1,0:T(8,128)(2,1)S(1)} copy-done((bf16[256,6144]{1,0:T(8,128)(2,1)S(1)}, bf16[256,6144]{1,0:T(8,128)(2,1)}, u32[]{:S(2)}) %copy-start) | copy-done | bytes 3145752
  9.1 1.9 %convolution_convert_fusion = bf16[6144,128]{1,0:T(8,128)(2,1)S(1)} fusion(bf16[256,6144]{1,0:T(8,128)(2,1)S(1)} %copy-done, bf16[256,128]{1,0:T(8,128)(2,1)} %param.7), kind=kOutput, calls=%fused_computation | convolution fusion | flops 403439616 | bytes 4784128 | tf_op jit(solution)/shard_map/dot_general | solution.py:9
  10.9 0.0 copy-start.1
  11.0 0.0 copy-start.2
  11.0 1.8 %convert_element_type.20 = f32[6144,128]{1,0:T(8,128)} convert(bf16[6144,128]{1,0:T(8,128)(2,1)S(1)} %convolution_convert_fusion) | non-fusion elementwise | flops 786432 | bytes 4718592 | tf_op jit(solution)/shard_map/convert_element_type | solution.py:13
  12.8 0.0 reduce-scatter.2.cloned.1.call-update
  12.8 0.0 all-reduce.2.cloned.1.call-start
  12.9 69.1 %reduce-scatter.2.cloned.1.call-done = f32[384,128]{1,0:T(8,128)} async-done(((f32[6144,128]{1,0:T(8,128)}), f32[384,128]{1,0:T(8,128)}) %reduce-scatter.2.cloned.1.call-update) | async-done | bytes 196624 | tf_op jit(solution)/shard_map/reduce_scatter | solution.py:13
  82.0 0.0 all-reduce.2.cloned.1.call-update
  82.0 0.0 all-gather.2.cloned.1.call-start
  82.8 22.7 %all-reduce.2.cloned.1.call-done = f32[384,128]{1,0:T(8,128)} async-done(((f32[384,128]{1,0:T(8,128)}), f32[384,128]{1,0:T(8,128)}) %all-reduce.2.cloned.1.call-update) | async-done | bytes 196624 | tf_op jit(solution)/shard_map/psum | solution.py:14
  105.4 0.0 copy-done.1
  105.4 0.0 copy-done.2
  105.4 1.9 %fusion.2 = (bf16[384,128]{1,0:T(8,128)(2,1)}, f32[384,128]{1,0:T(8,128)}, f32[384,128]{1,0:T(8,128)}, f32[384,128]{1,0:T(8,128)}) fusion(f32[384,128]{1,0:T(8,128)S(1)} %copy-done.1, f32[]{:T(128)} %bitcast.1, f32[]{:T(128)} %bitcast, f32[384,128]{1,0:T(8,128)} %all-reduce.2.cloned.1.call-done, f32[384,128]{1,0:T(8,128)S(1)} %copy-done.2, f32[384,128]{1,0:T(8,128)} %param.9), kind=kLoop, calls=%fused_computation.7 | loop fusion | flops 786432 | bytes 1474568 | tf_op jit(solution)/shard_map/convert_element_type | solution.py:23
  107.4 0.0 all-gather.2.cloned.1.call-update
  107.4 40.0 %all-gather.2.cloned.1.call-done = bf16[6144,128]{1,0:T(8,128)(2,1)} async-done(((bf16[384,128]{1,0:T(8,128)(2,1)}), bf16[6144,128]{1,0:T(8,128)(2,1)}) %all-gather.2.cloned.1.call-update) | async-done | bytes 1572880 | tf_op jit(solution)/shard_map/all_gather | solution.py:27
  147.4 2.6 %fusion = bf16[256,128]{0,1:T(8,128)(2,1)S(1)} fusion(bf16[6144,128]{1,0:T(8,128)(2,1)} %all-gather.2.cloned.1.call-done, bf16[256,6144]{1,0:T(8,128)(2,1)S(1)} %copy-done), kind=kOutput, calls=%fused_computation.2 | convolution fusion | flops 402685952 | bytes 4784128 | tf_op jit(solution)/shard_map/dot_general | solution.py:25
  150.0 0.7 copy.10
Async XLA Ops:
  7.2 1.9 %copy-start = (bf16[256,6144]{1,0:T(8,128)(2,1)S(1)}, bf16[256,6144]{1,0:T(8,128)(2,1)}, u32[]{:S(2)}) copy-start(bf16[256,6144]{1,0:T(8,128)(2,1)} %param.6) | copy-start | bytes 9437188
  7.2 74.8 %reduce-scatter.2.cloned.1.call-start = ((), (), s32[]{:S(2)}) async-start(), calls=%async_computation.1 | async-start | bytes 3342336 | tf_op jit(solution)/shard_map/reduce_scatter | solution.py:13
  10.9 94.5 %copy-start.1 = (f32[384,128]{1,0:T(8,128)S(1)}, f32[384,128]{1,0:T(8,128)}, u32[]{:S(2)}) copy-start(f32[384,128]{1,0:T(8,128)} %param.8) | copy-start | bytes 589828
  11.0 94.5 %copy-start.2 = (f32[384,128]{1,0:T(8,128)S(1)}, f32[384,128]{1,0:T(8,128)}, u32[]{:S(2)}) copy-start(f32[384,128]{1,0:T(8,128)} %param.10) | copy-start | bytes 589828
  12.8 92.6 %all-reduce.2.cloned.1.call-start = ((), (), s32[]{:S(2)}) async-start(), calls=%async_computation.2 | async-start | bytes 393216 | tf_op jit(solution)/shard_map/psum | solution.py:14
  82.0 65.4 %all-gather.2.cloned.1.call-start = ((), (), s32[]{:S(2)}) async-start(), calls=%async_computation.3 | async-start | bytes 1671168 | tf_op jit(solution)/shard_map/all_gather | solution.py:27
Sparse Core Ops, SparseCore 0:
  13.0 68.9 reduce-scatter.1
  84.2 21.1 all-reduce.1
  107.7 39.6 all-gather.1
where the time goes:
time: 158 us; the launch traced here: 157 us
  waiting for transfers between devices  132 us (84%)
  between operations  14.5 us (9%)
  matrix products  4.47 us (3%)
  other arithmetic  3.78 us (2%)
  local copies, waits for them, and re-layouts  2.59 us (2%)
    reduce_scatter x1, waiting for transfers between devices, per_device(): lax.psum_scatter(rounded.astype(jnp.float32), 'seq', scatter_dimension=0,...  69.1 us
    all_gather x1, waiting for transfers between devices, per_device(): lax.all_gather(weight_new, 'seq', axis=0, tiled=True)  40 us
    psum x1, waiting for transfers between devices, per_device(): grad = lax.psum(row_grad, 'rep')  22.7 us
  transfers between devices with their start and end apart: 3, of which 3 were waited for; matrix products, arithmetic and copies ran while one was open for 0% of the time, Pallas kernels for 0%

commit v1 on v0

v1 whole, which is shorter than its diff:
```python
import jax
import jax.numpy as jnp
from jax import lax
from jax.experimental import pallas as pl
from jax.experimental.pallas import tpu as pltpu
from jax.sharding import PartitionSpec as P

AXES = ("seq", "rep")


def adamw(grad, master, moment_one, moment_two, step_count):
    count = step_count[0].astype(jnp.float32)
    beta_one = 0.9
    beta_two = 0.95
    first = beta_one * moment_one + (1.0 - beta_one) * grad
    second = beta_two * moment_two + (1.0 - beta_two) * grad * grad
    first_hat = first / (1.0 - jnp.power(beta_one, count))
    second_hat = second / (1.0 - jnp.power(beta_two, count))
    updated = master - 0.01 * (first_hat / (jnp.sqrt(second_hat) + 1e-08) + 0.1 * master)
    return updated, first, second


def logits_kernel(places, half, acts_ref, *refs):
    me_ref, pieces, out_ref, weight = refs[0], refs[1:-2], refs[-2], refs[-1]
    me = me_ref[0]
    for piece, masks in zip(pieces, places):
        for j, mask in enumerate(masks):
            row = pl.multiple_of(jnp.bitwise_xor(me, mask) * half, half)
            weight[pl.ds(row, half), :] = piece[j]
    out_ref[...] = jnp.dot(
        acts_ref[...], weight[...], preferred_element_type=jnp.float32
    ).astype(out_ref.dtype)


def solution(mesh):
    n_seq, n_rep = mesh.shape["seq"], mesh.shape["rep"]
    devices = n_seq * n_rep
    core = n_rep
    low = [a * 2 * n_rep + b for a in range(4) for b in range(n_rep)]
    high = [8 * n_rep * j for j in range(n_seq // 8)]

    def swap(x, mask):
        return lax.ppermute(x, AXES, [(i, i ^ mask) for i in range(devices)])

    def per_device(acts, grad_logits, master, moment_one, moment_two, step_count):
        rows, experts = master.shape
        half = rows // n_rep
        seq, rep = lax.axis_index("seq"), lax.axis_index("rep")
        me = seq * n_rep + rep
        my_core, my_low = seq % 2, (seq // 2) % 4
        my_high = seq // 8

        product = lax.dot_general(
            acts, grad_logits, (((0,), (0,)), ((), ())), preferred_element_type=jnp.float32
        ).astype(jnp.bfloat16)
        by_core = product.reshape(n_seq // 2, 2, rows, experts)
        away = lax.dynamic_index_in_dim(by_core, 1 - my_core, 1, keepdims=False)
        kept = lax.dynamic_index_in_dim(by_core, my_core, 1, keepdims=False)
        arrived = swap(away, core)
        chip = (kept.astype(jnp.float32) + arrived.astype(jnp.float32)).astype(jnp.bfloat16)
        chip = chip.reshape(len(high), 4, n_rep, half, experts)

        total = None
        for mask in low:
            other_low = jnp.bitwise_xor(my_low, mask // (2 * n_rep))
            other_rep = jnp.bitwise_xor(rep, mask % n_rep)
            part = lax.dynamic_slice(
                chip, (0, other_low, other_rep, 0, 0), (len(high), 1, 1, half, experts)
            ).reshape(len(high), half, experts)
            if mask:
                part = swap(part, mask)
            part = part.astype(jnp.float32)
            total = part if total is None else total + part

        grad = None
        for j, mask in enumerate(high):
            part = lax.dynamic_index_in_dim(total, jnp.bitwise_xor(my_high, j), 0, keepdims=False)
            if mask:
                part = swap(part, mask)
            grad = part if grad is None else grad + part

        mine = [
            lax.dynamic_slice_in_dim(a, rep * half, half, 0)
            for a in (master, moment_one, moment_two)
        ]
        weight = adamw(grad, *mine, step_count)[0].astype(jnp.bfloat16)

        other = swap(grad, 1)
        whole = jnp.where(
            rep == 0,
            jnp.concatenate([grad, other], 0),
            jnp.concatenate([other, grad], 0),
        )
        updated, first, second = adamw(whole, master, moment_one, moment_two, step_count)

        column = jnp.stack([swap(weight, mask) if mask else weight for mask in high])
        cube = [swap(column, mask) if mask else column for mask in low]
        pair = [swap(piece, core) for piece in cube]
        pieces = cube + pair
        places = [[m ^ h for h in high] for m in low] + [[m ^ core ^ h for h in high] for m in low]
        if half % 16 == 0:
            vmem = pl.BlockSpec(memory_space=pltpu.VMEM)
            logits = pl.pallas_call(
                lambda *refs: logits_kernel(places, half, *refs),
                out_shape=jax.ShapeDtypeStruct((acts.shape[0], experts), jnp.bfloat16),
                in_specs=[vmem, pl.BlockSpec(memory_space=pltpu.SMEM)] + [vmem] * len(pieces),
                out_specs=vmem,
                scratch_shapes=[pltpu.VMEM((n_seq * rows, experts), jnp.bfloat16)],
                compiler_params=pltpu.CompilerParams(vmem_limit_bytes=32 * 2**20),
            )(acts, me.reshape(1), *pieces)
        else:
            order = jnp.argsort(jnp.bitwise_xor(me, jnp.array(places).reshape(-1)))
            full = jnp.concatenate(pieces)[order].reshape(n_seq * rows, experts)
            logits = jnp.dot(acts, full, preferred_element_type=jnp.float32).astype(jnp.bfloat16)
        return updated, first, second, logits

    rows_of, tokens = P("seq", None), P(AXES, None)
    return jax.shard_map(
        per_device,
        mesh=mesh,
        in_specs=(tokens, tokens, rows_of, rows_of, rows_of, P()),
        out_specs=(rows_of, rows_of, rows_of, tokens),
        check_vma=False,
    )
```

time: 158 us -> 64.5 us (0.41)
  waiting for transfers between devices: 132 us -> 17.4 us
  starting transfers between devices: 0.12 us -> 27.5 us
  between operations: 14.5 us -> 1.56 us
  local copies, waits for them, and re-layouts: 2.59 us -> 7.1 us
  Pallas kernels: 0 us -> 2.79 us
    reduce_scatter x1 -> x0, waiting for transfers between devices: 69.1 us -> none  [per_device(): lax.psum_scatter(rounded.astype(jnp.float32), 'seq', scatter_dimension=0,...]
    all_gather x1 -> x0, waiting for transfers between devices: 40 us -> none  [per_device(): lax.all_gather(weight_new, 'seq', axis=0, tiled=True)]
    ppermute x0 -> x26, starting transfers between devices: none -> 27.5 us  [swap(): return lax.ppermute(x, AXES, [(i, i ^ mask) for i in range(devices)])]
    psum x1 -> x0, waiting for transfers between devices: 22.7 us -> none  [per_device(): grad = lax.psum(row_grad, 'rep')]
    ppermute x0 -> x26, waiting for transfers between devices: none -> 17.4 us  [swap(): return lax.ppermute(x, AXES, [(i, i ^ mask) for i in range(devices)])]
    unnamed x7 -> x24, local copies, waits for them, and re-layouts: 2.59 us -> 5.67 us
    pallas_call x0 -> x1, Pallas kernels: none -> 2.79 us  [per_device(): pl.pallas_call(lambda *refs: logits_kernel(places, half, *refs), out_shap...]
    convert_element_type x2, other arithmetic: 3.78 us -> 1.29 us  [the longest x1 1.08 us: per_device(): weight = adamw(grad, *mine, step_count)[0].astype(jnp.bfloat16)]
  transfers between devices with their start and end apart: 3 -> 26, of which waited for: 3 -> 11; matrix products, arithmetic and copies ran while one was open for 0% -> 3% of each run, Pallas kernels for 0% -> 0%
where the time goes in v1:
time: 64.5 us; the launch traced here: 64.1 us
  starting transfers between devices  27.5 us (43%)
  waiting for transfers between devices  17.4 us (27%)
  local copies, waits for them, and re-layouts  7.1 us (11%)
  other arithmetic  4.77 us (7%)
  matrix products  2.93 us (5%)
  Pallas kernels  2.79 us (4%)
  between operations  1.56 us (2%)
    ppermute x26, starting transfers between devices, swap(): return lax.ppermute(x, AXES, [(i, i ^ mask) for i in range(devices)])  27.5 us
    ppermute x26, waiting for transfers between devices, swap(): return lax.ppermute(x, AXES, [(i, i ^ mask) for i in range(devices)])  17.4 us
    unnamed x24, local copies, waits for them, and re-layouts  5.67 us
    dot_general x1, matrix products, per_device(): lax.dot_general(acts, grad_logits, (((0,), (0,)), ((), ())), preferred_el...  2.93 us
    pallas_call x1, Pallas kernels, per_device(): pl.pallas_call(lambda *refs: logits_kernel(places, half, *refs), out_shap...  2.79 us
    sub x1, other arithmetic, adamw(): master - 0.01 * (first_hat / (jnp.sqrt(second_hat) + 1e-08) + 0.1 * master)  2.19 us
  transfers between devices with their start and end apart: 26, of which 11 were waited for; matrix products, arithmetic and copies ran while one was open for 3% of the time, Pallas kernels for 0%

profile of v1, /device:TPU:0, one launch (start us, length us, event | category | flops | bytes accessed | tf_op | source)
XLA Modules:
  0.0 64.1 jit_solution(14169863868880703285)
XLA Ops:
  1.5 2.9 %convolution_convert_fusion = bf16[6144,128]{1,0:T(8,128)(2,1)S(1)} fusion(bf16[256,6144]{1,0:T(8,128)(2,1)} %refs_0_.1, bf16[256,128]{1,0:T(8,128)(2,1)S(1)} %copy-done), kind=kOutput, calls=%fused_computation | convolution fusion | flops 403439616 | bytes 4784128 | tf_op jit(solution)/shard_map/dot_general | solution.py:53
  5.0 1.9 %collective-permute-done = bf16[8,384,128]{2,1,0:T(8,128)(2,1)S(1)} collective-permute-done((bf16[8,384,128]{2,1,0:T(8,128)(2,1)S(1)}, bf16[8,384,128]{2,1,0:T(8,128)(2,1)S(1)}, u32[]{:S(2)}, u32[]{:S(2)}) %collective-permute-start) | collective-permute-done | bytes 786464 | tf_op jit(solution)/shard_map/ppermute | solution.py:43
  8.7 4.8 %collective-permute-start.7 = (bf16[2,192,128]{2,1,0:T(8,128)(2,1)S(1)}, bf16[2,192,128]{2,1,0:T(8,128)(2,1)S(1)}, u32[]{:S(2)}, u32[]{:S(2)}) collective-permute-start(bf16[2,192,128]{2,1,0:T(8,128)(2,1)S(1)} %get-tuple-element.10), channel_id=1, source_target_pairs={{0,13},{1,12},{2,15},{3,14},{4,9},{5,8},{6,11},{7,10},{8,5},{9,4},... | collective-permute-start | bytes 294920 | tf_op jit(solution)/shard_map/ppermute | solution.py:43
  14.0 1.5 %collective-permute-start.5 = (bf16[2,192,128]{2,1,0:T(8,128)(2,1)}, bf16[2,192,128]{2,1,0:T(8,128)(2,1)}, u32[]{:S(2)}, u32[]{:S(2)}) collective-permute-start(bf16[2,192,128]{2,1,0:T(8,128)(2,1)} %get-tuple-element.12), channel_id=1, source_target_pairs={{0,9},{1,8},{2,11},{3,10},{4,13},{5,12},{6,15},{7,14},{8,1},{9,0},... | collective-permute-start | bytes 294920 | tf_op jit(solution)/shard_map/ppermute | solution.py:43
  15.6 2.8 %collective-permute-start.3 = (bf16[2,192,128]{2,1,0:T(8,128)(2,1)}, bf16[2,192,128]{2,1,0:T(8,128)(2,1)}, u32[]{:S(2)}, u32[]{:S(2)}) collective-permute-start(bf16[2,192,128]{2,1,0:T(8,128)(2,1)} %get-tuple-element.14), channel_id=1, source_target_pairs={{0,5},{1,4},{2,7},{3,6},{4,1},{5,0},{6,3},{7,2},{8,13},{9,12},{10,... | collective-permute-start | bytes 294920 | tf_op jit(solution)/shard_map/ppermute | solution.py:43
  19.0 1.1 %collective-permute-done.6 = bf16[2,192,128]{2,1,0:T(8,128)(2,1)S(1)} collective-permute-done((bf16[2,192,128]{2,1,0:T(8,128)(2,1)S(1)}, bf16[2,192,128]{2,1,0:T(8,128)(2,1)S(1)}, u32[]{:S(2)}, u32[]{:S(2)}) %collective-permute-start.6) | collective-permute-done | bytes 98336 | tf_op jit(solution)/shard_map/ppermute | solution.py:43
  21.2 1.2 %collective-permute-done.5 = bf16[2,192,128]{2,1,0:T(8,128)(2,1)} collective-permute-done((bf16[2,192,128]{2,1,0:T(8,128)(2,1)}, bf16[2,192,128]{2,1,0:T(8,128)(2,1)}, u32[]{:S(2)}, u32[]{:S(2)}) %collective-permute-start.5) | collective-permute-done | bytes 98336 | tf_op jit(solution)/shard_map/ppermute | solution.py:43
  23.8 1.8 %collective-permute-done.1 = bf16[2,192,128]{2,1,0:T(8,128)(2,1)} collective-permute-done((bf16[2,192,128]{2,1,0:T(8,128)(2,1)S(1)}, bf16[2,192,128]{2,1,0:T(8,128)(2,1)}, u32[]{:S(2)}, u32[]{:S(2)}) %collective-permute-start.1) | collective-permute-done | bytes 98336 | tf_op jit(solution)/shard_map/ppermute | solution.py:43
  25.5 1.3 %fusion.7 = f32[2,192,128]{2,1,0:T(8,128)S(1)} fusion(bf16[2,192,128]{2,1,0:T(8,128)(2,1)S(1)} %collective-permute-done.7, bf16[2,192,128]{2,1,0:T(8,128)(2,1)} %copy-done.11, bf16[2,192,128]{2,1,0:T(8,128)(2,1)} %collective-permute-done.5, bf16[2,192,128]{2,1,0:T(8,128)(2,1)} %collective-permute-done.4, bf16[2,192,128]{2,1,0:T(8,128)(2,1)} %collective-permute-done.3, ...), kind=kLoop, calls=%fused_computation.13 | loop fusion | flops 737280 | bytes 983048 | tf_op jit(solution)/shard_map/add | solution.py:73
  27.5 2.6 %collective-permute-start.8 = (f32[192,128]{1,0:T(8,128)}, f32[192,128]{1,0:T(8,128)S(1)}, u32[]{:S(2)}, u32[]{:S(2)}) collective-permute-start(f32[192,128]{1,0:T(8,128)} %dynamic-slice_bitcast_fusion.1), channel_id=1, source_target_pairs={{0,16},{1,17},{2,18},{3,19},{4,20},{5,21},{6,22},{7,23},{8,24},{9,... | collective-permute-start | bytes 294920 | tf_op jit(solution)/shard_map/ppermute | solution.py:43
  30.8 3.4 %collective-permute-done.8 = f32[192,128]{1,0:T(8,128)S(1)} collective-permute-done((f32[192,128]{1,0:T(8,128)}, f32[192,128]{1,0:T(8,128)S(1)}, u32[]{:S(2)}, u32[]{:S(2)}) %collective-permute-start.8) | collective-permute-done | bytes 98336 | tf_op jit(solution)/shard_map/ppermute | solution.py:43
  34.2 1.1 %subtract_convert_fusion = (bf16[192,128]{1,0:T(8,128)(2,1)S(1)}, f32[192,128]{1,0:T(8,128)S(1)}) fusion(f32[384,128]{1,0:T(8,128)} %param.8, s32[]{:T(128)S(6)} %select_n.89, f32[384,128]{1,0:T(8,128)} %param.10, f32[384,128]{1,0:T(8,128)} %param.9, f32[]{:T(128)} %bitcast.15, f32[]{:T(128)} %bitcast.14, f32[192,128]{1,0:T(8,128)S(1)} %collective-permute-done.8, ...), kind=kLoop, calls=%fused_computation.25 | loop fusion | flops 417792 | bytes 638992 | tf_op jit(solution)/shard_map/convert_element_type | solution.py:86
  35.3 1.7 %collective-permute-start.10 = (bf16[192,128]{1,0:T(8,128)(2,1)S(1)}, bf16[192,128]{1,0:T(8,128)(2,1)S(1)}, u32[]{:S(2)}, u32[]{:S(2)}) collective-permute-start(bf16[192,128]{1,0:T(8,128)(2,1)S(1)} %get-tuple-element.4), channel_id=1, source_target_pairs={{0,16},{1,17},{2,18},{3,19},{4,20},{5,21},{6,22},{7,23},{8,24},{9,... | collective-permute-start | bytes 147464 | tf_op jit(solution)/shard_map/ppermute | solution.py:43
  37.8 3.1 %collective-permute-done.10 = bf16[192,128]{1,0:T(8,128)(2,1)S(1)} collective-permute-done((bf16[192,128]{1,0:T(8,128)(2,1)S(1)}, bf16[192,128]{1,0:T(8,128)(2,1)S(1)}, u32[]{:S(2)}, u32[]{:S(2)}) %collective-permute-start.10) | collective-permute-done | bytes 49184 | tf_op jit(solution)/shard_map/ppermute | solution.py:43
  42.6 1.9 %collective-permute-start.13 = (bf16[2,192,128]{2,1,0:T(8,128)(2,1)S(1)}, bf16[2,192,128]{2,1,0:T(8,128)(2,1)S(1)}, u32[]{:S(2)}, u32[]{:S(2)}) collective-permute-start(bf16[2,192,128]{2,1,0:T(8,128)(2,1)S(1)} %pad_maximum_fusion.refs_2_), channel_id=1, source_target_pairs={{0,5},{1,4},{2,7},{3,6},{4,1},{5,0},{6,3},{7,2},{8,13},{9,12},{10,... | collective-permute-start | bytes 294920 | tf_op jit(solution)/shard_map/ppermute | solution.py:43
  44.9 1.8 %collective-permute-start.15 = (bf16[2,192,128]{2,1,0:T(8,128)(2,1)S(1)}, bf16[2,192,128]{2,1,0:T(8,128)(2,1)S(1)}, u32[]{:S(2)}, u32[]{:S(2)}) collective-permute-start(bf16[2,192,128]{2,1,0:T(8,128)(2,1)S(1)} %pad_maximum_fusion.refs_2_), channel_id=1, source_target_pairs={{0,9},{1,8},{2,11},{3,10},{4,13},{5,12},{6,15},{7,14},{8,1},{9,0},... | collective-permute-start | bytes 294920 | tf_op jit(solution)/shard_map/ppermute | solution.py:43
  46.7 2.1 %collective-permute-start.16 = (bf16[2,192,128]{2,1,0:T(8,128)(2,1)S(1)}, bf16[2,192,128]{2,1,0:T(8,128)(2,1)}, u32[]{:S(2)}, u32[]{:S(2)}) collective-permute-start(bf16[2,192,128]{2,1,0:T(8,128)(2,1)S(1)} %pad_maximum_fusion.refs_2_), channel_id=1, source_target_pairs={{0,12},{1,13},{2,14},{3,15},{4,8},{5,9},{6,10},{7,11},{8,4},{9,5},... | collective-permute-start | bytes 294920 | tf_op jit(solution)/shard_map/ppermute | solution.py:43
  48.8 1.5 %collective-permute-start.17 = (bf16[2,192,128]{2,1,0:T(8,128)(2,1)S(1)}, bf16[2,192,128]{2,1,0:T(8,128)(2,1)}, u32[]{:S(2)}, u32[]{:S(2)}) collective-permute-start(bf16[2,192,128]{2,1,0:T(8,128)(2,1)S(1)} %pad_maximum_fusion.refs_2_), channel_id=1, source_target_pairs={{0,13},{1,12},{2,15},{3,14},{4,9},{5,8},{6,11},{7,10},{8,5},{9,4},... | collective-permute-start | bytes 294920 | tf_op jit(solution)/shard_map/ppermute | solution.py:43
  52.6 2.7 %collective-permute-done.17.refs_9_ = bf16[2,192,128]{2,1,0:T(8,128)(2,1)} collective-permute-done((bf16[2,192,128]{2,1,0:T(8,128)(2,1)S(1)}, bf16[2,192,128]{2,1,0:T(8,128)(2,1)}, u32[]{:S(2)}, u32[]{:S(2)}) %collective-permute-start.17) | collective-permute-done | bytes 98336 | tf_op jit(solution)/shard_map/ppermute | solution.py:43
  56.4 2.2 %multiply_subtract_fusion = (f32[384,128]{1,0:T(8,128)}, f32[384,128]{1,0:T(8,128)}, f32[384,128]{1,0:T(8,128)}) fusion(f32[384,128]{1,0:T(8,128)} %param.8, f32[]{:T(128)} %bitcast.15, f32[]{:T(128)} %bitcast.14, f32[192,128]{1,0:T(8,128)} %copy-done.9, f32[192,128]{1,0:T(8,128)} %copy-done.10, pred[]{:T(512)S(6)} %eq.6, f32[384,128]{1,0:T(8,128)} %param.10, ...), kind=kLoop, calls=%fused_computation.14 | loop fusion | flops 884736 | bytes 1376265 | tf_op jit(solution)/shard_map/sub | solution.py:19
  58.6 0.9 %copy-done.3 = bf16[2,192,128]{2,1,0:T(8,128)(2,1)S(1)} copy-done((bf16[2,192,128]{2,1,0:T(8,128)(2,1)S(1)}, bf16[2,192,128]{2,1,0:T(8,128)(2,1)}, u32[]{:S(2)}) %copy-start.3) | copy-done | bytes 98328
  59.5 0.9 %copy-done.5 = bf16[2,192,128]{2,1,0:T(8,128)(2,1)S(1)} copy-done((bf16[2,192,128]{2,1,0:T(8,128)(2,1)S(1)}, bf16[2,192,128]{2,1,0:T(8,128)(2,1)}, u32[]{:S(2)}) %copy-start.5) | copy-done | bytes 98328
  60.4 0.9 %copy-done.7 = bf16[2,192,128]{2,1,0:T(8,128)(2,1)S(1)} copy-done((bf16[2,192,128]{2,1,0:T(8,128)(2,1)S(1)}, bf16[2,192,128]{2,1,0:T(8,128)(2,1)}, u32[]{:S(2)}) %copy-start.7) | copy-done | bytes 98328
  61.3 2.8 %shard_map.93 = bf16[256,128]{1,0:T(8,128)(2,1)} custom-call(bf16[256,6144]{1,0:T(8,128)(2,1)S(1)} %copy-done.1, s32[1]{0:T(128)} %bitcast.16.refs_1_, bf16[2,192,128]{2,1,0:T(8,128)(2,1)S(1)} %pad_maximum_fusion.refs_2_, bf16[2,192,128]{2,1,0:T(8,128)(2,1)S(1)} %collective-permute-done.11.refs_3_, bf16[2,192,128]{2,1,0:T(8,128)(2,1)S(1)} %collective-permute-done.12.refs_4_, ...), custom_call_target="tpu_custom_call" | custom-call | tf_op jit(solution)/shard_map/pallas_call | solution.py:103
  (62 shorter events, 13.6 us)
Async XLA Ops:
  8.7 9.7 %collective-permute-start.7 = (bf16[2,192,128]{2,1,0:T(8,128)(2,1)S(1)}, bf16[2,192,128]{2,1,0:T(8,128)(2,1)S(1)}, u32[]{:S(2)}, u32[]{:S(2)}) collective-permute-start(bf16[2,192,128]{2,1,0:T(8,128)(2,1)S(1)} %get-tuple-element.10), channel_id=1, source_target_pairs={{0,13},{1,12},{2,15},{3,14},{4,9},{5,8},{6,11},{7,10},{8,5},{9,4},... | collective-permute-start | bytes 294920 | tf_op jit(solution)/shard_map/ppermute | solution.py:43
  13.6 6.6 %collective-permute-start.6 = (bf16[2,192,128]{2,1,0:T(8,128)(2,1)S(1)}, bf16[2,192,128]{2,1,0:T(8,128)(2,1)S(1)}, u32[]{:S(2)}, u32[]{:S(2)}) collective-permute-start(bf16[2,192,128]{2,1,0:T(8,128)(2,1)S(1)} %get-tuple-element.11), channel_id=1, source_target_pairs={{0,12},{1,13},{2,14},{3,15},{4,8},{5,9},{6,10},{7,11},{8,4},{9,5},... | collective-permute-start | bytes 294920 | tf_op jit(solution)/shard_map/ppermute | solution.py:43
  14.0 8.4 %collective-permute-start.5 = (bf16[2,192,128]{2,1,0:T(8,128)(2,1)}, bf16[2,192,128]{2,1,0:T(8,128)(2,1)}, u32[]{:S(2)}, u32[]{:S(2)}) collective-permute-start(bf16[2,192,128]{2,1,0:T(8,128)(2,1)} %get-tuple-element.12), channel_id=1, source_target_pairs={{0,9},{1,8},{2,11},{3,10},{4,13},{5,12},{6,15},{7,14},{8,1},{9,0},... | collective-permute-start | bytes 294920 | tf_op jit(solution)/shard_map/ppermute | solution.py:43
  15.5 7.7 %collective-permute-start.4 = (bf16[2,192,128]{2,1,0:T(8,128)(2,1)}, bf16[2,192,128]{2,1,0:T(8,128)(2,1)}, u32[]{:S(2)}, u32[]{:S(2)}) collective-permute-start(bf16[2,192,128]{2,1,0:T(8,128)(2,1)} %get-tuple-element.13), channel_id=1, source_target_pairs={{0,8},{1,9},{2,10},{3,11},{4,12},{5,13},{6,14},{7,15},{8,0},{9,1},... | collective-permute-start | bytes 294920 | tf_op jit(solution)/shard_map/ppermute | solution.py:43
  15.6 7.7 %collective-permute-start.3 = (bf16[2,192,128]{2,1,0:T(8,128)(2,1)}, bf16[2,192,128]{2,1,0:T(8,128)(2,1)}, u32[]{:S(2)}, u32[]{:S(2)}) collective-permute-start(bf16[2,192,128]{2,1,0:T(8,128)(2,1)} %get-tuple-element.14), channel_id=1, source_target_pairs={{0,5},{1,4},{2,7},{3,6},{4,1},{5,0},{6,3},{7,2},{8,13},{9,12},{10,... | collective-permute-start | bytes 294920 | tf_op jit(solution)/shard_map/ppermute | solution.py:43
  18.4 5.4 %collective-permute-start.2 = (bf16[2,192,128]{2,1,0:T(8,128)(2,1)S(1)}, bf16[2,192,128]{2,1,0:T(8,128)(2,1)}, u32[]{:S(2)}, u32[]{:S(2)}) collective-permute-start(bf16[2,192,128]{2,1,0:T(8,128)(2,1)S(1)} %get-tuple-element.15), channel_id=1, source_target_pairs={{0,4},{1,5},{2,6},{3,7},{4,0},{5,1},{6,2},{7,3},{8,12},{9,13},{10,... | collective-permute-start | bytes 294920 | tf_op jit(solution)/shard_map/ppermute | solution.py:43
  20.8 4.7 %collective-permute-start.1 = (bf16[2,192,128]{2,1,0:T(8,128)(2,1)S(1)}, bf16[2,192,128]{2,1,0:T(8,128)(2,1)}, u32[]{:S(2)}, u32[]{:S(2)}) collective-permute-start(bf16[2,192,128]{2,1,0:T(8,128)(2,1)S(1)} %get-tuple-element.9), channel_id=1, source_target_pairs={{0,1},{1,0},{2,3},{3,2},{4,5},{5,4},{6,7},{7,6},{8,9},{9,8},{10,11... | collective-permute-start | bytes 294920 | tf_op jit(solution)/shard_map/ppermute | solution.py:43
  27.5 6.8 %collective-permute-start.8 = (f32[192,128]{1,0:T(8,128)}, f32[192,128]{1,0:T(8,128)S(1)}, u32[]{:S(2)}, u32[]{:S(2)}) collective-permute-start(f32[192,128]{1,0:T(8,128)} %dynamic-slice_bitcast_fusion.1), channel_id=1, source_target_pairs={{0,16},{1,17},{2,18},{3,19},{4,20},{5,21},{6,22},{7,23},{8,24},{9,... | collective-permute-start | bytes 294920 | tf_op jit(solution)/shard_map/ppermute | solution.py:43
  35.3 5.6 %collective-permute-start.10 = (bf16[192,128]{1,0:T(8,128)(2,1)S(1)}, bf16[192,128]{1,0:T(8,128)(2,1)S(1)}, u32[]{:S(2)}, u32[]{:S(2)}) collective-permute-start(bf16[192,128]{1,0:T(8,128)(2,1)S(1)} %get-tuple-element.4), channel_id=1, source_target_pairs={{0,16},{1,17},{2,18},{3,19},{4,20},{5,21},{6,22},{7,23},{8,24},{9,... | collective-permute-start | bytes 147464 | tf_op jit(solution)/shard_map/ppermute | solution.py:43
  37.0 7.8 %collective-permute-start.9 = (f32[192,128]{1,0:T(8,128)S(1)}, f32[192,128]{1,0:T(8,128)S(1)}, u32[]{:S(2)}, u32[]{:S(2)}) collective-permute-start(f32[192,128]{1,0:T(8,128)S(1)} %get-tuple-element.5), channel_id=1, source_target_pairs={{0,1},{1,0},{2,3},{3,2},{4,5},{5,4},{6,7},{7,6},{8,9},{9,8},{10,11... | collective-permute-start | bytes 294920 | tf_op jit(solution)/shard_map/ppermute | solution.py:43
  40.9 5.8 %collective-permute-start.11 = (bf16[2,192,128]{2,1,0:T(8,128)(2,1)S(1)}, bf16[2,192,128]{2,1,0:T(8,128)(2,1)S(1)}, u32[]{:S(2)}, u32[]{:S(2)}) collective-permute-start(bf16[2,192,128]{2,1,0:T(8,128)(2,1)S(1)} %pad_maximum_fusion.refs_2_), channel_id=1, source_target_pairs={{0,1},{1,0},{2,3},{3,2},{4,5},{5,4},{6,7},{7,6},{8,9},{9,8},{10,11... | collective-permute-start | bytes 294920 | tf_op jit(solution)/shard_map/ppermute | solution.py:43
  41.8 7.1 %collective-permute-start.12 = (bf16[2,192,128]{2,1,0:T(8,128)(2,1)S(1)}, bf16[2,192,128]{2,1,0:T(8,128)(2,1)S(1)}, u32[]{:S(2)}, u32[]{:S(2)}) collective-permute-start(bf16[2,192,128]{2,1,0:T(8,128)(2,1)S(1)} %pad_maximum_fusion.refs_2_), channel_id=1, source_target_pairs={{0,4},{1,5},{2,6},{3,7},{4,0},{5,1},{6,2},{7,3},{8,12},{9,13},{10,... | collective-permute-start | bytes 294920 | tf_op jit(solution)/shard_map/ppermute | solution.py:43
  42.6 7.7 %collective-permute-start.13 = (bf16[2,192,128]{2,1,0:T(8,128)(2,1)S(1)}, bf16[2,192,128]{2,1,0:T(8,128)(2,1)S(1)}, u32[]{:S(2)}, u32[]{:S(2)}) collective-permute-start(bf16[2,192,128]{2,1,0:T(8,128)(2,1)S(1)} %pad_maximum_fusion.refs_2_), channel_id=1, source_target_pairs={{0,5},{1,4},{2,7},{3,6},{4,1},{5,0},{6,3},{7,2},{8,13},{9,12},{10,... | collective-permute-start | bytes 294920 | tf_op jit(solution)/shard_map/ppermute | solution.py:43
  44.5 5.9 %collective-permute-start.14 = (bf16[2,192,128]{2,1,0:T(8,128)(2,1)S(1)}, bf16[2,192,128]{2,1,0:T(8,128)(2,1)S(1)}, u32[]{:S(2)}, u32[]{:S(2)}) collective-permute-start(bf16[2,192,128]{2,1,0:T(8,128)(2,1)S(1)} %pad_maximum_fusion.refs_2_), channel_id=1, source_target_pairs={{0,8},{1,9},{2,10},{3,11},{4,12},{5,13},{6,14},{7,15},{8,0},{9,1},... | collective-permute-start | bytes 294920 | tf_op jit(solution)/shard_map/ppermute | solution.py:43
  44.9 6.6 %collective-permute-start.15 = (bf16[2,192,128]{2,1,0:T(8,128)(2,1)S(1)}, bf16[2,192,128]{2,1,0:T(8,128)(2,1)S(1)}, u32[]{:S(2)}, u32[]{:S(2)}) collective-permute-start(bf16[2,192,128]{2,1,0:T(8,128)(2,1)S(1)} %pad_maximum_fusion.refs_2_), channel_id=1, source_target_pairs={{0,9},{1,8},{2,11},{3,10},{4,13},{5,12},{6,15},{7,14},{8,1},{9,0},... | collective-permute-start | bytes 294920 | tf_op jit(solution)/shard_map/ppermute | solution.py:43
  46.7 5.7 %collective-permute-start.16 = (bf16[2,192,128]{2,1,0:T(8,128)(2,1)S(1)}, bf16[2,192,128]{2,1,0:T(8,128)(2,1)}, u32[]{:S(2)}, u32[]{:S(2)}) collective-permute-start(bf16[2,192,128]{2,1,0:T(8,128)(2,1)S(1)} %pad_maximum_fusion.refs_2_), channel_id=1, source_target_pairs={{0,12},{1,13},{2,14},{3,15},{4,8},{5,9},{6,10},{7,11},{8,4},{9,5},... | collective-permute-start | bytes 294920 | tf_op jit(solution)/shard_map/ppermute | solution.py:43
  48.8 6.5 %collective-permute-start.17 = (bf16[2,192,128]{2,1,0:T(8,128)(2,1)S(1)}, bf16[2,192,128]{2,1,0:T(8,128)(2,1)}, u32[]{:S(2)}, u32[]{:S(2)}) collective-permute-start(bf16[2,192,128]{2,1,0:T(8,128)(2,1)S(1)} %pad_maximum_fusion.refs_2_), channel_id=1, source_target_pairs={{0,13},{1,12},{2,15},{3,14},{4,9},{5,8},{6,11},{7,10},{8,5},{9,4},... | collective-permute-start | bytes 294920 | tf_op jit(solution)/shard_map/ppermute | solution.py:43
  50.4 5.0 %collective-permute-start.18 = (bf16[2,192,128]{2,1,0:T(8,128)(2,1)S(1)}, bf16[2,192,128]{2,1,0:T(8,128)(2,1)}, u32[]{:S(2)}, u32[]{:S(2)}) collective-permute-start(bf16[2,192,128]{2,1,0:T(8,128)(2,1)S(1)} %pad_maximum_fusion.refs_2_), channel_id=1, source_target_pairs={{0,2},{1,3},{2,0},{3,1},{4,6},{5,7},{6,4},{7,5},{8,10},{9,11},{10,... | collective-permute-start | bytes 294920 | tf_op jit(solution)/shard_map/ppermute | solution.py:43
  50.4 5.5 %collective-permute-start.19 = (bf16[2,192,128]{2,1,0:T(8,128)(2,1)S(1)}, bf16[2,192,128]{2,1,0:T(8,128)(2,1)}, u32[]{:S(2)}, u32[]{:S(2)}) collective-permute-start(bf16[2,192,128]{2,1,0:T(8,128)(2,1)S(1)} %collective-permute-done.11.refs_3_), channel_id=1, source_target_pairs={{0,2},{1,3},{2,0},{3,1},{4,6},{5,7},{6,4},{7,5},{8,10},{9,11},{10,... | collective-permute-start | bytes 294920 | tf_op jit(solution)/shard_map/ppermute | solution.py:43
  52.1 3.8 %collective-permute-start.20 = (bf16[2,192,128]{2,1,0:T(8,128)(2,1)S(1)}, bf16[2,192,128]{2,1,0:T(8,128)(2,1)}, u32[]{:S(2)}, u32[]{:S(2)}) collective-permute-start(bf16[2,192,128]{2,1,0:T(8,128)(2,1)S(1)} %collective-permute-done.12.refs_4_), channel_id=1, source_target_pairs={{0,2},{1,3},{2,0},{3,1},{4,6},{5,7},{6,4},{7,5},{8,10},{9,11},{10,... | collective-permute-start | bytes 294920 | tf_op jit(solution)/shard_map/ppermute | solution.py:43
  52.4 6.2 %collective-permute-start.21 = (bf16[2,192,128]{2,1,0:T(8,128)(2,1)}, bf16[2,192,128]{2,1,0:T(8,128)(2,1)S(1)}, u32[]{:S(2)}, u32[]{:S(2)}) collective-permute-start(bf16[2,192,128]{2,1,0:T(8,128)(2,1)} %copy-done.2), channel_id=1, source_target_pairs={{0,2},{1,3},{2,0},{3,1},{4,6},{5,7},{6,4},{7,5},{8,10},{9,11},{10,... | collective-permute-start | bytes 294920 | tf_op jit(solution)/shard_map/ppermute | solution.py:43
  55.3 3.2 %collective-permute-start.22 = (bf16[2,192,128]{2,1,0:T(8,128)(2,1)}, bf16[2,192,128]{2,1,0:T(8,128)(2,1)S(1)}, u32[]{:S(2)}, u32[]{:S(2)}) collective-permute-start(bf16[2,192,128]{2,1,0:T(8,128)(2,1)} %copy-done.4), channel_id=1, source_target_pairs={{0,2},{1,3},{2,0},{3,1},{4,6},{5,7},{6,4},{7,5},{8,10},{9,11},{10,... | collective-permute-start | bytes 294920 | tf_op jit(solution)/shard_map/ppermute | solution.py:43
  55.3 3.2 %collective-permute-start.23 = (bf16[2,192,128]{2,1,0:T(8,128)(2,1)}, bf16[2,192,128]{2,1,0:T(8,128)(2,1)S(1)}, u32[]{:S(2)}, u32[]{:S(2)}) collective-permute-start(bf16[2,192,128]{2,1,0:T(8,128)(2,1)} %copy-done.6), channel_id=1, source_target_pairs={{0,2},{1,3},{2,0},{3,1},{4,6},{5,7},{6,4},{7,5},{8,10},{9,11},{10,... | collective-permute-start | bytes 294920 | tf_op jit(solution)/shard_map/ppermute | solution.py:43
  55.9 2.7 %collective-permute-start.24 = (bf16[2,192,128]{2,1,0:T(8,128)(2,1)}, bf16[2,192,128]{2,1,0:T(8,128)(2,1)S(1)}, u32[]{:S(2)}, u32[]{:S(2)}) collective-permute-start(bf16[2,192,128]{2,1,0:T(8,128)(2,1)} %collective-permute-done.16.refs_8_), channel_id=1, source_target_pairs={{0,2},{1,3},{2,0},{3,1},{4,6},{5,7},{6,4},{7,5},{8,10},{9,11},{10,... | collective-permute-start | bytes 294920 | tf_op jit(solution)/shard_map/ppermute | solution.py:43
  (14 other events, 73.0 us)

commit v2 on v1

v2 whole, which is shorter than its diff:
```python
import jax
import jax.numpy as jnp
from jax import lax
from jax.experimental import pallas as pl
from jax.experimental.pallas import tpu as pltpu
from jax.sharding import Mesh
from jax.sharding import PartitionSpec as P

CUBE = ("low", "rep")


def adamw(grad, master, moment_one, moment_two, step_count):
    count = step_count[0].astype(jnp.float32)
    beta_one = 0.9
    beta_two = 0.95
    first = beta_one * moment_one + (1.0 - beta_one) * grad
    second = beta_two * moment_two + (1.0 - beta_two) * grad * grad
    first_hat = first / (1.0 - jnp.power(beta_one, count))
    second_hat = second / (1.0 - jnp.power(beta_two, count))
    updated = master - 0.01 * (first_hat / (jnp.sqrt(second_hat) + 1e-08) + 0.1 * master)
    return updated, first, second


def logits_kernel(n_rep, half, where_ref, acts_ref, own_ref, other_ref, out_ref, weight):
    my_high, my_core = where_ref[0], where_ref[1]
    cube, highs = own_ref.shape[:2]
    for piece, core in ((own_ref, my_core), (other_ref, 1 - my_core)):
        for k in range(cube):
            for j in range(highs):
                owner = (jnp.bitwise_xor(my_high, j) * (cube // n_rep) + k // n_rep) * 2 + core
                row = pl.multiple_of((owner * n_rep + k % n_rep) * half, half)
                weight[pl.ds(row, half), :] = piece[k, j]
    out_ref[...] = jnp.dot(
        acts_ref[...], weight[...], preferred_element_type=jnp.float32
    ).astype(out_ref.dtype)


def solution(mesh):
    n_seq, n_rep = mesh.shape["seq"], mesh.shape["rep"]
    n_low = 4
    n_high = n_seq // (2 * n_low)
    cube = n_low * n_rep
    fine = Mesh(
        mesh.devices.reshape(n_high, n_low, 2, n_rep), ("high", "low", "core", "rep")
    )

    def swap(x, axis, mask=1):
        return lax.ppermute(x, axis, [(i, i ^ mask) for i in range(fine.shape[axis])])

    def per_device(acts, grad_logits, master, moment_one, moment_two, step_count):
        rows, experts = master.shape
        half = rows // n_rep
        rep = lax.axis_index("rep")
        my_core, my_high = lax.axis_index("core"), lax.axis_index("high")

        product = lax.dot_general(
            acts, grad_logits, (((0,), (0,)), ((), ())), preferred_element_type=jnp.float32
        ).astype(jnp.bfloat16)
        by_core = product.reshape(n_seq // 2, 2, rows, experts)
        away = lax.dynamic_index_in_dim(by_core, 1 - my_core, 1, keepdims=False)
        kept = lax.dynamic_index_in_dim(by_core, my_core, 1, keepdims=False)
        arrived = swap(away, "core")
        chip = (kept.astype(jnp.float32) + arrived.astype(jnp.float32)).astype(jnp.bfloat16)
        chip = chip.reshape(n_high, cube, half, experts).transpose(1, 0, 2, 3)
        parts = lax.all_to_all(chip, CUBE, 0, 0, tiled=True)
        total = jnp.sum(parts.astype(jnp.float32), axis=0)

        grad = None
        for j in range(n_high):
            part = lax.dynamic_index_in_dim(total, jnp.bitwise_xor(my_high, j), 0, keepdims=False)
            if j:
                part = swap(part, "high", j)
            grad = part if grad is None else grad + part

        mine = [
            lax.dynamic_slice_in_dim(a, rep * half, half, 0)
            for a in (master, moment_one, moment_two)
        ]
        weight = adamw(grad, *mine, step_count)[0].astype(jnp.bfloat16)

        other = swap(grad, "rep")
        whole = jnp.where(
            rep == 0,
            jnp.concatenate([grad, other], 0),
            jnp.concatenate([other, grad], 0),
        )
        updated, first, second = adamw(whole, master, moment_one, moment_two, step_count)

        column = jnp.stack([swap(weight, "high", j) if j else weight for j in range(n_high)])
        column = jnp.broadcast_to(column, (cube, n_high, half, experts))
        own = lax.all_to_all(column, CUBE, 0, 0, tiled=True)
        across = swap(own, "core")
        if half % 16 == 0:
            vmem = pl.BlockSpec(memory_space=pltpu.VMEM)
            logits = pl.pallas_call(
                lambda *refs: logits_kernel(n_rep, half, *refs),
                out_shape=jax.ShapeDtypeStruct((acts.shape[0], experts), jnp.bfloat16),
                in_specs=[pl.BlockSpec(memory_space=pltpu.SMEM)] + [vmem] * 3,
                out_specs=vmem,
                scratch_shapes=[pltpu.VMEM((n_seq * rows, experts), jnp.bfloat16)],
                compiler_params=pltpu.CompilerParams(vmem_limit_bytes=32 * 2**20),
            )(jnp.stack([my_high, my_core]), acts, own, across)
        else:
            both = jnp.where(my_core == 0, jnp.stack([own, across]), jnp.stack([across, own]))
            both = both[:, :, jnp.bitwise_xor(my_high, jnp.arange(n_high))]
            full = both.reshape(2, n_low, n_rep, n_high, half, experts).transpose(3, 1, 0, 2, 4, 5)
            full = full.reshape(n_seq * rows, experts)
            logits = jnp.dot(acts, full, preferred_element_type=jnp.float32).astype(jnp.bfloat16)
        return updated, first, second, logits

    rows_of, tokens = P(("high", "low", "core"), None), P(("high", "low", "core", "rep"), None)
    return jax.shard_map(
        per_device,
        mesh=fine,
        in_specs=(tokens, tokens, rows_of, rows_of, rows_of, P()),
        out_specs=(rows_of, rows_of, rows_of, tokens),
        check_vma=False,
    )
```

time: 64.5 us -> 63.8 us (0.989)
  starting transfers between devices: 27.5 us -> 10.7 us
  blocking collectives: 0 us -> 14.1 us
  waiting for transfers between devices: 17.4 us -> 26.7 us
  local copies, waits for them, and re-layouts: 7.1 us -> 2.02 us
  other arithmetic: 4.77 us -> 2.43 us
    ppermute x26 -> x5, starting transfers between devices: 27.5 us -> 4.46 us  [swap(): lax.ppermute(x, axis, [(i, i ^ mask) for i in range(fine.shape[axis])])]
    all_to_all x0 -> x1, blocking collectives: none -> 14.1 us  [per_device(): own = lax.all_to_all(column, CUBE, 0, 0, tiled=True)]
    all_to_all x0 -> x1, waiting for transfers between devices: none -> 12 us  [per_device(): parts = lax.all_to_all(chip, CUBE, 0, 0, tiled=True)]
    all_to_all x0 -> x1, starting transfers between devices: none -> 6.24 us  [per_device(): parts = lax.all_to_all(chip, CUBE, 0, 0, tiled=True)]
    unnamed x24 -> x10, local copies, waits for them, and re-layouts: 5.67 us -> 0.85 us
    ppermute x26 -> x5, waiting for transfers between devices: 17.4 us -> 14.7 us  [swap(): lax.ppermute(x, axis, [(i, i ^ mask) for i in range(fine.shape[axis])])]
    add x1 -> x0, other arithmetic: 1.28 us -> none  [per_device(): total = part if total is None else total + part]
    convert_element_type x1, other arithmetic: 1.08 us -> 0.11 us  [per_device(): weight = adamw(grad, *mine, step_count)[0].astype(jnp.bfloat16)]
  transfers between devices with their start and end apart: 26 -> 6, of which waited for: 11 -> 5; matrix products, arithmetic and copies ran while one was open for 3% -> 3% of each run, Pallas kernels for 0% -> 0%
where the time goes in v2:
time: 63.8 us; the launch traced here: 63.4 us
  waiting for transfers between devices  26.7 us (42%)
  blocking collectives  14.1 us (22%)
  starting transfers between devices  10.7 us (17%)
  Pallas kernels  3.09 us (5%)
  matrix products  2.93 us (5%)
  other arithmetic  2.43 us (4%)
  local copies, waits for them, and re-layouts  2.02 us (3%)
  between operations  1.45 us (2%)
    ppermute x5, waiting for transfers between devices, swap(): lax.ppermute(x, axis, [(i, i ^ mask) for i in range(fine.shape[axis])])  14.7 us
    all_to_all x1, blocking collectives, per_device(): own = lax.all_to_all(column, CUBE, 0, 0, tiled=True)  14.1 us
    all_to_all x1, waiting for transfers between devices, per_device(): parts = lax.all_to_all(chip, CUBE, 0, 0, tiled=True)  12 us
    all_to_all x1, starting transfers between devices, per_device(): parts = lax.all_to_all(chip, CUBE, 0, 0, tiled=True)  6.24 us
    ppermute x5, starting transfers between devices, swap(): lax.ppermute(x, axis, [(i, i ^ mask) for i in range(fine.shape[axis])])  4.46 us
    pallas_call x1, Pallas kernels, per_device(): pl.pallas_call(lambda *refs: logits_kernel(n_rep, half, *refs), out_shape...  3.09 us
    dot_general x1, matrix products, per_device(): lax.dot_general(acts, grad_logits, (((0,), (0,)), ((), ())), preferred_el...  2.93 us
    sub x1, other arithmetic, adamw(): master - 0.01 * (first_hat / (jnp.sqrt(second_hat) + 1e-08) + 0.1 * master)  1.91 us
  transfers between devices with their start and end apart: 6, of which 5 were waited for; matrix products, arithmetic and copies ran while one was open for 3% of the time, Pallas kernels for 0%

profile of v2, /device:TPU:0, one launch (start us, length us, event | category | flops | bytes accessed | tf_op | source)
XLA Modules:
  0.0 63.4 jit_solution(12111730876093950449)
XLA Ops:
  0.6 0.0 copy-start
  0.7 0.8 %copy-done = bf16[256,128]{1,0:T(8,128)(2,1)S(1)} copy-done((bf16[256,128]{1,0:T(8,128)(2,1)S(1)}, bf16[256,128]{1,0:T(8,128)(2,1)}, u32[]{:S(2)}) %copy-start) | copy-done | bytes 65560
  1.5 2.9 %convolution_convert_fusion = bf16[6144,128]{1,0:T(8,128)(2,1)S(1)} fusion(bf16[256,6144]{1,0:T(8,128)(2,1)} %refs_1_.1, bf16[256,128]{1,0:T(8,128)(2,1)S(1)} %copy-done), kind=kOutput, calls=%fused_computation | convolution fusion | flops 403439616 | bytes 4784128 | tf_op jit(solution)/shard_map/dot_general | solution.py:56
  4.4 0.1 dynamic-slice_bitcast_fusion
  4.5 0.5 collective-permute-start
  5.0 1.9 %collective-permute-done = bf16[8,384,128]{2,1,0:T(8,128)(2,1)S(1)} collective-permute-done((bf16[8,384,128]{2,1,0:T(8,128)(2,1)S(1)}, bf16[8,384,128]{2,1,0:T(8,128)(2,1)S(1)}, u32[]{:S(2)}, u32[]{:S(2)}) %collective-permute-start) | collective-permute-done | bytes 786464 | tf_op jit(solution)/shard_map/ppermute | solution.py:48
  6.9 0.2 fusion
  7.1 0.9 %copy.11 = bf16[8,2,192,128]{3,2,1,0:T(8,128)(2,1)} copy(bf16[8,2,192,128]{3,2,0,1:T(8,128)(2,1)S(1)} %bitcast.26) | data formatting | bytes 1572864 | tf_op jit(solution)/shard_map/transpose | solution.py:64
  8.1 6.2 %all-to-all-start = ((bf16[8,2,192,128]{3,2,1,0:T(8,128)(2,1)}), bf16[8,2,192,128]{3,2,1,0:T(8,128)(2,1)S(1)}, u32[]{:S(2)}, u32[]{:S(2)}) async-start(bf16[8,2,192,128]{3,2,1,0:T(8,128)(2,1)} %copy.11), calls=%async_computation | async-start | bytes 1572864 | tf_op jit(solution)/shard_map/all_to_all | solution.py:65
  14.3 12.0 %all-to-all-done = bf16[8,2,192,128]{3,2,1,0:T(8,128)(2,1)S(1)} async-done(((bf16[8,2,192,128]{3,2,1,0:T(8,128)(2,1)}), bf16[8,2,192,128]{3,2,1,0:T(8,128)(2,1)S(1)}, u32[]{:S(2)}, u32[]{:S(2)}) %all-to-all-start) | async-done | bytes 786464 | tf_op jit(solution)/shard_map/all_to_all | solution.py:65
  26.3 0.1 convert_reduce_fusion
  26.4 2.7 %collective-permute-start.1 = (f32[192,128]{1,0:T(8,128)S(1)}, f32[192,128]{1,0:T(8,128)S(1)}, u32[]{:S(2)}, u32[]{:S(2)}) collective-permute-start(f32[192,128]{1,0:T(8,128)S(1)} %dynamic-slice_bitcast_fusion.1), channel_id=1, source_target_pairs={{0,16},{16,0},{1,17},{17,1},{2,18},{18,2},{3,19},{19,3},{4,20},{20... | collective-permute-start | bytes 294920 | tf_op jit(solution)/shard_map/ppermute | solution.py:48
  29.8 3.9 %collective-permute-done.1 = f32[192,128]{1,0:T(8,128)S(1)} collective-permute-done((f32[192,128]{1,0:T(8,128)S(1)}, f32[192,128]{1,0:T(8,128)S(1)}, u32[]{:S(2)}, u32[]{:S(2)}) %collective-permute-start.1) | collective-permute-done | bytes 98336 | tf_op jit(solution)/shard_map/ppermute | solution.py:48
  33.7 0.1 subtract_convert_fusion
  33.8 1.1 %collective-permute-start.3 = (bf16[192,128]{1,0:T(8,128)(2,1)S(1)}, bf16[192,128]{1,0:T(8,128)(2,1)S(1)}, u32[]{:S(2)}, u32[]{:S(2)}) collective-permute-start(bf16[192,128]{1,0:T(8,128)(2,1)S(1)} %get-tuple-element.4), channel_id=1, source_target_pairs={{0,16},{16,0},{1,17},{17,1},{2,18},{18,2},{3,19},{19,3},{4,20},{20... | collective-permute-start | bytes 147464 | tf_op jit(solution)/shard_map/ppermute | solution.py:48
  34.9 4.0 %collective-permute-done.3 = bf16[192,128]{1,0:T(8,128)(2,1)S(1)} collective-permute-done((bf16[192,128]{1,0:T(8,128)(2,1)S(1)}, bf16[192,128]{1,0:T(8,128)(2,1)S(1)}, u32[]{:S(2)}, u32[]{:S(2)}) %collective-permute-start.3) | collective-permute-done | bytes 49184 | tf_op jit(solution)/shard_map/ppermute | solution.py:48
  38.9 0.0 copy-start.1
  38.9 0.1 broadcast_in_dim.3
  39.1 14.1 %all_to_all.10.refs_2_ = bf16[8,2,192,128]{3,2,1,0:T(8,128)(2,1)} all-to-all(bf16[8,2,192,128]{3,2,1,0:T(8,128)(2,1)S(1)} %broadcast_in_dim.3), channel_id=1, replica_groups=mesh['high'=2,'low'=4,'core'=2,'rep'=2] {'low','rep'}, dimensions={0} | all-to-all | bytes 1572864 | tf_op jit(solution)/shard_map/all_to_all | solution.py:91
  53.2 0.2 collective-permute-start.2
  53.4 0.1 pad_add_fusion.refs_0_
  53.5 4.9 %collective-permute-done.2 = f32[192,128]{1,0:T(8,128)S(1)} collective-permute-done((f32[192,128]{1,0:T(8,128)S(1)}, f32[192,128]{1,0:T(8,128)S(1)}, u32[]{:S(2)}, u32[]{:S(2)}) %collective-permute-start.2) | collective-permute-done | bytes 98336 | tf_op jit(solution)/shard_map/ppermute | solution.py:48
  58.4 1.9 %multiply_subtract_fusion = (f32[384,128]{1,0:T(8,128)}, f32[384,128]{1,0:T(8,128)}, f32[384,128]{1,0:T(8,128)}) fusion(f32[384,128]{1,0:T(8,128)S(1)} %copy-done.2, f32[]{:T(128)} %bitcast.8, f32[]{:T(128)} %bitcast.7, f32[192,128]{1,0:T(8,128)S(1)} %get-tuple-element.5, f32[192,128]{1,0:T(8,128)S(1)} %collective-permute-done.2, pred[]{:T(512)S(6)} %eq.3, ...), kind=kLoop, calls=%fused_computation.8 | loop fusion | flops 884736 | bytes 1376265 | tf_op jit(solution)/shard_map/sub | solution.py:20
  60.3 3.1 %shard_map.93 = bf16[256,128]{1,0:T(8,128)(2,1)} custom-call(s32[2]{0:T(128)S(1)} %pad_add_fusion.refs_0_, bf16[256,6144]{1,0:T(8,128)(2,1)S(1)} %copy-done.1, bf16[8,2,192,128]{3,2,1,0:T(8,128)(2,1)} %all_to_all.10.refs_2_, bf16[8,2,192,128]{3,2,1,0:T(8,128)(2,1)} %collective-permute-done.4.refs_3_), custom_call_target="tpu_custom_call" | custom-call | tf_op jit(solution)/shard_map/pallas_call | solution.py:95
  (11 shorter events, 0.0 us)
Async XLA Ops:
  0.6 0.8 %copy-start = (bf16[256,128]{1,0:T(8,128)(2,1)S(1)}, bf16[256,128]{1,0:T(8,128)(2,1)}, u32[]{:S(2)}) copy-start(bf16[256,128]{1,0:T(8,128)(2,1)} %param.7) | copy-start | bytes 196612
  4.5 2.4 %collective-permute-start = (bf16[8,384,128]{2,1,0:T(8,128)(2,1)S(1)}, bf16[8,384,128]{2,1,0:T(8,128)(2,1)S(1)}, u32[]{:S(2)}, u32[]{:S(2)}) collective-permute-start(bf16[8,384,128]{2,1,0:T(8,128)(2,1)S(1)} %dynamic-slice_bitcast_fusion), channel_id=1, source_target_pairs={{0,2},{2,0},{1,3},{3,1},{4,6},{6,4},{5,7},{7,5},{8,10},{10,8},{9,1... | collective-permute-start | bytes 2359304 | tf_op jit(solution)/shard_map/ppermute | solution.py:48
  8.1 25.6 %copy-start.2 = (f32[384,128]{1,0:T(8,128)S(1)}, f32[384,128]{1,0:T(8,128)}, u32[]{:S(2)}) copy-start(f32[384,128]{1,0:T(8,128)} %param.8) | copy-start | bytes 589828
  8.1 25.6 %copy-start.3 = (f32[384,128]{1,0:T(8,128)S(1)}, f32[384,128]{1,0:T(8,128)}, u32[]{:S(2)}) copy-start(f32[384,128]{1,0:T(8,128)} %param.10) | copy-start | bytes 589828
  8.1 25.6 %copy-start.4 = (f32[384,128]{1,0:T(8,128)S(1)}, f32[384,128]{1,0:T(8,128)}, u32[]{:S(2)}) copy-start(f32[384,128]{1,0:T(8,128)} %param.9) | copy-start | bytes 589828
  8.1 18.2 %all-to-all-start = ((bf16[8,2,192,128]{3,2,1,0:T(8,128)(2,1)}), bf16[8,2,192,128]{3,2,1,0:T(8,128)(2,1)S(1)}, u32[]{:S(2)}, u32[]{:S(2)}) async-start(bf16[8,2,192,128]{3,2,1,0:T(8,128)(2,1)} %copy.11), calls=%async_computation | async-start | bytes 1572864 | tf_op jit(solution)/shard_map/all_to_all | solution.py:65
  26.4 7.3 %collective-permute-start.1 = (f32[192,128]{1,0:T(8,128)S(1)}, f32[192,128]{1,0:T(8,128)S(1)}, u32[]{:S(2)}, u32[]{:S(2)}) collective-permute-start(f32[192,128]{1,0:T(8,128)S(1)} %dynamic-slice_bitcast_fusion.1), channel_id=1, source_target_pairs={{0,16},{16,0},{1,17},{17,1},{2,18},{18,2},{3,19},{19,3},{4,20},{20... | collective-permute-start | bytes 294920 | tf_op jit(solution)/shard_map/ppermute | solution.py:48
  33.8 5.1 %collective-permute-start.3 = (bf16[192,128]{1,0:T(8,128)(2,1)S(1)}, bf16[192,128]{1,0:T(8,128)(2,1)S(1)}, u32[]{:S(2)}, u32[]{:S(2)}) collective-permute-start(bf16[192,128]{1,0:T(8,128)(2,1)S(1)} %get-tuple-element.4), channel_id=1, source_target_pairs={{0,16},{16,0},{1,17},{17,1},{2,18},{18,2},{3,19},{19,3},{4,20},{20... | collective-permute-start | bytes 147464 | tf_op jit(solution)/shard_map/ppermute | solution.py:48
  38.9 21.4 %copy-start.1 = (bf16[256,6144]{1,0:T(8,128)(2,1)S(1)}, bf16[256,6144]{1,0:T(8,128)(2,1)}, u32[]{:S(2)}) copy-start(bf16[256,6144]{1,0:T(8,128)(2,1)} %refs_1_.1) | copy-start | bytes 9437188
  53.2 7.1 %collective-permute-start.4 = (bf16[8,2,192,128]{3,2,1,0:T(8,128)(2,1)}, bf16[8,2,192,128]{3,2,1,0:T(8,128)(2,1)}, u32[]{:S(2)}, u32[]{:S(2)}) collective-permute-start(bf16[8,2,192,128]{3,2,1,0:T(8,128)(2,1)} %all_to_all.10.refs_2_), channel_id=1, source_target_pairs={{0,2},{2,0},{1,3},{3,1},{4,6},{6,4},{5,7},{7,5},{8,10},{10,8},{9,1... | collective-permute-start | bytes 2359304 | tf_op jit(solution)/shard_map/ppermute | solution.py:48
  53.2 5.2 %collective-permute-start.2 = (f32[192,128]{1,0:T(8,128)S(1)}, f32[192,128]{1,0:T(8,128)S(1)}, u32[]{:S(2)}, u32[]{:S(2)}) collective-permute-start(f32[192,128]{1,0:T(8,128)S(1)} %get-tuple-element.5), channel_id=1, source_target_pairs={{0,1},{1,0},{2,3},{3,2},{4,5},{5,4},{6,7},{7,6},{8,9},{9,8},{10,11... | collective-permute-start | bytes 294920 | tf_op jit(solution)/shard_map/ppermute | solution.py:48

commit v3 on v2

v3 whole, which is shorter than its diff:
```python
import jax
import jax.numpy as jnp
from jax import lax
from jax.experimental import pallas as pl
from jax.experimental.pallas import tpu as pltpu
from jax.sharding import Mesh
from jax.sharding import PartitionSpec as P

AXES = ("high", "low", "core", "rep")
N_LOW = 4


def parity(n):
    return (n ^ (n >> 1)) & 1


def adamw(grad, master, moment_one, moment_two, step_count):
    count = step_count[0].astype(jnp.float32)
    beta_one = 0.9
    beta_two = 0.95
    first = beta_one * moment_one + (1.0 - beta_one) * grad
    second = beta_two * moment_two + (1.0 - beta_two) * grad * grad
    first_hat = first / (1.0 - jnp.power(beta_one, count))
    second_hat = second / (1.0 - jnp.power(beta_two, count))
    updated = master - 0.01 * (first_hat / (jnp.sqrt(second_hat) + 1e-08) + 0.1 * master)
    return updated, first, second


def block_row(where, chip, c, j):
    high, low, core, rep = where
    k, flip, by_core = chip
    rep = rep ^ flip ^ core if by_core else rep ^ flip
    return (((high ^ j) * N_LOW + (low ^ k)) * 2 + c) * 2 + rep


def logits_kernel(half, chips, where_ref, acts_ref, *refs):
    pieces, out_ref, weight = refs[:-2], refs[-2], refs[-1]
    where = [where_ref[i] for i in range(4)]
    for piece, chip in zip(pieces, chips):
        for c in range(piece.shape[0]):
            for j in range(piece.shape[1]):
                row = pl.multiple_of(block_row(where, chip, c, j) * half, half)
                weight[pl.ds(row, half), :] = piece[c, j]
    out_ref[...] = jnp.dot(
        acts_ref[...], weight[...], preferred_element_type=jnp.float32
    ).astype(out_ref.dtype)


def solution(mesh):
    n_seq, n_rep = mesh.shape["seq"], mesh.shape["rep"]
    n_high = n_seq // (2 * N_LOW)
    fine = Mesh(mesh.devices.reshape(n_high, N_LOW, 2, n_rep), AXES)

    def swap(x, axis, mask=1):
        return lax.ppermute(x, axis, [(i, i ^ mask) for i in range(fine.shape[axis])])

    def to_partner(x, k):
        axes = ("low", "core", "rep")
        pairs = []
        for low in range(N_LOW):
            for c in range(2):
                for r in range(n_rep):
                    flip = parity(k) ^ c
                    if k or flip:
                        there = ((low ^ k) * 2 + c) * n_rep + (r ^ flip)
                        pairs.append(((low * 2 + c) * n_rep + r, there))
        return lax.ppermute(x, axes, pairs)

    def per_device(acts, grad_logits, master, moment_one, moment_two, step_count):
        rows, experts = master.shape
        half = rows // n_rep
        high, low, core, rep = (lax.axis_index(a) for a in AXES)
        first_core = core == 0

        product = lax.dot_general(
            acts, grad_logits, (((0,), (0,)), ((), ())), preferred_element_type=jnp.float32
        ).astype(jnp.bfloat16)
        product = product.reshape(n_high, N_LOW, 2, n_rep, half, experts)

        def for_partner(k, of_core):
            chip = (0, low ^ k, 0, rep ^ parity(k) ^ of_core, 0, 0)
            block = lax.dynamic_slice(product, chip, (n_high, 1, 2, 1, half, experts))
            return block.reshape(n_high, 2, half, experts)

        away = jnp.stack([for_partner(k, 1 - core) for k in range(N_LOW)])
        arrived = swap(away, "core").astype(jnp.float32)
        total = None
        for k in range(N_LOW):
            chip = (for_partner(k, core).astype(jnp.float32) + arrived[k]).astype(jnp.bfloat16)
            part = to_partner(chip, k)
            if k == 0:
                part = jnp.where(first_core, chip, part)
            part = part.astype(jnp.float32)
            total = part if total is None else total + part

        def of_core(x, c):
            return lax.dynamic_index_in_dim(x, c, 1, keepdims=False)

        total = of_core(total, core) + swap(of_core(total, 1 - core), "core")

        grad = None
        for j in range(n_high):
            part = lax.dynamic_index_in_dim(total, high ^ j, 0, keepdims=False)
            if j:
                part = swap(part, "high", j)
            grad = part if grad is None else grad + part

        mine = [
            lax.dynamic_slice_in_dim(a, rep * half, half, 0)
            for a in (master, moment_one, moment_two)
        ]
        weight = adamw(grad, *mine, step_count)[0].astype(jnp.bfloat16)

        column = jnp.stack([swap(weight, "high", j) if j else weight for j in range(n_high)])
        other = swap(grad, "rep")
        whole = jnp.where(
            rep == 0,
            jnp.concatenate([grad, other], 0),
            jnp.concatenate([other, grad], 0),
        )
        updated, first, second = adamw(whole, master, moment_one, moment_two, step_count)

        across = swap(column, "core")
        own = jnp.where(first_core, jnp.stack([column, across]), jnp.stack([across, column]))
        got = [to_partner(own, k) for k in range(N_LOW)]
        over = [swap(piece, "core") for piece in got]
        pieces = [own, jnp.where(first_core, over[0], got[0])] + got[1:] + over[1:]
        chips = [(0, 0, False), (0, 1, False)]
        chips += [(k, parity(k), True) for k in range(1, N_LOW)]
        chips += [(k, parity(k) ^ 1, True) for k in range(1, N_LOW)]
        where = (high, low, core, rep)
        if half % 16 == 0:
            vmem = pl.BlockSpec(memory_space=pltpu.VMEM)
            logits = pl.pallas_call(
                lambda *refs: logits_kernel(half, chips, *refs),
                out_shape=jax.ShapeDtypeStruct((acts.shape[0], experts), jnp.bfloat16),
                in_specs=[pl.BlockSpec(memory_space=pltpu.SMEM)] + [vmem] * (1 + len(pieces)),
                out_specs=vmem,
                scratch_shapes=[pltpu.VMEM((n_seq * rows, experts), jnp.bfloat16)],
                compiler_params=pltpu.CompilerParams(vmem_limit_bytes=32 * 2**20),
            )(jnp.stack(where), acts, *pieces)
        else:
            blocks = jnp.stack(pieces).reshape(-1, half, experts)
            places = [
                block_row(where, chip, c, j)
                for chip in chips
                for c in range(2)
                for j in range(n_high)
            ]
            full = jnp.zeros_like(blocks).at[jnp.stack(places)].set(blocks)
            full = full.reshape(n_seq * rows, experts)
            logits = jnp.dot(acts, full, preferred_element_type=jnp.float32).astype(jnp.bfloat16)
        return updated, first, second, logits

    rows_of, tokens = P(AXES[:3], None), P(AXES, None)
    return jax.shard_map(
        per_device,
        mesh=fine,
        in_specs=(tokens, tokens, rows_of, rows_of, rows_of, P()),
        out_specs=(rows_of, rows_of, rows_of, tokens),
        check_vma=False,
    )
```

time: 63.8 us -> 63.1 us (0.989)
  blocking collectives: 14.1 us -> 0 us
  starting transfers between devices: 10.7 us -> 24.7 us
  other arithmetic: 2.43 us -> 4.05 us
  waiting for transfers between devices: 26.7 us -> 25.8 us
  Pallas kernels: 3.09 us -> 2.25 us
    all_to_all x1 -> x0, blocking collectives: 14.1 us -> none  [per_device(): own = lax.all_to_all(column, CUBE, 0, 0, tiled=True)]
    all_to_all x1 -> x0, waiting for transfers between devices: 12 us -> none  [per_device(): parts = lax.all_to_all(chip, CUBE, 0, 0, tiled=True)]
    ppermute x0 -> x8, starting transfers between devices: none -> 11.8 us  [to_partner(): return lax.ppermute(x, axes, pairs)]
    ppermute x0 -> x8, waiting for transfers between devices: none -> 10.6 us  [to_partner(): return lax.ppermute(x, axes, pairs)]
    ppermute x5 -> x10, starting transfers between devices: 4.46 us -> 12.9 us  [swap(): lax.ppermute(x, axis, [(i, i ^ mask) for i in range(fine.shape[axis])])]
    all_to_all x1 -> x0, starting transfers between devices: 6.24 us -> none  [per_device(): parts = lax.all_to_all(chip, CUBE, 0, 0, tiled=True)]
    convert_element_type x1, other arithmetic: 0.11 us -> 1.28 us  [per_device(): weight = adamw(grad, *mine, step_count)[0].astype(jnp.bfloat16)]
    transpose x1 -> x0, local copies, waits for them, and re-layouts: 0.94 us -> none  [per_device(): chip = chip.reshape(n_high, cube, half, experts).transpose(1, 0, 2, 3)]
  transfers between devices with their start and end apart: 6 -> 18, of which waited for: 5 -> 12; matrix products, arithmetic and copies ran while one was open for 3% -> 3% of each run, Pallas kernels for 0% -> 0%
where the time goes in v3:
time: 63.1 us; the launch traced here: 62.8 us
  waiting for transfers between devices  25.8 us (41%)
  starting transfers between devices  24.7 us (39%)
  other arithmetic  4.05 us (6%)
  matrix products  2.93 us (5%)
  Pallas kernels  2.25 us (4%)
  local copies, waits for them, and re-layouts  1.55 us (2%)
  between operations  1.53 us (2%)
    ppermute x10, waiting for transfers between devices, swap(): lax.ppermute(x, axis, [(i, i ^ mask) for i in range(fine.shape[axis])])  15.3 us
    ppermute x10, starting transfers between devices, swap(): lax.ppermute(x, axis, [(i, i ^ mask) for i in range(fine.shape[axis])])  12.9 us
    ppermute x8, starting transfers between devices, to_partner(): return lax.ppermute(x, axes, pairs)  11.8 us
    ppermute x8, waiting for transfers between devices, to_partner(): return lax.ppermute(x, axes, pairs)  10.6 us
    dot_general x1, matrix products, per_device(): lax.dot_general(acts, grad_logits, (((0,), (0,)), ((), ())), preferred_el...  2.93 us
    pallas_call x1, Pallas kernels, per_device(): pl.pallas_call(lambda *refs: logits_kernel(half, chips, *refs), out_shape...  2.25 us
    sub x1, other arithmetic, adamw(): master - 0.01 * (first_hat / (jnp.sqrt(second_hat) + 1e-08) + 0.1 * master)  2 us
    unnamed x6, local copies, waits for them, and re-layouts  1.44 us
  transfers between devices with their start and end apart: 18, of which 12 were waited for; matrix products, arithmetic and copies ran while one was open for 3% of the time, Pallas kernels for 0%

profile of v3, /device:TPU:0, one launch (start us, length us, event | category | flops | bytes accessed | tf_op | source)
XLA Modules:
  0.0 62.8 jit_solution(10079667946659489806)
XLA Ops:
  0.7 0.8 %copy-done = bf16[256,128]{1,0:T(8,128)(2,1)S(1)} copy-done((bf16[256,128]{1,0:T(8,128)(2,1)S(1)}, bf16[256,128]{1,0:T(8,128)(2,1)}, u32[]{:S(2)}) %copy-start) | copy-done | bytes 65560
  1.5 2.9 %convolution_convert_fusion = bf16[6144,128]{1,0:T(8,128)(2,1)S(1)} fusion(bf16[256,6144]{1,0:T(8,128)(2,1)} %refs_1_.1, bf16[256,128]{1,0:T(8,128)(2,1)S(1)} %copy-done), kind=kOutput, calls=%fused_computation | convolution fusion | flops 403439616 | bytes 4784128 | tf_op jit(solution)/shard_map/dot_general | solution.py:75
  5.1 1.9 %collective-permute-done = bf16[4,2,2,192,128]{4,3,2,1,0:T(8,128)(2,1)S(1)} collective-permute-done((bf16[4,2,2,192,128]{4,3,2,1,0:T(8,128)(2,1)S(1)}, bf16[4,2,2,192,128]{4,3,2,1,0:T(8,128)(2,1)S(1)}, u32[]{:S(2)}, u32[]{:S(2)}) %collective-permute-start) | collective-permute-done | bytes 786464 | tf_op jit(solution)/shard_map/ppermute | solution.py:55
  8.1 3.9 %collective-permute-start.2 = (bf16[2,2,192,128]{3,2,1,0:T(8,128)(2,1)S(1)}, bf16[2,2,192,128]{3,2,1,0:T(8,128)(2,1)S(1)}, u32[]{:S(2)}, u32[]{:S(2)}) collective-permute-start(bf16[2,2,192,128]{3,2,1,0:T(8,128)(2,1)S(1)} %get-tuple-element.12), channel_id=1, source_target_pairs={{0,5},{1,4},{2,6},{3,7},{4,1},{5,0},{6,2},{7,3},{8,13},{9,12},{10,... | collective-permute-start | bytes 589832 | tf_op jit(solution)/shard_map/ppermute | solution.py:67
  12.0 1.5 %collective-permute-start.3 = (bf16[2,2,192,128]{3,2,1,0:T(8,128)(2,1)S(1)}, bf16[2,2,192,128]{3,2,1,0:T(8,128)(2,1)S(1)}, u32[]{:S(2)}, u32[]{:S(2)}) collective-permute-start(bf16[2,2,192,128]{3,2,1,0:T(8,128)(2,1)S(1)} %get-tuple-element.11), channel_id=1, source_target_pairs={{0,9},{1,8},{2,10},{3,11},{4,13},{5,12},{6,14},{7,15},{8,1},{9,0},... | collective-permute-start | bytes 589832 | tf_op jit(solution)/shard_map/ppermute | solution.py:67
  13.5 3.3 %collective-permute-done.2 = bf16[2,2,192,128]{3,2,1,0:T(8,128)(2,1)S(1)} collective-permute-done((bf16[2,2,192,128]{3,2,1,0:T(8,128)(2,1)S(1)}, bf16[2,2,192,128]{3,2,1,0:T(8,128)(2,1)S(1)}, u32[]{:S(2)}, u32[]{:S(2)}) %collective-permute-start.2) | collective-permute-done | bytes 196640 | tf_op jit(solution)/shard_map/ppermute | solution.py:67
  16.9 3.7 %collective-permute-done.3 = bf16[2,2,192,128]{3,2,1,0:T(8,128)(2,1)S(1)} collective-permute-done((bf16[2,2,192,128]{3,2,1,0:T(8,128)(2,1)S(1)}, bf16[2,2,192,128]{3,2,1,0:T(8,128)(2,1)S(1)}, u32[]{:S(2)}, u32[]{:S(2)}) %collective-permute-start.3) | collective-permute-done | bytes 196640 | tf_op jit(solution)/shard_map/ppermute | solution.py:67
  20.6 2.1 %collective-permute-done.4 = bf16[2,2,192,128]{3,2,1,0:T(8,128)(2,1)S(1)} collective-permute-done((bf16[2,2,192,128]{3,2,1,0:T(8,128)(2,1)S(1)}, bf16[2,2,192,128]{3,2,1,0:T(8,128)(2,1)S(1)}, u32[]{:S(2)}, u32[]{:S(2)}) %collective-permute-start.4) | collective-permute-done | bytes 196640 | tf_op jit(solution)/shard_map/ppermute | solution.py:67
  23.5 1.1 %collective-permute-done.5 = f32[2,192,128]{2,1,0:T(8,128)S(1)} collective-permute-done((f32[2,192,128]{2,1,0:T(8,128)S(1)}, f32[2,192,128]{2,1,0:T(8,128)S(1)}, u32[]{:S(2)}, u32[]{:S(2)}) %collective-permute-start.5) | collective-permute-done | bytes 196640 | tf_op jit(solution)/shard_map/ppermute | solution.py:55
  24.6 3.3 %collective-permute-start.6 = (f32[192,128]{1,0:T(8,128)S(1)}, f32[192,128]{1,0:T(8,128)S(1)}, u32[]{:S(2)}, u32[]{:S(2)}) collective-permute-start(f32[192,128]{1,0:T(8,128)S(1)} %dynamic-slice_bitcast_fusion.5), channel_id=1, source_target_pairs={{0,16},{16,0},{1,17},{17,1},{2,18},{18,2},{3,19},{19,3},{4,20},{20... | collective-permute-start | bytes 294920 | tf_op jit(solution)/shard_map/ppermute | solution.py:55
  28.6 4.5 %collective-permute-done.6 = f32[192,128]{1,0:T(8,128)S(1)} collective-permute-done((f32[192,128]{1,0:T(8,128)S(1)}, f32[192,128]{1,0:T(8,128)S(1)}, u32[]{:S(2)}, u32[]{:S(2)}) %collective-permute-start.6) | collective-permute-done | bytes 98336 | tf_op jit(solution)/shard_map/ppermute | solution.py:55
  33.7 1.3 %subtract_convert_fusion = (bf16[192,128]{1,0:T(8,128)(2,1)S(1)}, f32[192,128]{1,0:T(8,128)S(1)}) fusion(f32[384,128]{1,0:T(8,128)} %param.8, s32[]{:T(128)S(6)} %select_n.91, f32[384,128]{1,0:T(8,128)} %param.10, f32[384,128]{1,0:T(8,128)} %param.9, f32[]{:T(128)} %bitcast.18, f32[]{:T(128)} %bitcast.17, f32[192,128]{1,0:T(8,128)} %copy-done.2, ...), kind=kLoop, calls=%fused_computation.37 | loop fusion | flops 417792 | bytes 638992 | tf_op jit(solution)/shard_map/convert_element_type | solution.py:112
  35.7 5.4 %collective-permute-done.8 = bf16[192,128]{1,0:T(8,128)(2,1)S(1)} collective-permute-done((bf16[192,128]{1,0:T(8,128)(2,1)S(1)}, bf16[192,128]{1,0:T(8,128)(2,1)S(1)}, u32[]{:S(2)}, u32[]{:S(2)}) %collective-permute-start.8) | collective-permute-done | bytes 49184 | tf_op jit(solution)/shard_map/ppermute | solution.py:55
  41.2 1.3 %collective-permute-done.9 = bf16[2,192,128]{2,1,0:T(8,128)(2,1)S(1)} collective-permute-done((bf16[2,192,128]{2,1,0:T(8,128)(2,1)S(1)}, bf16[2,192,128]{2,1,0:T(8,128)(2,1)S(1)}, u32[]{:S(2)}, u32[]{:S(2)}) %collective-permute-start.9) | collective-permute-done | bytes 98336 | tf_op jit(solution)/shard_map/ppermute | solution.py:55
  42.5 1.3 %collective-permute-start.10 = (bf16[2,2,192,128]{3,2,1,0:T(8,128)(2,1)S(1)}, bf16[2,2,192,128]{3,2,1,0:T(8,128)(2,1)}, u32[]{:S(2)}, u32[]{:S(2)}) collective-permute-start(bf16[2,2,192,128]{3,2,1,0:T(8,128)(2,1)S(1)} %maximum_select_fusion.1.refs_2_), channel_id=1, source_target_pairs={{2,3},{3,2},{6,7},{7,6},{10,11},{11,10},{14,15},{15,14},{18,19},{1... | collective-permute-start | bytes 589832 | tf_op jit(solution)/shard_map/ppermute | solution.py:67
  43.8 1.6 %collective-permute-start.7 = (f32[192,128]{1,0:T(8,128)S(1)}, f32[192,128]{1,0:T(8,128)S(1)}, u32[]{:S(2)}, u32[]{:S(2)}) collective-permute-start(f32[192,128]{1,0:T(8,128)S(1)} %get-tuple-element.5), channel_id=1, source_target_pairs={{0,1},{1,0},{2,3},{3,2},{4,5},{5,4},{6,7},{7,6},{8,9},{9,8},{10,11... | collective-permute-start | bytes 294920 | tf_op jit(solution)/shard_map/ppermute | solution.py:55
  45.5 1.4 %collective-permute-start.12 = (bf16[2,2,192,128]{3,2,1,0:T(8,128)(2,1)S(1)}, bf16[2,2,192,128]{3,2,1,0:T(8,128)(2,1)S(1)}, u32[]{:S(2)}, u32[]{:S(2)}) collective-permute-start(bf16[2,2,192,128]{3,2,1,0:T(8,128)(2,1)S(1)} %maximum_select_fusion.1.refs_2_), channel_id=1, source_target_pairs={{0,5},{1,4},{2,6},{3,7},{4,1},{5,0},{6,2},{7,3},{8,13},{9,12},{10,... | collective-permute-start | bytes 589832 | tf_op jit(solution)/shard_map/ppermute | solution.py:67
  46.9 1.1 %collective-permute-start.13 = (bf16[2,2,192,128]{3,2,1,0:T(8,128)(2,1)S(1)}, bf16[2,2,192,128]{3,2,1,0:T(8,128)(2,1)S(1)}, u32[]{:S(2)}, u32[]{:S(2)}) collective-permute-start(bf16[2,2,192,128]{3,2,1,0:T(8,128)(2,1)S(1)} %maximum_select_fusion.1.refs_2_), channel_id=1, source_target_pairs={{0,9},{1,8},{2,10},{3,11},{4,13},{5,12},{6,14},{7,15},{8,1},{9,0},... | collective-permute-start | bytes 589832 | tf_op jit(solution)/shard_map/ppermute | solution.py:67
  48.0 1.9 %collective-permute-start.14 = (bf16[2,2,192,128]{3,2,1,0:T(8,128)(2,1)S(1)}, bf16[2,2,192,128]{3,2,1,0:T(8,128)(2,1)S(1)}, u32[]{:S(2)}, u32[]{:S(2)}) collective-permute-start(bf16[2,2,192,128]{3,2,1,0:T(8,128)(2,1)S(1)} %maximum_select_fusion.1.refs_2_), channel_id=1, source_target_pairs={{0,12},{1,13},{2,15},{3,14},{4,8},{5,9},{6,11},{7,10},{8,4},{9,5},... | collective-permute-start | bytes 589832 | tf_op jit(solution)/shard_map/ppermute | solution.py:67
  49.9 0.9 %collective-permute-start.11 = (bf16[2,2,192,128]{3,2,1,0:T(8,128)(2,1)}, bf16[2,2,192,128]{3,2,1,0:T(8,128)(2,1)S(1)}, u32[]{:S(2)}, u32[]{:S(2)}) collective-permute-start(bf16[2,2,192,128]{3,2,1,0:T(8,128)(2,1)} %collective-permute-done.10), channel_id=1, source_target_pairs={{0,2},{2,0},{1,3},{3,1},{4,6},{6,4},{5,7},{7,5},{8,10},{10,8},{9,1... | collective-permute-start | bytes 589832 | tf_op jit(solution)/shard_map/ppermute | solution.py:55
  50.8 2.0 %multiply_subtract_fusion = (f32[384,128]{1,0:T(8,128)}, f32[384,128]{1,0:T(8,128)}, f32[384,128]{1,0:T(8,128)}) fusion(f32[384,128]{1,0:T(8,128)} %param.8, f32[]{:T(128)} %bitcast.18, f32[]{:T(128)} %bitcast.17, f32[192,128]{1,0:T(8,128)S(1)} %get-tuple-element.5, f32[192,128]{1,0:T(8,128)S(1)} %collective-permute-done.7, pred[]{:T(512)S(6)} %eq.6, ...), kind=kLoop, calls=%fused_computation.20 | loop fusion | flops 884736 | bytes 1376265 | tf_op jit(solution)/shard_map/sub | solution.py:25
  52.8 1.4 %collective-permute-done.12.refs_4_ = bf16[2,2,192,128]{3,2,1,0:T(8,128)(2,1)S(1)} collective-permute-done((bf16[2,2,192,128]{3,2,1,0:T(8,128)(2,1)S(1)}, bf16[2,2,192,128]{3,2,1,0:T(8,128)(2,1)S(1)}, u32[]{:S(2)}, u32[]{:S(2)}) %collective-permute-start.12) | collective-permute-done | bytes 196640 | tf_op jit(solution)/shard_map/ppermute | solution.py:67
  54.2 4.7 %collective-permute-start.15 = (bf16[2,2,192,128]{3,2,1,0:T(8,128)(2,1)S(1)}, bf16[2,2,192,128]{3,2,1,0:T(8,128)(2,1)S(1)}, u32[]{:S(2)}, u32[]{:S(2)}) collective-permute-start(bf16[2,2,192,128]{3,2,1,0:T(8,128)(2,1)S(1)} %collective-permute-done.12.refs_4_), channel_id=1, source_target_pairs={{0,2},{2,0},{1,3},{3,1},{4,6},{6,4},{5,7},{7,5},{8,10},{10,8},{9,1... | collective-permute-start | bytes 589832 | tf_op jit(solution)/shard_map/ppermute | solution.py:55
  60.6 2.2 %shard_map.93 = bf16[256,128]{1,0:T(8,128)(2,1)} custom-call(s32[4]{0:T(128)S(1)} %pad_add_fusion.refs_0_, bf16[256,6144]{1,0:T(8,128)(2,1)S(1)} %copy-done.1, bf16[2,2,192,128]{3,2,1,0:T(8,128)(2,1)S(1)} %maximum_select_fusion.1.refs_2_, bf16[2,2,192,128]{3,2,1,0:T(8,128)(2,1)S(1)} %broadcast_select_fusion.refs_3_, ...), custom_call_target="tpu_custom_call" | custom-call | tf_op jit(solution)/shard_map/pallas_call | solution.py:134
  (34 shorter events, 5.9 us)
Async XLA Ops:
  0.6 0.8 %copy-start = (bf16[256,128]{1,0:T(8,128)(2,1)S(1)}, bf16[256,128]{1,0:T(8,128)(2,1)}, u32[]{:S(2)}) copy-start(bf16[256,128]{1,0:T(8,128)(2,1)} %param.7) | copy-start | bytes 196612
  4.6 2.4 %collective-permute-start = (bf16[4,2,2,192,128]{4,3,2,1,0:T(8,128)(2,1)S(1)}, bf16[4,2,2,192,128]{4,3,2,1,0:T(8,128)(2,1)S(1)}, u32[]{:S(2)}, u32[]{:S(2)}) collective-permute-start(bf16[4,2,2,192,128]{4,3,2,1,0:T(8,128)(2,1)S(1)} %pad_maximum_fusion), channel_id=1, source_target_pairs={{0,2},{2,0},{1,3},{3,1},{4,6},{6,4},{5,7},{7,5},{8,10},{10,8},{9,1... | collective-permute-start | bytes 2359304 | tf_op jit(solution)/shard_map/ppermute | solution.py:55
  7.4 6.1 %collective-permute-start.1 = (bf16[2,2,192,128]{3,2,1,0:T(8,128)(2,1)S(1)}, bf16[2,2,192,128]{3,2,1,0:T(8,128)(2,1)S(1)}, u32[]{:S(2)}, u32[]{:S(2)}) collective-permute-start(bf16[2,2,192,128]{3,2,1,0:T(8,128)(2,1)S(1)} %get-tuple-element.9), channel_id=1, source_target_pairs={{2,3},{3,2},{6,7},{7,6},{10,11},{11,10},{14,15},{15,14},{18,19},{1... | collective-permute-start | bytes 589832 | tf_op jit(solution)/shard_map/ppermute | solution.py:67
  8.1 8.8 %collective-permute-start.2 = (bf16[2,2,192,128]{3,2,1,0:T(8,128)(2,1)S(1)}, bf16[2,2,192,128]{3,2,1,0:T(8,128)(2,1)S(1)}, u32[]{:S(2)}, u32[]{:S(2)}) collective-permute-start(bf16[2,2,192,128]{3,2,1,0:T(8,128)(2,1)S(1)} %get-tuple-element.12), channel_id=1, source_target_pairs={{0,5},{1,4},{2,6},{3,7},{4,1},{5,0},{6,2},{7,3},{8,13},{9,12},{10,... | collective-permute-start | bytes 589832 | tf_op jit(solution)/shard_map/ppermute | solution.py:67
  12.0 8.6 %collective-permute-start.3 = (bf16[2,2,192,128]{3,2,1,0:T(8,128)(2,1)S(1)}, bf16[2,2,192,128]{3,2,1,0:T(8,128)(2,1)S(1)}, u32[]{:S(2)}, u32[]{:S(2)}) collective-permute-start(bf16[2,2,192,128]{3,2,1,0:T(8,128)(2,1)S(1)} %get-tuple-element.11), channel_id=1, source_target_pairs={{0,9},{1,8},{2,10},{3,11},{4,13},{5,12},{6,14},{7,15},{8,1},{9,0},... | collective-permute-start | bytes 589832 | tf_op jit(solution)/shard_map/ppermute | solution.py:67
  13.5 9.2 %collective-permute-start.4 = (bf16[2,2,192,128]{3,2,1,0:T(8,128)(2,1)S(1)}, bf16[2,2,192,128]{3,2,1,0:T(8,128)(2,1)S(1)}, u32[]{:S(2)}, u32[]{:S(2)}) collective-permute-start(bf16[2,2,192,128]{3,2,1,0:T(8,128)(2,1)S(1)} %get-tuple-element.10), channel_id=1, source_target_pairs={{0,12},{1,13},{2,15},{3,14},{4,8},{5,9},{6,11},{7,10},{8,4},{9,5},... | collective-permute-start | bytes 589832 | tf_op jit(solution)/shard_map/ppermute | solution.py:67
  22.8 1.7 %collective-permute-start.5 = (f32[2,192,128]{2,1,0:T(8,128)S(1)}, f32[2,192,128]{2,1,0:T(8,128)S(1)}, u32[]{:S(2)}, u32[]{:S(2)}) collective-permute-start(f32[2,192,128]{2,1,0:T(8,128)S(1)} %dynamic-slice_bitcast_fusion), channel_id=1, source_target_pairs={{0,2},{2,0},{1,3},{3,1},{4,6},{6,4},{5,7},{7,5},{8,10},{10,8},{9,1... | collective-permute-start | bytes 589832 | tf_op jit(solution)/shard_map/ppermute | solution.py:55
  24.6 8.5 %collective-permute-start.6 = (f32[192,128]{1,0:T(8,128)S(1)}, f32[192,128]{1,0:T(8,128)S(1)}, u32[]{:S(2)}, u32[]{:S(2)}) collective-permute-start(f32[192,128]{1,0:T(8,128)S(1)} %dynamic-slice_bitcast_fusion.5), channel_id=1, source_target_pairs={{0,16},{16,0},{1,17},{17,1},{2,18},{18,2},{3,19},{19,3},{4,20},{20... | collective-permute-start | bytes 294920 | tf_op jit(solution)/shard_map/ppermute | solution.py:55
  33.1 0.6 %copy-start.2 = (f32[192,128]{1,0:T(8,128)}, f32[192,128]{1,0:T(8,128)S(1)}, u32[]{:S(2)}) copy-start(f32[192,128]{1,0:T(8,128)S(1)} %collective-permute-done.6) | copy-start | bytes 294916
  33.7 26.9 %copy-start.1 = (bf16[256,6144]{1,0:T(8,128)(2,1)S(1)}, bf16[256,6144]{1,0:T(8,128)(2,1)}, u32[]{:S(2)}) copy-start(bf16[256,6144]{1,0:T(8,128)(2,1)} %refs_1_.1) | copy-start | bytes 9437188
  35.0 6.1 %collective-permute-start.8 = (bf16[192,128]{1,0:T(8,128)(2,1)S(1)}, bf16[192,128]{1,0:T(8,128)(2,1)S(1)}, u32[]{:S(2)}, u32[]{:S(2)}) collective-permute-start(bf16[192,128]{1,0:T(8,128)(2,1)S(1)} %get-tuple-element.4), channel_id=1, source_target_pairs={{0,16},{16,0},{1,17},{17,1},{2,18},{18,2},{3,19},{19,3},{4,20},{20... | collective-permute-start | bytes 147464 | tf_op jit(solution)/shard_map/ppermute | solution.py:55
  41.1 1.4 %collective-permute-start.9 = (bf16[2,192,128]{2,1,0:T(8,128)(2,1)S(1)}, bf16[2,192,128]{2,1,0:T(8,128)(2,1)S(1)}, u32[]{:S(2)}, u32[]{:S(2)}) collective-permute-start(bf16[2,192,128]{2,1,0:T(8,128)(2,1)S(1)} %get-tuple-element.18), channel_id=1, source_target_pairs={{0,2},{2,0},{1,3},{3,1},{4,6},{6,4},{5,7},{7,5},{8,10},{10,8},{9,1... | collective-permute-start | bytes 294920 | tf_op jit(solution)/shard_map/ppermute | solution.py:55
  42.5 7.4 %collective-permute-start.10 = (bf16[2,2,192,128]{3,2,1,0:T(8,128)(2,1)S(1)}, bf16[2,2,192,128]{3,2,1,0:T(8,128)(2,1)}, u32[]{:S(2)}, u32[]{:S(2)}) collective-permute-start(bf16[2,2,192,128]{3,2,1,0:T(8,128)(2,1)S(1)} %maximum_select_fusion.1.refs_2_), channel_id=1, source_target_pairs={{2,3},{3,2},{6,7},{7,6},{10,11},{11,10},{14,15},{15,14},{18,19},{1... | collective-permute-start | bytes 589832 | tf_op jit(solution)/shard_map/ppermute | solution.py:67
  43.8 6.9 %collective-permute-start.7 = (f32[192,128]{1,0:T(8,128)S(1)}, f32[192,128]{1,0:T(8,128)S(1)}, u32[]{:S(2)}, u32[]{:S(2)}) collective-permute-start(f32[192,128]{1,0:T(8,128)S(1)} %get-tuple-element.5), channel_id=1, source_target_pairs={{0,1},{1,0},{2,3},{3,2},{4,5},{5,4},{6,7},{7,6},{8,9},{9,8},{10,11... | collective-permute-start | bytes 294920 | tf_op jit(solution)/shard_map/ppermute | solution.py:55
  45.5 8.7 %collective-permute-start.12 = (bf16[2,2,192,128]{3,2,1,0:T(8,128)(2,1)S(1)}, bf16[2,2,192,128]{3,2,1,0:T(8,128)(2,1)S(1)}, u32[]{:S(2)}, u32[]{:S(2)}) collective-permute-start(bf16[2,2,192,128]{3,2,1,0:T(8,128)(2,1)S(1)} %maximum_select_fusion.1.refs_2_), channel_id=1, source_target_pairs={{0,5},{1,4},{2,6},{3,7},{4,1},{5,0},{6,2},{7,3},{8,13},{9,12},{10,... | collective-permute-start | bytes 589832 | tf_op jit(solution)/shard_map/ppermute | solution.py:67
  46.9 12.0 %collective-permute-start.13 = (bf16[2,2,192,128]{3,2,1,0:T(8,128)(2,1)S(1)}, bf16[2,2,192,128]{3,2,1,0:T(8,128)(2,1)S(1)}, u32[]{:S(2)}, u32[]{:S(2)}) collective-permute-start(bf16[2,2,192,128]{3,2,1,0:T(8,128)(2,1)S(1)} %maximum_select_fusion.1.refs_2_), channel_id=1, source_target_pairs={{0,9},{1,8},{2,10},{3,11},{4,13},{5,12},{6,14},{7,15},{8,1},{9,0},... | collective-permute-start | bytes 589832 | tf_op jit(solution)/shard_map/ppermute | solution.py:67
  48.0 10.9 %collective-permute-start.14 = (bf16[2,2,192,128]{3,2,1,0:T(8,128)(2,1)S(1)}, bf16[2,2,192,128]{3,2,1,0:T(8,128)(2,1)S(1)}, u32[]{:S(2)}, u32[]{:S(2)}) collective-permute-start(bf16[2,2,192,128]{3,2,1,0:T(8,128)(2,1)S(1)} %maximum_select_fusion.1.refs_2_), channel_id=1, source_target_pairs={{0,12},{1,13},{2,15},{3,14},{4,8},{5,9},{6,11},{7,10},{8,4},{9,5},... | collective-permute-start | bytes 589832 | tf_op jit(solution)/shard_map/ppermute | solution.py:67
  49.9 9.5 %collective-permute-start.11 = (bf16[2,2,192,128]{3,2,1,0:T(8,128)(2,1)}, bf16[2,2,192,128]{3,2,1,0:T(8,128)(2,1)S(1)}, u32[]{:S(2)}, u32[]{:S(2)}) collective-permute-start(bf16[2,2,192,128]{3,2,1,0:T(8,128)(2,1)} %collective-permute-done.10), channel_id=1, source_target_pairs={{0,2},{2,0},{1,3},{3,1},{4,6},{6,4},{5,7},{7,5},{8,10},{10,8},{9,1... | collective-permute-start | bytes 589832 | tf_op jit(solution)/shard_map/ppermute | solution.py:55
  54.2 5.7 %collective-permute-start.15 = (bf16[2,2,192,128]{3,2,1,0:T(8,128)(2,1)S(1)}, bf16[2,2,192,128]{3,2,1,0:T(8,128)(2,1)S(1)}, u32[]{:S(2)}, u32[]{:S(2)}) collective-permute-start(bf16[2,2,192,128]{3,2,1,0:T(8,128)(2,1)S(1)} %collective-permute-done.12.refs_4_), channel_id=1, source_target_pairs={{0,2},{2,0},{1,3},{3,1},{4,6},{6,4},{5,7},{7,5},{8,10},{10,8},{9,1... | collective-permute-start | bytes 589832 | tf_op jit(solution)/shard_map/ppermute | solution.py:55
  58.9 1.4 %collective-permute-start.16 = (bf16[2,2,192,128]{3,2,1,0:T(8,128)(2,1)S(1)}, bf16[2,2,192,128]{3,2,1,0:T(8,128)(2,1)S(1)}, u32[]{:S(2)}, u32[]{:S(2)}) collective-permute-start(bf16[2,2,192,128]{3,2,1,0:T(8,128)(2,1)S(1)} %collective-permute-done.13.refs_5_), channel_id=1, source_target_pairs={{0,2},{2,0},{1,3},{3,1},{4,6},{6,4},{5,7},{7,5},{8,10},{10,8},{9,1... | collective-permute-start | bytes 589832 | tf_op jit(solution)/shard_map/ppermute | solution.py:55
  58.9 1.6 %collective-permute-start.17 = (bf16[2,2,192,128]{3,2,1,0:T(8,128)(2,1)S(1)}, bf16[2,2,192,128]{3,2,1,0:T(8,128)(2,1)S(1)}, u32[]{:S(2)}, u32[]{:S(2)}) collective-permute-start(bf16[2,2,192,128]{3,2,1,0:T(8,128)(2,1)S(1)} %collective-permute-done.14.refs_6_), channel_id=1, source_target_pairs={{0,2},{2,0},{1,3},{3,1},{4,6},{6,4},{5,7},{7,5},{8,10},{10,8},{9,1... | collective-permute-start | bytes 589832 | tf_op jit(solution)/shard_map/ppermute | solution.py:55

commit v4 on v3

v4 whole, which is shorter than its diff:
```python
import jax
import jax.numpy as jnp
from jax import lax
from jax.experimental import pallas as pl
from jax.experimental.pallas import tpu as pltpu
from jax.sharding import Mesh
from jax.sharding import PartitionSpec as P

AXES = ("high", "low", "core", "rep")
N_LOW = 4
ORDER = (((0, 1), (1, 0), (2, 0)), ((1, 0), (2, 0), (0, 1)))
STEPS = [(a, b, c) for a in range(2) for b in range(2) for c in range(2)]


def change(core, taken):
    low = rep = 0
    for step, one in zip(ORDER[core], taken):
        if one:
            low, rep = low ^ step[0], rep ^ step[1]
    return low, rep


def change_here(core, taken):
    (low0, rep0), (low1, rep1) = change(0, taken), change(1, taken)
    return low0 + core * (low1 - low0), rep0 + core * (rep1 - rep0)


def adamw(grad, master, moment_one, moment_two, step_count):
    count = step_count[0].astype(jnp.float32)
    beta_one = 0.9
    beta_two = 0.95
    first = beta_one * moment_one + (1.0 - beta_one) * grad
    second = beta_two * moment_two + (1.0 - beta_two) * grad * grad
    first_hat = first / (1.0 - jnp.power(beta_one, count))
    second_hat = second / (1.0 - jnp.power(beta_two, count))
    updated = master - 0.01 * (first_hat / (jnp.sqrt(second_hat) + 1e-08) + 0.1 * master)
    return updated, first, second


def block_row(where, taken, of_core, j):
    high, low, core, rep = where
    owner = core ^ of_core
    d_low, d_rep = change_here(owner, taken)
    return (((high ^ j) * N_LOW + (low ^ d_low)) * 2 + owner) * 2 + (rep ^ d_rep)


def logits_kernel(half, chips, where_ref, acts_ref, *refs):
    pieces, out_ref, weight = refs[:-2], refs[-2], refs[-1]
    where = [where_ref[i] for i in range(4)]
    for piece, (of_core, reached) in zip(pieces, chips):
        for i, taken in enumerate(reached):
            for j in range(piece.shape[1]):
                row = pl.multiple_of(block_row(where, taken, of_core, j) * half, half)
                weight[pl.ds(row, half), :] = piece[i, j]
    out_ref[...] = jnp.dot(
        acts_ref[...], weight[...], preferred_element_type=jnp.float32
    ).astype(out_ref.dtype)


def solution(mesh):
    n_seq, n_rep = mesh.shape["seq"], mesh.shape["rep"]
    n_high = n_seq // (2 * N_LOW)
    fine = Mesh(mesh.devices.reshape(n_high, N_LOW, 2, n_rep), AXES)

    def swap(x, axis, mask=1):
        return lax.ppermute(x, axis, [(i, i ^ mask) for i in range(fine.shape[axis])])

    def step_swap(x, step):
        pairs = []
        for low in range(N_LOW):
            for core in range(2):
                d_low, d_rep = ORDER[core][step]
                for rep in range(n_rep):
                    there = ((low ^ d_low) * 2 + core) * n_rep + (rep ^ d_rep)
                    pairs.append(((low * 2 + core) * n_rep + rep, there))
        return lax.ppermute(x, AXES[1:], pairs)

    def per_device(acts, grad_logits, master, moment_one, moment_two, step_count):
        rows, experts = master.shape
        half = rows // n_rep
        where = high, low, core, rep = tuple(lax.axis_index(a) for a in AXES)
        f32, bf16 = jnp.float32, jnp.bfloat16

        product = lax.dot_general(
            acts, grad_logits, (((0,), (0,)), ((), ())), preferred_element_type=f32
        ).astype(bf16)
        product = product.reshape(n_high, N_LOW, 2, n_rep, half, experts)

        def blocks(owner, taken):
            d_low, d_rep = change_here(owner, taken)
            at = (0, low ^ d_low, owner, rep ^ d_rep, 0, 0)
            block = lax.dynamic_slice(product, at, (n_high, 1, 1, 1, half, experts))
            return block.reshape(n_high, half, experts)

        parts = []
        for a in (1, 0):
            away = jnp.stack([blocks(1 - core, taken) for taken in STEPS if taken[0] == a])
            kept = jnp.stack([blocks(core, taken) for taken in STEPS if taken[0] == a])
            parts.append(kept.astype(f32) + swap(away, "core").astype(f32))
        total = parts[1] + step_swap(parts[0].astype(bf16), 0).astype(f32)
        total = total[:2] + step_swap(total[2:].astype(bf16), 1).astype(f32)
        total = total[0] + step_swap(total[1], 2)

        grad = None
        for j in range(n_high):
            part = lax.dynamic_index_in_dim(total, high ^ j, 0, keepdims=False)
            if j:
                part = swap(part, "high", j)
            grad = part if grad is None else grad + part

        mine = [
            lax.dynamic_slice_in_dim(a, rep * half, half, 0)
            for a in (master, moment_one, moment_two)
        ]
        weight = adamw(grad, *mine, step_count)[0].astype(bf16)

        column = jnp.stack([swap(weight, "high", j) if j else weight for j in range(n_high)])
        other = swap(grad, "rep")
        column, other = lax.optimization_barrier((column, other))
        whole = jnp.where(
            rep == 0,
            jnp.concatenate([grad, other], 0),
            jnp.concatenate([other, grad], 0),
        )
        state = adamw(whole, master, moment_one, moment_two, step_count)

        near = column[None]
        near = jnp.concatenate([near, step_swap(near, 2)])
        near = jnp.concatenate([near, step_swap(near, 1)])
        far = step_swap(near, 0)
        near_over = swap(near, "core")
        far, state = lax.optimization_barrier((far, state))
        far_over = swap(far, "core")
        pieces = [near, far, near_over, far_over]
        near_taken, far_taken = STEPS[:4], STEPS[4:]
        chips = [(0, near_taken), (0, far_taken), (1, near_taken), (1, far_taken)]
        if half % 16 == 0:
            vmem = pl.BlockSpec(memory_space=pltpu.VMEM)
            logits = pl.pallas_call(
                lambda *refs: logits_kernel(half, chips, *refs),
                out_shape=jax.ShapeDtypeStruct((acts.shape[0], experts), bf16),
                in_specs=[pl.BlockSpec(memory_space=pltpu.SMEM)] + [vmem] * (1 + len(pieces)),
                out_specs=vmem,
                scratch_shapes=[pltpu.VMEM((n_seq * rows, experts), bf16)],
                compiler_params=pltpu.CompilerParams(vmem_limit_bytes=32 * 2**20),
            )(jnp.stack(where), acts, *pieces)
        else:
            places = [
                block_row(where, taken, of_core, j)
                for of_core, reached in chips
                for taken in reached
                for j in range(n_high)
            ]
            received = jnp.concatenate(pieces).reshape(-1, half, experts)
            full = jnp.zeros_like(received).at[jnp.stack(places)].set(received)
            full = full.reshape(n_seq * rows, experts)
            logits = jnp.dot(acts, full, preferred_element_type=f32).astype(bf16)
        return *state, logits

    rows_of, tokens = P(AXES[:3], None), P(AXES, None)
    return jax.shard_map(
        per_device,
        mesh=fine,
        in_specs=(tokens, tokens, rows_of, rows_of, rows_of, P()),
        out_specs=(rows_of, rows_of, rows_of, tokens),
        check_vma=False,
    )
```

time: 63.1 us -> 72.1 us (1.14)
  waiting for transfers between devices: 25.8 us -> 34.8 us
  starting transfers between devices: 24.7 us -> 20.9 us
  local copies, waits for them, and re-layouts: 1.55 us -> 3.15 us
  other arithmetic: 4.05 us -> 5.48 us
    ppermute x8 -> x6, waiting for transfers between devices: 10.6 us -> 26.7 us  [step_swap(): return lax.ppermute(x, AXES[1:], pairs)]
    ppermute x10 -> x7, waiting for transfers between devices: 15.3 us -> 8.16 us  [swap(): lax.ppermute(x, axis, [(i, i ^ mask) for i in range(fine.shape[axis])])]
    ppermute x10 -> x7, starting transfers between devices: 12.9 us -> 8.33 us  [swap(): lax.ppermute(x, axis, [(i, i ^ mask) for i in range(fine.shape[axis])])]
    add x2 -> x3, other arithmetic: 0.14 us -> 1.22 us  [the longest x1 1.04 us: per_device(): total = total[0] + step_swap(total[1], 2)]
    concatenate x0 -> x2, other arithmetic: none -> 0.81 us  [the longest x1 0.79 us: per_device(): near = jnp.concatenate([near, step_swap(near, 1)])]
    ppermute x8 -> x6, starting transfers between devices: 11.8 us -> 12.6 us  [step_swap(): return lax.ppermute(x, AXES[1:], pairs)]
    unnamed x6 -> x8, local copies, waits for them, and re-layouts: 1.44 us -> 2.12 us
    convert_element_type x3 -> x2, other arithmetic: 1.67 us -> 1.25 us  [the longest x1 1.13 us: per_device(): weight = adamw(grad, *mine, step_count)[0].astype(bf16)]
  transfers between devices with their start and end apart: 18 -> 13, of which waited for: 12 -> 11; matrix products, arithmetic and copies ran while one was open for 3% -> 3% of each run, Pallas kernels for 0% -> 0%
where the time goes in v4:
time: 72.1 us; the launch traced here: 71.8 us
  waiting for transfers between devices  34.8 us (48%)
  starting transfers between devices  20.9 us (29%)
  other arithmetic  5.48 us (8%)
  local copies, waits for them, and re-layouts  3.15 us (4%)
  matrix products  2.93 us (4%)
  Pallas kernels  2.83 us (4%)
  between operations  1.59 us (2%)
    ppermute x6, waiting for transfers between devices, step_swap(): return lax.ppermute(x, AXES[1:], pairs)  26.7 us
    ppermute x6, starting transfers between devices, step_swap(): return lax.ppermute(x, AXES[1:], pairs)  12.6 us
    ppermute x7, starting transfers between devices, swap(): lax.ppermute(x, axis, [(i, i ^ mask) for i in range(fine.shape[axis])])  8.33 us
    ppermute x7, waiting for transfers between devices, swap(): lax.ppermute(x, axis, [(i, i ^ mask) for i in range(fine.shape[axis])])  8.16 us
    dot_general x1, matrix products, per_device(): lax.dot_general(acts, grad_logits, (((0,), (0,)), ((), ())), preferred_el...  2.93 us
    pallas_call x1, Pallas kernels, per_device(): pl.pallas_call(lambda *refs: logits_kernel(half, chips, *refs), out_shape...  2.83 us
    unnamed x8, local copies, waits for them, and re-layouts  2.12 us
    sub x1, other arithmetic, adamw(): master - 0.01 * (first_hat / (jnp.sqrt(second_hat) + 1e-08) + 0.1 * master)  2 us
  transfers between devices with their start and end apart: 13, of which 11 were waited for; matrix products, arithmetic and copies ran while one was open for 3% of the time, Pallas kernels for 0%

profile of v4, /device:TPU:0, one launch (start us, length us, event | category | flops | bytes accessed | tf_op | source)
XLA Modules:
  0.0 71.8 jit_solution(10867706361237735892)
XLA Ops:
  1.5 2.9 %convolution_convert_fusion = bf16[6144,128]{1,0:T(8,128)(2,1)S(1)} fusion(bf16[256,6144]{1,0:T(8,128)(2,1)} %refs_1_.1, bf16[256,128]{1,0:T(8,128)(2,1)S(1)} %copy-done), kind=kOutput, calls=%fused_computation | convolution fusion | flops 403439616 | bytes 4784128 | tf_op jit(solution)/shard_map/dot_general | solution.py:84
  5.5 1.2 %collective-permute-done.1 = bf16[4,2,192,128]{3,2,1,0:T(8,128)(2,1)S(1)} collective-permute-done((bf16[4,2,192,128]{3,2,1,0:T(8,128)(2,1)S(1)}, bf16[4,2,192,128]{3,2,1,0:T(8,128)(2,1)S(1)}, u32[]{:S(2)}, u32[]{:S(2)}) %collective-permute-start.1) | collective-permute-done | bytes 393248 | tf_op jit(solution)/shard_map/ppermute | solution.py:66
  6.8 3.0 %collective-permute-start.2 = (bf16[4,2,192,128]{3,2,1,0:T(8,128)(2,1)S(1)}, bf16[4,2,192,128]{3,2,1,0:T(8,128)(2,1)S(1)}, u32[]{:S(2)}, u32[]{:S(2)}) collective-permute-start(bf16[4,2,192,128]{3,2,1,0:T(8,128)(2,1)S(1)} %add_convert_fusion), channel_id=1, source_target_pairs={{0,1},{1,0},{2,6},{3,7},{4,5},{5,4},{6,2},{7,3},{8,9},{9,8},{10,14... | collective-permute-start | bytes 1179656 | tf_op jit(solution)/shard_map/ppermute | solution.py:76
  9.8 5.7 %collective-permute-done.2 = bf16[4,2,192,128]{3,2,1,0:T(8,128)(2,1)S(1)} collective-permute-done((bf16[4,2,192,128]{3,2,1,0:T(8,128)(2,1)S(1)}, bf16[4,2,192,128]{3,2,1,0:T(8,128)(2,1)S(1)}, u32[]{:S(2)}, u32[]{:S(2)}) %collective-permute-start.2) | collective-permute-done | bytes 393248 | tf_op jit(solution)/shard_map/ppermute | solution.py:76
  15.7 2.0 %collective-permute-start.3 = (bf16[2,2,192,128]{3,2,1,0:T(8,128)(2,1)S(1)}, bf16[2,2,192,128]{3,2,1,0:T(8,128)(2,1)S(1)}, u32[]{:S(2)}, u32[]{:S(2)}) collective-permute-start(bf16[2,2,192,128]{3,2,1,0:T(8,128)(2,1)S(1)} %slice.27), channel_id=1, source_target_pairs={{0,4},{1,5},{2,10},{3,11},{4,0},{5,1},{6,14},{7,15},{8,12},{9,13},... | collective-permute-start | bytes 589832 | tf_op jit(solution)/shard_map/ppermute | solution.py:76
  17.7 3.7 %collective-permute-done.3 = bf16[2,2,192,128]{3,2,1,0:T(8,128)(2,1)S(1)} collective-permute-done((bf16[2,2,192,128]{3,2,1,0:T(8,128)(2,1)S(1)}, bf16[2,2,192,128]{3,2,1,0:T(8,128)(2,1)S(1)}, u32[]{:S(2)}, u32[]{:S(2)}) %collective-permute-start.3) | collective-permute-done | bytes 196640 | tf_op jit(solution)/shard_map/ppermute | solution.py:76
  22.3 2.1 %collective-permute-start.4 = (f32[2,192,128]{2,1,0:T(8,128)S(1)}, f32[2,192,128]{2,1,0:T(8,128)}, u32[]{:S(2)}, u32[]{:S(2)}) collective-permute-start(f32[2,192,128]{2,1,0:T(8,128)S(1)} %slice_bitcast_fusion), channel_id=1, source_target_pairs={{0,8},{1,9},{2,3},{3,2},{4,12},{5,13},{6,7},{7,6},{8,0},{9,1},{10,... | collective-permute-start | bytes 589832 | tf_op jit(solution)/shard_map/ppermute | solution.py:76
  24.4 3.8 %collective-permute-done.4 = f32[2,192,128]{2,1,0:T(8,128)} collective-permute-done((f32[2,192,128]{2,1,0:T(8,128)S(1)}, f32[2,192,128]{2,1,0:T(8,128)}, u32[]{:S(2)}, u32[]{:S(2)}) %collective-permute-start.4) | collective-permute-done | bytes 196640 | tf_op jit(solution)/shard_map/ppermute | solution.py:76
  28.1 1.0 %fusion.1 = f32[2,192,128]{2,1,0:T(8,128)S(1)} fusion(f32[2,192,128]{2,1,0:T(8,128)} %collective-permute-done.4, f32[2,2,192,128]{3,2,1,0:T(8,128)} %copy-done.2), kind=kLoop, calls=%fused_computation.12 | loop fusion | flops 49152 | bytes 589824 | tf_op jit(solution)/shard_map/add | solution.py:102
  29.8 3.0 %collective-permute-start.5 = (f32[192,128]{1,0:T(8,128)}, f32[192,128]{1,0:T(8,128)S(1)}, u32[]{:S(2)}, u32[]{:S(2)}) collective-permute-start(f32[192,128]{1,0:T(8,128)} %dynamic-slice_bitcast_fusion), channel_id=1, source_target_pairs={{0,16},{16,0},{1,17},{17,1},{2,18},{18,2},{3,19},{19,3},{4,20},{20... | collective-permute-start | bytes 294920 | tf_op jit(solution)/shard_map/ppermute | solution.py:66
  33.6 2.1 %collective-permute-done.5 = f32[192,128]{1,0:T(8,128)S(1)} collective-permute-done((f32[192,128]{1,0:T(8,128)}, f32[192,128]{1,0:T(8,128)S(1)}, u32[]{:S(2)}, u32[]{:S(2)}) %collective-permute-start.5) | collective-permute-done | bytes 98336 | tf_op jit(solution)/shard_map/ppermute | solution.py:66
  36.3 1.1 %subtract_convert_fusion = (bf16[192,128]{1,0:T(8,128)(2,1)S(1)}, f32[192,128]{1,0:T(8,128)S(1)}) fusion(f32[384,128]{1,0:T(8,128)} %param.8, s32[]{:T(128)S(6)} %select_n.112, f32[384,128]{1,0:T(8,128)} %param.10, f32[384,128]{1,0:T(8,128)} %param.9, f32[]{:T(128)} %bitcast.22, f32[]{:T(128)} %bitcast.21, f32[192,128]{1,0:T(8,128)} %copy-done.3, ...), kind=kLoop, calls=%fused_computation.26 | loop fusion | flops 417792 | bytes 638992 | tf_op jit(solution)/shard_map/convert_element_type | solution.py:115
  37.4 3.1 %collective-permute-start.6 = (bf16[192,128]{1,0:T(8,128)(2,1)S(1)}, bf16[192,128]{1,0:T(8,128)(2,1)S(1)}, u32[]{:S(2)}, u32[]{:S(2)}) collective-permute-start(bf16[192,128]{1,0:T(8,128)(2,1)S(1)} %get-tuple-element.19), channel_id=1, source_target_pairs={{0,16},{16,0},{1,17},{17,1},{2,18},{18,2},{3,19},{19,3},{4,20},{20... | collective-permute-start | bytes 147464 | tf_op jit(solution)/shard_map/ppermute | solution.py:66
  40.5 1.6 %collective-permute-start.7 = (f32[192,128]{1,0:T(8,128)S(1)}, f32[192,128]{1,0:T(8,128)S(1)}, u32[]{:S(2)}, u32[]{:S(2)}) collective-permute-start(f32[192,128]{1,0:T(8,128)S(1)} %get-tuple-element.20), channel_id=1, source_target_pairs={{0,1},{1,0},{2,3},{3,2},{4,5},{5,4},{6,7},{7,6},{8,9},{9,8},{10,11... | collective-permute-start | bytes 294920 | tf_op jit(solution)/shard_map/ppermute | solution.py:66
  42.6 2.5 %collective-permute-done.7 = f32[192,128]{1,0:T(8,128)S(1)} collective-permute-done((f32[192,128]{1,0:T(8,128)S(1)}, f32[192,128]{1,0:T(8,128)S(1)}, u32[]{:S(2)}, u32[]{:S(2)}) %collective-permute-start.7) | collective-permute-done | bytes 98336 | tf_op jit(solution)/shard_map/ppermute | solution.py:66
  45.1 2.4 %collective-permute-start.8 = (bf16[1,2,192,128]{3,2,1,0:T(8,128)(2,1)S(1)}, bf16[1,2,192,128]{3,2,1,0:T(8,128)(2,1)S(1)}, u32[]{:S(2)}, u32[]{:S(2)}) collective-permute-start(bf16[1,2,192,128]{3,2,1,0:T(8,128)(2,1)S(1)} %bitcast.57), channel_id=1, source_target_pairs={{0,8},{1,9},{2,3},{3,2},{4,12},{5,13},{6,7},{7,6},{8,0},{9,1},{10,... | collective-permute-start | bytes 294920 | tf_op jit(solution)/shard_map/ppermute | solution.py:76
  47.6 2.6 %collective-permute-done.8 = bf16[1,2,192,128]{3,2,1,0:T(8,128)(2,1)S(1)} collective-permute-done((bf16[1,2,192,128]{3,2,1,0:T(8,128)(2,1)S(1)}, bf16[1,2,192,128]{3,2,1,0:T(8,128)(2,1)S(1)}, u32[]{:S(2)}, u32[]{:S(2)}) %collective-permute-start.8) | collective-permute-done | bytes 98336 | tf_op jit(solution)/shard_map/ppermute | solution.py:76
  50.2 1.6 %collective-permute-start.9 = (bf16[2,2,192,128]{3,2,1,0:T(8,128)(2,1)S(1)}, bf16[2,2,192,128]{3,2,1,0:T(8,128)(2,1)S(1)}, u32[]{:S(2)}, u32[]{:S(2)}) collective-permute-start(bf16[2,2,192,128]{3,2,1,0:T(8,128)(2,1)S(1)} %pad_maximum_fusion.3), channel_id=1, source_target_pairs={{0,4},{1,5},{2,10},{3,11},{4,0},{5,1},{6,14},{7,15},{8,12},{9,13},... | collective-permute-start | bytes 589832 | tf_op jit(solution)/shard_map/ppermute | solution.py:76
  51.7 6.4 %collective-permute-done.9 = bf16[2,2,192,128]{3,2,1,0:T(8,128)(2,1)S(1)} collective-permute-done((bf16[2,2,192,128]{3,2,1,0:T(8,128)(2,1)S(1)}, bf16[2,2,192,128]{3,2,1,0:T(8,128)(2,1)S(1)}, u32[]{:S(2)}, u32[]{:S(2)}) %collective-permute-start.9) | collective-permute-done | bytes 196640 | tf_op jit(solution)/shard_map/ppermute | solution.py:76
  58.9 1.6 %collective-permute-start.10 = (bf16[4,2,192,128]{3,2,1,0:T(8,128)(2,1)}, bf16[4,2,192,128]{3,2,1,0:T(8,128)(2,1)}, u32[]{:S(2)}, u32[]{:S(2)}) collective-permute-start(bf16[4,2,192,128]{3,2,1,0:T(8,128)(2,1)} %pad_maximum_fusion.2.refs_2_), channel_id=1, source_target_pairs={{0,1},{1,0},{2,6},{3,7},{4,5},{5,4},{6,2},{7,3},{8,9},{9,8},{10,14... | collective-permute-start | bytes 1179656 | tf_op jit(solution)/shard_map/ppermute | solution.py:76
  60.5 2.0 %multiply_subtract_fusion = (f32[384,128]{1,0:T(8,128)}, f32[384,128]{1,0:T(8,128)}, f32[384,128]{1,0:T(8,128)}) fusion(f32[384,128]{1,0:T(8,128)} %param.8, f32[]{:T(128)} %bitcast.22, f32[]{:T(128)} %bitcast.21, f32[192,128]{1,0:T(8,128)S(1)} %get-tuple-element.20, f32[192,128]{1,0:T(8,128)S(1)} %collective-permute-done.7, pred[]{:T(512)S(6)} %eq.3, ...), kind=kLoop, calls=%fused_computation.15 | loop fusion | flops 884736 | bytes 1376265 | tf_op jit(solution)/shard_map/sub | solution.py:36
  62.5 4.5 %collective-permute-done.10.refs_3_ = bf16[4,2,192,128]{3,2,1,0:T(8,128)(2,1)} collective-permute-done((bf16[4,2,192,128]{3,2,1,0:T(8,128)(2,1)}, bf16[4,2,192,128]{3,2,1,0:T(8,128)(2,1)}, u32[]{:S(2)}, u32[]{:S(2)}) %collective-permute-start.10) | collective-permute-done | bytes 393248 | tf_op jit(solution)/shard_map/ppermute | solution.py:76
  67.1 1.9 %collective-permute-done.12.refs_5_ = bf16[4,2,192,128]{3,2,1,0:T(8,128)(2,1)S(1)} collective-permute-done((bf16[4,2,192,128]{3,2,1,0:T(8,128)(2,1)}, bf16[4,2,192,128]{3,2,1,0:T(8,128)(2,1)S(1)}, u32[]{:S(2)}, u32[]{:S(2)}) %collective-permute-start.12) | collective-permute-done | bytes 393248 | tf_op jit(solution)/shard_map/ppermute | solution.py:66
  68.9 2.8 %shard_map.93 = bf16[256,128]{1,0:T(8,128)(2,1)} custom-call(s32[4]{0:T(128)S(1)} %pad_add_fusion.refs_0_, bf16[256,6144]{1,0:T(8,128)(2,1)S(1)} %copy-done.1, bf16[4,2,192,128]{3,2,1,0:T(8,128)(2,1)} %pad_maximum_fusion.2.refs_2_, bf16[4,2,192,128]{3,2,1,0:T(8,128)(2,1)} %collective-permute-done.10.refs_3_, ...), custom_call_target="tpu_custom_call" | custom-call | tf_op jit(solution)/shard_map/pallas_call | solution.py:139
  (29 shorter events, 5.6 us)
Async XLA Ops:
  0.6 0.8 %copy-start = (bf16[256,128]{1,0:T(8,128)(2,1)S(1)}, bf16[256,128]{1,0:T(8,128)(2,1)}, u32[]{:S(2)}) copy-start(bf16[256,128]{1,0:T(8,128)(2,1)} %param.7) | copy-start | bytes 196612
  4.8 1.9 %collective-permute-start.1 = (bf16[4,2,192,128]{3,2,1,0:T(8,128)(2,1)S(1)}, bf16[4,2,192,128]{3,2,1,0:T(8,128)(2,1)S(1)}, u32[]{:S(2)}, u32[]{:S(2)}) collective-permute-start(bf16[4,2,192,128]{3,2,1,0:T(8,128)(2,1)S(1)} %pad_maximum_fusion.1), channel_id=1, source_target_pairs={{0,2},{2,0},{1,3},{3,1},{4,6},{6,4},{5,7},{7,5},{8,10},{10,8},{9,1... | collective-permute-start | bytes 1179656 | tf_op jit(solution)/shard_map/ppermute | solution.py:66
  5.4 4.4 %collective-permute-start = (bf16[4,2,192,128]{3,2,1,0:T(8,128)(2,1)S(1)}, bf16[4,2,192,128]{3,2,1,0:T(8,128)(2,1)S(1)}, u32[]{:S(2)}, u32[]{:S(2)}) collective-permute-start(bf16[4,2,192,128]{3,2,1,0:T(8,128)(2,1)S(1)} %pad_maximum_fusion), channel_id=1, source_target_pairs={{0,2},{2,0},{1,3},{3,1},{4,6},{6,4},{5,7},{7,5},{8,10},{10,8},{9,1... | collective-permute-start | bytes 1179656 | tf_op jit(solution)/shard_map/ppermute | solution.py:66
  6.8 8.7 %collective-permute-start.2 = (bf16[4,2,192,128]{3,2,1,0:T(8,128)(2,1)S(1)}, bf16[4,2,192,128]{3,2,1,0:T(8,128)(2,1)S(1)}, u32[]{:S(2)}, u32[]{:S(2)}) collective-permute-start(bf16[4,2,192,128]{3,2,1,0:T(8,128)(2,1)S(1)} %add_convert_fusion), channel_id=1, source_target_pairs={{0,1},{1,0},{2,6},{3,7},{4,5},{5,4},{6,2},{7,3},{8,9},{9,8},{10,14... | collective-permute-start | bytes 1179656 | tf_op jit(solution)/shard_map/ppermute | solution.py:76
  15.7 53.2 %copy-start.1 = (bf16[256,6144]{1,0:T(8,128)(2,1)S(1)}, bf16[256,6144]{1,0:T(8,128)(2,1)}, u32[]{:S(2)}) copy-start(bf16[256,6144]{1,0:T(8,128)(2,1)} %refs_1_.1) | copy-start | bytes 9437188
  15.7 5.7 %collective-permute-start.3 = (bf16[2,2,192,128]{3,2,1,0:T(8,128)(2,1)S(1)}, bf16[2,2,192,128]{3,2,1,0:T(8,128)(2,1)S(1)}, u32[]{:S(2)}, u32[]{:S(2)}) collective-permute-start(bf16[2,2,192,128]{3,2,1,0:T(8,128)(2,1)S(1)} %slice.27), channel_id=1, source_target_pairs={{0,4},{1,5},{2,10},{3,11},{4,0},{5,1},{6,14},{7,15},{8,12},{9,13},... | collective-permute-start | bytes 589832 | tf_op jit(solution)/shard_map/ppermute | solution.py:76
  21.5 0.8 %copy-start.2 = (f32[2,2,192,128]{3,2,1,0:T(8,128)}, f32[2,2,192,128]{3,2,1,0:T(8,128)S(1)}, u32[]{:S(2)}) copy-start(f32[2,2,192,128]{3,2,1,0:T(8,128)S(1)} %slice_add_fusion) | copy-start | bytes 1179652
  22.3 5.9 %collective-permute-start.4 = (f32[2,192,128]{2,1,0:T(8,128)S(1)}, f32[2,192,128]{2,1,0:T(8,128)}, u32[]{:S(2)}, u32[]{:S(2)}) collective-permute-start(f32[2,192,128]{2,1,0:T(8,128)S(1)} %slice_bitcast_fusion), channel_id=1, source_target_pairs={{0,8},{1,9},{2,3},{3,2},{4,12},{5,13},{6,7},{7,6},{8,0},{9,1},{10,... | collective-permute-start | bytes 589832 | tf_op jit(solution)/shard_map/ppermute | solution.py:76
  29.8 5.8 %collective-permute-start.5 = (f32[192,128]{1,0:T(8,128)}, f32[192,128]{1,0:T(8,128)S(1)}, u32[]{:S(2)}, u32[]{:S(2)}) collective-permute-start(f32[192,128]{1,0:T(8,128)} %dynamic-slice_bitcast_fusion), channel_id=1, source_target_pairs={{0,16},{16,0},{1,17},{17,1},{2,18},{18,2},{3,19},{19,3},{4,20},{20... | collective-permute-start | bytes 294920 | tf_op jit(solution)/shard_map/ppermute | solution.py:66
  35.7 0.6 copy-start.3
  37.4 5.2 %collective-permute-start.6 = (bf16[192,128]{1,0:T(8,128)(2,1)S(1)}, bf16[192,128]{1,0:T(8,128)(2,1)S(1)}, u32[]{:S(2)}, u32[]{:S(2)}) collective-permute-start(bf16[192,128]{1,0:T(8,128)(2,1)S(1)} %get-tuple-element.19), channel_id=1, source_target_pairs={{0,16},{16,0},{1,17},{17,1},{2,18},{18,2},{3,19},{19,3},{4,20},{20... | collective-permute-start | bytes 147464 | tf_op jit(solution)/shard_map/ppermute | solution.py:66
  40.5 4.6 %collective-permute-start.7 = (f32[192,128]{1,0:T(8,128)S(1)}, f32[192,128]{1,0:T(8,128)S(1)}, u32[]{:S(2)}, u32[]{:S(2)}) collective-permute-start(f32[192,128]{1,0:T(8,128)S(1)} %get-tuple-element.20), channel_id=1, source_target_pairs={{0,1},{1,0},{2,3},{3,2},{4,5},{5,4},{6,7},{7,6},{8,9},{9,8},{10,11... | collective-permute-start | bytes 294920 | tf_op jit(solution)/shard_map/ppermute | solution.py:66
  45.1 5.0 %collective-permute-start.8 = (bf16[1,2,192,128]{3,2,1,0:T(8,128)(2,1)S(1)}, bf16[1,2,192,128]{3,2,1,0:T(8,128)(2,1)S(1)}, u32[]{:S(2)}, u32[]{:S(2)}) collective-permute-start(bf16[1,2,192,128]{3,2,1,0:T(8,128)(2,1)S(1)} %bitcast.57), channel_id=1, source_target_pairs={{0,8},{1,9},{2,3},{3,2},{4,12},{5,13},{6,7},{7,6},{8,0},{9,1},{10,... | collective-permute-start | bytes 294920 | tf_op jit(solution)/shard_map/ppermute | solution.py:76
  50.2 7.9 %collective-permute-start.9 = (bf16[2,2,192,128]{3,2,1,0:T(8,128)(2,1)S(1)}, bf16[2,2,192,128]{3,2,1,0:T(8,128)(2,1)S(1)}, u32[]{:S(2)}, u32[]{:S(2)}) collective-permute-start(bf16[2,2,192,128]{3,2,1,0:T(8,128)(2,1)S(1)} %pad_maximum_fusion.3), channel_id=1, source_target_pairs={{0,4},{1,5},{2,10},{3,11},{4,0},{5,1},{6,14},{7,15},{8,12},{9,13},... | collective-permute-start | bytes 589832 | tf_op jit(solution)/shard_map/ppermute | solution.py:76
  58.9 8.1 %collective-permute-start.10 = (bf16[4,2,192,128]{3,2,1,0:T(8,128)(2,1)}, bf16[4,2,192,128]{3,2,1,0:T(8,128)(2,1)}, u32[]{:S(2)}, u32[]{:S(2)}) collective-permute-start(bf16[4,2,192,128]{3,2,1,0:T(8,128)(2,1)} %pad_maximum_fusion.2.refs_2_), channel_id=1, source_target_pairs={{0,1},{1,0},{2,6},{3,7},{4,5},{5,4},{6,2},{7,3},{8,9},{9,8},{10,14... | collective-permute-start | bytes 1179656 | tf_op jit(solution)/shard_map/ppermute | solution.py:76
  62.5 4.6 %collective-permute-start.11 = (bf16[4,2,192,128]{3,2,1,0:T(8,128)(2,1)}, bf16[4,2,192,128]{3,2,1,0:T(8,128)(2,1)S(1)}, u32[]{:S(2)}, u32[]{:S(2)}) collective-permute-start(bf16[4,2,192,128]{3,2,1,0:T(8,128)(2,1)} %pad_maximum_fusion.2.refs_2_), channel_id=1, source_target_pairs={{0,2},{2,0},{1,3},{3,1},{4,6},{6,4},{5,7},{7,5},{8,10},{10,8},{9,1... | collective-permute-start | bytes 1179656 | tf_op jit(solution)/shard_map/ppermute | solution.py:66
  67.0 1.9 %collective-permute-start.12 = (bf16[4,2,192,128]{3,2,1,0:T(8,128)(2,1)}, bf16[4,2,192,128]{3,2,1,0:T(8,128)(2,1)S(1)}, u32[]{:S(2)}, u32[]{:S(2)}) collective-permute-start(bf16[4,2,192,128]{3,2,1,0:T(8,128)(2,1)} %collective-permute-done.10.refs_3_), channel_id=1, source_target_pairs={{0,2},{2,0},{1,3},{3,1},{4,6},{6,4},{5,7},{7,5},{8,10},{10,8},{9,1... | collective-permute-start | bytes 1179656 | tf_op jit(solution)/shard_map/ppermute | solution.py:66

commit v5 on v3

v5 whole, which is shorter than its diff:
```python
import jax
import jax.numpy as jnp
from jax import lax
from jax.experimental import pallas as pl
from jax.experimental.pallas import tpu as pltpu
from jax.sharding import Mesh
from jax.sharding import PartitionSpec as P

AXES = ("high", "low", "core", "rep")
N_LOW = 4
SLOTS = (0, 3, 1, 2)


def parity(n):
    return (n ^ (n >> 1)) & 1


def adamw(grad, master, moment_one, moment_two, step_count):
    count = step_count[0].astype(jnp.float32)
    beta_one = 0.9
    beta_two = 0.95
    first = beta_one * moment_one + (1.0 - beta_one) * grad
    second = beta_two * moment_two + (1.0 - beta_two) * grad * grad
    first_hat = first / (1.0 - jnp.power(beta_one, count))
    second_hat = second / (1.0 - jnp.power(beta_two, count))
    updated = master - 0.01 * (first_hat / (jnp.sqrt(second_hat) + 1e-08) + 0.1 * master)
    return updated, first, second


def logits_kernel(half, chips, n_high, where_ref, acts_ref, *refs):
    pieces, before, out_ref, weight = refs[: len(chips)], refs[len(chips) : -2], refs[-2], refs[-1]
    high, low, _, rep = [where_ref[i] for i in range(4)]
    total = before[0][...] if before else None
    for piece, (_, flip, slot) in zip(pieces, chips):
        row = pl.multiple_of((rep ^ flip) * half, half)
        for c in range(2):
            for j in range(n_high):
                weight[slot, j, c, pl.ds(row, half), :] = piece[c, j]
    wide = 4 * half
    experts = weight.shape[-1]
    for slot, k in dict.fromkeys((slot, k) for k, _, slot in chips):
        for j in range(n_high):
            column = pl.multiple_of(((high ^ j) * N_LOW + (low ^ k)) * wide, wide)
            part = jnp.dot(
                acts_ref[:, pl.ds(column, wide)],
                weight[slot, j].reshape(wide, experts),
                preferred_element_type=jnp.float32,
            )
            total = part if total is None else total + part
    out_ref[...] = total.astype(out_ref.dtype)


def solution(mesh):
    n_seq, n_rep = mesh.shape["seq"], mesh.shape["rep"]
    n_high = n_seq // (2 * N_LOW)
    fine = Mesh(mesh.devices.reshape(n_high, N_LOW, 2, n_rep), AXES)

    def swap(x, axis, mask=1):
        return lax.ppermute(x, axis, [(i, i ^ mask) for i in range(fine.shape[axis])])

    def to_partner(x, k):
        pairs = []
        for low in range(N_LOW):
            for core in range(2):
                d_low, d_rep = k ^ (3 * core), parity(k) ^ core
                for rep in range(n_rep):
                    if d_low or d_rep:
                        there = ((low ^ d_low) * 2 + core) * n_rep + (rep ^ d_rep)
                        pairs.append(((low * 2 + core) * n_rep + rep, there))
        return lax.ppermute(x, AXES[1:], pairs)

    def per_device(acts, grad_logits, master, moment_one, moment_two, step_count):
        rows, experts = master.shape
        half = rows // n_rep
        where = high, low, core, rep = tuple(lax.axis_index(a) for a in AXES)
        first_core = core == 0
        f32, bf16 = jnp.float32, jnp.bfloat16

        product = lax.dot_general(
            acts, grad_logits, (((0,), (0,)), ((), ())), preferred_element_type=f32
        ).astype(bf16)
        product = product.reshape(n_high, N_LOW, 2, n_rep, half, experts)

        def for_partner(k, of_core):
            chip = (0, low ^ k ^ (3 * of_core), 0, rep ^ parity(k) ^ of_core, 0, 0)
            block = lax.dynamic_slice(product, chip, (n_high, 1, 2, 1, half, experts))
            return block.reshape(n_high, 2, half, experts)

        total = None
        for slots in (SLOTS[:2], SLOTS[2:]):
            away = jnp.stack([for_partner(k, 1 - core) for k in slots])
            arrived = swap(away, "core").astype(f32)
            for i, k in enumerate(slots):
                chip = (for_partner(k, core).astype(f32) + arrived[i]).astype(bf16)
                part = to_partner(chip, k)
                if k == 0:
                    part = jnp.where(first_core, chip, part)
                part = part.astype(f32)
                total = part if total is None else total + part

        def of_core(x, c):
            return lax.dynamic_index_in_dim(x, c, 1, keepdims=False)

        total = of_core(total, core) + swap(of_core(total, 1 - core), "core")

        grad = None
        for j in range(n_high):
            part = lax.dynamic_index_in_dim(total, high ^ j, 0, keepdims=False)
            if j:
                part = swap(part, "high", j)
            grad = part if grad is None else grad + part

        mine = [
            lax.dynamic_slice_in_dim(a, rep * half, half, 0)
            for a in (master, moment_one, moment_two)
        ]
        weight = adamw(grad, *mine, step_count)[0].astype(bf16)

        column = jnp.stack([swap(weight, "high", j) if j else weight for j in range(n_high)])
        other = swap(grad, "rep")
        across = swap(column, "core")
        across, other = lax.optimization_barrier((across, other))
        own = jnp.where(first_core, jnp.stack([column, across]), jnp.stack([across, column]))

        whole = jnp.where(
            rep == 0,
            jnp.concatenate([grad, other], 0),
            jnp.concatenate([other, grad], 0),
        )
        state = adamw(whole, master, moment_one, moment_two, step_count)

        got = {k: to_partner(own, k) for k in SLOTS}
        got[SLOTS[1]], state = lax.optimization_barrier((got[SLOTS[1]], state))
        over = {k: swap(got[k], "core") for k in SLOTS}

        logits = None
        for pair in (SLOTS[:2], SLOTS[2:]):
            pieces, chips = [], []
            for k in pair:
                by_core = [jnp.where(first_core, got[k], over[k]), jnp.where(first_core, over[k], got[k])]
                if k == 0:
                    by_core[0] = own
                for c in range(2):
                    d_low, d_rep = k ^ (3 * c), parity(k) ^ c
                    pieces.append(by_core[c])
                    chips.append((d_low, d_rep, 0 if d_low == pair[0] else 1))
            last = pair == SLOTS[2:]
            if half % 16 == 0:
                vmem = pl.BlockSpec(memory_space=pltpu.VMEM)
                before = [] if logits is None else [logits]
                logits = pl.pallas_call(
                    lambda *refs, chips=chips: logits_kernel(half, chips, n_high, *refs),
                    out_shape=jax.ShapeDtypeStruct((acts.shape[0], experts), bf16 if last else f32),
                    in_specs=[pl.BlockSpec(memory_space=pltpu.SMEM)]
                    + [vmem] * (1 + len(pieces) + len(before)),
                    out_specs=vmem,
                    scratch_shapes=[pltpu.VMEM((2, n_high, 2, rows, experts), bf16)],
                    compiler_params=pltpu.CompilerParams(vmem_limit_bytes=32 * 2**20),
                )(jnp.stack(where), acts, *pieces, *before)
            else:
                places = [
                    (((high ^ j) * N_LOW + (low ^ d_low)) * 2 + c) * n_rep + (rep ^ d_rep)
                    for d_low, d_rep, _ in chips
                    for c in range(2)
                    for j in range(n_high)
                ]
                received = jnp.concatenate(pieces).reshape(-1, half, experts)
                full = jnp.zeros((2 * received.shape[0], half, experts), bf16)
                full = full.at[jnp.stack(places)].set(received).reshape(n_seq * rows, experts)
                part = jnp.dot(acts, full, preferred_element_type=f32)
                logits = part if logits is None else (logits + part).astype(bf16)
        return *state, logits

    rows_of, tokens = P(AXES[:3], None), P(AXES, None)
    return jax.shard_map(
        per_device,
        mesh=fine,
        in_specs=(tokens, tokens, rows_of, rows_of, rows_of, P()),
        out_specs=(rows_of, rows_of, rows_of, tokens),
        check_vma=False,
    )
```

time: 63.1 us -> 67.3 us (1.067)
  other arithmetic: 4.05 us -> 9.47 us
  starting transfers between devices: 24.7 us -> 22.3 us
  local copies, waits for them, and re-layouts: 1.55 us -> 2.93 us
  waiting for transfers between devices: 25.8 us -> 24.7 us
  Pallas kernels: 2.25 us -> 2.96 us
    ppermute x10 -> x11, starting transfers between devices: 12.9 us -> 10.4 us  [swap(): lax.ppermute(x, axis, [(i, i ^ mask) for i in range(fine.shape[axis])])]
    convert_element_type x3 -> x4, other arithmetic: 1.67 us -> 3.16 us  [the longest x1 1.13 us: per_device(): weight = adamw(grad, *mine, step_count)[0].astype(bf16)]
    ppermute x10 -> x11, waiting for transfers between devices: 15.3 us -> 13.8 us  [swap(): lax.ppermute(x, axis, [(i, i ^ mask) for i in range(fine.shape[axis])])]
    add x1, other arithmetic: 0.12 us -> 1.24 us  [per_device(): total = part if total is None else total + part]
    add x1, other arithmetic: 0.02 us -> 1.04 us  [per_device(): total = of_core(total, core) + swap(of_core(total, 1 - core), 'core')]
    select_n x1, other arithmetic: 0.02 us -> 0.99 us  [per_device(): jnp.where(first_core, jnp.stack([column, across]), jnp.stack([across, col...]
    unnamed x6 -> x10, local copies, waits for them, and re-layouts: 1.44 us -> 2.18 us
    pallas_call x1 -> x2, Pallas kernels: 2.25 us -> 2.96 us  [per_device(): pl.pallas_call(lambda *refs, chips=chips: logits_kernel(half, chips, n_hi...]
  transfers between devices with their start and end apart: 18 -> 19, of which waited for: 12 -> 11; matrix products, arithmetic and copies ran while one was open for 3% -> 5% of each run, Pallas kernels for 0% -> 2%
where the time goes in v5:
time: 67.3 us; the launch traced here: 66.9 us
  waiting for transfers between devices  24.7 us (37%)
  starting transfers between devices  22.3 us (33%)
  other arithmetic  9.47 us (14%)
  Pallas kernels  2.96 us (4%)
  local copies, waits for them, and re-layouts  2.93 us (4%)
  matrix products  2.93 us (4%)
  between operations  1.58 us (2%)
    ppermute x11, waiting for transfers between devices, swap(): lax.ppermute(x, axis, [(i, i ^ mask) for i in range(fine.shape[axis])])  13.8 us
    ppermute x8, starting transfers between devices, to_partner(): return lax.ppermute(x, AXES[1:], pairs)  11.9 us
    ppermute x8, waiting for transfers between devices, to_partner(): return lax.ppermute(x, AXES[1:], pairs)  10.9 us
    ppermute x11, starting transfers between devices, swap(): lax.ppermute(x, axis, [(i, i ^ mask) for i in range(fine.shape[axis])])  10.4 us
    pallas_call x2, Pallas kernels, per_device(): pl.pallas_call(lambda *refs, chips=chips: logits_kernel(half, chips, n_hi...  2.96 us
    dot_general x1, matrix products, per_device(): lax.dot_general(acts, grad_logits, (((0,), (0,)), ((), ())), preferred_el...  2.93 us
    unnamed x10, local copies, waits for them, and re-layouts  2.18 us
    sub x1, other arithmetic, adamw(): master - 0.01 * (first_hat / (jnp.sqrt(second_hat) + 1e-08) + 0.1 * master)  2.11 us
  transfers between devices with their start and end apart: 19, of which 11 were waited for; matrix products, arithmetic and copies ran while one was open for 5% of the time, Pallas kernels for 2%

profile of v5, /device:TPU:0, one launch (start us, length us, event | category | flops | bytes accessed | tf_op | source)
XLA Modules:
  0.0 66.9 jit_solution(5735906927207232970)
XLA Ops:
  1.5 2.9 %convolution_convert_fusion = bf16[6144,128]{1,0:T(8,128)(2,1)S(1)} fusion(bf16[256,6144]{1,0:T(8,128)(2,1)} %refs_1_.3, bf16[256,128]{1,0:T(8,128)(2,1)S(1)} %copy-done), kind=kOutput, calls=%fused_computation | convolution fusion | flops 403439616 | bytes 4784128 | tf_op jit(solution)/shard_map/dot_general | solution.py:79
  5.2 1.2 %collective-permute-done.3 = bf16[2,2,2,192,128]{4,3,2,1,0:T(8,128)(2,1)S(1)} collective-permute-done((bf16[2,2,2,192,128]{4,3,2,1,0:T(8,128)(2,1)S(1)}, bf16[2,2,2,192,128]{4,3,2,1,0:T(8,128)(2,1)S(1)}, u32[]{:S(2)}, u32[]{:S(2)}) %collective-permute-start.3) | collective-permute-done | bytes 393248 | tf_op jit(solution)/shard_map/ppermute | solution.py:59
  7.1 1.0 %convert_element_type.68 = f32[2,2,2,192,128]{4,3,2,1,0:T(8,128)S(1)} convert(bf16[2,2,2,192,128]{4,3,2,1,0:T(8,128)(2,1)} %collective-permute-done) | non-fusion elementwise | flops 196608 | bytes 1179648 | tf_op jit(solution)/shard_map/convert_element_type | solution.py:92
  9.1 1.3 %collective-permute-start.1 = (bf16[2,2,192,128]{3,2,1,0:T(8,128)(2,1)S(1)}, bf16[2,2,192,128]{3,2,1,0:T(8,128)(2,1)}, u32[]{:S(2)}, u32[]{:S(2)}) collective-permute-start(bf16[2,2,192,128]{3,2,1,0:T(8,128)(2,1)S(1)} %get-tuple-element.21), channel_id=1, source_target_pairs={{2,15},{3,14},{6,11},{7,10},{10,7},{11,6},{14,3},{15,2},{18,31},{1... | collective-permute-start | bytes 589832 | tf_op jit(solution)/shard_map/ppermute | solution.py:70
  10.4 3.9 %collective-permute-start.2 = (bf16[2,2,192,128]{3,2,1,0:T(8,128)(2,1)}, bf16[2,2,192,128]{3,2,1,0:T(8,128)(2,1)}, u32[]{:S(2)}, u32[]{:S(2)}) collective-permute-start(bf16[2,2,192,128]{3,2,1,0:T(8,128)(2,1)} %get-tuple-element.22), channel_id=1, source_target_pairs={{0,12},{1,13},{2,3},{3,2},{4,8},{5,9},{6,7},{7,6},{8,4},{9,5},{10,... | collective-permute-start | bytes 589832 | tf_op jit(solution)/shard_map/ppermute | solution.py:70
  14.3 1.5 %collective-permute-start.4 = (bf16[2,2,192,128]{3,2,1,0:T(8,128)(2,1)}, bf16[2,2,192,128]{3,2,1,0:T(8,128)(2,1)}, u32[]{:S(2)}, u32[]{:S(2)}) collective-permute-start(bf16[2,2,192,128]{3,2,1,0:T(8,128)(2,1)} %get-tuple-element.26), channel_id=1, source_target_pairs={{0,5},{1,4},{2,10},{3,11},{4,1},{5,0},{6,14},{7,15},{8,13},{9,12},... | collective-permute-start | bytes 589832 | tf_op jit(solution)/shard_map/ppermute | solution.py:70
  15.8 3.8 %collective-permute-done.2 = bf16[2,2,192,128]{3,2,1,0:T(8,128)(2,1)} collective-permute-done((bf16[2,2,192,128]{3,2,1,0:T(8,128)(2,1)}, bf16[2,2,192,128]{3,2,1,0:T(8,128)(2,1)}, u32[]{:S(2)}, u32[]{:S(2)}) %collective-permute-start.2) | collective-permute-done | bytes 196640 | tf_op jit(solution)/shard_map/ppermute | solution.py:70
  19.6 5.9 %collective-permute-done.4 = bf16[2,2,192,128]{3,2,1,0:T(8,128)(2,1)} collective-permute-done((bf16[2,2,192,128]{3,2,1,0:T(8,128)(2,1)}, bf16[2,2,192,128]{3,2,1,0:T(8,128)(2,1)}, u32[]{:S(2)}, u32[]{:S(2)}) %collective-permute-start.4) | collective-permute-done | bytes 196640 | tf_op jit(solution)/shard_map/ppermute | solution.py:70
  25.7 1.2 %convert_add_fusion = f32[2,2,192,128]{3,2,1,0:T(8,128)S(1)} fusion(bf16[2,2,192,128]{3,2,1,0:T(8,128)(2,1)} %collective-permute-done.5, bf16[2,2,192,128]{3,2,1,0:T(8,128)(2,1)} %collective-permute-done.4, bf16[2,2,192,128]{3,2,1,0:T(8,128)(2,1)} %collective-permute-done.2, bf16[2,2,192,128]{3,2,1,0:T(8,128)(2,1)S(1)} %get-tuple-element.21, ...), kind=kLoop, calls=%fused_computation.15 | loop fusion | flops 786432 | bytes 1376257 | tf_op jit(solution)/shard_map/add | solution.py:99
  27.9 1.4 %collective-permute-done.6 = f32[2,192,128]{2,1,0:T(8,128)} collective-permute-done((f32[2,192,128]{2,1,0:T(8,128)S(1)}, f32[2,192,128]{2,1,0:T(8,128)}, u32[]{:S(2)}, u32[]{:S(2)}) %collective-permute-start.6) | collective-permute-done | bytes 196640 | tf_op jit(solution)/shard_map/ppermute | solution.py:59
  29.3 1.0 %bitcast_add_fusion = f32[2,192,128]{2,1,0:T(8,128)S(1)} fusion(f32[2,192,128]{2,1,0:T(8,128)} %collective-permute-done.6, f32[2,2,192,128]{3,2,1,0:T(8,128)} %copy-done.2, s32[]{:T(128)S(6)} %select_n.122), kind=kLoop, calls=%fused_computation.20 | loop fusion | flops 49152 | bytes 589828 | tf_op jit(solution)/shard_map/add | solution.py:104
  31.0 2.6 %collective-permute-start.7 = (f32[192,128]{1,0:T(8,128)}, f32[192,128]{1,0:T(8,128)S(1)}, u32[]{:S(2)}, u32[]{:S(2)}) collective-permute-start(f32[192,128]{1,0:T(8,128)} %dynamic-slice_bitcast_fusion.5), channel_id=1, source_target_pairs={{0,16},{16,0},{1,17},{17,1},{2,18},{18,2},{3,19},{19,3},{4,20},{20... | collective-permute-start | bytes 294920 | tf_op jit(solution)/shard_map/ppermute | solution.py:59
  34.4 4.8 %collective-permute-done.7 = f32[192,128]{1,0:T(8,128)S(1)} collective-permute-done((f32[192,128]{1,0:T(8,128)}, f32[192,128]{1,0:T(8,128)S(1)}, u32[]{:S(2)}, u32[]{:S(2)}) %collective-permute-start.7) | collective-permute-done | bytes 98336 | tf_op jit(solution)/shard_map/ppermute | solution.py:59
  39.8 1.1 %subtract_convert_fusion = (bf16[192,128]{1,0:T(8,128)(2,1)S(1)}, f32[192,128]{1,0:T(8,128)S(1)}) fusion(f32[384,128]{1,0:T(8,128)} %param.8, s32[]{:T(128)S(6)} %select_n.108, f32[384,128]{1,0:T(8,128)} %param.10, f32[384,128]{1,0:T(8,128)} %param.9, f32[]{:T(128)} %bitcast.18, f32[]{:T(128)} %bitcast.17, f32[192,128]{1,0:T(8,128)} %copy-done.4, ...), kind=kLoop, calls=%fused_computation.44 | loop fusion | flops 417792 | bytes 638992 | tf_op jit(solution)/shard_map/convert_element_type | solution.py:117
  41.6 1.2 %collective-permute-start.10 = (f32[192,128]{1,0:T(8,128)S(1)}, f32[192,128]{1,0:T(8,128)S(1)}, u32[]{:S(2)}, u32[]{:S(2)}) collective-permute-start(f32[192,128]{1,0:T(8,128)S(1)} %get-tuple-element.20), channel_id=1, source_target_pairs={{0,1},{1,0},{2,3},{3,2},{4,5},{5,4},{6,7},{7,6},{8,9},{9,8},{10,11... | collective-permute-start | bytes 294920 | tf_op jit(solution)/shard_map/ppermute | solution.py:59
  42.8 4.1 %collective-permute-done.8 = bf16[192,128]{1,0:T(8,128)(2,1)S(1)} collective-permute-done((bf16[192,128]{1,0:T(8,128)(2,1)S(1)}, bf16[192,128]{1,0:T(8,128)(2,1)S(1)}, u32[]{:S(2)}, u32[]{:S(2)}) %collective-permute-start.8) | collective-permute-done | bytes 49184 | tf_op jit(solution)/shard_map/ppermute | solution.py:59
  47.6 1.6 %collective-permute-done.9 = bf16[2,192,128]{2,1,0:T(8,128)(2,1)} collective-permute-done((bf16[2,192,128]{2,1,0:T(8,128)(2,1)}, bf16[2,192,128]{2,1,0:T(8,128)(2,1)}, u32[]{:S(2)}, u32[]{:S(2)}) %collective-permute-start.9) | collective-permute-done | bytes 98336 | tf_op jit(solution)/shard_map/ppermute | solution.py:59
  50.2 1.1 %collective-permute-start.11 = (bf16[2,2,192,128]{3,2,1,0:T(8,128)(2,1)S(1)}, bf16[2,2,192,128]{3,2,1,0:T(8,128)(2,1)S(1)}, u32[]{:S(2)}, u32[]{:S(2)}) collective-permute-start(bf16[2,2,192,128]{3,2,1,0:T(8,128)(2,1)S(1)} %maximum_select_fusion.refs_2_), channel_id=1, source_target_pairs={{0,12},{1,13},{2,3},{3,2},{4,8},{5,9},{6,7},{7,6},{8,4},{9,5},{10,... | collective-permute-start | bytes 589832 | tf_op jit(solution)/shard_map/ppermute | solution.py:70
  52.0 2.1 %collective-permute-start.14 = (bf16[2,2,192,128]{3,2,1,0:T(8,128)(2,1)S(1)}, bf16[2,2,192,128]{3,2,1,0:T(8,128)(2,1)S(1)}, u32[]{:S(2)}, u32[]{:S(2)}) collective-permute-start(bf16[2,2,192,128]{3,2,1,0:T(8,128)(2,1)S(1)} %maximum_select_fusion.refs_2_), channel_id=1, source_target_pairs={{0,9},{1,8},{2,6},{3,7},{4,13},{5,12},{6,2},{7,3},{8,1},{9,0},{10,... | collective-permute-start | bytes 589832 | tf_op jit(solution)/shard_map/ppermute | solution.py:70
  54.1 1.3 %collective-permute-start.12 = (bf16[2,2,192,128]{3,2,1,0:T(8,128)(2,1)S(1)}, bf16[2,2,192,128]{3,2,1,0:T(8,128)(2,1)S(1)}, u32[]{:S(2)}, u32[]{:S(2)}) collective-permute-start(bf16[2,2,192,128]{3,2,1,0:T(8,128)(2,1)S(1)} %maximum_select_fusion.refs_2_), channel_id=1, source_target_pairs={{0,5},{1,4},{2,10},{3,11},{4,1},{5,0},{6,14},{7,15},{8,13},{9,12},... | collective-permute-start | bytes 589832 | tf_op jit(solution)/shard_map/ppermute | solution.py:70
  55.4 2.1 %multiply_subtract_fusion = (f32[384,128]{1,0:T(8,128)}, f32[384,128]{1,0:T(8,128)}, f32[384,128]{1,0:T(8,128)}) fusion(f32[384,128]{1,0:T(8,128)} %param.8, f32[]{:T(128)} %bitcast.18, f32[]{:T(128)} %bitcast.17, f32[192,128]{1,0:T(8,128)S(1)} %get-tuple-element.20, f32[192,128]{1,0:T(8,128)} %copy-done.3, pred[]{:T(512)S(6)} %eq.7, f32[384,128]{1,0:T(8,128)} %param.10, ...), kind=kLoop, calls=%fused_computation.21 | loop fusion | flops 884736 | bytes 1376265 | tf_op jit(solution)/shard_map/sub | solution.py:26
  58.4 3.4 %collective-permute-start.17 = (bf16[2,2,192,128]{3,2,1,0:T(8,128)(2,1)S(1)}, bf16[2,2,192,128]{3,2,1,0:T(8,128)(2,1)S(1)}, u32[]{:S(2)}, u32[]{:S(2)}) collective-permute-start(bf16[2,2,192,128]{3,2,1,0:T(8,128)(2,1)S(1)} %collective-permute-done.16), channel_id=1, source_target_pairs={{0,2},{2,0},{1,3},{3,1},{4,6},{6,4},{5,7},{7,5},{8,10},{10,8},{9,1... | collective-permute-start | bytes 589832 | tf_op jit(solution)/shard_map/ppermute | solution.py:59
  63.7 1.2 %shard_map.93.refs_6_ = f32[256,128]{1,0:T(8,128)S(1)} custom-call(s32[4]{0:T(128)S(1)} %pad_add_fusion.refs_0_, bf16[256,6144]{1,0:T(8,128)(2,1)S(1)} %copy-done.1, bf16[2,2,192,128]{3,2,1,0:T(8,128)(2,1)S(1)} %maximum_select_fusion.refs_2_, bf16[2,2,192,128]{3,2,1,0:T(8,128)(2,1)S(1)} %broadcast_select_fusion.2.refs_3_, ...), custom_call_target="tpu_custom_call" | custom-call | tf_op jit(solution)/shard_map/pallas_call | solution.py:151
  65.1 1.8 %shard_map.94 = bf16[256,128]{1,0:T(8,128)(2,1)} custom-call(s32[4]{0:T(128)S(1)} %pad_add_fusion.refs_0_, bf16[256,6144]{1,0:T(8,128)(2,1)S(1)} %copy-done.1, bf16[2,2,192,128]{3,2,1,0:T(8,128)(2,1)S(1)} %get-tuple-element.36.refs_2_, bf16[2,2,192,128]{3,2,1,0:T(8,128)(2,1)S(1)} %get-tuple-element.35.refs_3_, ...), custom_call_target="tpu_custom_call" | custom-call | tf_op jit(solution)/shard_map/pallas_call | solution.py:151
  (46 shorter events, 11.7 us)
Async XLA Ops:
  0.6 0.8 %copy-start = (bf16[256,128]{1,0:T(8,128)(2,1)S(1)}, bf16[256,128]{1,0:T(8,128)(2,1)}, u32[]{:S(2)}) copy-start(bf16[256,128]{1,0:T(8,128)(2,1)} %param.7) | copy-start | bytes 196612
  4.5 1.9 %collective-permute-start.3 = (bf16[2,2,2,192,128]{4,3,2,1,0:T(8,128)(2,1)S(1)}, bf16[2,2,2,192,128]{4,3,2,1,0:T(8,128)(2,1)S(1)}, u32[]{:S(2)}, u32[]{:S(2)}) collective-permute-start(bf16[2,2,2,192,128]{4,3,2,1,0:T(8,128)(2,1)S(1)} %pad_maximum_fusion.1), channel_id=1, source_target_pairs={{0,2},{2,0},{1,3},{3,1},{4,6},{6,4},{5,7},{7,5},{8,10},{10,8},{9,1... | collective-permute-start | bytes 1179656 | tf_op jit(solution)/shard_map/ppermute | solution.py:59
  5.1 2.0 %collective-permute-start = (bf16[2,2,2,192,128]{4,3,2,1,0:T(8,128)(2,1)S(1)}, bf16[2,2,2,192,128]{4,3,2,1,0:T(8,128)(2,1)}, u32[]{:S(2)}, u32[]{:S(2)}) collective-permute-start(bf16[2,2,2,192,128]{4,3,2,1,0:T(8,128)(2,1)S(1)} %pad_maximum_fusion), channel_id=1, source_target_pairs={{0,2},{2,0},{1,3},{3,1},{4,6},{6,4},{5,7},{7,5},{8,10},{10,8},{9,1... | collective-permute-start | bytes 1179656 | tf_op jit(solution)/shard_map/ppermute | solution.py:59
  9.1 6.7 %collective-permute-start.1 = (bf16[2,2,192,128]{3,2,1,0:T(8,128)(2,1)S(1)}, bf16[2,2,192,128]{3,2,1,0:T(8,128)(2,1)}, u32[]{:S(2)}, u32[]{:S(2)}) collective-permute-start(bf16[2,2,192,128]{3,2,1,0:T(8,128)(2,1)S(1)} %get-tuple-element.21), channel_id=1, source_target_pairs={{2,15},{3,14},{6,11},{7,10},{10,7},{11,6},{14,3},{15,2},{18,31},{1... | collective-permute-start | bytes 589832 | tf_op jit(solution)/shard_map/ppermute | solution.py:70
  10.4 9.1 %collective-permute-start.2 = (bf16[2,2,192,128]{3,2,1,0:T(8,128)(2,1)}, bf16[2,2,192,128]{3,2,1,0:T(8,128)(2,1)}, u32[]{:S(2)}, u32[]{:S(2)}) collective-permute-start(bf16[2,2,192,128]{3,2,1,0:T(8,128)(2,1)} %get-tuple-element.22), channel_id=1, source_target_pairs={{0,12},{1,13},{2,3},{3,2},{4,8},{5,9},{6,7},{7,6},{8,4},{9,5},{10,... | collective-permute-start | bytes 589832 | tf_op jit(solution)/shard_map/ppermute | solution.py:70
  14.3 11.1 %collective-permute-start.4 = (bf16[2,2,192,128]{3,2,1,0:T(8,128)(2,1)}, bf16[2,2,192,128]{3,2,1,0:T(8,128)(2,1)}, u32[]{:S(2)}, u32[]{:S(2)}) collective-permute-start(bf16[2,2,192,128]{3,2,1,0:T(8,128)(2,1)} %get-tuple-element.26), channel_id=1, source_target_pairs={{0,5},{1,4},{2,10},{3,11},{4,1},{5,0},{6,14},{7,15},{8,13},{9,12},... | collective-permute-start | bytes 589832 | tf_op jit(solution)/shard_map/ppermute | solution.py:70
  15.8 9.9 %collective-permute-start.5 = (bf16[2,2,192,128]{3,2,1,0:T(8,128)(2,1)}, bf16[2,2,192,128]{3,2,1,0:T(8,128)(2,1)}, u32[]{:S(2)}, u32[]{:S(2)}) collective-permute-start(bf16[2,2,192,128]{3,2,1,0:T(8,128)(2,1)} %get-tuple-element.25), channel_id=1, source_target_pairs={{0,9},{1,8},{2,6},{3,7},{4,13},{5,12},{6,2},{7,3},{8,1},{9,0},{10,... | collective-permute-start | bytes 589832 | tf_op jit(solution)/shard_map/ppermute | solution.py:70
  15.8 47.9 %copy-start.1 = (bf16[256,6144]{1,0:T(8,128)(2,1)S(1)}, bf16[256,6144]{1,0:T(8,128)(2,1)}, u32[]{:S(2)}) copy-start(bf16[256,6144]{1,0:T(8,128)(2,1)} %refs_1_.3) | copy-start | bytes 9437188
  26.9 0.8 %copy-start.2 = (f32[2,2,192,128]{3,2,1,0:T(8,128)}, f32[2,2,192,128]{3,2,1,0:T(8,128)S(1)}, u32[]{:S(2)}) copy-start(f32[2,2,192,128]{3,2,1,0:T(8,128)S(1)} %convert_add_fusion) | copy-start | bytes 1179652
  27.7 1.6 %collective-permute-start.6 = (f32[2,192,128]{2,1,0:T(8,128)S(1)}, f32[2,192,128]{2,1,0:T(8,128)}, u32[]{:S(2)}, u32[]{:S(2)}) collective-permute-start(f32[2,192,128]{2,1,0:T(8,128)S(1)} %dynamic-slice_bitcast_fusion), channel_id=1, source_target_pairs={{0,2},{2,0},{1,3},{3,1},{4,6},{6,4},{5,7},{7,5},{8,10},{10,8},{9,1... | collective-permute-start | bytes 589832 | tf_op jit(solution)/shard_map/ppermute | solution.py:59
  31.0 8.1 %collective-permute-start.7 = (f32[192,128]{1,0:T(8,128)}, f32[192,128]{1,0:T(8,128)S(1)}, u32[]{:S(2)}, u32[]{:S(2)}) collective-permute-start(f32[192,128]{1,0:T(8,128)} %dynamic-slice_bitcast_fusion.5), channel_id=1, source_target_pairs={{0,16},{16,0},{1,17},{17,1},{2,18},{18,2},{3,19},{19,3},{4,20},{20... | collective-permute-start | bytes 294920 | tf_op jit(solution)/shard_map/ppermute | solution.py:59
  39.1 0.6 copy-start.4
  40.9 6.0 %collective-permute-start.8 = (bf16[192,128]{1,0:T(8,128)(2,1)S(1)}, bf16[192,128]{1,0:T(8,128)(2,1)S(1)}, u32[]{:S(2)}, u32[]{:S(2)}) collective-permute-start(bf16[192,128]{1,0:T(8,128)(2,1)S(1)} %get-tuple-element.19), channel_id=1, source_target_pairs={{0,16},{16,0},{1,17},{17,1},{2,18},{18,2},{3,19},{19,3},{4,20},{20... | collective-permute-start | bytes 147464 | tf_op jit(solution)/shard_map/ppermute | solution.py:59
  41.6 5.9 %collective-permute-start.10 = (f32[192,128]{1,0:T(8,128)S(1)}, f32[192,128]{1,0:T(8,128)S(1)}, u32[]{:S(2)}, u32[]{:S(2)}) collective-permute-start(f32[192,128]{1,0:T(8,128)S(1)} %get-tuple-element.20), channel_id=1, source_target_pairs={{0,1},{1,0},{2,3},{3,2},{4,5},{5,4},{6,7},{7,6},{8,9},{9,8},{10,11... | collective-permute-start | bytes 294920 | tf_op jit(solution)/shard_map/ppermute | solution.py:59
  47.6 1.6 %collective-permute-start.9 = (bf16[2,192,128]{2,1,0:T(8,128)(2,1)}, bf16[2,192,128]{2,1,0:T(8,128)(2,1)}, u32[]{:S(2)}, u32[]{:S(2)}) collective-permute-start(bf16[2,192,128]{2,1,0:T(8,128)(2,1)} %get-tuple-element.38), channel_id=1, source_target_pairs={{0,2},{2,0},{1,3},{3,1},{4,6},{6,4},{5,7},{7,5},{8,10},{10,8},{9,1... | collective-permute-start | bytes 294920 | tf_op jit(solution)/shard_map/ppermute | solution.py:59
  47.6 4.4 %copy-start.3 = (f32[192,128]{1,0:T(8,128)}, f32[192,128]{1,0:T(8,128)S(1)}, u32[]{:S(2)}) copy-start(f32[192,128]{1,0:T(8,128)S(1)} %collective-permute-done.10) | copy-start | bytes 294916
  50.2 7.3 %collective-permute-start.11 = (bf16[2,2,192,128]{3,2,1,0:T(8,128)(2,1)S(1)}, bf16[2,2,192,128]{3,2,1,0:T(8,128)(2,1)S(1)}, u32[]{:S(2)}, u32[]{:S(2)}) collective-permute-start(bf16[2,2,192,128]{3,2,1,0:T(8,128)(2,1)S(1)} %maximum_select_fusion.refs_2_), channel_id=1, source_target_pairs={{0,12},{1,13},{2,3},{3,2},{4,8},{5,9},{6,7},{7,6},{8,4},{9,5},{10,... | collective-permute-start | bytes 589832 | tf_op jit(solution)/shard_map/ppermute | solution.py:70
  51.3 7.1 %collective-permute-start.16 = (bf16[2,2,192,128]{3,2,1,0:T(8,128)(2,1)S(1)}, bf16[2,2,192,128]{3,2,1,0:T(8,128)(2,1)S(1)}, u32[]{:S(2)}, u32[]{:S(2)}) collective-permute-start(bf16[2,2,192,128]{3,2,1,0:T(8,128)(2,1)S(1)} %maximum_select_fusion.refs_2_), channel_id=1, source_target_pairs={{2,15},{3,14},{6,11},{7,10},{10,7},{11,6},{14,3},{15,2},{18,31},{1... | collective-permute-start | bytes 589832 | tf_op jit(solution)/shard_map/ppermute | solution.py:70
  52.0 9.8 %collective-permute-start.14 = (bf16[2,2,192,128]{3,2,1,0:T(8,128)(2,1)S(1)}, bf16[2,2,192,128]{3,2,1,0:T(8,128)(2,1)S(1)}, u32[]{:S(2)}, u32[]{:S(2)}) collective-permute-start(bf16[2,2,192,128]{3,2,1,0:T(8,128)(2,1)S(1)} %maximum_select_fusion.refs_2_), channel_id=1, source_target_pairs={{0,9},{1,8},{2,6},{3,7},{4,13},{5,12},{6,2},{7,3},{8,1},{9,0},{10,... | collective-permute-start | bytes 589832 | tf_op jit(solution)/shard_map/ppermute | solution.py:70
  54.1 9.5 %collective-permute-start.12 = (bf16[2,2,192,128]{3,2,1,0:T(8,128)(2,1)S(1)}, bf16[2,2,192,128]{3,2,1,0:T(8,128)(2,1)S(1)}, u32[]{:S(2)}, u32[]{:S(2)}) collective-permute-start(bf16[2,2,192,128]{3,2,1,0:T(8,128)(2,1)S(1)} %maximum_select_fusion.refs_2_), channel_id=1, source_target_pairs={{0,5},{1,4},{2,10},{3,11},{4,1},{5,0},{6,14},{7,15},{8,13},{9,12},... | collective-permute-start | bytes 589832 | tf_op jit(solution)/shard_map/ppermute | solution.py:70
  57.5 6.1 %collective-permute-start.18 = (bf16[2,2,192,128]{3,2,1,0:T(8,128)(2,1)S(1)}, bf16[2,2,192,128]{3,2,1,0:T(8,128)(2,1)S(1)}, u32[]{:S(2)}, u32[]{:S(2)}) collective-permute-start(bf16[2,2,192,128]{3,2,1,0:T(8,128)(2,1)S(1)} %collective-permute-done.11), channel_id=1, source_target_pairs={{0,2},{2,0},{1,3},{3,1},{4,6},{6,4},{5,7},{7,5},{8,10},{10,8},{9,1... | collective-permute-start | bytes 589832 | tf_op jit(solution)/shard_map/ppermute | solution.py:59
  58.4 5.2 %collective-permute-start.17 = (bf16[2,2,192,128]{3,2,1,0:T(8,128)(2,1)S(1)}, bf16[2,2,192,128]{3,2,1,0:T(8,128)(2,1)S(1)}, u32[]{:S(2)}, u32[]{:S(2)}) collective-permute-start(bf16[2,2,192,128]{3,2,1,0:T(8,128)(2,1)S(1)} %collective-permute-done.16), channel_id=1, source_target_pairs={{0,2},{2,0},{1,3},{3,1},{4,6},{6,4},{5,7},{7,5},{8,10},{10,8},{9,1... | collective-permute-start | bytes 589832 | tf_op jit(solution)/shard_map/ppermute | solution.py:59
  61.8 3.1 %collective-permute-start.15 = (bf16[2,2,192,128]{3,2,1,0:T(8,128)(2,1)S(1)}, bf16[2,2,192,128]{3,2,1,0:T(8,128)(2,1)S(1)}, u32[]{:S(2)}, u32[]{:S(2)}) collective-permute-start(bf16[2,2,192,128]{3,2,1,0:T(8,128)(2,1)S(1)} %collective-permute-done.14), channel_id=1, source_target_pairs={{0,2},{2,0},{1,3},{3,1},{4,6},{6,4},{5,7},{7,5},{8,10},{10,8},{9,1... | collective-permute-start | bytes 589832 | tf_op jit(solution)/shard_map/ppermute | solution.py:59
  63.6 1.4 %collective-permute-start.13 = (bf16[2,2,192,128]{3,2,1,0:T(8,128)(2,1)S(1)}, bf16[2,2,192,128]{3,2,1,0:T(8,128)(2,1)S(1)}, u32[]{:S(2)}, u32[]{:S(2)}) collective-permute-start(bf16[2,2,192,128]{3,2,1,0:T(8,128)(2,1)S(1)} %collective-permute-done.12), channel_id=1, source_target_pairs={{0,2},{2,0},{1,3},{3,1},{4,6},{6,4},{5,7},{7,5},{8,10},{10,8},{9,1... | collective-permute-start | bytes 589832 | tf_op jit(solution)/shard_map/ppermute | solution.py:59

commit v6 on v5

--- a/solution.py
+++ b/solution.py
@@ -8,7 +8,7 @@
 
 AXES = ("high", "low", "core", "rep")
 N_LOW = 4
-SLOTS = (0, 3, 1, 2)
+SLOTS = (1, 2, 3, 0)
 
 
 def parity(n):
@@ -27,20 +27,22 @@
     return updated, first, second
 
 
-def logits_kernel(half, chips, n_high, where_ref, acts_ref, *refs):
-    pieces, before, out_ref, weight = refs[: len(chips)], refs[len(chips) : -2], refs[-2], refs[-1]
-    high, low, _, rep = [where_ref[i] for i in range(4)]
+def logits_kernel(half, pair, n_high, where_ref, acts_ref, *refs):
+    pieces, before, out_ref, weight = refs[:4], refs[4:-2], refs[-2], refs[-1]
+    high, low, core, rep = [where_ref[i] for i in range(4)]
     total = before[0][...] if before else None
-    for piece, (_, flip, slot) in zip(pieces, chips):
-        row = pl.multiple_of((rep ^ flip) * half, half)
+    for i, piece in enumerate(pieces):
+        k, of_core = pair[i // 2], core ^ (i % 2)
+        slot = of_core ^ (i // 2)
+        row = pl.multiple_of((rep ^ parity(k) ^ of_core) * half, half)
         for c in range(2):
             for j in range(n_high):
                 weight[slot, j, c, pl.ds(row, half), :] = piece[c, j]
     wide = 4 * half
     experts = weight.shape[-1]
-    for slot, k in dict.fromkeys((slot, k) for k, _, slot in chips):
+    for slot in range(2):
         for j in range(n_high):
-            column = pl.multiple_of(((high ^ j) * N_LOW + (low ^ k)) * wide, wide)
+            column = pl.multiple_of(((high ^ j) * N_LOW + (low ^ pair[slot])) * wide, wide)
             part = jnp.dot(
                 acts_ref[:, pl.ds(column, wide)],
                 weight[slot, j].reshape(wide, experts),
@@ -64,9 +66,8 @@
             for core in range(2):
                 d_low, d_rep = k ^ (3 * core), parity(k) ^ core
                 for rep in range(n_rep):
-                    if d_low or d_rep:
-                        there = ((low ^ d_low) * 2 + core) * n_rep + (rep ^ d_rep)
-                        pairs.append(((low * 2 + core) * n_rep + rep, there))
+                    there = ((low ^ d_low) * 2 + core) * n_rep + (rep ^ d_rep)
+                    pairs.append(((low * 2 + core) * n_rep + rep, there))
         return lax.ppermute(x, AXES[1:], pairs)
 
     def per_device(acts, grad_logits, master, moment_one, moment_two, step_count):
@@ -93,8 +94,6 @@
             for i, k in enumerate(slots):
                 chip = (for_partner(k, core).astype(f32) + arrived[i]).astype(bf16)
                 part = to_partner(chip, k)
-                if k == 0:
-                    part = jnp.where(first_core, chip, part)
                 part = part.astype(f32)
                 total = part if total is None else total + part
 
@@ -135,32 +134,26 @@
 
         logits = None
         for pair in (SLOTS[:2], SLOTS[2:]):
-            pieces, chips = [], []
-            for k in pair:
-                by_core = [jnp.where(first_core, got[k], over[k]), jnp.where(first_core, over[k], got[k])]
-                if k == 0:
-                    by_core[0] = own
-                for c in range(2):
-                    d_low, d_rep = k ^ (3 * c), parity(k) ^ c
-                    pieces.append(by_core[c])
-                    chips.append((d_low, d_rep, 0 if d_low == pair[0] else 1))
+            pieces = [x[k] for k in pair for x in (got, over)]
             last = pair == SLOTS[2:]
             if half % 16 == 0:
                 vmem = pl.BlockSpec(memory_space=pltpu.VMEM)
                 before = [] if logits is None else [logits]
                 logits = pl.pallas_call(
-                    lambda *refs, chips=chips: logits_kernel(half, chips, n_high, *refs),
+                    lambda *refs, pair=pair: logits_kernel(half, pair, n_high, *refs),
                     out_shape=jax.ShapeDtypeStruct((acts.shape[0], experts), bf16 if last else f32),
                     in_specs=[pl.BlockSpec(memory_space=pltpu.SMEM)]
                     + [vmem] * (1 + len(pieces) + len(before)),
                     out_specs=vmem,
                     scratch_shapes=[pltpu.VMEM((2, n_high, 2, rows, experts), bf16)],
-                    compiler_params=pltpu.CompilerParams(vmem_limit_bytes=32 * 2**20),
+                    compiler_params=pltpu.CompilerParams(vmem_limit_bytes=10 * 2**20),
                 )(jnp.stack(where), acts, *pieces, *before)
             else:
                 places = [
-                    (((high ^ j) * N_LOW + (low ^ d_low)) * 2 + c) * n_rep + (rep ^ d_rep)
-                    for d_low, d_rep, _ in chips
+                    (((high ^ j) * N_LOW + (low ^ k ^ (3 * of_core))) * 2 + c) * n_rep
+                    + (rep ^ parity(k) ^ of_core)
+                    for k in pair
+                    for of_core in (core, 1 - core)
                     for c in range(2)
                     for j in range(n_high)
                 ]

time: 67.3 us -> 64 us (0.951)
  starting transfers between devices: 22.3 us -> 19.2 us
  other arithmetic: 9.47 us -> 8.37 us
  waiting for transfers between devices: 24.7 us -> 25.7 us
    ppermute x11, starting transfers between devices: 10.4 us -> 7.43 us  [swap(): lax.ppermute(x, axis, [(i, i ^ mask) for i in range(fine.shape[axis])])]
    ppermute x8, waiting for transfers between devices: 10.9 us -> 12.3 us  [to_partner(): return lax.ppermute(x, AXES[1:], pairs)]
    convert_element_type x2, other arithmetic: 1.1 us -> 0.11 us  [per_device(): arrived = swap(away, 'core').astype(f32)]
    unnamed x10 -> x8, local copies, waits for them, and re-layouts: 2.18 us -> 2.17 us
  transfers between devices with their start and end apart: 19 -> 19, of which waited for: 11 -> 11; matrix products, arithmetic and copies ran while one was open for 5% -> 4% of each run, Pallas kernels for 2% -> 2%
where the time goes in v6:
time: 64 us; the launch traced here: 63.7 us
  waiting for transfers between devices  25.7 us (40%)
  starting transfers between devices  19.2 us (30%)
  other arithmetic  8.37 us (13%)
  Pallas kernels  2.96 us (5%)
  matrix products  2.93 us (5%)
  local copies, waits for them, and re-layouts  2.91 us (5%)
  between operations  1.54 us (2%)
    ppermute x11, waiting for transfers between devices, swap(): lax.ppermute(x, axis, [(i, i ^ mask) for i in range(fine.shape[axis])])  13.4 us
    ppermute x8, waiting for transfers between devices, to_partner(): return lax.ppermute(x, AXES[1:], pairs)  12.3 us
    ppermute x8, starting transfers between devices, to_partner(): return lax.ppermute(x, AXES[1:], pairs)  11.8 us
    ppermute x11, starting transfers between devices, swap(): lax.ppermute(x, axis, [(i, i ^ mask) for i in range(fine.shape[axis])])  7.43 us
    pallas_call x2, Pallas kernels, per_device(): pl.pallas_call(lambda *refs, pair=pair: logits_kernel(half, pair, n_high,...  2.96 us
    dot_general x1, matrix products, per_device(): lax.dot_general(acts, grad_logits, (((0,), (0,)), ((), ())), preferred_el...  2.93 us
    unnamed x8, local copies, waits for them, and re-layouts  2.17 us
    sub x1, other arithmetic, adamw(): master - 0.01 * (first_hat / (jnp.sqrt(second_hat) + 1e-08) + 0.1 * master)  2.01 us
  transfers between devices with their start and end apart: 19, of which 11 were waited for; matrix products, arithmetic and copies ran while one was open for 4% of the time, Pallas kernels for 2%

profile of v6, /device:TPU:0, one launch (start us, length us, event | category | flops | bytes accessed | tf_op | source)
XLA Modules:
  0.0 63.7 jit_solution(12334462100889682394)
XLA Ops:
  1.5 2.9 %convolution_convert_fusion = bf16[6144,128]{1,0:T(8,128)(2,1)S(1)} fusion(bf16[256,6144]{1,0:T(8,128)(2,1)} %refs_1_.3, bf16[256,128]{1,0:T(8,128)(2,1)S(1)} %copy-done), kind=kOutput, calls=%fused_computation | convolution fusion | flops 403439616 | bytes 4784128 | tf_op jit(solution)/shard_map/dot_general | solution.py:80
  5.2 1.2 %collective-permute-done.3 = bf16[2,2,2,192,128]{4,3,2,1,0:T(8,128)(2,1)S(1)} collective-permute-done((bf16[2,2,2,192,128]{4,3,2,1,0:T(8,128)(2,1)S(1)}, bf16[2,2,2,192,128]{4,3,2,1,0:T(8,128)(2,1)S(1)}, u32[]{:S(2)}, u32[]{:S(2)}) %collective-permute-start.3) | collective-permute-done | bytes 393248 | tf_op jit(solution)/shard_map/ppermute | solution.py:61
  8.0 3.8 %collective-permute-start.1 = (bf16[2,2,192,128]{3,2,1,0:T(8,128)(2,1)}, bf16[2,2,192,128]{3,2,1,0:T(8,128)(2,1)}, u32[]{:S(2)}, u32[]{:S(2)}) collective-permute-start(bf16[2,2,192,128]{3,2,1,0:T(8,128)(2,1)} %get-tuple-element.21), channel_id=1, source_target_pairs={{0,5},{1,4},{2,10},{3,11},{4,1},{5,0},{6,14},{7,15},{8,13},{9,12},... | collective-permute-start | bytes 589832 | tf_op jit(solution)/shard_map/ppermute | solution.py:71
  11.8 1.5 %collective-permute-start.2 = (bf16[2,2,192,128]{3,2,1,0:T(8,128)(2,1)}, bf16[2,2,192,128]{3,2,1,0:T(8,128)(2,1)}, u32[]{:S(2)}, u32[]{:S(2)}) collective-permute-start(bf16[2,2,192,128]{3,2,1,0:T(8,128)(2,1)} %get-tuple-element.22), channel_id=1, source_target_pairs={{0,9},{1,8},{2,6},{3,7},{4,13},{5,12},{6,2},{7,3},{8,1},{9,0},{10,... | collective-permute-start | bytes 589832 | tf_op jit(solution)/shard_map/ppermute | solution.py:71
  13.4 1.3 %collective-permute-start.5 = (bf16[2,2,192,128]{3,2,1,0:T(8,128)(2,1)S(1)}, bf16[2,2,192,128]{3,2,1,0:T(8,128)(2,1)}, u32[]{:S(2)}, u32[]{:S(2)}) collective-permute-start(bf16[2,2,192,128]{3,2,1,0:T(8,128)(2,1)S(1)} %get-tuple-element.25), channel_id=1, source_target_pairs={{0,0},{1,1},{2,15},{3,14},{4,4},{5,5},{6,11},{7,10},{8,8},{9,9},{1... | collective-permute-start | bytes 589832 | tf_op jit(solution)/shard_map/ppermute | solution.py:71
  14.7 2.5 %collective-permute-done.1 = bf16[2,2,192,128]{3,2,1,0:T(8,128)(2,1)} collective-permute-done((bf16[2,2,192,128]{3,2,1,0:T(8,128)(2,1)}, bf16[2,2,192,128]{3,2,1,0:T(8,128)(2,1)}, u32[]{:S(2)}, u32[]{:S(2)}) %collective-permute-start.1) | collective-permute-done | bytes 196640 | tf_op jit(solution)/shard_map/ppermute | solution.py:71
  17.1 1.9 %collective-permute-done.2 = bf16[2,2,192,128]{3,2,1,0:T(8,128)(2,1)} collective-permute-done((bf16[2,2,192,128]{3,2,1,0:T(8,128)(2,1)}, bf16[2,2,192,128]{3,2,1,0:T(8,128)(2,1)}, u32[]{:S(2)}, u32[]{:S(2)}) %collective-permute-start.2) | collective-permute-done | bytes 196640 | tf_op jit(solution)/shard_map/ppermute | solution.py:71
  19.0 2.8 %collective-permute-done.4 = bf16[2,2,192,128]{3,2,1,0:T(8,128)(2,1)} collective-permute-done((bf16[2,2,192,128]{3,2,1,0:T(8,128)(2,1)}, bf16[2,2,192,128]{3,2,1,0:T(8,128)(2,1)}, u32[]{:S(2)}, u32[]{:S(2)}) %collective-permute-start.4) | collective-permute-done | bytes 196640 | tf_op jit(solution)/shard_map/ppermute | solution.py:71
  21.8 1.3 %convert_add_fusion = f32[2,2,192,128]{3,2,1,0:T(8,128)S(1)} fusion(bf16[2,2,192,128]{3,2,1,0:T(8,128)(2,1)} %collective-permute-done.5, bf16[2,2,192,128]{3,2,1,0:T(8,128)(2,1)} %collective-permute-done.4, bf16[2,2,192,128]{3,2,1,0:T(8,128)(2,1)} %collective-permute-done.2, bf16[2,2,192,128]{3,2,1,0:T(8,128)(2,1)} %collective-permute-done.1), kind=kLoop, calls=%fused_computation.15 | loop fusion | flops 688128 | bytes 1179648 | tf_op jit(solution)/shard_map/add | solution.py:98
  23.9 1.5 %collective-permute-start.6 = (f32[2,192,128]{2,1,0:T(8,128)S(1)}, f32[2,192,128]{2,1,0:T(8,128)}, u32[]{:S(2)}, u32[]{:S(2)}) collective-permute-start(f32[2,192,128]{2,1,0:T(8,128)S(1)} %dynamic-slice_bitcast_fusion), channel_id=1, source_target_pairs={{0,2},{2,0},{1,3},{3,1},{4,6},{6,4},{5,7},{7,5},{8,10},{10,8},{9,1... | collective-permute-start | bytes 589832 | tf_op jit(solution)/shard_map/ppermute | solution.py:61
  25.4 1.2 %collective-permute-done.6 = f32[2,192,128]{2,1,0:T(8,128)} collective-permute-done((f32[2,192,128]{2,1,0:T(8,128)S(1)}, f32[2,192,128]{2,1,0:T(8,128)}, u32[]{:S(2)}, u32[]{:S(2)}) %collective-permute-start.6) | collective-permute-done | bytes 196640 | tf_op jit(solution)/shard_map/ppermute | solution.py:61
  28.3 2.6 %collective-permute-start.7 = (f32[192,128]{1,0:T(8,128)}, f32[192,128]{1,0:T(8,128)S(1)}, u32[]{:S(2)}, u32[]{:S(2)}) collective-permute-start(f32[192,128]{1,0:T(8,128)} %dynamic-slice_bitcast_fusion.5), channel_id=1, source_target_pairs={{0,16},{16,0},{1,17},{17,1},{2,18},{18,2},{3,19},{19,3},{4,20},{20... | collective-permute-start | bytes 294920 | tf_op jit(solution)/shard_map/ppermute | solution.py:61
  31.6 4.9 %collective-permute-done.7 = f32[192,128]{1,0:T(8,128)S(1)} collective-permute-done((f32[192,128]{1,0:T(8,128)}, f32[192,128]{1,0:T(8,128)S(1)}, u32[]{:S(2)}, u32[]{:S(2)}) %collective-permute-start.7) | collective-permute-done | bytes 98336 | tf_op jit(solution)/shard_map/ppermute | solution.py:61
  37.2 1.1 %subtract_convert_fusion = (bf16[192,128]{1,0:T(8,128)(2,1)S(1)}, f32[192,128]{1,0:T(8,128)S(1)}) fusion(f32[384,128]{1,0:T(8,128)} %param.8, s32[]{:T(128)S(6)} %select_n.76, f32[384,128]{1,0:T(8,128)} %param.10, f32[384,128]{1,0:T(8,128)} %param.9, f32[]{:T(128)} %bitcast.18, f32[]{:T(128)} %bitcast.17, f32[192,128]{1,0:T(8,128)} %copy-done.3, ...), kind=kLoop, calls=%fused_computation.37 | loop fusion | flops 417792 | bytes 638992 | tf_op jit(solution)/shard_map/convert_element_type | solution.py:116
  40.0 3.9 %collective-permute-done.8 = bf16[192,128]{1,0:T(8,128)(2,1)S(1)} collective-permute-done((bf16[192,128]{1,0:T(8,128)(2,1)S(1)}, bf16[192,128]{1,0:T(8,128)(2,1)S(1)}, u32[]{:S(2)}, u32[]{:S(2)}) %collective-permute-start.8) | collective-permute-done | bytes 49184 | tf_op jit(solution)/shard_map/ppermute | solution.py:61
  44.6 1.6 %collective-permute-done.9 = bf16[2,192,128]{2,1,0:T(8,128)(2,1)} collective-permute-done((bf16[2,192,128]{2,1,0:T(8,128)(2,1)}, bf16[2,192,128]{2,1,0:T(8,128)(2,1)}, u32[]{:S(2)}, u32[]{:S(2)}) %collective-permute-start.9) | collective-permute-done | bytes 98336 | tf_op jit(solution)/shard_map/ppermute | solution.py:61
  47.2 1.1 %collective-permute-start.11 = (bf16[2,2,192,128]{3,2,1,0:T(8,128)(2,1)S(1)}, bf16[2,2,192,128]{3,2,1,0:T(8,128)(2,1)S(1)}, u32[]{:S(2)}, u32[]{:S(2)}) collective-permute-start(bf16[2,2,192,128]{3,2,1,0:T(8,128)(2,1)S(1)} %maximum_select_fusion), channel_id=1, source_target_pairs={{0,9},{1,8},{2,6},{3,7},{4,13},{5,12},{6,2},{7,3},{8,1},{9,0},{10,... | collective-permute-start | bytes 589832 | tf_op jit(solution)/shard_map/ppermute | solution.py:71
  48.4 1.7 %collective-permute-start.16 = (bf16[2,2,192,128]{3,2,1,0:T(8,128)(2,1)S(1)}, bf16[2,2,192,128]{3,2,1,0:T(8,128)(2,1)S(1)}, u32[]{:S(2)}, u32[]{:S(2)}) collective-permute-start(bf16[2,2,192,128]{3,2,1,0:T(8,128)(2,1)S(1)} %maximum_select_fusion), channel_id=1, source_target_pairs={{0,5},{1,4},{2,10},{3,11},{4,1},{5,0},{6,14},{7,15},{8,13},{9,12},... | collective-permute-start | bytes 589832 | tf_op jit(solution)/shard_map/ppermute | solution.py:71
  50.1 1.6 %collective-permute-start.12 = (bf16[2,2,192,128]{3,2,1,0:T(8,128)(2,1)S(1)}, bf16[2,2,192,128]{3,2,1,0:T(8,128)(2,1)S(1)}, u32[]{:S(2)}, u32[]{:S(2)}) collective-permute-start(bf16[2,2,192,128]{3,2,1,0:T(8,128)(2,1)S(1)} %maximum_select_fusion), channel_id=1, source_target_pairs={{0,12},{1,13},{2,3},{3,2},{4,8},{5,9},{6,7},{7,6},{8,4},{9,5},{10,... | collective-permute-start | bytes 589832 | tf_op jit(solution)/shard_map/ppermute | solution.py:71
  52.4 2.0 %multiply_subtract_fusion = (f32[384,128]{1,0:T(8,128)}, f32[384,128]{1,0:T(8,128)}, f32[384,128]{1,0:T(8,128)}) fusion(f32[384,128]{1,0:T(8,128)} %param.8, f32[]{:T(128)} %bitcast.18, f32[]{:T(128)} %bitcast.17, f32[192,128]{1,0:T(8,128)S(1)} %get-tuple-element.20, f32[192,128]{1,0:T(8,128)S(1)} %collective-permute-done.10, pred[]{:T(512)S(6)} %eq.7, ...), kind=kLoop, calls=%fused_computation.21 | loop fusion | flops 884736 | bytes 1376265 | tf_op jit(solution)/shard_map/sub | solution.py:26
  54.4 2.1 %collective-permute-done.11.refs_4_ = bf16[2,2,192,128]{3,2,1,0:T(8,128)(2,1)S(1)} collective-permute-done((bf16[2,2,192,128]{3,2,1,0:T(8,128)(2,1)S(1)}, bf16[2,2,192,128]{3,2,1,0:T(8,128)(2,1)S(1)}, u32[]{:S(2)}, u32[]{:S(2)}) %collective-permute-start.11) | collective-permute-done | bytes 196640 | tf_op jit(solution)/shard_map/ppermute | solution.py:71
  57.0 3.1 %collective-permute-done.12.refs_2_ = bf16[2,2,192,128]{3,2,1,0:T(8,128)(2,1)S(1)} collective-permute-done((bf16[2,2,192,128]{3,2,1,0:T(8,128)(2,1)S(1)}, bf16[2,2,192,128]{3,2,1,0:T(8,128)(2,1)S(1)}, u32[]{:S(2)}, u32[]{:S(2)}) %collective-permute-start.12) | collective-permute-done | bytes 196640 | tf_op jit(solution)/shard_map/ppermute | solution.py:71
  60.7 1.2 %shard_map.93.refs_6_ = f32[256,128]{1,0:T(8,128)S(1)} custom-call(s32[4]{0:T(128)S(1)} %pad_add_fusion.refs_0_, bf16[256,6144]{1,0:T(8,128)(2,1)S(1)} %copy-done.1, bf16[2,2,192,128]{3,2,1,0:T(8,128)(2,1)S(1)} %collective-permute-done.16.refs_2_, bf16[2,2,192,128]{3,2,1,0:T(8,128)(2,1)S(1)} %collective-permute-done.17.refs_3_, ...), custom_call_target="tpu_custom_call" | custom-call | tf_op jit(solution)/shard_map/pallas_call | solution.py:142
  61.9 1.8 %shard_map.94 = bf16[256,128]{1,0:T(8,128)(2,1)} custom-call(s32[4]{0:T(128)S(1)} %pad_add_fusion.refs_0_, bf16[256,6144]{1,0:T(8,128)(2,1)S(1)} %copy-done.1, bf16[2,2,192,128]{3,2,1,0:T(8,128)(2,1)S(1)} %collective-permute-done.12.refs_2_, bf16[2,2,192,128]{3,2,1,0:T(8,128)(2,1)S(1)} %collective-permute-done.13.refs_3_, ...), custom_call_target="tpu_custom_call" | custom-call | tf_op jit(solution)/shard_map/pallas_call | solution.py:142
  (40 shorter events, 11.4 us)
Async XLA Ops:
  0.6 0.8 %copy-start = (bf16[256,128]{1,0:T(8,128)(2,1)S(1)}, bf16[256,128]{1,0:T(8,128)(2,1)}, u32[]{:S(2)}) copy-start(bf16[256,128]{1,0:T(8,128)(2,1)} %param.7) | copy-start | bytes 196612
  4.5 1.9 %collective-permute-start.3 = (bf16[2,2,2,192,128]{4,3,2,1,0:T(8,128)(2,1)S(1)}, bf16[2,2,2,192,128]{4,3,2,1,0:T(8,128)(2,1)S(1)}, u32[]{:S(2)}, u32[]{:S(2)}) collective-permute-start(bf16[2,2,2,192,128]{4,3,2,1,0:T(8,128)(2,1)S(1)} %pad_maximum_fusion.1), channel_id=1, source_target_pairs={{0,2},{2,0},{1,3},{3,1},{4,6},{6,4},{5,7},{7,5},{8,10},{10,8},{9,1... | collective-permute-start | bytes 1179656 | tf_op jit(solution)/shard_map/ppermute | solution.py:61
  5.1 1.9 %collective-permute-start = (bf16[2,2,2,192,128]{4,3,2,1,0:T(8,128)(2,1)S(1)}, bf16[2,2,2,192,128]{4,3,2,1,0:T(8,128)(2,1)S(1)}, u32[]{:S(2)}, u32[]{:S(2)}) collective-permute-start(bf16[2,2,2,192,128]{4,3,2,1,0:T(8,128)(2,1)S(1)} %pad_maximum_fusion), channel_id=1, source_target_pairs={{0,2},{2,0},{1,3},{3,1},{4,6},{6,4},{5,7},{7,5},{8,10},{10,8},{9,1... | collective-permute-start | bytes 1179656 | tf_op jit(solution)/shard_map/ppermute | solution.py:61
  8.0 52.7 %copy-start.1 = (bf16[256,6144]{1,0:T(8,128)(2,1)S(1)}, bf16[256,6144]{1,0:T(8,128)(2,1)}, u32[]{:S(2)}) copy-start(bf16[256,6144]{1,0:T(8,128)(2,1)} %refs_1_.3) | copy-start | bytes 9437188
  8.0 9.1 %collective-permute-start.1 = (bf16[2,2,192,128]{3,2,1,0:T(8,128)(2,1)}, bf16[2,2,192,128]{3,2,1,0:T(8,128)(2,1)}, u32[]{:S(2)}, u32[]{:S(2)}) collective-permute-start(bf16[2,2,192,128]{3,2,1,0:T(8,128)(2,1)} %get-tuple-element.21), channel_id=1, source_target_pairs={{0,5},{1,4},{2,10},{3,11},{4,1},{5,0},{6,14},{7,15},{8,13},{9,12},... | collective-permute-start | bytes 589832 | tf_op jit(solution)/shard_map/ppermute | solution.py:71
  11.8 7.2 %collective-permute-start.2 = (bf16[2,2,192,128]{3,2,1,0:T(8,128)(2,1)}, bf16[2,2,192,128]{3,2,1,0:T(8,128)(2,1)}, u32[]{:S(2)}, u32[]{:S(2)}) collective-permute-start(bf16[2,2,192,128]{3,2,1,0:T(8,128)(2,1)} %get-tuple-element.22), channel_id=1, source_target_pairs={{0,9},{1,8},{2,6},{3,7},{4,13},{5,12},{6,2},{7,3},{8,1},{9,0},{10,... | collective-permute-start | bytes 589832 | tf_op jit(solution)/shard_map/ppermute | solution.py:71
  13.3 8.5 %collective-permute-start.4 = (bf16[2,2,192,128]{3,2,1,0:T(8,128)(2,1)}, bf16[2,2,192,128]{3,2,1,0:T(8,128)(2,1)}, u32[]{:S(2)}, u32[]{:S(2)}) collective-permute-start(bf16[2,2,192,128]{3,2,1,0:T(8,128)(2,1)} %get-tuple-element.26), channel_id=1, source_target_pairs={{0,12},{1,13},{2,3},{3,2},{4,8},{5,9},{6,7},{7,6},{8,4},{9,5},{10,... | collective-permute-start | bytes 589832 | tf_op jit(solution)/shard_map/ppermute | solution.py:71
  13.4 8.5 %collective-permute-start.5 = (bf16[2,2,192,128]{3,2,1,0:T(8,128)(2,1)S(1)}, bf16[2,2,192,128]{3,2,1,0:T(8,128)(2,1)}, u32[]{:S(2)}, u32[]{:S(2)}) collective-permute-start(bf16[2,2,192,128]{3,2,1,0:T(8,128)(2,1)S(1)} %get-tuple-element.25), channel_id=1, source_target_pairs={{0,0},{1,1},{2,15},{3,14},{4,4},{5,5},{6,11},{7,10},{8,8},{9,9},{1... | collective-permute-start | bytes 589832 | tf_op jit(solution)/shard_map/ppermute | solution.py:71
  23.1 0.7 %copy-start.2 = (f32[2,2,192,128]{3,2,1,0:T(8,128)}, f32[2,2,192,128]{3,2,1,0:T(8,128)S(1)}, u32[]{:S(2)}) copy-start(f32[2,2,192,128]{3,2,1,0:T(8,128)S(1)} %convert_add_fusion) | copy-start | bytes 1179652
  23.9 2.7 %collective-permute-start.6 = (f32[2,192,128]{2,1,0:T(8,128)S(1)}, f32[2,192,128]{2,1,0:T(8,128)}, u32[]{:S(2)}, u32[]{:S(2)}) collective-permute-start(f32[2,192,128]{2,1,0:T(8,128)S(1)} %dynamic-slice_bitcast_fusion), channel_id=1, source_target_pairs={{0,2},{2,0},{1,3},{3,1},{4,6},{6,4},{5,7},{7,5},{8,10},{10,8},{9,1... | collective-permute-start | bytes 589832 | tf_op jit(solution)/shard_map/ppermute | solution.py:61
  28.3 8.3 %collective-permute-start.7 = (f32[192,128]{1,0:T(8,128)}, f32[192,128]{1,0:T(8,128)S(1)}, u32[]{:S(2)}, u32[]{:S(2)}) collective-permute-start(f32[192,128]{1,0:T(8,128)} %dynamic-slice_bitcast_fusion.5), channel_id=1, source_target_pairs={{0,16},{16,0},{1,17},{17,1},{2,18},{18,2},{3,19},{19,3},{4,20},{20... | collective-permute-start | bytes 294920 | tf_op jit(solution)/shard_map/ppermute | solution.py:61
  36.6 0.6 %copy-start.3 = (f32[192,128]{1,0:T(8,128)}, f32[192,128]{1,0:T(8,128)S(1)}, u32[]{:S(2)}) copy-start(f32[192,128]{1,0:T(8,128)S(1)} %collective-permute-done.7) | copy-start | bytes 294916
  38.4 5.6 %collective-permute-start.8 = (bf16[192,128]{1,0:T(8,128)(2,1)S(1)}, bf16[192,128]{1,0:T(8,128)(2,1)S(1)}, u32[]{:S(2)}, u32[]{:S(2)}) collective-permute-start(bf16[192,128]{1,0:T(8,128)(2,1)S(1)} %get-tuple-element.19), channel_id=1, source_target_pairs={{0,16},{16,0},{1,17},{17,1},{2,18},{18,2},{3,19},{19,3},{4,20},{20... | collective-permute-start | bytes 147464 | tf_op jit(solution)/shard_map/ppermute | solution.py:61
  39.0 5.6 %collective-permute-start.10 = (f32[192,128]{1,0:T(8,128)S(1)}, f32[192,128]{1,0:T(8,128)S(1)}, u32[]{:S(2)}, u32[]{:S(2)}) collective-permute-start(f32[192,128]{1,0:T(8,128)S(1)} %get-tuple-element.20), channel_id=1, source_target_pairs={{0,1},{1,0},{2,3},{3,2},{4,5},{5,4},{6,7},{7,6},{8,9},{9,8},{10,11... | collective-permute-start | bytes 294920 | tf_op jit(solution)/shard_map/ppermute | solution.py:61
  44.6 1.6 %collective-permute-start.9 = (bf16[2,192,128]{2,1,0:T(8,128)(2,1)}, bf16[2,192,128]{2,1,0:T(8,128)(2,1)}, u32[]{:S(2)}, u32[]{:S(2)}) collective-permute-start(bf16[2,192,128]{2,1,0:T(8,128)(2,1)} %get-tuple-element.32), channel_id=1, source_target_pairs={{0,2},{2,0},{1,3},{3,1},{4,6},{6,4},{5,7},{7,5},{8,10},{10,8},{9,1... | collective-permute-start | bytes 294920 | tf_op jit(solution)/shard_map/ppermute | solution.py:61
  47.2 9.2 %collective-permute-start.11 = (bf16[2,2,192,128]{3,2,1,0:T(8,128)(2,1)S(1)}, bf16[2,2,192,128]{3,2,1,0:T(8,128)(2,1)S(1)}, u32[]{:S(2)}, u32[]{:S(2)}) collective-permute-start(bf16[2,2,192,128]{3,2,1,0:T(8,128)(2,1)S(1)} %maximum_select_fusion), channel_id=1, source_target_pairs={{0,9},{1,8},{2,6},{3,7},{4,13},{5,12},{6,2},{7,3},{8,1},{9,0},{10,... | collective-permute-start | bytes 589832 | tf_op jit(solution)/shard_map/ppermute | solution.py:71
  48.4 8.1 %collective-permute-start.16 = (bf16[2,2,192,128]{3,2,1,0:T(8,128)(2,1)S(1)}, bf16[2,2,192,128]{3,2,1,0:T(8,128)(2,1)S(1)}, u32[]{:S(2)}, u32[]{:S(2)}) collective-permute-start(bf16[2,2,192,128]{3,2,1,0:T(8,128)(2,1)S(1)} %maximum_select_fusion), channel_id=1, source_target_pairs={{0,5},{1,4},{2,10},{3,11},{4,1},{5,0},{6,14},{7,15},{8,13},{9,12},... | collective-permute-start | bytes 589832 | tf_op jit(solution)/shard_map/ppermute | solution.py:71
  50.1 10.0 %collective-permute-start.12 = (bf16[2,2,192,128]{3,2,1,0:T(8,128)(2,1)S(1)}, bf16[2,2,192,128]{3,2,1,0:T(8,128)(2,1)S(1)}, u32[]{:S(2)}, u32[]{:S(2)}) collective-permute-start(bf16[2,2,192,128]{3,2,1,0:T(8,128)(2,1)S(1)} %maximum_select_fusion), channel_id=1, source_target_pairs={{0,12},{1,13},{2,3},{3,2},{4,8},{5,9},{6,7},{7,6},{8,4},{9,5},{10,... | collective-permute-start | bytes 589832 | tf_op jit(solution)/shard_map/ppermute | solution.py:71
  51.7 8.4 %collective-permute-start.14 = (bf16[2,2,192,128]{3,2,1,0:T(8,128)(2,1)S(1)}, bf16[2,2,192,128]{3,2,1,0:T(8,128)(2,1)S(1)}, u32[]{:S(2)}, u32[]{:S(2)}) collective-permute-start(bf16[2,2,192,128]{3,2,1,0:T(8,128)(2,1)S(1)} %maximum_select_fusion), channel_id=1, source_target_pairs={{0,0},{1,1},{2,15},{3,14},{4,4},{5,5},{6,11},{7,10},{8,8},{9,9},{1... | collective-permute-start | bytes 589832 | tf_op jit(solution)/shard_map/ppermute | solution.py:71
  56.4 4.2 %collective-permute-start.18 = (bf16[2,2,192,128]{3,2,1,0:T(8,128)(2,1)S(1)}, bf16[2,2,192,128]{3,2,1,0:T(8,128)(2,1)S(1)}, u32[]{:S(2)}, u32[]{:S(2)}) collective-permute-start(bf16[2,2,192,128]{3,2,1,0:T(8,128)(2,1)S(1)} %collective-permute-done.11.refs_4_), channel_id=1, source_target_pairs={{0,2},{2,0},{1,3},{3,1},{4,6},{6,4},{5,7},{7,5},{8,10},{10,8},{9,1... | collective-permute-start | bytes 589832 | tf_op jit(solution)/shard_map/ppermute | solution.py:61
  56.4 4.2 %collective-permute-start.17 = (bf16[2,2,192,128]{3,2,1,0:T(8,128)(2,1)S(1)}, bf16[2,2,192,128]{3,2,1,0:T(8,128)(2,1)S(1)}, u32[]{:S(2)}, u32[]{:S(2)}) collective-permute-start(bf16[2,2,192,128]{3,2,1,0:T(8,128)(2,1)S(1)} %collective-permute-done.16.refs_2_), channel_id=1, source_target_pairs={{0,2},{2,0},{1,3},{3,1},{4,6},{6,4},{5,7},{7,5},{8,10},{10,8},{9,1... | collective-permute-start | bytes 589832 | tf_op jit(solution)/shard_map/ppermute | solution.py:61
  60.1 1.8 %collective-permute-start.13 = (bf16[2,2,192,128]{3,2,1,0:T(8,128)(2,1)S(1)}, bf16[2,2,192,128]{3,2,1,0:T(8,128)(2,1)S(1)}, u32[]{:S(2)}, u32[]{:S(2)}) collective-permute-start(bf16[2,2,192,128]{3,2,1,0:T(8,128)(2,1)S(1)} %collective-permute-done.12.refs_2_), channel_id=1, source_target_pairs={{0,2},{2,0},{1,3},{3,1},{4,6},{6,4},{5,7},{7,5},{8,10},{10,8},{9,1... | collective-permute-start | bytes 589832 | tf_op jit(solution)/shard_map/ppermute | solution.py:61
  60.1 1.8 %collective-permute-start.15 = (bf16[2,2,192,128]{3,2,1,0:T(8,128)(2,1)S(1)}, bf16[2,2,192,128]{3,2,1,0:T(8,128)(2,1)S(1)}, u32[]{:S(2)}, u32[]{:S(2)}) collective-permute-start(bf16[2,2,192,128]{3,2,1,0:T(8,128)(2,1)S(1)} %collective-permute-done.14.refs_4_), channel_id=1, source_target_pairs={{0,2},{2,0},{1,3},{3,1},{4,6},{6,4},{5,7},{7,5},{8,10},{10,8},{9,1... | collective-permute-start | bytes 589832 | tf_op jit(solution)/shard_map/ppermute | solution.py:61

commit v7 on v6

v7 whole, which is shorter than its diff:
```python
import functools

import jax
import jax.numpy as jnp
from jax import lax
from jax.experimental import pallas as pl
from jax.experimental.pallas import tpu as pltpu
from jax.sharding import Mesh
from jax.sharding import PartitionSpec as P

AXES = ("high", "low", "core", "rep")
N_LOW = 4
FIRST = (1, 2)
VMEM_LIMIT = 8 * 2**20


def parity(n):
    return (n ^ (n >> 1)) & 1


def adamw(grad, master, moment_one, moment_two, step_count):
    count = step_count[0].astype(jnp.float32)
    beta_one = 0.9
    beta_two = 0.95
    first = beta_one * moment_one + (1.0 - beta_one) * grad
    second = beta_two * moment_two + (1.0 - beta_two) * grad * grad
    first_hat = first / (1.0 - jnp.power(beta_one, count))
    second_hat = second / (1.0 - jnp.power(beta_two, count))
    updated = master - 0.01 * (first_hat / (jnp.sqrt(second_hat) + 1e-08) + 0.1 * master)
    return updated, first, second


def load_columns(acts_ref, chunks, sems, high, low, n_high):
    wide = chunks.shape[-1]
    copies = []
    for p, at in enumerate(low):
        for j in range(n_high):
            column = pl.multiple_of(((high ^ j) * N_LOW + at) * wide, wide)
            n = p * n_high + j
            copy = pltpu.make_async_copy(acts_ref.at[:, pl.ds(column, wide)], chunks.at[n], sems.at[n])
            copy.start()
            copies.append(copy)
    return copies


def partial_products(copies, chunks, grad_ref, blocks):
    for n, copy in enumerate(copies):
        copy.wait()
        product = lax.dot_general(
            chunks[n], grad_ref[...], (((0,), (0,)), ((), ())), preferred_element_type=jnp.float32
        )
        blocks[...] = product.astype(blocks.dtype).reshape(blocks.shape)
        yield n


def first_grad_kernel(n_high, where_ref, acts_ref, grad_ref, away_ref, kept_ref, chunks, blocks, sems):
    _, low, core, rep = [where_ref[i] for i in range(4)]
    copies = load_columns(acts_ref, chunks, sems, 0, [low ^ k for k in FIRST], n_high)
    for n in partial_products(copies, chunks, grad_ref, blocks):
        p, j = divmod(n, n_high)
        flip = rep ^ core ^ parity(FIRST[p])
        for c in range(2):
            kept_ref[p ^ core, c, j] = blocks[c, flip]
            away_ref[p ^ core ^ 1, c, j] = blocks[c, flip ^ 1]


def second_grad_kernel(n_high, where_ref, acts_ref, grad_ref, away_ref, kept_ref, chunks, blocks, sems):
    _, low, core, rep = [where_ref[i] for i in range(4)]
    at = [low ^ (3 * (1 - core)), low ^ (3 * core)]
    copies = load_columns(acts_ref, chunks, sems, 0, at, n_high)
    for n in partial_products(copies, chunks, grad_ref, blocks):
        p, j = divmod(n, n_high)
        slot_ref = kept_ref if p == 0 else away_ref
        flip = rep ^ core ^ p
        for c in range(2):
            slot_ref[c, j] = blocks[c, flip]
        kept_ref[2 + (core ^ p), j] = blocks[core, flip ^ 1]
        away_ref[2 + (core ^ p), j] = blocks[core ^ 1, flip ^ 1]


def logits_kernel(n_high, lows, place, where_ref, acts_ref, *refs):
    *pieces, out_ref, chunks, weight, sems = refs
    before = None
    if len(pieces[-1].shape) == 2:
        *pieces, before = pieces
    high, low, core, rep = [where_ref[i] for i in range(4)]
    copies = load_columns(acts_ref, chunks, sems, high, [low ^ k for k in lows], n_high)
    half, experts = weight.shape[-2:]
    for i, piece in enumerate(pieces):
        for b, (slot, owner, of_rep) in enumerate(place(core, rep, i)):
            for j in range(n_high):
                weight[slot, j, owner, of_rep] = piece[b, j]
    total = None if before is None else before[...]
    for n, copy in enumerate(copies):
        slot, j = divmod(n, n_high)
        copy.wait()
        part = jnp.dot(
            chunks[n],
            weight[slot, j].reshape(4 * half, experts),
            preferred_element_type=jnp.float32,
        )
        total = part if total is None else total + part
    out_ref[...] = total.astype(out_ref.dtype)


def first_place(core, rep, i):
    k, of_core = FIRST[i // 2], core ^ (i % 2)
    return [(of_core ^ (i // 2), c, rep ^ parity(k) ^ of_core) for c in range(2)]


def second_place(core, rep, i):
    if i < 2:
        of_core = core ^ i
        return [(of_core, c, rep ^ of_core) for c in range(2)]
    owner = core ^ (i % 2)
    return [(0, owner, rep ^ 1)] if i < 4 else [(1, owner, rep)]


def solution(mesh):
    n_seq, n_rep = mesh.shape["seq"], mesh.shape["rep"]
    n_high = n_seq // (2 * N_LOW)
    fine = Mesh(mesh.devices.reshape(n_high, N_LOW, 2, n_rep), AXES)

    def swap(x, axis, mask=1):
        return lax.ppermute(x, axis, [(i, i ^ mask) for i in range(fine.shape[axis])])

    def cube_swap(x, change):
        pairs = []
        for low in range(N_LOW):
            for core in range(2):
                d_low, d_rep = change(core)
                for rep in range(n_rep):
                    there = ((low ^ d_low) * 2 + core) * n_rep + (rep ^ d_rep)
                    pairs.append(((low * 2 + core) * n_rep + rep, there))
        return lax.ppermute(x, AXES[1:], pairs)

    def to_partner(x, k):
        return cube_swap(x, lambda core: (k ^ (3 * core), parity(k) ^ core))

    def to_corner(x):
        return cube_swap(x, lambda core: (3, 1))

    def per_device(acts, grad_logits, master, moment_one, moment_two, step_count):
        tokens, experts = grad_logits.shape
        rows = master.shape[0]
        half = rows // n_rep
        high, low, core, rep = (lax.axis_index(a) for a in AXES)
        where = jnp.stack([high, low, core, rep])
        first_core = core == 0
        f32, bf16 = jnp.float32, jnp.bfloat16
        in_kernels = half % 16 == 0 and (4 * half) % 128 == 0

        smem = pl.BlockSpec(memory_space=pltpu.SMEM)
        vmem = pl.BlockSpec(memory_space=pltpu.VMEM)
        anywhere = pl.BlockSpec(memory_space=pl.ANY)
        chunks = [
            pltpu.VMEM((2 * n_high, tokens, 4 * half), bf16),
            pltpu.VMEM((2, 2, half, experts), bf16),
            pltpu.SemaphoreType.DMA((2 * n_high,)),
        ]
        params = pltpu.CompilerParams(vmem_limit_bytes=VMEM_LIMIT)

        if in_kernels:
            acts = pltpu.with_memory_space_constraint(acts, pltpu.HBM)

            def products(kernel, blocks, grad_logits):
                shape = pltpu.VMEM((*blocks, n_high, half, experts), bf16)
                return pl.pallas_call(
                    functools.partial(kernel, n_high),
                    out_shape=(shape, shape),
                    in_specs=[smem, anywhere, vmem],
                    out_specs=(vmem, vmem),
                    scratch_shapes=chunks,
                    compiler_params=params,
                )(where, acts, grad_logits)

            away_first, kept_first = products(first_grad_kernel, (2, 2), grad_logits)
            away_first, later = lax.optimization_barrier((away_first, grad_logits))
            away_second, kept_second = products(second_grad_kernel, (4,), later)
        else:
            product = lax.dot_general(
                acts, grad_logits, (((0,), (0,)), ((), ())), preferred_element_type=f32
            ).astype(bf16)
            product = product.reshape(n_high, N_LOW, 2, n_rep, half, experts)

            def block(d_low, owner, d_rep):
                at = (0, low ^ d_low, owner, rep ^ d_rep, 0, 0)
                part = lax.dynamic_slice(product, at, (n_high, 1, 1, 1, half, experts))
                return part.reshape(n_high, half, experts)

            def slot(k, of_core):
                change = k ^ (3 * of_core), parity(k) ^ of_core
                return [block(change[0], c, change[1]) for c in range(2)]

            def both(of_core):
                first = jnp.stack([jnp.stack(slot(k, of_core)) for k in FIRST])
                rest = [block(3, of_core, 1), block(0, of_core, 0)]
                return first, jnp.stack(slot(3, of_core) + rest)

            away_first, away_second = both(1 - core)
            kept_first, kept_second = both(core)

        summed = kept_first.astype(f32) + swap(away_first, "core").astype(f32)
        parts = [to_partner(summed[i].astype(bf16), k) for i, k in enumerate(FIRST)]
        summed = kept_second.astype(f32) + swap(away_second, "core").astype(f32)
        parts.append(to_partner(summed[:2].astype(bf16), 3))
        parts.append(to_corner(summed[2].astype(bf16)))
        *parts, corner = [x.astype(f32) for x in lax.optimization_barrier(parts)]
        total = sum(parts)

        def of_core(x, c):
            return lax.dynamic_index_in_dim(x, c, 0, keepdims=False)

        total = of_core(total, core) + swap(of_core(total, 1 - core), "core") + summed[3] + corner

        grad = None
        for j in range(n_high):
            part = lax.dynamic_index_in_dim(total, high ^ j, 0, keepdims=False)
            if j:
                part = swap(part, "high", j)
            grad = part if grad is None else grad + part

        mine = [
            lax.dynamic_slice_in_dim(a, rep * half, half, 0)
            for a in (master, moment_one, moment_two)
        ]
        weight = adamw(grad, *mine, step_count)[0].astype(bf16)

        column = jnp.stack([swap(weight, "high", j) if j else weight for j in range(n_high)])
        other = swap(grad, "rep")
        across = swap(column, "core")
        across, other = lax.optimization_barrier((across, other))
        chip = jnp.where(first_core, jnp.stack([column, across]), jnp.stack([across, column]))

        whole = jnp.where(
            rep == 0,
            jnp.concatenate([grad, other], 0),
            jnp.concatenate([other, grad], 0),
        )
        state = adamw(whole, master, moment_one, moment_two, step_count)

        got = [to_partner(chip, k) for k in (*FIRST, 3)]
        corner = to_corner(column)
        got[0], state = lax.optimization_barrier((got[0], state))
        got[2], corner = lax.optimization_barrier((got[2], corner))
        over = [swap(x, "core") for x in got]
        corner_over = swap(corner, "core")

        first = [x[i] for i in range(2) for x in (got, over)]
        second = [got[2], over[2], corner[None], corner_over[None], column[None], across[None]]
        stages = ((FIRST, first_place, first), ((3, 0), second_place, second))
        logits = None
        for lows, place, pieces in stages:
            if in_kernels:
                before = [] if logits is None else [logits]
                operands = [
                    pltpu.with_memory_space_constraint(x, pltpu.VMEM) for x in pieces + before
                ]
                logits = pl.pallas_call(
                    functools.partial(logits_kernel, n_high, lows, place),
                    out_shape=jax.ShapeDtypeStruct((tokens, experts), bf16 if before else f32),
                    in_specs=[smem, anywhere] + [vmem] * len(operands),
                    out_specs=vmem,
                    scratch_shapes=[
                        chunks[0],
                        pltpu.VMEM((2, n_high, 2, 2, half, experts), bf16),
                        chunks[2],
                    ],
                    compiler_params=params,
                )(where, acts, *operands)
            else:
                at = jnp.array(lows)
                places = jnp.stack(
                    [
                        (((high ^ j) * N_LOW + (low ^ at[which])) * 2 + owner) * n_rep + of_rep
                        for i in range(len(pieces))
                        for which, owner, of_rep in place(core, rep, i)
                        for j in range(n_high)
                    ]
                )
                received = jnp.concatenate(pieces).reshape(-1, half, experts)
                full = jnp.zeros((2 * received.shape[0], half, experts), bf16)
                full = full.at[places].set(received).reshape(n_seq * rows, experts)
                part = jnp.dot(acts, full, preferred_element_type=f32)
                logits = part if logits is None else (logits + part).astype(bf16)
        return *state, logits

    rows_of, tokens_of = P(AXES[:3], None), P(AXES, None)
    return jax.shard_map(
        per_device,
        mesh=fine,
        in_specs=(tokens_of, tokens_of, rows_of, rows_of, rows_of, P()),
        out_specs=(rows_of, rows_of, rows_of, tokens_of),
        check_vma=False,
    )
```

time: 64 us -> 61.1 us (0.955)
  Pallas kernels: 2.96 us -> 12.3 us
  other arithmetic: 8.37 us -> 1.45 us
  matrix products: 2.93 us -> 0 us
  waiting for transfers between devices: 25.7 us -> 23.2 us
  starting transfers between devices: 19.2 us -> 21.4 us
  local copies, waits for them, and re-layouts: 2.91 us -> 0.95 us
    pallas_call x2 -> x4, Pallas kernels: 2.96 us -> 12.3 us  [the longest x2 6.29 us: products(): pl.pallas_call(functools.partial(kernel, n_high), out_shape=(shape, shape...]
    ppermute x8, starting transfers between devices: 11.8 us -> 15.3 us  [cube_swap(): return lax.ppermute(x, AXES[1:], pairs)]
    dot_general x1 -> x0, matrix products: 2.93 us -> none  [per_device(): lax.dot_general(acts, grad_logits, (((0,), (0,)), ((), ())), preferred_el...]
    ppermute x11, waiting for transfers between devices: 13.4 us -> 10.8 us  [swap(): lax.ppermute(x, axis, [(i, i ^ mask) for i in range(fine.shape[axis])])]
    add x2, other arithmetic: 2.36 us -> 0.1 us  [the longest x1 0.07 us: per_device(): total = sum(parts)]
    ppermute x11, starting transfers between devices: 7.43 us -> 6.08 us  [swap(): lax.ppermute(x, axis, [(i, i ^ mask) for i in range(fine.shape[axis])])]
    unnamed x8, local copies, waits for them, and re-layouts: 2.17 us -> 0.86 us
    sub x1, other arithmetic: 2.01 us -> 0.89 us  [adamw(): master - 0.01 * (first_hat / (jnp.sqrt(second_hat) + 1e-08) + 0.1 * master)]
  transfers between devices with their start and end apart: 19 -> 19, of which waited for: 11 -> 7; matrix products, arithmetic and copies ran while one was open for 4% -> 2% of each run, Pallas kernels for 2% -> 10%
where the time goes in v7:
time: 61.1 us; the launch traced here: 60.8 us
  waiting for transfers between devices  23.2 us (38%)
  starting transfers between devices  21.4 us (35%)
  Pallas kernels  12.3 us (20%)
  between operations  1.56 us (3%)
  other arithmetic  1.45 us (2%)
  local copies, waits for them, and re-layouts  0.95 us (2%)
    ppermute x8, starting transfers between devices, cube_swap(): return lax.ppermute(x, AXES[1:], pairs)  15.3 us
    ppermute x8, waiting for transfers between devices, cube_swap(): return lax.ppermute(x, AXES[1:], pairs)  12.4 us
    ppermute x11, waiting for transfers between devices, swap(): lax.ppermute(x, axis, [(i, i ^ mask) for i in range(fine.shape[axis])])  10.8 us
    pallas_call x2, Pallas kernels, products(): pl.pallas_call(functools.partial(kernel, n_high), out_shape=(shape, shape...  6.29 us
    ppermute x11, starting transfers between devices, swap(): lax.ppermute(x, axis, [(i, i ^ mask) for i in range(fine.shape[axis])])  6.08 us
    pallas_call x2, Pallas kernels, per_device(): pl.pallas_call(functools.partial(logits_kernel, n_high, lows, place), out...  6.01 us
  transfers between devices with their start and end apart: 19, of which 7 were waited for; matrix products, arithmetic and copies ran while one was open for 2% of the time, Pallas kernels for 10%

profile of v7, /device:TPU:0, one launch (start us, length us, event | category | flops | bytes accessed | tf_op | source)
XLA Modules:
  0.0 60.8 jit_solution(16357361519074306071)
XLA Ops:
  0.7 0.8 %copy-done = bf16[256,128]{1,0:T(8,128)(2,1)S(1)} copy-done((bf16[256,128]{1,0:T(8,128)(2,1)S(1)}, bf16[256,128]{1,0:T(8,128)(2,1)}, u32[]{:S(2)}) %copy-start) | copy-done | bytes 65560
  1.6 3.1 %shard_map.93 = (bf16[2,2,2,192,128]{4,3,2,1,0:T(8,128)(2,1)S(1)}, bf16[2,2,2,192,128]{4,3,2,1,0:T(8,128)(2,1)S(1)}) custom-call(s32[4]{0:T(128)S(1)} %pad_add_fusion.where_ref, bf16[256,6144]{1,0:T(8,128)(2,1)} %acts_ref.7, bf16[256,128]{1,0:T(8,128)(2,1)S(1)} %copy-done), custom_call_target="tpu_custom_call" | custom-call | tf_op jit(solution)/shard_map/pallas_call | solution.py:168
  4.7 0.5 collective-permute-start
  5.2 3.1 %shard_map.94 = (bf16[4,2,192,128]{3,2,1,0:T(8,128)(2,1)S(1)}, bf16[4,2,192,128]{3,2,1,0:T(8,128)(2,1)S(1)}) custom-call(s32[4]{0:T(128)S(1)} %pad_add_fusion.where_ref, bf16[256,6144]{1,0:T(8,128)(2,1)} %acts_ref.7, bf16[256,128]{1,0:T(8,128)(2,1)S(1)} %copy-done), custom_call_target="tpu_custom_call" | custom-call | tf_op jit(solution)/shard_map/pallas_call | solution.py:168
  8.7 4.0 %collective-permute-start.2 = (bf16[2,2,192,128]{3,2,1,0:T(8,128)(2,1)S(1)}, bf16[2,2,192,128]{3,2,1,0:T(8,128)(2,1)S(1)}, u32[]{:S(2)}, u32[]{:S(2)}) collective-permute-start(bf16[2,2,192,128]{3,2,1,0:T(8,128)(2,1)S(1)} %get-tuple-element.47), channel_id=1, source_target_pairs={{0,9},{1,8},{2,6},{3,7},{4,13},{5,12},{6,2},{7,3},{8,1},{9,0},{10,... | collective-permute-start | bytes 589832 | tf_op jit(solution)/shard_map/ppermute | solution.py:135
  12.7 1.4 %collective-permute-start.1 = (bf16[2,2,192,128]{3,2,1,0:T(8,128)(2,1)S(1)}, bf16[2,2,192,128]{3,2,1,0:T(8,128)(2,1)S(1)}, u32[]{:S(2)}, u32[]{:S(2)}) collective-permute-start(bf16[2,2,192,128]{3,2,1,0:T(8,128)(2,1)S(1)} %get-tuple-element.48), channel_id=1, source_target_pairs={{0,5},{1,4},{2,10},{3,11},{4,1},{5,0},{6,14},{7,15},{8,13},{9,12},... | collective-permute-start | bytes 589832 | tf_op jit(solution)/shard_map/ppermute | solution.py:135
  14.5 3.8 %collective-permute-start.5 = (bf16[2,192,128]{2,1,0:T(8,128)(2,1)S(1)}, bf16[2,192,128]{2,1,0:T(8,128)(2,1)S(1)}, u32[]{:S(2)}, u32[]{:S(2)}) collective-permute-start(bf16[2,192,128]{2,1,0:T(8,128)(2,1)S(1)} %slice_bitcast_fusion.3), channel_id=1, source_target_pairs={{0,13},{1,12},{2,15},{3,14},{4,9},{5,8},{6,11},{7,10},{8,5},{9,4},... | collective-permute-start | bytes 294920 | tf_op jit(solution)/shard_map/ppermute | solution.py:135
  18.3 5.0 %collective-permute-done.5 = bf16[2,192,128]{2,1,0:T(8,128)(2,1)S(1)} collective-permute-done((bf16[2,192,128]{2,1,0:T(8,128)(2,1)S(1)}, bf16[2,192,128]{2,1,0:T(8,128)(2,1)S(1)}, u32[]{:S(2)}, u32[]{:S(2)}) %collective-permute-start.5) | collective-permute-done | bytes 98336 | tf_op jit(solution)/shard_map/ppermute | solution.py:135
  24.1 1.4 %collective-permute-done.6 = f32[2,192,128]{2,1,0:T(8,128)S(1)} collective-permute-done((f32[2,192,128]{2,1,0:T(8,128)S(1)}, f32[2,192,128]{2,1,0:T(8,128)S(1)}, u32[]{:S(2)}, u32[]{:S(2)}) %collective-permute-start.6) | collective-permute-done | bytes 196640 | tf_op jit(solution)/shard_map/ppermute | solution.py:125
  25.6 3.0 %collective-permute-start.7 = (f32[192,128]{1,0:T(8,128)S(1)}, f32[192,128]{1,0:T(8,128)S(1)}, u32[]{:S(2)}, u32[]{:S(2)}) collective-permute-start(f32[192,128]{1,0:T(8,128)S(1)} %dynamic-slice_bitcast_fusion.1), channel_id=1, source_target_pairs={{0,16},{16,0},{1,17},{17,1},{2,18},{18,2},{3,19},{19,3},{4,20},{20... | collective-permute-start | bytes 294920 | tf_op jit(solution)/shard_map/ppermute | solution.py:125
  29.3 4.5 %collective-permute-done.7 = f32[192,128]{1,0:T(8,128)S(1)} collective-permute-done((f32[192,128]{1,0:T(8,128)S(1)}, f32[192,128]{1,0:T(8,128)S(1)}, u32[]{:S(2)}, u32[]{:S(2)}) %collective-permute-start.7) | collective-permute-done | bytes 98336 | tf_op jit(solution)/shard_map/ppermute | solution.py:125
  33.9 0.7 %collective-permute-start.8 = (bf16[192,128]{1,0:T(8,128)(2,1)S(1)}, bf16[192,128]{1,0:T(8,128)(2,1)S(1)}, u32[]{:S(2)}, u32[]{:S(2)}) collective-permute-start(bf16[192,128]{1,0:T(8,128)(2,1)S(1)} %get-tuple-element.43), channel_id=1, source_target_pairs={{0,16},{16,0},{1,17},{17,1},{2,18},{18,2},{3,19},{19,3},{4,20},{20... | collective-permute-start | bytes 147464 | tf_op jit(solution)/shard_map/ppermute | solution.py:125
  34.6 0.6 collective-permute-start.10
  35.2 4.2 %collective-permute-done.8 = bf16[192,128]{1,0:T(8,128)(2,1)S(1)} collective-permute-done((bf16[192,128]{1,0:T(8,128)(2,1)S(1)}, bf16[192,128]{1,0:T(8,128)(2,1)S(1)}, u32[]{:S(2)}, u32[]{:S(2)}) %collective-permute-start.8) | collective-permute-done | bytes 49184 | tf_op jit(solution)/shard_map/ppermute | solution.py:125
  39.5 1.3 %collective-permute-start.13 = (bf16[2,192,128]{2,1,0:T(8,128)(2,1)S(1)}, bf16[2,192,128]{2,1,0:T(8,128)(2,1)S(1)}, u32[]{:S(2)}, u32[]{:S(2)}) collective-permute-start(bf16[2,192,128]{2,1,0:T(8,128)(2,1)S(1)} %get-tuple-element.50), channel_id=1, source_target_pairs={{0,13},{1,12},{2,15},{3,14},{4,9},{5,8},{6,11},{7,10},{8,5},{9,4},... | collective-permute-start | bytes 294920 | tf_op jit(solution)/shard_map/ppermute | solution.py:135
  40.9 2.3 %collective-permute-start.17 = (bf16[2,2,192,128]{3,2,1,0:T(8,128)(2,1)S(1)}, bf16[2,2,192,128]{3,2,1,0:T(8,128)(2,1)S(1)}, u32[]{:S(2)}, u32[]{:S(2)}) collective-permute-start(bf16[2,2,192,128]{3,2,1,0:T(8,128)(2,1)S(1)} %maximum_select_fusion), channel_id=1, source_target_pairs={{0,9},{1,8},{2,6},{3,7},{4,13},{5,12},{6,2},{7,3},{8,1},{9,0},{10,... | collective-permute-start | bytes 589832 | tf_op jit(solution)/shard_map/ppermute | solution.py:135
  43.2 0.8 %collective-permute-start.12 = (bf16[2,2,192,128]{3,2,1,0:T(8,128)(2,1)S(1)}, bf16[2,2,192,128]{3,2,1,0:T(8,128)(2,1)S(1)}, u32[]{:S(2)}, u32[]{:S(2)}) collective-permute-start(bf16[2,2,192,128]{3,2,1,0:T(8,128)(2,1)S(1)} %maximum_select_fusion), channel_id=1, source_target_pairs={{0,12},{1,13},{2,3},{3,2},{4,8},{5,9},{6,7},{7,6},{8,4},{9,5},{10,... | collective-permute-start | bytes 589832 | tf_op jit(solution)/shard_map/ppermute | solution.py:135
  44.0 1.4 %collective-permute-start.11 = (bf16[2,2,192,128]{3,2,1,0:T(8,128)(2,1)S(1)}, bf16[2,2,192,128]{3,2,1,0:T(8,128)(2,1)S(1)}, u32[]{:S(2)}, u32[]{:S(2)}) collective-permute-start(bf16[2,2,192,128]{3,2,1,0:T(8,128)(2,1)S(1)} %maximum_select_fusion), channel_id=1, source_target_pairs={{0,5},{1,4},{2,10},{3,11},{4,1},{5,0},{6,14},{7,15},{8,13},{9,12},... | collective-permute-start | bytes 589832 | tf_op jit(solution)/shard_map/ppermute | solution.py:135
  45.3 0.9 %multiply_subtract_fusion = (f32[384,128]{1,0:T(8,128)}, f32[384,128]{1,0:T(8,128)}, f32[384,128]{1,0:T(8,128)}) fusion(f32[384,128]{1,0:T(8,128)S(1)} %copy-done.1, f32[]{:T(128)} %bitcast.13, f32[]{:T(128)} %bitcast.12, f32[192,128]{1,0:T(8,128)S(1)} %get-tuple-element.44, f32[192,128]{1,0:T(8,128)S(1)} %collective-permute-done.10, pred[]{:T(512)S(6)} %eq.7, ...), kind=kLoop, calls=%fused_computation.13 | loop fusion | flops 884736 | bytes 1376265 | tf_op jit(solution)/shard_map/sub | solution.py:29
  46.2 6.8 %collective-permute-done.11.refs_0_ = bf16[2,2,192,128]{3,2,1,0:T(8,128)(2,1)S(1)} collective-permute-done((bf16[2,2,192,128]{3,2,1,0:T(8,128)(2,1)S(1)}, bf16[2,2,192,128]{3,2,1,0:T(8,128)(2,1)S(1)}, u32[]{:S(2)}, u32[]{:S(2)}) %collective-permute-start.11) | collective-permute-done | bytes 196640 | tf_op jit(solution)/shard_map/ppermute | solution.py:135
  53.1 0.5 collective-permute-start.18
  54.1 0.7 %collective-permute-done.18.refs_3_ = bf16[2,2,192,128]{3,2,1,0:T(8,128)(2,1)S(1)} collective-permute-done((bf16[2,2,192,128]{3,2,1,0:T(8,128)(2,1)S(1)}, bf16[2,2,192,128]{3,2,1,0:T(8,128)(2,1)S(1)}, u32[]{:S(2)}, u32[]{:S(2)}) %collective-permute-start.18) | collective-permute-done | bytes 196640 | tf_op jit(solution)/shard_map/ppermute | solution.py:125
  54.8 2.6 %shard_map.95.refs_6_ = f32[256,128]{1,0:T(8,128)S(1)} custom-call(s32[4]{0:T(128)S(1)} %pad_add_fusion.where_ref, bf16[256,6144]{1,0:T(8,128)(2,1)} %acts_ref.7, bf16[2,2,192,128]{3,2,1,0:T(8,128)(2,1)S(1)} %collective-permute-done.11.refs_0_, bf16[2,2,192,128]{3,2,1,0:T(8,128)(2,1)S(1)} %collective-permute-done.16.refs_1_, ...), custom_call_target="tpu_custom_call" | custom-call | tf_op jit(solution)/shard_map/pallas_call | solution.py:259
  57.4 3.4 %shard_map.96 = bf16[256,128]{1,0:T(8,128)(2,1)} custom-call(s32[4]{0:T(128)S(1)} %pad_add_fusion.where_ref, bf16[256,6144]{1,0:T(8,128)(2,1)} %acts_ref.7, bf16[2,2,192,128]{3,2,1,0:T(8,128)(2,1)S(1)} %collective-permute-done.12.refs_0_, bf16[2,2,192,128]{3,2,1,0:T(8,128)(2,1)S(1)} %collective-permute-done.14.refs_1_, ...), custom_call_target="tpu_custom_call" | custom-call | tf_op jit(solution)/shard_map/pallas_call | solution.py:259
  (40 shorter events, 2.1 us)
Async XLA Ops:
  0.7 0.8 %copy-start = (bf16[256,128]{1,0:T(8,128)(2,1)S(1)}, bf16[256,128]{1,0:T(8,128)(2,1)}, u32[]{:S(2)}) copy-start(bf16[256,128]{1,0:T(8,128)(2,1)} %grad_ref.2) | copy-start | bytes 196612
  4.7 3.8 %collective-permute-start = (bf16[2,2,2,192,128]{4,3,2,1,0:T(8,128)(2,1)S(1)}, bf16[2,2,2,192,128]{4,3,2,1,0:T(8,128)(2,1)S(1)}, u32[]{:S(2)}, u32[]{:S(2)}) collective-permute-start(bf16[2,2,2,192,128]{4,3,2,1,0:T(8,128)(2,1)S(1)} %get-tuple-element.24), channel_id=1, source_target_pairs={{0,2},{2,0},{1,3},{3,1},{4,6},{6,4},{5,7},{7,5},{8,10},{10,8},{9,1... | collective-permute-start | bytes 1179656 | tf_op jit(solution)/shard_map/ppermute | solution.py:125
  8.4 5.8 %collective-permute-start.3 = (bf16[4,2,192,128]{3,2,1,0:T(8,128)(2,1)S(1)}, bf16[4,2,192,128]{3,2,1,0:T(8,128)(2,1)S(1)}, u32[]{:S(2)}, u32[]{:S(2)}) collective-permute-start(bf16[4,2,192,128]{3,2,1,0:T(8,128)(2,1)S(1)} %get-tuple-element.27), channel_id=1, source_target_pairs={{0,2},{2,0},{1,3},{3,1},{4,6},{6,4},{5,7},{7,5},{8,10},{10,8},{9,1... | collective-permute-start | bytes 1179656 | tf_op jit(solution)/shard_map/ppermute | solution.py:125
  8.6 25.1 %copy-start.1 = (f32[384,128]{1,0:T(8,128)S(1)}, f32[384,128]{1,0:T(8,128)}, u32[]{:S(2)}) copy-start(f32[384,128]{1,0:T(8,128)} %param.8) | copy-start | bytes 589828
  8.6 25.1 %copy-start.2 = (f32[384,128]{1,0:T(8,128)S(1)}, f32[384,128]{1,0:T(8,128)}, u32[]{:S(2)}) copy-start(f32[384,128]{1,0:T(8,128)} %param.10) | copy-start | bytes 589828
  8.6 25.1 %copy-start.3 = (f32[384,128]{1,0:T(8,128)S(1)}, f32[384,128]{1,0:T(8,128)}, u32[]{:S(2)}) copy-start(f32[384,128]{1,0:T(8,128)} %param.9) | copy-start | bytes 589828
  8.7 14.7 %collective-permute-start.2 = (bf16[2,2,192,128]{3,2,1,0:T(8,128)(2,1)S(1)}, bf16[2,2,192,128]{3,2,1,0:T(8,128)(2,1)S(1)}, u32[]{:S(2)}, u32[]{:S(2)}) collective-permute-start(bf16[2,2,192,128]{3,2,1,0:T(8,128)(2,1)S(1)} %get-tuple-element.47), channel_id=1, source_target_pairs={{0,9},{1,8},{2,6},{3,7},{4,13},{5,12},{6,2},{7,3},{8,1},{9,0},{10,... | collective-permute-start | bytes 589832 | tf_op jit(solution)/shard_map/ppermute | solution.py:135
  12.7 11.1 %collective-permute-start.1 = (bf16[2,2,192,128]{3,2,1,0:T(8,128)(2,1)S(1)}, bf16[2,2,192,128]{3,2,1,0:T(8,128)(2,1)S(1)}, u32[]{:S(2)}, u32[]{:S(2)}) collective-permute-start(bf16[2,2,192,128]{3,2,1,0:T(8,128)(2,1)S(1)} %get-tuple-element.48), channel_id=1, source_target_pairs={{0,5},{1,4},{2,10},{3,11},{4,1},{5,0},{6,14},{7,15},{8,13},{9,12},... | collective-permute-start | bytes 589832 | tf_op jit(solution)/shard_map/ppermute | solution.py:135
  14.3 9.5 %collective-permute-start.4 = (bf16[2,2,192,128]{3,2,1,0:T(8,128)(2,1)S(1)}, bf16[2,2,192,128]{3,2,1,0:T(8,128)(2,1)S(1)}, u32[]{:S(2)}, u32[]{:S(2)}) collective-permute-start(bf16[2,2,192,128]{3,2,1,0:T(8,128)(2,1)S(1)} %slice.26), channel_id=1, source_target_pairs={{0,12},{1,13},{2,3},{3,2},{4,8},{5,9},{6,7},{7,6},{8,4},{9,5},{10,... | collective-permute-start | bytes 589832 | tf_op jit(solution)/shard_map/ppermute | solution.py:135
  14.5 8.9 %collective-permute-start.5 = (bf16[2,192,128]{2,1,0:T(8,128)(2,1)S(1)}, bf16[2,192,128]{2,1,0:T(8,128)(2,1)S(1)}, u32[]{:S(2)}, u32[]{:S(2)}) collective-permute-start(bf16[2,192,128]{2,1,0:T(8,128)(2,1)S(1)} %slice_bitcast_fusion.3), channel_id=1, source_target_pairs={{0,13},{1,12},{2,15},{3,14},{4,9},{5,8},{6,11},{7,10},{8,5},{9,4},... | collective-permute-start | bytes 294920 | tf_op jit(solution)/shard_map/ppermute | solution.py:135
  24.0 1.5 %collective-permute-start.6 = (f32[2,192,128]{2,1,0:T(8,128)S(1)}, f32[2,192,128]{2,1,0:T(8,128)S(1)}, u32[]{:S(2)}, u32[]{:S(2)}) collective-permute-start(f32[2,192,128]{2,1,0:T(8,128)S(1)} %dynamic-slice_bitcast_fusion), channel_id=1, source_target_pairs={{0,2},{2,0},{1,3},{3,1},{4,6},{6,4},{5,7},{7,5},{8,10},{10,8},{9,1... | collective-permute-start | bytes 589832 | tf_op jit(solution)/shard_map/ppermute | solution.py:125
  25.6 8.2 %collective-permute-start.7 = (f32[192,128]{1,0:T(8,128)S(1)}, f32[192,128]{1,0:T(8,128)S(1)}, u32[]{:S(2)}, u32[]{:S(2)}) collective-permute-start(f32[192,128]{1,0:T(8,128)S(1)} %dynamic-slice_bitcast_fusion.1), channel_id=1, source_target_pairs={{0,16},{16,0},{1,17},{17,1},{2,18},{18,2},{3,19},{19,3},{4,20},{20... | collective-permute-start | bytes 294920 | tf_op jit(solution)/shard_map/ppermute | solution.py:125
  33.9 5.5 %collective-permute-start.8 = (bf16[192,128]{1,0:T(8,128)(2,1)S(1)}, bf16[192,128]{1,0:T(8,128)(2,1)S(1)}, u32[]{:S(2)}, u32[]{:S(2)}) collective-permute-start(bf16[192,128]{1,0:T(8,128)(2,1)S(1)} %get-tuple-element.43), channel_id=1, source_target_pairs={{0,16},{16,0},{1,17},{17,1},{2,18},{18,2},{3,19},{19,3},{4,20},{20... | collective-permute-start | bytes 147464 | tf_op jit(solution)/shard_map/ppermute | solution.py:125
  34.6 6.3 %collective-permute-start.10 = (f32[192,128]{1,0:T(8,128)S(1)}, f32[192,128]{1,0:T(8,128)S(1)}, u32[]{:S(2)}, u32[]{:S(2)}) collective-permute-start(f32[192,128]{1,0:T(8,128)S(1)} %get-tuple-element.44), channel_id=1, source_target_pairs={{0,1},{1,0},{2,3},{3,2},{4,5},{5,4},{6,7},{7,6},{8,9},{9,8},{10,11... | collective-permute-start | bytes 294920 | tf_op jit(solution)/shard_map/ppermute | solution.py:125
  39.4 1.4 %collective-permute-start.9 = (bf16[2,192,128]{2,1,0:T(8,128)(2,1)S(1)}, bf16[2,192,128]{2,1,0:T(8,128)(2,1)S(1)}, u32[]{:S(2)}, u32[]{:S(2)}) collective-permute-start(bf16[2,192,128]{2,1,0:T(8,128)(2,1)S(1)} %get-tuple-element.50), channel_id=1, source_target_pairs={{0,2},{2,0},{1,3},{3,1},{4,6},{6,4},{5,7},{7,5},{8,10},{10,8},{9,1... | collective-permute-start | bytes 294920 | tf_op jit(solution)/shard_map/ppermute | solution.py:125
  39.5 14.1 %collective-permute-start.13 = (bf16[2,192,128]{2,1,0:T(8,128)(2,1)S(1)}, bf16[2,192,128]{2,1,0:T(8,128)(2,1)S(1)}, u32[]{:S(2)}, u32[]{:S(2)}) collective-permute-start(bf16[2,192,128]{2,1,0:T(8,128)(2,1)S(1)} %get-tuple-element.50), channel_id=1, source_target_pairs={{0,13},{1,12},{2,15},{3,14},{4,9},{5,8},{6,11},{7,10},{8,5},{9,4},... | collective-permute-start | bytes 294920 | tf_op jit(solution)/shard_map/ppermute | solution.py:135
  40.9 12.2 %collective-permute-start.17 = (bf16[2,2,192,128]{3,2,1,0:T(8,128)(2,1)S(1)}, bf16[2,2,192,128]{3,2,1,0:T(8,128)(2,1)S(1)}, u32[]{:S(2)}, u32[]{:S(2)}) collective-permute-start(bf16[2,2,192,128]{3,2,1,0:T(8,128)(2,1)S(1)} %maximum_select_fusion), channel_id=1, source_target_pairs={{0,9},{1,8},{2,6},{3,7},{4,13},{5,12},{6,2},{7,3},{8,1},{9,0},{10,... | collective-permute-start | bytes 589832 | tf_op jit(solution)/shard_map/ppermute | solution.py:135
  43.2 10.4 %collective-permute-start.12 = (bf16[2,2,192,128]{3,2,1,0:T(8,128)(2,1)S(1)}, bf16[2,2,192,128]{3,2,1,0:T(8,128)(2,1)S(1)}, u32[]{:S(2)}, u32[]{:S(2)}) collective-permute-start(bf16[2,2,192,128]{3,2,1,0:T(8,128)(2,1)S(1)} %maximum_select_fusion), channel_id=1, source_target_pairs={{0,12},{1,13},{2,3},{3,2},{4,8},{5,9},{6,7},{7,6},{8,4},{9,5},{10,... | collective-permute-start | bytes 589832 | tf_op jit(solution)/shard_map/ppermute | solution.py:135
  44.0 9.1 %collective-permute-start.11 = (bf16[2,2,192,128]{3,2,1,0:T(8,128)(2,1)S(1)}, bf16[2,2,192,128]{3,2,1,0:T(8,128)(2,1)S(1)}, u32[]{:S(2)}, u32[]{:S(2)}) collective-permute-start(bf16[2,2,192,128]{3,2,1,0:T(8,128)(2,1)S(1)} %maximum_select_fusion), channel_id=1, source_target_pairs={{0,5},{1,4},{2,10},{3,11},{4,1},{5,0},{6,14},{7,15},{8,13},{9,12},... | collective-permute-start | bytes 589832 | tf_op jit(solution)/shard_map/ppermute | solution.py:135
  53.1 1.7 %collective-permute-start.16 = (bf16[2,2,192,128]{3,2,1,0:T(8,128)(2,1)S(1)}, bf16[2,2,192,128]{3,2,1,0:T(8,128)(2,1)S(1)}, u32[]{:S(2)}, u32[]{:S(2)}) collective-permute-start(bf16[2,2,192,128]{3,2,1,0:T(8,128)(2,1)S(1)} %collective-permute-done.11.refs_0_), channel_id=1, source_target_pairs={{0,2},{2,0},{1,3},{3,1},{4,6},{6,4},{5,7},{7,5},{8,10},{10,8},{9,1... | collective-permute-start | bytes 589832 | tf_op jit(solution)/shard_map/ppermute | solution.py:125
  53.1 1.7 %collective-permute-start.18 = (bf16[2,2,192,128]{3,2,1,0:T(8,128)(2,1)S(1)}, bf16[2,2,192,128]{3,2,1,0:T(8,128)(2,1)S(1)}, u32[]{:S(2)}, u32[]{:S(2)}) collective-permute-start(bf16[2,2,192,128]{3,2,1,0:T(8,128)(2,1)S(1)} %collective-permute-done.17.refs_2_), channel_id=1, source_target_pairs={{0,2},{2,0},{1,3},{3,1},{4,6},{6,4},{5,7},{7,5},{8,10},{10,8},{9,1... | collective-permute-start | bytes 589832 | tf_op jit(solution)/shard_map/ppermute | solution.py:125
  53.6 3.9 %collective-permute-start.14 = (bf16[2,2,192,128]{3,2,1,0:T(8,128)(2,1)S(1)}, bf16[2,2,192,128]{3,2,1,0:T(8,128)(2,1)S(1)}, u32[]{:S(2)}, u32[]{:S(2)}) collective-permute-start(bf16[2,2,192,128]{3,2,1,0:T(8,128)(2,1)S(1)} %collective-permute-done.12.refs_0_), channel_id=1, source_target_pairs={{0,2},{2,0},{1,3},{3,1},{4,6},{6,4},{5,7},{7,5},{8,10},{10,8},{9,1... | collective-permute-start | bytes 589832 | tf_op jit(solution)/shard_map/ppermute | solution.py:125
  53.7 3.8 %collective-permute-start.15 = (bf16[2,192,128]{2,1,0:T(8,128)(2,1)S(1)}, bf16[2,192,128]{2,1,0:T(8,128)(2,1)S(1)}, u32[]{:S(2)}, u32[]{:S(2)}) collective-permute-start(bf16[2,192,128]{2,1,0:T(8,128)(2,1)S(1)} %collective-permute-done.13), channel_id=1, source_target_pairs={{0,2},{2,0},{1,3},{3,1},{4,6},{6,4},{5,7},{7,5},{8,10},{10,8},{9,1... | collective-permute-start | bytes 294920 | tf_op jit(solution)/shard_map/ppermute | solution.py:125

commit v8 on v7

--- a/solution.py
+++ b/solution.py
@@ -43,60 +43,73 @@
     return copies
 
 
-def partial_products(copies, chunks, grad_ref, blocks):
+def grad_kernel(n_high, where_ref, acts_ref, grad_ref, *refs):
+    state_refs, refs = refs[:3], refs[3:]
+    away_first, kept_first, away_second, kept_second, mine_ref, chunks, logit_grads, blocks, sems = refs
+    _, low, core, rep = [where_ref[i] for i in range(4)]
+    half = blocks.shape[2]
+    last = sems.shape[0]
+    loads = pltpu.make_async_copy(grad_ref, logit_grads, sems.at[last - 1])
+    loads.start()
+    at = [low ^ k for k in FIRST] + [low ^ (3 * (1 - core)), low ^ (3 * core)]
+    copies = load_columns(acts_ref, chunks, sems, 0, at, n_high)
+    rows = pl.ds(pl.multiple_of(rep * half, half), half)
+    state = [
+        pltpu.make_async_copy(ref.at[rows], mine_ref.at[i], sems.at[last - 4 + i])
+        for i, ref in enumerate(state_refs)
+    ]
+    for copy in state:
+        copy.start()
+    loads.wait()
     for n, copy in enumerate(copies):
         copy.wait()
         product = lax.dot_general(
-            chunks[n], grad_ref[...], (((0,), (0,)), ((), ())), preferred_element_type=jnp.float32
+            chunks[n], logit_grads[...], (((0,), (0,)), ((), ())), preferred_element_type=jnp.float32
         )
         blocks[...] = product.astype(blocks.dtype).reshape(blocks.shape)
-        yield n
-
-
-def first_grad_kernel(n_high, where_ref, acts_ref, grad_ref, away_ref, kept_ref, chunks, blocks, sems):
-    _, low, core, rep = [where_ref[i] for i in range(4)]
-    copies = load_columns(acts_ref, chunks, sems, 0, [low ^ k for k in FIRST], n_high)
-    for n in partial_products(copies, chunks, grad_ref, blocks):
         p, j = divmod(n, n_high)
-        flip = rep ^ core ^ parity(FIRST[p])
-        for c in range(2):
-            kept_ref[p ^ core, c, j] = blocks[c, flip]
-            away_ref[p ^ core ^ 1, c, j] = blocks[c, flip ^ 1]
-
-
-def second_grad_kernel(n_high, where_ref, acts_ref, grad_ref, away_ref, kept_ref, chunks, blocks, sems):
-    _, low, core, rep = [where_ref[i] for i in range(4)]
-    at = [low ^ (3 * (1 - core)), low ^ (3 * core)]
-    copies = load_columns(acts_ref, chunks, sems, 0, at, n_high)
-    for n in partial_products(copies, chunks, grad_ref, blocks):
-        p, j = divmod(n, n_high)
-        slot_ref = kept_ref if p == 0 else away_ref
-        flip = rep ^ core ^ p
-        for c in range(2):
-            slot_ref[c, j] = blocks[c, flip]
-        kept_ref[2 + (core ^ p), j] = blocks[core, flip ^ 1]
-        away_ref[2 + (core ^ p), j] = blocks[core ^ 1, flip ^ 1]
-
-
-def logits_kernel(n_high, lows, place, where_ref, acts_ref, *refs):
-    *pieces, out_ref, chunks, weight, sems = refs
+        if p < 2:
+            flip = rep ^ core ^ parity(FIRST[p])
+            for c in range(2):
+                kept_first[p ^ core, c, j] = blocks[c, flip]
+                away_first[p ^ core ^ 1, c, j] = blocks[c, flip ^ 1]
+        else:
+            p = p - 2
+            slot = kept_second if p == 0 else away_second
+            flip = rep ^ core ^ p
+            for c in range(2):
+                slot[c, j] = blocks[c, flip]
+            kept_second[2 + (core ^ p), j] = blocks[core, flip ^ 1]
+            away_second[2 + (core ^ p), j] = blocks[core ^ 1, flip ^ 1]
+    for copy in state:
+        copy.wait()
+
+
+def columns_kernel(n_high, where_ref, acts_ref, first_ref, second_ref, sems):
+    high, low = where_ref[0], where_ref[1]
+    copies = []
+    for i, (lows, out) in enumerate(((FIRST, first_ref), ((3, 0), second_ref))):
+        copies += load_columns(acts_ref, out, sems.at[i], high, [low ^ k for k in lows], n_high)
+    for copy in copies:
+        copy.wait()
+
+
+def logits_kernel(n_high, place, where_ref, columns_ref, *refs):
+    *pieces, out_ref, weight = refs
     before = None
     if len(pieces[-1].shape) == 2:
         *pieces, before = pieces
-    high, low, core, rep = [where_ref[i] for i in range(4)]
-    copies = load_columns(acts_ref, chunks, sems, high, [low ^ k for k in lows], n_high)
+    core, rep = where_ref[2], where_ref[3]
     half, experts = weight.shape[-2:]
     for i, piece in enumerate(pieces):
-        for b, (slot, owner, of_rep) in enumerate(place(core, rep, i)):
+        for b, (chip, owner, of_rep) in enumerate(place(core, rep, i)):
             for j in range(n_high):
-                weight[slot, j, owner, of_rep] = piece[b, j]
+                weight[chip, j, owner, of_rep] = piece[b, j]
     total = None if before is None else before[...]
-    for n, copy in enumerate(copies):
-        slot, j = divmod(n, n_high)
-        copy.wait()
+    for n in range(2 * n_high):
         part = jnp.dot(
-            chunks[n],
-            weight[slot, j].reshape(4 * half, experts),
+            columns_ref[n],
+            weight[n // n_high, n % n_high].reshape(4 * half, experts),
             preferred_element_type=jnp.float32,
         )
         total = part if total is None else total + part
@@ -153,30 +166,31 @@
         smem = pl.BlockSpec(memory_space=pltpu.SMEM)
         vmem = pl.BlockSpec(memory_space=pltpu.VMEM)
         anywhere = pl.BlockSpec(memory_space=pl.ANY)
-        chunks = [
-            pltpu.VMEM((2 * n_high, tokens, 4 * half), bf16),
-            pltpu.VMEM((2, 2, half, experts), bf16),
-            pltpu.SemaphoreType.DMA((2 * n_high,)),
-        ]
         params = pltpu.CompilerParams(vmem_limit_bytes=VMEM_LIMIT)
+        state_in = (master, moment_one, moment_two)
 
         if in_kernels:
             acts = pltpu.with_memory_space_constraint(acts, pltpu.HBM)
-
-            def products(kernel, blocks, grad_logits):
-                shape = pltpu.VMEM((*blocks, n_high, half, experts), bf16)
-                return pl.pallas_call(
-                    functools.partial(kernel, n_high),
-                    out_shape=(shape, shape),
-                    in_specs=[smem, anywhere, vmem],
-                    out_specs=(vmem, vmem),
-                    scratch_shapes=chunks,
-                    compiler_params=params,
-                )(where, acts, grad_logits)
-
-            away_first, kept_first = products(first_grad_kernel, (2, 2), grad_logits)
-            away_first, later = lax.optimization_barrier((away_first, grad_logits))
-            away_second, kept_second = products(second_grad_kernel, (4,), later)
+            first_shape = pltpu.VMEM((2, 2, n_high, half, experts), bf16)
+            second_shape = pltpu.VMEM((4, n_high, half, experts), bf16)
+            away_first, kept_first, away_second, kept_second, mine = pl.pallas_call(
+                functools.partial(grad_kernel, n_high),
+                out_shape=(first_shape, first_shape, second_shape, second_shape)
+                + (pltpu.VMEM((3, half, experts), f32),),
+                in_specs=[smem] + [anywhere] * 5,
+                out_specs=(vmem,) * 5,
+                scratch_shapes=[
+                    pltpu.VMEM((4 * n_high, tokens, 4 * half), bf16),
+                    pltpu.VMEM((tokens, experts), bf16),
+                    pltpu.VMEM((2, 2, half, experts), bf16),
+                    pltpu.SemaphoreType.DMA((4 * n_high + 4,)),
+                ],
+                compiler_params=params,
+            )(
+                where,
+                acts,
+                *(pltpu.with_memory_space_constraint(x, pltpu.HBM) for x in (grad_logits, *state_in)),
+            )
         else:
             product = lax.dot_general(
                 acts, grad_logits, (((0,), (0,)), ((), ())), preferred_element_type=f32
@@ -199,6 +213,7 @@
 
             away_first, away_second = both(1 - core)
             kept_first, kept_second = both(core)
+            mine = jnp.stack([lax.dynamic_slice_in_dim(x, rep * half, half, 0) for x in state_in])
 
         summed = kept_first.astype(f32) + swap(away_first, "core").astype(f32)
         parts = [to_partner(summed[i].astype(bf16), k) for i, k in enumerate(FIRST)]
@@ -217,13 +232,8 @@
         for j in range(n_high):
             part = lax.dynamic_index_in_dim(total, high ^ j, 0, keepdims=False)
             if j:
-                part = swap(part, "high", j)
+                part = swap(part.astype(bf16), "high", j).astype(f32)
             grad = part if grad is None else grad + part
-
-        mine = [
-            lax.dynamic_slice_in_dim(a, rep * half, half, 0)
-            for a in (master, moment_one, moment_two)
-        ]
         weight = adamw(grad, *mine, step_count)[0].astype(bf16)
 
         column = jnp.stack([swap(weight, "high", j) if j else weight for j in range(n_high)])
@@ -237,11 +247,22 @@
             jnp.concatenate([grad, other], 0),
             jnp.concatenate([other, grad], 0),
         )
-        state = adamw(whole, master, moment_one, moment_two, step_count)
+        state = adamw(whole, *state_in, step_count)
 
         got = [to_partner(chip, k) for k in (*FIRST, 3)]
         corner = to_corner(column)
-        got[0], state = lax.optimization_barrier((got[0], state))
+        columns = [None, None]
+        if in_kernels:
+            state, late_acts = lax.optimization_barrier((state, acts))
+            columns = pl.pallas_call(
+                functools.partial(columns_kernel, n_high),
+                out_shape=(pltpu.VMEM((2 * n_high, tokens, 4 * half), bf16),) * 2,
+                in_specs=[smem, anywhere],
+                out_specs=(vmem, vmem),
+                scratch_shapes=[pltpu.SemaphoreType.DMA((2, 2 * n_high))],
+                compiler_params=params,
+            )(where, pltpu.with_memory_space_constraint(late_acts, pltpu.HBM))
+        got[0], state, columns = lax.optimization_barrier((got[0], state, columns))
         got[2], corner = lax.optimization_barrier((got[2], corner))
         over = [swap(x, "core") for x in got]
         corner_over = swap(corner, "core")
@@ -250,24 +271,20 @@
         second = [got[2], over[2], corner[None], corner_over[None], column[None], across[None]]
         stages = ((FIRST, first_place, first), ((3, 0), second_place, second))
         logits = None
-        for lows, place, pieces in stages:
+        for (lows, place, pieces), acts_columns in zip(stages, columns):
             if in_kernels:
                 before = [] if logits is None else [logits]
                 operands = [
-                    pltpu.with_memory_space_constraint(x, pltpu.VMEM) for x in pieces + before
+                    pltpu.with_memory_space_constraint(x, pltpu.VMEM) for x in [acts_columns] + pieces + before
                 ]
                 logits = pl.pallas_call(
-                    functools.partial(logits_kernel, n_high, lows, place),
+                    functools.partial(logits_kernel, n_high, place),
                     out_shape=jax.ShapeDtypeStruct((tokens, experts), bf16 if before else f32),
-                    in_specs=[smem, anywhere] + [vmem] * len(operands),
+                    in_specs=[smem] + [vmem] * len(operands),
                     out_specs=vmem,
-                    scratch_shapes=[
-                        chunks[0],
-                        pltpu.VMEM((2, n_high, 2, 2, half, experts), bf16),
-                        chunks[2],
-                    ],
+                    scratch_shapes=[pltpu.VMEM((2, n_high, 2, 2, half, experts), bf16)],
                     compiler_params=params,
-                )(where, acts, *operands)
+                )(where, *operands)
             else:
                 at = jnp.array(lows)
                 places = jnp.stack(

time: 61.1 us -> 54.1 us (0.89)
  waiting for transfers between devices: 23.2 us -> 19.1 us
  Pallas kernels: 12.3 us -> 10.2 us
  local copies, waits for them, and re-layouts: 0.95 us -> 0.11 us
    ppermute x8, waiting for transfers between devices: 12.4 us -> 9.88 us  [cube_swap(): return lax.ppermute(x, AXES[1:], pairs)]
    pallas_call x4, Pallas kernels: 12.3 us -> 10.2 us  [the longest x1 4.8 us: per_device(): pl.pallas_call(functools.partial(grad_kernel, n_high), out_shape=(first_s...]
    ppermute x11, waiting for transfers between devices: 10.8 us -> 9.26 us  [swap(): lax.ppermute(x, axis, [(i, i ^ mask) for i in range(fine.shape[axis])])]
    ppermute x11, starting transfers between devices: 6.08 us -> 7.04 us  [swap(): lax.ppermute(x, axis, [(i, i ^ mask) for i in range(fine.shape[axis])])]
    ppermute x8, starting transfers between devices: 15.3 us -> 14.4 us  [cube_swap(): return lax.ppermute(x, AXES[1:], pairs)]
    unnamed x8 -> x6, local copies, waits for them, and re-layouts: 0.86 us -> 0.02 us
  transfers between devices with their start and end apart: 19 -> 19, of which waited for: 7 -> 10; matrix products, arithmetic and copies ran while one was open for 2% -> 2% of each run, Pallas kernels for 10% -> 7%
where the time goes in v8:
time: 54.1 us; the launch traced here: 53.9 us
  starting transfers between devices  21.5 us (40%)
  waiting for transfers between devices  19.1 us (35%)
  Pallas kernels  10.2 us (19%)
  between operations  1.53 us (3%)
  other arithmetic  1.45 us (3%)
    ppermute x8, starting transfers between devices, cube_swap(): return lax.ppermute(x, AXES[1:], pairs)  14.4 us
    ppermute x8, waiting for transfers between devices, cube_swap(): return lax.ppermute(x, AXES[1:], pairs)  9.88 us
    ppermute x11, waiting for transfers between devices, swap(): lax.ppermute(x, axis, [(i, i ^ mask) for i in range(fine.shape[axis])])  9.26 us
    ppermute x11, starting transfers between devices, swap(): lax.ppermute(x, axis, [(i, i ^ mask) for i in range(fine.shape[axis])])  7.04 us
    pallas_call x1, Pallas kernels, per_device(): pl.pallas_call(functools.partial(grad_kernel, n_high), out_shape=(first_s...  4.8 us
    pallas_call x2, Pallas kernels, per_device(): pl.pallas_call(functools.partial(logits_kernel, n_high, place), out_shape...  2.95 us
    pallas_call x1, Pallas kernels, per_device(): pl.pallas_call(functools.partial(columns_kernel, n_high), out_shape=(pltp...  2.46 us
  transfers between devices with their start and end apart: 19, of which 10 were waited for; matrix products, arithmetic and copies ran while one was open for 2% of the time, Pallas kernels for 7%

profile of v8, /device:TPU:0, one launch (start us, length us, event | category | flops | bytes accessed | tf_op | source)
XLA Modules:
  0.0 53.9 jit_solution(6164062804797963342)
XLA Ops:
  0.7 4.8 %shard_map.93 = (bf16[2,2,2,192,128]{4,3,2,1,0:T(8,128)(2,1)S(1)}, bf16[2,2,2,192,128]{4,3,2,1,0:T(8,128)(2,1)S(1)}, bf16[4,2,192,128]{3,2,1,0:T(8,128)(2,1)S(1)...) custom-call(s32[4]{0:T(128)S(1)} %pad_add_fusion.where_ref, bf16[256,6144]{1,0:T(8,128)(2,1)} %acts_ref.2, ...), custom_call_target="tpu_custom_call" | custom-call | tf_op jit(solution)/shard_map/pallas_call | solution.py:176
  6.1 1.3 %collective-permute-done.3 = bf16[4,2,192,128]{3,2,1,0:T(8,128)(2,1)S(1)} collective-permute-done((bf16[4,2,192,128]{3,2,1,0:T(8,128)(2,1)S(1)}, bf16[4,2,192,128]{3,2,1,0:T(8,128)(2,1)S(1)}, u32[]{:S(2)}, u32[]{:S(2)}) %collective-permute-start.3) | collective-permute-done | bytes 393248 | tf_op jit(solution)/shard_map/ppermute | solution.py:138
  7.5 3.9 %collective-permute-start.4 = (bf16[2,2,192,128]{3,2,1,0:T(8,128)(2,1)S(1)}, bf16[2,2,192,128]{3,2,1,0:T(8,128)(2,1)S(1)}, u32[]{:S(2)}, u32[]{:S(2)}) collective-permute-start(bf16[2,2,192,128]{3,2,1,0:T(8,128)(2,1)S(1)} %slice.26), channel_id=1, source_target_pairs={{0,12},{1,13},{2,3},{3,2},{4,8},{5,9},{6,7},{7,6},{8,4},{9,5},{10,... | collective-permute-start | bytes 589832 | tf_op jit(solution)/shard_map/ppermute | solution.py:148
  11.6 1.6 %collective-permute-start.1 = (bf16[2,2,192,128]{3,2,1,0:T(8,128)(2,1)S(1)}, bf16[2,2,192,128]{3,2,1,0:T(8,128)(2,1)S(1)}, u32[]{:S(2)}, u32[]{:S(2)}) collective-permute-start(bf16[2,2,192,128]{3,2,1,0:T(8,128)(2,1)S(1)} %get-tuple-element.62), channel_id=1, source_target_pairs={{0,5},{1,4},{2,10},{3,11},{4,1},{5,0},{6,14},{7,15},{8,13},{9,12},... | collective-permute-start | bytes 589832 | tf_op jit(solution)/shard_map/ppermute | solution.py:148
  13.5 3.6 %collective-permute-start.5 = (bf16[2,192,128]{2,1,0:T(8,128)(2,1)S(1)}, bf16[2,192,128]{2,1,0:T(8,128)(2,1)S(1)}, u32[]{:S(2)}, u32[]{:S(2)}) collective-permute-start(bf16[2,192,128]{2,1,0:T(8,128)(2,1)S(1)} %slice_bitcast_fusion.3), channel_id=1, source_target_pairs={{0,13},{1,12},{2,15},{3,14},{4,9},{5,8},{6,11},{7,10},{8,5},{9,4},... | collective-permute-start | bytes 294920 | tf_op jit(solution)/shard_map/ppermute | solution.py:148
  17.1 6.6 %collective-permute-done.5 = bf16[2,192,128]{2,1,0:T(8,128)(2,1)S(1)} collective-permute-done((bf16[2,192,128]{2,1,0:T(8,128)(2,1)S(1)}, bf16[2,192,128]{2,1,0:T(8,128)(2,1)S(1)}, u32[]{:S(2)}, u32[]{:S(2)}) %collective-permute-start.5) | collective-permute-done | bytes 98336 | tf_op jit(solution)/shard_map/ppermute | solution.py:148
  24.3 1.4 %collective-permute-done.6 = f32[2,192,128]{2,1,0:T(8,128)S(1)} collective-permute-done((f32[2,192,128]{2,1,0:T(8,128)S(1)}, f32[2,192,128]{2,1,0:T(8,128)S(1)}, u32[]{:S(2)}, u32[]{:S(2)}) %collective-permute-start.6) | collective-permute-done | bytes 196640 | tf_op jit(solution)/shard_map/ppermute | solution.py:138
  25.8 2.7 %collective-permute-start.7 = (bf16[192,128]{1,0:T(8,128)(2,1)S(1)}, bf16[192,128]{1,0:T(8,128)(2,1)S(1)}, u32[]{:S(2)}, u32[]{:S(2)}) collective-permute-start(bf16[192,128]{1,0:T(8,128)(2,1)S(1)} %fusion.12), channel_id=1, source_target_pairs={{0,16},{16,0},{1,17},{17,1},{2,18},{18,2},{3,19},{19,3},{4,20},{20... | collective-permute-start | bytes 147464 | tf_op jit(solution)/shard_map/ppermute | solution.py:138
  29.1 2.7 %collective-permute-done.7 = bf16[192,128]{1,0:T(8,128)(2,1)S(1)} collective-permute-done((bf16[192,128]{1,0:T(8,128)(2,1)S(1)}, bf16[192,128]{1,0:T(8,128)(2,1)S(1)}, u32[]{:S(2)}, u32[]{:S(2)}) %collective-permute-start.7) | collective-permute-done | bytes 49184 | tf_op jit(solution)/shard_map/ppermute | solution.py:138
  31.9 1.6 %collective-permute-start.8 = (bf16[192,128]{1,0:T(8,128)(2,1)S(1)}, bf16[192,128]{1,0:T(8,128)(2,1)S(1)}, u32[]{:S(2)}, u32[]{:S(2)}) collective-permute-start(bf16[192,128]{1,0:T(8,128)(2,1)S(1)} %get-tuple-element.57), channel_id=1, source_target_pairs={{0,16},{16,0},{1,17},{17,1},{2,18},{18,2},{3,19},{19,3},{4,20},{20... | collective-permute-start | bytes 147464 | tf_op jit(solution)/shard_map/ppermute | solution.py:138
  33.6 0.9 %collective-permute-start.10 = (f32[192,128]{1,0:T(8,128)S(1)}, f32[192,128]{1,0:T(8,128)S(1)}, u32[]{:S(2)}, u32[]{:S(2)}) collective-permute-start(f32[192,128]{1,0:T(8,128)S(1)} %get-tuple-element.58), channel_id=1, source_target_pairs={{0,1},{1,0},{2,3},{3,2},{4,5},{5,4},{6,7},{7,6},{8,9},{9,8},{10,11... | collective-permute-start | bytes 294920 | tf_op jit(solution)/shard_map/ppermute | solution.py:138
  34.5 3.0 %collective-permute-done.8 = bf16[192,128]{1,0:T(8,128)(2,1)S(1)} collective-permute-done((bf16[192,128]{1,0:T(8,128)(2,1)S(1)}, bf16[192,128]{1,0:T(8,128)(2,1)S(1)}, u32[]{:S(2)}, u32[]{:S(2)}) %collective-permute-start.8) | collective-permute-done | bytes 49184 | tf_op jit(solution)/shard_map/ppermute | solution.py:138
  37.6 0.6 %collective-permute-start.13 = (bf16[2,192,128]{2,1,0:T(8,128)(2,1)S(1)}, bf16[2,192,128]{2,1,0:T(8,128)(2,1)S(1)}, u32[]{:S(2)}, u32[]{:S(2)}) collective-permute-start(bf16[2,192,128]{2,1,0:T(8,128)(2,1)S(1)} %get-tuple-element.64), channel_id=1, source_target_pairs={{0,13},{1,12},{2,15},{3,14},{4,9},{5,8},{6,11},{7,10},{8,5},{9,4},... | collective-permute-start | bytes 294920 | tf_op jit(solution)/shard_map/ppermute | solution.py:148
  38.2 0.7 %collective-permute-done.9 = bf16[2,192,128]{2,1,0:T(8,128)(2,1)S(1)} collective-permute-done((bf16[2,192,128]{2,1,0:T(8,128)(2,1)S(1)}, bf16[2,192,128]{2,1,0:T(8,128)(2,1)S(1)}, u32[]{:S(2)}, u32[]{:S(2)}) %collective-permute-start.9) | collective-permute-done | bytes 98336 | tf_op jit(solution)/shard_map/ppermute | solution.py:138
  38.9 1.6 %collective-permute-start.11 = (bf16[2,2,192,128]{3,2,1,0:T(8,128)(2,1)S(1)}, bf16[2,2,192,128]{3,2,1,0:T(8,128)(2,1)S(1)}, u32[]{:S(2)}, u32[]{:S(2)}) collective-permute-start(bf16[2,2,192,128]{3,2,1,0:T(8,128)(2,1)S(1)} %maximum_select_fusion), channel_id=1, source_target_pairs={{0,5},{1,4},{2,10},{3,11},{4,1},{5,0},{6,14},{7,15},{8,13},{9,12},... | collective-permute-start | bytes 589832 | tf_op jit(solution)/shard_map/ppermute | solution.py:148
  40.5 1.8 %collective-permute-start.17 = (bf16[2,2,192,128]{3,2,1,0:T(8,128)(2,1)S(1)}, bf16[2,2,192,128]{3,2,1,0:T(8,128)(2,1)S(1)}, u32[]{:S(2)}, u32[]{:S(2)}) collective-permute-start(bf16[2,2,192,128]{3,2,1,0:T(8,128)(2,1)S(1)} %maximum_select_fusion), channel_id=1, source_target_pairs={{0,9},{1,8},{2,6},{3,7},{4,13},{5,12},{6,2},{7,3},{8,1},{9,0},{10,... | collective-permute-start | bytes 589832 | tf_op jit(solution)/shard_map/ppermute | solution.py:148
  42.2 1.1 %collective-permute-start.12 = (bf16[2,2,192,128]{3,2,1,0:T(8,128)(2,1)S(1)}, bf16[2,2,192,128]{3,2,1,0:T(8,128)(2,1)S(1)}, u32[]{:S(2)}, u32[]{:S(2)}) collective-permute-start(bf16[2,2,192,128]{3,2,1,0:T(8,128)(2,1)S(1)} %maximum_select_fusion), channel_id=1, source_target_pairs={{0,12},{1,13},{2,3},{3,2},{4,8},{5,9},{6,7},{7,6},{8,4},{9,5},{10,... | collective-permute-start | bytes 589832 | tf_op jit(solution)/shard_map/ppermute | solution.py:148
  43.4 0.9 %multiply_subtract_fusion = (f32[384,128]{1,0:T(8,128)}, f32[384,128]{1,0:T(8,128)}, f32[384,128]{1,0:T(8,128)}) fusion(f32[384,128]{1,0:T(8,128)S(1)} %copy-done, f32[]{:T(128)} %bitcast.16, f32[]{:T(128)} %bitcast.14, f32[192,128]{1,0:T(8,128)S(1)} %get-tuple-element.58, f32[192,128]{1,0:T(8,128)S(1)} %collective-permute-done.10, pred[]{:T(512)S(6)} %eq.7, ...), kind=kLoop, calls=%fused_computation.13 | loop fusion | flops 884736 | bytes 1376265 | tf_op jit(solution)/shard_map/sub | solution.py:29
  44.3 2.5 %shard_map.94 = (bf16[4,256,768]{2,1,0:T(8,128)(2,1)S(1)}, bf16[4,256,768]{2,1,0:T(8,128)(2,1)S(1)}) custom-call(s32[4]{0:T(128)S(1)} %pad_add_fusion.where_ref, bf16[256,6144]{1,0:T(8,128)(2,1)} %acts_ref.2), custom_call_target="tpu_custom_call" | custom-call | tf_op jit(solution)/shard_map/pallas_call | solution.py:257
  46.8 2.3 %collective-permute-done.11.refs_0_ = bf16[2,2,192,128]{3,2,1,0:T(8,128)(2,1)S(1)} collective-permute-done((bf16[2,2,192,128]{3,2,1,0:T(8,128)(2,1)S(1)}, bf16[2,2,192,128]{3,2,1,0:T(8,128)(2,1)S(1)}, u32[]{:S(2)}, u32[]{:S(2)}) %collective-permute-start.11) | collective-permute-done | bytes 196640 | tf_op jit(solution)/shard_map/ppermute | solution.py:148
  49.6 0.6 %collective-permute-done.12.refs_0_ = bf16[2,2,192,128]{3,2,1,0:T(8,128)(2,1)S(1)} collective-permute-done((bf16[2,2,192,128]{3,2,1,0:T(8,128)(2,1)S(1)}, bf16[2,2,192,128]{3,2,1,0:T(8,128)(2,1)S(1)}, u32[]{:S(2)}, u32[]{:S(2)}) %collective-permute-start.12) | collective-permute-done | bytes 196640 | tf_op jit(solution)/shard_map/ppermute | solution.py:148
  50.2 0.6 %collective-permute-start.14 = (bf16[2,2,192,128]{3,2,1,0:T(8,128)(2,1)S(1)}, bf16[2,2,192,128]{3,2,1,0:T(8,128)(2,1)S(1)}, u32[]{:S(2)}, u32[]{:S(2)}) collective-permute-start(bf16[2,2,192,128]{3,2,1,0:T(8,128)(2,1)S(1)} %collective-permute-done.12.refs_0_), channel_id=1, source_target_pairs={{0,2},{2,0},{1,3},{3,1},{4,6},{6,4},{5,7},{7,5},{8,10},{10,8},{9,1... | collective-permute-start | bytes 589832 | tf_op jit(solution)/shard_map/ppermute | solution.py:138
  50.8 1.2 %shard_map.95.refs_6_ = f32[256,128]{1,0:T(8,128)S(1)} custom-call(s32[4]{0:T(128)S(1)} %pad_add_fusion.where_ref, bf16[4,256,768]{2,1,0:T(8,128)(2,1)S(1)} %get-tuple-element.52.columns_ref, bf16[2,2,192,128]{3,2,1,0:T(8,128)(2,1)S(1)} %collective-permute-done.11.refs_0_, bf16[2,2,192,128]{3,2,1,0:T(8,128)(2,1)S(1)} %collective-permute-done.16.refs_1_, ...), custom_call_target="tpu_custom_call" | custom-call | tf_op jit(solution)/shard_map/pallas_call | solution.py:280
  52.1 1.8 %shard_map.96 = bf16[256,128]{1,0:T(8,128)(2,1)} custom-call(s32[4]{0:T(128)S(1)} %pad_add_fusion.where_ref, bf16[4,256,768]{2,1,0:T(8,128)(2,1)S(1)} %get-tuple-element.49.columns_ref, bf16[2,2,192,128]{3,2,1,0:T(8,128)(2,1)S(1)} %collective-permute-done.12.refs_0_, bf16[2,2,192,128]{3,2,1,0:T(8,128)(2,1)S(1)} %collective-permute-done.14.refs_1_, ...), custom_call_target="tpu_custom_call" | custom-call | tf_op jit(solution)/shard_map/pallas_call | solution.py:280
  (38 shorter events, 2.7 us)
Async XLA Ops:
  5.5 1.9 %collective-permute-start.3 = (bf16[4,2,192,128]{3,2,1,0:T(8,128)(2,1)S(1)}, bf16[4,2,192,128]{3,2,1,0:T(8,128)(2,1)S(1)}, u32[]{:S(2)}, u32[]{:S(2)}) collective-permute-start(bf16[4,2,192,128]{3,2,1,0:T(8,128)(2,1)S(1)} %get-tuple-element.33), channel_id=1, source_target_pairs={{0,2},{2,0},{1,3},{3,1},{4,6},{6,4},{5,7},{7,5},{8,10},{10,8},{9,1... | collective-permute-start | bytes 1179656 | tf_op jit(solution)/shard_map/ppermute | solution.py:138
  6.0 5.4 %collective-permute-start = (bf16[2,2,2,192,128]{4,3,2,1,0:T(8,128)(2,1)S(1)}, bf16[2,2,2,192,128]{4,3,2,1,0:T(8,128)(2,1)S(1)}, u32[]{:S(2)}, u32[]{:S(2)}) collective-permute-start(bf16[2,2,2,192,128]{4,3,2,1,0:T(8,128)(2,1)S(1)} %get-tuple-element.31), channel_id=1, source_target_pairs={{0,2},{2,0},{1,3},{3,1},{4,6},{6,4},{5,7},{7,5},{8,10},{10,8},{9,1... | collective-permute-start | bytes 1179656 | tf_op jit(solution)/shard_map/ppermute | solution.py:138
  7.5 16.2 %collective-permute-start.4 = (bf16[2,2,192,128]{3,2,1,0:T(8,128)(2,1)S(1)}, bf16[2,2,192,128]{3,2,1,0:T(8,128)(2,1)S(1)}, u32[]{:S(2)}, u32[]{:S(2)}) collective-permute-start(bf16[2,2,192,128]{3,2,1,0:T(8,128)(2,1)S(1)} %slice.26), channel_id=1, source_target_pairs={{0,12},{1,13},{2,3},{3,2},{4,8},{5,9},{6,7},{7,6},{8,4},{9,5},{10,... | collective-permute-start | bytes 589832 | tf_op jit(solution)/shard_map/ppermute | solution.py:148
  11.6 12.4 %collective-permute-start.1 = (bf16[2,2,192,128]{3,2,1,0:T(8,128)(2,1)S(1)}, bf16[2,2,192,128]{3,2,1,0:T(8,128)(2,1)S(1)}, u32[]{:S(2)}, u32[]{:S(2)}) collective-permute-start(bf16[2,2,192,128]{3,2,1,0:T(8,128)(2,1)S(1)} %get-tuple-element.62), channel_id=1, source_target_pairs={{0,5},{1,4},{2,10},{3,11},{4,1},{5,0},{6,14},{7,15},{8,13},{9,12},... | collective-permute-start | bytes 589832 | tf_op jit(solution)/shard_map/ppermute | solution.py:148
  13.2 10.9 %collective-permute-start.2 = (bf16[2,2,192,128]{3,2,1,0:T(8,128)(2,1)S(1)}, bf16[2,2,192,128]{3,2,1,0:T(8,128)(2,1)S(1)}, u32[]{:S(2)}, u32[]{:S(2)}) collective-permute-start(bf16[2,2,192,128]{3,2,1,0:T(8,128)(2,1)S(1)} %get-tuple-element.61), channel_id=1, source_target_pairs={{0,9},{1,8},{2,6},{3,7},{4,13},{5,12},{6,2},{7,3},{8,1},{9,0},{10,... | collective-permute-start | bytes 589832 | tf_op jit(solution)/shard_map/ppermute | solution.py:148
  13.5 10.2 %collective-permute-start.5 = (bf16[2,192,128]{2,1,0:T(8,128)(2,1)S(1)}, bf16[2,192,128]{2,1,0:T(8,128)(2,1)S(1)}, u32[]{:S(2)}, u32[]{:S(2)}) collective-permute-start(bf16[2,192,128]{2,1,0:T(8,128)(2,1)S(1)} %slice_bitcast_fusion.3), channel_id=1, source_target_pairs={{0,13},{1,12},{2,15},{3,14},{4,9},{5,8},{6,11},{7,10},{8,5},{9,4},... | collective-permute-start | bytes 294920 | tf_op jit(solution)/shard_map/ppermute | solution.py:148
  24.1 19.3 %copy-start = (f32[384,128]{1,0:T(8,128)S(1)}, f32[384,128]{1,0:T(8,128)}, u32[]{:S(2)}) copy-start(f32[384,128]{1,0:T(8,128)} %refs_0_.1) | copy-start | bytes 589828
  24.1 19.3 %copy-start.1 = (f32[384,128]{1,0:T(8,128)S(1)}, f32[384,128]{1,0:T(8,128)}, u32[]{:S(2)}) copy-start(f32[384,128]{1,0:T(8,128)} %refs_1_.1) | copy-start | bytes 589828
  24.1 19.3 %copy-start.2 = (f32[384,128]{1,0:T(8,128)S(1)}, f32[384,128]{1,0:T(8,128)}, u32[]{:S(2)}) copy-start(f32[384,128]{1,0:T(8,128)} %refs_2_.1) | copy-start | bytes 589828
  24.2 1.5 %collective-permute-start.6 = (f32[2,192,128]{2,1,0:T(8,128)S(1)}, f32[2,192,128]{2,1,0:T(8,128)S(1)}, u32[]{:S(2)}, u32[]{:S(2)}) collective-permute-start(f32[2,192,128]{2,1,0:T(8,128)S(1)} %dynamic-slice_bitcast_fusion), channel_id=1, source_target_pairs={{0,2},{2,0},{1,3},{3,1},{4,6},{6,4},{5,7},{7,5},{8,10},{10,8},{9,1... | collective-permute-start | bytes 589832 | tf_op jit(solution)/shard_map/ppermute | solution.py:138
  25.8 6.1 %collective-permute-start.7 = (bf16[192,128]{1,0:T(8,128)(2,1)S(1)}, bf16[192,128]{1,0:T(8,128)(2,1)S(1)}, u32[]{:S(2)}, u32[]{:S(2)}) collective-permute-start(bf16[192,128]{1,0:T(8,128)(2,1)S(1)} %fusion.12), channel_id=1, source_target_pairs={{0,16},{16,0},{1,17},{17,1},{2,18},{18,2},{3,19},{19,3},{4,20},{20... | collective-permute-start | bytes 147464 | tf_op jit(solution)/shard_map/ppermute | solution.py:138
  31.9 5.6 %collective-permute-start.8 = (bf16[192,128]{1,0:T(8,128)(2,1)S(1)}, bf16[192,128]{1,0:T(8,128)(2,1)S(1)}, u32[]{:S(2)}, u32[]{:S(2)}) collective-permute-start(bf16[192,128]{1,0:T(8,128)(2,1)S(1)} %get-tuple-element.57), channel_id=1, source_target_pairs={{0,16},{16,0},{1,17},{17,1},{2,18},{18,2},{3,19},{19,3},{4,20},{20... | collective-permute-start | bytes 147464 | tf_op jit(solution)/shard_map/ppermute | solution.py:138
  33.6 4.6 %collective-permute-start.10 = (f32[192,128]{1,0:T(8,128)S(1)}, f32[192,128]{1,0:T(8,128)S(1)}, u32[]{:S(2)}, u32[]{:S(2)}) collective-permute-start(f32[192,128]{1,0:T(8,128)S(1)} %get-tuple-element.58), channel_id=1, source_target_pairs={{0,1},{1,0},{2,3},{3,2},{4,5},{5,4},{6,7},{7,6},{8,9},{9,8},{10,11... | collective-permute-start | bytes 294920 | tf_op jit(solution)/shard_map/ppermute | solution.py:138
  37.5 1.4 %collective-permute-start.9 = (bf16[2,192,128]{2,1,0:T(8,128)(2,1)S(1)}, bf16[2,192,128]{2,1,0:T(8,128)(2,1)S(1)}, u32[]{:S(2)}, u32[]{:S(2)}) collective-permute-start(bf16[2,192,128]{2,1,0:T(8,128)(2,1)S(1)} %get-tuple-element.64), channel_id=1, source_target_pairs={{0,2},{2,0},{1,3},{3,1},{4,6},{6,4},{5,7},{7,5},{8,10},{10,8},{9,1... | collective-permute-start | bytes 294920 | tf_op jit(solution)/shard_map/ppermute | solution.py:138
  37.6 12.0 %collective-permute-start.13 = (bf16[2,192,128]{2,1,0:T(8,128)(2,1)S(1)}, bf16[2,192,128]{2,1,0:T(8,128)(2,1)S(1)}, u32[]{:S(2)}, u32[]{:S(2)}) collective-permute-start(bf16[2,192,128]{2,1,0:T(8,128)(2,1)S(1)} %get-tuple-element.64), channel_id=1, source_target_pairs={{0,13},{1,12},{2,15},{3,14},{4,9},{5,8},{6,11},{7,10},{8,5},{9,4},... | collective-permute-start | bytes 294920 | tf_op jit(solution)/shard_map/ppermute | solution.py:148
  38.9 10.2 %collective-permute-start.11 = (bf16[2,2,192,128]{3,2,1,0:T(8,128)(2,1)S(1)}, bf16[2,2,192,128]{3,2,1,0:T(8,128)(2,1)S(1)}, u32[]{:S(2)}, u32[]{:S(2)}) collective-permute-start(bf16[2,2,192,128]{3,2,1,0:T(8,128)(2,1)S(1)} %maximum_select_fusion), channel_id=1, source_target_pairs={{0,5},{1,4},{2,10},{3,11},{4,1},{5,0},{6,14},{7,15},{8,13},{9,12},... | collective-permute-start | bytes 589832 | tf_op jit(solution)/shard_map/ppermute | solution.py:148
  40.5 8.6 %collective-permute-start.17 = (bf16[2,2,192,128]{3,2,1,0:T(8,128)(2,1)S(1)}, bf16[2,2,192,128]{3,2,1,0:T(8,128)(2,1)S(1)}, u32[]{:S(2)}, u32[]{:S(2)}) collective-permute-start(bf16[2,2,192,128]{3,2,1,0:T(8,128)(2,1)S(1)} %maximum_select_fusion), channel_id=1, source_target_pairs={{0,9},{1,8},{2,6},{3,7},{4,13},{5,12},{6,2},{7,3},{8,1},{9,0},{10,... | collective-permute-start | bytes 589832 | tf_op jit(solution)/shard_map/ppermute | solution.py:148
  42.2 8.0 %collective-permute-start.12 = (bf16[2,2,192,128]{3,2,1,0:T(8,128)(2,1)S(1)}, bf16[2,2,192,128]{3,2,1,0:T(8,128)(2,1)S(1)}, u32[]{:S(2)}, u32[]{:S(2)}) collective-permute-start(bf16[2,2,192,128]{3,2,1,0:T(8,128)(2,1)S(1)} %maximum_select_fusion), channel_id=1, source_target_pairs={{0,12},{1,13},{2,3},{3,2},{4,8},{5,9},{6,7},{7,6},{8,4},{9,5},{10,... | collective-permute-start | bytes 589832 | tf_op jit(solution)/shard_map/ppermute | solution.py:148
  49.1 1.7 %collective-permute-start.16 = (bf16[2,2,192,128]{3,2,1,0:T(8,128)(2,1)S(1)}, bf16[2,2,192,128]{3,2,1,0:T(8,128)(2,1)S(1)}, u32[]{:S(2)}, u32[]{:S(2)}) collective-permute-start(bf16[2,2,192,128]{3,2,1,0:T(8,128)(2,1)S(1)} %collective-permute-done.11.refs_0_), channel_id=1, source_target_pairs={{0,2},{2,0},{1,3},{3,1},{4,6},{6,4},{5,7},{7,5},{8,10},{10,8},{9,1... | collective-permute-start | bytes 589832 | tf_op jit(solution)/shard_map/ppermute | solution.py:138
  49.1 1.7 %collective-permute-start.18 = (bf16[2,2,192,128]{3,2,1,0:T(8,128)(2,1)S(1)}, bf16[2,2,192,128]{3,2,1,0:T(8,128)(2,1)S(1)}, u32[]{:S(2)}, u32[]{:S(2)}) collective-permute-start(bf16[2,2,192,128]{3,2,1,0:T(8,128)(2,1)S(1)} %collective-permute-done.17.refs_2_), channel_id=1, source_target_pairs={{0,2},{2,0},{1,3},{3,1},{4,6},{6,4},{5,7},{7,5},{8,10},{10,8},{9,1... | collective-permute-start | bytes 589832 | tf_op jit(solution)/shard_map/ppermute | solution.py:138
  50.2 1.9 %collective-permute-start.14 = (bf16[2,2,192,128]{3,2,1,0:T(8,128)(2,1)S(1)}, bf16[2,2,192,128]{3,2,1,0:T(8,128)(2,1)S(1)}, u32[]{:S(2)}, u32[]{:S(2)}) collective-permute-start(bf16[2,2,192,128]{3,2,1,0:T(8,128)(2,1)S(1)} %collective-permute-done.12.refs_0_), channel_id=1, source_target_pairs={{0,2},{2,0},{1,3},{3,1},{4,6},{6,4},{5,7},{7,5},{8,10},{10,8},{9,1... | collective-permute-start | bytes 589832 | tf_op jit(solution)/shard_map/ppermute | solution.py:138
  50.8 1.3 %collective-permute-start.15 = (bf16[2,192,128]{2,1,0:T(8,128)(2,1)S(1)}, bf16[2,192,128]{2,1,0:T(8,128)(2,1)S(1)}, u32[]{:S(2)}, u32[]{:S(2)}) collective-permute-start(bf16[2,192,128]{2,1,0:T(8,128)(2,1)S(1)} %collective-permute-done.13), channel_id=1, source_target_pairs={{0,2},{2,0},{1,3},{3,1},{4,6},{6,4},{5,7},{7,5},{8,10},{10,8},{9,1... | collective-permute-start | bytes 294920 | tf_op jit(solution)/shard_map/ppermute | solution.py:138

commit v9 on v8

v9 whole, which is shorter than its diff:
```python
import functools

import jax
import jax.numpy as jnp
from jax import lax
from jax.experimental import pallas as pl
from jax.experimental.pallas import tpu as pltpu
from jax.sharding import Mesh
from jax.sharding import PartitionSpec as P

AXES = ("high", "low", "core", "rep")
N_LOW = 4
FIRST = (1, 2)
VMEM_LIMIT = 8 * 2**20


def parity(n):
    return (n ^ (n >> 1)) & 1


def adamw(grad, master, moment_one, moment_two, step_count):
    count = step_count[0].astype(jnp.float32)
    beta_one = 0.9
    beta_two = 0.95
    first = beta_one * moment_one + (1.0 - beta_one) * grad
    second = beta_two * moment_two + (1.0 - beta_two) * grad * grad
    first_hat = first / (1.0 - jnp.power(beta_one, count))
    second_hat = second / (1.0 - jnp.power(beta_two, count))
    updated = master - 0.01 * (first_hat / (jnp.sqrt(second_hat) + 1e-08) + 0.1 * master)
    return updated, first, second


def near_places(core, n_high):
    return [(k, 0) for k in FIRST] + [(k, j) for k in (3 * (1 - core), 3 * core) for j in range(n_high)]


def far_places(n_high):
    return [(k, j) for k in FIRST for j in range(1, n_high)]


def load_columns(acts_ref, columns, sems, first_sem, high, low, places):
    wide = columns.shape[-1]
    copies = []
    for n, (k, j) in enumerate(places):
        column = pl.multiple_of(((high ^ j) * N_LOW + (low ^ k)) * wide, wide)
        copy = pltpu.make_async_copy(
            acts_ref.at[:, pl.ds(column, wide)], columns.at[n], sems.at[first_sem + n]
        )
        copy.start()
        copies.append(copy)
    return copies


def grad_kernel(n_high, where_ref, acts_ref, grad_ref, *refs):
    state_refs, refs = refs[:3], refs[3:]
    away_far, away_near, away_rest, kept_far, kept_near, kept_rest = refs[:6]
    mine_ref, near_columns, far_columns, logit_grads, blocks, sems = refs[6:]
    high, low, core, rep = [where_ref[i] for i in range(4)]
    half = blocks.shape[2]
    last = sems.shape[0]
    loads = pltpu.make_async_copy(grad_ref, logit_grads, sems.at[last - 1])
    loads.start()
    places = near_places(core, n_high), far_places(n_high)
    loaded = []
    for at, columns in zip(places, (near_columns, far_columns)):
        copies = load_columns(acts_ref, columns, sems, len(loaded), high, low, at)
        loaded += [(copy, columns, n) for n, copy in enumerate(copies)]
    rows = pl.ds(pl.multiple_of(rep * half, half), half)
    state = [
        pltpu.make_async_copy(ref.at[rows], mine_ref.at[i], sems.at[last - 4 + i])
        for i, ref in enumerate(state_refs)
    ]
    for copy in state:
        copy.start()
    loads.wait()
    for copy, columns, m in loaded:
        copy.wait()
        product = lax.dot_general(
            columns[m], logit_grads[...], (((0,), (0,)), ((), ())), preferred_element_type=jnp.float32
        )
        blocks[...] = product.astype(blocks.dtype).reshape(blocks.shape)
        if columns is far_columns:
            p, j = divmod(m, n_high - 1)
            j = j + 1
        else:
            p, j = (m, 0) if m < 2 else divmod(m - 2, n_high)
        if columns is far_columns or m < 2:
            flip = rep ^ core ^ parity(FIRST[p])
            for c in range(2):
                if j:
                    kept_far[p ^ core, c, j - 1] = blocks[c, flip]
                    away_far[p ^ core ^ 1, c, j - 1] = blocks[c, flip ^ 1]
                else:
                    kept_near[p ^ core, c] = blocks[c, flip]
                    away_near[p ^ core ^ 1, c] = blocks[c, flip ^ 1]
        else:
            slot = kept_rest if p == 0 else away_rest
            flip = rep ^ core ^ p
            for c in range(2):
                slot[c, j] = blocks[c, flip]
            kept_rest[2 + (core ^ p), j] = blocks[core, flip ^ 1]
            away_rest[2 + (core ^ p), j] = blocks[core ^ 1, flip ^ 1]
    for copy in state:
        copy.wait()


def logits_kernel(place, where_ref, columns_ref, *refs):
    *pieces, out_ref, weight = refs
    before = None
    if len(pieces[-1].shape) == 2:
        *pieces, before = pieces
    half, experts = weight.shape[-2:]
    for piece, blocks in zip(pieces, place(where_ref[2], where_ref[3])):
        for index, n, owner, of_rep in blocks:
            weight[n, owner, of_rep] = piece[index]
    total = None if before is None else before[...]
    for n in range(weight.shape[0]):
        part = jnp.dot(
            columns_ref[n],
            weight[n].reshape(4 * half, experts),
            preferred_element_type=jnp.float32,
        )
        total = part if total is None else total + part
    out_ref[...] = total.astype(out_ref.dtype)


def slot_owner(core, rep, i, slot, c):
    of_core = core ^ i
    return of_core ^ slot, c, rep ^ parity(FIRST[slot]) ^ of_core


def near_place(core, rep, n_high):
    pieces = []
    for i in range(2):
        at = [(slot, c, *slot_owner(core, rep, i, slot, c)) for slot in range(2) for c in range(2)]
        pieces.append([((slot, c), n, owner, of_rep) for slot, c, n, owner, of_rep in at])
    low_3, low_0 = 2 + n_high * core, 2 + n_high * (1 - core)
    for i in range(2):
        of_core = core ^ i
        blocks = []
        for j in range(n_high):
            blocks += [((c, j), 2 + n_high * i + j, c, rep ^ of_core) for c in range(2)]
            blocks.append(((2, j), low_3 + j, of_core, rep ^ 1))
        pieces.append(blocks)
    pieces.append([((c, j), low_0 + j, c, rep) for c in range(2) for j in range(n_high)])
    return pieces


def far_place(core, rep, n_high):
    pieces = []
    for i in range(2):
        blocks = []
        for slot in range(2):
            for c in range(2):
                which, owner, of_rep = slot_owner(core, rep, i, slot, c)
                for j in range(n_high - 1):
                    blocks.append(((slot, c, j), which * (n_high - 1) + j, owner, of_rep))
        pieces.append(blocks)
    return pieces


def solution(mesh):
    n_seq, n_rep = mesh.shape["seq"], mesh.shape["rep"]
    n_high = n_seq // (2 * N_LOW)
    fine = Mesh(mesh.devices.reshape(n_high, N_LOW, 2, n_rep), AXES)

    def swap(x, axis, mask=1):
        return lax.ppermute(x, axis, [(i, i ^ mask) for i in range(fine.shape[axis])])

    def cube_swap(x, change):
        pairs = []
        for low in range(N_LOW):
            for core in range(2):
                d_low, d_rep = change(core)
                for rep in range(n_rep):
                    there = ((low ^ d_low) * 2 + core) * n_rep + (rep ^ d_rep)
                    pairs.append(((low * 2 + core) * n_rep + rep, there))
        return lax.ppermute(x, AXES[1:], pairs)

    def to_partner(x, k):
        return cube_swap(x, lambda core: (k ^ (3 * core), parity(k) ^ core))

    def to_corner(x):
        return cube_swap(x, lambda core: (3, 1))

    def per_device(acts, grad_logits, master, moment_one, moment_two, step_count):
        tokens, experts = grad_logits.shape
        rows = master.shape[0]
        half = rows // n_rep
        high, low, core, rep = (lax.axis_index(a) for a in AXES)
        where = jnp.stack([high, low, core, rep])
        first_core = core == 0
        f32, bf16 = jnp.float32, jnp.bfloat16
        in_kernels = half % 16 == 0 and (4 * half) % 128 == 0

        smem = pl.BlockSpec(memory_space=pltpu.SMEM)
        vmem = pl.BlockSpec(memory_space=pltpu.VMEM)
        anywhere = pl.BlockSpec(memory_space=pl.ANY)
        params = pltpu.CompilerParams(vmem_limit_bytes=VMEM_LIMIT)
        state_in = (master, moment_one, moment_two)

        if in_kernels:
            acts = pltpu.with_memory_space_constraint(acts, pltpu.HBM)
            shapes = [(2, 2, n_high - 1), (2, 2), (4, n_high)] * 2
            outs = [pltpu.VMEM((*shape, half, experts), bf16) for shape in shapes]
            outs.append(pltpu.VMEM((3, half, experts), f32))
            counts = 2 + 2 * n_high, 2 * (n_high - 1)
            outs += [pltpu.VMEM((n, tokens, 4 * half), bf16) for n in counts]
            *sorted_rows, mine, near_columns, far_columns = pl.pallas_call(
                functools.partial(grad_kernel, n_high),
                out_shape=outs,
                in_specs=[smem] + [anywhere] * 5,
                out_specs=[vmem] * len(outs),
                scratch_shapes=[
                    pltpu.VMEM((tokens, experts), bf16),
                    pltpu.VMEM((2, 2, half, experts), bf16),
                    pltpu.SemaphoreType.DMA((4 * n_high + 4,)),
                ],
                compiler_params=params,
            )(
                where,
                acts,
                *(pltpu.with_memory_space_constraint(x, pltpu.HBM) for x in (grad_logits, *state_in)),
            )
            away, kept = sorted_rows[:3], sorted_rows[3:]
            columns = (near_columns, far_columns)
        else:
            columns = (None, None)
            product = lax.dot_general(
                acts, grad_logits, (((0,), (0,)), ((), ())), preferred_element_type=f32
            ).astype(bf16)
            product = product.reshape(n_high, N_LOW, 2, n_rep, half, experts)
            product = product[high ^ jnp.arange(n_high)]

            def block(d_low, owner, d_rep):
                at = (0, low ^ d_low, owner, rep ^ d_rep, 0, 0)
                part = lax.dynamic_slice(product, at, (n_high, 1, 1, 1, half, experts))
                return part.reshape(n_high, half, experts)

            def slot(k, of_core):
                change = k ^ (3 * of_core), parity(k) ^ of_core
                return jnp.stack([block(change[0], c, change[1]) for c in range(2)])

            def sort_rows(of_core):
                first = jnp.stack([slot(k, of_core) for k in FIRST])
                rest = [slot(3, of_core), block(3, of_core, 1)[None], block(0, of_core, 0)[None]]
                return first[:, :, 1:], first[:, :, 0], jnp.concatenate(rest)

            away, kept = sort_rows(1 - core), sort_rows(core)
            mine = jnp.stack([lax.dynamic_slice_in_dim(x, rep * half, half, 0) for x in state_in])

        far, near, rest = [
            mine_too.astype(f32) + swap(theirs, "core").astype(f32)
            for mine_too, theirs in zip(kept, away)
        ]
        far = [to_partner(far[i].astype(bf16), k) for i, k in enumerate(FIRST)]
        slot_3 = to_partner(rest[:2].astype(bf16), 3)
        corner = to_corner(rest[2].astype(bf16))
        home = rest[3]
        near = [to_partner(near[i].astype(bf16), k) for i, k in enumerate(FIRST)]

        *far, slot_3, corner = [x.astype(f32) for x in lax.optimization_barrier((*far, slot_3, corner))]
        mine_only = corner + home
        far = far[0] + far[1] + slot_3[:, 1:]
        far = [far[c] + jnp.where(core == c, mine_only[1:], 0.0) for c in range(2)]
        far = jnp.stack(far, 1).astype(bf16)
        total = near[0].astype(f32) + near[1].astype(f32) + slot_3[:, 0]
        for j in range(1, n_high):
            total = total + swap(far[j - 1], "high", j).astype(f32)
        theirs = swap(lax.dynamic_index_in_dim(total, 1 - core, 0, keepdims=False), "core")
        grad = lax.dynamic_index_in_dim(total, core, 0, keepdims=False) + theirs + mine_only[0]

        weight = adamw(grad, *mine, step_count)[0].astype(bf16)
        across = swap(weight, "core")
        near = jnp.where(core == 0, jnp.stack([weight, across]), jnp.stack([across, weight]))
        far = [swap(near, "high", j) for j in range(1, n_high)]
        got_near = [to_partner(near, k) for k in FIRST]
        other = swap(grad, "rep")
        got_near, far = lax.optimization_barrier((got_near, far))
        chip = jnp.stack([near, *far], 1)
        far = chip[:, 1:]
        slot_3 = to_partner(chip, 3)
        corner = to_corner(lax.dynamic_index_in_dim(chip, core, 0, keepdims=False))
        got_far = [to_partner(far, k) for k in FIRST]

        whole = jnp.where(
            rep == 0,
            jnp.concatenate([grad, other], 0),
            jnp.concatenate([other, grad], 0),
        )
        state = adamw(whole, *state_in, step_count)
        got_far, slot_3, corner, state = lax.optimization_barrier((got_far, slot_3, corner, state))
        near = jnp.stack(got_near)
        near_over = swap(near, "core")
        rest = jnp.concatenate([slot_3, corner[None]])
        rest_over = swap(rest, "core")
        far = jnp.stack(got_far)
        far_over = swap(far, "core")

        pieces = ([near, near_over, rest, rest_over, chip], [far, far_over])
        stages = (near_places(core, n_high), far_places(n_high))
        logits = None
        for blocks, place, received, acts_columns in zip(
            stages, (near_place, far_place), pieces, columns
        ):
            before = [] if logits is None else [logits]
            if in_kernels:
                operands = [
                    pltpu.with_memory_space_constraint(x, pltpu.VMEM)
                    for x in [acts_columns] + received + before
                ]
                logits = pl.pallas_call(
                    functools.partial(logits_kernel, functools.partial(place, n_high=n_high)),
                    out_shape=jax.ShapeDtypeStruct((tokens, experts), bf16 if before else f32),
                    in_specs=[smem] + [vmem] * len(operands),
                    out_specs=vmem,
                    scratch_shapes=[pltpu.VMEM((len(blocks), 2, 2, half, experts), bf16)],
                    compiler_params=params,
                )(where, *operands)
            else:
                at = jnp.stack([((high ^ j) * N_LOW + (low ^ k)) * 2 for k, j in blocks])
                full = jnp.zeros((2 * n_seq, half, experts), bf16)
                rows_at, values = [], []
                for piece, put in zip(received, place(core, rep, n_high)):
                    for index, n, owner, of_rep in put:
                        rows_at.append((at[n] + owner) * n_rep + of_rep)
                        values.append(piece[index])
                full = full.at[jnp.stack(rows_at)].set(jnp.stack(values))
                part = jnp.dot(acts, full.reshape(n_seq * rows, experts), preferred_element_type=f32)
                logits = (logits + part).astype(bf16) if before else part
        return *state, logits

    rows_of, tokens_of = P(AXES[:3], None), P(AXES, None)
    return jax.shard_map(
        per_device,
        mesh=fine,
        in_specs=(tokens_of, tokens_of, rows_of, rows_of, rows_of, P()),
        out_specs=(rows_of, rows_of, rows_of, tokens_of),
        check_vma=False,
    )
```

time: 54.1 us -> 68.3 us (1.26)
  other arithmetic: 1.45 us -> 8.49 us
  starting transfers between devices: 21.5 us -> 28 us
  local copies, waits for them, and re-layouts: 0.11 us -> 4.93 us
  waiting for transfers between devices: 19.1 us -> 16.4 us
  Pallas kernels: 10.2 us -> 8.52 us
    ppermute x8 -> x12, starting transfers between devices: 14.4 us -> 20.3 us  [cube_swap(): return lax.ppermute(x, AXES[1:], pairs)]
    another operation x3 -> x8, other arithmetic: 0.25 us -> 4.03 us
    unnamed x6 -> x10, local copies, waits for them, and re-layouts: 0.02 us -> 3.39 us
    ppermute x11, waiting for transfers between devices: 9.26 us -> 6.36 us  [swap(): lax.ppermute(x, axis, [(i, i ^ mask) for i in range(fine.shape[axis])])]
    pallas_call x4 -> x3, Pallas kernels: 10.2 us -> 8.52 us  [the longest x1 5.57 us: per_device(): pl.pallas_call(functools.partial(grad_kernel, n_high), out_shape=outs, in...]
    sub x1, other arithmetic: 0.9 us -> 2.02 us  [adamw(): master - 0.01 * (first_hat / (jnp.sqrt(second_hat) + 1e-08) + 0.1 * master)]
    convert_element_type x1, other arithmetic: 0.1 us -> 1.19 us  [per_device(): weight = adamw(grad, *mine, step_count)[0].astype(bf16)]
    add x2 -> x3, other arithmetic: 0.1 us -> 1.09 us  [the longest x1 1.04 us: per_device(): total = total + swap(far[j - 1], 'high', j).astype(f32)]
  transfers between devices with their start and end apart: 19 -> 23, of which waited for: 10 -> 10; matrix products, arithmetic and copies ran while one was open for 2% -> 11% of each run, Pallas kernels for 7% -> 2%
where the time goes in v9:
time: 68.3 us; the launch traced here: 68 us
  starting transfers between devices  28 us (41%)
  waiting for transfers between devices  16.4 us (24%)
  Pallas kernels  8.52 us (12%)
  other arithmetic  8.49 us (12%)
  local copies, waits for them, and re-layouts  4.93 us (7%)
  between operations  1.6 us (2%)
    ppermute x12, starting transfers between devices, cube_swap(): return lax.ppermute(x, AXES[1:], pairs)  20.3 us
    ppermute x12, waiting for transfers between devices, cube_swap(): return lax.ppermute(x, AXES[1:], pairs)  10.1 us
    ppermute x11, starting transfers between devices, swap(): lax.ppermute(x, axis, [(i, i ^ mask) for i in range(fine.shape[axis])])  7.69 us
    ppermute x11, waiting for transfers between devices, swap(): lax.ppermute(x, axis, [(i, i ^ mask) for i in range(fine.shape[axis])])  6.36 us
    pallas_call x1, Pallas kernels, per_device(): pl.pallas_call(functools.partial(grad_kernel, n_high), out_shape=outs, in...  5.57 us
    unnamed x10, local copies, waits for them, and re-layouts  3.39 us
    another operation x4, other arithmetic  3.31 us
    pallas_call x2, Pallas kernels, per_device(): pl.pallas_call(functools.partial(logits_kernel, functools.partial(place,...  2.95 us
  transfers between devices with their start and end apart: 23, of which 10 were waited for; matrix products, arithmetic and copies ran while one was open for 11% of the time, Pallas kernels for 2%

profile of v9, /device:TPU:0, one launch (start us, length us, event | category | flops | bytes accessed | tf_op | source)
XLA Modules:
  0.0 68.0 jit_solution(100705842450649403)
XLA Ops:
  0.7 5.6 %shard_map.93 = (bf16[2,2,1,192,128]{4,3,2,1,0:T(8,128)(2,1)}, bf16[2,2,192,128]{3,2,1,0:T(8,128)(2,1)}, bf16[4,2,192,128]{3,2,1,0:T(8,128)(2,1)S(1)}, bf16[2,2,...) custom-call(s32[4]{0:T(128)S(1)} %pad_add_fusion.where_ref, ...), custom_call_target="tpu_custom_call" | custom-call | tf_op jit(solution)/shard_map/pallas_call | solution.py:209
  10.3 1.1 %add_convert_fusion = bf16[2,2,1,192,128]{4,3,1,2,0:T(8,128)(2,1)S(1)} fusion(bf16[2,2,1,192,128]{4,3,1,2,0:T(8,128)(2,1)} %collective-permute-done.3, bf16[2,2,1,192,128]{4,3,2,1,0:T(8,128)(2,1)} %copy-done.2), kind=kLoop, calls=%fused_computation.1 | loop fusion | flops 393216 | bytes 589824 | tf_op jit(solution)/shard_map/convert.5
  11.4 4.0 %collective-permute-start.5 = (bf16[2,1,192,128]{3,2,0,1:T(8,128)(2,1)S(1)}, bf16[2,1,192,128]{3,2,0,1:T(8,128)(2,1)S(1)}, u32[]{:S(2)}, u32[]{:S(2)}) collective-permute-start(bf16[2,1,192,128]{3,2,0,1:T(8,128)(2,1)S(1)} %get-tuple-element.61), channel_id=1, source_target_pairs={{0,9},{1,8},{2,6},{3,7},{4,13},{5,12},{6,2},{7,3},{8,1},{9,0},{10,... | collective-permute-start | bytes 294920 | tf_op jit(solution)/shard_map/ppermute | solution.py:178
  15.3 1.4 %collective-permute-start.4 = (bf16[2,1,192,128]{3,2,0,1:T(8,128)(2,1)S(1)}, bf16[2,1,192,128]{3,2,0,1:T(8,128)(2,1)S(1)}, u32[]{:S(2)}, u32[]{:S(2)}) collective-permute-start(bf16[2,1,192,128]{3,2,0,1:T(8,128)(2,1)S(1)} %get-tuple-element.62), channel_id=1, source_target_pairs={{0,5},{1,4},{2,10},{3,11},{4,1},{5,0},{6,14},{7,15},{8,13},{9,12},... | collective-permute-start | bytes 294920 | tf_op jit(solution)/shard_map/ppermute | solution.py:178
  16.8 1.1 %add_convert_fusion.1 = bf16[2,2,192,128]{3,2,1,0:T(8,128)(2,1)S(1)} fusion(bf16[2,2,192,128]{3,2,1,0:T(8,128)(2,1)} %collective-permute-done, bf16[2,2,192,128]{3,2,1,0:T(8,128)(2,1)} %copy-done.1), kind=kLoop, calls=%fused_computation.2 | loop fusion | flops 393216 | bytes 589824 | tf_op jit(solution)/shard_map/convert.7
  17.8 1.1 %fusion.20 = (bf16[4,2,192,128]{3,2,0,1:T(8,128)(2,1)S(1)}, f32[4,2,192,128]{3,2,0,1:T(8,128)S(1)}) fusion(bf16[4,2,192,128]{3,2,0,1:T(8,128)(2,1)} %collective-permute-done.6, bf16[4,2,192,128]{3,2,1,0:T(8,128)(2,1)S(1)} %get-tuple-element.32), kind=kLoop, calls=%fused_computation.54 | loop fusion | flops 786432 | bytes 1966080 | tf_op jit(solution)/shard_map/convert.3
  19.0 1.4 %collective-permute-start.8 = (bf16[2,192,128]{2,1,0:T(8,128)(2,1)S(1)}, bf16[2,192,128]{2,1,0:T(8,128)(2,1)S(1)}, u32[]{:S(2)}, u32[]{:S(2)}) collective-permute-start(bf16[2,192,128]{2,1,0:T(8,128)(2,1)S(1)} %slice_bitcast_fusion.5), channel_id=1, source_target_pairs={{0,13},{1,12},{2,15},{3,14},{4,9},{5,8},{6,11},{7,10},{8,5},{9,4},... | collective-permute-start | bytes 294920 | tf_op jit(solution)/shard_map/ppermute | solution.py:178
  20.5 2.5 %collective-permute-start.7 = (bf16[2,2,192,128]{3,2,0,1:T(8,128)(2,1)S(1)}, bf16[2,2,192,128]{3,2,0,1:T(8,128)(2,1)S(1)}, u32[]{:S(2)}, u32[]{:S(2)}) collective-permute-start(bf16[2,2,192,128]{3,2,0,1:T(8,128)(2,1)S(1)} %slice.63), channel_id=1, source_target_pairs={{0,12},{1,13},{2,3},{3,2},{4,8},{5,9},{6,7},{7,6},{8,4},{9,5},{10,... | collective-permute-start | bytes 589832 | tf_op jit(solution)/shard_map/ppermute | solution.py:178
  24.1 1.4 %collective-permute-start.2 = (bf16[2,192,128]{2,1,0:T(8,128)(2,1)}, bf16[2,192,128]{2,1,0:T(8,128)(2,1)}, u32[]{:S(2)}, u32[]{:S(2)}) collective-permute-start(bf16[2,192,128]{2,1,0:T(8,128)(2,1)} %get-tuple-element.60), channel_id=1, source_target_pairs={{0,9},{1,8},{2,6},{3,7},{4,13},{5,12},{6,2},{7,3},{8,1},{9,0},{10,... | collective-permute-start | bytes 294920 | tf_op jit(solution)/shard_map/ppermute | solution.py:178
  26.6 1.3 %collective-permute-done.7 = bf16[2,2,192,128]{3,2,0,1:T(8,128)(2,1)S(1)} collective-permute-done((bf16[2,2,192,128]{3,2,0,1:T(8,128)(2,1)S(1)}, bf16[2,2,192,128]{3,2,0,1:T(8,128)(2,1)S(1)}, u32[]{:S(2)}, u32[]{:S(2)}) %collective-permute-start.7) | collective-permute-done | bytes 196640 | tf_op jit(solution)/shard_map/ppermute | solution.py:178
  29.2 2.6 %collective-permute-start.9 = (bf16[2,192,128]{2,1,0:T(8,128)(2,1)}, bf16[2,192,128]{2,1,0:T(8,128)(2,1)}, u32[]{:S(2)}, u32[]{:S(2)}) collective-permute-start(bf16[2,192,128]{2,1,0:T(8,128)(2,1)} %pad_maximum_fusion.4), channel_id=1, source_target_pairs={{0,16},{16,0},{1,17},{17,1},{2,18},{18,2},{3,19},{19,3},{4,20},{20... | collective-permute-start | bytes 294920 | tf_op jit(solution)/shard_map/ppermute | solution.py:168
  31.8 4.3 %collective-permute-done.9 = bf16[2,192,128]{2,1,0:T(8,128)(2,1)} collective-permute-done((bf16[2,192,128]{2,1,0:T(8,128)(2,1)}, bf16[2,192,128]{2,1,0:T(8,128)(2,1)}, u32[]{:S(2)}, u32[]{:S(2)}) %collective-permute-start.9) | collective-permute-done | bytes 98336 | tf_op jit(solution)/shard_map/ppermute | solution.py:168
  39.2 1.2 %fusion.19 = (bf16[192,128]{1,0:T(8,128)(2,1)S(1)}, f32[192,128]{1,0:T(8,128)S(1)}) fusion(f32[3,192,128]{2,1,0:T(8,128)} %copy-done, f32[]{:T(128)} %bitcast.22, f32[]{:T(128)} %bitcast.20, f32[2,192,128]{2,1,0:T(8,128)} %copy-done.4, f32[192,128]{1,0:T(8,128)S(1)} %collective-permute-done.10, f32[2,192,128]{2,1,0:T(8,128)} %copy-done.3, s32[]{:T(128)S(6)} %select_n.55), kind=kLoop, calls=%fused_computation.51 | loop fusion | flops 442368 | bytes 737292 | tf_op jit(solution)/shard_map/convert_element_type | solution.py:273
  40.6 1.4 %collective-permute-start.19 = (f32[192,128]{1,0:T(8,128)S(1)}, f32[192,128]{1,0:T(8,128)S(1)}, u32[]{:S(2)}, u32[]{:S(2)}) collective-permute-start(f32[192,128]{1,0:T(8,128)S(1)} %get-tuple-element.54), channel_id=1, source_target_pairs={{0,1},{1,0},{2,3},{3,2},{4,5},{5,4},{6,7},{7,6},{8,9},{9,8},{10,11... | collective-permute-start | bytes 294920 | tf_op jit(solution)/shard_map/ppermute | solution.py:168
  42.0 1.8 %collective-permute-start.14 = (bf16[2,192,128]{2,1,0:T(8,128)(2,1)S(1)}, bf16[2,192,128]{2,1,0:T(8,128)(2,1)S(1)}, u32[]{:S(2)}, u32[]{:S(2)}) collective-permute-start(bf16[2,192,128]{2,1,0:T(8,128)(2,1)S(1)} %maximum_select_fusion.1), channel_id=1, source_target_pairs={{0,16},{16,0},{1,17},{17,1},{2,18},{18,2},{3,19},{19,3},{4,20},{20... | collective-permute-start | bytes 294920 | tf_op jit(solution)/shard_map/ppermute | solution.py:168
  43.8 2.3 %collective-permute-start.13 = (bf16[2,192,128]{2,1,0:T(8,128)(2,1)S(1)}, bf16[2,192,128]{2,1,0:T(8,128)(2,1)S(1)}, u32[]{:S(2)}, u32[]{:S(2)}) collective-permute-start(bf16[2,192,128]{2,1,0:T(8,128)(2,1)S(1)} %maximum_select_fusion.1), channel_id=1, source_target_pairs={{0,9},{1,8},{2,6},{3,7},{4,13},{5,12},{6,2},{7,3},{8,1},{9,0},{10,... | collective-permute-start | bytes 294920 | tf_op jit(solution)/shard_map/ppermute | solution.py:178
  46.1 1.4 %collective-permute-start.12 = (bf16[2,192,128]{2,1,0:T(8,128)(2,1)S(1)}, bf16[2,192,128]{2,1,0:T(8,128)(2,1)S(1)}, u32[]{:S(2)}, u32[]{:S(2)}) collective-permute-start(bf16[2,192,128]{2,1,0:T(8,128)(2,1)S(1)} %maximum_select_fusion.1), channel_id=1, source_target_pairs={{0,5},{1,4},{2,10},{3,11},{4,1},{5,0},{6,14},{7,15},{8,13},{9,12},... | collective-permute-start | bytes 294920 | tf_op jit(solution)/shard_map/ppermute | solution.py:178
  47.5 2.0 %multiply_subtract_fusion = (f32[384,128]{1,0:T(8,128)}, f32[384,128]{1,0:T(8,128)}, f32[384,128]{1,0:T(8,128)}) fusion(f32[384,128]{1,0:T(8,128)} %refs_0_.1, f32[]{:T(128)} %bitcast.22, f32[]{:T(128)} %bitcast.20, f32[192,128]{1,0:T(8,128)S(1)} %get-tuple-element.54, f32[192,128]{1,0:T(8,128)S(1)} %collective-permute-done.19, pred[]{:T(512)S(6)} %eq.12, ...), kind=kLoop, calls=%fused_computation.18 | loop fusion | flops 884736 | bytes 1376265 | tf_op jit(solution)/shard_map/sub | solution.py:29
  50.0 1.9 %collective-permute-done.13 = bf16[2,192,128]{2,1,0:T(8,128)(2,1)S(1)} collective-permute-done((bf16[2,192,128]{2,1,0:T(8,128)(2,1)S(1)}, bf16[2,192,128]{2,1,0:T(8,128)(2,1)S(1)}, u32[]{:S(2)}, u32[]{:S(2)}) %collective-permute-start.13) | collective-permute-done | bytes 98336 | tf_op jit(solution)/shard_map/ppermute | solution.py:178
  52.9 1.4 %collective-permute-start.15 = (bf16[2,1,192,128]{3,2,0,1:T(8,128)(2,1)S(1)}, bf16[2,1,192,128]{3,2,0,1:T(8,128)(2,1)S(1)}, u32[]{:S(2)}, u32[]{:S(2)}) collective-permute-start(bf16[2,1,192,128]{3,2,0,1:T(8,128)(2,1)S(1)} %bitcast.91), channel_id=1, source_target_pairs={{0,5},{1,4},{2,10},{3,11},{4,1},{5,0},{6,14},{7,15},{8,13},{9,12},... | collective-permute-start | bytes 294920 | tf_op jit(solution)/shard_map/ppermute | solution.py:178
  54.2 2.5 %collective-permute-start.17 = (bf16[2,2,192,128]{3,2,0,1:T(8,128)(2,1)S(1)}, bf16[2,2,192,128]{3,2,0,1:T(8,128)(2,1)S(1)}, u32[]{:S(2)}, u32[]{:S(2)}) collective-permute-start(bf16[2,2,192,128]{3,2,0,1:T(8,128)(2,1)S(1)} %pad_maximum_fusion.1), channel_id=1, source_target_pairs={{0,12},{1,13},{2,3},{3,2},{4,8},{5,9},{6,7},{7,6},{8,4},{9,5},{10,... | collective-permute-start | bytes 589832 | tf_op jit(solution)/shard_map/ppermute | solution.py:178
  57.8 5.5 %collective-permute-done.18 = bf16[2,192,128]{2,1,0:T(8,128)(2,1)S(1)} collective-permute-done((bf16[2,192,128]{2,1,0:T(8,128)(2,1)S(1)}, bf16[2,192,128]{2,1,0:T(8,128)(2,1)S(1)}, u32[]{:S(2)}, u32[]{:S(2)}) %collective-permute-start.18) | collective-permute-done | bytes 98336 | tf_op jit(solution)/shard_map/ppermute | solution.py:178
  65.0 1.4 %shard_map.94.refs_2_ = f32[256,128]{1,0:T(8,128)S(1)} custom-call(s32[4]{0:T(128)S(1)} %pad_add_fusion.where_ref, bf16[6,256,768]{2,1,0:T(8,128)(2,1)S(1)} %get-tuple-element.45.columns_ref, bf16[2,2,192,128]{3,2,1,0:T(8,128)(2,1)S(1)} %pad_maximum_fusion.3.refs_0_, bf16[2,2,192,128]{3,2,1,0:T(8,128)(2,1)S(1)} %collective-permute-done.21.refs_1_, ...), custom_call_target="tpu_custom_call" | custom-call | tf_op jit(solution)/shard_map/pallas_call | solution.py:312
  66.4 1.6 %shard_map.95 = bf16[256,128]{1,0:T(8,128)(2,1)} custom-call(s32[4]{0:T(128)S(1)} %pad_add_fusion.where_ref, bf16[2,256,768]{2,1,0:T(8,128)(2,1)S(1)} %get-tuple-element.42.columns_ref, bf16[2,2,1,192,128]{4,3,2,1,0:T(8,128)(2,1)S(1)} %pad_maximum_fusion.2.refs_0_, bf16[2,2,1,192,128]{4,3,2,1,0:T(8,128)(2,1)S(1)} %collective-permute-done.20.refs_1_, ...), custom_call_target="tpu_custom_call" | custom-call | tf_op jit(solution)/shard_map/pallas_call | solution.py:312
  (63 shorter events, 14.3 us)
Async XLA Ops:
  6.3 0.7 %copy-start = (f32[3,192,128]{2,1,0:T(8,128)}, f32[3,192,128]{2,1,0:T(8,128)S(1)}, u32[]{:S(2)}) copy-start(f32[3,192,128]{2,1,0:T(8,128)S(1)} %get-tuple-element.27) | copy-start | bytes 884740
  8.4 1.9 %collective-permute-start.3 = (bf16[2,2,1,192,128]{4,3,1,2,0:T(8,128)(2,1)}, bf16[2,2,1,192,128]{4,3,1,2,0:T(8,128)(2,1)}, u32[]{:S(2)}, u32[]{:S(2)}) collective-permute-start(bf16[2,2,1,192,128]{4,3,1,2,0:T(8,128)(2,1)} %bitcast.9), channel_id=1, source_target_pairs={{0,2},{2,0},{1,3},{3,1},{4,6},{6,4},{5,7},{7,5},{8,10},{10,8},{9,1... | collective-permute-start | bytes 589832 | tf_op jit(solution)/shard_map/ppermute | solution.py:168
  8.8 7.9 %collective-permute-start = (bf16[2,2,192,128]{3,2,1,0:T(8,128)(2,1)}, bf16[2,2,192,128]{3,2,1,0:T(8,128)(2,1)}, u32[]{:S(2)}, u32[]{:S(2)}) collective-permute-start(bf16[2,2,192,128]{3,2,1,0:T(8,128)(2,1)} %get-tuple-element.29), channel_id=1, source_target_pairs={{0,2},{2,0},{1,3},{3,1},{4,6},{6,4},{5,7},{7,5},{8,10},{10,8},{9,1... | collective-permute-start | bytes 589832 | tf_op jit(solution)/shard_map/ppermute | solution.py:168
  9.7 8.2 %collective-permute-start.6 = (bf16[4,2,192,128]{3,2,0,1:T(8,128)(2,1)}, bf16[4,2,192,128]{3,2,0,1:T(8,128)(2,1)}, u32[]{:S(2)}, u32[]{:S(2)}) collective-permute-start(bf16[4,2,192,128]{3,2,0,1:T(8,128)(2,1)} %copy.13), channel_id=1, source_target_pairs={{0,2},{2,0},{1,3},{3,1},{4,6},{6,4},{5,7},{7,5},{8,10},{10,8},{9,1... | collective-permute-start | bytes 1179656 | tf_op jit(solution)/shard_map/ppermute | solution.py:168
  11.4 12.8 %collective-permute-start.5 = (bf16[2,1,192,128]{3,2,0,1:T(8,128)(2,1)S(1)}, bf16[2,1,192,128]{3,2,0,1:T(8,128)(2,1)S(1)}, u32[]{:S(2)}, u32[]{:S(2)}) collective-permute-start(bf16[2,1,192,128]{3,2,0,1:T(8,128)(2,1)S(1)} %get-tuple-element.61), channel_id=1, source_target_pairs={{0,9},{1,8},{2,6},{3,7},{4,13},{5,12},{6,2},{7,3},{8,1},{9,0},{10,... | collective-permute-start | bytes 294920 | tf_op jit(solution)/shard_map/ppermute | solution.py:178
  15.3 10.2 %collective-permute-start.4 = (bf16[2,1,192,128]{3,2,0,1:T(8,128)(2,1)S(1)}, bf16[2,1,192,128]{3,2,0,1:T(8,128)(2,1)S(1)}, u32[]{:S(2)}, u32[]{:S(2)}) collective-permute-start(bf16[2,1,192,128]{3,2,0,1:T(8,128)(2,1)S(1)} %get-tuple-element.62), channel_id=1, source_target_pairs={{0,5},{1,4},{2,10},{3,11},{4,1},{5,0},{6,14},{7,15},{8,13},{9,12},... | collective-permute-start | bytes 294920 | tf_op jit(solution)/shard_map/ppermute | solution.py:178
  19.0 7.5 %collective-permute-start.8 = (bf16[2,192,128]{2,1,0:T(8,128)(2,1)S(1)}, bf16[2,192,128]{2,1,0:T(8,128)(2,1)S(1)}, u32[]{:S(2)}, u32[]{:S(2)}) collective-permute-start(bf16[2,192,128]{2,1,0:T(8,128)(2,1)S(1)} %slice_bitcast_fusion.5), channel_id=1, source_target_pairs={{0,13},{1,12},{2,15},{3,14},{4,9},{5,8},{6,11},{7,10},{8,5},{9,4},... | collective-permute-start | bytes 294920 | tf_op jit(solution)/shard_map/ppermute | solution.py:178
  20.5 7.4 %collective-permute-start.7 = (bf16[2,2,192,128]{3,2,0,1:T(8,128)(2,1)S(1)}, bf16[2,2,192,128]{3,2,0,1:T(8,128)(2,1)S(1)}, u32[]{:S(2)}, u32[]{:S(2)}) collective-permute-start(bf16[2,2,192,128]{3,2,0,1:T(8,128)(2,1)S(1)} %slice.63), channel_id=1, source_target_pairs={{0,12},{1,13},{2,3},{3,2},{4,8},{5,9},{6,7},{7,6},{8,4},{9,5},{10,... | collective-permute-start | bytes 589832 | tf_op jit(solution)/shard_map/ppermute | solution.py:178
  23.7 8.2 %collective-permute-start.1 = (bf16[2,192,128]{2,1,0:T(8,128)(2,1)}, bf16[2,192,128]{2,1,0:T(8,128)(2,1)}, u32[]{:S(2)}, u32[]{:S(2)}) collective-permute-start(bf16[2,192,128]{2,1,0:T(8,128)(2,1)} %get-tuple-element.59), channel_id=1, source_target_pairs={{0,5},{1,4},{2,10},{3,11},{4,1},{5,0},{6,14},{7,15},{8,13},{9,12},... | collective-permute-start | bytes 294920 | tf_op jit(solution)/shard_map/ppermute | solution.py:178
  24.1 7.7 %collective-permute-start.2 = (bf16[2,192,128]{2,1,0:T(8,128)(2,1)}, bf16[2,192,128]{2,1,0:T(8,128)(2,1)}, u32[]{:S(2)}, u32[]{:S(2)}) collective-permute-start(bf16[2,192,128]{2,1,0:T(8,128)(2,1)} %get-tuple-element.60), channel_id=1, source_target_pairs={{0,9},{1,8},{2,6},{3,7},{4,13},{5,12},{6,2},{7,3},{8,1},{9,0},{10,... | collective-permute-start | bytes 294920 | tf_op jit(solution)/shard_map/ppermute | solution.py:178
  29.2 6.9 %collective-permute-start.9 = (bf16[2,192,128]{2,1,0:T(8,128)(2,1)}, bf16[2,192,128]{2,1,0:T(8,128)(2,1)}, u32[]{:S(2)}, u32[]{:S(2)}) collective-permute-start(bf16[2,192,128]{2,1,0:T(8,128)(2,1)} %pad_maximum_fusion.4), channel_id=1, source_target_pairs={{0,16},{16,0},{1,17},{17,1},{2,18},{18,2},{3,19},{19,3},{4,20},{20... | collective-permute-start | bytes 294920 | tf_op jit(solution)/shard_map/ppermute | solution.py:168
  37.9 1.4 %collective-permute-start.10 = (f32[192,128]{1,0:T(8,128)S(1)}, f32[192,128]{1,0:T(8,128)S(1)}, u32[]{:S(2)}, u32[]{:S(2)}) collective-permute-start(f32[192,128]{1,0:T(8,128)S(1)} %dynamic-slice_bitcast_fusion), channel_id=1, source_target_pairs={{0,2},{2,0},{1,3},{3,1},{4,6},{6,4},{5,7},{7,5},{8,10},{10,8},{9,1... | collective-permute-start | bytes 294920 | tf_op jit(solution)/shard_map/ppermute | solution.py:168
  40.4 1.6 %collective-permute-start.11 = (bf16[192,128]{1,0:T(8,128)(2,1)S(1)}, bf16[192,128]{1,0:T(8,128)(2,1)S(1)}, u32[]{:S(2)}, u32[]{:S(2)}) collective-permute-start(bf16[192,128]{1,0:T(8,128)(2,1)S(1)} %get-tuple-element.53), channel_id=1, source_target_pairs={{0,2},{2,0},{1,3},{3,1},{4,6},{6,4},{5,7},{7,5},{8,10},{10,8},{9,1... | collective-permute-start | bytes 147464 | tf_op jit(solution)/shard_map/ppermute | solution.py:168
  40.6 6.9 %collective-permute-start.19 = (f32[192,128]{1,0:T(8,128)S(1)}, f32[192,128]{1,0:T(8,128)S(1)}, u32[]{:S(2)}, u32[]{:S(2)}) collective-permute-start(f32[192,128]{1,0:T(8,128)S(1)} %get-tuple-element.54), channel_id=1, source_target_pairs={{0,1},{1,0},{2,3},{3,2},{4,5},{5,4},{6,7},{7,6},{8,9},{9,8},{10,11... | collective-permute-start | bytes 294920 | tf_op jit(solution)/shard_map/ppermute | solution.py:168
  42.0 7.9 %collective-permute-start.14 = (bf16[2,192,128]{2,1,0:T(8,128)(2,1)S(1)}, bf16[2,192,128]{2,1,0:T(8,128)(2,1)S(1)}, u32[]{:S(2)}, u32[]{:S(2)}) collective-permute-start(bf16[2,192,128]{2,1,0:T(8,128)(2,1)S(1)} %maximum_select_fusion.1), channel_id=1, source_target_pairs={{0,16},{16,0},{1,17},{17,1},{2,18},{18,2},{3,19},{19,3},{4,20},{20... | collective-permute-start | bytes 294920 | tf_op jit(solution)/shard_map/ppermute | solution.py:168
  43.8 8.1 %collective-permute-start.13 = (bf16[2,192,128]{2,1,0:T(8,128)(2,1)S(1)}, bf16[2,192,128]{2,1,0:T(8,128)(2,1)S(1)}, u32[]{:S(2)}, u32[]{:S(2)}) collective-permute-start(bf16[2,192,128]{2,1,0:T(8,128)(2,1)S(1)} %maximum_select_fusion.1), channel_id=1, source_target_pairs={{0,9},{1,8},{2,6},{3,7},{4,13},{5,12},{6,2},{7,3},{8,1},{9,0},{10,... | collective-permute-start | bytes 294920 | tf_op jit(solution)/shard_map/ppermute | solution.py:178
  46.1 6.2 %collective-permute-start.12 = (bf16[2,192,128]{2,1,0:T(8,128)(2,1)S(1)}, bf16[2,192,128]{2,1,0:T(8,128)(2,1)S(1)}, u32[]{:S(2)}, u32[]{:S(2)}) collective-permute-start(bf16[2,192,128]{2,1,0:T(8,128)(2,1)S(1)} %maximum_select_fusion.1), channel_id=1, source_target_pairs={{0,5},{1,4},{2,10},{3,11},{4,1},{5,0},{6,14},{7,15},{8,13},{9,12},... | collective-permute-start | bytes 294920 | tf_op jit(solution)/shard_map/ppermute | solution.py:178
  52.3 11.0 %collective-permute-start.16 = (bf16[2,1,192,128]{3,2,0,1:T(8,128)(2,1)S(1)}, bf16[2,1,192,128]{3,2,0,1:T(8,128)(2,1)S(1)}, u32[]{:S(2)}, u32[]{:S(2)}) collective-permute-start(bf16[2,1,192,128]{3,2,0,1:T(8,128)(2,1)S(1)} %bitcast.90), channel_id=1, source_target_pairs={{0,9},{1,8},{2,6},{3,7},{4,13},{5,12},{6,2},{7,3},{8,1},{9,0},{10,... | collective-permute-start | bytes 294920 | tf_op jit(solution)/shard_map/ppermute | solution.py:178
  52.9 10.4 %collective-permute-start.15 = (bf16[2,1,192,128]{3,2,0,1:T(8,128)(2,1)S(1)}, bf16[2,1,192,128]{3,2,0,1:T(8,128)(2,1)S(1)}, u32[]{:S(2)}, u32[]{:S(2)}) collective-permute-start(bf16[2,1,192,128]{3,2,0,1:T(8,128)(2,1)S(1)} %bitcast.91), channel_id=1, source_target_pairs={{0,5},{1,4},{2,10},{3,11},{4,1},{5,0},{6,14},{7,15},{8,13},{9,12},... | collective-permute-start | bytes 294920 | tf_op jit(solution)/shard_map/ppermute | solution.py:178
  54.2 9.0 %collective-permute-start.17 = (bf16[2,2,192,128]{3,2,0,1:T(8,128)(2,1)S(1)}, bf16[2,2,192,128]{3,2,0,1:T(8,128)(2,1)S(1)}, u32[]{:S(2)}, u32[]{:S(2)}) collective-permute-start(bf16[2,2,192,128]{3,2,0,1:T(8,128)(2,1)S(1)} %pad_maximum_fusion.1), channel_id=1, source_target_pairs={{0,12},{1,13},{2,3},{3,2},{4,8},{5,9},{6,7},{7,6},{8,4},{9,5},{10,... | collective-permute-start | bytes 589832 | tf_op jit(solution)/shard_map/ppermute | solution.py:178
  56.8 6.5 %collective-permute-start.18 = (bf16[2,192,128]{2,1,0:T(8,128)(2,1)S(1)}, bf16[2,192,128]{2,1,0:T(8,128)(2,1)S(1)}, u32[]{:S(2)}, u32[]{:S(2)}) collective-permute-start(bf16[2,192,128]{2,1,0:T(8,128)(2,1)S(1)} %fusion.11), channel_id=1, source_target_pairs={{0,13},{1,12},{2,15},{3,14},{4,9},{5,8},{6,11},{7,10},{8,5},{9,4},... | collective-permute-start | bytes 294920 | tf_op jit(solution)/shard_map/ppermute | solution.py:178
  57.7 7.3 %collective-permute-start.21 = (bf16[2,2,192,128]{3,2,1,0:T(8,128)(2,1)S(1)}, bf16[2,2,192,128]{3,2,1,0:T(8,128)(2,1)S(1)}, u32[]{:S(2)}, u32[]{:S(2)}) collective-permute-start(bf16[2,2,192,128]{3,2,1,0:T(8,128)(2,1)S(1)} %pad_maximum_fusion.3.refs_0_), channel_id=1, source_target_pairs={{0,2},{2,0},{1,3},{3,1},{4,6},{6,4},{5,7},{7,5},{8,10},{10,8},{9,1... | collective-permute-start | bytes 589832 | tf_op jit(solution)/shard_map/ppermute | solution.py:168
  63.3 1.6 %collective-permute-start.22 = (bf16[3,2,192,128]{3,2,0,1:T(8,128)(2,1)S(1)}, bf16[3,2,192,128]{3,2,0,1:T(8,128)(2,1)S(1)}, u32[]{:S(2)}, u32[]{:S(2)}) collective-permute-start(bf16[3,2,192,128]{3,2,0,1:T(8,128)(2,1)S(1)} %pad_maximum_fusion), channel_id=1, source_target_pairs={{0,2},{2,0},{1,3},{3,1},{4,6},{6,4},{5,7},{7,5},{8,10},{10,8},{9,1... | collective-permute-start | bytes 884744 | tf_op jit(solution)/shard_map/ppermute | solution.py:168
  63.4 3.0 %collective-permute-start.20 = (bf16[2,2,1,192,128]{4,3,2,1,0:T(8,128)(2,1)S(1)}, bf16[2,2,1,192,128]{4,3,2,1,0:T(8,128)(2,1)S(1)}, u32[]{:S(2)}, u32[]{:S(2)}) collective-permute-start(bf16[2,2,1,192,128]{4,3,2,1,0:T(8,128)(2,1)S(1)} %pad_maximum_fusion.2.refs_0_), channel_id=1, source_target_pairs={{0,2},{2,0},{1,3},{3,1},{4,6},{6,4},{5,7},{7,5},{8,10},{10,8},{9,1... | collective-permute-start | bytes 589832 | tf_op jit(solution)/shard_map/ppermute | solution.py:168
  (4 other events, 2.7 us)

commit v10 on v9

--- a/solution.py
+++ b/solution.py
@@ -10,12 +10,13 @@
 
 AXES = ("high", "low", "core", "rep")
 N_LOW = 4
-FIRST = (1, 2)
 VMEM_LIMIT = 8 * 2**20
 
 
-def parity(n):
-    return (n ^ (n >> 1)) & 1
+def partner(slot, core):
+    if slot < 2:
+        return 1 + core, 1 ^ slot ^ core
+    return 3 * (1 - core), core
 
 
 def adamw(grad, master, moment_one, moment_two, step_count):
@@ -31,11 +32,12 @@
 
 
 def near_places(core, n_high):
-    return [(k, 0) for k in FIRST] + [(k, j) for k in (3 * (1 - core), 3 * core) for j in range(n_high)]
-
-
-def far_places(n_high):
-    return [(k, j) for k in FIRST for j in range(1, n_high)]
+    slot_2 = [(partner(2, c)[0], j) for c in (core, 1 - core) for j in range(n_high)]
+    return [(partner(0, c)[0], 0) for c in (core, 1 - core)] + slot_2
+
+
+def far_places(core, n_high):
+    return [(partner(0, c)[0], j) for c in (core, 1 - core) for j in range(1, n_high)]
 
 
 def load_columns(acts_ref, columns, sems, first_sem, high, low, places):
@@ -60,7 +62,7 @@
     last = sems.shape[0]
     loads = pltpu.make_async_copy(grad_ref, logit_grads, sems.at[last - 1])
     loads.start()
-    places = near_places(core, n_high), far_places(n_high)
+    places = near_places(core, n_high), far_places(core, n_high)
     loaded = []
     for at, columns in zip(places, (near_columns, far_columns)):
         copies = load_columns(acts_ref, columns, sems, len(loaded), high, low, at)
@@ -84,23 +86,31 @@
             j = j + 1
         else:
             p, j = (m, 0) if m < 2 else divmod(m - 2, n_high)
+        far, near, rest = (kept_far, kept_near, kept_rest) if p == 0 else (away_far, away_near, away_rest)
+        of_core = core ^ p
         if columns is far_columns or m < 2:
-            flip = rep ^ core ^ parity(FIRST[p])
+            for slot in range(2):
+                of_rep = rep ^ partner(slot, of_core)[1]
+                for c in range(2):
+                    if j:
+                        far[slot, c, j - 1] = blocks[c, of_rep]
+                    else:
+                        near[slot, c] = blocks[c, of_rep]
+        else:
+            of_rep = rep ^ partner(2, of_core)[1]
             for c in range(2):
-                if j:
-                    kept_far[p ^ core, c, j - 1] = blocks[c, flip]
-                    away_far[p ^ core ^ 1, c, j - 1] = blocks[c, flip ^ 1]
-                else:
-                    kept_near[p ^ core, c] = blocks[c, flip]
-                    away_near[p ^ core ^ 1, c] = blocks[c, flip ^ 1]
-        else:
-            slot = kept_rest if p == 0 else away_rest
-            flip = rep ^ core ^ p
-            for c in range(2):
-                slot[c, j] = blocks[c, flip]
-            kept_rest[2 + (core ^ p), j] = blocks[core, flip ^ 1]
-            away_rest[2 + (core ^ p), j] = blocks[core ^ 1, flip ^ 1]
+                rest[c, j] = blocks[c, of_rep]
+            kept_rest[2 + of_core, j] = blocks[core, of_rep ^ 1]
+            away_rest[2 + of_core, j] = blocks[core ^ 1, of_rep ^ 1]
     for copy in state:
+        copy.wait()
+
+
+def columns_kernel(n_high, where_ref, acts_ref, near_columns, far_columns, sems):
+    high, low, core = [where_ref[i] for i in range(3)]
+    copies = load_columns(acts_ref, near_columns, sems, 0, high, low, near_places(core, n_high))
+    copies += load_columns(acts_ref, far_columns, sems, len(copies), high, low, far_places(core, n_high))
+    for copy in copies:
         copy.wait()
 
 
@@ -124,22 +134,18 @@
     out_ref[...] = total.astype(out_ref.dtype)
 
 
-def slot_owner(core, rep, i, slot, c):
-    of_core = core ^ i
-    return of_core ^ slot, c, rep ^ parity(FIRST[slot]) ^ of_core
-
-
 def near_place(core, rep, n_high):
     pieces = []
     for i in range(2):
-        at = [(slot, c, *slot_owner(core, rep, i, slot, c)) for slot in range(2) for c in range(2)]
-        pieces.append([((slot, c), n, owner, of_rep) for slot, c, n, owner, of_rep in at])
+        of_rep = [rep ^ partner(slot, core ^ i)[1] for slot in range(2)]
+        pieces.append([((slot, c), i, c, of_rep[slot]) for slot in range(2) for c in range(2)])
     low_3, low_0 = 2 + n_high * core, 2 + n_high * (1 - core)
     for i in range(2):
         of_core = core ^ i
+        of_rep = rep ^ partner(2, of_core)[1]
         blocks = []
         for j in range(n_high):
-            blocks += [((c, j), 2 + n_high * i + j, c, rep ^ of_core) for c in range(2)]
+            blocks += [((c, j), 2 + n_high * i + j, c, of_rep) for c in range(2)]
             blocks.append(((2, j), low_3 + j, of_core, rep ^ 1))
         pieces.append(blocks)
     pieces.append([((c, j), low_0 + j, c, rep) for c in range(2) for j in range(n_high)])
@@ -151,10 +157,10 @@
     for i in range(2):
         blocks = []
         for slot in range(2):
+            of_rep = rep ^ partner(slot, core ^ i)[1]
             for c in range(2):
-                which, owner, of_rep = slot_owner(core, rep, i, slot, c)
                 for j in range(n_high - 1):
-                    blocks.append(((slot, c, j), which * (n_high - 1) + j, owner, of_rep))
+                    blocks.append(((slot, c, j), i * (n_high - 1) + j, c, of_rep))
         pieces.append(blocks)
     return pieces
 
@@ -177,8 +183,8 @@
                     pairs.append(((low * 2 + core) * n_rep + rep, there))
         return lax.ppermute(x, AXES[1:], pairs)
 
-    def to_partner(x, k):
-        return cube_swap(x, lambda core: (k ^ (3 * core), parity(k) ^ core))
+    def to_partner(x, slot):
+        return cube_swap(x, lambda core: partner(slot, core))
 
     def to_corner(x):
         return cube_swap(x, lambda core: (3, 1))
@@ -205,13 +211,14 @@
             outs = [pltpu.VMEM((*shape, half, experts), bf16) for shape in shapes]
             outs.append(pltpu.VMEM((3, half, experts), f32))
             counts = 2 + 2 * n_high, 2 * (n_high - 1)
-            outs += [pltpu.VMEM((n, tokens, 4 * half), bf16) for n in counts]
-            *sorted_rows, mine, near_columns, far_columns = pl.pallas_call(
+            columns = [pltpu.VMEM((n, tokens, 4 * half), bf16) for n in counts]
+            *sorted_rows, mine = pl.pallas_call(
                 functools.partial(grad_kernel, n_high),
                 out_shape=outs,
                 in_specs=[smem] + [anywhere] * 5,
                 out_specs=[vmem] * len(outs),
-                scratch_shapes=[
+                scratch_shapes=columns
+                + [
                     pltpu.VMEM((tokens, experts), bf16),
                     pltpu.VMEM((2, 2, half, experts), bf16),
                     pltpu.SemaphoreType.DMA((4 * n_high + 4,)),
@@ -223,9 +230,7 @@
                 *(pltpu.with_memory_space_constraint(x, pltpu.HBM) for x in (grad_logits, *state_in)),
             )
             away, kept = sorted_rows[:3], sorted_rows[3:]
-            columns = (near_columns, far_columns)
         else:
-            columns = (None, None)
             product = lax.dot_general(
                 acts, grad_logits, (((0,), (0,)), ((), ())), preferred_element_type=f32
             ).astype(bf16)
@@ -237,13 +242,13 @@
                 part = lax.dynamic_slice(product, at, (n_high, 1, 1, 1, half, experts))
                 return part.reshape(n_high, half, experts)
 
-            def slot(k, of_core):
-                change = k ^ (3 * of_core), parity(k) ^ of_core
-                return jnp.stack([block(change[0], c, change[1]) for c in range(2)])
-
             def sort_rows(of_core):
-                first = jnp.stack([slot(k, of_core) for k in FIRST])
-                rest = [slot(3, of_core), block(3, of_core, 1)[None], block(0, of_core, 0)[None]]
+                slots = []
+                for slot in range(3):
+                    d_low, d_rep = partner(slot, of_core)
+                    slots.append(jnp.stack([block(d_low, c, d_rep) for c in range(2)]))
+                first = jnp.stack(slots[:2])
+                rest = [slots[2], block(3, of_core, 1)[None], block(0, of_core, 0)[None]]
                 return first[:, :, 1:], first[:, :, 0], jnp.concatenate(rest)
 
             away, kept = sort_rows(1 - core), sort_rows(core)
@@ -253,20 +258,34 @@
             mine_too.astype(f32) + swap(theirs, "core").astype(f32)
             for mine_too, theirs in zip(kept, away)
         ]
-        far = [to_partner(far[i].astype(bf16), k) for i, k in enumerate(FIRST)]
-        slot_3 = to_partner(rest[:2].astype(bf16), 3)
+        far = [to_partner(far[slot].astype(bf16), slot) for slot in range(2)]
+        slot_2 = to_partner(rest[:2].astype(bf16), 2)
         corner = to_corner(rest[2].astype(bf16))
         home = rest[3]
-        near = [to_partner(near[i].astype(bf16), k) for i, k in enumerate(FIRST)]
-
-        *far, slot_3, corner = [x.astype(f32) for x in lax.optimization_barrier((*far, slot_3, corner))]
+        near = [to_partner(near[slot].astype(bf16), slot) for slot in range(2)]
+
+        *far, slot_2, corner = [x.astype(f32) for x in lax.optimization_barrier((*far, slot_2, corner))]
         mine_only = corner + home
-        far = far[0] + far[1] + slot_3[:, 1:]
+        far = far[0] + far[1] + slot_2[:, 1:]
         far = [far[c] + jnp.where(core == c, mine_only[1:], 0.0) for c in range(2)]
         far = jnp.stack(far, 1).astype(bf16)
-        total = near[0].astype(f32) + near[1].astype(f32) + slot_3[:, 0]
-        for j in range(1, n_high):
-            total = total + swap(far[j - 1], "high", j).astype(f32)
+        sent = [swap(far[j - 1], "high", j) for j in range(1, n_high)]
+        near, late_acts = lax.optimization_barrier((near, acts))
+        total = near[0].astype(f32) + near[1].astype(f32) + slot_2[:, 0]
+        for part in sent:
+            total = total + part.astype(f32)
+        if in_kernels:
+            columns = pl.pallas_call(
+                functools.partial(columns_kernel, n_high),
+                out_shape=columns,
+                in_specs=[smem, anywhere],
+                out_specs=[vmem, vmem],
+                scratch_shapes=[pltpu.SemaphoreType.DMA((4 * n_high,))],
+                compiler_params=params,
+            )(where, pltpu.with_memory_space_constraint(late_acts, pltpu.HBM))
+            total, columns = lax.optimization_barrier((total, columns))
+        else:
+            columns = (None, None)
         theirs = swap(lax.dynamic_index_in_dim(total, 1 - core, 0, keepdims=False), "core")
         grad = lax.dynamic_index_in_dim(total, core, 0, keepdims=False) + theirs + mine_only[0]
 
@@ -274,14 +293,14 @@
         across = swap(weight, "core")
         near = jnp.where(core == 0, jnp.stack([weight, across]), jnp.stack([across, weight]))
         far = [swap(near, "high", j) for j in range(1, n_high)]
-        got_near = [to_partner(near, k) for k in FIRST]
+        got_near = [to_partner(near, slot) for slot in range(2)]
+        got_near, far, grad = lax.optimization_barrier((got_near, far, grad))
         other = swap(grad, "rep")
-        got_near, far = lax.optimization_barrier((got_near, far))
         chip = jnp.stack([near, *far], 1)
         far = chip[:, 1:]
-        slot_3 = to_partner(chip, 3)
+        slot_2 = to_partner(chip, 2)
         corner = to_corner(lax.dynamic_index_in_dim(chip, core, 0, keepdims=False))
-        got_far = [to_partner(far, k) for k in FIRST]
+        got_far = [to_partner(far, slot) for slot in range(2)]
 
         whole = jnp.where(
             rep == 0,
@@ -289,16 +308,16 @@
             jnp.concatenate([other, grad], 0),
         )
         state = adamw(whole, *state_in, step_count)
-        got_far, slot_3, corner, state = lax.optimization_barrier((got_far, slot_3, corner, state))
+        got_far, slot_2, corner, state = lax.optimization_barrier((got_far, slot_2, corner, state))
         near = jnp.stack(got_near)
         near_over = swap(near, "core")
-        rest = jnp.concatenate([slot_3, corner[None]])
+        rest = jnp.concatenate([slot_2, corner[None]])
         rest_over = swap(rest, "core")
         far = jnp.stack(got_far)
         far_over = swap(far, "core")
 
         pieces = ([near, near_over, rest, rest_over, chip], [far, far_over])
-        stages = (near_places(core, n_high), far_places(n_high))
+        stages = (near_places(core, n_high), far_places(core, n_high))
         logits = None
         for blocks, place, received, acts_columns in zip(
             stages, (near_place, far_place), pieces, columns

time: 68.3 us -> 65 us (0.952)
  other arithmetic: 8.49 us -> 5.36 us
  Pallas kernels: 8.52 us -> 10.2 us
  local copies, waits for them, and re-layouts: 4.93 us -> 4.09 us
  waiting for transfers between devices: 16.4 us -> 15.7 us
    ppermute x12, waiting for transfers between devices: 10.1 us -> 6.15 us  [cube_swap(): return lax.ppermute(x, AXES[1:], pairs)]
    ppermute x11, waiting for transfers between devices: 6.36 us -> 9.52 us  [swap(): lax.ppermute(x, axis, [(i, i ^ mask) for i in range(fine.shape[axis])])]
    another operation x4, other arithmetic: 3.31 us -> 0.25 us
    pallas_call x0 -> x1, Pallas kernels: none -> 2.46 us  [per_device(): pl.pallas_call(functools.partial(columns_kernel, n_high), out_shape=colum...]
    ppermute x12, starting transfers between devices: 20.3 us -> 18.9 us  [cube_swap(): return lax.ppermute(x, AXES[1:], pairs)]
    ppermute x11, starting transfers between devices: 7.69 us -> 8.93 us  [swap(): lax.ppermute(x, axis, [(i, i ^ mask) for i in range(fine.shape[axis])])]
    pallas_call x1, Pallas kernels: 5.57 us -> 4.8 us  [per_device(): pl.pallas_call(functools.partial(grad_kernel, n_high), out_shape=outs, in...]
    pallas_call x1, local copies, waits for them, and re-layouts: 0.77 us -> 0.03 us  [per_device(): pl.pallas_call(functools.partial(grad_kernel, n_high), out_shape=outs, in...]
  transfers between devices with their start and end apart: 23 -> 23, of which waited for: 10 -> 10; matrix products, arithmetic and copies ran while one was open for 11% -> 4% of each run, Pallas kernels for 2% -> 6%
where the time goes in v10:
time: 65 us; the launch traced here: 64.7 us
  starting transfers between devices  27.8 us (43%)
  waiting for transfers between devices  15.7 us (24%)
  Pallas kernels  10.2 us (16%)
  other arithmetic  5.36 us (8%)
  local copies, waits for them, and re-layouts  4.09 us (6%)
  between operations  1.61 us (2%)
    ppermute x12, starting transfers between devices, cube_swap(): return lax.ppermute(x, AXES[1:], pairs)  18.9 us
    ppermute x11, waiting for transfers between devices, swap(): lax.ppermute(x, axis, [(i, i ^ mask) for i in range(fine.shape[axis])])  9.52 us
    ppermute x11, starting transfers between devices, swap(): lax.ppermute(x, axis, [(i, i ^ mask) for i in range(fine.shape[axis])])  8.93 us
    ppermute x12, waiting for transfers between devices, cube_swap(): return lax.ppermute(x, AXES[1:], pairs)  6.15 us
    pallas_call x1, Pallas kernels, per_device(): pl.pallas_call(functools.partial(grad_kernel, n_high), out_shape=outs, in...  4.8 us
    unnamed x14, local copies, waits for them, and re-layouts  3.31 us
    pallas_call x2, Pallas kernels, per_device(): pl.pallas_call(functools.partial(logits_kernel, functools.partial(place,...  2.95 us
    pallas_call x1, Pallas kernels, per_device(): pl.pallas_call(functools.partial(columns_kernel, n_high), out_shape=colum...  2.46 us
  transfers between devices with their start and end apart: 23, of which 10 were waited for; matrix products, arithmetic and copies ran while one was open for 4% of the time, Pallas kernels for 6%

profile of v10, /device:TPU:0, one launch (start us, length us, event | category | flops | bytes accessed | tf_op | source)
XLA Modules:
  0.0 64.7 jit_solution(16889396214864001350)
XLA Ops:
  0.7 4.8 %shard_map.93 = (bf16[2,2,1,192,128]{4,3,2,1,0:T(8,128)(2,1)S(1)}, bf16[2,2,192,128]{3,2,1,0:T(8,128)(2,1)S(1)}, bf16[4,2,192,128]{3,2,1,0:T(8,128)(2,1)S(1)}, b...) custom-call(s32[4]{0:T(128)S(1)} %pad_add_fusion.where_ref, ...), custom_call_target="tpu_custom_call" | custom-call | tf_op jit(solution)/shard_map/pallas_call | solution.py:215
  7.2 3.9 %collective-permute-start.4 = (bf16[2,1,192,128]{3,2,0,1:T(8,128)(2,1)S(1)}, bf16[2,1,192,128]{3,2,0,1:T(8,128)(2,1)S(1)}, u32[]{:S(2)}, u32[]{:S(2)}) collective-permute-start(bf16[2,1,192,128]{3,2,0,1:T(8,128)(2,1)S(1)} %get-tuple-element.76), channel_id=1, source_target_pairs={{0,5},{1,4},{2,10},{3,11},{4,1},{5,0},{6,14},{7,15},{8,13},{9,12},... | collective-permute-start | bytes 294920 | tf_op jit(solution)/shard_map/ppermute | solution.py:184
  11.8 2.6 %collective-permute-start.7 = (bf16[2,2,192,128]{3,2,0,1:T(8,128)(2,1)S(1)}, bf16[2,2,192,128]{3,2,0,1:T(8,128)(2,1)S(1)}, u32[]{:S(2)}, u32[]{:S(2)}) collective-permute-start(bf16[2,2,192,128]{3,2,0,1:T(8,128)(2,1)S(1)} %slice.63), channel_id=1, source_target_pairs={{0,12},{1,13},{2,3},{3,2},{4,8},{5,9},{6,7},{7,6},{8,4},{9,5},{10,... | collective-permute-start | bytes 589832 | tf_op jit(solution)/shard_map/ppermute | solution.py:184
  14.5 2.9 %collective-permute-start.1 = (bf16[2,192,128]{2,1,0:T(8,128)(2,1)S(1)}, bf16[2,192,128]{2,1,0:T(8,128)(2,1)S(1)}, u32[]{:S(2)}, u32[]{:S(2)}) collective-permute-start(bf16[2,192,128]{2,1,0:T(8,128)(2,1)S(1)} %get-tuple-element.74), channel_id=1, source_target_pairs={{0,5},{1,4},{2,10},{3,11},{4,1},{5,0},{6,14},{7,15},{8,13},{9,12},... | collective-permute-start | bytes 294920 | tf_op jit(solution)/shard_map/ppermute | solution.py:184
  17.9 4.7 %collective-permute-done.8 = bf16[2,192,128]{2,1,0:T(8,128)(2,1)S(1)} collective-permute-done((bf16[2,192,128]{2,1,0:T(8,128)(2,1)S(1)}, bf16[2,192,128]{2,1,0:T(8,128)(2,1)S(1)}, u32[]{:S(2)}, u32[]{:S(2)}) %collective-permute-start.8) | collective-permute-done | bytes 98336 | tf_op jit(solution)/shard_map/ppermute | solution.py:184
  24.1 2.9 %collective-permute-start.9 = (bf16[2,192,128]{2,1,0:T(8,128)(2,1)S(1)}, bf16[2,192,128]{2,1,0:T(8,128)(2,1)}, u32[]{:S(2)}, u32[]{:S(2)}) collective-permute-start(bf16[2,192,128]{2,1,0:T(8,128)(2,1)S(1)} %pad_maximum_fusion.4), channel_id=1, source_target_pairs={{0,16},{16,0},{1,17},{17,1},{2,18},{18,2},{3,19},{19,3},{4,20},{20... | collective-permute-start | bytes 294920 | tf_op jit(solution)/shard_map/ppermute | solution.py:174
  27.7 2.5 %shard_map.94 = (bf16[6,256,768]{2,1,0:T(8,128)(2,1)S(1)}, bf16[2,256,768]{2,1,0:T(8,128)(2,1)S(1)}) custom-call(s32[4]{0:T(128)S(1)} %pad_add_fusion.where_ref, bf16[256,6144]{1,0:T(8,128)(2,1)} %acts_ref.2), custom_call_target="tpu_custom_call" | custom-call | tf_op jit(solution)/shard_map/pallas_call | solution.py:278
  30.2 1.0 %fusion.3 = f32[2,192,128]{2,1,0:T(8,128)S(1)} fusion(f32[2,2,192,128]{3,2,0,1:T(8,128)S(1)} %copy-done.1, bf16[2,192,128]{2,1,0:T(8,128)(2,1)} %collective-permute-done.9, bf16[2,192,128]{2,1,0:T(8,128)(2,1)} %collective-permute-done.2, bf16[2,192,128]{2,1,0:T(8,128)(2,1)S(1)} %copy-done.6), kind=kLoop, calls=%fused_computation.14 | loop fusion | flops 294912 | bytes 688128 | tf_op jit(solution)/shard_map/add | solution.py:276
  33.3 0.8 %collective-permute-done.10 = f32[192,128]{1,0:T(8,128)S(1)} collective-permute-done((f32[192,128]{1,0:T(8,128)}, f32[192,128]{1,0:T(8,128)S(1)}, u32[]{:S(2)}, u32[]{:S(2)}) %collective-permute-start.10) | collective-permute-done | bytes 98336 | tf_op jit(solution)/shard_map/ppermute | solution.py:174
  34.7 1.7 %fusion.19 = (bf16[192,128]{1,0:T(8,128)(2,1)S(1)}, f32[192,128]{1,0:T(8,128)}) fusion(f32[3,192,128]{2,1,0:T(8,128)S(1)} %get-tuple-element.34, f32[]{:T(128)} %bitcast.22, f32[]{:T(128)} %bitcast.20, f32[2,192,128]{2,1,0:T(8,128)} %copy-done.3, f32[192,128]{1,0:T(8,128)} %copy-done.4, f32[2,192,128]{2,1,0:T(8,128)} %copy-done.2, s32[]{:T(128)S(6)} %select_n.55), kind=kLoop, calls=%fused_computation.51 | loop fusion | flops 442368 | bytes 737292 | tf_op jit(solution)/shard_map/convert_element_type | solution.py:292
  36.5 1.1 %collective-permute-done.11 = bf16[192,128]{1,0:T(8,128)(2,1)S(1)} collective-permute-done((bf16[192,128]{1,0:T(8,128)(2,1)S(1)}, bf16[192,128]{1,0:T(8,128)(2,1)S(1)}, u32[]{:S(2)}, u32[]{:S(2)}) %collective-permute-start.11) | collective-permute-done | bytes 49184 | tf_op jit(solution)/shard_map/ppermute | solution.py:174
  37.6 2.2 %collective-permute-start.12 = (bf16[2,192,128]{2,1,0:T(8,128)(2,1)S(1)}, bf16[2,192,128]{2,1,0:T(8,128)(2,1)S(1)}, u32[]{:S(2)}, u32[]{:S(2)}) collective-permute-start(bf16[2,192,128]{2,1,0:T(8,128)(2,1)S(1)} %maximum_select_fusion.1), channel_id=1, source_target_pairs={{0,5},{1,4},{2,10},{3,11},{4,1},{5,0},{6,14},{7,15},{8,13},{9,12},... | collective-permute-start | bytes 294920 | tf_op jit(solution)/shard_map/ppermute | solution.py:184
  39.8 0.9 %collective-permute-start.13 = (bf16[2,192,128]{2,1,0:T(8,128)(2,1)S(1)}, bf16[2,192,128]{2,1,0:T(8,128)(2,1)S(1)}, u32[]{:S(2)}, u32[]{:S(2)}) collective-permute-start(bf16[2,192,128]{2,1,0:T(8,128)(2,1)S(1)} %maximum_select_fusion.1), channel_id=1, source_target_pairs={{0,4},{1,5},{2,11},{3,10},{4,0},{5,1},{6,15},{7,14},{8,12},{9,13},... | collective-permute-start | bytes 294920 | tf_op jit(solution)/shard_map/ppermute | solution.py:184
  40.7 2.6 %collective-permute-start.14 = (bf16[2,192,128]{2,1,0:T(8,128)(2,1)S(1)}, bf16[2,192,128]{2,1,0:T(8,128)(2,1)S(1)}, u32[]{:S(2)}, u32[]{:S(2)}) collective-permute-start(bf16[2,192,128]{2,1,0:T(8,128)(2,1)S(1)} %maximum_select_fusion.1), channel_id=1, source_target_pairs={{0,16},{16,0},{1,17},{17,1},{2,18},{18,2},{3,19},{19,3},{4,20},{20... | collective-permute-start | bytes 294920 | tf_op jit(solution)/shard_map/ppermute | solution.py:174
  44.4 2.2 %collective-permute-done.14 = bf16[2,192,128]{2,1,0:T(8,128)(2,1)S(1)} collective-permute-done((bf16[2,192,128]{2,1,0:T(8,128)(2,1)S(1)}, bf16[2,192,128]{2,1,0:T(8,128)(2,1)S(1)}, u32[]{:S(2)}, u32[]{:S(2)}) %collective-permute-start.14) | collective-permute-done | bytes 98336 | tf_op jit(solution)/shard_map/ppermute | solution.py:174
  46.6 1.1 %collective-permute-start.15 = (bf16[2,1,192,128]{3,2,0,1:T(8,128)(2,1)S(1)}, bf16[2,1,192,128]{3,2,0,1:T(8,128)(2,1)S(1)}, u32[]{:S(2)}, u32[]{:S(2)}) collective-permute-start(bf16[2,1,192,128]{3,2,0,1:T(8,128)(2,1)S(1)} %bitcast.93), channel_id=1, source_target_pairs={{0,5},{1,4},{2,10},{3,11},{4,1},{5,0},{6,14},{7,15},{8,13},{9,12},... | collective-permute-start | bytes 294920 | tf_op jit(solution)/shard_map/ppermute | solution.py:184
  47.7 0.9 %collective-permute-start.16 = (bf16[2,1,192,128]{3,2,0,1:T(8,128)(2,1)S(1)}, bf16[2,1,192,128]{3,2,0,1:T(8,128)(2,1)S(1)}, u32[]{:S(2)}, u32[]{:S(2)}) collective-permute-start(bf16[2,1,192,128]{3,2,0,1:T(8,128)(2,1)S(1)} %bitcast.94), channel_id=1, source_target_pairs={{0,4},{1,5},{2,11},{3,10},{4,0},{5,1},{6,15},{7,14},{8,12},{9,13},... | collective-permute-start | bytes 294920 | tf_op jit(solution)/shard_map/ppermute | solution.py:184
  48.6 1.5 %collective-permute-start.19 = (f32[192,128]{1,0:T(8,128)}, f32[192,128]{1,0:T(8,128)S(1)}, u32[]{:S(2)}, u32[]{:S(2)}) collective-permute-start(f32[192,128]{1,0:T(8,128)} %get-tuple-element.52), channel_id=1, source_target_pairs={{0,1},{1,0},{2,3},{3,2},{4,5},{5,4},{6,7},{7,6},{8,9},{9,8},{10,11... | collective-permute-start | bytes 294920 | tf_op jit(solution)/shard_map/ppermute | solution.py:174
  50.2 3.3 %collective-permute-start.18 = (bf16[2,192,128]{2,1,0:T(8,128)(2,1)S(1)}, bf16[2,192,128]{2,1,0:T(8,128)(2,1)S(1)}, u32[]{:S(2)}, u32[]{:S(2)}) collective-permute-start(bf16[2,192,128]{2,1,0:T(8,128)(2,1)S(1)} %fusion.11), channel_id=1, source_target_pairs={{0,13},{1,12},{2,15},{3,14},{4,9},{5,8},{6,11},{7,10},{8,5},{9,4},... | collective-permute-start | bytes 294920 | tf_op jit(solution)/shard_map/ppermute | solution.py:184
  53.6 4.1 %collective-permute-done.19 = f32[192,128]{1,0:T(8,128)S(1)} collective-permute-done((f32[192,128]{1,0:T(8,128)}, f32[192,128]{1,0:T(8,128)S(1)}, u32[]{:S(2)}, u32[]{:S(2)}) %collective-permute-start.19) | collective-permute-done | bytes 98336 | tf_op jit(solution)/shard_map/ppermute | solution.py:174
  57.7 2.1 %multiply_subtract_fusion = (f32[384,128]{1,0:T(8,128)}, f32[384,128]{1,0:T(8,128)}, f32[384,128]{1,0:T(8,128)}) fusion(f32[384,128]{1,0:T(8,128)} %refs_0_.1, f32[]{:T(128)} %bitcast.22, f32[]{:T(128)} %bitcast.20, f32[192,128]{1,0:T(8,128)} %get-tuple-element.52, f32[192,128]{1,0:T(8,128)S(1)} %collective-permute-done.19, pred[]{:T(512)S(6)} %eq.12, ...), kind=kLoop, calls=%fused_computation.18 | loop fusion | flops 884736 | bytes 1376265 | tf_op jit(solution)/shard_map/sub | solution.py:30
  60.8 0.9 %collective-permute-done.22 = bf16[3,2,192,128]{3,2,0,1:T(8,128)(2,1)S(1)} collective-permute-done((bf16[3,2,192,128]{3,2,0,1:T(8,128)(2,1)S(1)}, bf16[3,2,192,128]{3,2,0,1:T(8,128)(2,1)S(1)}, u32[]{:S(2)}, u32[]{:S(2)}) %collective-permute-start.22) | collective-permute-done | bytes 294944 | tf_op jit(solution)/shard_map/ppermute | solution.py:174
  61.8 1.4 %shard_map.95.refs_2_ = f32[256,128]{1,0:T(8,128)S(1)} custom-call(s32[4]{0:T(128)S(1)} %pad_add_fusion.where_ref, bf16[6,256,768]{2,1,0:T(8,128)(2,1)S(1)} %get-tuple-element.59.columns_ref, bf16[2,2,192,128]{3,2,1,0:T(8,128)(2,1)S(1)} %pad_maximum_fusion.3.refs_0_, bf16[2,2,192,128]{3,2,1,0:T(8,128)(2,1)S(1)} %collective-permute-done.21.refs_1_, ...), custom_call_target="tpu_custom_call" | custom-call | tf_op jit(solution)/shard_map/pallas_call | solution.py:331
  63.2 1.6 %shard_map.96 = bf16[256,128]{1,0:T(8,128)(2,1)} custom-call(s32[4]{0:T(128)S(1)} %pad_add_fusion.where_ref, bf16[2,256,768]{2,1,0:T(8,128)(2,1)S(1)} %get-tuple-element.56.columns_ref, bf16[2,2,1,192,128]{4,3,2,1,0:T(8,128)(2,1)S(1)} %pad_maximum_fusion.2.refs_0_, bf16[2,2,1,192,128]{4,3,2,1,0:T(8,128)(2,1)S(1)} %collective-permute-done.20.refs_1_, ...), custom_call_target="tpu_custom_call" | custom-call | tf_op jit(solution)/shard_map/pallas_call | solution.py:331
  (68 shorter events, 9.6 us)
Async XLA Ops:
  5.5 1.6 %collective-permute-start.3 = (bf16[2,2,1,192,128]{4,3,1,2,0:T(8,128)(2,1)S(1)}, bf16[2,2,1,192,128]{4,3,1,2,0:T(8,128)(2,1)S(1)}, u32[]{:S(2)}, u32[]{:S(2)}) collective-permute-start(bf16[2,2,1,192,128]{4,3,1,2,0:T(8,128)(2,1)S(1)} %bitcast.88), channel_id=1, source_target_pairs={{0,2},{2,0},{1,3},{3,1},{4,6},{6,4},{5,7},{7,5},{8,10},{10,8},{9,1... | collective-permute-start | bytes 589832 | tf_op jit(solution)/shard_map/ppermute | solution.py:174
  6.1 5.6 %collective-permute-start.6 = (bf16[4,2,192,128]{3,2,0,1:T(8,128)(2,1)S(1)}, bf16[4,2,192,128]{3,2,0,1:T(8,128)(2,1)S(1)}, u32[]{:S(2)}, u32[]{:S(2)}) collective-permute-start(bf16[4,2,192,128]{3,2,0,1:T(8,128)(2,1)S(1)} %copy.13), channel_id=1, source_target_pairs={{0,2},{2,0},{1,3},{3,1},{4,6},{6,4},{5,7},{7,5},{8,10},{10,8},{9,1... | collective-permute-start | bytes 1179656 | tf_op jit(solution)/shard_map/ppermute | solution.py:174
  6.2 5.4 %collective-permute-start = (bf16[2,2,192,128]{3,2,1,0:T(8,128)(2,1)S(1)}, bf16[2,2,192,128]{3,2,1,0:T(8,128)(2,1)S(1)}, u32[]{:S(2)}, u32[]{:S(2)}) collective-permute-start(bf16[2,2,192,128]{3,2,1,0:T(8,128)(2,1)S(1)} %get-tuple-element.36), channel_id=1, source_target_pairs={{0,2},{2,0},{1,3},{3,1},{4,6},{6,4},{5,7},{7,5},{8,10},{10,8},{9,1... | collective-permute-start | bytes 589832 | tf_op jit(solution)/shard_map/ppermute | solution.py:174
  7.2 10.1 %collective-permute-start.4 = (bf16[2,1,192,128]{3,2,0,1:T(8,128)(2,1)S(1)}, bf16[2,1,192,128]{3,2,0,1:T(8,128)(2,1)S(1)}, u32[]{:S(2)}, u32[]{:S(2)}) collective-permute-start(bf16[2,1,192,128]{3,2,0,1:T(8,128)(2,1)S(1)} %get-tuple-element.76), channel_id=1, source_target_pairs={{0,5},{1,4},{2,10},{3,11},{4,1},{5,0},{6,14},{7,15},{8,13},{9,12},... | collective-permute-start | bytes 294920 | tf_op jit(solution)/shard_map/ppermute | solution.py:184
  11.1 6.8 %collective-permute-start.5 = (bf16[2,1,192,128]{3,2,0,1:T(8,128)(2,1)S(1)}, bf16[2,1,192,128]{3,2,0,1:T(8,128)(2,1)S(1)}, u32[]{:S(2)}, u32[]{:S(2)}) collective-permute-start(bf16[2,1,192,128]{3,2,0,1:T(8,128)(2,1)S(1)} %get-tuple-element.75), channel_id=1, source_target_pairs={{0,4},{1,5},{2,11},{3,10},{4,0},{5,1},{6,15},{7,14},{8,12},{9,13},... | collective-permute-start | bytes 294920 | tf_op jit(solution)/shard_map/ppermute | solution.py:184
  11.8 10.8 %collective-permute-start.7 = (bf16[2,2,192,128]{3,2,0,1:T(8,128)(2,1)S(1)}, bf16[2,2,192,128]{3,2,0,1:T(8,128)(2,1)S(1)}, u32[]{:S(2)}, u32[]{:S(2)}) collective-permute-start(bf16[2,2,192,128]{3,2,0,1:T(8,128)(2,1)S(1)} %slice.63), channel_id=1, source_target_pairs={{0,12},{1,13},{2,3},{3,2},{4,8},{5,9},{6,7},{7,6},{8,4},{9,5},{10,... | collective-permute-start | bytes 589832 | tf_op jit(solution)/shard_map/ppermute | solution.py:184
  14.4 8.2 %collective-permute-start.8 = (bf16[2,192,128]{2,1,0:T(8,128)(2,1)S(1)}, bf16[2,192,128]{2,1,0:T(8,128)(2,1)S(1)}, u32[]{:S(2)}, u32[]{:S(2)}) collective-permute-start(bf16[2,192,128]{2,1,0:T(8,128)(2,1)S(1)} %slice_bitcast_fusion.5), channel_id=1, source_target_pairs={{0,13},{1,12},{2,15},{3,14},{4,9},{5,8},{6,11},{7,10},{8,5},{9,4},... | collective-permute-start | bytes 294920 | tf_op jit(solution)/shard_map/ppermute | solution.py:184
  14.5 12.6 %collective-permute-start.1 = (bf16[2,192,128]{2,1,0:T(8,128)(2,1)S(1)}, bf16[2,192,128]{2,1,0:T(8,128)(2,1)S(1)}, u32[]{:S(2)}, u32[]{:S(2)}) collective-permute-start(bf16[2,192,128]{2,1,0:T(8,128)(2,1)S(1)} %get-tuple-element.74), channel_id=1, source_target_pairs={{0,5},{1,4},{2,10},{3,11},{4,1},{5,0},{6,14},{7,15},{8,13},{9,12},... | collective-permute-start | bytes 294920 | tf_op jit(solution)/shard_map/ppermute | solution.py:184
  17.3 10.4 %collective-permute-start.2 = (bf16[2,192,128]{2,1,0:T(8,128)(2,1)S(1)}, bf16[2,192,128]{2,1,0:T(8,128)(2,1)}, u32[]{:S(2)}, u32[]{:S(2)}) collective-permute-start(bf16[2,192,128]{2,1,0:T(8,128)(2,1)S(1)} %get-tuple-element.73), channel_id=1, source_target_pairs={{0,4},{1,5},{2,11},{3,10},{4,0},{5,1},{6,15},{7,14},{8,12},{9,13},... | collective-permute-start | bytes 294920 | tf_op jit(solution)/shard_map/ppermute | solution.py:184
  24.1 6.1 %collective-permute-start.9 = (bf16[2,192,128]{2,1,0:T(8,128)(2,1)S(1)}, bf16[2,192,128]{2,1,0:T(8,128)(2,1)}, u32[]{:S(2)}, u32[]{:S(2)}) collective-permute-start(bf16[2,192,128]{2,1,0:T(8,128)(2,1)S(1)} %pad_maximum_fusion.4), channel_id=1, source_target_pairs={{0,16},{16,0},{1,17},{17,1},{2,18},{18,2},{3,19},{19,3},{4,20},{20... | collective-permute-start | bytes 294920 | tf_op jit(solution)/shard_map/ppermute | solution.py:174
  27.1 3.1 %copy-start.1 = (f32[2,2,192,128]{3,2,0,1:T(8,128)S(1)}, f32[2,2,192,128]{3,2,0,1:T(8,128)}, u32[]{:S(2)}) copy-start(f32[2,2,192,128]{3,2,0,1:T(8,128)} %copy-done) | copy-start | bytes 1179652
  32.5 1.5 %collective-permute-start.10 = (f32[192,128]{1,0:T(8,128)}, f32[192,128]{1,0:T(8,128)S(1)}, u32[]{:S(2)}, u32[]{:S(2)}) collective-permute-start(f32[192,128]{1,0:T(8,128)} %dynamic-slice_bitcast_fusion), channel_id=1, source_target_pairs={{0,2},{2,0},{1,3},{3,1},{4,6},{6,4},{5,7},{7,5},{8,10},{10,8},{9,1... | collective-permute-start | bytes 294920 | tf_op jit(solution)/shard_map/ppermute | solution.py:174
  36.4 1.2 %collective-permute-start.11 = (bf16[192,128]{1,0:T(8,128)(2,1)S(1)}, bf16[192,128]{1,0:T(8,128)(2,1)S(1)}, u32[]{:S(2)}, u32[]{:S(2)}) collective-permute-start(bf16[192,128]{1,0:T(8,128)(2,1)S(1)} %get-tuple-element.67), channel_id=1, source_target_pairs={{0,2},{2,0},{1,3},{3,1},{4,6},{6,4},{5,7},{7,5},{8,10},{10,8},{9,1... | collective-permute-start | bytes 147464 | tf_op jit(solution)/shard_map/ppermute | solution.py:174
  37.6 6.1 %collective-permute-start.12 = (bf16[2,192,128]{2,1,0:T(8,128)(2,1)S(1)}, bf16[2,192,128]{2,1,0:T(8,128)(2,1)S(1)}, u32[]{:S(2)}, u32[]{:S(2)}) collective-permute-start(bf16[2,192,128]{2,1,0:T(8,128)(2,1)S(1)} %maximum_select_fusion.1), channel_id=1, source_target_pairs={{0,5},{1,4},{2,10},{3,11},{4,1},{5,0},{6,14},{7,15},{8,13},{9,12},... | collective-permute-start | bytes 294920 | tf_op jit(solution)/shard_map/ppermute | solution.py:184
  39.8 4.6 %collective-permute-start.13 = (bf16[2,192,128]{2,1,0:T(8,128)(2,1)S(1)}, bf16[2,192,128]{2,1,0:T(8,128)(2,1)S(1)}, u32[]{:S(2)}, u32[]{:S(2)}) collective-permute-start(bf16[2,192,128]{2,1,0:T(8,128)(2,1)S(1)} %maximum_select_fusion.1), channel_id=1, source_target_pairs={{0,4},{1,5},{2,11},{3,10},{4,0},{5,1},{6,15},{7,14},{8,12},{9,13},... | collective-permute-start | bytes 294920 | tf_op jit(solution)/shard_map/ppermute | solution.py:184
  40.7 5.9 %collective-permute-start.14 = (bf16[2,192,128]{2,1,0:T(8,128)(2,1)S(1)}, bf16[2,192,128]{2,1,0:T(8,128)(2,1)S(1)}, u32[]{:S(2)}, u32[]{:S(2)}) collective-permute-start(bf16[2,192,128]{2,1,0:T(8,128)(2,1)S(1)} %maximum_select_fusion.1), channel_id=1, source_target_pairs={{0,16},{16,0},{1,17},{17,1},{2,18},{18,2},{3,19},{19,3},{4,20},{20... | collective-permute-start | bytes 294920 | tf_op jit(solution)/shard_map/ppermute | solution.py:174
  46.6 13.2 %collective-permute-start.15 = (bf16[2,1,192,128]{3,2,0,1:T(8,128)(2,1)S(1)}, bf16[2,1,192,128]{3,2,0,1:T(8,128)(2,1)S(1)}, u32[]{:S(2)}, u32[]{:S(2)}) collective-permute-start(bf16[2,1,192,128]{3,2,0,1:T(8,128)(2,1)S(1)} %bitcast.93), channel_id=1, source_target_pairs={{0,5},{1,4},{2,10},{3,11},{4,1},{5,0},{6,14},{7,15},{8,13},{9,12},... | collective-permute-start | bytes 294920 | tf_op jit(solution)/shard_map/ppermute | solution.py:184
  47.7 12.1 %collective-permute-start.16 = (bf16[2,1,192,128]{3,2,0,1:T(8,128)(2,1)S(1)}, bf16[2,1,192,128]{3,2,0,1:T(8,128)(2,1)S(1)}, u32[]{:S(2)}, u32[]{:S(2)}) collective-permute-start(bf16[2,1,192,128]{3,2,0,1:T(8,128)(2,1)S(1)} %bitcast.94), channel_id=1, source_target_pairs={{0,4},{1,5},{2,11},{3,10},{4,0},{5,1},{6,15},{7,14},{8,12},{9,13},... | collective-permute-start | bytes 294920 | tf_op jit(solution)/shard_map/ppermute | solution.py:184
  48.6 9.0 %collective-permute-start.19 = (f32[192,128]{1,0:T(8,128)}, f32[192,128]{1,0:T(8,128)S(1)}, u32[]{:S(2)}, u32[]{:S(2)}) collective-permute-start(f32[192,128]{1,0:T(8,128)} %get-tuple-element.52), channel_id=1, source_target_pairs={{0,1},{1,0},{2,3},{3,2},{4,5},{5,4},{6,7},{7,6},{8,9},{9,8},{10,11... | collective-permute-start | bytes 294920 | tf_op jit(solution)/shard_map/ppermute | solution.py:174
  50.2 9.6 %collective-permute-start.18 = (bf16[2,192,128]{2,1,0:T(8,128)(2,1)S(1)}, bf16[2,192,128]{2,1,0:T(8,128)(2,1)S(1)}, u32[]{:S(2)}, u32[]{:S(2)}) collective-permute-start(bf16[2,192,128]{2,1,0:T(8,128)(2,1)S(1)} %fusion.11), channel_id=1, source_target_pairs={{0,13},{1,12},{2,15},{3,14},{4,9},{5,8},{6,11},{7,10},{8,5},{9,4},... | collective-permute-start | bytes 294920 | tf_op jit(solution)/shard_map/ppermute | solution.py:184
  53.5 6.6 %collective-permute-start.17 = (bf16[2,2,192,128]{3,2,0,1:T(8,128)(2,1)S(1)}, bf16[2,2,192,128]{3,2,0,1:T(8,128)(2,1)S(1)}, u32[]{:S(2)}, u32[]{:S(2)}) collective-permute-start(bf16[2,2,192,128]{3,2,0,1:T(8,128)(2,1)S(1)} %pad_maximum_fusion.1), channel_id=1, source_target_pairs={{0,12},{1,13},{2,3},{3,2},{4,8},{5,9},{6,7},{7,6},{8,4},{9,5},{10,... | collective-permute-start | bytes 589832 | tf_op jit(solution)/shard_map/ppermute | solution.py:184
  57.7 4.1 %collective-permute-start.21 = (bf16[2,2,192,128]{3,2,1,0:T(8,128)(2,1)S(1)}, bf16[2,2,192,128]{3,2,1,0:T(8,128)(2,1)S(1)}, u32[]{:S(2)}, u32[]{:S(2)}) collective-permute-start(bf16[2,2,192,128]{3,2,1,0:T(8,128)(2,1)S(1)} %pad_maximum_fusion.3.refs_0_), channel_id=1, source_target_pairs={{0,2},{2,0},{1,3},{3,1},{4,6},{6,4},{5,7},{7,5},{8,10},{10,8},{9,1... | collective-permute-start | bytes 589832 | tf_op jit(solution)/shard_map/ppermute | solution.py:174
  60.1 1.6 %collective-permute-start.22 = (bf16[3,2,192,128]{3,2,0,1:T(8,128)(2,1)S(1)}, bf16[3,2,192,128]{3,2,0,1:T(8,128)(2,1)S(1)}, u32[]{:S(2)}, u32[]{:S(2)}) collective-permute-start(bf16[3,2,192,128]{3,2,0,1:T(8,128)(2,1)S(1)} %pad_maximum_fusion), channel_id=1, source_target_pairs={{0,2},{2,0},{1,3},{3,1},{4,6},{6,4},{5,7},{7,5},{8,10},{10,8},{9,1... | collective-permute-start | bytes 884744 | tf_op jit(solution)/shard_map/ppermute | solution.py:174
  60.5 2.7 %collective-permute-start.20 = (bf16[2,2,1,192,128]{4,3,2,1,0:T(8,128)(2,1)S(1)}, bf16[2,2,1,192,128]{4,3,2,1,0:T(8,128)(2,1)S(1)}, u32[]{:S(2)}, u32[]{:S(2)}) collective-permute-start(bf16[2,2,1,192,128]{4,3,2,1,0:T(8,128)(2,1)S(1)} %pad_maximum_fusion.2.refs_0_), channel_id=1, source_target_pairs={{0,2},{2,0},{1,3},{3,1},{4,6},{6,4},{5,7},{7,5},{8,10},{10,8},{9,1... | collective-permute-start | bytes 589832 | tf_op jit(solution)/shard_map/ppermute | solution.py:174
  (6 other events, 5.9 us)

commit v11 on v8

v11 whole, which is shorter than its diff:
```python
import functools

import jax
import jax.numpy as jnp
from jax import lax
from jax.experimental import pallas as pl
from jax.experimental.pallas import tpu as pltpu
from jax.sharding import Mesh
from jax.sharding import PartitionSpec as P

AXES = ("high", "low", "core", "rep")
N_LOW = 4
CHIPS = ((1, 0), (2, 1), (2, 0), (1, 1), (0, 1), (3, 0), (3, 1), (0, 0))
LOWS = ((1, 2), (0, 3))
VMEM_LIMIT = 8 * 2**20


def slot_of(chip, core):
    slot = CHIPS.index(chip)
    return slot if slot >= 6 else slot ^ core


def adamw(grad, master, moment_one, moment_two, step_count):
    count = step_count[0].astype(jnp.float32)
    beta_one = 0.9
    beta_two = 0.95
    first = beta_one * moment_one + (1.0 - beta_one) * grad
    second = beta_two * moment_two + (1.0 - beta_two) * grad * grad
    first_hat = first / (1.0 - jnp.power(beta_one, count))
    second_hat = second / (1.0 - jnp.power(beta_two, count))
    updated = master - 0.01 * (first_hat / (jnp.sqrt(second_hat) + 1e-08) + 0.1 * master)
    return updated, first, second


def load_columns(acts_ref, columns, sems, high, low, lows, n_high):
    wide = columns.shape[-1]
    copies = []
    for p, k in enumerate(lows):
        for j in range(n_high):
            column = pl.multiple_of(((high ^ j) * N_LOW + (low ^ k)) * wide, wide)
            n = p * n_high + j
            copy = pltpu.make_async_copy(acts_ref.at[:, pl.ds(column, wide)], columns.at[n], sems.at[n])
            copy.start()
            copies.append(copy)
    return copies


def grad_kernel(n_high, where_ref, acts_ref, grad_ref, *refs):
    state_refs, refs = refs[:3], refs[3:]
    away, kept, refs = refs[:2], refs[2:4], refs[4:]
    mine_ref, columns, logit_grads, blocks, sems = refs
    high, low, core, rep = [where_ref[i] for i in range(4)]
    half = blocks.shape[2]
    last = sems.shape[0]
    loads = pltpu.make_async_copy(grad_ref, logit_grads, sems.at[last - 1])
    loads.start()
    lows = LOWS[0] + LOWS[1]
    copies = load_columns(acts_ref, columns, sems, high, low, lows, n_high)
    rows = pl.ds(pl.multiple_of(rep * half, half), half)
    state = [
        pltpu.make_async_copy(ref.at[rows], mine_ref.at[i], sems.at[last - 4 + i])
        for i, ref in enumerate(state_refs)
    ]
    for copy in state:
        copy.start()
    loads.wait()
    for n, copy in enumerate(copies):
        copy.wait()
        product = lax.dot_general(
            columns[n], logit_grads[...], (((0,), (0,)), ((), ())), preferred_element_type=jnp.float32
        )
        blocks[...] = product.astype(blocks.dtype).reshape(blocks.shape)
        p, j = divmod(n, n_high)
        for d_rep in range(2):
            for outs, owner in ((kept, core), (away, 1 - core)):
                slot = slot_of((lows[p], d_rep), owner)
                outs[p // 2][slot - 4 * (p // 2), j] = blocks[owner, rep ^ d_rep]
    for copy in state:
        copy.wait()


def columns_kernel(n_high, where_ref, acts_ref, first_ref, second_ref, sems):
    high, low = where_ref[0], where_ref[1]
    copies = []
    for i, (lows, out) in enumerate(zip(LOWS, (first_ref, second_ref))):
        copies += load_columns(acts_ref, out, sems.at[i], high, low, lows, n_high)
    for copy in copies:
        copy.wait()


def logits_kernel(n_high, group, where_ref, columns_ref, *refs):
    *pieces, out_ref, weight = refs
    before = None
    if len(pieces[-1].shape) == 2:
        *pieces, before = pieces
    core, rep = where_ref[2], where_ref[3]
    half, experts = weight.shape[-2:]
    for i, piece in enumerate(pieces):
        owner = core ^ (i % 2)
        for n, place, of_rep in places(group, owner, rep, i // 2, piece.shape[0]):
            for j in range(n_high):
                weight[place, j, owner, of_rep] = piece[n, j]
    total = None if before is None else before[...]
    for n in range(2 * n_high):
        part = jnp.dot(
            columns_ref[n],
            weight[n // n_high, n % n_high].reshape(4 * half, experts),
            preferred_element_type=jnp.float32,
        )
        total = part if total is None else total + part
    out_ref[...] = total.astype(out_ref.dtype)


def places(group, owner, rep, home, count):
    out = []
    for n in range(count):
        slot = 7 if home else 4 * group + n
        chip_low, d_rep = CHIPS[slot]
        flip = owner if slot < 6 else 0
        out.append((n, LOWS[group].index(chip_low) ^ flip, rep ^ d_rep ^ flip))
    return out


def solution(mesh):
    n_seq, n_rep = mesh.shape["seq"], mesh.shape["rep"]
    n_high = n_seq // (2 * N_LOW)
    fine = Mesh(mesh.devices.reshape(n_high, N_LOW, 2, n_rep), AXES)

    def swap(x, axis, mask=1):
        return lax.ppermute(x, axis, [(i, i ^ mask) for i in range(fine.shape[axis])])

    def cube_swap(x, change):
        pairs = []
        for low in range(N_LOW):
            for core in range(2):
                d_low, d_rep = change(core)
                for rep in range(n_rep):
                    there = ((low ^ d_low) * 2 + core) * n_rep + (rep ^ d_rep)
                    pairs.append(((low * 2 + core) * n_rep + rep, there))
        return lax.ppermute(x, AXES[1:], pairs)

    def to_slot(x, slot):
        return cube_swap(x, lambda core: CHIPS[slot ^ core if slot < 6 else slot])

    def per_device(acts, grad_logits, master, moment_one, moment_two, step_count):
        tokens, experts = grad_logits.shape
        rows = master.shape[0]
        half = rows // n_rep
        high, low, core, rep = (lax.axis_index(a) for a in AXES)
        where = jnp.stack([high, low, core, rep])
        f32, bf16 = jnp.float32, jnp.bfloat16
        in_kernels = half % 16 == 0 and (4 * half) % 128 == 0

        smem = pl.BlockSpec(memory_space=pltpu.SMEM)
        vmem = pl.BlockSpec(memory_space=pltpu.VMEM)
        anywhere = pl.BlockSpec(memory_space=pl.ANY)
        params = pltpu.CompilerParams(vmem_limit_bytes=VMEM_LIMIT)
        state_in = (master, moment_one, moment_two)

        if in_kernels:
            acts = pltpu.with_memory_space_constraint(acts, pltpu.HBM)
            shape = pltpu.VMEM((4, n_high, half, experts), bf16)
            *sorted_rows, mine = pl.pallas_call(
                functools.partial(grad_kernel, n_high),
                out_shape=[shape] * 4 + [pltpu.VMEM((3, half, experts), f32)],
                in_specs=[smem] + [anywhere] * 5,
                out_specs=[vmem] * 5,
                scratch_shapes=[
                    pltpu.VMEM((4 * n_high, tokens, 4 * half), bf16),
                    pltpu.VMEM((tokens, experts), bf16),
                    pltpu.VMEM((2, 2, half, experts), bf16),
                    pltpu.SemaphoreType.DMA((4 * n_high + 4,)),
                ],
                compiler_params=params,
            )(
                where,
                acts,
                *(pltpu.with_memory_space_constraint(x, pltpu.HBM) for x in (grad_logits, *state_in)),
            )
            away, kept = sorted_rows[:2], sorted_rows[2:]
        else:
            product = lax.dot_general(
                acts, grad_logits, (((0,), (0,)), ((), ())), preferred_element_type=f32
            ).astype(bf16)
            product = product.reshape(n_high, N_LOW, 2, n_rep, half, experts)
            product = product[high ^ jnp.arange(n_high)]

            def sort_rows(owner):
                blocks = []
                for slot in range(8):
                    flip = owner if slot < 6 else 0
                    d_low, d_rep = CHIPS[slot]
                    at = (0, low ^ d_low ^ (3 * flip), owner, rep ^ d_rep ^ flip, 0, 0)
                    part = lax.dynamic_slice(product, at, (n_high, 1, 1, 1, half, experts))
                    blocks.append(part.reshape(n_high, half, experts))
                return jnp.stack(blocks[:4]), jnp.stack(blocks[4:])

            away, kept = sort_rows(1 - core), sort_rows(core)
            mine = jnp.stack([lax.dynamic_slice_in_dim(x, rep * half, half, 0) for x in state_in])

        parts = []
        for own, theirs in zip(kept, away):
            summed = own.astype(f32) + swap(theirs, "core").astype(f32)
            for n in range(4):
                slot = len(parts)
                parts.append(summed[n] if slot == 7 else to_slot(summed[n].astype(bf16), slot))
        parts = lax.optimization_barrier(parts)
        total = sum(x.astype(f32) for x in parts)

        grad = total[0]
        for j in range(1, n_high):
            grad = grad + swap(total[j].astype(bf16), "high", j).astype(f32)
        weight = adamw(grad, *mine, step_count)[0].astype(bf16)

        column = jnp.stack([swap(weight, "high", j) if j else weight for j in range(n_high)])
        other = swap(grad, "rep")
        column, other = lax.optimization_barrier((column, other))
        got = [to_slot(column, slot) for slot in range(7)]
        across = swap(column, "core")

        whole = jnp.where(
            rep == 0,
            jnp.concatenate([grad, other], 0),
            jnp.concatenate([other, grad], 0),
        )
        got[:2], whole, late_acts = lax.optimization_barrier((got[:2], whole, acts))
        state = adamw(whole, *state_in, step_count)

        columns = [None, None]
        if in_kernels:
            columns = pl.pallas_call(
                functools.partial(columns_kernel, n_high),
                out_shape=(pltpu.VMEM((2 * n_high, tokens, 4 * half), bf16),) * 2,
                in_specs=[smem, anywhere],
                out_specs=(vmem, vmem),
                scratch_shapes=[pltpu.SemaphoreType.DMA((2, 2 * n_high))],
                compiler_params=params,
            )(where, pltpu.with_memory_space_constraint(late_acts, pltpu.HBM))
        got[:4], state, columns = lax.optimization_barrier((got[:4], state, columns))
        first, second = jnp.stack(got[:4]), jnp.stack(got[4:])
        first_over, second_over = swap(first, "core"), swap(second, "core")
        pieces = ([first, first_over], [second, second_over, column[None], across[None]])
        logits = None
        for group, (received, acts_columns) in enumerate(zip(pieces, columns)):
            if in_kernels:
                before = [] if logits is None else [logits]
                operands = [
                    pltpu.with_memory_space_constraint(x, pltpu.VMEM) for x in [acts_columns] + received + before
                ]
                logits = pl.pallas_call(
                    functools.partial(logits_kernel, n_high, group),
                    out_shape=jax.ShapeDtypeStruct((tokens, experts), bf16 if before else f32),
                    in_specs=[smem] + [vmem] * len(operands),
                    out_specs=vmem,
                    scratch_shapes=[pltpu.VMEM((2, n_high, 2, 2, half, experts), bf16)],
                    compiler_params=params,
                )(where, *operands)
            else:
                rows_at, values = [], []
                for i, piece in enumerate(received):
                    owner = core ^ (i % 2)
                    for n, place, of_rep in places(group, owner, rep, i // 2, piece.shape[0]):
                        d_low = jnp.array(LOWS[group])[place]
                        for j in range(n_high):
                            at = ((high ^ j) * N_LOW + (low ^ d_low)) * 2 + owner
                            rows_at.append(at * n_rep + of_rep)
                            values.append(piece[n, j])
                full = jnp.zeros((2 * n_seq, half, experts), bf16)
                full = full.at[jnp.stack(rows_at)].set(jnp.stack(values))
                full = full.reshape(n_seq * rows, experts)
                part = jnp.dot(acts, full, preferred_element_type=f32)
                logits = part if logits is None else (logits + part).astype(bf16)
        return *state, logits

    rows_of, tokens_of = P(AXES[:3], None), P(AXES, None)
    return jax.shard_map(
        per_device,
        mesh=fine,
        in_specs=(tokens_of, tokens_of, rows_of, rows_of, rows_of, P()),
        out_specs=(rows_of, rows_of, rows_of, tokens_of),
        check_vma=False,
    )
```

time: 54.1 us -> 55.4 us (1.024)
  starting transfers between devices: 21.5 us -> 28.4 us
  waiting for transfers between devices: 19.1 us -> 13.5 us
    ppermute x8 -> x14, starting transfers between devices: 14.4 us -> 20.7 us  [cube_swap(): return lax.ppermute(x, AXES[1:], pairs)]
    ppermute x8 -> x14, waiting for transfers between devices: 9.88 us -> 5.94 us  [cube_swap(): return lax.ppermute(x, AXES[1:], pairs)]
    ppermute x11 -> x8, waiting for transfers between devices: 9.26 us -> 7.56 us  [swap(): lax.ppermute(x, axis, [(i, i ^ mask) for i in range(fine.shape[axis])])]
    ppermute x11 -> x8, starting transfers between devices: 7.04 us -> 7.67 us  [swap(): lax.ppermute(x, axis, [(i, i ^ mask) for i in range(fine.shape[axis])])]
  transfers between devices with their start and end apart: 19 -> 22, of which waited for: 10 -> 9; matrix products, arithmetic and copies ran while one was open for 2% -> 2% of each run, Pallas kernels for 7% -> 7%
where the time goes in v11:
time: 55.4 us; the launch traced here: 55.2 us
  starting transfers between devices  28.4 us (51%)
  waiting for transfers between devices  13.5 us (24%)
  Pallas kernels  10.2 us (18%)
  between operations  1.56 us (3%)
  other arithmetic  1.5 us (3%)
    ppermute x14, starting transfers between devices, cube_swap(): return lax.ppermute(x, AXES[1:], pairs)  20.7 us
    ppermute x8, starting transfers between devices, swap(): lax.ppermute(x, axis, [(i, i ^ mask) for i in range(fine.shape[axis])])  7.67 us
    ppermute x8, waiting for transfers between devices, swap(): lax.ppermute(x, axis, [(i, i ^ mask) for i in range(fine.shape[axis])])  7.56 us
    ppermute x14, waiting for transfers between devices, cube_swap(): return lax.ppermute(x, AXES[1:], pairs)  5.94 us
    pallas_call x1, Pallas kernels, per_device(): pl.pallas_call(functools.partial(grad_kernel, n_high), out_shape=[shape]...  4.8 us
    pallas_call x2, Pallas kernels, per_device(): pl.pallas_call(functools.partial(logits_kernel, n_high, group), out_shape...  2.96 us
    pallas_call x1, Pallas kernels, per_device(): pl.pallas_call(functools.partial(columns_kernel, n_high), out_shape=(pltp...  2.46 us
  transfers between devices with their start and end apart: 22, of which 9 were waited for; matrix products, arithmetic and copies ran while one was open for 2% of the time, Pallas kernels for 7%

profile of v11, /device:TPU:0, one launch (start us, length us, event | category | flops | bytes accessed | tf_op | source)
XLA Modules:
  0.0 55.2 jit_solution(14586330716975419837)
XLA Ops:
  0.7 4.8 %shard_map.93 = (bf16[4,2,192,128]{3,2,1,0:T(8,128)(2,1)S(1)}, bf16[4,2,192,128]{3,2,1,0:T(8,128)(2,1)S(1)}, bf16[4,2,192,128]{3,2,1,0:T(8,128)(2,1)S(1)}, bf16[...) custom-call(s32[4]{0:T(128)S(1)} %pad_add_fusion.where_ref, bf16[256,6144]{1,0:T(8,128)(2,1)} %acts_ref.2, ...), custom_call_target="tpu_custom_call" | custom-call | tf_op jit(solution)/shard_map/pallas_call | solution.py:163
  6.1 1.3 %collective-permute-done.5 = bf16[4,2,192,128]{3,2,1,0:T(8,128)(2,1)S(1)} collective-permute-done((bf16[4,2,192,128]{3,2,1,0:T(8,128)(2,1)S(1)}, bf16[4,2,192,128]{3,2,1,0:T(8,128)(2,1)S(1)}, u32[]{:S(2)}, u32[]{:S(2)}) %collective-permute-start.5) | collective-permute-done | bytes 393248 | tf_op jit(solution)/shard_map/ppermute | solution.py:130
  7.5 3.0 %collective-permute-start.6 = (bf16[2,192,128]{2,1,0:T(8,128)(2,1)S(1)}, bf16[2,192,128]{2,1,0:T(8,128)(2,1)S(1)}, u32[]{:S(2)}, u32[]{:S(2)}) collective-permute-start(bf16[2,192,128]{2,1,0:T(8,128)(2,1)S(1)} %get-tuple-element.73), channel_id=1, source_target_pairs={{0,1},{1,0},{2,14},{3,15},{4,5},{5,4},{6,10},{7,11},{8,9},{9,8},{1... | collective-permute-start | bytes 294920 | tf_op jit(solution)/shard_map/ppermute | solution.py:140
  10.5 2.5 %collective-permute-start.7 = (bf16[2,192,128]{2,1,0:T(8,128)(2,1)S(1)}, bf16[2,192,128]{2,1,0:T(8,128)(2,1)S(1)}, u32[]{:S(2)}, u32[]{:S(2)}) collective-permute-start(bf16[2,192,128]{2,1,0:T(8,128)(2,1)S(1)} %get-tuple-element.72), channel_id=1, source_target_pairs={{0,12},{1,13},{2,3},{3,2},{4,8},{5,9},{6,7},{7,6},{8,4},{9,5},{10,... | collective-permute-start | bytes 294920 | tf_op jit(solution)/shard_map/ppermute | solution.py:140
  13.2 1.9 %collective-permute-start.1 = (bf16[2,192,128]{2,1,0:T(8,128)(2,1)S(1)}, bf16[2,192,128]{2,1,0:T(8,128)(2,1)S(1)}, u32[]{:S(2)}, u32[]{:S(2)}) collective-permute-start(bf16[2,192,128]{2,1,0:T(8,128)(2,1)S(1)} %get-tuple-element.77), channel_id=1, source_target_pairs={{0,4},{1,5},{2,11},{3,10},{4,0},{5,1},{6,15},{7,14},{8,12},{9,13},... | collective-permute-start | bytes 294920 | tf_op jit(solution)/shard_map/ppermute | solution.py:140
  15.1 2.5 %collective-permute-start.2 = (bf16[2,192,128]{2,1,0:T(8,128)(2,1)S(1)}, bf16[2,192,128]{2,1,0:T(8,128)(2,1)S(1)}, u32[]{:S(2)}, u32[]{:S(2)}) collective-permute-start(bf16[2,192,128]{2,1,0:T(8,128)(2,1)S(1)} %get-tuple-element.76), channel_id=1, source_target_pairs={{0,9},{1,8},{2,6},{3,7},{4,13},{5,12},{6,2},{7,3},{8,1},{9,0},{10,... | collective-permute-start | bytes 294920 | tf_op jit(solution)/shard_map/ppermute | solution.py:140
  19.1 1.6 %collective-permute-done.8 = bf16[2,192,128]{2,1,0:T(8,128)(2,1)S(1)} collective-permute-done((bf16[2,192,128]{2,1,0:T(8,128)(2,1)S(1)}, bf16[2,192,128]{2,1,0:T(8,128)(2,1)S(1)}, u32[]{:S(2)}, u32[]{:S(2)}) %collective-permute-start.8) | collective-permute-done | bytes 98336 | tf_op jit(solution)/shard_map/ppermute | solution.py:140
  21.2 1.1 %collective-permute-done.3 = bf16[2,192,128]{2,1,0:T(8,128)(2,1)S(1)} collective-permute-done((bf16[2,192,128]{2,1,0:T(8,128)(2,1)S(1)}, bf16[2,192,128]{2,1,0:T(8,128)(2,1)S(1)}, u32[]{:S(2)}, u32[]{:S(2)}) %collective-permute-start.3) | collective-permute-done | bytes 98336 | tf_op jit(solution)/shard_map/ppermute | solution.py:140
  22.4 1.3 %collective-permute-done.4 = bf16[2,192,128]{2,1,0:T(8,128)(2,1)S(1)} collective-permute-done((bf16[2,192,128]{2,1,0:T(8,128)(2,1)S(1)}, bf16[2,192,128]{2,1,0:T(8,128)(2,1)S(1)}, u32[]{:S(2)}, u32[]{:S(2)}) %collective-permute-start.4) | collective-permute-done | bytes 98336 | tf_op jit(solution)/shard_map/ppermute | solution.py:140
  23.7 2.7 %collective-permute-start.9 = (bf16[192,128]{1,0:T(8,128)(2,1)S(1)}, bf16[192,128]{1,0:T(8,128)(2,1)S(1)}, u32[]{:S(2)}, u32[]{:S(2)}) collective-permute-start(bf16[192,128]{1,0:T(8,128)(2,1)S(1)} %fusion.11), channel_id=1, source_target_pairs={{0,16},{16,0},{1,17},{17,1},{2,18},{18,2},{3,19},{19,3},{4,20},{20... | collective-permute-start | bytes 147464 | tf_op jit(solution)/shard_map/ppermute | solution.py:130
  27.1 1.7 %collective-permute-done.9 = bf16[192,128]{1,0:T(8,128)(2,1)S(1)} collective-permute-done((bf16[192,128]{1,0:T(8,128)(2,1)S(1)}, bf16[192,128]{1,0:T(8,128)(2,1)S(1)}, u32[]{:S(2)}, u32[]{:S(2)}) %collective-permute-start.9) | collective-permute-done | bytes 49184 | tf_op jit(solution)/shard_map/ppermute | solution.py:130
  28.9 2.7 %collective-permute-start.10 = (bf16[192,128]{1,0:T(8,128)(2,1)S(1)}, bf16[192,128]{1,0:T(8,128)(2,1)S(1)}, u32[]{:S(2)}, u32[]{:S(2)}) collective-permute-start(bf16[192,128]{1,0:T(8,128)(2,1)S(1)} %get-tuple-element.67), channel_id=1, source_target_pairs={{0,16},{16,0},{1,17},{17,1},{2,18},{18,2},{3,19},{19,3},{4,20},{20... | collective-permute-start | bytes 147464 | tf_op jit(solution)/shard_map/ppermute | solution.py:130
  31.6 1.1 %collective-permute-start.11 = (f32[192,128]{1,0:T(8,128)S(1)}, f32[192,128]{1,0:T(8,128)S(1)}, u32[]{:S(2)}, u32[]{:S(2)}) collective-permute-start(f32[192,128]{1,0:T(8,128)S(1)} %get-tuple-element.68), channel_id=1, source_target_pairs={{0,1},{1,0},{2,3},{3,2},{4,5},{5,4},{6,7},{7,6},{8,9},{9,8},{10,11... | collective-permute-start | bytes 294920 | tf_op jit(solution)/shard_map/ppermute | solution.py:130
  32.7 1.3 %collective-permute-done.10 = bf16[192,128]{1,0:T(8,128)(2,1)S(1)} collective-permute-done((bf16[192,128]{1,0:T(8,128)(2,1)S(1)}, bf16[192,128]{1,0:T(8,128)(2,1)S(1)}, u32[]{:S(2)}, u32[]{:S(2)}) %collective-permute-start.10) | collective-permute-done | bytes 49184 | tf_op jit(solution)/shard_map/ppermute | solution.py:130
  34.0 3.3 %collective-permute-done.11 = f32[192,128]{1,0:T(8,128)S(1)} collective-permute-done((f32[192,128]{1,0:T(8,128)S(1)}, f32[192,128]{1,0:T(8,128)S(1)}, u32[]{:S(2)}, u32[]{:S(2)}) %collective-permute-start.11) | collective-permute-done | bytes 98336 | tf_op jit(solution)/shard_map/ppermute | solution.py:130
  37.3 2.9 %collective-permute-start.13 = (bf16[2,192,128]{2,1,0:T(8,128)(2,1)S(1)}, bf16[2,192,128]{2,1,0:T(8,128)(2,1)S(1)}, u32[]{:S(2)}, u32[]{:S(2)}) collective-permute-start(bf16[2,192,128]{2,1,0:T(8,128)(2,1)S(1)} %pad_maximum_fusion.2), channel_id=1, source_target_pairs={{0,9},{1,8},{2,6},{3,7},{4,13},{5,12},{6,2},{7,3},{8,1},{9,0},{10,... | collective-permute-start | bytes 294920 | tf_op jit(solution)/shard_map/ppermute | solution.py:140
  40.1 2.1 %collective-permute-start.15 = (bf16[2,192,128]{2,1,0:T(8,128)(2,1)S(1)}, bf16[2,192,128]{2,1,0:T(8,128)(2,1)S(1)}, u32[]{:S(2)}, u32[]{:S(2)}) collective-permute-start(bf16[2,192,128]{2,1,0:T(8,128)(2,1)S(1)} %pad_maximum_fusion.2), channel_id=1, source_target_pairs={{0,5},{1,4},{2,10},{3,11},{4,1},{5,0},{6,14},{7,15},{8,13},{9,12},... | collective-permute-start | bytes 294920 | tf_op jit(solution)/shard_map/ppermute | solution.py:140
  42.2 1.1 %collective-permute-start.16 = (bf16[2,192,128]{2,1,0:T(8,128)(2,1)S(1)}, bf16[2,192,128]{2,1,0:T(8,128)(2,1)S(1)}, u32[]{:S(2)}, u32[]{:S(2)}) collective-permute-start(bf16[2,192,128]{2,1,0:T(8,128)(2,1)S(1)} %pad_maximum_fusion.2), channel_id=1, source_target_pairs={{0,1},{1,0},{2,14},{3,15},{4,5},{5,4},{6,10},{7,11},{8,9},{9,8},{1... | collective-permute-start | bytes 294920 | tf_op jit(solution)/shard_map/ppermute | solution.py:140
  43.3 1.9 %collective-permute-start.17 = (bf16[2,192,128]{2,1,0:T(8,128)(2,1)S(1)}, bf16[2,192,128]{2,1,0:T(8,128)(2,1)S(1)}, u32[]{:S(2)}, u32[]{:S(2)}) collective-permute-start(bf16[2,192,128]{2,1,0:T(8,128)(2,1)S(1)} %pad_maximum_fusion.2), channel_id=1, source_target_pairs={{0,12},{1,13},{2,3},{3,2},{4,8},{5,9},{6,7},{7,6},{8,4},{9,5},{10,... | collective-permute-start | bytes 294920 | tf_op jit(solution)/shard_map/ppermute | solution.py:140
  45.2 1.5 %collective-permute-start.18 = (bf16[2,192,128]{2,1,0:T(8,128)(2,1)S(1)}, bf16[2,192,128]{2,1,0:T(8,128)(2,1)S(1)}, u32[]{:S(2)}, u32[]{:S(2)}) collective-permute-start(bf16[2,192,128]{2,1,0:T(8,128)(2,1)S(1)} %pad_maximum_fusion.2), channel_id=1, source_target_pairs={{0,13},{1,12},{2,15},{3,14},{4,9},{5,8},{6,11},{7,10},{8,5},{9,4},... | collective-permute-start | bytes 294920 | tf_op jit(solution)/shard_map/ppermute | solution.py:140
  47.6 2.5 %shard_map.94 = (bf16[4,256,768]{2,1,0:T(8,128)(2,1)S(1)}, bf16[4,256,768]{2,1,0:T(8,128)(2,1)S(1)}) custom-call(s32[4]{0:T(128)S(1)} %pad_add_fusion.where_ref, bf16[256,6144]{1,0:T(8,128)(2,1)} %acts_ref.2), custom_call_target="tpu_custom_call" | custom-call | tf_op jit(solution)/shard_map/pallas_call | solution.py:231
  50.2 1.4 %collective-permute-done.18 = bf16[2,192,128]{2,1,0:T(8,128)(2,1)S(1)} collective-permute-done((bf16[2,192,128]{2,1,0:T(8,128)(2,1)S(1)}, bf16[2,192,128]{2,1,0:T(8,128)(2,1)S(1)}, u32[]{:S(2)}, u32[]{:S(2)}) %collective-permute-start.18) | collective-permute-done | bytes 98336 | tf_op jit(solution)/shard_map/ppermute | solution.py:140
  52.2 1.2 %shard_map.95.refs_4_ = f32[256,128]{1,0:T(8,128)S(1)} custom-call(s32[4]{0:T(128)S(1)} %pad_add_fusion.where_ref, bf16[4,256,768]{2,1,0:T(8,128)(2,1)S(1)} %get-tuple-element.59.columns_ref, bf16[4,2,192,128]{3,2,1,0:T(8,128)(2,1)S(1)} %pad_maximum_fusion.refs_0_, bf16[4,2,192,128]{3,2,1,0:T(8,128)(2,1)S(1)} %collective-permute-done.21.refs_1_), custom_call_target="tpu_custom_call" | custom-call | tf_op jit(solution)/shard_map/pallas_call | solution.py:250
  53.4 1.8 %shard_map.96 = bf16[256,128]{1,0:T(8,128)(2,1)} custom-call(s32[4]{0:T(128)S(1)} %pad_add_fusion.where_ref, bf16[4,256,768]{2,1,0:T(8,128)(2,1)S(1)} %get-tuple-element.58.columns_ref, bf16[3,2,192,128]{3,2,1,0:T(8,128)(2,1)S(1)} %pad_maximum_fusion.1.refs_0_, bf16[3,2,192,128]{3,2,1,0:T(8,128)(2,1)S(1)} %collective-permute-done.19.refs_1_, ...), custom_call_target="tpu_custom_call" | custom-call | tf_op jit(solution)/shard_map/pallas_call | solution.py:250
  (44 shorter events, 4.8 us)
Async XLA Ops:
  5.5 1.9 %collective-permute-start.5 = (bf16[4,2,192,128]{3,2,1,0:T(8,128)(2,1)S(1)}, bf16[4,2,192,128]{3,2,1,0:T(8,128)(2,1)S(1)}, u32[]{:S(2)}, u32[]{:S(2)}) collective-permute-start(bf16[4,2,192,128]{3,2,1,0:T(8,128)(2,1)S(1)} %get-tuple-element.38), channel_id=1, source_target_pairs={{0,2},{2,0},{1,3},{3,1},{4,6},{6,4},{5,7},{7,5},{8,10},{10,8},{9,1... | collective-permute-start | bytes 1179656 | tf_op jit(solution)/shard_map/ppermute | solution.py:130
  6.0 7.0 %collective-permute-start = (bf16[4,2,192,128]{3,2,1,0:T(8,128)(2,1)S(1)}, bf16[4,2,192,128]{3,2,1,0:T(8,128)(2,1)S(1)}, u32[]{:S(2)}, u32[]{:S(2)}) collective-permute-start(bf16[4,2,192,128]{3,2,1,0:T(8,128)(2,1)S(1)} %get-tuple-element.36), channel_id=1, source_target_pairs={{0,2},{2,0},{1,3},{3,1},{4,6},{6,4},{5,7},{7,5},{8,10},{10,8},{9,1... | collective-permute-start | bytes 1179656 | tf_op jit(solution)/shard_map/ppermute | solution.py:130
  7.5 10.1 %collective-permute-start.6 = (bf16[2,192,128]{2,1,0:T(8,128)(2,1)S(1)}, bf16[2,192,128]{2,1,0:T(8,128)(2,1)S(1)}, u32[]{:S(2)}, u32[]{:S(2)}) collective-permute-start(bf16[2,192,128]{2,1,0:T(8,128)(2,1)S(1)} %get-tuple-element.73), channel_id=1, source_target_pairs={{0,1},{1,0},{2,14},{3,15},{4,5},{5,4},{6,10},{7,11},{8,9},{9,8},{1... | collective-permute-start | bytes 294920 | tf_op jit(solution)/shard_map/ppermute | solution.py:140
  10.5 7.6 %collective-permute-start.7 = (bf16[2,192,128]{2,1,0:T(8,128)(2,1)S(1)}, bf16[2,192,128]{2,1,0:T(8,128)(2,1)S(1)}, u32[]{:S(2)}, u32[]{:S(2)}) collective-permute-start(bf16[2,192,128]{2,1,0:T(8,128)(2,1)S(1)} %get-tuple-element.72), channel_id=1, source_target_pairs={{0,12},{1,13},{2,3},{3,2},{4,8},{5,9},{6,7},{7,6},{8,4},{9,5},{10,... | collective-permute-start | bytes 294920 | tf_op jit(solution)/shard_map/ppermute | solution.py:140
  13.0 7.7 %collective-permute-start.8 = (bf16[2,192,128]{2,1,0:T(8,128)(2,1)S(1)}, bf16[2,192,128]{2,1,0:T(8,128)(2,1)S(1)}, u32[]{:S(2)}, u32[]{:S(2)}) collective-permute-start(bf16[2,192,128]{2,1,0:T(8,128)(2,1)S(1)} %get-tuple-element.71), channel_id=1, source_target_pairs={{0,13},{1,12},{2,15},{3,14},{4,9},{5,8},{6,11},{7,10},{8,5},{9,4},... | collective-permute-start | bytes 294920 | tf_op jit(solution)/shard_map/ppermute | solution.py:140
  13.2 33.5 %copy-start = (f32[384,128]{1,0:T(8,128)S(1)}, f32[384,128]{1,0:T(8,128)}, u32[]{:S(2)}) copy-start(f32[384,128]{1,0:T(8,128)} %refs_0_.1) | copy-start | bytes 589828
  13.2 33.5 %copy-start.1 = (f32[384,128]{1,0:T(8,128)S(1)}, f32[384,128]{1,0:T(8,128)}, u32[]{:S(2)}) copy-start(f32[384,128]{1,0:T(8,128)} %refs_1_.1) | copy-start | bytes 589828
  13.2 7.5 %collective-permute-start.1 = (bf16[2,192,128]{2,1,0:T(8,128)(2,1)S(1)}, bf16[2,192,128]{2,1,0:T(8,128)(2,1)S(1)}, u32[]{:S(2)}, u32[]{:S(2)}) collective-permute-start(bf16[2,192,128]{2,1,0:T(8,128)(2,1)S(1)} %get-tuple-element.77), channel_id=1, source_target_pairs={{0,4},{1,5},{2,11},{3,10},{4,0},{5,1},{6,15},{7,14},{8,12},{9,13},... | collective-permute-start | bytes 294920 | tf_op jit(solution)/shard_map/ppermute | solution.py:140
  15.1 6.1 %collective-permute-start.2 = (bf16[2,192,128]{2,1,0:T(8,128)(2,1)S(1)}, bf16[2,192,128]{2,1,0:T(8,128)(2,1)S(1)}, u32[]{:S(2)}, u32[]{:S(2)}) collective-permute-start(bf16[2,192,128]{2,1,0:T(8,128)(2,1)S(1)} %get-tuple-element.76), channel_id=1, source_target_pairs={{0,9},{1,8},{2,6},{3,7},{4,13},{5,12},{6,2},{7,3},{8,1},{9,0},{10,... | collective-permute-start | bytes 294920 | tf_op jit(solution)/shard_map/ppermute | solution.py:140
  17.6 4.7 %collective-permute-start.3 = (bf16[2,192,128]{2,1,0:T(8,128)(2,1)S(1)}, bf16[2,192,128]{2,1,0:T(8,128)(2,1)S(1)}, u32[]{:S(2)}, u32[]{:S(2)}) collective-permute-start(bf16[2,192,128]{2,1,0:T(8,128)(2,1)S(1)} %get-tuple-element.75), channel_id=1, source_target_pairs={{0,8},{1,9},{2,7},{3,6},{4,12},{5,13},{6,3},{7,2},{8,0},{9,1},{10,... | collective-permute-start | bytes 294920 | tf_op jit(solution)/shard_map/ppermute | solution.py:140
  18.1 5.5 %collective-permute-start.4 = (bf16[2,192,128]{2,1,0:T(8,128)(2,1)S(1)}, bf16[2,192,128]{2,1,0:T(8,128)(2,1)S(1)}, u32[]{:S(2)}, u32[]{:S(2)}) collective-permute-start(bf16[2,192,128]{2,1,0:T(8,128)(2,1)S(1)} %get-tuple-element.74), channel_id=1, source_target_pairs={{0,5},{1,4},{2,10},{3,11},{4,1},{5,0},{6,14},{7,15},{8,13},{9,12},... | collective-permute-start | bytes 294920 | tf_op jit(solution)/shard_map/ppermute | solution.py:140
  23.7 5.1 %collective-permute-start.9 = (bf16[192,128]{1,0:T(8,128)(2,1)S(1)}, bf16[192,128]{1,0:T(8,128)(2,1)S(1)}, u32[]{:S(2)}, u32[]{:S(2)}) collective-permute-start(bf16[192,128]{1,0:T(8,128)(2,1)S(1)} %fusion.11), channel_id=1, source_target_pairs={{0,16},{16,0},{1,17},{17,1},{2,18},{18,2},{3,19},{19,3},{4,20},{20... | collective-permute-start | bytes 147464 | tf_op jit(solution)/shard_map/ppermute | solution.py:130
  28.9 5.1 %collective-permute-start.10 = (bf16[192,128]{1,0:T(8,128)(2,1)S(1)}, bf16[192,128]{1,0:T(8,128)(2,1)S(1)}, u32[]{:S(2)}, u32[]{:S(2)}) collective-permute-start(bf16[192,128]{1,0:T(8,128)(2,1)S(1)} %get-tuple-element.67), channel_id=1, source_target_pairs={{0,16},{16,0},{1,17},{17,1},{2,18},{18,2},{3,19},{19,3},{4,20},{20... | collective-permute-start | bytes 147464 | tf_op jit(solution)/shard_map/ppermute | solution.py:130
  31.6 5.7 %collective-permute-start.11 = (f32[192,128]{1,0:T(8,128)S(1)}, f32[192,128]{1,0:T(8,128)S(1)}, u32[]{:S(2)}, u32[]{:S(2)}) collective-permute-start(f32[192,128]{1,0:T(8,128)S(1)} %get-tuple-element.68), channel_id=1, source_target_pairs={{0,1},{1,0},{2,3},{3,2},{4,5},{5,4},{6,7},{7,6},{8,9},{9,8},{10,11... | collective-permute-start | bytes 294920 | tf_op jit(solution)/shard_map/ppermute | solution.py:130
  37.3 6.1 %collective-permute-start.12 = (bf16[2,192,128]{2,1,0:T(8,128)(2,1)S(1)}, bf16[2,192,128]{2,1,0:T(8,128)(2,1)S(1)}, u32[]{:S(2)}, u32[]{:S(2)}) collective-permute-start(bf16[2,192,128]{2,1,0:T(8,128)(2,1)S(1)} %pad_maximum_fusion.2), channel_id=1, source_target_pairs={{0,4},{1,5},{2,11},{3,10},{4,0},{5,1},{6,15},{7,14},{8,12},{9,13},... | collective-permute-start | bytes 294920 | tf_op jit(solution)/shard_map/ppermute | solution.py:140
  37.3 7.9 %collective-permute-start.13 = (bf16[2,192,128]{2,1,0:T(8,128)(2,1)S(1)}, bf16[2,192,128]{2,1,0:T(8,128)(2,1)S(1)}, u32[]{:S(2)}, u32[]{:S(2)}) collective-permute-start(bf16[2,192,128]{2,1,0:T(8,128)(2,1)S(1)} %pad_maximum_fusion.2), channel_id=1, source_target_pairs={{0,9},{1,8},{2,6},{3,7},{4,13},{5,12},{6,2},{7,3},{8,1},{9,0},{10,... | collective-permute-start | bytes 294920 | tf_op jit(solution)/shard_map/ppermute | solution.py:140
  40.1 9.9 %collective-permute-start.14 = (bf16[2,192,128]{2,1,0:T(8,128)(2,1)S(1)}, bf16[2,192,128]{2,1,0:T(8,128)(2,1)S(1)}, u32[]{:S(2)}, u32[]{:S(2)}) collective-permute-start(bf16[2,192,128]{2,1,0:T(8,128)(2,1)S(1)} %pad_maximum_fusion.2), channel_id=1, source_target_pairs={{0,8},{1,9},{2,7},{3,6},{4,12},{5,13},{6,3},{7,2},{8,0},{9,1},{10,... | collective-permute-start | bytes 294920 | tf_op jit(solution)/shard_map/ppermute | solution.py:140
  40.1 9.9 %collective-permute-start.15 = (bf16[2,192,128]{2,1,0:T(8,128)(2,1)S(1)}, bf16[2,192,128]{2,1,0:T(8,128)(2,1)S(1)}, u32[]{:S(2)}, u32[]{:S(2)}) collective-permute-start(bf16[2,192,128]{2,1,0:T(8,128)(2,1)S(1)} %pad_maximum_fusion.2), channel_id=1, source_target_pairs={{0,5},{1,4},{2,10},{3,11},{4,1},{5,0},{6,14},{7,15},{8,13},{9,12},... | collective-permute-start | bytes 294920 | tf_op jit(solution)/shard_map/ppermute | solution.py:140
  42.2 8.0 %collective-permute-start.16 = (bf16[2,192,128]{2,1,0:T(8,128)(2,1)S(1)}, bf16[2,192,128]{2,1,0:T(8,128)(2,1)S(1)}, u32[]{:S(2)}, u32[]{:S(2)}) collective-permute-start(bf16[2,192,128]{2,1,0:T(8,128)(2,1)S(1)} %pad_maximum_fusion.2), channel_id=1, source_target_pairs={{0,1},{1,0},{2,14},{3,15},{4,5},{5,4},{6,10},{7,11},{8,9},{9,8},{1... | collective-permute-start | bytes 294920 | tf_op jit(solution)/shard_map/ppermute | solution.py:140
  43.3 6.9 %collective-permute-start.17 = (bf16[2,192,128]{2,1,0:T(8,128)(2,1)S(1)}, bf16[2,192,128]{2,1,0:T(8,128)(2,1)S(1)}, u32[]{:S(2)}, u32[]{:S(2)}) collective-permute-start(bf16[2,192,128]{2,1,0:T(8,128)(2,1)S(1)} %pad_maximum_fusion.2), channel_id=1, source_target_pairs={{0,12},{1,13},{2,3},{3,2},{4,8},{5,9},{6,7},{7,6},{8,4},{9,5},{10,... | collective-permute-start | bytes 294920 | tf_op jit(solution)/shard_map/ppermute | solution.py:140
  45.2 6.4 %collective-permute-start.18 = (bf16[2,192,128]{2,1,0:T(8,128)(2,1)S(1)}, bf16[2,192,128]{2,1,0:T(8,128)(2,1)S(1)}, u32[]{:S(2)}, u32[]{:S(2)}) collective-permute-start(bf16[2,192,128]{2,1,0:T(8,128)(2,1)S(1)} %pad_maximum_fusion.2), channel_id=1, source_target_pairs={{0,13},{1,12},{2,15},{3,14},{4,9},{5,8},{6,11},{7,10},{8,5},{9,4},... | collective-permute-start | bytes 294920 | tf_op jit(solution)/shard_map/ppermute | solution.py:140
  50.1 2.1 %collective-permute-start.21 = (bf16[4,2,192,128]{3,2,1,0:T(8,128)(2,1)S(1)}, bf16[4,2,192,128]{3,2,1,0:T(8,128)(2,1)S(1)}, u32[]{:S(2)}, u32[]{:S(2)}) collective-permute-start(bf16[4,2,192,128]{3,2,1,0:T(8,128)(2,1)S(1)} %pad_maximum_fusion.refs_0_), channel_id=1, source_target_pairs={{0,2},{2,0},{1,3},{3,1},{4,6},{6,4},{5,7},{7,5},{8,10},{10,8},{9,1... | collective-permute-start | bytes 1179656 | tf_op jit(solution)/shard_map/ppermute | solution.py:130
  51.6 1.8 %collective-permute-start.19 = (bf16[3,2,192,128]{3,2,1,0:T(8,128)(2,1)S(1)}, bf16[3,2,192,128]{3,2,1,0:T(8,128)(2,1)S(1)}, u32[]{:S(2)}, u32[]{:S(2)}) collective-permute-start(bf16[3,2,192,128]{3,2,1,0:T(8,128)(2,1)S(1)} %pad_maximum_fusion.1.refs_0_), channel_id=1, source_target_pairs={{0,2},{2,0},{1,3},{3,1},{4,6},{6,4},{5,7},{7,5},{8,10},{10,8},{9,1... | collective-permute-start | bytes 884744 | tf_op jit(solution)/shard_map/ppermute | solution.py:130
  51.7 1.7 %collective-permute-start.20 = (bf16[2,192,128]{2,1,0:T(8,128)(2,1)S(1)}, bf16[2,192,128]{2,1,0:T(8,128)(2,1)S(1)}, u32[]{:S(2)}, u32[]{:S(2)}) collective-permute-start(bf16[2,192,128]{2,1,0:T(8,128)(2,1)S(1)} %pad_maximum_fusion.2), channel_id=1, source_target_pairs={{0,2},{2,0},{1,3},{3,1},{4,6},{6,4},{5,7},{7,5},{8,10},{10,8},{9,1... | collective-permute-start | bytes 294920 | tf_op jit(solution)/shard_map/ppermute | solution.py:130
  (1 other events, 33.5 us)

commit v12 on v11

--- a/solution.py
+++ b/solution.py
@@ -12,6 +12,7 @@
 N_LOW = 4
 CHIPS = ((1, 0), (2, 1), (2, 0), (1, 1), (0, 1), (3, 0), (3, 1), (0, 0))
 LOWS = ((1, 2), (0, 3))
+NEXT = ((1, 0), (2, 0), (0, 1))
 VMEM_LIMIT = 8 * 2**20
 
 
@@ -93,11 +94,9 @@
     before = None
     if len(pieces[-1].shape) == 2:
         *pieces, before = pieces
-    core, rep = where_ref[2], where_ref[3]
     half, experts = weight.shape[-2:]
-    for i, piece in enumerate(pieces):
-        owner = core ^ (i % 2)
-        for n, place, of_rep in places(group, owner, rep, i // 2, piece.shape[0]):
+    for piece, blocks in zip(pieces, places(group, where_ref[2], where_ref[3])):
+        for n, (place, owner, of_rep) in enumerate(blocks):
             for j in range(n_high):
                 weight[place, j, owner, of_rep] = piece[n, j]
     total = None if before is None else before[...]
@@ -111,14 +110,16 @@
     out_ref[...] = total.astype(out_ref.dtype)
 
 
-def places(group, owner, rep, home, count):
-    out = []
-    for n in range(count):
-        slot = 7 if home else 4 * group + n
-        chip_low, d_rep = CHIPS[slot]
-        flip = owner if slot < 6 else 0
-        out.append((n, LOWS[group].index(chip_low) ^ flip, rep ^ d_rep ^ flip))
-    return out
+def places(group, core, rep):
+    pieces = []
+    for chip in NEXT[:2] if group == 0 else NEXT[2:]:
+        for by in (core, 1 - core):
+            place = LOWS[group].index(chip[0]) ^ by
+            pieces.append([(place, owner, rep ^ chip[1] ^ by) for owner in range(2)])
+    if group == 1:
+        pieces += [[(1, owner, rep ^ 1)] for owner in (core, 1 - core)]
+        pieces += [[(0, owner, rep)] for owner in (core, 1 - core)]
+    return pieces
 
 
 def solution(mesh):
@@ -141,6 +142,13 @@
 
     def to_slot(x, slot):
         return cube_swap(x, lambda core: CHIPS[slot ^ core if slot < 6 else slot])
+
+    def to_next(x, slot):
+        d_low, d_rep = NEXT[slot]
+        return cube_swap(x, lambda core: (d_low ^ (3 * core), d_rep ^ core))
+
+    def to_corner(x):
+        return cube_swap(x, lambda core: (3, 1))
 
     def per_device(acts, grad_logits, master, moment_one, moment_two, step_count):
         tokens, experts = grad_logits.shape
@@ -213,21 +221,23 @@
         weight = adamw(grad, *mine, step_count)[0].astype(bf16)
 
         column = jnp.stack([swap(weight, "high", j) if j else weight for j in range(n_high)])
+        column, grad = lax.optimization_barrier((column, grad))
         other = swap(grad, "rep")
-        column, other = lax.optimization_barrier((column, other))
-        got = [to_slot(column, slot) for slot in range(7)]
+        corner = to_corner(column)
         across = swap(column, "core")
+        chip = jnp.where(core == 0, jnp.stack([column, across]), jnp.stack([across, column]))
+        got = [to_next(chip, slot) for slot in range(3)]
 
         whole = jnp.where(
             rep == 0,
             jnp.concatenate([grad, other], 0),
             jnp.concatenate([other, grad], 0),
         )
-        got[:2], whole, late_acts = lax.optimization_barrier((got[:2], whole, acts))
         state = adamw(whole, *state_in, step_count)
 
         columns = [None, None]
         if in_kernels:
+            state, late_acts = lax.optimization_barrier((state, acts))
             columns = pl.pallas_call(
                 functools.partial(columns_kernel, n_high),
                 out_shape=(pltpu.VMEM((2 * n_high, tokens, 4 * half), bf16),) * 2,
@@ -236,10 +246,13 @@
                 scratch_shapes=[pltpu.SemaphoreType.DMA((2, 2 * n_high))],
                 compiler_params=params,
             )(where, pltpu.with_memory_space_constraint(late_acts, pltpu.HBM))
-        got[:4], state, columns = lax.optimization_barrier((got[:4], state, columns))
-        first, second = jnp.stack(got[:4]), jnp.stack(got[4:])
-        first_over, second_over = swap(first, "core"), swap(second, "core")
-        pieces = ([first, first_over], [second, second_over, column[None], across[None]])
+        got[0], state, columns = lax.optimization_barrier((got[0], state, columns))
+        got[2], corner = lax.optimization_barrier((got[2], corner))
+        over = [swap(x, "core") for x in got]
+        corner_over = swap(corner, "core")
+        first = [x[slot] for slot in range(2) for x in (got, over)]
+        second = [got[2], over[2], corner[None], corner_over[None], column[None], across[None]]
+        pieces = (first, second)
         logits = None
         for group, (received, acts_columns) in enumerate(zip(pieces, columns)):
             if in_kernels:
@@ -257,9 +270,8 @@
                 )(where, *operands)
             else:
                 rows_at, values = [], []
-                for i, piece in enumerate(received):
-                    owner = core ^ (i % 2)
-                    for n, place, of_rep in places(group, owner, rep, i // 2, piece.shape[0]):
+                for piece, blocks in zip(received, places(group, core, rep)):
+                    for n, (place, owner, of_rep) in enumerate(blocks):
                         d_low = jnp.array(LOWS[group])[place]
                         for j in range(n_high):
                             at = ((high ^ j) * N_LOW + (low ^ d_low)) * 2 + owner

time: 55.4 us -> 55.6 us (level)
  waiting for transfers between devices: 13.5 us -> 17.7 us
  starting transfers between devices: 28.4 us -> 24.4 us
    ppermute x8 -> x10, waiting for transfers between devices: 7.56 us -> 13.2 us  [swap(): lax.ppermute(x, axis, [(i, i ^ mask) for i in range(fine.shape[axis])])]
    ppermute x14 -> x11, starting transfers between devices: 20.7 us -> 16.2 us  [cube_swap(): return lax.ppermute(x, AXES[1:], pairs)]
    ppermute x14 -> x11, waiting for transfers between devices: 5.94 us -> 4.58 us  [cube_swap(): return lax.ppermute(x, AXES[1:], pairs)]
    ppermute x8 -> x10, starting transfers between devices: 7.67 us -> 8.28 us  [swap(): lax.ppermute(x, axis, [(i, i ^ mask) for i in range(fine.shape[axis])])]
  transfers between devices with their start and end apart: 22 -> 21, of which waited for: 9 -> 10; matrix products, arithmetic and copies ran while one was open for 2% -> 2% of each run, Pallas kernels for 7% -> 7%
where the time goes in v12:
time: 55.6 us; the launch traced here: 55.5 us
  starting transfers between devices  24.4 us (44%)
  waiting for transfers between devices  17.7 us (32%)
  Pallas kernels  10.2 us (18%)
  between operations  1.55 us (3%)
  other arithmetic  1.44 us (3%)
    ppermute x11, starting transfers between devices, cube_swap(): return lax.ppermute(x, AXES[1:], pairs)  16.2 us
    ppermute x10, waiting for transfers between devices, swap(): lax.ppermute(x, axis, [(i, i ^ mask) for i in range(fine.shape[axis])])  13.2 us
    ppermute x10, starting transfers between devices, swap(): lax.ppermute(x, axis, [(i, i ^ mask) for i in range(fine.shape[axis])])  8.28 us
    pallas_call x1, Pallas kernels, per_device(): pl.pallas_call(functools.partial(grad_kernel, n_high), out_shape=[shape]...  4.8 us
    ppermute x11, waiting for transfers between devices, cube_swap(): return lax.ppermute(x, AXES[1:], pairs)  4.58 us
    pallas_call x2, Pallas kernels, per_device(): pl.pallas_call(functools.partial(logits_kernel, n_high, group), out_shape...  2.96 us
    pallas_call x1, Pallas kernels, per_device(): pl.pallas_call(functools.partial(columns_kernel, n_high), out_shape=(pltp...  2.46 us
  transfers between devices with their start and end apart: 21, of which 10 were waited for; matrix products, arithmetic and copies ran while one was open for 2% of the time, Pallas kernels for 7%

profile of v12, /device:TPU:0, one launch (start us, length us, event | category | flops | bytes accessed | tf_op | source)
XLA Modules:
  0.0 55.5 jit_solution(13621807033551325973)
XLA Ops:
  0.7 4.8 %shard_map.93 = (bf16[4,2,192,128]{3,2,1,0:T(8,128)(2,1)S(1)}, bf16[4,2,192,128]{3,2,1,0:T(8,128)(2,1)S(1)}, bf16[4,2,192,128]{3,2,1,0:T(8,128)(2,1)S(1)}, bf16[...) custom-call(s32[4]{0:T(128)S(1)} %pad_add_fusion.where_ref, bf16[256,6144]{1,0:T(8,128)(2,1)} %acts_ref.2, ...), custom_call_target="tpu_custom_call" | custom-call | tf_op jit(solution)/shard_map/pallas_call | solution.py:171
  6.1 1.3 %collective-permute-done.5 = bf16[4,2,192,128]{3,2,1,0:T(8,128)(2,1)S(1)} collective-permute-done((bf16[4,2,192,128]{3,2,1,0:T(8,128)(2,1)S(1)}, bf16[4,2,192,128]{3,2,1,0:T(8,128)(2,1)S(1)}, u32[]{:S(2)}, u32[]{:S(2)}) %collective-permute-start.5) | collective-permute-done | bytes 393248 | tf_op jit(solution)/shard_map/ppermute | solution.py:131
  7.5 3.0 %collective-permute-start.6 = (bf16[2,192,128]{2,1,0:T(8,128)(2,1)S(1)}, bf16[2,192,128]{2,1,0:T(8,128)(2,1)S(1)}, u32[]{:S(2)}, u32[]{:S(2)}) collective-permute-start(bf16[2,192,128]{2,1,0:T(8,128)(2,1)S(1)} %get-tuple-element.71), channel_id=1, source_target_pairs={{0,1},{1,0},{2,14},{3,15},{4,5},{5,4},{6,10},{7,11},{8,9},{9,8},{1... | collective-permute-start | bytes 294920 | tf_op jit(solution)/shard_map/ppermute | solution.py:141
  10.5 2.5 %collective-permute-start.7 = (bf16[2,192,128]{2,1,0:T(8,128)(2,1)S(1)}, bf16[2,192,128]{2,1,0:T(8,128)(2,1)S(1)}, u32[]{:S(2)}, u32[]{:S(2)}) collective-permute-start(bf16[2,192,128]{2,1,0:T(8,128)(2,1)S(1)} %get-tuple-element.70), channel_id=1, source_target_pairs={{0,12},{1,13},{2,3},{3,2},{4,8},{5,9},{6,7},{7,6},{8,4},{9,5},{10,... | collective-permute-start | bytes 294920 | tf_op jit(solution)/shard_map/ppermute | solution.py:141
  13.2 1.9 %collective-permute-start.1 = (bf16[2,192,128]{2,1,0:T(8,128)(2,1)S(1)}, bf16[2,192,128]{2,1,0:T(8,128)(2,1)S(1)}, u32[]{:S(2)}, u32[]{:S(2)}) collective-permute-start(bf16[2,192,128]{2,1,0:T(8,128)(2,1)S(1)} %get-tuple-element.75), channel_id=1, source_target_pairs={{0,4},{1,5},{2,11},{3,10},{4,0},{5,1},{6,15},{7,14},{8,12},{9,13},... | collective-permute-start | bytes 294920 | tf_op jit(solution)/shard_map/ppermute | solution.py:141
  15.1 2.5 %collective-permute-start.2 = (bf16[2,192,128]{2,1,0:T(8,128)(2,1)S(1)}, bf16[2,192,128]{2,1,0:T(8,128)(2,1)S(1)}, u32[]{:S(2)}, u32[]{:S(2)}) collective-permute-start(bf16[2,192,128]{2,1,0:T(8,128)(2,1)S(1)} %get-tuple-element.74), channel_id=1, source_target_pairs={{0,9},{1,8},{2,6},{3,7},{4,13},{5,12},{6,2},{7,3},{8,1},{9,0},{10,... | collective-permute-start | bytes 294920 | tf_op jit(solution)/shard_map/ppermute | solution.py:141
  18.1 0.9 %collective-permute-start.4 = (bf16[2,192,128]{2,1,0:T(8,128)(2,1)S(1)}, bf16[2,192,128]{2,1,0:T(8,128)(2,1)S(1)}, u32[]{:S(2)}, u32[]{:S(2)}) collective-permute-start(bf16[2,192,128]{2,1,0:T(8,128)(2,1)S(1)} %get-tuple-element.72), channel_id=1, source_target_pairs={{0,5},{1,4},{2,10},{3,11},{4,1},{5,0},{6,14},{7,15},{8,13},{9,12},... | collective-permute-start | bytes 294920 | tf_op jit(solution)/shard_map/ppermute | solution.py:141
  19.1 1.6 %collective-permute-done.8 = bf16[2,192,128]{2,1,0:T(8,128)(2,1)S(1)} collective-permute-done((bf16[2,192,128]{2,1,0:T(8,128)(2,1)S(1)}, bf16[2,192,128]{2,1,0:T(8,128)(2,1)S(1)}, u32[]{:S(2)}, u32[]{:S(2)}) %collective-permute-start.8) | collective-permute-done | bytes 98336 | tf_op jit(solution)/shard_map/ppermute | solution.py:141
  20.7 0.5 collective-permute-done.2
  21.2 1.1 %collective-permute-done.3 = bf16[2,192,128]{2,1,0:T(8,128)(2,1)S(1)} collective-permute-done((bf16[2,192,128]{2,1,0:T(8,128)(2,1)S(1)}, bf16[2,192,128]{2,1,0:T(8,128)(2,1)S(1)}, u32[]{:S(2)}, u32[]{:S(2)}) %collective-permute-start.3) | collective-permute-done | bytes 98336 | tf_op jit(solution)/shard_map/ppermute | solution.py:141
  22.4 1.3 %collective-permute-done.4 = bf16[2,192,128]{2,1,0:T(8,128)(2,1)S(1)} collective-permute-done((bf16[2,192,128]{2,1,0:T(8,128)(2,1)S(1)}, bf16[2,192,128]{2,1,0:T(8,128)(2,1)S(1)}, u32[]{:S(2)}, u32[]{:S(2)}) %collective-permute-start.4) | collective-permute-done | bytes 98336 | tf_op jit(solution)/shard_map/ppermute | solution.py:141
  23.7 2.7 %collective-permute-start.9 = (bf16[192,128]{1,0:T(8,128)(2,1)S(1)}, bf16[192,128]{1,0:T(8,128)(2,1)S(1)}, u32[]{:S(2)}, u32[]{:S(2)}) collective-permute-start(bf16[192,128]{1,0:T(8,128)(2,1)S(1)} %fusion.11), channel_id=1, source_target_pairs={{0,16},{16,0},{1,17},{17,1},{2,18},{18,2},{3,19},{19,3},{4,20},{20... | collective-permute-start | bytes 147464 | tf_op jit(solution)/shard_map/ppermute | solution.py:131
  27.1 1.7 %collective-permute-done.9 = bf16[192,128]{1,0:T(8,128)(2,1)S(1)} collective-permute-done((bf16[192,128]{1,0:T(8,128)(2,1)S(1)}, bf16[192,128]{1,0:T(8,128)(2,1)S(1)}, u32[]{:S(2)}, u32[]{:S(2)}) %collective-permute-start.9) | collective-permute-done | bytes 49184 | tf_op jit(solution)/shard_map/ppermute | solution.py:131
  28.9 2.7 %collective-permute-start.10 = (bf16[192,128]{1,0:T(8,128)(2,1)S(1)}, bf16[192,128]{1,0:T(8,128)(2,1)S(1)}, u32[]{:S(2)}, u32[]{:S(2)}) collective-permute-start(bf16[192,128]{1,0:T(8,128)(2,1)S(1)} %get-tuple-element.65), channel_id=1, source_target_pairs={{0,16},{16,0},{1,17},{17,1},{2,18},{18,2},{3,19},{19,3},{4,20},{20... | collective-permute-start | bytes 147464 | tf_op jit(solution)/shard_map/ppermute | solution.py:131
  31.6 2.4 %collective-permute-done.10 = bf16[192,128]{1,0:T(8,128)(2,1)S(1)} collective-permute-done((bf16[192,128]{1,0:T(8,128)(2,1)S(1)}, bf16[192,128]{1,0:T(8,128)(2,1)S(1)}, u32[]{:S(2)}, u32[]{:S(2)}) %collective-permute-start.10) | collective-permute-done | bytes 49184 | tf_op jit(solution)/shard_map/ppermute | solution.py:131
  34.1 2.1 %collective-permute-start.15 = (bf16[2,192,128]{2,1,0:T(8,128)(2,1)S(1)}, bf16[2,192,128]{2,1,0:T(8,128)(2,1)S(1)}, u32[]{:S(2)}, u32[]{:S(2)}) collective-permute-start(bf16[2,192,128]{2,1,0:T(8,128)(2,1)S(1)} %pad_maximum_fusion), channel_id=1, source_target_pairs={{0,13},{1,12},{2,15},{3,14},{4,9},{5,8},{6,11},{7,10},{8,5},{9,4},... | collective-permute-start | bytes 294920 | tf_op jit(solution)/shard_map/ppermute | solution.py:141
  36.1 1.2 %collective-permute-start.13 = (f32[192,128]{1,0:T(8,128)S(1)}, f32[192,128]{1,0:T(8,128)S(1)}, u32[]{:S(2)}, u32[]{:S(2)}) collective-permute-start(f32[192,128]{1,0:T(8,128)S(1)} %get-tuple-element.47), channel_id=1, source_target_pairs={{0,1},{1,0},{2,3},{3,2},{4,5},{5,4},{6,7},{7,6},{8,9},{9,8},{10,11... | collective-permute-start | bytes 294920 | tf_op jit(solution)/shard_map/ppermute | solution.py:131
  37.4 1.5 %collective-permute-start.12 = (bf16[2,2,192,128]{3,2,1,0:T(8,128)(2,1)S(1)}, bf16[2,2,192,128]{3,2,1,0:T(8,128)(2,1)S(1)}, u32[]{:S(2)}, u32[]{:S(2)}) collective-permute-start(bf16[2,2,192,128]{3,2,1,0:T(8,128)(2,1)S(1)} %maximum_select_fusion), channel_id=1, source_target_pairs={{0,4},{1,5},{2,11},{3,10},{4,0},{5,1},{6,15},{7,14},{8,12},{9,13},... | collective-permute-start | bytes 589832 | tf_op jit(solution)/shard_map/ppermute | solution.py:141
  39.2 1.0 %collective-permute-start.14 = (bf16[2,2,192,128]{3,2,1,0:T(8,128)(2,1)S(1)}, bf16[2,2,192,128]{3,2,1,0:T(8,128)(2,1)S(1)}, u32[]{:S(2)}, u32[]{:S(2)}) collective-permute-start(bf16[2,2,192,128]{3,2,1,0:T(8,128)(2,1)S(1)} %maximum_select_fusion), channel_id=1, source_target_pairs={{0,1},{1,0},{2,14},{3,15},{4,5},{5,4},{6,10},{7,11},{8,9},{9,8},{1... | collective-permute-start | bytes 589832 | tf_op jit(solution)/shard_map/ppermute | solution.py:141
  40.1 7.2 %collective-permute-done.13 = f32[192,128]{1,0:T(8,128)S(1)} collective-permute-done((f32[192,128]{1,0:T(8,128)S(1)}, f32[192,128]{1,0:T(8,128)S(1)}, u32[]{:S(2)}, u32[]{:S(2)}) %collective-permute-start.13) | collective-permute-done | bytes 98336 | tf_op jit(solution)/shard_map/ppermute | solution.py:131
  47.3 0.9 %multiply_subtract_fusion = (f32[384,128]{1,0:T(8,128)}, f32[384,128]{1,0:T(8,128)}, f32[384,128]{1,0:T(8,128)}) fusion(f32[384,128]{1,0:T(8,128)S(1)} %copy-done, f32[]{:T(128)} %bitcast.18, f32[]{:T(128)} %bitcast.16, f32[192,128]{1,0:T(8,128)S(1)} %get-tuple-element.47, f32[192,128]{1,0:T(8,128)S(1)} %collective-permute-done.13, pred[]{:T(512)S(6)} %eq.7, ...), kind=kLoop, calls=%fused_computation.7 | loop fusion | flops 884736 | bytes 1376265 | tf_op jit(solution)/shard_map/sub | solution.py:32
  48.2 2.5 %shard_map.94 = (bf16[4,256,768]{2,1,0:T(8,128)(2,1)S(1)}, bf16[4,256,768]{2,1,0:T(8,128)(2,1)S(1)}) custom-call(s32[4]{0:T(128)S(1)} %pad_add_fusion.where_ref, bf16[256,6144]{1,0:T(8,128)(2,1)} %acts_ref.2), custom_call_target="tpu_custom_call" | custom-call | tf_op jit(solution)/shard_map/pallas_call | solution.py:241
  52.5 1.2 %shard_map.95.refs_6_ = f32[256,128]{1,0:T(8,128)S(1)} custom-call(s32[4]{0:T(128)S(1)} %pad_add_fusion.where_ref, bf16[4,256,768]{2,1,0:T(8,128)(2,1)S(1)} %get-tuple-element.60.columns_ref, bf16[2,2,192,128]{3,2,1,0:T(8,128)(2,1)S(1)} %collective-permute-done.12.refs_0_, bf16[2,2,192,128]{3,2,1,0:T(8,128)(2,1)S(1)} %collective-permute-done.18.refs_1_, ...), custom_call_target="tpu_custom_call" | custom-call | tf_op jit(solution)/shard_map/pallas_call | solution.py:263
  53.7 1.8 %shard_map.96 = bf16[256,128]{1,0:T(8,128)(2,1)} custom-call(s32[4]{0:T(128)S(1)} %pad_add_fusion.where_ref, bf16[4,256,768]{2,1,0:T(8,128)(2,1)S(1)} %get-tuple-element.57.columns_ref, bf16[2,2,192,128]{3,2,1,0:T(8,128)(2,1)S(1)} %collective-permute-done.14.refs_0_, bf16[2,2,192,128]{3,2,1,0:T(8,128)(2,1)S(1)} %collective-permute-done.16.refs_1_, ...), custom_call_target="tpu_custom_call" | custom-call | tf_op jit(solution)/shard_map/pallas_call | solution.py:263
  (40 shorter events, 3.9 us)
Async XLA Ops:
  5.5 1.9 %collective-permute-start.5 = (bf16[4,2,192,128]{3,2,1,0:T(8,128)(2,1)S(1)}, bf16[4,2,192,128]{3,2,1,0:T(8,128)(2,1)S(1)}, u32[]{:S(2)}, u32[]{:S(2)}) collective-permute-start(bf16[4,2,192,128]{3,2,1,0:T(8,128)(2,1)S(1)} %get-tuple-element.37), channel_id=1, source_target_pairs={{0,2},{2,0},{1,3},{3,1},{4,6},{6,4},{5,7},{7,5},{8,10},{10,8},{9,1... | collective-permute-start | bytes 1179656 | tf_op jit(solution)/shard_map/ppermute | solution.py:131
  6.0 7.0 %collective-permute-start = (bf16[4,2,192,128]{3,2,1,0:T(8,128)(2,1)S(1)}, bf16[4,2,192,128]{3,2,1,0:T(8,128)(2,1)S(1)}, u32[]{:S(2)}, u32[]{:S(2)}) collective-permute-start(bf16[4,2,192,128]{3,2,1,0:T(8,128)(2,1)S(1)} %get-tuple-element.35), channel_id=1, source_target_pairs={{0,2},{2,0},{1,3},{3,1},{4,6},{6,4},{5,7},{7,5},{8,10},{10,8},{9,1... | collective-permute-start | bytes 1179656 | tf_op jit(solution)/shard_map/ppermute | solution.py:131
  7.5 10.1 %collective-permute-start.6 = (bf16[2,192,128]{2,1,0:T(8,128)(2,1)S(1)}, bf16[2,192,128]{2,1,0:T(8,128)(2,1)S(1)}, u32[]{:S(2)}, u32[]{:S(2)}) collective-permute-start(bf16[2,192,128]{2,1,0:T(8,128)(2,1)S(1)} %get-tuple-element.71), channel_id=1, source_target_pairs={{0,1},{1,0},{2,14},{3,15},{4,5},{5,4},{6,10},{7,11},{8,9},{9,8},{1... | collective-permute-start | bytes 294920 | tf_op jit(solution)/shard_map/ppermute | solution.py:141
  10.5 7.6 %collective-permute-start.7 = (bf16[2,192,128]{2,1,0:T(8,128)(2,1)S(1)}, bf16[2,192,128]{2,1,0:T(8,128)(2,1)S(1)}, u32[]{:S(2)}, u32[]{:S(2)}) collective-permute-start(bf16[2,192,128]{2,1,0:T(8,128)(2,1)S(1)} %get-tuple-element.70), channel_id=1, source_target_pairs={{0,12},{1,13},{2,3},{3,2},{4,8},{5,9},{6,7},{7,6},{8,4},{9,5},{10,... | collective-permute-start | bytes 294920 | tf_op jit(solution)/shard_map/ppermute | solution.py:141
  13.0 7.7 %collective-permute-start.8 = (bf16[2,192,128]{2,1,0:T(8,128)(2,1)S(1)}, bf16[2,192,128]{2,1,0:T(8,128)(2,1)S(1)}, u32[]{:S(2)}, u32[]{:S(2)}) collective-permute-start(bf16[2,192,128]{2,1,0:T(8,128)(2,1)S(1)} %get-tuple-element.69), channel_id=1, source_target_pairs={{0,13},{1,12},{2,15},{3,14},{4,9},{5,8},{6,11},{7,10},{8,5},{9,4},... | collective-permute-start | bytes 294920 | tf_op jit(solution)/shard_map/ppermute | solution.py:141
  13.2 34.2 %copy-start = (f32[384,128]{1,0:T(8,128)S(1)}, f32[384,128]{1,0:T(8,128)}, u32[]{:S(2)}) copy-start(f32[384,128]{1,0:T(8,128)} %refs_0_.1) | copy-start | bytes 589828
  13.2 34.1 %copy-start.1 = (f32[384,128]{1,0:T(8,128)S(1)}, f32[384,128]{1,0:T(8,128)}, u32[]{:S(2)}) copy-start(f32[384,128]{1,0:T(8,128)} %refs_1_.1) | copy-start | bytes 589828
  13.2 34.1 %copy-start.2 = (f32[384,128]{1,0:T(8,128)S(1)}, f32[384,128]{1,0:T(8,128)}, u32[]{:S(2)}) copy-start(f32[384,128]{1,0:T(8,128)} %refs_2_.1) | copy-start | bytes 589828
  13.2 7.5 %collective-permute-start.1 = (bf16[2,192,128]{2,1,0:T(8,128)(2,1)S(1)}, bf16[2,192,128]{2,1,0:T(8,128)(2,1)S(1)}, u32[]{:S(2)}, u32[]{:S(2)}) collective-permute-start(bf16[2,192,128]{2,1,0:T(8,128)(2,1)S(1)} %get-tuple-element.75), channel_id=1, source_target_pairs={{0,4},{1,5},{2,11},{3,10},{4,0},{5,1},{6,15},{7,14},{8,12},{9,13},... | collective-permute-start | bytes 294920 | tf_op jit(solution)/shard_map/ppermute | solution.py:141
  15.1 6.1 %collective-permute-start.2 = (bf16[2,192,128]{2,1,0:T(8,128)(2,1)S(1)}, bf16[2,192,128]{2,1,0:T(8,128)(2,1)S(1)}, u32[]{:S(2)}, u32[]{:S(2)}) collective-permute-start(bf16[2,192,128]{2,1,0:T(8,128)(2,1)S(1)} %get-tuple-element.74), channel_id=1, source_target_pairs={{0,9},{1,8},{2,6},{3,7},{4,13},{5,12},{6,2},{7,3},{8,1},{9,0},{10,... | collective-permute-start | bytes 294920 | tf_op jit(solution)/shard_map/ppermute | solution.py:141
  17.6 4.7 %collective-permute-start.3 = (bf16[2,192,128]{2,1,0:T(8,128)(2,1)S(1)}, bf16[2,192,128]{2,1,0:T(8,128)(2,1)S(1)}, u32[]{:S(2)}, u32[]{:S(2)}) collective-permute-start(bf16[2,192,128]{2,1,0:T(8,128)(2,1)S(1)} %get-tuple-element.73), channel_id=1, source_target_pairs={{0,8},{1,9},{2,7},{3,6},{4,12},{5,13},{6,3},{7,2},{8,0},{9,1},{10,... | collective-permute-start | bytes 294920 | tf_op jit(solution)/shard_map/ppermute | solution.py:141
  18.1 5.5 %collective-permute-start.4 = (bf16[2,192,128]{2,1,0:T(8,128)(2,1)S(1)}, bf16[2,192,128]{2,1,0:T(8,128)(2,1)S(1)}, u32[]{:S(2)}, u32[]{:S(2)}) collective-permute-start(bf16[2,192,128]{2,1,0:T(8,128)(2,1)S(1)} %get-tuple-element.72), channel_id=1, source_target_pairs={{0,5},{1,4},{2,10},{3,11},{4,1},{5,0},{6,14},{7,15},{8,13},{9,12},... | collective-permute-start | bytes 294920 | tf_op jit(solution)/shard_map/ppermute | solution.py:141
  23.7 5.1 %collective-permute-start.9 = (bf16[192,128]{1,0:T(8,128)(2,1)S(1)}, bf16[192,128]{1,0:T(8,128)(2,1)S(1)}, u32[]{:S(2)}, u32[]{:S(2)}) collective-permute-start(bf16[192,128]{1,0:T(8,128)(2,1)S(1)} %fusion.11), channel_id=1, source_target_pairs={{0,16},{16,0},{1,17},{17,1},{2,18},{18,2},{3,19},{19,3},{4,20},{20... | collective-permute-start | bytes 147464 | tf_op jit(solution)/shard_map/ppermute | solution.py:131
  28.9 5.1 %collective-permute-start.10 = (bf16[192,128]{1,0:T(8,128)(2,1)S(1)}, bf16[192,128]{1,0:T(8,128)(2,1)S(1)}, u32[]{:S(2)}, u32[]{:S(2)}) collective-permute-start(bf16[192,128]{1,0:T(8,128)(2,1)S(1)} %get-tuple-element.65), channel_id=1, source_target_pairs={{0,16},{16,0},{1,17},{17,1},{2,18},{18,2},{3,19},{19,3},{4,20},{20... | collective-permute-start | bytes 147464 | tf_op jit(solution)/shard_map/ppermute | solution.py:131
  34.0 3.4 %collective-permute-start.11 = (bf16[2,192,128]{2,1,0:T(8,128)(2,1)S(1)}, bf16[2,192,128]{2,1,0:T(8,128)(2,1)S(1)}, u32[]{:S(2)}, u32[]{:S(2)}) collective-permute-start(bf16[2,192,128]{2,1,0:T(8,128)(2,1)S(1)} %pad_maximum_fusion), channel_id=1, source_target_pairs={{0,2},{2,0},{1,3},{3,1},{4,6},{6,4},{5,7},{7,5},{8,10},{10,8},{9,1... | collective-permute-start | bytes 294920 | tf_op jit(solution)/shard_map/ppermute | solution.py:131
  34.1 17.2 %collective-permute-start.15 = (bf16[2,192,128]{2,1,0:T(8,128)(2,1)S(1)}, bf16[2,192,128]{2,1,0:T(8,128)(2,1)S(1)}, u32[]{:S(2)}, u32[]{:S(2)}) collective-permute-start(bf16[2,192,128]{2,1,0:T(8,128)(2,1)S(1)} %pad_maximum_fusion), channel_id=1, source_target_pairs={{0,13},{1,12},{2,15},{3,14},{4,9},{5,8},{6,11},{7,10},{8,5},{9,4},... | collective-permute-start | bytes 294920 | tf_op jit(solution)/shard_map/ppermute | solution.py:141
  36.1 11.2 %collective-permute-start.13 = (f32[192,128]{1,0:T(8,128)S(1)}, f32[192,128]{1,0:T(8,128)S(1)}, u32[]{:S(2)}, u32[]{:S(2)}) collective-permute-start(f32[192,128]{1,0:T(8,128)S(1)} %get-tuple-element.47), channel_id=1, source_target_pairs={{0,1},{1,0},{2,3},{3,2},{4,5},{5,4},{6,7},{7,6},{8,9},{9,8},{10,11... | collective-permute-start | bytes 294920 | tf_op jit(solution)/shard_map/ppermute | solution.py:131
  37.4 13.3 %collective-permute-start.12 = (bf16[2,2,192,128]{3,2,1,0:T(8,128)(2,1)S(1)}, bf16[2,2,192,128]{3,2,1,0:T(8,128)(2,1)S(1)}, u32[]{:S(2)}, u32[]{:S(2)}) collective-permute-start(bf16[2,2,192,128]{3,2,1,0:T(8,128)(2,1)S(1)} %maximum_select_fusion), channel_id=1, source_target_pairs={{0,4},{1,5},{2,11},{3,10},{4,0},{5,1},{6,15},{7,14},{8,12},{9,13},... | collective-permute-start | bytes 589832 | tf_op jit(solution)/shard_map/ppermute | solution.py:141
  38.8 11.9 %collective-permute-start.19 = (bf16[2,2,192,128]{3,2,1,0:T(8,128)(2,1)S(1)}, bf16[2,2,192,128]{3,2,1,0:T(8,128)(2,1)S(1)}, u32[]{:S(2)}, u32[]{:S(2)}) collective-permute-start(bf16[2,2,192,128]{3,2,1,0:T(8,128)(2,1)S(1)} %maximum_select_fusion), channel_id=1, source_target_pairs={{0,8},{1,9},{2,7},{3,6},{4,12},{5,13},{6,3},{7,2},{8,0},{9,1},{10,... | collective-permute-start | bytes 589832 | tf_op jit(solution)/shard_map/ppermute | solution.py:141
  39.2 12.1 %collective-permute-start.14 = (bf16[2,2,192,128]{3,2,1,0:T(8,128)(2,1)S(1)}, bf16[2,2,192,128]{3,2,1,0:T(8,128)(2,1)S(1)}, u32[]{:S(2)}, u32[]{:S(2)}) collective-permute-start(bf16[2,2,192,128]{3,2,1,0:T(8,128)(2,1)S(1)} %maximum_select_fusion), channel_id=1, source_target_pairs={{0,1},{1,0},{2,14},{3,15},{4,5},{5,4},{6,10},{7,11},{8,9},{9,8},{1... | collective-permute-start | bytes 589832 | tf_op jit(solution)/shard_map/ppermute | solution.py:141
  50.7 1.5 %collective-permute-start.18 = (bf16[2,2,192,128]{3,2,1,0:T(8,128)(2,1)S(1)}, bf16[2,2,192,128]{3,2,1,0:T(8,128)(2,1)S(1)}, u32[]{:S(2)}, u32[]{:S(2)}) collective-permute-start(bf16[2,2,192,128]{3,2,1,0:T(8,128)(2,1)S(1)} %collective-permute-done.12.refs_0_), channel_id=1, source_target_pairs={{0,2},{2,0},{1,3},{3,1},{4,6},{6,4},{5,7},{7,5},{8,10},{10,8},{9,1... | collective-permute-start | bytes 589832 | tf_op jit(solution)/shard_map/ppermute | solution.py:131
  50.8 1.7 %collective-permute-start.20 = (bf16[2,2,192,128]{3,2,1,0:T(8,128)(2,1)S(1)}, bf16[2,2,192,128]{3,2,1,0:T(8,128)(2,1)S(1)}, u32[]{:S(2)}, u32[]{:S(2)}) collective-permute-start(bf16[2,2,192,128]{3,2,1,0:T(8,128)(2,1)S(1)} %collective-permute-done.19.refs_2_), channel_id=1, source_target_pairs={{0,2},{2,0},{1,3},{3,1},{4,6},{6,4},{5,7},{7,5},{8,10},{10,8},{9,1... | collective-permute-start | bytes 589832 | tf_op jit(solution)/shard_map/ppermute | solution.py:131
  51.3 2.4 %collective-permute-start.16 = (bf16[2,2,192,128]{3,2,1,0:T(8,128)(2,1)S(1)}, bf16[2,2,192,128]{3,2,1,0:T(8,128)(2,1)S(1)}, u32[]{:S(2)}, u32[]{:S(2)}) collective-permute-start(bf16[2,2,192,128]{3,2,1,0:T(8,128)(2,1)S(1)} %collective-permute-done.14.refs_0_), channel_id=1, source_target_pairs={{0,2},{2,0},{1,3},{3,1},{4,6},{6,4},{5,7},{7,5},{8,10},{10,8},{9,1... | collective-permute-start | bytes 589832 | tf_op jit(solution)/shard_map/ppermute | solution.py:131
  51.4 2.3 %collective-permute-start.17 = (bf16[2,192,128]{2,1,0:T(8,128)(2,1)S(1)}, bf16[2,192,128]{2,1,0:T(8,128)(2,1)S(1)}, u32[]{:S(2)}, u32[]{:S(2)}) collective-permute-start(bf16[2,192,128]{2,1,0:T(8,128)(2,1)S(1)} %collective-permute-done.15), channel_id=1, source_target_pairs={{0,2},{2,0},{1,3},{3,1},{4,6},{6,4},{5,7},{7,5},{8,10},{10,8},{9,1... | collective-permute-start | bytes 294920 | tf_op jit(solution)/shard_map/ppermute | solution.py:131

commit v13 on v12

--- a/solution.py
+++ b/solution.py
@@ -112,12 +112,15 @@
 
 def places(group, core, rep):
     pieces = []
-    for chip in NEXT[:2] if group == 0 else NEXT[2:]:
-        for by in (core, 1 - core):
+    for by in (core, 1 - core):
+        blocks = []
+        for chip in NEXT[:2] if group == 0 else NEXT[2:]:
             place = LOWS[group].index(chip[0]) ^ by
-            pieces.append([(place, owner, rep ^ chip[1] ^ by) for owner in range(2)])
+            blocks += [(place, owner, rep ^ chip[1] ^ by) for owner in range(2)]
+        if group == 1:
+            blocks.append((1, by, rep ^ 1))
+        pieces.append(blocks)
     if group == 1:
-        pieces += [[(1, owner, rep ^ 1)] for owner in (core, 1 - core)]
         pieces += [[(0, owner, rep)] for owner in (core, 1 - core)]
     return pieces
 
@@ -221,10 +224,10 @@
         weight = adamw(grad, *mine, step_count)[0].astype(bf16)
 
         column = jnp.stack([swap(weight, "high", j) if j else weight for j in range(n_high)])
-        column, grad = lax.optimization_barrier((column, grad))
         other = swap(grad, "rep")
         corner = to_corner(column)
         across = swap(column, "core")
+        across, other = lax.optimization_barrier((across, other))
         chip = jnp.where(core == 0, jnp.stack([column, across]), jnp.stack([across, column]))
         got = [to_next(chip, slot) for slot in range(3)]
 
@@ -247,11 +250,9 @@
                 compiler_params=params,
             )(where, pltpu.with_memory_space_constraint(late_acts, pltpu.HBM))
         got[0], state, columns = lax.optimization_barrier((got[0], state, columns))
-        got[2], corner = lax.optimization_barrier((got[2], corner))
-        over = [swap(x, "core") for x in got]
-        corner_over = swap(corner, "core")
-        first = [x[slot] for slot in range(2) for x in (got, over)]
-        second = [got[2], over[2], corner[None], corner_over[None], column[None], across[None]]
+        first, second = jnp.concatenate(got[:2]), jnp.concatenate([got[2], corner[None]])
+        first, second = [first, swap(first, "core")], [second, swap(second, "core")]
+        second += [column[None], across[None]]
         pieces = (first, second)
         logits = None
         for group, (received, acts_columns) in enumerate(zip(pieces, columns)):

time: 55.6 us -> 51 us (0.917)
  waiting for transfers between devices: 17.7 us -> 12.9 us
    ppermute x10 -> x8, waiting for transfers between devices: 13.2 us -> 4.69 us  [swap(): lax.ppermute(x, axis, [(i, i ^ mask) for i in range(fine.shape[axis])])]
    ppermute x11, waiting for transfers between devices: 4.58 us -> 8.21 us  [cube_swap(): return lax.ppermute(x, AXES[1:], pairs)]
    ppermute x11, starting transfers between devices: 16.2 us -> 16.9 us  [cube_swap(): return lax.ppermute(x, AXES[1:], pairs)]
    ppermute x10 -> x8, starting transfers between devices: 8.28 us -> 7.74 us  [swap(): lax.ppermute(x, axis, [(i, i ^ mask) for i in range(fine.shape[axis])])]
  transfers between devices with their start and end apart: 21 -> 19, of which waited for: 10 -> 11; matrix products, arithmetic and copies ran while one was open for 2% -> 3% of each run, Pallas kernels for 7% -> 7%
where the time goes in v13:
time: 51 us; the launch traced here: 50.9 us
  starting transfers between devices  24.6 us (48%)
  waiting for transfers between devices  12.9 us (25%)
  Pallas kernels  10.2 us (20%)
  between operations  1.54 us (3%)
  other arithmetic  1.46 us (3%)
    ppermute x11, starting transfers between devices, cube_swap(): return lax.ppermute(x, AXES[1:], pairs)  16.9 us
    ppermute x11, waiting for transfers between devices, cube_swap(): return lax.ppermute(x, AXES[1:], pairs)  8.21 us
    ppermute x8, starting transfers between devices, swap(): lax.ppermute(x, axis, [(i, i ^ mask) for i in range(fine.shape[axis])])  7.74 us
    pallas_call x1, Pallas kernels, per_device(): pl.pallas_call(functools.partial(grad_kernel, n_high), out_shape=[shape]...  4.8 us
    ppermute x8, waiting for transfers between devices, swap(): lax.ppermute(x, axis, [(i, i ^ mask) for i in range(fine.shape[axis])])  4.69 us
    pallas_call x2, Pallas kernels, per_device(): pl.pallas_call(functools.partial(logits_kernel, n_high, group), out_shape...  2.95 us
    pallas_call x1, Pallas kernels, per_device(): pl.pallas_call(functools.partial(columns_kernel, n_high), out_shape=(pltp...  2.46 us
  transfers between devices with their start and end apart: 19, of which 11 were waited for; matrix products, arithmetic and copies ran while one was open for 3% of the time, Pallas kernels for 7%

profile of v13, /device:TPU:0, one launch (start us, length us, event | category | flops | bytes accessed | tf_op | source)
XLA Modules:
  0.0 50.9 jit_solution(6744983086335819939)
XLA Ops:
  0.7 4.8 %shard_map.93 = (bf16[4,2,192,128]{3,2,1,0:T(8,128)(2,1)S(1)}, bf16[4,2,192,128]{3,2,1,0:T(8,128)(2,1)S(1)}, bf16[4,2,192,128]{3,2,1,0:T(8,128)(2,1)S(1)}, bf16[...) custom-call(s32[4]{0:T(128)S(1)} %pad_add_fusion.where_ref, bf16[256,6144]{1,0:T(8,128)(2,1)} %acts_ref.2, ...), custom_call_target="tpu_custom_call" | custom-call | tf_op jit(solution)/shard_map/pallas_call | solution.py:174
  6.1 1.3 %collective-permute-done.5 = bf16[4,2,192,128]{3,2,1,0:T(8,128)(2,1)S(1)} collective-permute-done((bf16[4,2,192,128]{3,2,1,0:T(8,128)(2,1)S(1)}, bf16[4,2,192,128]{3,2,1,0:T(8,128)(2,1)S(1)}, u32[]{:S(2)}, u32[]{:S(2)}) %collective-permute-start.5) | collective-permute-done | bytes 393248 | tf_op jit(solution)/shard_map/ppermute | solution.py:134
  7.5 3.0 %collective-permute-start.6 = (bf16[2,192,128]{2,1,0:T(8,128)(2,1)S(1)}, bf16[2,192,128]{2,1,0:T(8,128)(2,1)S(1)}, u32[]{:S(2)}, u32[]{:S(2)}) collective-permute-start(bf16[2,192,128]{2,1,0:T(8,128)(2,1)S(1)} %get-tuple-element.67), channel_id=1, source_target_pairs={{0,1},{1,0},{2,14},{3,15},{4,5},{5,4},{6,10},{7,11},{8,9},{9,8},{1... | collective-permute-start | bytes 294920 | tf_op jit(solution)/shard_map/ppermute | solution.py:144
  10.5 2.5 %collective-permute-start.7 = (bf16[2,192,128]{2,1,0:T(8,128)(2,1)S(1)}, bf16[2,192,128]{2,1,0:T(8,128)(2,1)S(1)}, u32[]{:S(2)}, u32[]{:S(2)}) collective-permute-start(bf16[2,192,128]{2,1,0:T(8,128)(2,1)S(1)} %get-tuple-element.66), channel_id=1, source_target_pairs={{0,12},{1,13},{2,3},{3,2},{4,8},{5,9},{6,7},{7,6},{8,4},{9,5},{10,... | collective-permute-start | bytes 294920 | tf_op jit(solution)/shard_map/ppermute | solution.py:144
  13.2 1.9 %collective-permute-start.1 = (bf16[2,192,128]{2,1,0:T(8,128)(2,1)S(1)}, bf16[2,192,128]{2,1,0:T(8,128)(2,1)S(1)}, u32[]{:S(2)}, u32[]{:S(2)}) collective-permute-start(bf16[2,192,128]{2,1,0:T(8,128)(2,1)S(1)} %get-tuple-element.71), channel_id=1, source_target_pairs={{0,4},{1,5},{2,11},{3,10},{4,0},{5,1},{6,15},{7,14},{8,12},{9,13},... | collective-permute-start | bytes 294920 | tf_op jit(solution)/shard_map/ppermute | solution.py:144
  15.1 2.5 %collective-permute-start.2 = (bf16[2,192,128]{2,1,0:T(8,128)(2,1)S(1)}, bf16[2,192,128]{2,1,0:T(8,128)(2,1)S(1)}, u32[]{:S(2)}, u32[]{:S(2)}) collective-permute-start(bf16[2,192,128]{2,1,0:T(8,128)(2,1)S(1)} %get-tuple-element.70), channel_id=1, source_target_pairs={{0,9},{1,8},{2,6},{3,7},{4,13},{5,12},{6,2},{7,3},{8,1},{9,0},{10,... | collective-permute-start | bytes 294920 | tf_op jit(solution)/shard_map/ppermute | solution.py:144
  18.1 0.9 %collective-permute-start.4 = (bf16[2,192,128]{2,1,0:T(8,128)(2,1)S(1)}, bf16[2,192,128]{2,1,0:T(8,128)(2,1)S(1)}, u32[]{:S(2)}, u32[]{:S(2)}) collective-permute-start(bf16[2,192,128]{2,1,0:T(8,128)(2,1)S(1)} %get-tuple-element.68), channel_id=1, source_target_pairs={{0,5},{1,4},{2,10},{3,11},{4,1},{5,0},{6,14},{7,15},{8,13},{9,12},... | collective-permute-start | bytes 294920 | tf_op jit(solution)/shard_map/ppermute | solution.py:144
  19.1 1.6 %collective-permute-done.8 = bf16[2,192,128]{2,1,0:T(8,128)(2,1)S(1)} collective-permute-done((bf16[2,192,128]{2,1,0:T(8,128)(2,1)S(1)}, bf16[2,192,128]{2,1,0:T(8,128)(2,1)S(1)}, u32[]{:S(2)}, u32[]{:S(2)}) %collective-permute-start.8) | collective-permute-done | bytes 98336 | tf_op jit(solution)/shard_map/ppermute | solution.py:144
  21.2 1.1 %collective-permute-done.3 = bf16[2,192,128]{2,1,0:T(8,128)(2,1)S(1)} collective-permute-done((bf16[2,192,128]{2,1,0:T(8,128)(2,1)S(1)}, bf16[2,192,128]{2,1,0:T(8,128)(2,1)S(1)}, u32[]{:S(2)}, u32[]{:S(2)}) %collective-permute-start.3) | collective-permute-done | bytes 98336 | tf_op jit(solution)/shard_map/ppermute | solution.py:144
  22.4 1.3 %collective-permute-done.4 = bf16[2,192,128]{2,1,0:T(8,128)(2,1)S(1)} collective-permute-done((bf16[2,192,128]{2,1,0:T(8,128)(2,1)S(1)}, bf16[2,192,128]{2,1,0:T(8,128)(2,1)S(1)}, u32[]{:S(2)}, u32[]{:S(2)}) %collective-permute-start.4) | collective-permute-done | bytes 98336 | tf_op jit(solution)/shard_map/ppermute | solution.py:144
  23.7 2.7 %collective-permute-start.9 = (bf16[192,128]{1,0:T(8,128)(2,1)S(1)}, bf16[192,128]{1,0:T(8,128)(2,1)S(1)}, u32[]{:S(2)}, u32[]{:S(2)}) collective-permute-start(bf16[192,128]{1,0:T(8,128)(2,1)S(1)} %fusion.11), channel_id=1, source_target_pairs={{0,16},{16,0},{1,17},{17,1},{2,18},{18,2},{3,19},{19,3},{4,20},{20... | collective-permute-start | bytes 147464 | tf_op jit(solution)/shard_map/ppermute | solution.py:134
  27.1 1.7 %collective-permute-done.9 = bf16[192,128]{1,0:T(8,128)(2,1)S(1)} collective-permute-done((bf16[192,128]{1,0:T(8,128)(2,1)S(1)}, bf16[192,128]{1,0:T(8,128)(2,1)S(1)}, u32[]{:S(2)}, u32[]{:S(2)}) %collective-permute-start.9) | collective-permute-done | bytes 49184 | tf_op jit(solution)/shard_map/ppermute | solution.py:134
  28.9 2.7 %collective-permute-start.10 = (bf16[192,128]{1,0:T(8,128)(2,1)S(1)}, bf16[192,128]{1,0:T(8,128)(2,1)S(1)}, u32[]{:S(2)}, u32[]{:S(2)}) collective-permute-start(bf16[192,128]{1,0:T(8,128)(2,1)S(1)} %get-tuple-element.61), channel_id=1, source_target_pairs={{0,16},{16,0},{1,17},{17,1},{2,18},{18,2},{3,19},{19,3},{4,20},{20... | collective-permute-start | bytes 147464 | tf_op jit(solution)/shard_map/ppermute | solution.py:134
  31.6 1.1 %collective-permute-start.12 = (f32[192,128]{1,0:T(8,128)S(1)}, f32[192,128]{1,0:T(8,128)S(1)}, u32[]{:S(2)}, u32[]{:S(2)}) collective-permute-start(f32[192,128]{1,0:T(8,128)S(1)} %get-tuple-element.62), channel_id=1, source_target_pairs={{0,1},{1,0},{2,3},{3,2},{4,5},{5,4},{6,7},{7,6},{8,9},{9,8},{10,11... | collective-permute-start | bytes 294920 | tf_op jit(solution)/shard_map/ppermute | solution.py:134
  32.7 1.3 %collective-permute-done.10 = bf16[192,128]{1,0:T(8,128)(2,1)S(1)} collective-permute-done((bf16[192,128]{1,0:T(8,128)(2,1)S(1)}, bf16[192,128]{1,0:T(8,128)(2,1)S(1)}, u32[]{:S(2)}, u32[]{:S(2)}) %collective-permute-start.10) | collective-permute-done | bytes 49184 | tf_op jit(solution)/shard_map/ppermute | solution.py:134
  34.1 2.1 %collective-permute-start.15 = (bf16[2,192,128]{2,1,0:T(8,128)(2,1)S(1)}, bf16[2,192,128]{2,1,0:T(8,128)(2,1)S(1)}, u32[]{:S(2)}, u32[]{:S(2)}) collective-permute-start(bf16[2,192,128]{2,1,0:T(8,128)(2,1)S(1)} %get-tuple-element.73), channel_id=1, source_target_pairs={{0,13},{1,12},{2,15},{3,14},{4,9},{5,8},{6,11},{7,10},{8,5},{9,4},... | collective-permute-start | bytes 294920 | tf_op jit(solution)/shard_map/ppermute | solution.py:144
  36.2 1.3 %collective-permute-start.13 = (bf16[2,2,192,128]{3,2,1,0:T(8,128)(2,1)S(1)}, bf16[2,2,192,128]{3,2,1,0:T(8,128)(2,1)S(1)}, u32[]{:S(2)}, u32[]{:S(2)}) collective-permute-start(bf16[2,2,192,128]{3,2,1,0:T(8,128)(2,1)S(1)} %maximum_select_fusion), channel_id=1, source_target_pairs={{0,4},{1,5},{2,11},{3,10},{4,0},{5,1},{6,15},{7,14},{8,12},{9,13},... | collective-permute-start | bytes 589832 | tf_op jit(solution)/shard_map/ppermute | solution.py:144
  37.5 1.4 %collective-permute-start.17 = (bf16[2,2,192,128]{3,2,1,0:T(8,128)(2,1)S(1)}, bf16[2,2,192,128]{3,2,1,0:T(8,128)(2,1)S(1)}, u32[]{:S(2)}, u32[]{:S(2)}) collective-permute-start(bf16[2,2,192,128]{3,2,1,0:T(8,128)(2,1)S(1)} %maximum_select_fusion), channel_id=1, source_target_pairs={{0,8},{1,9},{2,7},{3,6},{4,12},{5,13},{6,3},{7,2},{8,0},{9,1},{10,... | collective-permute-start | bytes 589832 | tf_op jit(solution)/shard_map/ppermute | solution.py:144
  39.7 0.9 %multiply_subtract_fusion = (f32[384,128]{1,0:T(8,128)}, f32[384,128]{1,0:T(8,128)}, f32[384,128]{1,0:T(8,128)}) fusion(f32[384,128]{1,0:T(8,128)S(1)} %copy-done, f32[]{:T(128)} %bitcast.18, f32[]{:T(128)} %bitcast.16, f32[192,128]{1,0:T(8,128)S(1)} %get-tuple-element.62, f32[192,128]{1,0:T(8,128)S(1)} %collective-permute-done.12, pred[]{:T(512)S(6)} %eq.7, ...), kind=kLoop, calls=%fused_computation.8 | loop fusion | flops 884736 | bytes 1376265 | tf_op jit(solution)/shard_map/sub | solution.py:32
  40.6 2.5 %shard_map.94 = (bf16[4,256,768]{2,1,0:T(8,128)(2,1)S(1)}, bf16[4,256,768]{2,1,0:T(8,128)(2,1)S(1)}) custom-call(s32[4]{0:T(128)S(1)} %pad_add_fusion.where_ref, bf16[256,6144]{1,0:T(8,128)(2,1)} %acts_ref.2), custom_call_target="tpu_custom_call" | custom-call | tf_op jit(solution)/shard_map/pallas_call | solution.py:244
  43.1 2.3 %collective-permute-done.13 = bf16[2,2,192,128]{3,2,1,0:T(8,128)(2,1)S(1)} collective-permute-done((bf16[2,2,192,128]{3,2,1,0:T(8,128)(2,1)S(1)}, bf16[2,2,192,128]{3,2,1,0:T(8,128)(2,1)S(1)}, u32[]{:S(2)}, u32[]{:S(2)}) %collective-permute-start.13) | collective-permute-done | bytes 196640 | tf_op jit(solution)/shard_map/ppermute | solution.py:144
  46.1 1.3 %collective-permute-done.14 = bf16[2,2,192,128]{3,2,1,0:T(8,128)(2,1)S(1)} collective-permute-done((bf16[2,2,192,128]{3,2,1,0:T(8,128)(2,1)S(1)}, bf16[2,2,192,128]{3,2,1,0:T(8,128)(2,1)S(1)}, u32[]{:S(2)}, u32[]{:S(2)}) %collective-permute-start.14) | collective-permute-done | bytes 196640 | tf_op jit(solution)/shard_map/ppermute | solution.py:144
  47.5 1.2 %shard_map.95.refs_4_ = f32[256,128]{1,0:T(8,128)S(1)} custom-call(s32[4]{0:T(128)S(1)} %pad_add_fusion.where_ref, bf16[4,256,768]{2,1,0:T(8,128)(2,1)S(1)} %get-tuple-element.56.columns_ref, bf16[4,2,192,128]{3,2,1,0:T(8,128)(2,1)S(1)} %constant_dynamic-update-slice_fusion.refs_0_, bf16[4,2,192,128]{3,2,1,0:T(8,128)(2,1)S(1)} %collective-permute-done.18.refs_1_), custom_call_target="tpu_custom_call" | custom-call | tf_op jit(solution)/shard_map/pallas_call | solution.py:264
  49.1 1.8 %shard_map.96 = bf16[256,128]{1,0:T(8,128)(2,1)} custom-call(s32[4]{0:T(128)S(1)} %pad_add_fusion.where_ref, bf16[4,256,768]{2,1,0:T(8,128)(2,1)S(1)} %get-tuple-element.55.columns_ref, bf16[3,2,192,128]{3,2,1,0:T(8,128)(2,1)S(1)} %pad_maximum_fusion.refs_0_, bf16[3,2,192,128]{3,2,1,0:T(8,128)(2,1)S(1)} %collective-permute-done.16.refs_1_, ...), custom_call_target="tpu_custom_call" | custom-call | tf_op jit(solution)/shard_map/pallas_call | solution.py:264
  (39 shorter events, 4.4 us)
Async XLA Ops:
  5.5 1.9 %collective-permute-start.5 = (bf16[4,2,192,128]{3,2,1,0:T(8,128)(2,1)S(1)}, bf16[4,2,192,128]{3,2,1,0:T(8,128)(2,1)S(1)}, u32[]{:S(2)}, u32[]{:S(2)}) collective-permute-start(bf16[4,2,192,128]{3,2,1,0:T(8,128)(2,1)S(1)} %get-tuple-element.35), channel_id=1, source_target_pairs={{0,2},{2,0},{1,3},{3,1},{4,6},{6,4},{5,7},{7,5},{8,10},{10,8},{9,1... | collective-permute-start | bytes 1179656 | tf_op jit(solution)/shard_map/ppermute | solution.py:134
  6.0 7.0 %collective-permute-start = (bf16[4,2,192,128]{3,2,1,0:T(8,128)(2,1)S(1)}, bf16[4,2,192,128]{3,2,1,0:T(8,128)(2,1)S(1)}, u32[]{:S(2)}, u32[]{:S(2)}) collective-permute-start(bf16[4,2,192,128]{3,2,1,0:T(8,128)(2,1)S(1)} %get-tuple-element.33), channel_id=1, source_target_pairs={{0,2},{2,0},{1,3},{3,1},{4,6},{6,4},{5,7},{7,5},{8,10},{10,8},{9,1... | collective-permute-start | bytes 1179656 | tf_op jit(solution)/shard_map/ppermute | solution.py:134
  7.5 10.1 %collective-permute-start.6 = (bf16[2,192,128]{2,1,0:T(8,128)(2,1)S(1)}, bf16[2,192,128]{2,1,0:T(8,128)(2,1)S(1)}, u32[]{:S(2)}, u32[]{:S(2)}) collective-permute-start(bf16[2,192,128]{2,1,0:T(8,128)(2,1)S(1)} %get-tuple-element.67), channel_id=1, source_target_pairs={{0,1},{1,0},{2,14},{3,15},{4,5},{5,4},{6,10},{7,11},{8,9},{9,8},{1... | collective-permute-start | bytes 294920 | tf_op jit(solution)/shard_map/ppermute | solution.py:144
  10.5 7.6 %collective-permute-start.7 = (bf16[2,192,128]{2,1,0:T(8,128)(2,1)S(1)}, bf16[2,192,128]{2,1,0:T(8,128)(2,1)S(1)}, u32[]{:S(2)}, u32[]{:S(2)}) collective-permute-start(bf16[2,192,128]{2,1,0:T(8,128)(2,1)S(1)} %get-tuple-element.66), channel_id=1, source_target_pairs={{0,12},{1,13},{2,3},{3,2},{4,8},{5,9},{6,7},{7,6},{8,4},{9,5},{10,... | collective-permute-start | bytes 294920 | tf_op jit(solution)/shard_map/ppermute | solution.py:144
  13.0 7.7 %collective-permute-start.8 = (bf16[2,192,128]{2,1,0:T(8,128)(2,1)S(1)}, bf16[2,192,128]{2,1,0:T(8,128)(2,1)S(1)}, u32[]{:S(2)}, u32[]{:S(2)}) collective-permute-start(bf16[2,192,128]{2,1,0:T(8,128)(2,1)S(1)} %get-tuple-element.65), channel_id=1, source_target_pairs={{0,13},{1,12},{2,15},{3,14},{4,9},{5,8},{6,11},{7,10},{8,5},{9,4},... | collective-permute-start | bytes 294920 | tf_op jit(solution)/shard_map/ppermute | solution.py:144
  13.2 26.6 %copy-start = (f32[384,128]{1,0:T(8,128)S(1)}, f32[384,128]{1,0:T(8,128)}, u32[]{:S(2)}) copy-start(f32[384,128]{1,0:T(8,128)} %refs_0_.1) | copy-start | bytes 589828
  13.2 26.6 %copy-start.1 = (f32[384,128]{1,0:T(8,128)S(1)}, f32[384,128]{1,0:T(8,128)}, u32[]{:S(2)}) copy-start(f32[384,128]{1,0:T(8,128)} %refs_1_.1) | copy-start | bytes 589828
  13.2 26.6 %copy-start.2 = (f32[384,128]{1,0:T(8,128)S(1)}, f32[384,128]{1,0:T(8,128)}, u32[]{:S(2)}) copy-start(f32[384,128]{1,0:T(8,128)} %refs_2_.1) | copy-start | bytes 589828
  13.2 7.5 %collective-permute-start.1 = (bf16[2,192,128]{2,1,0:T(8,128)(2,1)S(1)}, bf16[2,192,128]{2,1,0:T(8,128)(2,1)S(1)}, u32[]{:S(2)}, u32[]{:S(2)}) collective-permute-start(bf16[2,192,128]{2,1,0:T(8,128)(2,1)S(1)} %get-tuple-element.71), channel_id=1, source_target_pairs={{0,4},{1,5},{2,11},{3,10},{4,0},{5,1},{6,15},{7,14},{8,12},{9,13},... | collective-permute-start | bytes 294920 | tf_op jit(solution)/shard_map/ppermute | solution.py:144
  15.1 6.1 %collective-permute-start.2 = (bf16[2,192,128]{2,1,0:T(8,128)(2,1)S(1)}, bf16[2,192,128]{2,1,0:T(8,128)(2,1)S(1)}, u32[]{:S(2)}, u32[]{:S(2)}) collective-permute-start(bf16[2,192,128]{2,1,0:T(8,128)(2,1)S(1)} %get-tuple-element.70), channel_id=1, source_target_pairs={{0,9},{1,8},{2,6},{3,7},{4,13},{5,12},{6,2},{7,3},{8,1},{9,0},{10,... | collective-permute-start | bytes 294920 | tf_op jit(solution)/shard_map/ppermute | solution.py:144
  17.6 4.7 %collective-permute-start.3 = (bf16[2,192,128]{2,1,0:T(8,128)(2,1)S(1)}, bf16[2,192,128]{2,1,0:T(8,128)(2,1)S(1)}, u32[]{:S(2)}, u32[]{:S(2)}) collective-permute-start(bf16[2,192,128]{2,1,0:T(8,128)(2,1)S(1)} %get-tuple-element.69), channel_id=1, source_target_pairs={{0,8},{1,9},{2,7},{3,6},{4,12},{5,13},{6,3},{7,2},{8,0},{9,1},{10,... | collective-permute-start | bytes 294920 | tf_op jit(solution)/shard_map/ppermute | solution.py:144
  18.1 5.5 %collective-permute-start.4 = (bf16[2,192,128]{2,1,0:T(8,128)(2,1)S(1)}, bf16[2,192,128]{2,1,0:T(8,128)(2,1)S(1)}, u32[]{:S(2)}, u32[]{:S(2)}) collective-permute-start(bf16[2,192,128]{2,1,0:T(8,128)(2,1)S(1)} %get-tuple-element.68), channel_id=1, source_target_pairs={{0,5},{1,4},{2,10},{3,11},{4,1},{5,0},{6,14},{7,15},{8,13},{9,12},... | collective-permute-start | bytes 294920 | tf_op jit(solution)/shard_map/ppermute | solution.py:144
  23.7 5.1 %collective-permute-start.9 = (bf16[192,128]{1,0:T(8,128)(2,1)S(1)}, bf16[192,128]{1,0:T(8,128)(2,1)S(1)}, u32[]{:S(2)}, u32[]{:S(2)}) collective-permute-start(bf16[192,128]{1,0:T(8,128)(2,1)S(1)} %fusion.11), channel_id=1, source_target_pairs={{0,16},{16,0},{1,17},{17,1},{2,18},{18,2},{3,19},{19,3},{4,20},{20... | collective-permute-start | bytes 147464 | tf_op jit(solution)/shard_map/ppermute | solution.py:134
  28.9 5.1 %collective-permute-start.10 = (bf16[192,128]{1,0:T(8,128)(2,1)S(1)}, bf16[192,128]{1,0:T(8,128)(2,1)S(1)}, u32[]{:S(2)}, u32[]{:S(2)}) collective-permute-start(bf16[192,128]{1,0:T(8,128)(2,1)S(1)} %get-tuple-element.61), channel_id=1, source_target_pairs={{0,16},{16,0},{1,17},{17,1},{2,18},{18,2},{3,19},{19,3},{4,20},{20... | collective-permute-start | bytes 147464 | tf_op jit(solution)/shard_map/ppermute | solution.py:134
  31.6 4.6 %collective-permute-start.12 = (f32[192,128]{1,0:T(8,128)S(1)}, f32[192,128]{1,0:T(8,128)S(1)}, u32[]{:S(2)}, u32[]{:S(2)}) collective-permute-start(f32[192,128]{1,0:T(8,128)S(1)} %get-tuple-element.62), channel_id=1, source_target_pairs={{0,1},{1,0},{2,3},{3,2},{4,5},{5,4},{6,7},{7,6},{8,9},{9,8},{10,11... | collective-permute-start | bytes 294920 | tf_op jit(solution)/shard_map/ppermute | solution.py:134
  34.0 2.2 %collective-permute-start.11 = (bf16[2,192,128]{2,1,0:T(8,128)(2,1)S(1)}, bf16[2,192,128]{2,1,0:T(8,128)(2,1)S(1)}, u32[]{:S(2)}, u32[]{:S(2)}) collective-permute-start(bf16[2,192,128]{2,1,0:T(8,128)(2,1)S(1)} %get-tuple-element.73), channel_id=1, source_target_pairs={{0,2},{2,0},{1,3},{3,1},{4,6},{6,4},{5,7},{7,5},{8,10},{10,8},{9,1... | collective-permute-start | bytes 294920 | tf_op jit(solution)/shard_map/ppermute | solution.py:134
  34.1 12.0 %collective-permute-start.15 = (bf16[2,192,128]{2,1,0:T(8,128)(2,1)S(1)}, bf16[2,192,128]{2,1,0:T(8,128)(2,1)S(1)}, u32[]{:S(2)}, u32[]{:S(2)}) collective-permute-start(bf16[2,192,128]{2,1,0:T(8,128)(2,1)S(1)} %get-tuple-element.73), channel_id=1, source_target_pairs={{0,13},{1,12},{2,15},{3,14},{4,9},{5,8},{6,11},{7,10},{8,5},{9,4},... | collective-permute-start | bytes 294920 | tf_op jit(solution)/shard_map/ppermute | solution.py:144
  36.2 9.2 %collective-permute-start.13 = (bf16[2,2,192,128]{3,2,1,0:T(8,128)(2,1)S(1)}, bf16[2,2,192,128]{3,2,1,0:T(8,128)(2,1)S(1)}, u32[]{:S(2)}, u32[]{:S(2)}) collective-permute-start(bf16[2,2,192,128]{3,2,1,0:T(8,128)(2,1)S(1)} %maximum_select_fusion), channel_id=1, source_target_pairs={{0,4},{1,5},{2,11},{3,10},{4,0},{5,1},{6,15},{7,14},{8,12},{9,13},... | collective-permute-start | bytes 589832 | tf_op jit(solution)/shard_map/ppermute | solution.py:144
  37.5 7.9 %collective-permute-start.17 = (bf16[2,2,192,128]{3,2,1,0:T(8,128)(2,1)S(1)}, bf16[2,2,192,128]{3,2,1,0:T(8,128)(2,1)S(1)}, u32[]{:S(2)}, u32[]{:S(2)}) collective-permute-start(bf16[2,2,192,128]{3,2,1,0:T(8,128)(2,1)S(1)} %maximum_select_fusion), channel_id=1, source_target_pairs={{0,8},{1,9},{2,7},{3,6},{4,12},{5,13},{6,3},{7,2},{8,0},{9,1},{10,... | collective-permute-start | bytes 589832 | tf_op jit(solution)/shard_map/ppermute | solution.py:144
  38.9 8.5 %collective-permute-start.14 = (bf16[2,2,192,128]{3,2,1,0:T(8,128)(2,1)S(1)}, bf16[2,2,192,128]{3,2,1,0:T(8,128)(2,1)S(1)}, u32[]{:S(2)}, u32[]{:S(2)}) collective-permute-start(bf16[2,2,192,128]{3,2,1,0:T(8,128)(2,1)S(1)} %maximum_select_fusion), channel_id=1, source_target_pairs={{0,1},{1,0},{2,14},{3,15},{4,5},{5,4},{6,10},{7,11},{8,9},{9,8},{1... | collective-permute-start | bytes 589832 | tf_op jit(solution)/shard_map/ppermute | solution.py:144
  45.5 2.0 %collective-permute-start.18 = (bf16[4,2,192,128]{3,2,1,0:T(8,128)(2,1)S(1)}, bf16[4,2,192,128]{3,2,1,0:T(8,128)(2,1)S(1)}, u32[]{:S(2)}, u32[]{:S(2)}) collective-permute-start(bf16[4,2,192,128]{3,2,1,0:T(8,128)(2,1)S(1)} %constant_dynamic-update-slice_fusion.refs_0_), channel_id=1, source_target_pairs={{0,2},{2,0},{1,3},{3,1},{4,6},{6,4},{5,7},{7,5},{8,10},{10,8},{9,1... | collective-permute-start | bytes 1179656 | tf_op jit(solution)/shard_map/ppermute | solution.py:134
  47.4 1.6 %collective-permute-start.16 = (bf16[3,2,192,128]{3,2,1,0:T(8,128)(2,1)S(1)}, bf16[3,2,192,128]{3,2,1,0:T(8,128)(2,1)S(1)}, u32[]{:S(2)}, u32[]{:S(2)}) collective-permute-start(bf16[3,2,192,128]{3,2,1,0:T(8,128)(2,1)S(1)} %pad_maximum_fusion.refs_0_), channel_id=1, source_target_pairs={{0,2},{2,0},{1,3},{3,1},{4,6},{6,4},{5,7},{7,5},{8,10},{10,8},{9,1... | collective-permute-start | bytes 884744 | tf_op jit(solution)/shard_map/ppermute | solution.py:134

commit v14 on v13

--- a/solution.py
+++ b/solution.py
@@ -65,12 +65,11 @@
     for copy in state:
         copy.start()
     loads.wait()
+    turned = logit_grads[...].T
     for n, copy in enumerate(copies):
         copy.wait()
-        product = lax.dot_general(
-            columns[n], logit_grads[...], (((0,), (0,)), ((), ())), preferred_element_type=jnp.float32
-        )
-        blocks[...] = product.astype(blocks.dtype).reshape(blocks.shape)
+        product = jnp.dot(turned, columns[n], preferred_element_type=jnp.float32)
+        blocks[...] = product.astype(blocks.dtype).T.reshape(blocks.shape)
         p, j = divmod(n, n_high)
         for d_rep in range(2):
             for outs, owner in ((kept, core), (away, 1 - core)):
@@ -225,9 +224,9 @@
 
         column = jnp.stack([swap(weight, "high", j) if j else weight for j in range(n_high)])
         other = swap(grad, "rep")
-        corner = to_corner(column)
         across = swap(column, "core")
-        across, other = lax.optimization_barrier((across, other))
+        across, other, corner = lax.optimization_barrier((across, other, column))
+        corner = to_corner(corner)
         chip = jnp.where(core == 0, jnp.stack([column, across]), jnp.stack([across, column]))
         got = [to_next(chip, slot) for slot in range(3)]
 

time: 51 us -> 52.5 us (1.029)
  waiting for transfers between devices: 12.9 us -> 15.2 us
  Pallas kernels: 10.2 us -> 9.48 us
    ppermute x8, waiting for transfers between devices: 4.69 us -> 6.77 us  [swap(): lax.ppermute(x, axis, [(i, i ^ mask) for i in range(fine.shape[axis])])]
    pallas_call x1, Pallas kernels: 4.8 us -> 4.08 us  [per_device(): pl.pallas_call(functools.partial(grad_kernel, n_high), out_shape=[shape]...]
  transfers between devices with their start and end apart: 19 -> 19, of which waited for: 11 -> 11; matrix products, arithmetic and copies ran while one was open for 3% -> 2% of each run, Pallas kernels for 7% -> 7%
where the time goes in v14:
time: 52.5 us; the launch traced here: 52.3 us
  starting transfers between devices  24.6 us (47%)
  waiting for transfers between devices  15.2 us (29%)
  Pallas kernels  9.48 us (18%)
  between operations  1.55 us (3%)
  other arithmetic  1.46 us (3%)
    ppermute x11, starting transfers between devices, cube_swap(): return lax.ppermute(x, AXES[1:], pairs)  16.4 us
    ppermute x11, waiting for transfers between devices, cube_swap(): return lax.ppermute(x, AXES[1:], pairs)  8.4 us
    ppermute x8, starting transfers between devices, swap(): lax.ppermute(x, axis, [(i, i ^ mask) for i in range(fine.shape[axis])])  8.16 us
    ppermute x8, waiting for transfers between devices, swap(): lax.ppermute(x, axis, [(i, i ^ mask) for i in range(fine.shape[axis])])  6.77 us
    pallas_call x1, Pallas kernels, per_device(): pl.pallas_call(functools.partial(grad_kernel, n_high), out_shape=[shape]...  4.08 us
    pallas_call x2, Pallas kernels, per_device(): pl.pallas_call(functools.partial(logits_kernel, n_high, group), out_shape...  2.95 us
    pallas_call x1, Pallas kernels, per_device(): pl.pallas_call(functools.partial(columns_kernel, n_high), out_shape=(pltp...  2.46 us
  transfers between devices with their start and end apart: 19, of which 11 were waited for; matrix products, arithmetic and copies ran while one was open for 2% of the time, Pallas kernels for 7%

profile of v14, /device:TPU:0, one launch (start us, length us, event | category | flops | bytes accessed | tf_op | source)
XLA Modules:
  0.0 52.3 jit_solution(7665344593970498354)
XLA Ops:
  0.7 4.1 %shard_map.93 = (bf16[4,2,192,128]{3,2,1,0:T(8,128)(2,1)S(1)}, bf16[4,2,192,128]{3,2,1,0:T(8,128)(2,1)S(1)}, bf16[4,2,192,128]{3,2,1,0:T(8,128)(2,1)S(1)}, bf16[...) custom-call(s32[4]{0:T(128)S(1)} %pad_add_fusion.where_ref, bf16[256,6144]{1,0:T(8,128)(2,1)} %acts_ref.2, ...), custom_call_target="tpu_custom_call" | custom-call | tf_op jit(solution)/shard_map/pallas_call | solution.py:173
  5.4 1.3 %collective-permute-done.5 = bf16[4,2,192,128]{3,2,1,0:T(8,128)(2,1)S(1)} collective-permute-done((bf16[4,2,192,128]{3,2,1,0:T(8,128)(2,1)S(1)}, bf16[4,2,192,128]{3,2,1,0:T(8,128)(2,1)S(1)}, u32[]{:S(2)}, u32[]{:S(2)}) %collective-permute-start.5) | collective-permute-done | bytes 393248 | tf_op jit(solution)/shard_map/ppermute | solution.py:133
  6.8 3.0 %collective-permute-start.6 = (bf16[2,192,128]{2,1,0:T(8,128)(2,1)S(1)}, bf16[2,192,128]{2,1,0:T(8,128)(2,1)S(1)}, u32[]{:S(2)}, u32[]{:S(2)}) collective-permute-start(bf16[2,192,128]{2,1,0:T(8,128)(2,1)S(1)} %get-tuple-element.69), channel_id=1, source_target_pairs={{0,1},{1,0},{2,14},{3,15},{4,5},{5,4},{6,10},{7,11},{8,9},{9,8},{1... | collective-permute-start | bytes 294920 | tf_op jit(solution)/shard_map/ppermute | solution.py:143
  9.8 2.5 %collective-permute-start.7 = (bf16[2,192,128]{2,1,0:T(8,128)(2,1)S(1)}, bf16[2,192,128]{2,1,0:T(8,128)(2,1)S(1)}, u32[]{:S(2)}, u32[]{:S(2)}) collective-permute-start(bf16[2,192,128]{2,1,0:T(8,128)(2,1)S(1)} %get-tuple-element.68), channel_id=1, source_target_pairs={{0,12},{1,13},{2,3},{3,2},{4,8},{5,9},{6,7},{7,6},{8,4},{9,5},{10,... | collective-permute-start | bytes 294920 | tf_op jit(solution)/shard_map/ppermute | solution.py:143
  12.5 1.9 %collective-permute-start.1 = (bf16[2,192,128]{2,1,0:T(8,128)(2,1)S(1)}, bf16[2,192,128]{2,1,0:T(8,128)(2,1)S(1)}, u32[]{:S(2)}, u32[]{:S(2)}) collective-permute-start(bf16[2,192,128]{2,1,0:T(8,128)(2,1)S(1)} %get-tuple-element.73), channel_id=1, source_target_pairs={{0,4},{1,5},{2,11},{3,10},{4,0},{5,1},{6,15},{7,14},{8,12},{9,13},... | collective-permute-start | bytes 294920 | tf_op jit(solution)/shard_map/ppermute | solution.py:143
  14.4 2.5 %collective-permute-start.2 = (bf16[2,192,128]{2,1,0:T(8,128)(2,1)S(1)}, bf16[2,192,128]{2,1,0:T(8,128)(2,1)S(1)}, u32[]{:S(2)}, u32[]{:S(2)}) collective-permute-start(bf16[2,192,128]{2,1,0:T(8,128)(2,1)S(1)} %get-tuple-element.72), channel_id=1, source_target_pairs={{0,9},{1,8},{2,6},{3,7},{4,13},{5,12},{6,2},{7,3},{8,1},{9,0},{10,... | collective-permute-start | bytes 294920 | tf_op jit(solution)/shard_map/ppermute | solution.py:143
  17.4 0.9 %collective-permute-start.4 = (bf16[2,192,128]{2,1,0:T(8,128)(2,1)S(1)}, bf16[2,192,128]{2,1,0:T(8,128)(2,1)S(1)}, u32[]{:S(2)}, u32[]{:S(2)}) collective-permute-start(bf16[2,192,128]{2,1,0:T(8,128)(2,1)S(1)} %get-tuple-element.70), channel_id=1, source_target_pairs={{0,5},{1,4},{2,10},{3,11},{4,1},{5,0},{6,14},{7,15},{8,13},{9,12},... | collective-permute-start | bytes 294920 | tf_op jit(solution)/shard_map/ppermute | solution.py:143
  18.3 1.7 %collective-permute-done.8 = bf16[2,192,128]{2,1,0:T(8,128)(2,1)S(1)} collective-permute-done((bf16[2,192,128]{2,1,0:T(8,128)(2,1)S(1)}, bf16[2,192,128]{2,1,0:T(8,128)(2,1)S(1)}, u32[]{:S(2)}, u32[]{:S(2)}) %collective-permute-start.8) | collective-permute-done | bytes 98336 | tf_op jit(solution)/shard_map/ppermute | solution.py:143
  20.5 1.1 %collective-permute-done.3 = bf16[2,192,128]{2,1,0:T(8,128)(2,1)S(1)} collective-permute-done((bf16[2,192,128]{2,1,0:T(8,128)(2,1)S(1)}, bf16[2,192,128]{2,1,0:T(8,128)(2,1)S(1)}, u32[]{:S(2)}, u32[]{:S(2)}) %collective-permute-start.3) | collective-permute-done | bytes 98336 | tf_op jit(solution)/shard_map/ppermute | solution.py:143
  21.7 1.3 %collective-permute-done.4 = bf16[2,192,128]{2,1,0:T(8,128)(2,1)S(1)} collective-permute-done((bf16[2,192,128]{2,1,0:T(8,128)(2,1)S(1)}, bf16[2,192,128]{2,1,0:T(8,128)(2,1)S(1)}, u32[]{:S(2)}, u32[]{:S(2)}) %collective-permute-start.4) | collective-permute-done | bytes 98336 | tf_op jit(solution)/shard_map/ppermute | solution.py:143
  23.0 2.7 %collective-permute-start.9 = (bf16[192,128]{1,0:T(8,128)(2,1)S(1)}, bf16[192,128]{1,0:T(8,128)(2,1)S(1)}, u32[]{:S(2)}, u32[]{:S(2)}) collective-permute-start(bf16[192,128]{1,0:T(8,128)(2,1)S(1)} %fusion.11), channel_id=1, source_target_pairs={{0,16},{16,0},{1,17},{17,1},{2,18},{18,2},{3,19},{19,3},{4,20},{20... | collective-permute-start | bytes 147464 | tf_op jit(solution)/shard_map/ppermute | solution.py:133
  26.4 1.7 %collective-permute-done.9 = bf16[192,128]{1,0:T(8,128)(2,1)S(1)} collective-permute-done((bf16[192,128]{1,0:T(8,128)(2,1)S(1)}, bf16[192,128]{1,0:T(8,128)(2,1)S(1)}, u32[]{:S(2)}, u32[]{:S(2)}) %collective-permute-start.9) | collective-permute-done | bytes 49184 | tf_op jit(solution)/shard_map/ppermute | solution.py:133
  28.2 2.7 %collective-permute-start.10 = (bf16[192,128]{1,0:T(8,128)(2,1)S(1)}, bf16[192,128]{1,0:T(8,128)(2,1)S(1)}, u32[]{:S(2)}, u32[]{:S(2)}) collective-permute-start(bf16[192,128]{1,0:T(8,128)(2,1)S(1)} %get-tuple-element.63), channel_id=1, source_target_pairs={{0,16},{16,0},{1,17},{17,1},{2,18},{18,2},{3,19},{19,3},{4,20},{20... | collective-permute-start | bytes 147464 | tf_op jit(solution)/shard_map/ppermute | solution.py:133
  30.9 1.1 %collective-permute-start.12 = (f32[192,128]{1,0:T(8,128)S(1)}, f32[192,128]{1,0:T(8,128)S(1)}, u32[]{:S(2)}, u32[]{:S(2)}) collective-permute-start(f32[192,128]{1,0:T(8,128)S(1)} %get-tuple-element.64), channel_id=1, source_target_pairs={{0,1},{1,0},{2,3},{3,2},{4,5},{5,4},{6,7},{7,6},{8,9},{9,8},{10,11... | collective-permute-start | bytes 294920 | tf_op jit(solution)/shard_map/ppermute | solution.py:133
  32.0 1.3 %collective-permute-done.10 = bf16[192,128]{1,0:T(8,128)(2,1)S(1)} collective-permute-done((bf16[192,128]{1,0:T(8,128)(2,1)S(1)}, bf16[192,128]{1,0:T(8,128)(2,1)S(1)}, u32[]{:S(2)}, u32[]{:S(2)}) %collective-permute-start.10) | collective-permute-done | bytes 49184 | tf_op jit(solution)/shard_map/ppermute | solution.py:133
  33.3 2.2 %collective-permute-done.12 = f32[192,128]{1,0:T(8,128)S(1)} collective-permute-done((f32[192,128]{1,0:T(8,128)S(1)}, f32[192,128]{1,0:T(8,128)S(1)}, u32[]{:S(2)}, u32[]{:S(2)}) %collective-permute-start.12) | collective-permute-done | bytes 98336 | tf_op jit(solution)/shard_map/ppermute | solution.py:133
  36.4 1.8 %collective-permute-start.17 = (bf16[2,2,192,128]{3,2,1,0:T(8,128)(2,1)S(1)}, bf16[2,2,192,128]{3,2,1,0:T(8,128)(2,1)S(1)}, u32[]{:S(2)}, u32[]{:S(2)}) collective-permute-start(bf16[2,2,192,128]{3,2,1,0:T(8,128)(2,1)S(1)} %maximum_select_fusion), channel_id=1, source_target_pairs={{0,8},{1,9},{2,7},{3,6},{4,12},{5,13},{6,3},{7,2},{8,0},{9,1},{10,... | collective-permute-start | bytes 589832 | tf_op jit(solution)/shard_map/ppermute | solution.py:143
  39.0 0.9 %multiply_subtract_fusion = (f32[384,128]{1,0:T(8,128)}, f32[384,128]{1,0:T(8,128)}, f32[384,128]{1,0:T(8,128)}) fusion(f32[384,128]{1,0:T(8,128)S(1)} %copy-done, f32[]{:T(128)} %bitcast.18, f32[]{:T(128)} %bitcast.16, f32[192,128]{1,0:T(8,128)S(1)} %get-tuple-element.64, f32[192,128]{1,0:T(8,128)S(1)} %collective-permute-done.12, pred[]{:T(512)S(6)} %eq.7, ...), kind=kLoop, calls=%fused_computation.8 | loop fusion | flops 884736 | bytes 1376265 | tf_op jit(solution)/shard_map/sub | solution.py:32
  39.9 2.5 %shard_map.94 = (bf16[4,256,768]{2,1,0:T(8,128)(2,1)S(1)}, bf16[4,256,768]{2,1,0:T(8,128)(2,1)S(1)}) custom-call(s32[4]{0:T(128)S(1)} %pad_add_fusion.where_ref, bf16[256,6144]{1,0:T(8,128)(2,1)} %acts_ref.2), custom_call_target="tpu_custom_call" | custom-call | tf_op jit(solution)/shard_map/pallas_call | solution.py:243
  42.4 1.6 %collective-permute-start.15 = (bf16[2,192,128]{2,1,0:T(8,128)(2,1)S(1)}, bf16[2,192,128]{2,1,0:T(8,128)(2,1)S(1)}, u32[]{:S(2)}, u32[]{:S(2)}) collective-permute-start(bf16[2,192,128]{2,1,0:T(8,128)(2,1)S(1)} %get-tuple-element.57), channel_id=1, source_target_pairs={{0,13},{1,12},{2,15},{3,14},{4,9},{5,8},{6,11},{7,10},{8,5},{9,4},... | collective-permute-start | bytes 294920 | tf_op jit(solution)/shard_map/ppermute | solution.py:143
  44.9 1.0 %collective-permute-start.18 = (bf16[4,2,192,128]{3,2,1,0:T(8,128)(2,1)S(1)}, bf16[4,2,192,128]{3,2,1,0:T(8,128)(2,1)S(1)}, u32[]{:S(2)}, u32[]{:S(2)}) collective-permute-start(bf16[4,2,192,128]{3,2,1,0:T(8,128)(2,1)S(1)} %constant_dynamic-update-slice_fusion.refs_0_), channel_id=1, source_target_pairs={{0,2},{2,0},{1,3},{3,1},{4,6},{6,4},{5,7},{7,5},{8,10},{10,8},{9,1... | collective-permute-start | bytes 1179656 | tf_op jit(solution)/shard_map/ppermute | solution.py:133
  45.9 3.0 %collective-permute-done.15 = bf16[2,192,128]{2,1,0:T(8,128)(2,1)S(1)} collective-permute-done((bf16[2,192,128]{2,1,0:T(8,128)(2,1)S(1)}, bf16[2,192,128]{2,1,0:T(8,128)(2,1)S(1)}, u32[]{:S(2)}, u32[]{:S(2)}) %collective-permute-start.15) | collective-permute-done | bytes 98336 | tf_op jit(solution)/shard_map/ppermute | solution.py:143
  49.0 1.2 %shard_map.95.refs_4_ = f32[256,128]{1,0:T(8,128)S(1)} custom-call(s32[4]{0:T(128)S(1)} %pad_add_fusion.where_ref, bf16[4,256,768]{2,1,0:T(8,128)(2,1)S(1)} %get-tuple-element.58.columns_ref, bf16[4,2,192,128]{3,2,1,0:T(8,128)(2,1)S(1)} %constant_dynamic-update-slice_fusion.refs_0_, bf16[4,2,192,128]{3,2,1,0:T(8,128)(2,1)S(1)} %collective-permute-done.18.refs_1_), custom_call_target="tpu_custom_call" | custom-call | tf_op jit(solution)/shard_map/pallas_call | solution.py:263
  50.6 1.8 %shard_map.96 = bf16[256,128]{1,0:T(8,128)(2,1)} custom-call(s32[4]{0:T(128)S(1)} %pad_add_fusion.where_ref, bf16[4,256,768]{2,1,0:T(8,128)(2,1)S(1)} %get-tuple-element.56.columns_ref, bf16[3,2,192,128]{3,2,1,0:T(8,128)(2,1)S(1)} %pad_maximum_fusion.refs_0_, bf16[3,2,192,128]{3,2,1,0:T(8,128)(2,1)S(1)} %collective-permute-done.16.refs_1_, ...), custom_call_target="tpu_custom_call" | custom-call | tf_op jit(solution)/shard_map/pallas_call | solution.py:263
  (39 shorter events, 5.4 us)
Async XLA Ops:
  4.8 1.9 %collective-permute-start.5 = (bf16[4,2,192,128]{3,2,1,0:T(8,128)(2,1)S(1)}, bf16[4,2,192,128]{3,2,1,0:T(8,128)(2,1)S(1)}, u32[]{:S(2)}, u32[]{:S(2)}) collective-permute-start(bf16[4,2,192,128]{3,2,1,0:T(8,128)(2,1)S(1)} %get-tuple-element.36), channel_id=1, source_target_pairs={{0,2},{2,0},{1,3},{3,1},{4,6},{6,4},{5,7},{7,5},{8,10},{10,8},{9,1... | collective-permute-start | bytes 1179656 | tf_op jit(solution)/shard_map/ppermute | solution.py:133
  5.3 7.0 %collective-permute-start = (bf16[4,2,192,128]{3,2,1,0:T(8,128)(2,1)S(1)}, bf16[4,2,192,128]{3,2,1,0:T(8,128)(2,1)S(1)}, u32[]{:S(2)}, u32[]{:S(2)}) collective-permute-start(bf16[4,2,192,128]{3,2,1,0:T(8,128)(2,1)S(1)} %get-tuple-element.34), channel_id=1, source_target_pairs={{0,2},{2,0},{1,3},{3,1},{4,6},{6,4},{5,7},{7,5},{8,10},{10,8},{9,1... | collective-permute-start | bytes 1179656 | tf_op jit(solution)/shard_map/ppermute | solution.py:133
  6.8 10.1 %collective-permute-start.6 = (bf16[2,192,128]{2,1,0:T(8,128)(2,1)S(1)}, bf16[2,192,128]{2,1,0:T(8,128)(2,1)S(1)}, u32[]{:S(2)}, u32[]{:S(2)}) collective-permute-start(bf16[2,192,128]{2,1,0:T(8,128)(2,1)S(1)} %get-tuple-element.69), channel_id=1, source_target_pairs={{0,1},{1,0},{2,14},{3,15},{4,5},{5,4},{6,10},{7,11},{8,9},{9,8},{1... | collective-permute-start | bytes 294920 | tf_op jit(solution)/shard_map/ppermute | solution.py:143
  9.8 7.6 %collective-permute-start.7 = (bf16[2,192,128]{2,1,0:T(8,128)(2,1)S(1)}, bf16[2,192,128]{2,1,0:T(8,128)(2,1)S(1)}, u32[]{:S(2)}, u32[]{:S(2)}) collective-permute-start(bf16[2,192,128]{2,1,0:T(8,128)(2,1)S(1)} %get-tuple-element.68), channel_id=1, source_target_pairs={{0,12},{1,13},{2,3},{3,2},{4,8},{5,9},{6,7},{7,6},{8,4},{9,5},{10,... | collective-permute-start | bytes 294920 | tf_op jit(solution)/shard_map/ppermute | solution.py:143
  12.3 7.7 %collective-permute-start.8 = (bf16[2,192,128]{2,1,0:T(8,128)(2,1)S(1)}, bf16[2,192,128]{2,1,0:T(8,128)(2,1)S(1)}, u32[]{:S(2)}, u32[]{:S(2)}) collective-permute-start(bf16[2,192,128]{2,1,0:T(8,128)(2,1)S(1)} %get-tuple-element.67), channel_id=1, source_target_pairs={{0,13},{1,12},{2,15},{3,14},{4,9},{5,8},{6,11},{7,10},{8,5},{9,4},... | collective-permute-start | bytes 294920 | tf_op jit(solution)/shard_map/ppermute | solution.py:143
  12.4 26.6 %copy-start = (f32[384,128]{1,0:T(8,128)S(1)}, f32[384,128]{1,0:T(8,128)}, u32[]{:S(2)}) copy-start(f32[384,128]{1,0:T(8,128)} %refs_0_.1) | copy-start | bytes 589828
  12.5 26.6 %copy-start.1 = (f32[384,128]{1,0:T(8,128)S(1)}, f32[384,128]{1,0:T(8,128)}, u32[]{:S(2)}) copy-start(f32[384,128]{1,0:T(8,128)} %refs_1_.1) | copy-start | bytes 589828
  12.5 26.6 %copy-start.2 = (f32[384,128]{1,0:T(8,128)S(1)}, f32[384,128]{1,0:T(8,128)}, u32[]{:S(2)}) copy-start(f32[384,128]{1,0:T(8,128)} %refs_2_.1) | copy-start | bytes 589828
  12.5 7.5 %collective-permute-start.1 = (bf16[2,192,128]{2,1,0:T(8,128)(2,1)S(1)}, bf16[2,192,128]{2,1,0:T(8,128)(2,1)S(1)}, u32[]{:S(2)}, u32[]{:S(2)}) collective-permute-start(bf16[2,192,128]{2,1,0:T(8,128)(2,1)S(1)} %get-tuple-element.73), channel_id=1, source_target_pairs={{0,4},{1,5},{2,11},{3,10},{4,0},{5,1},{6,15},{7,14},{8,12},{9,13},... | collective-permute-start | bytes 294920 | tf_op jit(solution)/shard_map/ppermute | solution.py:143
  14.4 6.1 %collective-permute-start.2 = (bf16[2,192,128]{2,1,0:T(8,128)(2,1)S(1)}, bf16[2,192,128]{2,1,0:T(8,128)(2,1)S(1)}, u32[]{:S(2)}, u32[]{:S(2)}) collective-permute-start(bf16[2,192,128]{2,1,0:T(8,128)(2,1)S(1)} %get-tuple-element.72), channel_id=1, source_target_pairs={{0,9},{1,8},{2,6},{3,7},{4,13},{5,12},{6,2},{7,3},{8,1},{9,0},{10,... | collective-permute-start | bytes 294920 | tf_op jit(solution)/shard_map/ppermute | solution.py:143
  16.9 4.7 %collective-permute-start.3 = (bf16[2,192,128]{2,1,0:T(8,128)(2,1)S(1)}, bf16[2,192,128]{2,1,0:T(8,128)(2,1)S(1)}, u32[]{:S(2)}, u32[]{:S(2)}) collective-permute-start(bf16[2,192,128]{2,1,0:T(8,128)(2,1)S(1)} %get-tuple-element.71), channel_id=1, source_target_pairs={{0,8},{1,9},{2,7},{3,6},{4,12},{5,13},{6,3},{7,2},{8,0},{9,1},{10,... | collective-permute-start | bytes 294920 | tf_op jit(solution)/shard_map/ppermute | solution.py:143
  17.4 5.5 %collective-permute-start.4 = (bf16[2,192,128]{2,1,0:T(8,128)(2,1)S(1)}, bf16[2,192,128]{2,1,0:T(8,128)(2,1)S(1)}, u32[]{:S(2)}, u32[]{:S(2)}) collective-permute-start(bf16[2,192,128]{2,1,0:T(8,128)(2,1)S(1)} %get-tuple-element.70), channel_id=1, source_target_pairs={{0,5},{1,4},{2,10},{3,11},{4,1},{5,0},{6,14},{7,15},{8,13},{9,12},... | collective-permute-start | bytes 294920 | tf_op jit(solution)/shard_map/ppermute | solution.py:143
  23.0 5.1 %collective-permute-start.9 = (bf16[192,128]{1,0:T(8,128)(2,1)S(1)}, bf16[192,128]{1,0:T(8,128)(2,1)S(1)}, u32[]{:S(2)}, u32[]{:S(2)}) collective-permute-start(bf16[192,128]{1,0:T(8,128)(2,1)S(1)} %fusion.11), channel_id=1, source_target_pairs={{0,16},{16,0},{1,17},{17,1},{2,18},{18,2},{3,19},{19,3},{4,20},{20... | collective-permute-start | bytes 147464 | tf_op jit(solution)/shard_map/ppermute | solution.py:133
  28.2 5.1 %collective-permute-start.10 = (bf16[192,128]{1,0:T(8,128)(2,1)S(1)}, bf16[192,128]{1,0:T(8,128)(2,1)S(1)}, u32[]{:S(2)}, u32[]{:S(2)}) collective-permute-start(bf16[192,128]{1,0:T(8,128)(2,1)S(1)} %get-tuple-element.63), channel_id=1, source_target_pairs={{0,16},{16,0},{1,17},{17,1},{2,18},{18,2},{3,19},{19,3},{4,20},{20... | collective-permute-start | bytes 147464 | tf_op jit(solution)/shard_map/ppermute | solution.py:133
  30.9 4.6 %collective-permute-start.12 = (f32[192,128]{1,0:T(8,128)S(1)}, f32[192,128]{1,0:T(8,128)S(1)}, u32[]{:S(2)}, u32[]{:S(2)}) collective-permute-start(f32[192,128]{1,0:T(8,128)S(1)} %get-tuple-element.64), channel_id=1, source_target_pairs={{0,1},{1,0},{2,3},{3,2},{4,5},{5,4},{6,7},{7,6},{8,9},{9,8},{10,11... | collective-permute-start | bytes 294920 | tf_op jit(solution)/shard_map/ppermute | solution.py:133
  33.3 2.2 %collective-permute-start.11 = (bf16[2,192,128]{2,1,0:T(8,128)(2,1)S(1)}, bf16[2,192,128]{2,1,0:T(8,128)(2,1)S(1)}, u32[]{:S(2)}, u32[]{:S(2)}) collective-permute-start(bf16[2,192,128]{2,1,0:T(8,128)(2,1)S(1)} %get-tuple-element.57), channel_id=1, source_target_pairs={{0,2},{2,0},{1,3},{3,1},{4,6},{6,4},{5,7},{7,5},{8,10},{10,8},{9,1... | collective-permute-start | bytes 294920 | tf_op jit(solution)/shard_map/ppermute | solution.py:133
  35.5 9.3 %collective-permute-start.13 = (bf16[2,2,192,128]{3,2,1,0:T(8,128)(2,1)S(1)}, bf16[2,2,192,128]{3,2,1,0:T(8,128)(2,1)S(1)}, u32[]{:S(2)}, u32[]{:S(2)}) collective-permute-start(bf16[2,2,192,128]{3,2,1,0:T(8,128)(2,1)S(1)} %maximum_select_fusion), channel_id=1, source_target_pairs={{0,4},{1,5},{2,11},{3,10},{4,0},{5,1},{6,15},{7,14},{8,12},{9,13},... | collective-permute-start | bytes 589832 | tf_op jit(solution)/shard_map/ppermute | solution.py:143
  36.4 8.5 %collective-permute-start.17 = (bf16[2,2,192,128]{3,2,1,0:T(8,128)(2,1)S(1)}, bf16[2,2,192,128]{3,2,1,0:T(8,128)(2,1)S(1)}, u32[]{:S(2)}, u32[]{:S(2)}) collective-permute-start(bf16[2,2,192,128]{3,2,1,0:T(8,128)(2,1)S(1)} %maximum_select_fusion), channel_id=1, source_target_pairs={{0,8},{1,9},{2,7},{3,6},{4,12},{5,13},{6,3},{7,2},{8,0},{9,1},{10,... | collective-permute-start | bytes 589832 | tf_op jit(solution)/shard_map/ppermute | solution.py:143
  38.2 10.7 %collective-permute-start.14 = (bf16[2,2,192,128]{3,2,1,0:T(8,128)(2,1)S(1)}, bf16[2,2,192,128]{3,2,1,0:T(8,128)(2,1)S(1)}, u32[]{:S(2)}, u32[]{:S(2)}) collective-permute-start(bf16[2,2,192,128]{3,2,1,0:T(8,128)(2,1)S(1)} %maximum_select_fusion), channel_id=1, source_target_pairs={{0,1},{1,0},{2,14},{3,15},{4,5},{5,4},{6,10},{7,11},{8,9},{9,8},{1... | collective-permute-start | bytes 589832 | tf_op jit(solution)/shard_map/ppermute | solution.py:143
  42.4 6.5 %collective-permute-start.15 = (bf16[2,192,128]{2,1,0:T(8,128)(2,1)S(1)}, bf16[2,192,128]{2,1,0:T(8,128)(2,1)S(1)}, u32[]{:S(2)}, u32[]{:S(2)}) collective-permute-start(bf16[2,192,128]{2,1,0:T(8,128)(2,1)S(1)} %get-tuple-element.57), channel_id=1, source_target_pairs={{0,13},{1,12},{2,15},{3,14},{4,9},{5,8},{6,11},{7,10},{8,5},{9,4},... | collective-permute-start | bytes 294920 | tf_op jit(solution)/shard_map/ppermute | solution.py:143
  44.9 4.1 %collective-permute-start.18 = (bf16[4,2,192,128]{3,2,1,0:T(8,128)(2,1)S(1)}, bf16[4,2,192,128]{3,2,1,0:T(8,128)(2,1)S(1)}, u32[]{:S(2)}, u32[]{:S(2)}) collective-permute-start(bf16[4,2,192,128]{3,2,1,0:T(8,128)(2,1)S(1)} %constant_dynamic-update-slice_fusion.refs_0_), channel_id=1, source_target_pairs={{0,2},{2,0},{1,3},{3,1},{4,6},{6,4},{5,7},{7,5},{8,10},{10,8},{9,1... | collective-permute-start | bytes 1179656 | tf_op jit(solution)/shard_map/ppermute | solution.py:133
  48.9 1.6 %collective-permute-start.16 = (bf16[3,2,192,128]{3,2,1,0:T(8,128)(2,1)S(1)}, bf16[3,2,192,128]{3,2,1,0:T(8,128)(2,1)S(1)}, u32[]{:S(2)}, u32[]{:S(2)}) collective-permute-start(bf16[3,2,192,128]{3,2,1,0:T(8,128)(2,1)S(1)} %pad_maximum_fusion.refs_0_), channel_id=1, source_target_pairs={{0,2},{2,0},{1,3},{3,1},{4,6},{6,4},{5,7},{7,5},{8,10},{10,8},{9,1... | collective-permute-start | bytes 884744 | tf_op jit(solution)/shard_map/ppermute | solution.py:133

commit v15 on v14

--- a/solution.py
+++ b/solution.py
@@ -46,37 +46,49 @@
     return copies
 
 
-def grad_kernel(n_high, where_ref, acts_ref, grad_ref, *refs):
-    state_refs, refs = refs[:3], refs[3:]
-    away, kept, refs = refs[:2], refs[2:4], refs[4:]
-    mine_ref, columns, logit_grads, blocks, sems = refs
-    high, low, core, rep = [where_ref[i] for i in range(4)]
-    half = blocks.shape[2]
-    last = sems.shape[0]
-    loads = pltpu.make_async_copy(grad_ref, logit_grads, sems.at[last - 1])
-    loads.start()
-    lows = LOWS[0] + LOWS[1]
-    copies = load_columns(acts_ref, columns, sems, high, low, lows, n_high)
-    rows = pl.ds(pl.multiple_of(rep * half, half), half)
-    state = [
-        pltpu.make_async_copy(ref.at[rows], mine_ref.at[i], sems.at[last - 4 + i])
-        for i, ref in enumerate(state_refs)
-    ]
-    for copy in state:
-        copy.start()
-    loads.wait()
-    turned = logit_grads[...].T
-    for n, copy in enumerate(copies):
-        copy.wait()
+def sort_products(n_high, group, where_ref, turned, columns, away, kept, blocks, arrived):
+    core, rep = where_ref[2], where_ref[3]
+    for n in range(2 * n_high):
+        arrived(n)
         product = jnp.dot(turned, columns[n], preferred_element_type=jnp.float32)
         blocks[...] = product.astype(blocks.dtype).T.reshape(blocks.shape)
         p, j = divmod(n, n_high)
         for d_rep in range(2):
-            for outs, owner in ((kept, core), (away, 1 - core)):
-                slot = slot_of((lows[p], d_rep), owner)
-                outs[p // 2][slot - 4 * (p // 2), j] = blocks[owner, rep ^ d_rep]
-    for copy in state:
+            for out, owner in ((kept, core), (away, 1 - core)):
+                slot = slot_of((LOWS[group][p], d_rep), owner)
+                out[slot - 4 * group, j] = blocks[owner, rep ^ d_rep]
+
+
+def first_grad_kernel(n_high, where_ref, acts_ref, grad_ref, *refs):
+    state_refs, refs = refs[:3], refs[3:]
+    away, kept, mine_ref, later_ref, turned_ref, columns, logit_grads, blocks, sems = refs
+    high, low, _, rep = [where_ref[i] for i in range(4)]
+    half = blocks.shape[2]
+    loads = pltpu.make_async_copy(grad_ref, logit_grads, sems.at[2, 0])
+    loads.start()
+    first = load_columns(acts_ref, columns, sems.at[0], high, low, LOWS[1], n_high)
+    others = load_columns(acts_ref, later_ref, sems.at[1], high, low, LOWS[0], n_high)
+    rows = pl.ds(pl.multiple_of(rep * half, half), half)
+    for i, ref in enumerate(state_refs):
+        copy = pltpu.make_async_copy(ref.at[rows], mine_ref.at[i], sems.at[2, 1 + i])
+        copy.start()
+        others.append(copy)
+    loads.wait()
+    turned = logit_grads[...].T
+    turned_ref[...] = turned
+
+    def arrived(n):
+        if n % 2 == 0:
+            first[n].wait()
+            first[n + 1].wait()
+
+    sort_products(n_high, 1, where_ref, turned, columns, away, kept, blocks, arrived)
+    for copy in others:
         copy.wait()
+
+
+def second_grad_kernel(n_high, where_ref, columns, turned_ref, away, kept, blocks):
+    sort_products(n_high, 0, where_ref, turned_ref[...], columns, away, kept, blocks, lambda n: None)
 
 
 def columns_kernel(n_high, where_ref, acts_ref, first_ref, second_ref, sems):
@@ -170,16 +182,19 @@
         if in_kernels:
             acts = pltpu.with_memory_space_constraint(acts, pltpu.HBM)
             shape = pltpu.VMEM((4, n_high, half, experts), bf16)
-            *sorted_rows, mine = pl.pallas_call(
-                functools.partial(grad_kernel, n_high),
-                out_shape=[shape] * 4 + [pltpu.VMEM((3, half, experts), f32)],
+            columns_shape = pltpu.VMEM((2 * n_high, tokens, 4 * half), bf16)
+            blocks = pltpu.VMEM((2, 2, half, experts), bf16)
+            turned = pltpu.VMEM((experts, tokens), bf16)
+            away_second, kept_second, mine, later, turned = pl.pallas_call(
+                functools.partial(first_grad_kernel, n_high),
+                out_shape=[shape, shape, pltpu.VMEM((3, half, experts), f32), columns_shape, turned],
                 in_specs=[smem] + [anywhere] * 5,
                 out_specs=[vmem] * 5,
                 scratch_shapes=[
-                    pltpu.VMEM((4 * n_high, tokens, 4 * half), bf16),
+                    columns_shape,
                     pltpu.VMEM((tokens, experts), bf16),
-                    pltpu.VMEM((2, 2, half, experts), bf16),
-                    pltpu.SemaphoreType.DMA((4 * n_high + 4,)),
+                    blocks,
+                    pltpu.SemaphoreType.DMA((3, max(2 * n_high, 4))),
                 ],
                 compiler_params=params,
             )(
@@ -187,7 +202,20 @@
                 acts,
                 *(pltpu.with_memory_space_constraint(x, pltpu.HBM) for x in (grad_logits, *state_in)),
             )
-            away, kept = sorted_rows[:2], sorted_rows[2:]
+            away_first, kept_first = pl.pallas_call(
+                functools.partial(second_grad_kernel, n_high),
+                out_shape=[shape, shape],
+                in_specs=[smem, vmem, vmem],
+                out_specs=[vmem] * 2,
+                scratch_shapes=[blocks],
+                cost_estimate=pl.CostEstimate(
+                    flops=4 * n_high * tokens * experts * 4 * half,
+                    bytes_accessed=4 * n_high * tokens * 4 * half,
+                    transcendentals=0,
+                ),
+                compiler_params=params,
+            )(where, *(pltpu.with_memory_space_constraint(x, pltpu.VMEM) for x in (later, turned)))
+            away, kept = (away_first, away_second), (kept_first, kept_second)
         else:
             product = lax.dot_general(
                 acts, grad_logits, (((0,), (0,)), ((), ())), preferred_element_type=f32
@@ -208,9 +236,12 @@
             away, kept = sort_rows(1 - core), sort_rows(core)
             mine = jnp.stack([lax.dynamic_slice_in_dim(x, rep * half, half, 0) for x in state_in])
 
+        arrived = swap(away[1], "core")
+        arrived, away_first = lax.optimization_barrier((arrived, away[0]))
+        arrived = swap(away_first, "core"), arrived
         parts = []
-        for own, theirs in zip(kept, away):
-            summed = own.astype(f32) + swap(theirs, "core").astype(f32)
+        for own, theirs in zip(kept, arrived):
+            summed = own.astype(f32) + theirs.astype(f32)
             for n in range(4):
                 slot = len(parts)
                 parts.append(summed[n] if slot == 7 else to_slot(summed[n].astype(bf16), slot))
@@ -225,8 +256,8 @@
         column = jnp.stack([swap(weight, "high", j) if j else weight for j in range(n_high)])
         other = swap(grad, "rep")
         across = swap(column, "core")
-        across, other, corner = lax.optimization_barrier((across, other, column))
-        corner = to_corner(corner)
+        across, other = lax.optimization_barrier((across, other))
+        corner = to_corner(column)
         chip = jnp.where(core == 0, jnp.stack([column, across]), jnp.stack([across, column]))
         got = [to_next(chip, slot) for slot in range(3)]
 
@@ -248,7 +279,7 @@
                 scratch_shapes=[pltpu.SemaphoreType.DMA((2, 2 * n_high))],
                 compiler_params=params,
             )(where, pltpu.with_memory_space_constraint(late_acts, pltpu.HBM))
-        got[0], state, columns = lax.optimization_barrier((got[0], state, columns))
+        got[0], corner, state, columns = lax.optimization_barrier((got[0], corner, state, columns))
         first, second = jnp.concatenate(got[:2]), jnp.concatenate([got[2], corner[None]])
         first, second = [first, swap(first, "core")], [second, swap(second, "core")]
         second += [column[None], across[None]]

time: 52.5 us -> 48.9 us (0.931)
  waiting for transfers between devices: 15.2 us -> 11.6 us
    ppermute x8, waiting for transfers between devices: 6.77 us -> 3.59 us  [swap(): lax.ppermute(x, axis, [(i, i ^ mask) for i in range(fine.shape[axis])])]
    ppermute x11, starting transfers between devices: 16.4 us -> 17 us  [cube_swap(): return lax.ppermute(x, AXES[1:], pairs)]
    pallas_call x1 -> x2, Pallas kernels: 4.08 us -> 3.66 us  [the longest x1 2.6 us: per_device(): pl.pallas_call(functools.partial(first_grad_kernel, n_high), out_shape=[s...]
  transfers between devices with their start and end apart: 19 -> 19, of which waited for: 11 -> 10; matrix products, arithmetic and copies ran while one was open for 2% -> 3% of each run, Pallas kernels for 7% -> 10%
where the time goes in v15:
time: 48.9 us; the launch traced here: 48.8 us
  starting transfers between devices  25 us (51%)
  waiting for transfers between devices  11.6 us (24%)
  Pallas kernels  9.07 us (19%)
  between operations  1.56 us (3%)
  other arithmetic  1.46 us (3%)
    ppermute x11, starting transfers between devices, cube_swap(): return lax.ppermute(x, AXES[1:], pairs)  17 us
    ppermute x8, starting transfers between devices, swap(): lax.ppermute(x, axis, [(i, i ^ mask) for i in range(fine.shape[axis])])  8.04 us
    ppermute x11, waiting for transfers between devices, cube_swap(): return lax.ppermute(x, AXES[1:], pairs)  7.97 us
    ppermute x8, waiting for transfers between devices, swap(): lax.ppermute(x, axis, [(i, i ^ mask) for i in range(fine.shape[axis])])  3.59 us
    pallas_call x2, Pallas kernels, per_device(): pl.pallas_call(functools.partial(logits_kernel, n_high, group), out_shape...  2.96 us
    pallas_call x1, Pallas kernels, per_device(): pl.pallas_call(functools.partial(first_grad_kernel, n_high), out_shape=[s...  2.6 us
    pallas_call x1, Pallas kernels, per_device(): pl.pallas_call(functools.partial(columns_kernel, n_high), out_shape=(pltp...  2.46 us
    pallas_call x1, Pallas kernels, per_device(): pl.pallas_call(functools.partial(second_grad_kernel, n_high), out_shape=[...  1.06 us
  transfers between devices with their start and end apart: 19, of which 10 were waited for; matrix products, arithmetic and copies ran while one was open for 3% of the time, Pallas kernels for 10%

profile of v15, /device:TPU:0, one launch (start us, length us, event | category | flops | bytes accessed | tf_op | source)
XLA Modules:
  0.0 48.8 jit_solution(5504233258428692228)
XLA Ops:
  0.7 2.6 %shard_map.93 = (bf16[4,2,192,128]{3,2,1,0:T(8,128)(2,1)S(1)}, bf16[4,2,192,128]{3,2,1,0:T(8,128)(2,1)S(1)}, f32[3,192,128]{2,1,0:T(8,128)S(1)}, bf16[4,256,768]{2,1,0:T(8,128)(2,1)S(1)}, bf16[128,256]{1,0:T(8,128)(2,1)S(1)}) custom-call(s32[4]{0:T(128)S(1)} %pad_add_fusion.where_ref, bf16[256,6144]{1,0:T(8,128)(2,1)} %acts_ref.2, ...), custom_call_target="tpu_custom_call" | custom-call | tf_op jit(solution)/shard_map/pallas_call | solution.py:188
  3.8 1.1 %shard_map.94 = (bf16[4,2,192,128]{3,2,1,0:T(8,128)(2,1)S(1)}, bf16[4,2,192,128]{3,2,1,0:T(8,128)(2,1)S(1)}) custom-call(s32[4]{0:T(128)S(1)} %pad_add_fusion.where_ref, bf16[4,256,768]{2,1,0:T(8,128)(2,1)S(1)} %get-tuple-element.37.columns, bf16[128,256]{1,0:T(8,128)(2,1)S(1)} %get-tuple-element.38.turned_ref), custom_call_target="tpu_custom_call" | custom-call | flops 201326592 | bytes 1572864 | tf_op jit(solution)/shard_map/pallas_call | solution.py:205
  5.7 2.7 %collective-permute-start.6 = (bf16[2,192,128]{2,1,0:T(8,128)(2,1)S(1)}, bf16[2,192,128]{2,1,0:T(8,128)(2,1)S(1)}, u32[]{:S(2)}, u32[]{:S(2)}) collective-permute-start(bf16[2,192,128]{2,1,0:T(8,128)(2,1)S(1)} %get-tuple-element.77), channel_id=1, source_target_pairs={{0,1},{1,0},{2,14},{3,15},{4,5},{5,4},{6,10},{7,11},{8,9},{9,8},{1... | collective-permute-start | bytes 294920 | tf_op jit(solution)/shard_map/ppermute | solution.py:155
  8.4 2.5 %collective-permute-start.7 = (bf16[2,192,128]{2,1,0:T(8,128)(2,1)S(1)}, bf16[2,192,128]{2,1,0:T(8,128)(2,1)S(1)}, u32[]{:S(2)}, u32[]{:S(2)}) collective-permute-start(bf16[2,192,128]{2,1,0:T(8,128)(2,1)S(1)} %get-tuple-element.76), channel_id=1, source_target_pairs={{0,12},{1,13},{2,3},{3,2},{4,8},{5,9},{6,7},{7,6},{8,4},{9,5},{10,... | collective-permute-start | bytes 294920 | tf_op jit(solution)/shard_map/ppermute | solution.py:155
  11.1 1.9 %collective-permute-start.2 = (bf16[2,192,128]{2,1,0:T(8,128)(2,1)S(1)}, bf16[2,192,128]{2,1,0:T(8,128)(2,1)S(1)}, u32[]{:S(2)}, u32[]{:S(2)}) collective-permute-start(bf16[2,192,128]{2,1,0:T(8,128)(2,1)S(1)} %get-tuple-element.81), channel_id=1, source_target_pairs={{0,4},{1,5},{2,11},{3,10},{4,0},{5,1},{6,15},{7,14},{8,12},{9,13},... | collective-permute-start | bytes 294920 | tf_op jit(solution)/shard_map/ppermute | solution.py:155
  13.0 2.5 %collective-permute-start.3 = (bf16[2,192,128]{2,1,0:T(8,128)(2,1)S(1)}, bf16[2,192,128]{2,1,0:T(8,128)(2,1)S(1)}, u32[]{:S(2)}, u32[]{:S(2)}) collective-permute-start(bf16[2,192,128]{2,1,0:T(8,128)(2,1)S(1)} %get-tuple-element.80), channel_id=1, source_target_pairs={{0,9},{1,8},{2,6},{3,7},{4,13},{5,12},{6,2},{7,3},{8,1},{9,0},{10,... | collective-permute-start | bytes 294920 | tf_op jit(solution)/shard_map/ppermute | solution.py:155
  16.0 1.1 %collective-permute-start.5 = (bf16[2,192,128]{2,1,0:T(8,128)(2,1)S(1)}, bf16[2,192,128]{2,1,0:T(8,128)(2,1)S(1)}, u32[]{:S(2)}, u32[]{:S(2)}) collective-permute-start(bf16[2,192,128]{2,1,0:T(8,128)(2,1)S(1)} %get-tuple-element.78), channel_id=1, source_target_pairs={{0,5},{1,4},{2,10},{3,11},{4,1},{5,0},{6,14},{7,15},{8,13},{9,12},... | collective-permute-start | bytes 294920 | tf_op jit(solution)/shard_map/ppermute | solution.py:155
  17.1 2.0 %collective-permute-done.8 = bf16[2,192,128]{2,1,0:T(8,128)(2,1)S(1)} collective-permute-done((bf16[2,192,128]{2,1,0:T(8,128)(2,1)S(1)}, bf16[2,192,128]{2,1,0:T(8,128)(2,1)S(1)}, u32[]{:S(2)}, u32[]{:S(2)}) %collective-permute-start.8) | collective-permute-done | bytes 98336 | tf_op jit(solution)/shard_map/ppermute | solution.py:155
  19.4 1.2 %collective-permute-done.4 = bf16[2,192,128]{2,1,0:T(8,128)(2,1)S(1)} collective-permute-done((bf16[2,192,128]{2,1,0:T(8,128)(2,1)S(1)}, bf16[2,192,128]{2,1,0:T(8,128)(2,1)S(1)}, u32[]{:S(2)}, u32[]{:S(2)}) %collective-permute-start.4) | collective-permute-done | bytes 98336 | tf_op jit(solution)/shard_map/ppermute | solution.py:155
  20.5 1.0 %collective-permute-done.5 = bf16[2,192,128]{2,1,0:T(8,128)(2,1)S(1)} collective-permute-done((bf16[2,192,128]{2,1,0:T(8,128)(2,1)S(1)}, bf16[2,192,128]{2,1,0:T(8,128)(2,1)S(1)}, u32[]{:S(2)}, u32[]{:S(2)}) %collective-permute-start.5) | collective-permute-done | bytes 98336 | tf_op jit(solution)/shard_map/ppermute | solution.py:155
  21.7 2.7 %collective-permute-start.9 = (bf16[192,128]{1,0:T(8,128)(2,1)S(1)}, bf16[192,128]{1,0:T(8,128)(2,1)S(1)}, u32[]{:S(2)}, u32[]{:S(2)}) collective-permute-start(bf16[192,128]{1,0:T(8,128)(2,1)S(1)} %fusion.11), channel_id=1, source_target_pairs={{0,16},{16,0},{1,17},{17,1},{2,18},{18,2},{3,19},{19,3},{4,20},{20... | collective-permute-start | bytes 147464 | tf_op jit(solution)/shard_map/ppermute | solution.py:145
  25.1 1.7 %collective-permute-done.9 = bf16[192,128]{1,0:T(8,128)(2,1)S(1)} collective-permute-done((bf16[192,128]{1,0:T(8,128)(2,1)S(1)}, bf16[192,128]{1,0:T(8,128)(2,1)S(1)}, u32[]{:S(2)}, u32[]{:S(2)}) %collective-permute-start.9) | collective-permute-done | bytes 49184 | tf_op jit(solution)/shard_map/ppermute | solution.py:145
  26.8 2.7 %collective-permute-start.10 = (bf16[192,128]{1,0:T(8,128)(2,1)S(1)}, bf16[192,128]{1,0:T(8,128)(2,1)S(1)}, u32[]{:S(2)}, u32[]{:S(2)}) collective-permute-start(bf16[192,128]{1,0:T(8,128)(2,1)S(1)} %get-tuple-element.71), channel_id=1, source_target_pairs={{0,16},{16,0},{1,17},{17,1},{2,18},{18,2},{3,19},{19,3},{4,20},{20... | collective-permute-start | bytes 147464 | tf_op jit(solution)/shard_map/ppermute | solution.py:145
  29.5 1.1 %collective-permute-start.12 = (f32[192,128]{1,0:T(8,128)S(1)}, f32[192,128]{1,0:T(8,128)S(1)}, u32[]{:S(2)}, u32[]{:S(2)}) collective-permute-start(f32[192,128]{1,0:T(8,128)S(1)} %get-tuple-element.72), channel_id=1, source_target_pairs={{0,1},{1,0},{2,3},{3,2},{4,5},{5,4},{6,7},{7,6},{8,9},{9,8},{10,11... | collective-permute-start | bytes 294920 | tf_op jit(solution)/shard_map/ppermute | solution.py:145
  30.6 1.2 %collective-permute-done.10 = bf16[192,128]{1,0:T(8,128)(2,1)S(1)} collective-permute-done((bf16[192,128]{1,0:T(8,128)(2,1)S(1)}, bf16[192,128]{1,0:T(8,128)(2,1)S(1)}, u32[]{:S(2)}, u32[]{:S(2)}) %collective-permute-start.10) | collective-permute-done | bytes 49184 | tf_op jit(solution)/shard_map/ppermute | solution.py:145
  32.0 2.2 %collective-permute-start.14 = (bf16[2,192,128]{2,1,0:T(8,128)(2,1)S(1)}, bf16[2,192,128]{2,1,0:T(8,128)(2,1)S(1)}, u32[]{:S(2)}, u32[]{:S(2)}) collective-permute-start(bf16[2,192,128]{2,1,0:T(8,128)(2,1)S(1)} %get-tuple-element.83), channel_id=1, source_target_pairs={{0,13},{1,12},{2,15},{3,14},{4,9},{5,8},{6,11},{7,10},{8,5},{9,4},... | collective-permute-start | bytes 294920 | tf_op jit(solution)/shard_map/ppermute | solution.py:155
  34.2 1.3 %collective-permute-start.13 = (bf16[2,2,192,128]{3,2,1,0:T(8,128)(2,1)S(1)}, bf16[2,2,192,128]{3,2,1,0:T(8,128)(2,1)S(1)}, u32[]{:S(2)}, u32[]{:S(2)}) collective-permute-start(bf16[2,2,192,128]{3,2,1,0:T(8,128)(2,1)S(1)} %maximum_select_fusion), channel_id=1, source_target_pairs={{0,4},{1,5},{2,11},{3,10},{4,0},{5,1},{6,15},{7,14},{8,12},{9,13},... | collective-permute-start | bytes 589832 | tf_op jit(solution)/shard_map/ppermute | solution.py:155
  35.5 1.4 %collective-permute-start.17 = (bf16[2,2,192,128]{3,2,1,0:T(8,128)(2,1)S(1)}, bf16[2,2,192,128]{3,2,1,0:T(8,128)(2,1)S(1)}, u32[]{:S(2)}, u32[]{:S(2)}) collective-permute-start(bf16[2,2,192,128]{3,2,1,0:T(8,128)(2,1)S(1)} %maximum_select_fusion), channel_id=1, source_target_pairs={{0,8},{1,9},{2,7},{3,6},{4,12},{5,13},{6,3},{7,2},{8,0},{9,1},{10,... | collective-permute-start | bytes 589832 | tf_op jit(solution)/shard_map/ppermute | solution.py:155
  36.8 0.9 %collective-permute-start.15 = (bf16[2,2,192,128]{3,2,1,0:T(8,128)(2,1)S(1)}, bf16[2,2,192,128]{3,2,1,0:T(8,128)(2,1)S(1)}, u32[]{:S(2)}, u32[]{:S(2)}) collective-permute-start(bf16[2,2,192,128]{3,2,1,0:T(8,128)(2,1)S(1)} %maximum_select_fusion), channel_id=1, source_target_pairs={{0,1},{1,0},{2,14},{3,15},{4,5},{5,4},{6,10},{7,11},{8,9},{9,8},{1... | collective-permute-start | bytes 589832 | tf_op jit(solution)/shard_map/ppermute | solution.py:155
  38.7 2.5 %shard_map.95 = (bf16[4,256,768]{2,1,0:T(8,128)(2,1)S(1)}, bf16[4,256,768]{2,1,0:T(8,128)(2,1)S(1)}) custom-call(s32[4]{0:T(128)S(1)} %pad_add_fusion.where_ref, bf16[256,6144]{1,0:T(8,128)(2,1)} %acts_ref.2), custom_call_target="tpu_custom_call" | custom-call | tf_op jit(solution)/shard_map/pallas_call | solution.py:274
  41.1 2.2 %collective-permute-done.13 = bf16[2,2,192,128]{3,2,1,0:T(8,128)(2,1)S(1)} collective-permute-done((bf16[2,2,192,128]{3,2,1,0:T(8,128)(2,1)S(1)}, bf16[2,2,192,128]{3,2,1,0:T(8,128)(2,1)S(1)}, u32[]{:S(2)}, u32[]{:S(2)}) %collective-permute-start.13) | collective-permute-done | bytes 196640 | tf_op jit(solution)/shard_map/ppermute | solution.py:155
  44.0 1.3 %collective-permute-done.15 = bf16[2,2,192,128]{3,2,1,0:T(8,128)(2,1)S(1)} collective-permute-done((bf16[2,2,192,128]{3,2,1,0:T(8,128)(2,1)S(1)}, bf16[2,2,192,128]{3,2,1,0:T(8,128)(2,1)S(1)}, u32[]{:S(2)}, u32[]{:S(2)}) %collective-permute-start.15) | collective-permute-done | bytes 196640 | tf_op jit(solution)/shard_map/ppermute | solution.py:155
  45.4 1.2 %shard_map.96.refs_4_ = f32[256,128]{1,0:T(8,128)S(1)} custom-call(s32[4]{0:T(128)S(1)} %pad_add_fusion.where_ref, bf16[4,256,768]{2,1,0:T(8,128)(2,1)S(1)} %get-tuple-element.66.columns_ref, bf16[4,2,192,128]{3,2,1,0:T(8,128)(2,1)S(1)} %constant_dynamic-update-slice_fusion.refs_0_, bf16[4,2,192,128]{3,2,1,0:T(8,128)(2,1)S(1)} %collective-permute-done.18.refs_1_), custom_call_target="tpu_custom_call" | custom-call | tf_op jit(solution)/shard_map/pallas_call | solution.py:294
  47.0 1.8 %shard_map.97 = bf16[256,128]{1,0:T(8,128)(2,1)} custom-call(s32[4]{0:T(128)S(1)} %pad_add_fusion.where_ref, bf16[4,256,768]{2,1,0:T(8,128)(2,1)S(1)} %get-tuple-element.64.columns_ref, bf16[3,2,192,128]{3,2,1,0:T(8,128)(2,1)S(1)} %pad_maximum_fusion.refs_0_, bf16[3,2,192,128]{3,2,1,0:T(8,128)(2,1)S(1)} %collective-permute-done.16.refs_1_, ...), custom_call_target="tpu_custom_call" | custom-call | tf_op jit(solution)/shard_map/pallas_call | solution.py:294
  (40 shorter events, 4.6 us)
Async XLA Ops:
  3.3 1.9 %collective-permute-start = (bf16[4,2,192,128]{3,2,1,0:T(8,128)(2,1)S(1)}, bf16[4,2,192,128]{3,2,1,0:T(8,128)(2,1)S(1)}, u32[]{:S(2)}, u32[]{:S(2)}) collective-permute-start(bf16[4,2,192,128]{3,2,1,0:T(8,128)(2,1)S(1)} %get-tuple-element.40), channel_id=1, source_target_pairs={{0,2},{2,0},{1,3},{3,1},{4,6},{6,4},{5,7},{7,5},{8,10},{10,8},{9,1... | collective-permute-start | bytes 1179656 | tf_op jit(solution)/shard_map/ppermute | solution.py:145
  5.2 5.8 %collective-permute-start.1 = (bf16[4,2,192,128]{3,2,1,0:T(8,128)(2,1)S(1)}, bf16[4,2,192,128]{3,2,1,0:T(8,128)(2,1)S(1)}, u32[]{:S(2)}, u32[]{:S(2)}) collective-permute-start(bf16[4,2,192,128]{3,2,1,0:T(8,128)(2,1)S(1)} %get-tuple-element.42), channel_id=1, source_target_pairs={{0,2},{2,0},{1,3},{3,1},{4,6},{6,4},{5,7},{7,5},{8,10},{10,8},{9,1... | collective-permute-start | bytes 1179656 | tf_op jit(solution)/shard_map/ppermute | solution.py:145
  5.7 9.9 %collective-permute-start.6 = (bf16[2,192,128]{2,1,0:T(8,128)(2,1)S(1)}, bf16[2,192,128]{2,1,0:T(8,128)(2,1)S(1)}, u32[]{:S(2)}, u32[]{:S(2)}) collective-permute-start(bf16[2,192,128]{2,1,0:T(8,128)(2,1)S(1)} %get-tuple-element.77), channel_id=1, source_target_pairs={{0,1},{1,0},{2,14},{3,15},{4,5},{5,4},{6,10},{7,11},{8,9},{9,8},{1... | collective-permute-start | bytes 294920 | tf_op jit(solution)/shard_map/ppermute | solution.py:155
  8.4 7.6 %collective-permute-start.7 = (bf16[2,192,128]{2,1,0:T(8,128)(2,1)S(1)}, bf16[2,192,128]{2,1,0:T(8,128)(2,1)S(1)}, u32[]{:S(2)}, u32[]{:S(2)}) collective-permute-start(bf16[2,192,128]{2,1,0:T(8,128)(2,1)S(1)} %get-tuple-element.76), channel_id=1, source_target_pairs={{0,12},{1,13},{2,3},{3,2},{4,8},{5,9},{6,7},{7,6},{8,4},{9,5},{10,... | collective-permute-start | bytes 294920 | tf_op jit(solution)/shard_map/ppermute | solution.py:155
  10.9 8.2 %collective-permute-start.8 = (bf16[2,192,128]{2,1,0:T(8,128)(2,1)S(1)}, bf16[2,192,128]{2,1,0:T(8,128)(2,1)S(1)}, u32[]{:S(2)}, u32[]{:S(2)}) collective-permute-start(bf16[2,192,128]{2,1,0:T(8,128)(2,1)S(1)} %get-tuple-element.75), channel_id=1, source_target_pairs={{0,13},{1,12},{2,15},{3,14},{4,9},{5,8},{6,11},{7,10},{8,5},{9,4},... | collective-permute-start | bytes 294920 | tf_op jit(solution)/shard_map/ppermute | solution.py:155
  11.1 26.7 %copy-start = (f32[384,128]{1,0:T(8,128)S(1)}, f32[384,128]{1,0:T(8,128)}, u32[]{:S(2)}) copy-start(f32[384,128]{1,0:T(8,128)} %refs_0_.1) | copy-start | bytes 589828
  11.1 26.7 %copy-start.1 = (f32[384,128]{1,0:T(8,128)S(1)}, f32[384,128]{1,0:T(8,128)}, u32[]{:S(2)}) copy-start(f32[384,128]{1,0:T(8,128)} %refs_1_.1) | copy-start | bytes 589828
  11.1 26.7 %copy-start.2 = (f32[384,128]{1,0:T(8,128)S(1)}, f32[384,128]{1,0:T(8,128)}, u32[]{:S(2)}) copy-start(f32[384,128]{1,0:T(8,128)} %refs_2_.1) | copy-start | bytes 589828
  11.1 8.0 %collective-permute-start.2 = (bf16[2,192,128]{2,1,0:T(8,128)(2,1)S(1)}, bf16[2,192,128]{2,1,0:T(8,128)(2,1)S(1)}, u32[]{:S(2)}, u32[]{:S(2)}) collective-permute-start(bf16[2,192,128]{2,1,0:T(8,128)(2,1)S(1)} %get-tuple-element.81), channel_id=1, source_target_pairs={{0,4},{1,5},{2,11},{3,10},{4,0},{5,1},{6,15},{7,14},{8,12},{9,13},... | collective-permute-start | bytes 294920 | tf_op jit(solution)/shard_map/ppermute | solution.py:155
  13.0 6.3 %collective-permute-start.3 = (bf16[2,192,128]{2,1,0:T(8,128)(2,1)S(1)}, bf16[2,192,128]{2,1,0:T(8,128)(2,1)S(1)}, u32[]{:S(2)}, u32[]{:S(2)}) collective-permute-start(bf16[2,192,128]{2,1,0:T(8,128)(2,1)S(1)} %get-tuple-element.80), channel_id=1, source_target_pairs={{0,9},{1,8},{2,6},{3,7},{4,13},{5,12},{6,2},{7,3},{8,1},{9,0},{10,... | collective-permute-start | bytes 294920 | tf_op jit(solution)/shard_map/ppermute | solution.py:155
  15.6 4.9 %collective-permute-start.4 = (bf16[2,192,128]{2,1,0:T(8,128)(2,1)S(1)}, bf16[2,192,128]{2,1,0:T(8,128)(2,1)S(1)}, u32[]{:S(2)}, u32[]{:S(2)}) collective-permute-start(bf16[2,192,128]{2,1,0:T(8,128)(2,1)S(1)} %get-tuple-element.79), channel_id=1, source_target_pairs={{0,8},{1,9},{2,7},{3,6},{4,12},{5,13},{6,3},{7,2},{8,0},{9,1},{10,... | collective-permute-start | bytes 294920 | tf_op jit(solution)/shard_map/ppermute | solution.py:155
  16.0 5.5 %collective-permute-start.5 = (bf16[2,192,128]{2,1,0:T(8,128)(2,1)S(1)}, bf16[2,192,128]{2,1,0:T(8,128)(2,1)S(1)}, u32[]{:S(2)}, u32[]{:S(2)}) collective-permute-start(bf16[2,192,128]{2,1,0:T(8,128)(2,1)S(1)} %get-tuple-element.78), channel_id=1, source_target_pairs={{0,5},{1,4},{2,10},{3,11},{4,1},{5,0},{6,14},{7,15},{8,13},{9,12},... | collective-permute-start | bytes 294920 | tf_op jit(solution)/shard_map/ppermute | solution.py:155
  21.7 5.1 %collective-permute-start.9 = (bf16[192,128]{1,0:T(8,128)(2,1)S(1)}, bf16[192,128]{1,0:T(8,128)(2,1)S(1)}, u32[]{:S(2)}, u32[]{:S(2)}) collective-permute-start(bf16[192,128]{1,0:T(8,128)(2,1)S(1)} %fusion.11), channel_id=1, source_target_pairs={{0,16},{16,0},{1,17},{17,1},{2,18},{18,2},{3,19},{19,3},{4,20},{20... | collective-permute-start | bytes 147464 | tf_op jit(solution)/shard_map/ppermute | solution.py:145
  26.8 5.1 %collective-permute-start.10 = (bf16[192,128]{1,0:T(8,128)(2,1)S(1)}, bf16[192,128]{1,0:T(8,128)(2,1)S(1)}, u32[]{:S(2)}, u32[]{:S(2)}) collective-permute-start(bf16[192,128]{1,0:T(8,128)(2,1)S(1)} %get-tuple-element.71), channel_id=1, source_target_pairs={{0,16},{16,0},{1,17},{17,1},{2,18},{18,2},{3,19},{19,3},{4,20},{20... | collective-permute-start | bytes 147464 | tf_op jit(solution)/shard_map/ppermute | solution.py:145
  29.5 4.6 %collective-permute-start.12 = (f32[192,128]{1,0:T(8,128)S(1)}, f32[192,128]{1,0:T(8,128)S(1)}, u32[]{:S(2)}, u32[]{:S(2)}) collective-permute-start(f32[192,128]{1,0:T(8,128)S(1)} %get-tuple-element.72), channel_id=1, source_target_pairs={{0,1},{1,0},{2,3},{3,2},{4,5},{5,4},{6,7},{7,6},{8,9},{9,8},{10,11... | collective-permute-start | bytes 294920 | tf_op jit(solution)/shard_map/ppermute | solution.py:145
  31.9 2.3 %collective-permute-start.11 = (bf16[2,192,128]{2,1,0:T(8,128)(2,1)S(1)}, bf16[2,192,128]{2,1,0:T(8,128)(2,1)S(1)}, u32[]{:S(2)}, u32[]{:S(2)}) collective-permute-start(bf16[2,192,128]{2,1,0:T(8,128)(2,1)S(1)} %get-tuple-element.83), channel_id=1, source_target_pairs={{0,2},{2,0},{1,3},{3,1},{4,6},{6,4},{5,7},{7,5},{8,10},{10,8},{9,1... | collective-permute-start | bytes 294920 | tf_op jit(solution)/shard_map/ppermute | solution.py:145
  32.0 9.1 %collective-permute-start.14 = (bf16[2,192,128]{2,1,0:T(8,128)(2,1)S(1)}, bf16[2,192,128]{2,1,0:T(8,128)(2,1)S(1)}, u32[]{:S(2)}, u32[]{:S(2)}) collective-permute-start(bf16[2,192,128]{2,1,0:T(8,128)(2,1)S(1)} %get-tuple-element.83), channel_id=1, source_target_pairs={{0,13},{1,12},{2,15},{3,14},{4,9},{5,8},{6,11},{7,10},{8,5},{9,4},... | collective-permute-start | bytes 294920 | tf_op jit(solution)/shard_map/ppermute | solution.py:155
  34.2 9.2 %collective-permute-start.13 = (bf16[2,2,192,128]{3,2,1,0:T(8,128)(2,1)S(1)}, bf16[2,2,192,128]{3,2,1,0:T(8,128)(2,1)S(1)}, u32[]{:S(2)}, u32[]{:S(2)}) collective-permute-start(bf16[2,2,192,128]{3,2,1,0:T(8,128)(2,1)S(1)} %maximum_select_fusion), channel_id=1, source_target_pairs={{0,4},{1,5},{2,11},{3,10},{4,0},{5,1},{6,15},{7,14},{8,12},{9,13},... | collective-permute-start | bytes 589832 | tf_op jit(solution)/shard_map/ppermute | solution.py:155
  35.5 7.9 %collective-permute-start.17 = (bf16[2,2,192,128]{3,2,1,0:T(8,128)(2,1)S(1)}, bf16[2,2,192,128]{3,2,1,0:T(8,128)(2,1)S(1)}, u32[]{:S(2)}, u32[]{:S(2)}) collective-permute-start(bf16[2,2,192,128]{3,2,1,0:T(8,128)(2,1)S(1)} %maximum_select_fusion), channel_id=1, source_target_pairs={{0,8},{1,9},{2,7},{3,6},{4,12},{5,13},{6,3},{7,2},{8,0},{9,1},{10,... | collective-permute-start | bytes 589832 | tf_op jit(solution)/shard_map/ppermute | solution.py:155
  36.8 8.5 %collective-permute-start.15 = (bf16[2,2,192,128]{3,2,1,0:T(8,128)(2,1)S(1)}, bf16[2,2,192,128]{3,2,1,0:T(8,128)(2,1)S(1)}, u32[]{:S(2)}, u32[]{:S(2)}) collective-permute-start(bf16[2,2,192,128]{3,2,1,0:T(8,128)(2,1)S(1)} %maximum_select_fusion), channel_id=1, source_target_pairs={{0,1},{1,0},{2,14},{3,15},{4,5},{5,4},{6,10},{7,11},{8,9},{9,8},{1... | collective-permute-start | bytes 589832 | tf_op jit(solution)/shard_map/ppermute | solution.py:155
  43.4 2.0 %collective-permute-start.18 = (bf16[4,2,192,128]{3,2,1,0:T(8,128)(2,1)S(1)}, bf16[4,2,192,128]{3,2,1,0:T(8,128)(2,1)S(1)}, u32[]{:S(2)}, u32[]{:S(2)}) collective-permute-start(bf16[4,2,192,128]{3,2,1,0:T(8,128)(2,1)S(1)} %constant_dynamic-update-slice_fusion.refs_0_), channel_id=1, source_target_pairs={{0,2},{2,0},{1,3},{3,1},{4,6},{6,4},{5,7},{7,5},{8,10},{10,8},{9,1... | collective-permute-start | bytes 1179656 | tf_op jit(solution)/shard_map/ppermute | solution.py:145
  45.3 1.6 %collective-permute-start.16 = (bf16[3,2,192,128]{3,2,1,0:T(8,128)(2,1)S(1)}, bf16[3,2,192,128]{3,2,1,0:T(8,128)(2,1)S(1)}, u32[]{:S(2)}, u32[]{:S(2)}) collective-permute-start(bf16[3,2,192,128]{3,2,1,0:T(8,128)(2,1)S(1)} %pad_maximum_fusion.refs_0_), channel_id=1, source_target_pairs={{0,2},{2,0},{1,3},{3,1},{4,6},{6,4},{5,7},{7,5},{8,10},{10,8},{9,1... | collective-permute-start | bytes 884744 | tf_op jit(solution)/shard_map/ppermute | solution.py:145

commit v16 on v15

--- a/solution.py
+++ b/solution.py
@@ -10,15 +10,9 @@
 
 AXES = ("high", "low", "core", "rep")
 N_LOW = 4
-CHIPS = ((1, 0), (2, 1), (2, 0), (1, 1), (0, 1), (3, 0), (3, 1), (0, 0))
+NEXT = ((1, 0), (2, 0), (0, 1))
 LOWS = ((1, 2), (0, 3))
-NEXT = ((1, 0), (2, 0), (0, 1))
 VMEM_LIMIT = 8 * 2**20
-
-
-def slot_of(chip, core):
-    slot = CHIPS.index(chip)
-    return slot if slot >= 6 else slot ^ core
 
 
 def adamw(grad, master, moment_one, moment_two, step_count):
@@ -46,28 +40,40 @@
     return copies
 
 
+def grad_lows(group, core):
+    return LOWS[0] if group == 0 else (3 * core, 3 * (1 - core))
+
+
 def sort_products(n_high, group, where_ref, turned, columns, away, kept, blocks, arrived):
     core, rep = where_ref[2], where_ref[3]
+    here = rep ^ core
     for n in range(2 * n_high):
         arrived(n)
         product = jnp.dot(turned, columns[n], preferred_element_type=jnp.float32)
         blocks[...] = product.astype(blocks.dtype).T.reshape(blocks.shape)
         p, j = divmod(n, n_high)
-        for d_rep in range(2):
-            for out, owner in ((kept, core), (away, 1 - core)):
-                slot = slot_of((LOWS[group][p], d_rep), owner)
-                out[slot - 4 * group, j] = blocks[owner, rep ^ d_rep]
+        if group == 0:
+            for c in range(2):
+                kept[p ^ core, c, j] = blocks[c, here]
+                away[p ^ core ^ 1, c, j] = blocks[c, here ^ 1]
+        else:
+            slot = kept if p == 0 else away
+            for c in range(2):
+                slot[c, j] = blocks[c, here ^ 1 ^ p]
+            at = 3 - core if p == 0 else 2 + core
+            kept[at, j] = blocks[core, here ^ p]
+            away[at, j] = blocks[1 - core, here ^ p]
 
 
 def first_grad_kernel(n_high, where_ref, acts_ref, grad_ref, *refs):
     state_refs, refs = refs[:3], refs[3:]
     away, kept, mine_ref, later_ref, turned_ref, columns, logit_grads, blocks, sems = refs
-    high, low, _, rep = [where_ref[i] for i in range(4)]
+    high, low, core, rep = [where_ref[i] for i in range(4)]
     half = blocks.shape[2]
     loads = pltpu.make_async_copy(grad_ref, logit_grads, sems.at[2, 0])
     loads.start()
-    first = load_columns(acts_ref, columns, sems.at[0], high, low, LOWS[1], n_high)
-    others = load_columns(acts_ref, later_ref, sems.at[1], high, low, LOWS[0], n_high)
+    first = load_columns(acts_ref, columns, sems.at[0], high, low, grad_lows(1, core), n_high)
+    others = load_columns(acts_ref, later_ref, sems.at[1], high, low, grad_lows(0, core), n_high)
     rows = pl.ds(pl.multiple_of(rep * half, half), half)
     for i, ref in enumerate(state_refs):
         copy = pltpu.make_async_copy(ref.at[rows], mine_ref.at[i], sems.at[2, 1 + i])
@@ -154,9 +160,6 @@
                     pairs.append(((low * 2 + core) * n_rep + rep, there))
         return lax.ppermute(x, AXES[1:], pairs)
 
-    def to_slot(x, slot):
-        return cube_swap(x, lambda core: CHIPS[slot ^ core if slot < 6 else slot])
-
     def to_next(x, slot):
         d_low, d_rep = NEXT[slot]
         return cube_swap(x, lambda core: (d_low ^ (3 * core), d_rep ^ core))
@@ -181,13 +184,14 @@
 
         if in_kernels:
             acts = pltpu.with_memory_space_constraint(acts, pltpu.HBM)
-            shape = pltpu.VMEM((4, n_high, half, experts), bf16)
+            first = pltpu.VMEM((2, 2, n_high, half, experts), bf16)
+            second = pltpu.VMEM((4, n_high, half, experts), bf16)
             columns_shape = pltpu.VMEM((2 * n_high, tokens, 4 * half), bf16)
             blocks = pltpu.VMEM((2, 2, half, experts), bf16)
             turned = pltpu.VMEM((experts, tokens), bf16)
             away_second, kept_second, mine, later, turned = pl.pallas_call(
                 functools.partial(first_grad_kernel, n_high),
-                out_shape=[shape, shape, pltpu.VMEM((3, half, experts), f32), columns_shape, turned],
+                out_shape=[second, second, pltpu.VMEM((3, half, experts), f32), columns_shape, turned],
                 in_specs=[smem] + [anywhere] * 5,
                 out_specs=[vmem] * 5,
                 scratch_shapes=[
@@ -204,7 +208,7 @@
             )
             away_first, kept_first = pl.pallas_call(
                 functools.partial(second_grad_kernel, n_high),
-                out_shape=[shape, shape],
+                out_shape=[first, first],
                 in_specs=[smem, vmem, vmem],
                 out_specs=[vmem] * 2,
                 scratch_shapes=[blocks],
@@ -223,15 +227,18 @@
             product = product.reshape(n_high, N_LOW, 2, n_rep, half, experts)
             product = product[high ^ jnp.arange(n_high)]
 
-            def sort_rows(owner):
-                blocks = []
-                for slot in range(8):
-                    flip = owner if slot < 6 else 0
-                    d_low, d_rep = CHIPS[slot]
-                    at = (0, low ^ d_low ^ (3 * flip), owner, rep ^ d_rep ^ flip, 0, 0)
-                    part = lax.dynamic_slice(product, at, (n_high, 1, 1, 1, half, experts))
-                    blocks.append(part.reshape(n_high, half, experts))
-                return jnp.stack(blocks[:4]), jnp.stack(blocks[4:])
+            def block(d_low, owner, d_rep):
+                at = (0, low ^ d_low, owner, rep ^ d_rep, 0, 0)
+                part = lax.dynamic_slice(product, at, (n_high, 1, 1, 1, half, experts))
+                return part.reshape(n_high, half, experts)
+
+            def sort_rows(by):
+                slots = [
+                    jnp.stack([block(d_low ^ (3 * by), c, d_rep ^ by) for c in range(2)])
+                    for d_low, d_rep in NEXT
+                ]
+                rest = [slots[2], block(3, by, 1)[None], block(0, by, 0)[None]]
+                return jnp.stack(slots[:2]), jnp.concatenate(rest)
 
             away, kept = sort_rows(1 - core), sort_rows(core)
             mine = jnp.stack([lax.dynamic_slice_in_dim(x, rep * half, half, 0) for x in state_in])
@@ -239,14 +246,15 @@
         arrived = swap(away[1], "core")
         arrived, away_first = lax.optimization_barrier((arrived, away[0]))
         arrived = swap(away_first, "core"), arrived
-        parts = []
-        for own, theirs in zip(kept, arrived):
-            summed = own.astype(f32) + theirs.astype(f32)
-            for n in range(4):
-                slot = len(parts)
-                parts.append(summed[n] if slot == 7 else to_slot(summed[n].astype(bf16), slot))
-        parts = lax.optimization_barrier(parts)
-        total = sum(x.astype(f32) for x in parts)
+        first, second = [x.astype(f32) + y.astype(f32) for x, y in zip(kept, arrived)]
+        slots = [first[0], first[1], second[:2]]
+        slots = [to_next(x.astype(bf16), slot) for slot, x in enumerate(slots)]
+        corner = to_corner(second[2].astype(bf16))
+        home = second[3]
+        *slots, corner = [x.astype(f32) for x in lax.optimization_barrier((*slots, corner))]
+        total = slots[0] + slots[1] + slots[2]
+        theirs = swap(lax.dynamic_index_in_dim(total, 1 - core, 0, keepdims=False), "core")
+        total = lax.dynamic_index_in_dim(total, core, 0, keepdims=False) + theirs + home + corner
 
         grad = total[0]
         for j in range(1, n_high):
@@ -256,8 +264,8 @@
         column = jnp.stack([swap(weight, "high", j) if j else weight for j in range(n_high)])
         other = swap(grad, "rep")
         across = swap(column, "core")
-        across, other = lax.optimization_barrier((across, other))
-        corner = to_corner(column)
+        across, other, late_column = lax.optimization_barrier((across, other, column))
+        corner = to_corner(late_column)
         chip = jnp.where(core == 0, jnp.stack([column, across]), jnp.stack([across, column]))
         got = [to_next(chip, slot) for slot in range(3)]
 

time: 48.9 us -> 52.6 us (1.076)
  waiting for transfers between devices: 11.6 us -> 20.5 us
  starting transfers between devices: 25 us -> 19.6 us
    ppermute x8 -> x9, waiting for transfers between devices: 3.59 us -> 10 us  [swap(): lax.ppermute(x, axis, [(i, i ^ mask) for i in range(fine.shape[axis])])]
    ppermute x11 -> x8, starting transfers between devices: 17 us -> 12.1 us  [cube_swap(): return lax.ppermute(x, AXES[1:], pairs)]
    ppermute x11 -> x8, waiting for transfers between devices: 7.97 us -> 10.5 us  [cube_swap(): return lax.ppermute(x, AXES[1:], pairs)]
    ppermute x8 -> x9, starting transfers between devices: 8.04 us -> 7.49 us  [swap(): lax.ppermute(x, axis, [(i, i ^ mask) for i in range(fine.shape[axis])])]
  transfers between devices with their start and end apart: 19 -> 17, of which waited for: 10 -> 9; matrix products, arithmetic and copies ran while one was open for 3% -> 2% of each run, Pallas kernels for 10% -> 9%
where the time goes in v16:
time: 52.6 us; the launch traced here: 52.4 us
  waiting for transfers between devices  20.5 us (39%)
  starting transfers between devices  19.6 us (37%)
  Pallas kernels  9.07 us (17%)
  between operations  1.57 us (3%)
  other arithmetic  1.48 us (3%)
    ppermute x8, starting transfers between devices, cube_swap(): return lax.ppermute(x, AXES[1:], pairs)  12.1 us
    ppermute x8, waiting for transfers between devices, cube_swap(): return lax.ppermute(x, AXES[1:], pairs)  10.5 us
    ppermute x9, waiting for transfers between devices, swap(): lax.ppermute(x, axis, [(i, i ^ mask) for i in range(fine.shape[axis])])  10 us
    ppermute x9, starting transfers between devices, swap(): lax.ppermute(x, axis, [(i, i ^ mask) for i in range(fine.shape[axis])])  7.49 us
    pallas_call x2, Pallas kernels, per_device(): pl.pallas_call(functools.partial(logits_kernel, n_high, group), out_shape...  2.96 us
    pallas_call x1, Pallas kernels, per_device(): pl.pallas_call(functools.partial(first_grad_kernel, n_high), out_shape=[s...  2.6 us
    pallas_call x1, Pallas kernels, per_device(): pl.pallas_call(functools.partial(columns_kernel, n_high), out_shape=(pltp...  2.46 us
    pallas_call x1, Pallas kernels, per_device(): pl.pallas_call(functools.partial(second_grad_kernel, n_high), out_shape=[...  1.06 us
  transfers between devices with their start and end apart: 17, of which 9 were waited for; matrix products, arithmetic and copies ran while one was open for 2% of the time, Pallas kernels for 9%

profile of v16, /device:TPU:0, one launch (start us, length us, event | category | flops | bytes accessed | tf_op | source)
XLA Modules:
  0.0 52.4 jit_solution(5783104523122180232)
XLA Ops:
  0.7 2.6 %shard_map.93 = (bf16[4,2,192,128]{3,2,1,0:T(8,128)(2,1)S(1)}, bf16[4,2,192,128]{3,2,1,0:T(8,128)(2,1)S(1)}, f32[3,192,128]{2,1,0:T(8,128)S(1)}, bf16[4,256,768]{2,1,0:T(8,128)(2,1)S(1)}, bf16[128,256]{1,0:T(8,128)(2,1)S(1)}) custom-call(s32[4]{0:T(128)S(1)} %pad_add_fusion.where_ref, bf16[256,6144]{1,0:T(8,128)(2,1)} %acts_ref.2, ...), custom_call_target="tpu_custom_call" | custom-call | tf_op jit(solution)/shard_map/pallas_call | solution.py:192
  3.8 1.1 %shard_map.94 = (bf16[2,2,2,192,128]{4,3,2,1,0:T(8,128)(2,1)S(1)}, bf16[2,2,2,192,128]{4,3,2,1,0:T(8,128)(2,1)S(1)}) custom-call(s32[4]{0:T(128)S(1)} %pad_add_fusion.where_ref, bf16[4,256,768]{2,1,0:T(8,128)(2,1)S(1)} %get-tuple-element.34.columns, bf16[128,256]{1,0:T(8,128)(2,1)S(1)} %get-tuple-element.35.turned_ref), custom_call_target="tpu_custom_call" | custom-call | flops 201326592 | bytes 1572864 | tf_op jit(solution)/shard_map/pallas_call | solution.py:209
  5.7 2.7 %collective-permute-start.4 = (bf16[2,2,192,128]{3,2,1,0:T(8,128)(2,1)S(1)}, bf16[2,2,192,128]{3,2,1,0:T(8,128)(2,1)S(1)}, u32[]{:S(2)}, u32[]{:S(2)}) collective-permute-start(bf16[2,2,192,128]{3,2,1,0:T(8,128)(2,1)S(1)} %slice.35), channel_id=1, source_target_pairs={{0,1},{1,0},{2,14},{3,15},{4,5},{5,4},{6,10},{7,11},{8,9},{9,8},{1... | collective-permute-start | bytes 589832 | tf_op jit(solution)/shard_map/ppermute | solution.py:161
  8.6 1.6 %collective-permute-start.2 = (bf16[2,2,192,128]{3,2,1,0:T(8,128)(2,1)S(1)}, bf16[2,2,192,128]{3,2,1,0:T(8,128)(2,1)S(1)}, u32[]{:S(2)}, u32[]{:S(2)}) collective-permute-start(bf16[2,2,192,128]{3,2,1,0:T(8,128)(2,1)S(1)} %get-tuple-element.70), channel_id=1, source_target_pairs={{0,4},{1,5},{2,11},{3,10},{4,0},{5,1},{6,15},{7,14},{8,12},{9,13},... | collective-permute-start | bytes 589832 | tf_op jit(solution)/shard_map/ppermute | solution.py:161
  10.1 1.6 %collective-permute-start.3 = (bf16[2,2,192,128]{3,2,1,0:T(8,128)(2,1)S(1)}, bf16[2,2,192,128]{3,2,1,0:T(8,128)(2,1)S(1)}, u32[]{:S(2)}, u32[]{:S(2)}) collective-permute-start(bf16[2,2,192,128]{3,2,1,0:T(8,128)(2,1)S(1)} %get-tuple-element.69), channel_id=1, source_target_pairs={{0,8},{1,9},{2,7},{3,6},{4,12},{5,13},{6,3},{7,2},{8,0},{9,1},{10,... | collective-permute-start | bytes 589832 | tf_op jit(solution)/shard_map/ppermute | solution.py:161
  11.7 1.3 %collective-permute-start.5 = (bf16[2,192,128]{2,1,0:T(8,128)(2,1)S(1)}, bf16[2,192,128]{2,1,0:T(8,128)(2,1)S(1)}, u32[]{:S(2)}, u32[]{:S(2)}) collective-permute-start(bf16[2,192,128]{2,1,0:T(8,128)(2,1)S(1)} %slice_bitcast_fusion.4), channel_id=1, source_target_pairs={{0,13},{1,12},{2,15},{3,14},{4,9},{5,8},{6,11},{7,10},{8,5},{9,4},... | collective-permute-start | bytes 294920 | tf_op jit(solution)/shard_map/ppermute | solution.py:161
  13.0 7.2 %collective-permute-done.5 = bf16[2,192,128]{2,1,0:T(8,128)(2,1)S(1)} collective-permute-done((bf16[2,192,128]{2,1,0:T(8,128)(2,1)S(1)}, bf16[2,192,128]{2,1,0:T(8,128)(2,1)S(1)}, u32[]{:S(2)}, u32[]{:S(2)}) %collective-permute-start.5) | collective-permute-done | bytes 98336 | tf_op jit(solution)/shard_map/ppermute | solution.py:161
  20.4 1.4 %collective-permute-done.6 = f32[2,192,128]{2,1,0:T(8,128)S(1)} collective-permute-done((f32[2,192,128]{2,1,0:T(8,128)S(1)}, f32[2,192,128]{2,1,0:T(8,128)S(1)}, u32[]{:S(2)}, u32[]{:S(2)}) %collective-permute-start.6) | collective-permute-done | bytes 196640 | tf_op jit(solution)/shard_map/ppermute | solution.py:151
  21.9 2.7 %collective-permute-start.7 = (bf16[192,128]{1,0:T(8,128)(2,1)S(1)}, bf16[192,128]{1,0:T(8,128)(2,1)S(1)}, u32[]{:S(2)}, u32[]{:S(2)}) collective-permute-start(bf16[192,128]{1,0:T(8,128)(2,1)S(1)} %fusion.13), channel_id=1, source_target_pairs={{0,16},{16,0},{1,17},{17,1},{2,18},{18,2},{3,19},{19,3},{4,20},{20... | collective-permute-start | bytes 147464 | tf_op jit(solution)/shard_map/ppermute | solution.py:151
  25.3 2.7 %collective-permute-done.7 = bf16[192,128]{1,0:T(8,128)(2,1)S(1)} collective-permute-done((bf16[192,128]{1,0:T(8,128)(2,1)S(1)}, bf16[192,128]{1,0:T(8,128)(2,1)S(1)}, u32[]{:S(2)}, u32[]{:S(2)}) %collective-permute-start.7) | collective-permute-done | bytes 49184 | tf_op jit(solution)/shard_map/ppermute | solution.py:151
  28.1 1.6 %collective-permute-start.8 = (bf16[192,128]{1,0:T(8,128)(2,1)S(1)}, bf16[192,128]{1,0:T(8,128)(2,1)S(1)}, u32[]{:S(2)}, u32[]{:S(2)}) collective-permute-start(bf16[192,128]{1,0:T(8,128)(2,1)S(1)} %get-tuple-element.65), channel_id=1, source_target_pairs={{0,16},{16,0},{1,17},{17,1},{2,18},{18,2},{3,19},{19,3},{4,20},{20... | collective-permute-start | bytes 147464 | tf_op jit(solution)/shard_map/ppermute | solution.py:151
  29.7 0.9 %collective-permute-start.10 = (f32[192,128]{1,0:T(8,128)S(1)}, f32[192,128]{1,0:T(8,128)S(1)}, u32[]{:S(2)}, u32[]{:S(2)}) collective-permute-start(f32[192,128]{1,0:T(8,128)S(1)} %get-tuple-element.66), channel_id=1, source_target_pairs={{0,1},{1,0},{2,3},{3,2},{4,5},{5,4},{6,7},{7,6},{8,9},{9,8},{10,11... | collective-permute-start | bytes 294920 | tf_op jit(solution)/shard_map/ppermute | solution.py:151
  30.6 3.1 %collective-permute-done.8 = bf16[192,128]{1,0:T(8,128)(2,1)S(1)} collective-permute-done((bf16[192,128]{1,0:T(8,128)(2,1)S(1)}, bf16[192,128]{1,0:T(8,128)(2,1)S(1)}, u32[]{:S(2)}, u32[]{:S(2)}) %collective-permute-start.8) | collective-permute-done | bytes 49184 | tf_op jit(solution)/shard_map/ppermute | solution.py:151
  34.3 0.7 %collective-permute-done.9 = bf16[2,192,128]{2,1,0:T(8,128)(2,1)S(1)} collective-permute-done((bf16[2,192,128]{2,1,0:T(8,128)(2,1)S(1)}, bf16[2,192,128]{2,1,0:T(8,128)(2,1)S(1)}, u32[]{:S(2)}, u32[]{:S(2)}) %collective-permute-start.9) | collective-permute-done | bytes 98336 | tf_op jit(solution)/shard_map/ppermute | solution.py:151
  35.1 1.5 %collective-permute-start.11 = (bf16[2,2,192,128]{3,2,1,0:T(8,128)(2,1)S(1)}, bf16[2,2,192,128]{3,2,1,0:T(8,128)(2,1)S(1)}, u32[]{:S(2)}, u32[]{:S(2)}) collective-permute-start(bf16[2,2,192,128]{3,2,1,0:T(8,128)(2,1)S(1)} %maximum_select_fusion), channel_id=1, source_target_pairs={{0,4},{1,5},{2,11},{3,10},{4,0},{5,1},{6,15},{7,14},{8,12},{9,13},... | collective-permute-start | bytes 589832 | tf_op jit(solution)/shard_map/ppermute | solution.py:161
  36.6 1.5 %collective-permute-start.15 = (bf16[2,2,192,128]{3,2,1,0:T(8,128)(2,1)S(1)}, bf16[2,2,192,128]{3,2,1,0:T(8,128)(2,1)S(1)}, u32[]{:S(2)}, u32[]{:S(2)}) collective-permute-start(bf16[2,2,192,128]{3,2,1,0:T(8,128)(2,1)S(1)} %maximum_select_fusion), channel_id=1, source_target_pairs={{0,8},{1,9},{2,7},{3,6},{4,12},{5,13},{6,3},{7,2},{8,0},{9,1},{10,... | collective-permute-start | bytes 589832 | tf_op jit(solution)/shard_map/ppermute | solution.py:161
  38.7 1.4 %collective-permute-start.12 = (bf16[2,192,128]{2,1,0:T(8,128)(2,1)S(1)}, bf16[2,192,128]{2,1,0:T(8,128)(2,1)S(1)}, u32[]{:S(2)}, u32[]{:S(2)}) collective-permute-start(bf16[2,192,128]{2,1,0:T(8,128)(2,1)S(1)} %get-tuple-element.47), channel_id=1, source_target_pairs={{0,13},{1,12},{2,15},{3,14},{4,9},{5,8},{6,11},{7,10},{8,5},{9,4},... | collective-permute-start | bytes 294920 | tf_op jit(solution)/shard_map/ppermute | solution.py:161
  40.1 0.9 %multiply_subtract_fusion = (f32[384,128]{1,0:T(8,128)}, f32[384,128]{1,0:T(8,128)}, f32[384,128]{1,0:T(8,128)}) fusion(f32[384,128]{1,0:T(8,128)S(1)} %copy-done, f32[]{:T(128)} %bitcast.16, f32[]{:T(128)} %bitcast.14, f32[192,128]{1,0:T(8,128)S(1)} %get-tuple-element.66, f32[192,128]{1,0:T(8,128)S(1)} %collective-permute-done.10, pred[]{:T(512)S(6)} %eq.7, ...), kind=kLoop, calls=%fused_computation.14 | loop fusion | flops 884736 | bytes 1376265 | tf_op jit(solution)/shard_map/sub | solution.py:26
  41.0 2.5 %shard_map.95 = (bf16[4,256,768]{2,1,0:T(8,128)(2,1)S(1)}, bf16[4,256,768]{2,1,0:T(8,128)(2,1)S(1)}) custom-call(s32[4]{0:T(128)S(1)} %pad_add_fusion.where_ref, bf16[256,6144]{1,0:T(8,128)(2,1)} %acts_ref.2), custom_call_target="tpu_custom_call" | custom-call | tf_op jit(solution)/shard_map/pallas_call | solution.py:282
  43.5 3.3 %collective-permute-done.12 = bf16[2,192,128]{2,1,0:T(8,128)(2,1)S(1)} collective-permute-done((bf16[2,192,128]{2,1,0:T(8,128)(2,1)S(1)}, bf16[2,192,128]{2,1,0:T(8,128)(2,1)S(1)}, u32[]{:S(2)}, u32[]{:S(2)}) %collective-permute-start.12) | collective-permute-done | bytes 98336 | tf_op jit(solution)/shard_map/ppermute | solution.py:161
  46.9 1.2 %collective-permute-start.16 = (bf16[4,2,192,128]{3,2,1,0:T(8,128)(2,1)S(1)}, bf16[4,2,192,128]{3,2,1,0:T(8,128)(2,1)S(1)}, u32[]{:S(2)}, u32[]{:S(2)}) collective-permute-start(bf16[4,2,192,128]{3,2,1,0:T(8,128)(2,1)S(1)} %constant_dynamic-update-slice_fusion.refs_0_), channel_id=1, source_target_pairs={{0,2},{2,0},{1,3},{3,1},{4,6},{6,4},{5,7},{7,5},{8,10},{10,8},{9,1... | collective-permute-start | bytes 1179656 | tf_op jit(solution)/shard_map/ppermute | solution.py:151
  48.2 1.2 %collective-permute-done.16.refs_1_ = bf16[4,2,192,128]{3,2,1,0:T(8,128)(2,1)S(1)} collective-permute-done((bf16[4,2,192,128]{3,2,1,0:T(8,128)(2,1)S(1)}, bf16[4,2,192,128]{3,2,1,0:T(8,128)(2,1)S(1)}, u32[]{:S(2)}, u32[]{:S(2)}) %collective-permute-start.16) | collective-permute-done | bytes 393248 | tf_op jit(solution)/shard_map/ppermute | solution.py:151
  49.5 1.2 %shard_map.96.refs_4_ = f32[256,128]{1,0:T(8,128)S(1)} custom-call(s32[4]{0:T(128)S(1)} %pad_add_fusion.where_ref, bf16[4,256,768]{2,1,0:T(8,128)(2,1)S(1)} %get-tuple-element.60.columns_ref, bf16[4,2,192,128]{3,2,1,0:T(8,128)(2,1)S(1)} %constant_dynamic-update-slice_fusion.refs_0_, bf16[4,2,192,128]{3,2,1,0:T(8,128)(2,1)S(1)} %collective-permute-done.16.refs_1_), custom_call_target="tpu_custom_call" | custom-call | tf_op jit(solution)/shard_map/pallas_call | solution.py:302
  50.6 1.8 %shard_map.97 = bf16[256,128]{1,0:T(8,128)(2,1)} custom-call(s32[4]{0:T(128)S(1)} %pad_add_fusion.where_ref, bf16[4,256,768]{2,1,0:T(8,128)(2,1)S(1)} %get-tuple-element.58.columns_ref, bf16[3,2,192,128]{3,2,1,0:T(8,128)(2,1)S(1)} %pad_maximum_fusion.refs_0_, bf16[3,2,192,128]{3,2,1,0:T(8,128)(2,1)S(1)} %collective-permute-done.14.refs_1_, ...), custom_call_target="tpu_custom_call" | custom-call | tf_op jit(solution)/shard_map/pallas_call | solution.py:302
  (38 shorter events, 3.3 us)
Async XLA Ops:
  3.3 1.9 %collective-permute-start = (bf16[4,2,192,128]{3,2,1,0:T(8,128)(2,1)S(1)}, bf16[4,2,192,128]{3,2,1,0:T(8,128)(2,1)S(1)}, u32[]{:S(2)}, u32[]{:S(2)}) collective-permute-start(bf16[4,2,192,128]{3,2,1,0:T(8,128)(2,1)S(1)} %get-tuple-element.37), channel_id=1, source_target_pairs={{0,2},{2,0},{1,3},{3,1},{4,6},{6,4},{5,7},{7,5},{8,10},{10,8},{9,1... | collective-permute-start | bytes 1179656 | tf_op jit(solution)/shard_map/ppermute | solution.py:151
  5.2 3.2 %collective-permute-start.1 = (bf16[2,2,2,192,128]{4,3,2,1,0:T(8,128)(2,1)S(1)}, bf16[2,2,2,192,128]{4,3,2,1,0:T(8,128)(2,1)S(1)}, u32[]{:S(2)}, u32[]{:S(2)}) collective-permute-start(bf16[2,2,2,192,128]{4,3,2,1,0:T(8,128)(2,1)S(1)} %get-tuple-element.39), channel_id=1, source_target_pairs={{0,2},{2,0},{1,3},{3,1},{4,6},{6,4},{5,7},{7,5},{8,10},{10,8},{9,1... | collective-permute-start | bytes 1179656 | tf_op jit(solution)/shard_map/ppermute | solution.py:151
  5.7 14.5 %collective-permute-start.4 = (bf16[2,2,192,128]{3,2,1,0:T(8,128)(2,1)S(1)}, bf16[2,2,192,128]{3,2,1,0:T(8,128)(2,1)S(1)}, u32[]{:S(2)}, u32[]{:S(2)}) collective-permute-start(bf16[2,2,192,128]{3,2,1,0:T(8,128)(2,1)S(1)} %slice.35), channel_id=1, source_target_pairs={{0,1},{1,0},{2,14},{3,15},{4,5},{5,4},{6,10},{7,11},{8,9},{9,8},{1... | collective-permute-start | bytes 589832 | tf_op jit(solution)/shard_map/ppermute | solution.py:161
  8.6 11.6 %collective-permute-start.2 = (bf16[2,2,192,128]{3,2,1,0:T(8,128)(2,1)S(1)}, bf16[2,2,192,128]{3,2,1,0:T(8,128)(2,1)S(1)}, u32[]{:S(2)}, u32[]{:S(2)}) collective-permute-start(bf16[2,2,192,128]{3,2,1,0:T(8,128)(2,1)S(1)} %get-tuple-element.70), channel_id=1, source_target_pairs={{0,4},{1,5},{2,11},{3,10},{4,0},{5,1},{6,15},{7,14},{8,12},{9,13},... | collective-permute-start | bytes 589832 | tf_op jit(solution)/shard_map/ppermute | solution.py:161
  10.1 10.1 %collective-permute-start.3 = (bf16[2,2,192,128]{3,2,1,0:T(8,128)(2,1)S(1)}, bf16[2,2,192,128]{3,2,1,0:T(8,128)(2,1)S(1)}, u32[]{:S(2)}, u32[]{:S(2)}) collective-permute-start(bf16[2,2,192,128]{3,2,1,0:T(8,128)(2,1)S(1)} %get-tuple-element.69), channel_id=1, source_target_pairs={{0,8},{1,9},{2,7},{3,6},{4,12},{5,13},{6,3},{7,2},{8,0},{9,1},{10,... | collective-permute-start | bytes 589832 | tf_op jit(solution)/shard_map/ppermute | solution.py:161
  11.7 8.5 %collective-permute-start.5 = (bf16[2,192,128]{2,1,0:T(8,128)(2,1)S(1)}, bf16[2,192,128]{2,1,0:T(8,128)(2,1)S(1)}, u32[]{:S(2)}, u32[]{:S(2)}) collective-permute-start(bf16[2,192,128]{2,1,0:T(8,128)(2,1)S(1)} %slice_bitcast_fusion.4), channel_id=1, source_target_pairs={{0,13},{1,12},{2,15},{3,14},{4,9},{5,8},{6,11},{7,10},{8,5},{9,4},... | collective-permute-start | bytes 294920 | tf_op jit(solution)/shard_map/ppermute | solution.py:161
  20.3 19.9 %copy-start = (f32[384,128]{1,0:T(8,128)S(1)}, f32[384,128]{1,0:T(8,128)}, u32[]{:S(2)}) copy-start(f32[384,128]{1,0:T(8,128)} %refs_0_.1) | copy-start | bytes 589828
  20.3 19.8 %copy-start.1 = (f32[384,128]{1,0:T(8,128)S(1)}, f32[384,128]{1,0:T(8,128)}, u32[]{:S(2)}) copy-start(f32[384,128]{1,0:T(8,128)} %refs_1_.1) | copy-start | bytes 589828
  20.3 19.8 %copy-start.2 = (f32[384,128]{1,0:T(8,128)S(1)}, f32[384,128]{1,0:T(8,128)}, u32[]{:S(2)}) copy-start(f32[384,128]{1,0:T(8,128)} %refs_2_.1) | copy-start | bytes 589828
  20.4 1.5 %collective-permute-start.6 = (f32[2,192,128]{2,1,0:T(8,128)S(1)}, f32[2,192,128]{2,1,0:T(8,128)S(1)}, u32[]{:S(2)}, u32[]{:S(2)}) collective-permute-start(f32[2,192,128]{2,1,0:T(8,128)S(1)} %dynamic-slice_bitcast_fusion), channel_id=1, source_target_pairs={{0,2},{2,0},{1,3},{3,1},{4,6},{6,4},{5,7},{7,5},{8,10},{10,8},{9,1... | collective-permute-start | bytes 589832 | tf_op jit(solution)/shard_map/ppermute | solution.py:151
  21.9 6.1 %collective-permute-start.7 = (bf16[192,128]{1,0:T(8,128)(2,1)S(1)}, bf16[192,128]{1,0:T(8,128)(2,1)S(1)}, u32[]{:S(2)}, u32[]{:S(2)}) collective-permute-start(bf16[192,128]{1,0:T(8,128)(2,1)S(1)} %fusion.13), channel_id=1, source_target_pairs={{0,16},{16,0},{1,17},{17,1},{2,18},{18,2},{3,19},{19,3},{4,20},{20... | collective-permute-start | bytes 147464 | tf_op jit(solution)/shard_map/ppermute | solution.py:151
  28.1 5.6 %collective-permute-start.8 = (bf16[192,128]{1,0:T(8,128)(2,1)S(1)}, bf16[192,128]{1,0:T(8,128)(2,1)S(1)}, u32[]{:S(2)}, u32[]{:S(2)}) collective-permute-start(bf16[192,128]{1,0:T(8,128)(2,1)S(1)} %get-tuple-element.65), channel_id=1, source_target_pairs={{0,16},{16,0},{1,17},{17,1},{2,18},{18,2},{3,19},{19,3},{4,20},{20... | collective-permute-start | bytes 147464 | tf_op jit(solution)/shard_map/ppermute | solution.py:151
  29.7 4.6 %collective-permute-start.10 = (f32[192,128]{1,0:T(8,128)S(1)}, f32[192,128]{1,0:T(8,128)S(1)}, u32[]{:S(2)}, u32[]{:S(2)}) collective-permute-start(f32[192,128]{1,0:T(8,128)S(1)} %get-tuple-element.66), channel_id=1, source_target_pairs={{0,1},{1,0},{2,3},{3,2},{4,5},{5,4},{6,7},{7,6},{8,9},{9,8},{10,11... | collective-permute-start | bytes 294920 | tf_op jit(solution)/shard_map/ppermute | solution.py:151
  33.7 1.4 %collective-permute-start.9 = (bf16[2,192,128]{2,1,0:T(8,128)(2,1)S(1)}, bf16[2,192,128]{2,1,0:T(8,128)(2,1)S(1)}, u32[]{:S(2)}, u32[]{:S(2)}) collective-permute-start(bf16[2,192,128]{2,1,0:T(8,128)(2,1)S(1)} %get-tuple-element.47), channel_id=1, source_target_pairs={{0,2},{2,0},{1,3},{3,1},{4,6},{6,4},{5,7},{7,5},{8,10},{10,8},{9,1... | collective-permute-start | bytes 294920 | tf_op jit(solution)/shard_map/ppermute | solution.py:151
  35.1 11.7 %collective-permute-start.11 = (bf16[2,2,192,128]{3,2,1,0:T(8,128)(2,1)S(1)}, bf16[2,2,192,128]{3,2,1,0:T(8,128)(2,1)S(1)}, u32[]{:S(2)}, u32[]{:S(2)}) collective-permute-start(bf16[2,2,192,128]{3,2,1,0:T(8,128)(2,1)S(1)} %maximum_select_fusion), channel_id=1, source_target_pairs={{0,4},{1,5},{2,11},{3,10},{4,0},{5,1},{6,15},{7,14},{8,12},{9,13},... | collective-permute-start | bytes 589832 | tf_op jit(solution)/shard_map/ppermute | solution.py:161
  36.6 10.2 %collective-permute-start.15 = (bf16[2,2,192,128]{3,2,1,0:T(8,128)(2,1)S(1)}, bf16[2,2,192,128]{3,2,1,0:T(8,128)(2,1)S(1)}, u32[]{:S(2)}, u32[]{:S(2)}) collective-permute-start(bf16[2,2,192,128]{3,2,1,0:T(8,128)(2,1)S(1)} %maximum_select_fusion), channel_id=1, source_target_pairs={{0,8},{1,9},{2,7},{3,6},{4,12},{5,13},{6,3},{7,2},{8,0},{9,1},{10,... | collective-permute-start | bytes 589832 | tf_op jit(solution)/shard_map/ppermute | solution.py:161
  38.1 10.0 %collective-permute-start.13 = (bf16[2,2,192,128]{3,2,1,0:T(8,128)(2,1)S(1)}, bf16[2,2,192,128]{3,2,1,0:T(8,128)(2,1)S(1)}, u32[]{:S(2)}, u32[]{:S(2)}) collective-permute-start(bf16[2,2,192,128]{3,2,1,0:T(8,128)(2,1)S(1)} %maximum_select_fusion), channel_id=1, source_target_pairs={{0,1},{1,0},{2,14},{3,15},{4,5},{5,4},{6,10},{7,11},{8,9},{9,8},{1... | collective-permute-start | bytes 589832 | tf_op jit(solution)/shard_map/ppermute | solution.py:161
  38.7 8.1 %collective-permute-start.12 = (bf16[2,192,128]{2,1,0:T(8,128)(2,1)S(1)}, bf16[2,192,128]{2,1,0:T(8,128)(2,1)S(1)}, u32[]{:S(2)}, u32[]{:S(2)}) collective-permute-start(bf16[2,192,128]{2,1,0:T(8,128)(2,1)S(1)} %get-tuple-element.47), channel_id=1, source_target_pairs={{0,13},{1,12},{2,15},{3,14},{4,9},{5,8},{6,11},{7,10},{8,5},{9,4},... | collective-permute-start | bytes 294920 | tf_op jit(solution)/shard_map/ppermute | solution.py:161
  46.9 2.6 %collective-permute-start.16 = (bf16[4,2,192,128]{3,2,1,0:T(8,128)(2,1)S(1)}, bf16[4,2,192,128]{3,2,1,0:T(8,128)(2,1)S(1)}, u32[]{:S(2)}, u32[]{:S(2)}) collective-permute-start(bf16[4,2,192,128]{3,2,1,0:T(8,128)(2,1)S(1)} %constant_dynamic-update-slice_fusion.refs_0_), channel_id=1, source_target_pairs={{0,2},{2,0},{1,3},{3,1},{4,6},{6,4},{5,7},{7,5},{8,10},{10,8},{9,1... | collective-permute-start | bytes 1179656 | tf_op jit(solution)/shard_map/ppermute | solution.py:151
  48.1 2.5 %collective-permute-start.14 = (bf16[3,2,192,128]{3,2,1,0:T(8,128)(2,1)S(1)}, bf16[3,2,192,128]{3,2,1,0:T(8,128)(2,1)S(1)}, u32[]{:S(2)}, u32[]{:S(2)}) collective-permute-start(bf16[3,2,192,128]{3,2,1,0:T(8,128)(2,1)S(1)} %pad_maximum_fusion.refs_0_), channel_id=1, source_target_pairs={{0,2},{2,0},{1,3},{3,1},{4,6},{6,4},{5,7},{7,5},{8,10},{10,8},{9,1... | collective-permute-start | bytes 884744 | tf_op jit(solution)/shard_map/ppermute | solution.py:151

commit v17 on v15

--- a/solution.py
+++ b/solution.py
@@ -19,6 +19,10 @@
 def slot_of(chip, core):
     slot = CHIPS.index(chip)
     return slot if slot >= 6 else slot ^ core
+
+
+def position():
+    return [lax.axis_index(axis) for axis in AXES]
 
 
 def adamw(grad, master, moment_one, moment_two, step_count):
@@ -33,21 +37,21 @@
     return updated, first, second
 
 
-def load_columns(acts_ref, columns, sems, high, low, lows, n_high):
-    wide = columns.shape[-1]
+def load_columns(acts_ref, slices, sems, lows, n_high, wide):
+    high, low, _, _ = position()
     copies = []
     for p, k in enumerate(lows):
         for j in range(n_high):
             column = pl.multiple_of(((high ^ j) * N_LOW + (low ^ k)) * wide, wide)
             n = p * n_high + j
-            copy = pltpu.make_async_copy(acts_ref.at[:, pl.ds(column, wide)], columns.at[n], sems.at[n])
+            copy = pltpu.make_async_copy(acts_ref.at[:, pl.ds(column, wide)], slices(n), sems.at[n])
             copy.start()
             copies.append(copy)
     return copies
 
 
-def sort_products(n_high, group, where_ref, turned, columns, away, kept, blocks, arrived):
-    core, rep = where_ref[2], where_ref[3]
+def sort_products(n_high, group, turned, columns, away, kept, blocks, arrived):
+    _, _, core, rep = position()
     for n in range(2 * n_high):
         arrived(n)
         product = jnp.dot(turned, columns[n], preferred_element_type=jnp.float32)
@@ -59,15 +63,15 @@
                 out[slot - 4 * group, j] = blocks[owner, rep ^ d_rep]
 
 
-def first_grad_kernel(n_high, where_ref, acts_ref, grad_ref, *refs):
+def first_grad_kernel(n_high, acts_ref, grad_ref, *refs):
     state_refs, refs = refs[:3], refs[3:]
     away, kept, mine_ref, later_ref, turned_ref, columns, logit_grads, blocks, sems = refs
-    high, low, _, rep = [where_ref[i] for i in range(4)]
+    _, _, _, rep = position()
     half = blocks.shape[2]
     loads = pltpu.make_async_copy(grad_ref, logit_grads, sems.at[2, 0])
     loads.start()
-    first = load_columns(acts_ref, columns, sems.at[0], high, low, LOWS[1], n_high)
-    others = load_columns(acts_ref, later_ref, sems.at[1], high, low, LOWS[0], n_high)
+    first = load_columns(acts_ref, lambda n: columns.at[n], sems.at[0], LOWS[1], n_high, 4 * half)
+    others = load_columns(acts_ref, lambda n: later_ref.at[n], sems.at[1], LOWS[0], n_high, 4 * half)
     rows = pl.ds(pl.multiple_of(rep * half, half), half)
     for i, ref in enumerate(state_refs):
         copy = pltpu.make_async_copy(ref.at[rows], mine_ref.at[i], sems.at[2, 1 + i])
@@ -82,42 +86,42 @@
             first[n].wait()
             first[n + 1].wait()
 
-    sort_products(n_high, 1, where_ref, turned, columns, away, kept, blocks, arrived)
+    sort_products(n_high, 1, turned, columns, away, kept, blocks, arrived)
     for copy in others:
         copy.wait()
 
 
-def second_grad_kernel(n_high, where_ref, columns, turned_ref, away, kept, blocks):
-    sort_products(n_high, 0, where_ref, turned_ref[...], columns, away, kept, blocks, lambda n: None)
-
-
-def columns_kernel(n_high, where_ref, acts_ref, first_ref, second_ref, sems):
-    high, low = where_ref[0], where_ref[1]
+def second_grad_kernel(n_high, columns, turned_ref, away, kept, blocks):
+    sort_products(n_high, 0, turned_ref[...], columns, away, kept, blocks, lambda n: None)
+
+
+def columns_kernel(n_high, wide, acts_ref, first_ref, second_ref, sems):
     copies = []
     for i, (lows, out) in enumerate(zip(LOWS, (first_ref, second_ref))):
-        copies += load_columns(acts_ref, out, sems.at[i], high, low, lows, n_high)
+        slices = lambda n, out=out: out.at[:, pl.ds(n * wide, wide)]
+        copies += load_columns(acts_ref, slices, sems.at[i], lows, n_high, wide)
     for copy in copies:
         copy.wait()
 
 
-def logits_kernel(n_high, group, where_ref, columns_ref, *refs):
+def logits_kernel(n_high, group, columns_ref, *refs):
     *pieces, out_ref, weight = refs
     before = None
     if len(pieces[-1].shape) == 2:
         *pieces, before = pieces
+    _, _, core, rep = position()
     half, experts = weight.shape[-2:]
-    for piece, blocks in zip(pieces, places(group, where_ref[2], where_ref[3])):
+    for piece, blocks in zip(pieces, places(group, core, rep)):
         for n, (place, owner, of_rep) in enumerate(blocks):
             for j in range(n_high):
                 weight[place, j, owner, of_rep] = piece[n, j]
-    total = None if before is None else before[...]
-    for n in range(2 * n_high):
-        part = jnp.dot(
-            columns_ref[n],
-            weight[n // n_high, n % n_high].reshape(4 * half, experts),
-            preferred_element_type=jnp.float32,
-        )
-        total = part if total is None else total + part
+    total = jnp.dot(
+        columns_ref[...],
+        weight[...].reshape(8 * n_high * half, experts),
+        preferred_element_type=jnp.float32,
+    )
+    if before is not None:
+        total = total + before[...]
     out_ref[...] = total.astype(out_ref.dtype)
 
 
@@ -168,12 +172,10 @@
         tokens, experts = grad_logits.shape
         rows = master.shape[0]
         half = rows // n_rep
-        high, low, core, rep = (lax.axis_index(a) for a in AXES)
-        where = jnp.stack([high, low, core, rep])
+        high, low, core, rep = position()
         f32, bf16 = jnp.float32, jnp.bfloat16
         in_kernels = half % 16 == 0 and (4 * half) % 128 == 0
 
-        smem = pl.BlockSpec(memory_space=pltpu.SMEM)
         vmem = pl.BlockSpec(memory_space=pltpu.VMEM)
         anywhere = pl.BlockSpec(memory_space=pl.ANY)
         params = pltpu.CompilerParams(vmem_limit_bytes=VMEM_LIMIT)
@@ -188,7 +190,7 @@
             away_second, kept_second, mine, later, turned = pl.pallas_call(
                 functools.partial(first_grad_kernel, n_high),
                 out_shape=[shape, shape, pltpu.VMEM((3, half, experts), f32), columns_shape, turned],
-                in_specs=[smem] + [anywhere] * 5,
+                in_specs=[anywhere] * 5,
                 out_specs=[vmem] * 5,
                 scratch_shapes=[
                     columns_shape,
@@ -198,14 +200,13 @@
                 ],
                 compiler_params=params,
             )(
-                where,
                 acts,
                 *(pltpu.with_memory_space_constraint(x, pltpu.HBM) for x in (grad_logits, *state_in)),
             )
             away_first, kept_first = pl.pallas_call(
                 functools.partial(second_grad_kernel, n_high),
                 out_shape=[shape, shape],
-                in_specs=[smem, vmem, vmem],
+                in_specs=[vmem, vmem],
                 out_specs=[vmem] * 2,
                 scratch_shapes=[blocks],
                 cost_estimate=pl.CostEstimate(
@@ -214,7 +215,7 @@
                     transcendentals=0,
                 ),
                 compiler_params=params,
-            )(where, *(pltpu.with_memory_space_constraint(x, pltpu.VMEM) for x in (later, turned)))
+            )(*(pltpu.with_memory_space_constraint(x, pltpu.VMEM) for x in (later, turned)))
             away, kept = (away_first, away_second), (kept_first, kept_second)
         else:
             product = lax.dot_general(
@@ -272,13 +273,13 @@
         if in_kernels:
             state, late_acts = lax.optimization_barrier((state, acts))
             columns = pl.pallas_call(
-                functools.partial(columns_kernel, n_high),
-                out_shape=(pltpu.VMEM((2 * n_high, tokens, 4 * half), bf16),) * 2,
-                in_specs=[smem, anywhere],
+                functools.partial(columns_kernel, n_high, 4 * half),
+                out_shape=(pltpu.VMEM((tokens, 8 * n_high * half), bf16),) * 2,
+                in_specs=[anywhere],
                 out_specs=(vmem, vmem),
                 scratch_shapes=[pltpu.SemaphoreType.DMA((2, 2 * n_high))],
                 compiler_params=params,
-            )(where, pltpu.with_memory_space_constraint(late_acts, pltpu.HBM))
+            )(pltpu.with_memory_space_constraint(late_acts, pltpu.HBM))
         got[0], corner, state, columns = lax.optimization_barrier((got[0], corner, state, columns))
         first, second = jnp.concatenate(got[:2]), jnp.concatenate([got[2], corner[None]])
         first, second = [first, swap(first, "core")], [second, swap(second, "core")]
@@ -294,11 +295,11 @@
                 logits = pl.pallas_call(
                     functools.partial(logits_kernel, n_high, group),
                     out_shape=jax.ShapeDtypeStruct((tokens, experts), bf16 if before else f32),
-                    in_specs=[smem] + [vmem] * len(operands),
+                    in_specs=[vmem] * len(operands),
                     out_specs=vmem,
                     scratch_shapes=[pltpu.VMEM((2, n_high, 2, 2, half, experts), bf16)],
                     compiler_params=params,
-                )(where, *operands)
+                )(*operands)
             else:
                 rows_at, values = [], []
                 for piece, blocks in zip(received, places(group, core, rep)):

time: 48.9 us -> 47.8 us (0.978)
  Pallas kernels: 9.07 us -> 6.43 us
  waiting for transfers between devices: 11.6 us -> 13.1 us
    pallas_call x2, Pallas kernels: 2.96 us -> 1.89 us  [per_device(): pl.pallas_call(functools.partial(logits_kernel, n_high, group), out_shape...]
    ppermute x8, waiting for transfers between devices: 3.59 us -> 4.63 us  [swap(): lax.ppermute(x, axis, [(i, i ^ mask) for i in range(fine.shape[axis])])]
    pallas_call x1, Pallas kernels: 2.46 us -> 1.91 us  [per_device(): pl.pallas_call(functools.partial(columns_kernel, n_high, 4 * half), out_s...]
    ppermute x11, waiting for transfers between devices: 7.97 us -> 8.52 us  [cube_swap(): return lax.ppermute(x, AXES[1:], pairs)]
    pallas_call x1, Pallas kernels: 2.6 us -> 2.06 us  [per_device(): pl.pallas_call(functools.partial(first_grad_kernel, n_high), out_shape=[s...]
    pallas_call x1, Pallas kernels: 1.06 us -> 0.57 us  [per_device(): pl.pallas_call(functools.partial(second_grad_kernel, n_high), out_shape=[...]
  transfers between devices with their start and end apart: 19 -> 19, of which waited for: 10 -> 10; matrix products, arithmetic and copies ran while one was open for 3% -> 3% of each run, Pallas kernels for 10% -> 7%
where the time goes in v17:
time: 47.8 us; the launch traced here: 47.7 us
  starting transfers between devices  25 us (52%)
  waiting for transfers between devices  13.1 us (27%)
  Pallas kernels  6.43 us (13%)
  between operations  1.55 us (3%)
  other arithmetic  1.38 us (3%)
    ppermute x11, starting transfers between devices, cube_swap(): return lax.ppermute(x, AXES[1:], pairs)  17 us
    ppermute x11, waiting for transfers between devices, cube_swap(): return lax.ppermute(x, AXES[1:], pairs)  8.52 us
    ppermute x8, starting transfers between devices, swap(): lax.ppermute(x, axis, [(i, i ^ mask) for i in range(fine.shape[axis])])  8.03 us
    ppermute x8, waiting for transfers between devices, swap(): lax.ppermute(x, axis, [(i, i ^ mask) for i in range(fine.shape[axis])])  4.63 us
    pallas_call x1, Pallas kernels, per_device(): pl.pallas_call(functools.partial(first_grad_kernel, n_high), out_shape=[s...  2.06 us
    pallas_call x1, Pallas kernels, per_device(): pl.pallas_call(functools.partial(columns_kernel, n_high, 4 * half), out_s...  1.91 us
    pallas_call x2, Pallas kernels, per_device(): pl.pallas_call(functools.partial(logits_kernel, n_high, group), out_shape...  1.89 us
  transfers between devices with their start and end apart: 19, of which 10 were waited for; matrix products, arithmetic and copies ran while one was open for 3% of the time, Pallas kernels for 7%

profile of v17, /device:TPU:0, one launch (start us, length us, event | category | flops | bytes accessed | tf_op | source)
XLA Modules:
  0.0 47.7 jit_solution(987903152766454101)
XLA Ops:
  0.6 2.1 %shard_map.93 = (bf16[4,2,192,128]{3,2,1,0:T(8,128)(2,1)S(1)}, bf16[4,2,192,128]{3,2,1,0:T(8,128)(2,1)S(1)}, f32[3,192,128]{2,1,0:T(8,128)S(1)}, bf16[4,256,768]{2,1,0:T(8,128)(2,1)S(1)}, bf16[128,256]{1,0:T(8,128)(2,1)S(1)}) custom-call(bf16[256,6144]{1,0:T(8,128)(2,1)} %acts_ref.2, bf16[256,128]{1,0:T(8,128)(2,1)} %grad_ref.1, f32[384,128]{1,0:T(8,128)} %refs_0_.1, ...), custom_call_target="tpu_custom_call" | custom-call | tf_op jit(solution)/shard_map/pallas_call | solution.py:190
  5.1 2.7 %collective-permute-start.6 = (bf16[2,192,128]{2,1,0:T(8,128)(2,1)S(1)}, bf16[2,192,128]{2,1,0:T(8,128)(2,1)S(1)}, u32[]{:S(2)}, u32[]{:S(2)}) collective-permute-start(bf16[2,192,128]{2,1,0:T(8,128)(2,1)S(1)} %get-tuple-element.77), channel_id=1, source_target_pairs={{0,1},{1,0},{2,14},{3,15},{4,5},{5,4},{6,10},{7,11},{8,9},{9,8},{1... | collective-permute-start | bytes 294920 | tf_op jit(solution)/shard_map/ppermute | solution.py:159
  7.8 2.5 %collective-permute-start.7 = (bf16[2,192,128]{2,1,0:T(8,128)(2,1)S(1)}, bf16[2,192,128]{2,1,0:T(8,128)(2,1)S(1)}, u32[]{:S(2)}, u32[]{:S(2)}) collective-permute-start(bf16[2,192,128]{2,1,0:T(8,128)(2,1)S(1)} %get-tuple-element.76), channel_id=1, source_target_pairs={{0,12},{1,13},{2,3},{3,2},{4,8},{5,9},{6,7},{7,6},{8,4},{9,5},{10,... | collective-permute-start | bytes 294920 | tf_op jit(solution)/shard_map/ppermute | solution.py:159
  10.5 1.9 %collective-permute-start.2 = (bf16[2,192,128]{2,1,0:T(8,128)(2,1)S(1)}, bf16[2,192,128]{2,1,0:T(8,128)(2,1)S(1)}, u32[]{:S(2)}, u32[]{:S(2)}) collective-permute-start(bf16[2,192,128]{2,1,0:T(8,128)(2,1)S(1)} %get-tuple-element.81), channel_id=1, source_target_pairs={{0,4},{1,5},{2,11},{3,10},{4,0},{5,1},{6,15},{7,14},{8,12},{9,13},... | collective-permute-start | bytes 294920 | tf_op jit(solution)/shard_map/ppermute | solution.py:159
  12.4 2.5 %collective-permute-start.3 = (bf16[2,192,128]{2,1,0:T(8,128)(2,1)S(1)}, bf16[2,192,128]{2,1,0:T(8,128)(2,1)S(1)}, u32[]{:S(2)}, u32[]{:S(2)}) collective-permute-start(bf16[2,192,128]{2,1,0:T(8,128)(2,1)S(1)} %get-tuple-element.80), channel_id=1, source_target_pairs={{0,9},{1,8},{2,6},{3,7},{4,13},{5,12},{6,2},{7,3},{8,1},{9,0},{10,... | collective-permute-start | bytes 294920 | tf_op jit(solution)/shard_map/ppermute | solution.py:159
  15.4 1.1 %collective-permute-start.5 = (bf16[2,192,128]{2,1,0:T(8,128)(2,1)S(1)}, bf16[2,192,128]{2,1,0:T(8,128)(2,1)S(1)}, u32[]{:S(2)}, u32[]{:S(2)}) collective-permute-start(bf16[2,192,128]{2,1,0:T(8,128)(2,1)S(1)} %get-tuple-element.78), channel_id=1, source_target_pairs={{0,5},{1,4},{2,10},{3,11},{4,1},{5,0},{6,14},{7,15},{8,13},{9,12},... | collective-permute-start | bytes 294920 | tf_op jit(solution)/shard_map/ppermute | solution.py:159
  16.6 1.9 %collective-permute-done.8 = bf16[2,192,128]{2,1,0:T(8,128)(2,1)S(1)} collective-permute-done((bf16[2,192,128]{2,1,0:T(8,128)(2,1)S(1)}, bf16[2,192,128]{2,1,0:T(8,128)(2,1)S(1)}, u32[]{:S(2)}, u32[]{:S(2)}) %collective-permute-start.8) | collective-permute-done | bytes 98336 | tf_op jit(solution)/shard_map/ppermute | solution.py:159
  18.7 1.1 %collective-permute-done.4 = bf16[2,192,128]{2,1,0:T(8,128)(2,1)S(1)} collective-permute-done((bf16[2,192,128]{2,1,0:T(8,128)(2,1)S(1)}, bf16[2,192,128]{2,1,0:T(8,128)(2,1)S(1)}, u32[]{:S(2)}, u32[]{:S(2)}) %collective-permute-start.4) | collective-permute-done | bytes 98336 | tf_op jit(solution)/shard_map/ppermute | solution.py:159
  19.9 1.1 %collective-permute-done.5 = bf16[2,192,128]{2,1,0:T(8,128)(2,1)S(1)} collective-permute-done((bf16[2,192,128]{2,1,0:T(8,128)(2,1)S(1)}, bf16[2,192,128]{2,1,0:T(8,128)(2,1)S(1)}, u32[]{:S(2)}, u32[]{:S(2)}) %collective-permute-start.5) | collective-permute-done | bytes 98336 | tf_op jit(solution)/shard_map/ppermute | solution.py:159
  21.1 2.6 %collective-permute-start.9 = (bf16[192,128]{1,0:T(8,128)(2,1)S(1)}, bf16[192,128]{1,0:T(8,128)(2,1)S(1)}, u32[]{:S(2)}, u32[]{:S(2)}) collective-permute-start(bf16[192,128]{1,0:T(8,128)(2,1)S(1)} %fusion.11), channel_id=1, source_target_pairs={{0,16},{16,0},{1,17},{17,1},{2,18},{18,2},{3,19},{19,3},{4,20},{20... | collective-permute-start | bytes 147464 | tf_op jit(solution)/shard_map/ppermute | solution.py:149
  24.5 1.7 %collective-permute-done.9 = bf16[192,128]{1,0:T(8,128)(2,1)S(1)} collective-permute-done((bf16[192,128]{1,0:T(8,128)(2,1)S(1)}, bf16[192,128]{1,0:T(8,128)(2,1)S(1)}, u32[]{:S(2)}, u32[]{:S(2)}) %collective-permute-start.9) | collective-permute-done | bytes 49184 | tf_op jit(solution)/shard_map/ppermute | solution.py:149
  26.2 2.7 %collective-permute-start.10 = (bf16[192,128]{1,0:T(8,128)(2,1)S(1)}, bf16[192,128]{1,0:T(8,128)(2,1)S(1)}, u32[]{:S(2)}, u32[]{:S(2)}) collective-permute-start(bf16[192,128]{1,0:T(8,128)(2,1)S(1)} %get-tuple-element.71), channel_id=1, source_target_pairs={{0,16},{16,0},{1,17},{17,1},{2,18},{18,2},{3,19},{19,3},{4,20},{20... | collective-permute-start | bytes 147464 | tf_op jit(solution)/shard_map/ppermute | solution.py:149
  28.9 1.1 %collective-permute-start.12 = (f32[192,128]{1,0:T(8,128)S(1)}, f32[192,128]{1,0:T(8,128)S(1)}, u32[]{:S(2)}, u32[]{:S(2)}) collective-permute-start(f32[192,128]{1,0:T(8,128)S(1)} %get-tuple-element.72), channel_id=1, source_target_pairs={{0,1},{1,0},{2,3},{3,2},{4,5},{5,4},{6,7},{7,6},{8,9},{9,8},{10,11... | collective-permute-start | bytes 294920 | tf_op jit(solution)/shard_map/ppermute | solution.py:149
  30.0 1.3 %collective-permute-done.10 = bf16[192,128]{1,0:T(8,128)(2,1)S(1)} collective-permute-done((bf16[192,128]{1,0:T(8,128)(2,1)S(1)}, bf16[192,128]{1,0:T(8,128)(2,1)S(1)}, u32[]{:S(2)}, u32[]{:S(2)}) %collective-permute-start.10) | collective-permute-done | bytes 49184 | tf_op jit(solution)/shard_map/ppermute | solution.py:149
  31.4 2.2 %collective-permute-start.14 = (bf16[2,192,128]{2,1,0:T(8,128)(2,1)S(1)}, bf16[2,192,128]{2,1,0:T(8,128)(2,1)S(1)}, u32[]{:S(2)}, u32[]{:S(2)}) collective-permute-start(bf16[2,192,128]{2,1,0:T(8,128)(2,1)S(1)} %get-tuple-element.83), channel_id=1, source_target_pairs={{0,13},{1,12},{2,15},{3,14},{4,9},{5,8},{6,11},{7,10},{8,5},{9,4},... | collective-permute-start | bytes 294920 | tf_op jit(solution)/shard_map/ppermute | solution.py:159
  33.6 1.3 %collective-permute-start.13 = (bf16[2,2,192,128]{3,2,1,0:T(8,128)(2,1)S(1)}, bf16[2,2,192,128]{3,2,1,0:T(8,128)(2,1)S(1)}, u32[]{:S(2)}, u32[]{:S(2)}) collective-permute-start(bf16[2,2,192,128]{3,2,1,0:T(8,128)(2,1)S(1)} %maximum_select_fusion), channel_id=1, source_target_pairs={{0,4},{1,5},{2,11},{3,10},{4,0},{5,1},{6,15},{7,14},{8,12},{9,13},... | collective-permute-start | bytes 589832 | tf_op jit(solution)/shard_map/ppermute | solution.py:159
  34.8 1.4 %collective-permute-start.17 = (bf16[2,2,192,128]{3,2,1,0:T(8,128)(2,1)S(1)}, bf16[2,2,192,128]{3,2,1,0:T(8,128)(2,1)S(1)}, u32[]{:S(2)}, u32[]{:S(2)}) collective-permute-start(bf16[2,2,192,128]{3,2,1,0:T(8,128)(2,1)S(1)} %maximum_select_fusion), channel_id=1, source_target_pairs={{0,8},{1,9},{2,7},{3,6},{4,12},{5,13},{6,3},{7,2},{8,0},{9,1},{10,... | collective-permute-start | bytes 589832 | tf_op jit(solution)/shard_map/ppermute | solution.py:159
  36.2 0.9 %collective-permute-start.15 = (bf16[2,2,192,128]{3,2,1,0:T(8,128)(2,1)S(1)}, bf16[2,2,192,128]{3,2,1,0:T(8,128)(2,1)S(1)}, u32[]{:S(2)}, u32[]{:S(2)}) collective-permute-start(bf16[2,2,192,128]{3,2,1,0:T(8,128)(2,1)S(1)} %maximum_select_fusion), channel_id=1, source_target_pairs={{0,1},{1,0},{2,14},{3,15},{4,5},{5,4},{6,10},{7,11},{8,9},{9,8},{1... | collective-permute-start | bytes 589832 | tf_op jit(solution)/shard_map/ppermute | solution.py:159
  37.2 0.9 %multiply_subtract_fusion = (f32[384,128]{1,0:T(8,128)}, f32[384,128]{1,0:T(8,128)}, f32[384,128]{1,0:T(8,128)}) fusion(f32[384,128]{1,0:T(8,128)S(1)} %copy-done, f32[]{:T(128)} %bitcast.14, f32[]{:T(128)} %bitcast.12, f32[192,128]{1,0:T(8,128)S(1)} %get-tuple-element.72, f32[192,128]{1,0:T(8,128)S(1)} %collective-permute-done.12, pred[]{:T(512)S(6)} %eq.7, ...), kind=kLoop, calls=%fused_computation.8 | loop fusion | flops 884736 | bytes 1376265 | tf_op jit(solution)/shard_map/sub | solution.py:36
  38.1 1.9 %shard_map.95 = (bf16[256,3072]{1,0:T(8,128)(2,1)S(1)}, bf16[256,3072]{1,0:T(8,128)(2,1)S(1)}) custom-call(bf16[256,6144]{1,0:T(8,128)(2,1)} %acts_ref.2), custom_call_target="tpu_custom_call" | custom-call | tf_op jit(solution)/shard_map/pallas_call | solution.py:275
  40.0 2.8 %collective-permute-done.13 = bf16[2,2,192,128]{3,2,1,0:T(8,128)(2,1)S(1)} collective-permute-done((bf16[2,2,192,128]{3,2,1,0:T(8,128)(2,1)S(1)}, bf16[2,2,192,128]{3,2,1,0:T(8,128)(2,1)S(1)}, u32[]{:S(2)}, u32[]{:S(2)}) %collective-permute-start.13) | collective-permute-done | bytes 196640 | tf_op jit(solution)/shard_map/ppermute | solution.py:159
  43.4 1.3 %collective-permute-done.15 = bf16[2,2,192,128]{3,2,1,0:T(8,128)(2,1)S(1)} collective-permute-done((bf16[2,2,192,128]{3,2,1,0:T(8,128)(2,1)S(1)}, bf16[2,2,192,128]{3,2,1,0:T(8,128)(2,1)S(1)}, u32[]{:S(2)}, u32[]{:S(2)}) %collective-permute-start.15) | collective-permute-done | bytes 196640 | tf_op jit(solution)/shard_map/ppermute | solution.py:159
  45.5 0.9 %collective-permute-done.16.refs_1_ = bf16[3,2,192,128]{3,2,1,0:T(8,128)(2,1)S(1)} collective-permute-done((bf16[3,2,192,128]{3,2,1,0:T(8,128)(2,1)S(1)}, bf16[3,2,192,128]{3,2,1,0:T(8,128)(2,1)S(1)}, u32[]{:S(2)}, u32[]{:S(2)}) %collective-permute-start.16) | collective-permute-done | bytes 294944 | tf_op jit(solution)/shard_map/ppermute | solution.py:149
  46.4 1.3 %shard_map.97 = bf16[256,128]{1,0:T(8,128)(2,1)} custom-call(bf16[256,3072]{1,0:T(8,128)(2,1)S(1)} %get-tuple-element.64.columns_ref, bf16[3,2,192,128]{3,2,1,0:T(8,128)(2,1)S(1)} %pad_maximum_fusion.refs_0_, bf16[3,2,192,128]{3,2,1,0:T(8,128)(2,1)S(1)} %collective-permute-done.16.refs_1_, bf16[1,2,192,128]{3,2,1,0:T(8,128)(2,1)S(1)} %get-tuple-element.82.refs_2_, ...), custom_call_target="tpu_custom_call" | custom-call | tf_op jit(solution)/shard_map/pallas_call | solution.py:295
  (39 shorter events, 4.9 us)
Async XLA Ops:
  2.7 1.9 %collective-permute-start = (bf16[4,2,192,128]{3,2,1,0:T(8,128)(2,1)S(1)}, bf16[4,2,192,128]{3,2,1,0:T(8,128)(2,1)S(1)}, u32[]{:S(2)}, u32[]{:S(2)}) collective-permute-start(bf16[4,2,192,128]{3,2,1,0:T(8,128)(2,1)S(1)} %get-tuple-element.40), channel_id=1, source_target_pairs={{0,2},{2,0},{1,3},{3,1},{4,6},{6,4},{5,7},{7,5},{8,10},{10,8},{9,1... | collective-permute-start | bytes 1179656 | tf_op jit(solution)/shard_map/ppermute | solution.py:149
  4.6 5.8 %collective-permute-start.1 = (bf16[4,2,192,128]{3,2,1,0:T(8,128)(2,1)S(1)}, bf16[4,2,192,128]{3,2,1,0:T(8,128)(2,1)S(1)}, u32[]{:S(2)}, u32[]{:S(2)}) collective-permute-start(bf16[4,2,192,128]{3,2,1,0:T(8,128)(2,1)S(1)} %get-tuple-element.42), channel_id=1, source_target_pairs={{0,2},{2,0},{1,3},{3,1},{4,6},{6,4},{5,7},{7,5},{8,10},{10,8},{9,1... | collective-permute-start | bytes 1179656 | tf_op jit(solution)/shard_map/ppermute | solution.py:149
  5.1 9.9 %collective-permute-start.6 = (bf16[2,192,128]{2,1,0:T(8,128)(2,1)S(1)}, bf16[2,192,128]{2,1,0:T(8,128)(2,1)S(1)}, u32[]{:S(2)}, u32[]{:S(2)}) collective-permute-start(bf16[2,192,128]{2,1,0:T(8,128)(2,1)S(1)} %get-tuple-element.77), channel_id=1, source_target_pairs={{0,1},{1,0},{2,14},{3,15},{4,5},{5,4},{6,10},{7,11},{8,9},{9,8},{1... | collective-permute-start | bytes 294920 | tf_op jit(solution)/shard_map/ppermute | solution.py:159
  7.8 7.6 %collective-permute-start.7 = (bf16[2,192,128]{2,1,0:T(8,128)(2,1)S(1)}, bf16[2,192,128]{2,1,0:T(8,128)(2,1)S(1)}, u32[]{:S(2)}, u32[]{:S(2)}) collective-permute-start(bf16[2,192,128]{2,1,0:T(8,128)(2,1)S(1)} %get-tuple-element.76), channel_id=1, source_target_pairs={{0,12},{1,13},{2,3},{3,2},{4,8},{5,9},{6,7},{7,6},{8,4},{9,5},{10,... | collective-permute-start | bytes 294920 | tf_op jit(solution)/shard_map/ppermute | solution.py:159
  10.3 8.2 %collective-permute-start.8 = (bf16[2,192,128]{2,1,0:T(8,128)(2,1)S(1)}, bf16[2,192,128]{2,1,0:T(8,128)(2,1)S(1)}, u32[]{:S(2)}, u32[]{:S(2)}) collective-permute-start(bf16[2,192,128]{2,1,0:T(8,128)(2,1)S(1)} %get-tuple-element.75), channel_id=1, source_target_pairs={{0,13},{1,12},{2,15},{3,14},{4,9},{5,8},{6,11},{7,10},{8,5},{9,4},... | collective-permute-start | bytes 294920 | tf_op jit(solution)/shard_map/ppermute | solution.py:159
  10.5 26.7 %copy-start = (f32[384,128]{1,0:T(8,128)S(1)}, f32[384,128]{1,0:T(8,128)}, u32[]{:S(2)}) copy-start(f32[384,128]{1,0:T(8,128)} %refs_0_.1) | copy-start | bytes 589828
  10.5 26.7 %copy-start.1 = (f32[384,128]{1,0:T(8,128)S(1)}, f32[384,128]{1,0:T(8,128)}, u32[]{:S(2)}) copy-start(f32[384,128]{1,0:T(8,128)} %refs_1_.1) | copy-start | bytes 589828
  10.5 26.6 %copy-start.2 = (f32[384,128]{1,0:T(8,128)S(1)}, f32[384,128]{1,0:T(8,128)}, u32[]{:S(2)}) copy-start(f32[384,128]{1,0:T(8,128)} %refs_2_.1) | copy-start | bytes 589828
  10.5 8.0 %collective-permute-start.2 = (bf16[2,192,128]{2,1,0:T(8,128)(2,1)S(1)}, bf16[2,192,128]{2,1,0:T(8,128)(2,1)S(1)}, u32[]{:S(2)}, u32[]{:S(2)}) collective-permute-start(bf16[2,192,128]{2,1,0:T(8,128)(2,1)S(1)} %get-tuple-element.81), channel_id=1, source_target_pairs={{0,4},{1,5},{2,11},{3,10},{4,0},{5,1},{6,15},{7,14},{8,12},{9,13},... | collective-permute-start | bytes 294920 | tf_op jit(solution)/shard_map/ppermute | solution.py:159
  12.4 6.3 %collective-permute-start.3 = (bf16[2,192,128]{2,1,0:T(8,128)(2,1)S(1)}, bf16[2,192,128]{2,1,0:T(8,128)(2,1)S(1)}, u32[]{:S(2)}, u32[]{:S(2)}) collective-permute-start(bf16[2,192,128]{2,1,0:T(8,128)(2,1)S(1)} %get-tuple-element.80), channel_id=1, source_target_pairs={{0,9},{1,8},{2,6},{3,7},{4,13},{5,12},{6,2},{7,3},{8,1},{9,0},{10,... | collective-permute-start | bytes 294920 | tf_op jit(solution)/shard_map/ppermute | solution.py:159
  15.0 4.9 %collective-permute-start.4 = (bf16[2,192,128]{2,1,0:T(8,128)(2,1)S(1)}, bf16[2,192,128]{2,1,0:T(8,128)(2,1)S(1)}, u32[]{:S(2)}, u32[]{:S(2)}) collective-permute-start(bf16[2,192,128]{2,1,0:T(8,128)(2,1)S(1)} %get-tuple-element.79), channel_id=1, source_target_pairs={{0,8},{1,9},{2,7},{3,6},{4,12},{5,13},{6,3},{7,2},{8,0},{9,1},{10,... | collective-permute-start | bytes 294920 | tf_op jit(solution)/shard_map/ppermute | solution.py:159
  15.4 5.5 %collective-permute-start.5 = (bf16[2,192,128]{2,1,0:T(8,128)(2,1)S(1)}, bf16[2,192,128]{2,1,0:T(8,128)(2,1)S(1)}, u32[]{:S(2)}, u32[]{:S(2)}) collective-permute-start(bf16[2,192,128]{2,1,0:T(8,128)(2,1)S(1)} %get-tuple-element.78), channel_id=1, source_target_pairs={{0,5},{1,4},{2,10},{3,11},{4,1},{5,0},{6,14},{7,15},{8,13},{9,12},... | collective-permute-start | bytes 294920 | tf_op jit(solution)/shard_map/ppermute | solution.py:159
  21.1 5.1 %collective-permute-start.9 = (bf16[192,128]{1,0:T(8,128)(2,1)S(1)}, bf16[192,128]{1,0:T(8,128)(2,1)S(1)}, u32[]{:S(2)}, u32[]{:S(2)}) collective-permute-start(bf16[192,128]{1,0:T(8,128)(2,1)S(1)} %fusion.11), channel_id=1, source_target_pairs={{0,16},{16,0},{1,17},{17,1},{2,18},{18,2},{3,19},{19,3},{4,20},{20... | collective-permute-start | bytes 147464 | tf_op jit(solution)/shard_map/ppermute | solution.py:149
  26.2 5.1 %collective-permute-start.10 = (bf16[192,128]{1,0:T(8,128)(2,1)S(1)}, bf16[192,128]{1,0:T(8,128)(2,1)S(1)}, u32[]{:S(2)}, u32[]{:S(2)}) collective-permute-start(bf16[192,128]{1,0:T(8,128)(2,1)S(1)} %get-tuple-element.71), channel_id=1, source_target_pairs={{0,16},{16,0},{1,17},{17,1},{2,18},{18,2},{3,19},{19,3},{4,20},{20... | collective-permute-start | bytes 147464 | tf_op jit(solution)/shard_map/ppermute | solution.py:149
  28.9 4.6 %collective-permute-start.12 = (f32[192,128]{1,0:T(8,128)S(1)}, f32[192,128]{1,0:T(8,128)S(1)}, u32[]{:S(2)}, u32[]{:S(2)}) collective-permute-start(f32[192,128]{1,0:T(8,128)S(1)} %get-tuple-element.72), channel_id=1, source_target_pairs={{0,1},{1,0},{2,3},{3,2},{4,5},{5,4},{6,7},{7,6},{8,9},{9,8},{10,11... | collective-permute-start | bytes 294920 | tf_op jit(solution)/shard_map/ppermute | solution.py:149
  31.3 2.3 %collective-permute-start.11 = (bf16[2,192,128]{2,1,0:T(8,128)(2,1)S(1)}, bf16[2,192,128]{2,1,0:T(8,128)(2,1)S(1)}, u32[]{:S(2)}, u32[]{:S(2)}) collective-permute-start(bf16[2,192,128]{2,1,0:T(8,128)(2,1)S(1)} %get-tuple-element.83), channel_id=1, source_target_pairs={{0,2},{2,0},{1,3},{3,1},{4,6},{6,4},{5,7},{7,5},{8,10},{10,8},{9,1... | collective-permute-start | bytes 294920 | tf_op jit(solution)/shard_map/ppermute | solution.py:149
  31.4 8.6 %collective-permute-start.14 = (bf16[2,192,128]{2,1,0:T(8,128)(2,1)S(1)}, bf16[2,192,128]{2,1,0:T(8,128)(2,1)S(1)}, u32[]{:S(2)}, u32[]{:S(2)}) collective-permute-start(bf16[2,192,128]{2,1,0:T(8,128)(2,1)S(1)} %get-tuple-element.83), channel_id=1, source_target_pairs={{0,13},{1,12},{2,15},{3,14},{4,9},{5,8},{6,11},{7,10},{8,5},{9,4},... | collective-permute-start | bytes 294920 | tf_op jit(solution)/shard_map/ppermute | solution.py:159
  33.6 9.2 %collective-permute-start.13 = (bf16[2,2,192,128]{3,2,1,0:T(8,128)(2,1)S(1)}, bf16[2,2,192,128]{3,2,1,0:T(8,128)(2,1)S(1)}, u32[]{:S(2)}, u32[]{:S(2)}) collective-permute-start(bf16[2,2,192,128]{3,2,1,0:T(8,128)(2,1)S(1)} %maximum_select_fusion), channel_id=1, source_target_pairs={{0,4},{1,5},{2,11},{3,10},{4,0},{5,1},{6,15},{7,14},{8,12},{9,13},... | collective-permute-start | bytes 589832 | tf_op jit(solution)/shard_map/ppermute | solution.py:159
  34.8 7.9 %collective-permute-start.17 = (bf16[2,2,192,128]{3,2,1,0:T(8,128)(2,1)S(1)}, bf16[2,2,192,128]{3,2,1,0:T(8,128)(2,1)S(1)}, u32[]{:S(2)}, u32[]{:S(2)}) collective-permute-start(bf16[2,2,192,128]{3,2,1,0:T(8,128)(2,1)S(1)} %maximum_select_fusion), channel_id=1, source_target_pairs={{0,8},{1,9},{2,7},{3,6},{4,12},{5,13},{6,3},{7,2},{8,0},{9,1},{10,... | collective-permute-start | bytes 589832 | tf_op jit(solution)/shard_map/ppermute | solution.py:159
  36.2 8.5 %collective-permute-start.15 = (bf16[2,2,192,128]{3,2,1,0:T(8,128)(2,1)S(1)}, bf16[2,2,192,128]{3,2,1,0:T(8,128)(2,1)S(1)}, u32[]{:S(2)}, u32[]{:S(2)}) collective-permute-start(bf16[2,2,192,128]{3,2,1,0:T(8,128)(2,1)S(1)} %maximum_select_fusion), channel_id=1, source_target_pairs={{0,1},{1,0},{2,14},{3,15},{4,5},{5,4},{6,10},{7,11},{8,9},{9,8},{1... | collective-permute-start | bytes 589832 | tf_op jit(solution)/shard_map/ppermute | solution.py:159
  42.8 2.0 %collective-permute-start.18 = (bf16[4,2,192,128]{3,2,1,0:T(8,128)(2,1)S(1)}, bf16[4,2,192,128]{3,2,1,0:T(8,128)(2,1)S(1)}, u32[]{:S(2)}, u32[]{:S(2)}) collective-permute-start(bf16[4,2,192,128]{3,2,1,0:T(8,128)(2,1)S(1)} %constant_dynamic-update-slice_fusion.refs_0_), channel_id=1, source_target_pairs={{0,2},{2,0},{1,3},{3,1},{4,6},{6,4},{5,7},{7,5},{8,10},{10,8},{9,1... | collective-permute-start | bytes 1179656 | tf_op jit(solution)/shard_map/ppermute | solution.py:149
  44.7 1.6 %collective-permute-start.16 = (bf16[3,2,192,128]{3,2,1,0:T(8,128)(2,1)S(1)}, bf16[3,2,192,128]{3,2,1,0:T(8,128)(2,1)S(1)}, u32[]{:S(2)}, u32[]{:S(2)}) collective-permute-start(bf16[3,2,192,128]{3,2,1,0:T(8,128)(2,1)S(1)} %pad_maximum_fusion.refs_0_), channel_id=1, source_target_pairs={{0,2},{2,0},{1,3},{3,1},{4,6},{6,4},{5,7},{7,5},{8,10},{10,8},{9,1... | collective-permute-start | bytes 884744 | tf_op jit(solution)/shard_map/ppermute | solution.py:149

commit v18 on v17

--- a/solution.py
+++ b/solution.py
@@ -12,7 +12,7 @@
 N_LOW = 4
 CHIPS = ((1, 0), (2, 1), (2, 0), (1, 1), (0, 1), (3, 0), (3, 1), (0, 0))
 LOWS = ((1, 2), (0, 3))
-NEXT = ((1, 0), (2, 0), (0, 1))
+GATHERED = (((1, 0), (2, 0), (1, 1), (2, 1)), ((0, 1), (3, 0), (3, 1)))
 VMEM_LIMIT = 8 * 2**20
 
 
@@ -127,14 +127,8 @@
 
 def places(group, core, rep):
     pieces = []
-    for by in (core, 1 - core):
-        blocks = []
-        for chip in NEXT[:2] if group == 0 else NEXT[2:]:
-            place = LOWS[group].index(chip[0]) ^ by
-            blocks += [(place, owner, rep ^ chip[1] ^ by) for owner in range(2)]
-        if group == 1:
-            blocks.append((1, by, rep ^ 1))
-        pieces.append(blocks)
+    for owner in (core, 1 - core):
+        pieces.append([(LOWS[group].index(low), owner, rep ^ d_rep) for low, d_rep in GATHERED[group]])
     if group == 1:
         pieces += [[(0, owner, rep)] for owner in (core, 1 - core)]
     return pieces
@@ -161,12 +155,9 @@
     def to_slot(x, slot):
         return cube_swap(x, lambda core: CHIPS[slot ^ core if slot < 6 else slot])
 
-    def to_next(x, slot):
-        d_low, d_rep = NEXT[slot]
-        return cube_swap(x, lambda core: (d_low ^ (3 * core), d_rep ^ core))
-
-    def to_corner(x):
-        return cube_swap(x, lambda core: (3, 1))
+    def to_neighbour(x, axis):
+        change = {"x": (1, 0), "z": (2, 0), "y": (0, 1)}[axis]
+        return cube_swap(x, lambda core: change)
 
     def per_device(acts, grad_logits, master, moment_one, moment_two, step_count):
         tokens, experts = grad_logits.shape
@@ -256,11 +247,12 @@
 
         column = jnp.stack([swap(weight, "high", j) if j else weight for j in range(n_high)])
         other = swap(grad, "rep")
-        across = swap(column, "core")
-        across, other = lax.optimization_barrier((across, other))
-        corner = to_corner(column)
-        chip = jnp.where(core == 0, jnp.stack([column, across]), jnp.stack([across, column]))
-        got = [to_next(chip, slot) for slot in range(3)]
+        x, y, z = (to_neighbour(column, axis) for axis in "xyz")
+        x, other = lax.optimization_barrier((x, other))
+        xy, yz, zx = to_neighbour(x, "y"), to_neighbour(y, "z"), to_neighbour(z, "x")
+        xy, other, late_acts, late_column = lax.optimization_barrier((xy, other, acts, column))
+        across = swap(late_column, "core")
+        xyz = to_neighbour(xy, "z")
 
         whole = jnp.where(
             rep == 0,
@@ -271,7 +263,6 @@
 
         columns = [None, None]
         if in_kernels:
-            state, late_acts = lax.optimization_barrier((state, acts))
             columns = pl.pallas_call(
                 functools.partial(columns_kernel, n_high, 4 * half),
                 out_shape=(pltpu.VMEM((tokens, 8 * n_high * half), bf16),) * 2,
@@ -280,8 +271,8 @@
                 scratch_shapes=[pltpu.SemaphoreType.DMA((2, 2 * n_high))],
                 compiler_params=params,
             )(pltpu.with_memory_space_constraint(late_acts, pltpu.HBM))
-        got[0], corner, state, columns = lax.optimization_barrier((got[0], corner, state, columns))
-        first, second = jnp.concatenate(got[:2]), jnp.concatenate([got[2], corner[None]])
+        xyz, state, columns = lax.optimization_barrier((xyz, state, columns))
+        first, second = jnp.stack([x, z, xy, yz]), jnp.stack([y, zx, xyz])
         first, second = [first, swap(first, "core")], [second, swap(second, "core")]
         second += [column[None], across[None]]
         pieces = (first, second)

time: 47.8 us -> 49 us (1.025)
  starting transfers between devices: 25 us -> 27.7 us
  waiting for transfers between devices: 13.1 us -> 11.3 us
    ppermute x11 -> x14, starting transfers between devices: 17 us -> 20.1 us  [cube_swap(): return lax.ppermute(x, AXES[1:], pairs)]
    ppermute x11 -> x14, waiting for transfers between devices: 8.52 us -> 6.45 us  [cube_swap(): return lax.ppermute(x, AXES[1:], pairs)]
  transfers between devices with their start and end apart: 19 -> 22, of which waited for: 10 -> 13; matrix products, arithmetic and copies ran while one was open for 3% -> 3% of each run, Pallas kernels for 7% -> 6%
where the time goes in v18:
time: 49 us; the launch traced here: 48.5 us
  starting transfers between devices  27.7 us (57%)
  waiting for transfers between devices  11.3 us (23%)
  Pallas kernels  6.43 us (13%)
  between operations  1.51 us (3%)
  other arithmetic  1.42 us (3%)
    ppermute x14, starting transfers between devices, cube_swap(): return lax.ppermute(x, AXES[1:], pairs)  20.1 us
    ppermute x8, starting transfers between devices, swap(): lax.ppermute(x, axis, [(i, i ^ mask) for i in range(fine.shape[axis])])  7.61 us
    ppermute x14, waiting for transfers between devices, cube_swap(): return lax.ppermute(x, AXES[1:], pairs)  6.45 us
    ppermute x8, waiting for transfers between devices, swap(): lax.ppermute(x, axis, [(i, i ^ mask) for i in range(fine.shape[axis])])  4.84 us
    pallas_call x1, Pallas kernels, per_device(): pl.pallas_call(functools.partial(first_grad_kernel, n_high), out_shape=[s...  2.06 us
    pallas_call x1, Pallas kernels, per_device(): pl.pallas_call(functools.partial(columns_kernel, n_high, 4 * half), out_s...  1.91 us
    pallas_call x2, Pallas kernels, per_device(): pl.pallas_call(functools.partial(logits_kernel, n_high, group), out_shape...  1.89 us
  transfers between devices with their start and end apart: 22, of which 13 were waited for; matrix products, arithmetic and copies ran while one was open for 3% of the time, Pallas kernels for 6%

profile of v18, /device:TPU:0, one launch (start us, length us, event | category | flops | bytes accessed | tf_op | source)
XLA Modules:
  0.0 48.5 jit_solution(3911991563112745979)
XLA Ops:
  0.6 2.1 %shard_map.93 = (bf16[4,2,192,128]{3,2,1,0:T(8,128)(2,1)S(1)}, bf16[4,2,192,128]{3,2,1,0:T(8,128)(2,1)S(1)}, f32[3,192,128]{2,1,0:T(8,128)S(1)}, bf16[4,256,768]{2,1,0:T(8,128)(2,1)S(1)}, bf16[128,256]{1,0:T(8,128)(2,1)S(1)}) custom-call(bf16[256,6144]{1,0:T(8,128)(2,1)} %acts_ref.2, bf16[256,128]{1,0:T(8,128)(2,1)} %grad_ref.1, f32[384,128]{1,0:T(8,128)} %refs_0_.1, ...), custom_call_target="tpu_custom_call" | custom-call | tf_op jit(solution)/shard_map/pallas_call | solution.py:181
  3.8 0.8 %collective-permute-done = bf16[4,2,192,128]{3,2,1,0:T(8,128)(2,1)S(1)} collective-permute-done((bf16[4,2,192,128]{3,2,1,0:T(8,128)(2,1)S(1)}, bf16[4,2,192,128]{3,2,1,0:T(8,128)(2,1)S(1)}, u32[]{:S(2)}, u32[]{:S(2)}) %collective-permute-start) | collective-permute-done | bytes 393248 | tf_op jit(solution)/shard_map/ppermute | solution.py:143
  5.1 4.7 %collective-permute-start.8 = (bf16[2,192,128]{2,1,0:T(8,128)(2,1)S(1)}, bf16[2,192,128]{2,1,0:T(8,128)(2,1)S(1)}, u32[]{:S(2)}, u32[]{:S(2)}) collective-permute-start(bf16[2,192,128]{2,1,0:T(8,128)(2,1)S(1)} %get-tuple-element.73), channel_id=1, source_target_pairs={{0,13},{1,12},{2,15},{3,14},{4,9},{5,8},{6,11},{7,10},{8,5},{9,4},... | collective-permute-start | bytes 294920 | tf_op jit(solution)/shard_map/ppermute | solution.py:153
  10.6 2.8 %collective-permute-start.5 = (bf16[2,192,128]{2,1,0:T(8,128)(2,1)S(1)}, bf16[2,192,128]{2,1,0:T(8,128)(2,1)S(1)}, u32[]{:S(2)}, u32[]{:S(2)}) collective-permute-start(bf16[2,192,128]{2,1,0:T(8,128)(2,1)S(1)} %get-tuple-element.76), channel_id=1, source_target_pairs={{0,5},{1,4},{2,10},{3,11},{4,1},{5,0},{6,14},{7,15},{8,13},{9,12},... | collective-permute-start | bytes 294920 | tf_op jit(solution)/shard_map/ppermute | solution.py:153
  13.4 1.6 %collective-permute-start.4 = (bf16[2,192,128]{2,1,0:T(8,128)(2,1)S(1)}, bf16[2,192,128]{2,1,0:T(8,128)(2,1)S(1)}, u32[]{:S(2)}, u32[]{:S(2)}) collective-permute-start(bf16[2,192,128]{2,1,0:T(8,128)(2,1)S(1)} %get-tuple-element.77), channel_id=1, source_target_pairs={{0,8},{1,9},{2,7},{3,6},{4,12},{5,13},{6,3},{7,2},{8,0},{9,1},{10,... | collective-permute-start | bytes 294920 | tf_op jit(solution)/shard_map/ppermute | solution.py:153
  14.9 1.4 %collective-permute-start.3 = (bf16[2,192,128]{2,1,0:T(8,128)(2,1)S(1)}, bf16[2,192,128]{2,1,0:T(8,128)(2,1)S(1)}, u32[]{:S(2)}, u32[]{:S(2)}) collective-permute-start(bf16[2,192,128]{2,1,0:T(8,128)(2,1)S(1)} %get-tuple-element.78), channel_id=1, source_target_pairs={{0,9},{1,8},{2,6},{3,7},{4,13},{5,12},{6,2},{7,3},{8,1},{9,0},{10,... | collective-permute-start | bytes 294920 | tf_op jit(solution)/shard_map/ppermute | solution.py:153
  16.3 1.4 %collective-permute-start.2 = (bf16[2,192,128]{2,1,0:T(8,128)(2,1)S(1)}, bf16[2,192,128]{2,1,0:T(8,128)(2,1)S(1)}, u32[]{:S(2)}, u32[]{:S(2)}) collective-permute-start(bf16[2,192,128]{2,1,0:T(8,128)(2,1)S(1)} %get-tuple-element.79), channel_id=1, source_target_pairs={{0,4},{1,5},{2,11},{3,10},{4,0},{5,1},{6,15},{7,14},{8,12},{9,13},... | collective-permute-start | bytes 294920 | tf_op jit(solution)/shard_map/ppermute | solution.py:153
  17.8 0.9 %collective-permute-done.5 = bf16[2,192,128]{2,1,0:T(8,128)(2,1)S(1)} collective-permute-done((bf16[2,192,128]{2,1,0:T(8,128)(2,1)S(1)}, bf16[2,192,128]{2,1,0:T(8,128)(2,1)S(1)}, u32[]{:S(2)}, u32[]{:S(2)}) %collective-permute-start.5) | collective-permute-done | bytes 98336 | tf_op jit(solution)/shard_map/ppermute | solution.py:153
  18.7 1.8 %collective-permute-done.3 = bf16[2,192,128]{2,1,0:T(8,128)(2,1)S(1)} collective-permute-done((bf16[2,192,128]{2,1,0:T(8,128)(2,1)S(1)}, bf16[2,192,128]{2,1,0:T(8,128)(2,1)S(1)}, u32[]{:S(2)}, u32[]{:S(2)}) %collective-permute-start.3) | collective-permute-done | bytes 98336 | tf_op jit(solution)/shard_map/ppermute | solution.py:153
  21.0 2.7 %collective-permute-start.9 = (bf16[192,128]{1,0:T(8,128)(2,1)S(1)}, bf16[192,128]{1,0:T(8,128)(2,1)S(1)}, u32[]{:S(2)}, u32[]{:S(2)}) collective-permute-start(bf16[192,128]{1,0:T(8,128)(2,1)S(1)} %fusion.11), channel_id=1, source_target_pairs={{0,16},{16,0},{1,17},{17,1},{2,18},{18,2},{3,19},{19,3},{4,20},{20... | collective-permute-start | bytes 147464 | tf_op jit(solution)/shard_map/ppermute | solution.py:143
  24.4 1.8 %collective-permute-done.9 = bf16[192,128]{1,0:T(8,128)(2,1)S(1)} collective-permute-done((bf16[192,128]{1,0:T(8,128)(2,1)S(1)}, bf16[192,128]{1,0:T(8,128)(2,1)S(1)}, u32[]{:S(2)}, u32[]{:S(2)}) %collective-permute-start.9) | collective-permute-done | bytes 49184 | tf_op jit(solution)/shard_map/ppermute | solution.py:143
  26.3 2.6 %collective-permute-start.10 = (bf16[192,128]{1,0:T(8,128)(2,1)S(1)}, bf16[192,128]{1,0:T(8,128)(2,1)S(1)}, u32[]{:S(2)}, u32[]{:S(2)}) collective-permute-start(bf16[192,128]{1,0:T(8,128)(2,1)S(1)} %get-tuple-element.69), channel_id=1, source_target_pairs={{0,16},{16,0},{1,17},{17,1},{2,18},{18,2},{3,19},{19,3},{4,20},{20... | collective-permute-start | bytes 147464 | tf_op jit(solution)/shard_map/ppermute | solution.py:143
  29.0 0.8 %collective-permute-start.12 = (f32[192,128]{1,0:T(8,128)S(1)}, f32[192,128]{1,0:T(8,128)S(1)}, u32[]{:S(2)}, u32[]{:S(2)}) collective-permute-start(f32[192,128]{1,0:T(8,128)S(1)} %get-tuple-element.70), channel_id=1, source_target_pairs={{0,1},{1,0},{2,3},{3,2},{4,5},{5,4},{6,7},{7,6},{8,9},{9,8},{10,11... | collective-permute-start | bytes 294920 | tf_op jit(solution)/shard_map/ppermute | solution.py:143
  29.7 1.6 %collective-permute-done.10 = bf16[192,128]{1,0:T(8,128)(2,1)S(1)} collective-permute-done((bf16[192,128]{1,0:T(8,128)(2,1)S(1)}, bf16[192,128]{1,0:T(8,128)(2,1)S(1)}, u32[]{:S(2)}, u32[]{:S(2)}) %collective-permute-start.10) | collective-permute-done | bytes 49184 | tf_op jit(solution)/shard_map/ppermute | solution.py:143
  31.4 1.4 %collective-permute-start.11 = (bf16[2,192,128]{2,1,0:T(8,128)(2,1)S(1)}, bf16[2,192,128]{2,1,0:T(8,128)(2,1)S(1)}, u32[]{:S(2)}, u32[]{:S(2)}) collective-permute-start(bf16[2,192,128]{2,1,0:T(8,128)(2,1)S(1)} %get-tuple-element.64), channel_id=1, source_target_pairs={{0,4},{1,5},{2,6},{3,7},{4,0},{5,1},{6,2},{7,3},{8,12},{9,13},{10,... | collective-permute-start | bytes 294920 | tf_op jit(solution)/shard_map/ppermute | solution.py:153
  33.3 1.4 %collective-permute-start.16 = (bf16[2,192,128]{2,1,0:T(8,128)(2,1)S(1)}, bf16[2,192,128]{2,1,0:T(8,128)(2,1)S(1)}, u32[]{:S(2)}, u32[]{:S(2)}) collective-permute-start(bf16[2,192,128]{2,1,0:T(8,128)(2,1)S(1)} %get-tuple-element.64), channel_id=1, source_target_pairs={{0,8},{1,9},{2,10},{3,11},{4,12},{5,13},{6,14},{7,15},{8,0},{9,1},... | collective-permute-start | bytes 294920 | tf_op jit(solution)/shard_map/ppermute | solution.py:153
  34.7 1.4 %collective-permute-done.11 = bf16[2,192,128]{2,1,0:T(8,128)(2,1)S(1)} collective-permute-done((bf16[2,192,128]{2,1,0:T(8,128)(2,1)S(1)}, bf16[2,192,128]{2,1,0:T(8,128)(2,1)S(1)}, u32[]{:S(2)}, u32[]{:S(2)}) %collective-permute-start.11) | collective-permute-done | bytes 98336 | tf_op jit(solution)/shard_map/ppermute | solution.py:153
  36.1 0.9 %collective-permute-start.13 = (bf16[2,192,128]{2,1,0:T(8,128)(2,1)S(1)}, bf16[2,192,128]{2,1,0:T(8,128)(2,1)S(1)}, u32[]{:S(2)}, u32[]{:S(2)}) collective-permute-start(bf16[2,192,128]{2,1,0:T(8,128)(2,1)S(1)} %collective-permute-done.11), channel_id=1, source_target_pairs={{0,1},{1,0},{2,3},{3,2},{4,5},{5,4},{6,7},{7,6},{8,9},{9,8},{10,11... | collective-permute-start | bytes 294920 | tf_op jit(solution)/shard_map/ppermute | solution.py:153
  37.7 1.1 %collective-permute-start.20 = (bf16[2,192,128]{2,1,0:T(8,128)(2,1)S(1)}, bf16[2,192,128]{2,1,0:T(8,128)(2,1)S(1)}, u32[]{:S(2)}, u32[]{:S(2)}) collective-permute-start(bf16[2,192,128]{2,1,0:T(8,128)(2,1)S(1)} %collective-permute-done.15), channel_id=1, source_target_pairs={{0,8},{1,9},{2,10},{3,11},{4,12},{5,13},{6,14},{7,15},{8,0},{9,1},... | collective-permute-start | bytes 294920 | tf_op jit(solution)/shard_map/ppermute | solution.py:153
  38.9 1.1 %collective-permute-start.17 = (bf16[2,192,128]{2,1,0:T(8,128)(2,1)S(1)}, bf16[2,192,128]{2,1,0:T(8,128)(2,1)S(1)}, u32[]{:S(2)}, u32[]{:S(2)}) collective-permute-start(bf16[2,192,128]{2,1,0:T(8,128)(2,1)S(1)} %collective-permute-done.16), channel_id=1, source_target_pairs={{0,4},{1,5},{2,6},{3,7},{4,0},{5,1},{6,2},{7,3},{8,12},{9,13},{10,... | collective-permute-start | bytes 294920 | tf_op jit(solution)/shard_map/ppermute | solution.py:153
  40.7 1.2 %collective-permute-start.14 = (bf16[2,192,128]{2,1,0:T(8,128)(2,1)S(1)}, bf16[2,192,128]{2,1,0:T(8,128)(2,1)S(1)}, u32[]{:S(2)}, u32[]{:S(2)}) collective-permute-start(bf16[2,192,128]{2,1,0:T(8,128)(2,1)S(1)} %collective-permute-done.13), channel_id=1, source_target_pairs={{0,8},{1,9},{2,10},{3,11},{4,12},{5,13},{6,14},{7,15},{8,0},{9,1},... | collective-permute-start | bytes 294920 | tf_op jit(solution)/shard_map/ppermute | solution.py:153
  42.4 0.9 %multiply_subtract_fusion = (f32[384,128]{1,0:T(8,128)}, f32[384,128]{1,0:T(8,128)}, f32[384,128]{1,0:T(8,128)}) fusion(f32[384,128]{1,0:T(8,128)S(1)} %copy-done, f32[]{:T(128)} %bitcast.14, f32[]{:T(128)} %bitcast.12, f32[192,128]{1,0:T(8,128)S(1)} %get-tuple-element.70, f32[192,128]{1,0:T(8,128)S(1)} %collective-permute-done.12, pred[]{:T(512)S(6)} %eq.3, ...), kind=kLoop, calls=%fused_computation.8 | loop fusion | flops 884736 | bytes 1376265 | tf_op jit(solution)/shard_map/sub | solution.py:36
  43.3 1.9 %shard_map.95 = (bf16[256,3072]{1,0:T(8,128)(2,1)S(1)}, bf16[256,3072]{1,0:T(8,128)(2,1)S(1)}) custom-call(bf16[256,6144]{1,0:T(8,128)(2,1)} %acts_ref.2), custom_call_target="tpu_custom_call" | custom-call | tf_op jit(solution)/shard_map/pallas_call | solution.py:266
  47.2 1.3 %shard_map.97 = bf16[256,128]{1,0:T(8,128)(2,1)} custom-call(bf16[256,3072]{1,0:T(8,128)(2,1)S(1)} %get-tuple-element.62.columns_ref, bf16[3,2,192,128]{3,2,1,0:T(8,128)(2,1)S(1)} %pad_maximum_fusion.1.refs_0_, bf16[3,2,192,128]{3,2,1,0:T(8,128)(2,1)S(1)} %collective-permute-done.18.refs_1_, bf16[1,2,192,128]{3,2,1,0:T(8,128)(2,1)S(1)} %get-tuple-element.80.refs_2_, ...), custom_call_target="tpu_custom_call" | custom-call | tf_op jit(solution)/shard_map/pallas_call | solution.py:286
  (43 shorter events, 7.5 us)
Async XLA Ops:
  2.7 1.9 %collective-permute-start = (bf16[4,2,192,128]{3,2,1,0:T(8,128)(2,1)S(1)}, bf16[4,2,192,128]{3,2,1,0:T(8,128)(2,1)S(1)}, u32[]{:S(2)}, u32[]{:S(2)}) collective-permute-start(bf16[4,2,192,128]{3,2,1,0:T(8,128)(2,1)S(1)} %get-tuple-element.39), channel_id=1, source_target_pairs={{0,2},{2,0},{1,3},{3,1},{4,6},{6,4},{5,7},{7,5},{8,10},{10,8},{9,1... | collective-permute-start | bytes 1179656 | tf_op jit(solution)/shard_map/ppermute | solution.py:143
  4.6 5.8 %collective-permute-start.1 = (bf16[4,2,192,128]{3,2,1,0:T(8,128)(2,1)S(1)}, bf16[4,2,192,128]{3,2,1,0:T(8,128)(2,1)S(1)}, u32[]{:S(2)}, u32[]{:S(2)}) collective-permute-start(bf16[4,2,192,128]{3,2,1,0:T(8,128)(2,1)S(1)} %get-tuple-element.41), channel_id=1, source_target_pairs={{0,2},{2,0},{1,3},{3,1},{4,6},{6,4},{5,7},{7,5},{8,10},{10,8},{9,1... | collective-permute-start | bytes 1179656 | tf_op jit(solution)/shard_map/ppermute | solution.py:143
  5.1 9.8 %collective-permute-start.8 = (bf16[2,192,128]{2,1,0:T(8,128)(2,1)S(1)}, bf16[2,192,128]{2,1,0:T(8,128)(2,1)S(1)}, u32[]{:S(2)}, u32[]{:S(2)}) collective-permute-start(bf16[2,192,128]{2,1,0:T(8,128)(2,1)S(1)} %get-tuple-element.73), channel_id=1, source_target_pairs={{0,13},{1,12},{2,15},{3,14},{4,9},{5,8},{6,11},{7,10},{8,5},{9,4},... | collective-permute-start | bytes 294920 | tf_op jit(solution)/shard_map/ppermute | solution.py:153
  9.8 6.5 %collective-permute-start.7 = (bf16[2,192,128]{2,1,0:T(8,128)(2,1)S(1)}, bf16[2,192,128]{2,1,0:T(8,128)(2,1)S(1)}, u32[]{:S(2)}, u32[]{:S(2)}) collective-permute-start(bf16[2,192,128]{2,1,0:T(8,128)(2,1)S(1)} %get-tuple-element.74), channel_id=1, source_target_pairs={{0,12},{1,13},{2,3},{3,2},{4,8},{5,9},{6,7},{7,6},{8,4},{9,5},{10,... | collective-permute-start | bytes 294920 | tf_op jit(solution)/shard_map/ppermute | solution.py:153
  10.2 7.6 %collective-permute-start.6 = (bf16[2,192,128]{2,1,0:T(8,128)(2,1)S(1)}, bf16[2,192,128]{2,1,0:T(8,128)(2,1)S(1)}, u32[]{:S(2)}, u32[]{:S(2)}) collective-permute-start(bf16[2,192,128]{2,1,0:T(8,128)(2,1)S(1)} %get-tuple-element.75), channel_id=1, source_target_pairs={{0,1},{1,0},{2,14},{3,15},{4,5},{5,4},{6,10},{7,11},{8,9},{9,8},{1... | collective-permute-start | bytes 294920 | tf_op jit(solution)/shard_map/ppermute | solution.py:153
  10.6 8.1 %collective-permute-start.5 = (bf16[2,192,128]{2,1,0:T(8,128)(2,1)S(1)}, bf16[2,192,128]{2,1,0:T(8,128)(2,1)S(1)}, u32[]{:S(2)}, u32[]{:S(2)}) collective-permute-start(bf16[2,192,128]{2,1,0:T(8,128)(2,1)S(1)} %get-tuple-element.76), channel_id=1, source_target_pairs={{0,5},{1,4},{2,10},{3,11},{4,1},{5,0},{6,14},{7,15},{8,13},{9,12},... | collective-permute-start | bytes 294920 | tf_op jit(solution)/shard_map/ppermute | solution.py:153
  13.4 5.3 %collective-permute-start.4 = (bf16[2,192,128]{2,1,0:T(8,128)(2,1)S(1)}, bf16[2,192,128]{2,1,0:T(8,128)(2,1)S(1)}, u32[]{:S(2)}, u32[]{:S(2)}) collective-permute-start(bf16[2,192,128]{2,1,0:T(8,128)(2,1)S(1)} %get-tuple-element.77), channel_id=1, source_target_pairs={{0,8},{1,9},{2,7},{3,6},{4,12},{5,13},{6,3},{7,2},{8,0},{9,1},{10,... | collective-permute-start | bytes 294920 | tf_op jit(solution)/shard_map/ppermute | solution.py:153
  14.9 5.5 %collective-permute-start.3 = (bf16[2,192,128]{2,1,0:T(8,128)(2,1)S(1)}, bf16[2,192,128]{2,1,0:T(8,128)(2,1)S(1)}, u32[]{:S(2)}, u32[]{:S(2)}) collective-permute-start(bf16[2,192,128]{2,1,0:T(8,128)(2,1)S(1)} %get-tuple-element.78), channel_id=1, source_target_pairs={{0,9},{1,8},{2,6},{3,7},{4,13},{5,12},{6,2},{7,3},{8,1},{9,0},{10,... | collective-permute-start | bytes 294920 | tf_op jit(solution)/shard_map/ppermute | solution.py:153
  16.3 4.6 %collective-permute-start.2 = (bf16[2,192,128]{2,1,0:T(8,128)(2,1)S(1)}, bf16[2,192,128]{2,1,0:T(8,128)(2,1)S(1)}, u32[]{:S(2)}, u32[]{:S(2)}) collective-permute-start(bf16[2,192,128]{2,1,0:T(8,128)(2,1)S(1)} %get-tuple-element.79), channel_id=1, source_target_pairs={{0,4},{1,5},{2,11},{3,10},{4,0},{5,1},{6,15},{7,14},{8,12},{9,13},... | collective-permute-start | bytes 294920 | tf_op jit(solution)/shard_map/ppermute | solution.py:153
  17.8 24.7 %copy-start.1 = (f32[384,128]{1,0:T(8,128)S(1)}, f32[384,128]{1,0:T(8,128)}, u32[]{:S(2)}) copy-start(f32[384,128]{1,0:T(8,128)} %refs_1_.1) | copy-start | bytes 589828
  17.8 24.7 %copy-start.2 = (f32[384,128]{1,0:T(8,128)S(1)}, f32[384,128]{1,0:T(8,128)}, u32[]{:S(2)}) copy-start(f32[384,128]{1,0:T(8,128)} %refs_2_.1) | copy-start | bytes 589828
  21.0 5.2 %collective-permute-start.9 = (bf16[192,128]{1,0:T(8,128)(2,1)S(1)}, bf16[192,128]{1,0:T(8,128)(2,1)S(1)}, u32[]{:S(2)}, u32[]{:S(2)}) collective-permute-start(bf16[192,128]{1,0:T(8,128)(2,1)S(1)} %fusion.11), channel_id=1, source_target_pairs={{0,16},{16,0},{1,17},{17,1},{2,18},{18,2},{3,19},{19,3},{4,20},{20... | collective-permute-start | bytes 147464 | tf_op jit(solution)/shard_map/ppermute | solution.py:143
  26.3 5.1 %collective-permute-start.10 = (bf16[192,128]{1,0:T(8,128)(2,1)S(1)}, bf16[192,128]{1,0:T(8,128)(2,1)S(1)}, u32[]{:S(2)}, u32[]{:S(2)}) collective-permute-start(bf16[192,128]{1,0:T(8,128)(2,1)S(1)} %get-tuple-element.69), channel_id=1, source_target_pairs={{0,16},{16,0},{1,17},{17,1},{2,18},{18,2},{3,19},{19,3},{4,20},{20... | collective-permute-start | bytes 147464 | tf_op jit(solution)/shard_map/ppermute | solution.py:143
  29.0 5.7 %collective-permute-start.12 = (f32[192,128]{1,0:T(8,128)S(1)}, f32[192,128]{1,0:T(8,128)S(1)}, u32[]{:S(2)}, u32[]{:S(2)}) collective-permute-start(f32[192,128]{1,0:T(8,128)S(1)} %get-tuple-element.70), channel_id=1, source_target_pairs={{0,1},{1,0},{2,3},{3,2},{4,5},{5,4},{6,7},{7,6},{8,9},{9,8},{10,11... | collective-permute-start | bytes 294920 | tf_op jit(solution)/shard_map/ppermute | solution.py:143
  31.4 4.7 %collective-permute-start.11 = (bf16[2,192,128]{2,1,0:T(8,128)(2,1)S(1)}, bf16[2,192,128]{2,1,0:T(8,128)(2,1)S(1)}, u32[]{:S(2)}, u32[]{:S(2)}) collective-permute-start(bf16[2,192,128]{2,1,0:T(8,128)(2,1)S(1)} %get-tuple-element.64), channel_id=1, source_target_pairs={{0,4},{1,5},{2,6},{3,7},{4,0},{5,1},{6,2},{7,3},{8,12},{9,13},{10,... | collective-permute-start | bytes 294920 | tf_op jit(solution)/shard_map/ppermute | solution.py:153
  32.8 4.9 %collective-permute-start.15 = (bf16[2,192,128]{2,1,0:T(8,128)(2,1)S(1)}, bf16[2,192,128]{2,1,0:T(8,128)(2,1)S(1)}, u32[]{:S(2)}, u32[]{:S(2)}) collective-permute-start(bf16[2,192,128]{2,1,0:T(8,128)(2,1)S(1)} %get-tuple-element.64), channel_id=1, source_target_pairs={{0,1},{1,0},{2,3},{3,2},{4,5},{5,4},{6,7},{7,6},{8,9},{9,8},{10,11... | collective-permute-start | bytes 294920 | tf_op jit(solution)/shard_map/ppermute | solution.py:153
  33.3 5.5 %collective-permute-start.16 = (bf16[2,192,128]{2,1,0:T(8,128)(2,1)S(1)}, bf16[2,192,128]{2,1,0:T(8,128)(2,1)S(1)}, u32[]{:S(2)}, u32[]{:S(2)}) collective-permute-start(bf16[2,192,128]{2,1,0:T(8,128)(2,1)S(1)} %get-tuple-element.64), channel_id=1, source_target_pairs={{0,8},{1,9},{2,10},{3,11},{4,12},{5,13},{6,14},{7,15},{8,0},{9,1},... | collective-permute-start | bytes 294920 | tf_op jit(solution)/shard_map/ppermute | solution.py:153
  36.1 4.6 %collective-permute-start.13 = (bf16[2,192,128]{2,1,0:T(8,128)(2,1)S(1)}, bf16[2,192,128]{2,1,0:T(8,128)(2,1)S(1)}, u32[]{:S(2)}, u32[]{:S(2)}) collective-permute-start(bf16[2,192,128]{2,1,0:T(8,128)(2,1)S(1)} %collective-permute-done.11), channel_id=1, source_target_pairs={{0,1},{1,0},{2,3},{3,2},{4,5},{5,4},{6,7},{7,6},{8,9},{9,8},{10,11... | collective-permute-start | bytes 294920 | tf_op jit(solution)/shard_map/ppermute | solution.py:153
  37.7 4.6 %collective-permute-start.20 = (bf16[2,192,128]{2,1,0:T(8,128)(2,1)S(1)}, bf16[2,192,128]{2,1,0:T(8,128)(2,1)S(1)}, u32[]{:S(2)}, u32[]{:S(2)}) collective-permute-start(bf16[2,192,128]{2,1,0:T(8,128)(2,1)S(1)} %collective-permute-done.15), channel_id=1, source_target_pairs={{0,8},{1,9},{2,10},{3,11},{4,12},{5,13},{6,14},{7,15},{8,0},{9,1},... | collective-permute-start | bytes 294920 | tf_op jit(solution)/shard_map/ppermute | solution.py:153
  38.9 6.4 %collective-permute-start.17 = (bf16[2,192,128]{2,1,0:T(8,128)(2,1)S(1)}, bf16[2,192,128]{2,1,0:T(8,128)(2,1)S(1)}, u32[]{:S(2)}, u32[]{:S(2)}) collective-permute-start(bf16[2,192,128]{2,1,0:T(8,128)(2,1)S(1)} %collective-permute-done.16), channel_id=1, source_target_pairs={{0,4},{1,5},{2,6},{3,7},{4,0},{5,1},{6,2},{7,3},{8,12},{9,13},{10,... | collective-permute-start | bytes 294920 | tf_op jit(solution)/shard_map/ppermute | solution.py:153
  40.7 4.6 %collective-permute-start.14 = (bf16[2,192,128]{2,1,0:T(8,128)(2,1)S(1)}, bf16[2,192,128]{2,1,0:T(8,128)(2,1)S(1)}, u32[]{:S(2)}, u32[]{:S(2)}) collective-permute-start(bf16[2,192,128]{2,1,0:T(8,128)(2,1)S(1)} %collective-permute-done.13), channel_id=1, source_target_pairs={{0,8},{1,9},{2,10},{3,11},{4,12},{5,13},{6,14},{7,15},{8,0},{9,1},... | collective-permute-start | bytes 294920 | tf_op jit(solution)/shard_map/ppermute | solution.py:153
  42.3 3.6 %collective-permute-start.21 = (bf16[4,2,192,128]{3,2,1,0:T(8,128)(2,1)S(1)}, bf16[4,2,192,128]{3,2,1,0:T(8,128)(2,1)S(1)}, u32[]{:S(2)}, u32[]{:S(2)}) collective-permute-start(bf16[4,2,192,128]{3,2,1,0:T(8,128)(2,1)S(1)} %pad_maximum_fusion.refs_0_), channel_id=1, source_target_pairs={{0,2},{2,0},{1,3},{3,1},{4,6},{6,4},{5,7},{7,5},{8,10},{10,8},{9,1... | collective-permute-start | bytes 1179656 | tf_op jit(solution)/shard_map/ppermute | solution.py:143
  45.4 1.8 %collective-permute-start.18 = (bf16[3,2,192,128]{3,2,1,0:T(8,128)(2,1)S(1)}, bf16[3,2,192,128]{3,2,1,0:T(8,128)(2,1)S(1)}, u32[]{:S(2)}, u32[]{:S(2)}) collective-permute-start(bf16[3,2,192,128]{3,2,1,0:T(8,128)(2,1)S(1)} %pad_maximum_fusion.1.refs_0_), channel_id=1, source_target_pairs={{0,2},{2,0},{1,3},{3,1},{4,6},{6,4},{5,7},{7,5},{8,10},{10,8},{9,1... | collective-permute-start | bytes 884744 | tf_op jit(solution)/shard_map/ppermute | solution.py:143
  45.9 1.3 %collective-permute-start.19 = (bf16[2,192,128]{2,1,0:T(8,128)(2,1)S(1)}, bf16[2,192,128]{2,1,0:T(8,128)(2,1)S(1)}, u32[]{:S(2)}, u32[]{:S(2)}) collective-permute-start(bf16[2,192,128]{2,1,0:T(8,128)(2,1)S(1)} %get-tuple-element.64), channel_id=1, source_target_pairs={{0,2},{2,0},{1,3},{3,1},{4,6},{6,4},{5,7},{7,5},{8,10},{10,8},{9,1... | collective-permute-start | bytes 294920 | tf_op jit(solution)/shard_map/ppermute | solution.py:143
  (1 other events, 24.7 us)

commit v19 on v18

--- a/solution.py
+++ b/solution.py
@@ -245,24 +245,11 @@
             grad = grad + swap(total[j].astype(bf16), "high", j).astype(f32)
         weight = adamw(grad, *mine, step_count)[0].astype(bf16)
 
-        column = jnp.stack([swap(weight, "high", j) if j else weight for j in range(n_high)])
+        far = [swap(weight, "high", j) for j in range(1, n_high)]
         other = swap(grad, "rep")
-        x, y, z = (to_neighbour(column, axis) for axis in "xyz")
-        x, other = lax.optimization_barrier((x, other))
-        xy, yz, zx = to_neighbour(x, "y"), to_neighbour(y, "z"), to_neighbour(z, "x")
-        xy, other, late_acts, late_column = lax.optimization_barrier((xy, other, acts, column))
-        across = swap(late_column, "core")
-        xyz = to_neighbour(xy, "z")
-
-        whole = jnp.where(
-            rep == 0,
-            jnp.concatenate([grad, other], 0),
-            jnp.concatenate([other, grad], 0),
-        )
-        state = adamw(whole, *state_in, step_count)
-
         columns = [None, None]
         if in_kernels:
+            weight, late_acts = lax.optimization_barrier((weight, acts))
             columns = pl.pallas_call(
                 functools.partial(columns_kernel, n_high, 4 * half),
                 out_shape=(pltpu.VMEM((tokens, 8 * n_high * half), bf16),) * 2,
@@ -271,7 +258,22 @@
                 scratch_shapes=[pltpu.SemaphoreType.DMA((2, 2 * n_high))],
                 compiler_params=params,
             )(pltpu.with_memory_space_constraint(late_acts, pltpu.HBM))
-        xyz, state, columns = lax.optimization_barrier((xyz, state, columns))
+            far, columns = lax.optimization_barrier((far, columns))
+        column = jnp.stack([weight, *far])
+        x, y, z = (to_neighbour(column, axis) for axis in "xyz")
+        x, other = lax.optimization_barrier((x, other))
+        xy, yz, zx = to_neighbour(x, "y"), to_neighbour(y, "z"), to_neighbour(z, "x")
+        xy, late_column = lax.optimization_barrier((xy, column))
+        across = swap(late_column, "core")
+        xyz = to_neighbour(xy, "z")
+
+        whole = jnp.where(
+            rep == 0,
+            jnp.concatenate([grad, other], 0),
+            jnp.concatenate([other, grad], 0),
+        )
+        state = adamw(whole, *state_in, step_count)
+
         first, second = jnp.stack([x, z, xy, yz]), jnp.stack([y, zx, xyz])
         first, second = [first, swap(first, "core")], [second, swap(second, "core")]
         second += [column[None], across[None]]

time: 49 us -> 54.2 us (1.11)
  other arithmetic: 1.42 us -> 4.07 us
  Pallas kernels: 6.43 us -> 8.5 us
  waiting for transfers between devices: 11.3 us -> 11.9 us
    ppermute x14, waiting for transfers between devices: 6.45 us -> 9.4 us  [cube_swap(): return lax.ppermute(x, AXES[1:], pairs)]
    ppermute x8, waiting for transfers between devices: 4.84 us -> 2.46 us  [swap(): lax.ppermute(x, axis, [(i, i ^ mask) for i in range(fine.shape[axis])])]
    pallas_call x2, Pallas kernels: 1.89 us -> 3.96 us  [per_device(): pl.pallas_call(functools.partial(logits_kernel, n_high, group), out_shape...]
    sub x1, other arithmetic: 0.9 us -> 2.19 us  [adamw(): master - 0.01 * (first_hat / (jnp.sqrt(second_hat) + 1e-08) + 0.1 * master)]
    another operation x2, other arithmetic: 0.09 us -> 0.81 us  [per_device(): first, second = (jnp.stack([x, z, xy, yz]), jnp.stack([y, zx, xyz]))]
    broadcast_in_dim x1, other arithmetic: 0.01 us -> 0.65 us  [per_device(): second += [column[None], across[None]]]
  transfers between devices with their start and end apart: 22 -> 22, of which waited for: 13 -> 10; matrix products, arithmetic and copies ran while one was open for 3% -> 7% of each run, Pallas kernels for 6% -> 8%
where the time goes in v19:
time: 54.2 us; the launch traced here: 54 us
  starting transfers between devices  27.9 us (51%)
  waiting for transfers between devices  11.9 us (22%)
  Pallas kernels  8.5 us (16%)
  other arithmetic  4.07 us (8%)
  between operations  1.52 us (3%)
    ppermute x14, starting transfers between devices, cube_swap(): return lax.ppermute(x, AXES[1:], pairs)  19.9 us
    ppermute x14, waiting for transfers between devices, cube_swap(): return lax.ppermute(x, AXES[1:], pairs)  9.4 us
    ppermute x8, starting transfers between devices, swap(): lax.ppermute(x, axis, [(i, i ^ mask) for i in range(fine.shape[axis])])  8.01 us
    pallas_call x2, Pallas kernels, per_device(): pl.pallas_call(functools.partial(logits_kernel, n_high, group), out_shape...  3.96 us
    ppermute x8, waiting for transfers between devices, swap(): lax.ppermute(x, axis, [(i, i ^ mask) for i in range(fine.shape[axis])])  2.46 us
    sub x1, other arithmetic, adamw(): master - 0.01 * (first_hat / (jnp.sqrt(second_hat) + 1e-08) + 0.1 * master)  2.19 us
    pallas_call x1, Pallas kernels, per_device(): pl.pallas_call(functools.partial(first_grad_kernel, n_high), out_shape=[s...  2.06 us
    pallas_call x1, Pallas kernels, per_device(): pl.pallas_call(functools.partial(columns_kernel, n_high, 4 * half), out_s...  1.91 us
  transfers between devices with their start and end apart: 22, of which 10 were waited for; matrix products, arithmetic and copies ran while one was open for 7% of the time, Pallas kernels for 8%

profile of v19, /device:TPU:0, one launch (start us, length us, event | category | flops | bytes accessed | tf_op | source)
XLA Modules:
  0.0 54.0 jit_solution(9577052434631702609)
XLA Ops:
  0.6 2.1 %shard_map.93 = (bf16[4,2,192,128]{3,2,1,0:T(8,128)(2,1)S(1)}, bf16[4,2,192,128]{3,2,1,0:T(8,128)(2,1)S(1)}, f32[3,192,128]{2,1,0:T(8,128)S(1)}, bf16[4,256,768]{2,1,0:T(8,128)(2,1)S(1)}, bf16[128,256]{1,0:T(8,128)(2,1)S(1)}) custom-call(bf16[256,6144]{1,0:T(8,128)(2,1)} %acts_ref.2, bf16[256,128]{1,0:T(8,128)(2,1)} %grad_ref.1, f32[384,128]{1,0:T(8,128)} %refs_0_.1, ...), custom_call_target="tpu_custom_call" | custom-call | tf_op jit(solution)/shard_map/pallas_call | solution.py:181
  5.1 2.7 %collective-permute-start.6 = (bf16[2,192,128]{2,1,0:T(8,128)(2,1)S(1)}, bf16[2,192,128]{2,1,0:T(8,128)(2,1)S(1)}, u32[]{:S(2)}, u32[]{:S(2)}) collective-permute-start(bf16[2,192,128]{2,1,0:T(8,128)(2,1)S(1)} %get-tuple-element.69), channel_id=1, source_target_pairs={{0,1},{1,0},{2,14},{3,15},{4,5},{5,4},{6,10},{7,11},{8,9},{9,8},{1... | collective-permute-start | bytes 294920 | tf_op jit(solution)/shard_map/ppermute | solution.py:153
  7.8 2.5 %collective-permute-start.7 = (bf16[2,192,128]{2,1,0:T(8,128)(2,1)S(1)}, bf16[2,192,128]{2,1,0:T(8,128)(2,1)S(1)}, u32[]{:S(2)}, u32[]{:S(2)}) collective-permute-start(bf16[2,192,128]{2,1,0:T(8,128)(2,1)S(1)} %get-tuple-element.68), channel_id=1, source_target_pairs={{0,12},{1,13},{2,3},{3,2},{4,8},{5,9},{6,7},{7,6},{8,4},{9,5},{10,... | collective-permute-start | bytes 294920 | tf_op jit(solution)/shard_map/ppermute | solution.py:153
  10.5 1.9 %collective-permute-start.2 = (bf16[2,192,128]{2,1,0:T(8,128)(2,1)S(1)}, bf16[2,192,128]{2,1,0:T(8,128)(2,1)S(1)}, u32[]{:S(2)}, u32[]{:S(2)}) collective-permute-start(bf16[2,192,128]{2,1,0:T(8,128)(2,1)S(1)} %get-tuple-element.73), channel_id=1, source_target_pairs={{0,4},{1,5},{2,11},{3,10},{4,0},{5,1},{6,15},{7,14},{8,12},{9,13},... | collective-permute-start | bytes 294920 | tf_op jit(solution)/shard_map/ppermute | solution.py:153
  12.4 2.5 %collective-permute-start.3 = (bf16[2,192,128]{2,1,0:T(8,128)(2,1)S(1)}, bf16[2,192,128]{2,1,0:T(8,128)(2,1)S(1)}, u32[]{:S(2)}, u32[]{:S(2)}) collective-permute-start(bf16[2,192,128]{2,1,0:T(8,128)(2,1)S(1)} %get-tuple-element.72), channel_id=1, source_target_pairs={{0,9},{1,8},{2,6},{3,7},{4,13},{5,12},{6,2},{7,3},{8,1},{9,0},{10,... | collective-permute-start | bytes 294920 | tf_op jit(solution)/shard_map/ppermute | solution.py:153
  15.4 1.1 %collective-permute-start.5 = (bf16[2,192,128]{2,1,0:T(8,128)(2,1)S(1)}, bf16[2,192,128]{2,1,0:T(8,128)(2,1)S(1)}, u32[]{:S(2)}, u32[]{:S(2)}) collective-permute-start(bf16[2,192,128]{2,1,0:T(8,128)(2,1)S(1)} %get-tuple-element.70), channel_id=1, source_target_pairs={{0,5},{1,4},{2,10},{3,11},{4,1},{5,0},{6,14},{7,15},{8,13},{9,12},... | collective-permute-start | bytes 294920 | tf_op jit(solution)/shard_map/ppermute | solution.py:153
  16.6 1.9 %collective-permute-done.8 = bf16[2,192,128]{2,1,0:T(8,128)(2,1)S(1)} collective-permute-done((bf16[2,192,128]{2,1,0:T(8,128)(2,1)S(1)}, bf16[2,192,128]{2,1,0:T(8,128)(2,1)S(1)}, u32[]{:S(2)}, u32[]{:S(2)}) %collective-permute-start.8) | collective-permute-done | bytes 98336 | tf_op jit(solution)/shard_map/ppermute | solution.py:153
  18.7 1.1 %collective-permute-done.4 = bf16[2,192,128]{2,1,0:T(8,128)(2,1)S(1)} collective-permute-done((bf16[2,192,128]{2,1,0:T(8,128)(2,1)S(1)}, bf16[2,192,128]{2,1,0:T(8,128)(2,1)S(1)}, u32[]{:S(2)}, u32[]{:S(2)}) %collective-permute-start.4) | collective-permute-done | bytes 98336 | tf_op jit(solution)/shard_map/ppermute | solution.py:153
  19.9 1.1 %collective-permute-done.5 = bf16[2,192,128]{2,1,0:T(8,128)(2,1)S(1)} collective-permute-done((bf16[2,192,128]{2,1,0:T(8,128)(2,1)S(1)}, bf16[2,192,128]{2,1,0:T(8,128)(2,1)S(1)}, u32[]{:S(2)}, u32[]{:S(2)}) %collective-permute-start.5) | collective-permute-done | bytes 98336 | tf_op jit(solution)/shard_map/ppermute | solution.py:153
  21.0 2.6 %collective-permute-start.9 = (bf16[192,128]{1,0:T(8,128)(2,1)S(1)}, bf16[192,128]{1,0:T(8,128)(2,1)S(1)}, u32[]{:S(2)}, u32[]{:S(2)}) collective-permute-start(bf16[192,128]{1,0:T(8,128)(2,1)S(1)} %fusion.11), channel_id=1, source_target_pairs={{0,16},{16,0},{1,17},{17,1},{2,18},{18,2},{3,19},{19,3},{4,20},{20... | collective-permute-start | bytes 147464 | tf_op jit(solution)/shard_map/ppermute | solution.py:143
  24.4 1.7 %collective-permute-done.9 = bf16[192,128]{1,0:T(8,128)(2,1)S(1)} collective-permute-done((bf16[192,128]{1,0:T(8,128)(2,1)S(1)}, bf16[192,128]{1,0:T(8,128)(2,1)S(1)}, u32[]{:S(2)}, u32[]{:S(2)}) %collective-permute-start.9) | collective-permute-done | bytes 49184 | tf_op jit(solution)/shard_map/ppermute | solution.py:143
  26.2 2.7 %collective-permute-start.10 = (bf16[192,128]{1,0:T(8,128)(2,1)S(1)}, bf16[192,128]{1,0:T(8,128)(2,1)S(1)}, u32[]{:S(2)}, u32[]{:S(2)}) collective-permute-start(bf16[192,128]{1,0:T(8,128)(2,1)S(1)} %get-tuple-element.49), channel_id=1, source_target_pairs={{0,16},{16,0},{1,17},{17,1},{2,18},{18,2},{3,19},{19,3},{4,20},{20... | collective-permute-start | bytes 147464 | tf_op jit(solution)/shard_map/ppermute | solution.py:143
  28.9 1.9 %shard_map.95 = (bf16[256,3072]{1,0:T(8,128)(2,1)S(1)}, bf16[256,3072]{1,0:T(8,128)(2,1)S(1)}) custom-call(bf16[256,6144]{1,0:T(8,128)(2,1)} %acts_ref.2), custom_call_target="tpu_custom_call" | custom-call | tf_op jit(solution)/shard_map/pallas_call | solution.py:253
  30.8 1.2 %collective-permute-start.12 = (f32[192,128]{1,0:T(8,128)S(1)}, f32[192,128]{1,0:T(8,128)S(1)}, u32[]{:S(2)}, u32[]{:S(2)}) collective-permute-start(f32[192,128]{1,0:T(8,128)S(1)} %get-tuple-element.64), channel_id=1, source_target_pairs={{0,1},{1,0},{2,3},{3,2},{4,5},{5,4},{6,7},{7,6},{8,9},{9,8},{10,11... | collective-permute-start | bytes 294920 | tf_op jit(solution)/shard_map/ppermute | solution.py:143
  33.3 1.2 %collective-permute-start.13 = (bf16[2,192,128]{2,1,0:T(8,128)(2,1)S(1)}, bf16[2,192,128]{2,1,0:T(8,128)(2,1)S(1)}, u32[]{:S(2)}, u32[]{:S(2)}) collective-permute-start(bf16[2,192,128]{2,1,0:T(8,128)(2,1)S(1)} %get-tuple-element.58), channel_id=1, source_target_pairs={{0,1},{1,0},{2,3},{3,2},{4,5},{5,4},{6,7},{7,6},{8,9},{9,8},{10,11... | collective-permute-start | bytes 294920 | tf_op jit(solution)/shard_map/ppermute | solution.py:153
  34.5 1.7 %collective-permute-start.14 = (bf16[2,192,128]{2,1,0:T(8,128)(2,1)S(1)}, bf16[2,192,128]{2,1,0:T(8,128)(2,1)S(1)}, u32[]{:S(2)}, u32[]{:S(2)}) collective-permute-start(bf16[2,192,128]{2,1,0:T(8,128)(2,1)S(1)} %get-tuple-element.58), channel_id=1, source_target_pairs={{0,8},{1,9},{2,10},{3,11},{4,12},{5,13},{6,14},{7,15},{8,0},{9,1},... | collective-permute-start | bytes 294920 | tf_op jit(solution)/shard_map/ppermute | solution.py:153
  36.2 1.1 %collective-permute-done.11 = bf16[2,192,128]{2,1,0:T(8,128)(2,1)S(1)} collective-permute-done((bf16[2,192,128]{2,1,0:T(8,128)(2,1)S(1)}, bf16[2,192,128]{2,1,0:T(8,128)(2,1)S(1)}, u32[]{:S(2)}, u32[]{:S(2)}) %collective-permute-start.11) | collective-permute-done | bytes 98336 | tf_op jit(solution)/shard_map/ppermute | solution.py:153
  38.2 2.7 %collective-permute-start.20 = (bf16[2,192,128]{2,1,0:T(8,128)(2,1)S(1)}, bf16[2,192,128]{2,1,0:T(8,128)(2,1)S(1)}, u32[]{:S(2)}, u32[]{:S(2)}) collective-permute-start(bf16[2,192,128]{2,1,0:T(8,128)(2,1)S(1)} %collective-permute-done.13), channel_id=1, source_target_pairs={{0,8},{1,9},{2,10},{3,11},{4,12},{5,13},{6,14},{7,15},{8,0},{9,1},... | collective-permute-start | bytes 294920 | tf_op jit(solution)/shard_map/ppermute | solution.py:153
  41.9 1.6 %collective-permute-start.17 = (bf16[2,192,128]{2,1,0:T(8,128)(2,1)S(1)}, bf16[2,192,128]{2,1,0:T(8,128)(2,1)S(1)}, u32[]{:S(2)}, u32[]{:S(2)}) collective-permute-start(bf16[2,192,128]{2,1,0:T(8,128)(2,1)S(1)} %collective-permute-done.16), channel_id=1, source_target_pairs={{0,8},{1,9},{2,10},{3,11},{4,12},{5,13},{6,14},{7,15},{8,0},{9,1},... | collective-permute-start | bytes 294920 | tf_op jit(solution)/shard_map/ppermute | solution.py:153
  43.6 1.9 %collective-permute-done.15 = bf16[2,192,128]{2,1,0:T(8,128)(2,1)S(1)} collective-permute-done((bf16[2,192,128]{2,1,0:T(8,128)(2,1)S(1)}, bf16[2,192,128]{2,1,0:T(8,128)(2,1)S(1)}, u32[]{:S(2)}, u32[]{:S(2)}) %collective-permute-start.15) | collective-permute-done | bytes 98336 | tf_op jit(solution)/shard_map/ppermute | solution.py:153
  45.5 1.0 %collective-permute-done.17 = bf16[2,192,128]{2,1,0:T(8,128)(2,1)S(1)} collective-permute-done((bf16[2,192,128]{2,1,0:T(8,128)(2,1)S(1)}, bf16[2,192,128]{2,1,0:T(8,128)(2,1)S(1)}, u32[]{:S(2)}, u32[]{:S(2)}) %collective-permute-start.17) | collective-permute-done | bytes 98336 | tf_op jit(solution)/shard_map/ppermute | solution.py:153
  47.8 2.2 %multiply_subtract_fusion = (f32[384,128]{1,0:T(8,128)}, f32[384,128]{1,0:T(8,128)}, f32[384,128]{1,0:T(8,128)}) fusion(f32[384,128]{1,0:T(8,128)} %refs_0_.1, f32[]{:T(128)} %bitcast.14, f32[]{:T(128)} %bitcast.12, f32[192,128]{1,0:T(8,128)} %copy-done.1, f32[192,128]{1,0:T(8,128)} %copy-done.2, pred[]{:T(512)S(6)} %eq.3, f32[384,128]{1,0:T(8,128)} %refs_2_.1, ...), kind=kLoop, calls=%fused_computation.8 | loop fusion | flops 884736 | bytes 1376265 | tf_op jit(solution)/shard_map/sub | solution.py:36
  50.0 1.7 %shard_map.96.refs_4_ = f32[256,128]{1,0:T(8,128)S(1)} custom-call(bf16[256,3072]{1,0:T(8,128)(2,1)S(1)} %get-tuple-element.59.columns_ref, bf16[4,2,192,128]{3,2,1,0:T(8,128)(2,1)S(1)} %pad_maximum_fusion.refs_0_, bf16[4,2,192,128]{3,2,1,0:T(8,128)(2,1)} %collective-permute-done.21.refs_1_), custom_call_target="tpu_custom_call" | custom-call | tf_op jit(solution)/shard_map/pallas_call | solution.py:288
  51.7 2.3 %shard_map.97 = bf16[256,128]{1,0:T(8,128)(2,1)} custom-call(bf16[256,3072]{1,0:T(8,128)(2,1)S(1)} %get-tuple-element.55.columns_ref, bf16[3,2,192,128]{3,2,1,0:T(8,128)(2,1)} %pad_maximum_fusion.1.refs_0_, bf16[3,2,192,128]{3,2,1,0:T(8,128)(2,1)} %collective-permute-done.18.refs_1_, bf16[1,2,192,128]{3,2,1,0:T(8,128)(2,1)S(1)} %copy-done, ...), custom_call_target="tpu_custom_call" | custom-call | tf_op jit(solution)/shard_map/pallas_call | solution.py:288
  (45 shorter events, 8.1 us)
Async XLA Ops:
  2.7 1.9 %collective-permute-start = (bf16[4,2,192,128]{3,2,1,0:T(8,128)(2,1)S(1)}, bf16[4,2,192,128]{3,2,1,0:T(8,128)(2,1)S(1)}, u32[]{:S(2)}, u32[]{:S(2)}) collective-permute-start(bf16[4,2,192,128]{3,2,1,0:T(8,128)(2,1)S(1)} %get-tuple-element.35), channel_id=1, source_target_pairs={{0,2},{2,0},{1,3},{3,1},{4,6},{6,4},{5,7},{7,5},{8,10},{10,8},{9,1... | collective-permute-start | bytes 1179656 | tf_op jit(solution)/shard_map/ppermute | solution.py:143
  4.6 5.8 %collective-permute-start.1 = (bf16[4,2,192,128]{3,2,1,0:T(8,128)(2,1)S(1)}, bf16[4,2,192,128]{3,2,1,0:T(8,128)(2,1)S(1)}, u32[]{:S(2)}, u32[]{:S(2)}) collective-permute-start(bf16[4,2,192,128]{3,2,1,0:T(8,128)(2,1)S(1)} %get-tuple-element.37), channel_id=1, source_target_pairs={{0,2},{2,0},{1,3},{3,1},{4,6},{6,4},{5,7},{7,5},{8,10},{10,8},{9,1... | collective-permute-start | bytes 1179656 | tf_op jit(solution)/shard_map/ppermute | solution.py:143
  5.1 9.8 %collective-permute-start.6 = (bf16[2,192,128]{2,1,0:T(8,128)(2,1)S(1)}, bf16[2,192,128]{2,1,0:T(8,128)(2,1)S(1)}, u32[]{:S(2)}, u32[]{:S(2)}) collective-permute-start(bf16[2,192,128]{2,1,0:T(8,128)(2,1)S(1)} %get-tuple-element.69), channel_id=1, source_target_pairs={{0,1},{1,0},{2,14},{3,15},{4,5},{5,4},{6,10},{7,11},{8,9},{9,8},{1... | collective-permute-start | bytes 294920 | tf_op jit(solution)/shard_map/ppermute | solution.py:153
  7.8 7.6 %collective-permute-start.7 = (bf16[2,192,128]{2,1,0:T(8,128)(2,1)S(1)}, bf16[2,192,128]{2,1,0:T(8,128)(2,1)S(1)}, u32[]{:S(2)}, u32[]{:S(2)}) collective-permute-start(bf16[2,192,128]{2,1,0:T(8,128)(2,1)S(1)} %get-tuple-element.68), channel_id=1, source_target_pairs={{0,12},{1,13},{2,3},{3,2},{4,8},{5,9},{6,7},{7,6},{8,4},{9,5},{10,... | collective-permute-start | bytes 294920 | tf_op jit(solution)/shard_map/ppermute | solution.py:153
  10.3 8.1 %collective-permute-start.8 = (bf16[2,192,128]{2,1,0:T(8,128)(2,1)S(1)}, bf16[2,192,128]{2,1,0:T(8,128)(2,1)S(1)}, u32[]{:S(2)}, u32[]{:S(2)}) collective-permute-start(bf16[2,192,128]{2,1,0:T(8,128)(2,1)S(1)} %get-tuple-element.67), channel_id=1, source_target_pairs={{0,13},{1,12},{2,15},{3,14},{4,9},{5,8},{6,11},{7,10},{8,5},{9,4},... | collective-permute-start | bytes 294920 | tf_op jit(solution)/shard_map/ppermute | solution.py:153
  10.5 8.0 %collective-permute-start.2 = (bf16[2,192,128]{2,1,0:T(8,128)(2,1)S(1)}, bf16[2,192,128]{2,1,0:T(8,128)(2,1)S(1)}, u32[]{:S(2)}, u32[]{:S(2)}) collective-permute-start(bf16[2,192,128]{2,1,0:T(8,128)(2,1)S(1)} %get-tuple-element.73), channel_id=1, source_target_pairs={{0,4},{1,5},{2,11},{3,10},{4,0},{5,1},{6,15},{7,14},{8,12},{9,13},... | collective-permute-start | bytes 294920 | tf_op jit(solution)/shard_map/ppermute | solution.py:153
  12.4 6.4 %collective-permute-start.3 = (bf16[2,192,128]{2,1,0:T(8,128)(2,1)S(1)}, bf16[2,192,128]{2,1,0:T(8,128)(2,1)S(1)}, u32[]{:S(2)}, u32[]{:S(2)}) collective-permute-start(bf16[2,192,128]{2,1,0:T(8,128)(2,1)S(1)} %get-tuple-element.72), channel_id=1, source_target_pairs={{0,9},{1,8},{2,6},{3,7},{4,13},{5,12},{6,2},{7,3},{8,1},{9,0},{10,... | collective-permute-start | bytes 294920 | tf_op jit(solution)/shard_map/ppermute | solution.py:153
  14.9 4.9 %collective-permute-start.4 = (bf16[2,192,128]{2,1,0:T(8,128)(2,1)S(1)}, bf16[2,192,128]{2,1,0:T(8,128)(2,1)S(1)}, u32[]{:S(2)}, u32[]{:S(2)}) collective-permute-start(bf16[2,192,128]{2,1,0:T(8,128)(2,1)S(1)} %get-tuple-element.71), channel_id=1, source_target_pairs={{0,8},{1,9},{2,7},{3,6},{4,12},{5,13},{6,3},{7,2},{8,0},{9,1},{10,... | collective-permute-start | bytes 294920 | tf_op jit(solution)/shard_map/ppermute | solution.py:153
  15.4 5.5 %collective-permute-start.5 = (bf16[2,192,128]{2,1,0:T(8,128)(2,1)S(1)}, bf16[2,192,128]{2,1,0:T(8,128)(2,1)S(1)}, u32[]{:S(2)}, u32[]{:S(2)}) collective-permute-start(bf16[2,192,128]{2,1,0:T(8,128)(2,1)S(1)} %get-tuple-element.70), channel_id=1, source_target_pairs={{0,5},{1,4},{2,10},{3,11},{4,1},{5,0},{6,14},{7,15},{8,13},{9,12},... | collective-permute-start | bytes 294920 | tf_op jit(solution)/shard_map/ppermute | solution.py:153
  21.0 5.1 %collective-permute-start.9 = (bf16[192,128]{1,0:T(8,128)(2,1)S(1)}, bf16[192,128]{1,0:T(8,128)(2,1)S(1)}, u32[]{:S(2)}, u32[]{:S(2)}) collective-permute-start(bf16[192,128]{1,0:T(8,128)(2,1)S(1)} %fusion.11), channel_id=1, source_target_pairs={{0,16},{16,0},{1,17},{17,1},{2,18},{18,2},{3,19},{19,3},{4,20},{20... | collective-permute-start | bytes 147464 | tf_op jit(solution)/shard_map/ppermute | solution.py:143
  26.2 5.8 %collective-permute-start.10 = (bf16[192,128]{1,0:T(8,128)(2,1)S(1)}, bf16[192,128]{1,0:T(8,128)(2,1)S(1)}, u32[]{:S(2)}, u32[]{:S(2)}) collective-permute-start(bf16[192,128]{1,0:T(8,128)(2,1)S(1)} %get-tuple-element.49), channel_id=1, source_target_pairs={{0,16},{16,0},{1,17},{17,1},{2,18},{18,2},{3,19},{19,3},{4,20},{20... | collective-permute-start | bytes 147464 | tf_op jit(solution)/shard_map/ppermute | solution.py:143
  30.8 5.3 %collective-permute-start.12 = (f32[192,128]{1,0:T(8,128)S(1)}, f32[192,128]{1,0:T(8,128)S(1)}, u32[]{:S(2)}, u32[]{:S(2)}) collective-permute-start(f32[192,128]{1,0:T(8,128)S(1)} %get-tuple-element.64), channel_id=1, source_target_pairs={{0,1},{1,0},{2,3},{3,2},{4,5},{5,4},{6,7},{7,6},{8,9},{9,8},{10,11... | collective-permute-start | bytes 294920 | tf_op jit(solution)/shard_map/ppermute | solution.py:143
  32.7 8.2 %copy-start.3 = (bf16[2,192,128]{2,1,0:T(8,128)(2,1)}, bf16[2,192,128]{2,1,0:T(8,128)(2,1)S(1)}, u32[]{:S(2)}) copy-start(bf16[2,192,128]{2,1,0:T(8,128)(2,1)S(1)} %get-tuple-element.58) | copy-start | bytes 294916
  32.7 4.6 %collective-permute-start.11 = (bf16[2,192,128]{2,1,0:T(8,128)(2,1)S(1)}, bf16[2,192,128]{2,1,0:T(8,128)(2,1)S(1)}, u32[]{:S(2)}, u32[]{:S(2)}) collective-permute-start(bf16[2,192,128]{2,1,0:T(8,128)(2,1)S(1)} %get-tuple-element.58), channel_id=1, source_target_pairs={{0,4},{1,5},{2,6},{3,7},{4,0},{5,1},{6,2},{7,3},{8,12},{9,13},{10,... | collective-permute-start | bytes 294920 | tf_op jit(solution)/shard_map/ppermute | solution.py:153
  33.3 4.9 %collective-permute-start.13 = (bf16[2,192,128]{2,1,0:T(8,128)(2,1)S(1)}, bf16[2,192,128]{2,1,0:T(8,128)(2,1)S(1)}, u32[]{:S(2)}, u32[]{:S(2)}) collective-permute-start(bf16[2,192,128]{2,1,0:T(8,128)(2,1)S(1)} %get-tuple-element.58), channel_id=1, source_target_pairs={{0,1},{1,0},{2,3},{3,2},{4,5},{5,4},{6,7},{7,6},{8,9},{9,8},{10,11... | collective-permute-start | bytes 294920 | tf_op jit(solution)/shard_map/ppermute | solution.py:153
  34.5 6.4 %collective-permute-start.14 = (bf16[2,192,128]{2,1,0:T(8,128)(2,1)S(1)}, bf16[2,192,128]{2,1,0:T(8,128)(2,1)S(1)}, u32[]{:S(2)}, u32[]{:S(2)}) collective-permute-start(bf16[2,192,128]{2,1,0:T(8,128)(2,1)S(1)} %get-tuple-element.58), channel_id=1, source_target_pairs={{0,8},{1,9},{2,10},{3,11},{4,12},{5,13},{6,14},{7,15},{8,0},{9,1},... | collective-permute-start | bytes 294920 | tf_op jit(solution)/shard_map/ppermute | solution.py:153
  36.2 7.3 %copy-start.2 = (f32[192,128]{1,0:T(8,128)}, f32[192,128]{1,0:T(8,128)S(1)}, u32[]{:S(2)}) copy-start(f32[192,128]{1,0:T(8,128)S(1)} %collective-permute-done.12) | copy-start | bytes 294916
  37.3 4.6 %collective-permute-start.16 = (bf16[2,192,128]{2,1,0:T(8,128)(2,1)S(1)}, bf16[2,192,128]{2,1,0:T(8,128)(2,1)S(1)}, u32[]{:S(2)}, u32[]{:S(2)}) collective-permute-start(bf16[2,192,128]{2,1,0:T(8,128)(2,1)S(1)} %collective-permute-done.11), channel_id=1, source_target_pairs={{0,1},{1,0},{2,3},{3,2},{4,5},{5,4},{6,7},{7,6},{8,9},{9,8},{10,11... | collective-permute-start | bytes 294920 | tf_op jit(solution)/shard_map/ppermute | solution.py:153
  38.2 5.3 %collective-permute-start.20 = (bf16[2,192,128]{2,1,0:T(8,128)(2,1)S(1)}, bf16[2,192,128]{2,1,0:T(8,128)(2,1)S(1)}, u32[]{:S(2)}, u32[]{:S(2)}) collective-permute-start(bf16[2,192,128]{2,1,0:T(8,128)(2,1)S(1)} %collective-permute-done.13), channel_id=1, source_target_pairs={{0,8},{1,9},{2,10},{3,11},{4,12},{5,13},{6,14},{7,15},{8,0},{9,1},... | collective-permute-start | bytes 294920 | tf_op jit(solution)/shard_map/ppermute | solution.py:153
  40.9 4.6 %collective-permute-start.15 = (bf16[2,192,128]{2,1,0:T(8,128)(2,1)S(1)}, bf16[2,192,128]{2,1,0:T(8,128)(2,1)S(1)}, u32[]{:S(2)}, u32[]{:S(2)}) collective-permute-start(bf16[2,192,128]{2,1,0:T(8,128)(2,1)S(1)} %collective-permute-done.14), channel_id=1, source_target_pairs={{0,4},{1,5},{2,6},{3,7},{4,0},{5,1},{6,2},{7,3},{8,12},{9,13},{10,... | collective-permute-start | bytes 294920 | tf_op jit(solution)/shard_map/ppermute | solution.py:153
  41.9 4.6 %collective-permute-start.17 = (bf16[2,192,128]{2,1,0:T(8,128)(2,1)S(1)}, bf16[2,192,128]{2,1,0:T(8,128)(2,1)S(1)}, u32[]{:S(2)}, u32[]{:S(2)}) collective-permute-start(bf16[2,192,128]{2,1,0:T(8,128)(2,1)S(1)} %collective-permute-done.16), channel_id=1, source_target_pairs={{0,8},{1,9},{2,10},{3,11},{4,12},{5,13},{6,14},{7,15},{8,0},{9,1},... | collective-permute-start | bytes 294920 | tf_op jit(solution)/shard_map/ppermute | solution.py:153
  43.5 6.4 %collective-permute-start.21 = (bf16[4,2,192,128]{3,2,1,0:T(8,128)(2,1)S(1)}, bf16[4,2,192,128]{3,2,1,0:T(8,128)(2,1)}, u32[]{:S(2)}, u32[]{:S(2)}) collective-permute-start(bf16[4,2,192,128]{3,2,1,0:T(8,128)(2,1)S(1)} %pad_maximum_fusion.refs_0_), channel_id=1, source_target_pairs={{0,2},{2,0},{1,3},{3,1},{4,6},{6,4},{5,7},{7,5},{8,10},{10,8},{9,1... | collective-permute-start | bytes 1179656 | tf_op jit(solution)/shard_map/ppermute | solution.py:143
  47.3 4.4 %collective-permute-start.18 = (bf16[3,2,192,128]{3,2,1,0:T(8,128)(2,1)}, bf16[3,2,192,128]{3,2,1,0:T(8,128)(2,1)}, u32[]{:S(2)}, u32[]{:S(2)}) collective-permute-start(bf16[3,2,192,128]{3,2,1,0:T(8,128)(2,1)} %pad_maximum_fusion.1.refs_0_), channel_id=1, source_target_pairs={{0,2},{2,0},{1,3},{3,1},{4,6},{6,4},{5,7},{7,5},{8,10},{10,8},{9,1... | collective-permute-start | bytes 884744 | tf_op jit(solution)/shard_map/ppermute | solution.py:143
  47.3 4.4 %collective-permute-start.19 = (bf16[2,192,128]{2,1,0:T(8,128)(2,1)}, bf16[2,192,128]{2,1,0:T(8,128)(2,1)S(1)}, u32[]{:S(2)}, u32[]{:S(2)}) collective-permute-start(bf16[2,192,128]{2,1,0:T(8,128)(2,1)} %copy-done.3), channel_id=1, source_target_pairs={{0,2},{2,0},{1,3},{3,1},{4,6},{6,4},{5,7},{7,5},{8,10},{10,8},{9,1... | collective-permute-start | bytes 294920 | tf_op jit(solution)/shard_map/ppermute | solution.py:143
  (2 other events, 6.3 us)

commit v20 on v17

--- a/solution.py
+++ b/solution.py
@@ -14,11 +14,6 @@
 LOWS = ((1, 2), (0, 3))
 NEXT = ((1, 0), (2, 0), (0, 1))
 VMEM_LIMIT = 8 * 2**20
-
-
-def slot_of(chip, core):
-    slot = CHIPS.index(chip)
-    return slot if slot >= 6 else slot ^ core
 
 
 def position():
@@ -58,9 +53,9 @@
         blocks[...] = product.astype(blocks.dtype).T.reshape(blocks.shape)
         p, j = divmod(n, n_high)
         for d_rep in range(2):
+            chip = CHIPS.index((LOWS[group][p], d_rep)) - 4 * group
             for out, owner in ((kept, core), (away, 1 - core)):
-                slot = slot_of((LOWS[group][p], d_rep), owner)
-                out[slot - 4 * group, j] = blocks[owner, rep ^ d_rep]
+                out[chip, j] = blocks[owner, rep ^ d_rep]
 
 
 def first_grad_kernel(n_high, acts_ref, grad_ref, *refs):
@@ -158,8 +153,9 @@
                     pairs.append(((low * 2 + core) * n_rep + rep, there))
         return lax.ppermute(x, AXES[1:], pairs)
 
-    def to_slot(x, slot):
-        return cube_swap(x, lambda core: CHIPS[slot ^ core if slot < 6 else slot])
+    def to_neighbour(x, axis):
+        change = {"x": (1, 0), "z": (2, 0), "y": (0, 1)}[axis]
+        return cube_swap(x, lambda core: change)
 
     def to_next(x, slot):
         d_low, d_rep = NEXT[slot]
@@ -226,10 +222,8 @@
 
             def sort_rows(owner):
                 blocks = []
-                for slot in range(8):
-                    flip = owner if slot < 6 else 0
-                    d_low, d_rep = CHIPS[slot]
-                    at = (0, low ^ d_low ^ (3 * flip), owner, rep ^ d_rep ^ flip, 0, 0)
+                for d_low, d_rep in CHIPS:
+                    at = (0, low ^ d_low, owner, rep ^ d_rep, 0, 0)
                     part = lax.dynamic_slice(product, at, (n_high, 1, 1, 1, half, experts))
                     blocks.append(part.reshape(n_high, half, experts))
                 return jnp.stack(blocks[:4]), jnp.stack(blocks[4:])
@@ -240,14 +234,16 @@
         arrived = swap(away[1], "core")
         arrived, away_first = lax.optimization_barrier((arrived, away[0]))
         arrived = swap(away_first, "core"), arrived
-        parts = []
-        for own, theirs in zip(kept, arrived):
-            summed = own.astype(f32) + theirs.astype(f32)
-            for n in range(4):
-                slot = len(parts)
-                parts.append(summed[n] if slot == 7 else to_slot(summed[n].astype(bf16), slot))
-        parts = lax.optimization_barrier(parts)
-        total = sum(x.astype(f32) for x in parts)
+        (x, yz, z, xy), (y, zx, corner, home) = [
+            own.astype(f32) + theirs.astype(f32) for own, theirs in zip(kept, arrived)
+        ]
+        corner = to_corner(corner.astype(bf16))
+        z = z + to_neighbour(zx.astype(bf16), "x").astype(f32)
+        y = y + to_neighbour(yz.astype(bf16), "z").astype(f32)
+        x = x + to_neighbour(xy.astype(bf16), "y").astype(f32)
+        parts = [to_neighbour(part.astype(bf16), axis) for part, axis in ((z, "z"), (y, "y"), (x, "x"))]
+        parts = lax.optimization_barrier((corner, *parts))
+        total = home + sum(part.astype(f32) for part in parts)
 
         grad = total[0]
         for j in range(1, n_high):

time: 47.8 us -> 50 us (1.046)
  starting transfers between devices: 25 us -> 26.9 us
    ppermute x11, starting transfers between devices: 17 us -> 18.8 us  [cube_swap(): return lax.ppermute(x, AXES[1:], pairs)]
    ppermute x11, waiting for transfers between devices: 8.52 us -> 9.05 us  [cube_swap(): return lax.ppermute(x, AXES[1:], pairs)]
  transfers between devices with their start and end apart: 19 -> 19, of which waited for: 10 -> 10; matrix products, arithmetic and copies ran while one was open for 3% -> 3% of each run, Pallas kernels for 7% -> 6%
where the time goes in v20:
time: 50 us; the launch traced here: 49.9 us
  starting transfers between devices  26.9 us (54%)
  waiting for transfers between devices  13.5 us (27%)
  Pallas kernels  6.43 us (13%)
  between operations  1.54 us (3%)
  other arithmetic  1.42 us (3%)
    ppermute x11, starting transfers between devices, cube_swap(): return lax.ppermute(x, AXES[1:], pairs)  18.8 us
    ppermute x11, waiting for transfers between devices, cube_swap(): return lax.ppermute(x, AXES[1:], pairs)  9.05 us
    ppermute x8, starting transfers between devices, swap(): lax.ppermute(x, axis, [(i, i ^ mask) for i in range(fine.shape[axis])])  8.02 us
    ppermute x8, waiting for transfers between devices, swap(): lax.ppermute(x, axis, [(i, i ^ mask) for i in range(fine.shape[axis])])  4.47 us
    pallas_call x1, Pallas kernels, per_device(): pl.pallas_call(functools.partial(first_grad_kernel, n_high), out_shape=[s...  2.06 us
    pallas_call x1, Pallas kernels, per_device(): pl.pallas_call(functools.partial(columns_kernel, n_high, 4 * half), out_s...  1.91 us
    pallas_call x2, Pallas kernels, per_device(): pl.pallas_call(functools.partial(logits_kernel, n_high, group), out_shape...  1.9 us
  transfers between devices with their start and end apart: 19, of which 10 were waited for; matrix products, arithmetic and copies ran while one was open for 3% of the time, Pallas kernels for 6%

profile of v20, /device:TPU:0, one launch (start us, length us, event | category | flops | bytes accessed | tf_op | source)
XLA Modules:
  0.0 49.9 jit_solution(4154800893364344919)
XLA Ops:
  0.6 2.1 %shard_map.93 = (bf16[4,2,192,128]{3,2,1,0:T(8,128)(2,1)S(1)}, bf16[4,2,192,128]{3,2,1,0:T(8,128)(2,1)S(1)}, f32[3,192,128]{2,1,0:T(8,128)S(1)}, bf16[4,256,768]{2,1,0:T(8,128)(2,1)S(1)}, bf16[128,256]{1,0:T(8,128)(2,1)S(1)}) custom-call(bf16[256,6144]{1,0:T(8,128)(2,1)} %acts_ref.2, bf16[256,128]{1,0:T(8,128)(2,1)} %grad_ref.1, f32[384,128]{1,0:T(8,128)} %refs_0_.1, ...), custom_call_target="tpu_custom_call" | custom-call | tf_op jit(solution)/shard_map/pallas_call | solution.py:186
  3.8 0.8 %collective-permute-done = bf16[4,2,192,128]{3,2,1,0:T(8,128)(2,1)S(1)} collective-permute-done((bf16[4,2,192,128]{3,2,1,0:T(8,128)(2,1)S(1)}, bf16[4,2,192,128]{3,2,1,0:T(8,128)(2,1)S(1)}, u32[]{:S(2)}, u32[]{:S(2)}) %collective-permute-start) | collective-permute-done | bytes 393248 | tf_op jit(solution)/shard_map/ppermute | solution.py:144
  5.1 2.7 %collective-permute-start.3 = (bf16[2,192,128]{2,1,0:T(8,128)(2,1)S(1)}, bf16[2,192,128]{2,1,0:T(8,128)(2,1)S(1)}, u32[]{:S(2)}, u32[]{:S(2)}) collective-permute-start(bf16[2,192,128]{2,1,0:T(8,128)(2,1)S(1)} %get-tuple-element.73), channel_id=1, source_target_pairs={{0,4},{1,5},{2,6},{3,7},{4,0},{5,1},{6,2},{7,3},{8,12},{9,13},{10,... | collective-permute-start | bytes 294920 | tf_op jit(solution)/shard_map/ppermute | solution.py:154
  7.9 1.6 %collective-permute-start.7 = (bf16[2,192,128]{2,1,0:T(8,128)(2,1)S(1)}, bf16[2,192,128]{2,1,0:T(8,128)(2,1)S(1)}, u32[]{:S(2)}, u32[]{:S(2)}) collective-permute-start(bf16[2,192,128]{2,1,0:T(8,128)(2,1)S(1)} %get-tuple-element.71), channel_id=1, source_target_pairs={{0,1},{1,0},{2,3},{3,2},{4,5},{5,4},{6,7},{7,6},{8,9},{9,8},{10,11... | collective-permute-start | bytes 294920 | tf_op jit(solution)/shard_map/ppermute | solution.py:154
  9.5 2.3 %collective-permute-start.1 = (bf16[2,192,128]{2,1,0:T(8,128)(2,1)S(1)}, bf16[2,192,128]{2,1,0:T(8,128)(2,1)S(1)}, u32[]{:S(2)}, u32[]{:S(2)}) collective-permute-start(bf16[2,192,128]{2,1,0:T(8,128)(2,1)S(1)} %get-tuple-element.74), channel_id=1, source_target_pairs={{0,13},{1,12},{2,15},{3,14},{4,9},{5,8},{6,11},{7,10},{8,5},{9,4},... | collective-permute-start | bytes 294920 | tf_op jit(solution)/shard_map/ppermute | solution.py:154
  12.8 1.6 %collective-permute-start.4 = (bf16[2,192,128]{2,1,0:T(8,128)(2,1)S(1)}, bf16[2,192,128]{2,1,0:T(8,128)(2,1)S(1)}, u32[]{:S(2)}, u32[]{:S(2)}) collective-permute-start(bf16[2,192,128]{2,1,0:T(8,128)(2,1)S(1)} %get-tuple-element.66), channel_id=1, source_target_pairs={{0,8},{1,9},{2,10},{3,11},{4,12},{5,13},{6,14},{7,15},{8,0},{9,1},... | collective-permute-start | bytes 294920 | tf_op jit(solution)/shard_map/ppermute | solution.py:154
  14.5 1.4 %collective-permute-start.8 = (bf16[2,192,128]{2,1,0:T(8,128)(2,1)S(1)}, bf16[2,192,128]{2,1,0:T(8,128)(2,1)S(1)}, u32[]{:S(2)}, u32[]{:S(2)}) collective-permute-start(bf16[2,192,128]{2,1,0:T(8,128)(2,1)S(1)} %get-tuple-element.65), channel_id=1, source_target_pairs={{0,4},{1,5},{2,6},{3,7},{4,0},{5,1},{6,2},{7,3},{8,12},{9,13},{10,... | collective-permute-start | bytes 294920 | tf_op jit(solution)/shard_map/ppermute | solution.py:154
  15.9 2.0 %collective-permute-done.5 = bf16[2,192,128]{2,1,0:T(8,128)(2,1)S(1)} collective-permute-done((bf16[2,192,128]{2,1,0:T(8,128)(2,1)S(1)}, bf16[2,192,128]{2,1,0:T(8,128)(2,1)S(1)}, u32[]{:S(2)}, u32[]{:S(2)}) %collective-permute-start.5) | collective-permute-done | bytes 98336 | tf_op jit(solution)/shard_map/ppermute | solution.py:154
  17.9 1.6 %collective-permute-start.6 = (bf16[2,192,128]{2,1,0:T(8,128)(2,1)S(1)}, bf16[2,192,128]{2,1,0:T(8,128)(2,1)S(1)}, u32[]{:S(2)}, u32[]{:S(2)}) collective-permute-start(bf16[2,192,128]{2,1,0:T(8,128)(2,1)S(1)} %fusion.4), channel_id=1, source_target_pairs={{0,1},{1,0},{2,3},{3,2},{4,5},{5,4},{6,7},{7,6},{8,9},{9,8},{10,11... | collective-permute-start | bytes 294920 | tf_op jit(solution)/shard_map/ppermute | solution.py:154
  19.5 3.1 %collective-permute-done.6 = bf16[2,192,128]{2,1,0:T(8,128)(2,1)S(1)} collective-permute-done((bf16[2,192,128]{2,1,0:T(8,128)(2,1)S(1)}, bf16[2,192,128]{2,1,0:T(8,128)(2,1)S(1)}, u32[]{:S(2)}, u32[]{:S(2)}) %collective-permute-start.6) | collective-permute-done | bytes 98336 | tf_op jit(solution)/shard_map/ppermute | solution.py:154
  22.7 2.6 %collective-permute-start.9 = (bf16[192,128]{1,0:T(8,128)(2,1)S(1)}, bf16[192,128]{1,0:T(8,128)(2,1)S(1)}, u32[]{:S(2)}, u32[]{:S(2)}) collective-permute-start(bf16[192,128]{1,0:T(8,128)(2,1)S(1)} %fusion.18), channel_id=1, source_target_pairs={{0,16},{16,0},{1,17},{17,1},{2,18},{18,2},{3,19},{19,3},{4,20},{20... | collective-permute-start | bytes 147464 | tf_op jit(solution)/shard_map/ppermute | solution.py:144
  26.0 1.9 %collective-permute-done.9 = bf16[192,128]{1,0:T(8,128)(2,1)S(1)} collective-permute-done((bf16[192,128]{1,0:T(8,128)(2,1)S(1)}, bf16[192,128]{1,0:T(8,128)(2,1)S(1)}, u32[]{:S(2)}, u32[]{:S(2)}) %collective-permute-start.9) | collective-permute-done | bytes 49184 | tf_op jit(solution)/shard_map/ppermute | solution.py:144
  28.0 2.7 %collective-permute-start.10 = (bf16[192,128]{1,0:T(8,128)(2,1)S(1)}, bf16[192,128]{1,0:T(8,128)(2,1)S(1)}, u32[]{:S(2)}, u32[]{:S(2)}) collective-permute-start(bf16[192,128]{1,0:T(8,128)(2,1)S(1)} %get-tuple-element.63), channel_id=1, source_target_pairs={{0,16},{16,0},{1,17},{17,1},{2,18},{18,2},{3,19},{19,3},{4,20},{20... | collective-permute-start | bytes 147464 | tf_op jit(solution)/shard_map/ppermute | solution.py:144
  30.8 1.5 %collective-permute-start.12 = (f32[192,128]{1,0:T(8,128)S(1)}, f32[192,128]{1,0:T(8,128)S(1)}, u32[]{:S(2)}, u32[]{:S(2)}) collective-permute-start(f32[192,128]{1,0:T(8,128)S(1)} %get-tuple-element.64), channel_id=1, source_target_pairs={{0,1},{1,0},{2,3},{3,2},{4,5},{5,4},{6,7},{7,6},{8,9},{9,8},{10,11... | collective-permute-start | bytes 294920 | tf_op jit(solution)/shard_map/ppermute | solution.py:144
  32.3 0.8 %collective-permute-done.10 = bf16[192,128]{1,0:T(8,128)(2,1)S(1)} collective-permute-done((bf16[192,128]{1,0:T(8,128)(2,1)S(1)}, bf16[192,128]{1,0:T(8,128)(2,1)S(1)}, u32[]{:S(2)}, u32[]{:S(2)}) %collective-permute-start.10) | collective-permute-done | bytes 49184 | tf_op jit(solution)/shard_map/ppermute | solution.py:144
  33.2 3.6 %collective-permute-start.14 = (bf16[2,192,128]{2,1,0:T(8,128)(2,1)S(1)}, bf16[2,192,128]{2,1,0:T(8,128)(2,1)S(1)}, u32[]{:S(2)}, u32[]{:S(2)}) collective-permute-start(bf16[2,192,128]{2,1,0:T(8,128)(2,1)S(1)} %get-tuple-element.76), channel_id=1, source_target_pairs={{0,13},{1,12},{2,15},{3,14},{4,9},{5,8},{6,11},{7,10},{8,5},{9,4},... | collective-permute-start | bytes 294920 | tf_op jit(solution)/shard_map/ppermute | solution.py:154
  36.8 1.4 %collective-permute-start.13 = (bf16[2,2,192,128]{3,2,1,0:T(8,128)(2,1)S(1)}, bf16[2,2,192,128]{3,2,1,0:T(8,128)(2,1)S(1)}, u32[]{:S(2)}, u32[]{:S(2)}) collective-permute-start(bf16[2,2,192,128]{3,2,1,0:T(8,128)(2,1)S(1)} %maximum_select_fusion), channel_id=1, source_target_pairs={{0,4},{1,5},{2,11},{3,10},{4,0},{5,1},{6,15},{7,14},{8,12},{9,13},... | collective-permute-start | bytes 589832 | tf_op jit(solution)/shard_map/ppermute | solution.py:154
  38.8 1.5 %collective-permute-start.15 = (bf16[2,2,192,128]{3,2,1,0:T(8,128)(2,1)S(1)}, bf16[2,2,192,128]{3,2,1,0:T(8,128)(2,1)S(1)}, u32[]{:S(2)}, u32[]{:S(2)}) collective-permute-start(bf16[2,2,192,128]{3,2,1,0:T(8,128)(2,1)S(1)} %maximum_select_fusion), channel_id=1, source_target_pairs={{0,1},{1,0},{2,14},{3,15},{4,5},{5,4},{6,10},{7,11},{8,9},{9,8},{1... | collective-permute-start | bytes 589832 | tf_op jit(solution)/shard_map/ppermute | solution.py:154
  40.4 0.9 %multiply_subtract_fusion = (f32[384,128]{1,0:T(8,128)}, f32[384,128]{1,0:T(8,128)}, f32[384,128]{1,0:T(8,128)}) fusion(f32[384,128]{1,0:T(8,128)S(1)} %copy-done, f32[]{:T(128)} %bitcast.14, f32[]{:T(128)} %bitcast.12, f32[192,128]{1,0:T(8,128)S(1)} %get-tuple-element.64, f32[192,128]{1,0:T(8,128)S(1)} %collective-permute-done.12, pred[]{:T(512)S(6)} %eq.7, ...), kind=kLoop, calls=%fused_computation.18 | loop fusion | flops 884736 | bytes 1376265 | tf_op jit(solution)/shard_map/sub | solution.py:31
  41.3 1.9 %shard_map.95 = (bf16[256,3072]{1,0:T(8,128)(2,1)S(1)}, bf16[256,3072]{1,0:T(8,128)(2,1)S(1)}) custom-call(bf16[256,6144]{1,0:T(8,128)(2,1)} %acts_ref.2), custom_call_target="tpu_custom_call" | custom-call | tf_op jit(solution)/shard_map/pallas_call | solution.py:271
  43.2 2.7 %collective-permute-done.13 = bf16[2,2,192,128]{3,2,1,0:T(8,128)(2,1)S(1)} collective-permute-done((bf16[2,2,192,128]{3,2,1,0:T(8,128)(2,1)S(1)}, bf16[2,2,192,128]{3,2,1,0:T(8,128)(2,1)S(1)}, u32[]{:S(2)}, u32[]{:S(2)}) %collective-permute-start.13) | collective-permute-done | bytes 196640 | tf_op jit(solution)/shard_map/ppermute | solution.py:154
  46.9 1.0 %collective-permute-done.18.refs_1_ = bf16[4,2,192,128]{3,2,1,0:T(8,128)(2,1)S(1)} collective-permute-done((bf16[4,2,192,128]{3,2,1,0:T(8,128)(2,1)S(1)}, bf16[4,2,192,128]{3,2,1,0:T(8,128)(2,1)S(1)}, u32[]{:S(2)}, u32[]{:S(2)}) %collective-permute-start.18) | collective-permute-done | bytes 393248 | tf_op jit(solution)/shard_map/ppermute | solution.py:144
  47.9 0.6 %shard_map.96.refs_4_ = f32[256,128]{1,0:T(8,128)S(1)} custom-call(bf16[256,3072]{1,0:T(8,128)(2,1)S(1)} %get-tuple-element.58.columns_ref, bf16[4,2,192,128]{3,2,1,0:T(8,128)(2,1)S(1)} %constant_dynamic-update-slice_fusion.refs_0_, bf16[4,2,192,128]{3,2,1,0:T(8,128)(2,1)S(1)} %collective-permute-done.18.refs_1_), custom_call_target="tpu_custom_call" | custom-call | tf_op jit(solution)/shard_map/pallas_call | solution.py:291
  48.6 1.3 %shard_map.97 = bf16[256,128]{1,0:T(8,128)(2,1)} custom-call(bf16[256,3072]{1,0:T(8,128)(2,1)S(1)} %get-tuple-element.56.columns_ref, bf16[3,2,192,128]{3,2,1,0:T(8,128)(2,1)S(1)} %pad_maximum_fusion.refs_0_, bf16[3,2,192,128]{3,2,1,0:T(8,128)(2,1)S(1)} %collective-permute-done.16.refs_1_, bf16[1,2,192,128]{3,2,1,0:T(8,128)(2,1)S(1)} %get-tuple-element.75.refs_2_, ...), custom_call_target="tpu_custom_call" | custom-call | tf_op jit(solution)/shard_map/pallas_call | solution.py:291
  (40 shorter events, 4.7 us)
Async XLA Ops:
  2.7 1.9 %collective-permute-start = (bf16[4,2,192,128]{3,2,1,0:T(8,128)(2,1)S(1)}, bf16[4,2,192,128]{3,2,1,0:T(8,128)(2,1)S(1)}, u32[]{:S(2)}, u32[]{:S(2)}) collective-permute-start(bf16[4,2,192,128]{3,2,1,0:T(8,128)(2,1)S(1)} %get-tuple-element.34), channel_id=1, source_target_pairs={{0,2},{2,0},{1,3},{3,1},{4,6},{6,4},{5,7},{7,5},{8,10},{10,8},{9,1... | collective-permute-start | bytes 1179656 | tf_op jit(solution)/shard_map/ppermute | solution.py:144
  4.6 3.2 %collective-permute-start.2 = (bf16[4,2,192,128]{3,2,1,0:T(8,128)(2,1)S(1)}, bf16[4,2,192,128]{3,2,1,0:T(8,128)(2,1)S(1)}, u32[]{:S(2)}, u32[]{:S(2)}) collective-permute-start(bf16[4,2,192,128]{3,2,1,0:T(8,128)(2,1)S(1)} %get-tuple-element.40), channel_id=1, source_target_pairs={{0,2},{2,0},{1,3},{3,1},{4,6},{6,4},{5,7},{7,5},{8,10},{10,8},{9,1... | collective-permute-start | bytes 1179656 | tf_op jit(solution)/shard_map/ppermute | solution.py:144
  5.1 7.2 %collective-permute-start.3 = (bf16[2,192,128]{2,1,0:T(8,128)(2,1)S(1)}, bf16[2,192,128]{2,1,0:T(8,128)(2,1)S(1)}, u32[]{:S(2)}, u32[]{:S(2)}) collective-permute-start(bf16[2,192,128]{2,1,0:T(8,128)(2,1)S(1)} %get-tuple-element.73), channel_id=1, source_target_pairs={{0,4},{1,5},{2,6},{3,7},{4,0},{5,1},{6,2},{7,3},{8,12},{9,13},{10,... | collective-permute-start | bytes 294920 | tf_op jit(solution)/shard_map/ppermute | solution.py:154
  7.9 4.8 %collective-permute-start.7 = (bf16[2,192,128]{2,1,0:T(8,128)(2,1)S(1)}, bf16[2,192,128]{2,1,0:T(8,128)(2,1)S(1)}, u32[]{:S(2)}, u32[]{:S(2)}) collective-permute-start(bf16[2,192,128]{2,1,0:T(8,128)(2,1)S(1)} %get-tuple-element.71), channel_id=1, source_target_pairs={{0,1},{1,0},{2,3},{3,2},{4,5},{5,4},{6,7},{7,6},{8,9},{9,8},{10,11... | collective-permute-start | bytes 294920 | tf_op jit(solution)/shard_map/ppermute | solution.py:154
  9.5 10.0 %collective-permute-start.1 = (bf16[2,192,128]{2,1,0:T(8,128)(2,1)S(1)}, bf16[2,192,128]{2,1,0:T(8,128)(2,1)S(1)}, u32[]{:S(2)}, u32[]{:S(2)}) collective-permute-start(bf16[2,192,128]{2,1,0:T(8,128)(2,1)S(1)} %get-tuple-element.74), channel_id=1, source_target_pairs={{0,13},{1,12},{2,15},{3,14},{4,9},{5,8},{6,11},{7,10},{8,5},{9,4},... | collective-permute-start | bytes 294920 | tf_op jit(solution)/shard_map/ppermute | solution.py:154
  11.8 6.0 %collective-permute-start.5 = (bf16[2,192,128]{2,1,0:T(8,128)(2,1)S(1)}, bf16[2,192,128]{2,1,0:T(8,128)(2,1)S(1)}, u32[]{:S(2)}, u32[]{:S(2)}) collective-permute-start(bf16[2,192,128]{2,1,0:T(8,128)(2,1)S(1)} %get-tuple-element.72), channel_id=1, source_target_pairs={{0,8},{1,9},{2,10},{3,11},{4,12},{5,13},{6,14},{7,15},{8,0},{9,1},... | collective-permute-start | bytes 294920 | tf_op jit(solution)/shard_map/ppermute | solution.py:154
  12.8 27.6 %copy-start = (f32[384,128]{1,0:T(8,128)S(1)}, f32[384,128]{1,0:T(8,128)}, u32[]{:S(2)}) copy-start(f32[384,128]{1,0:T(8,128)} %refs_0_.1) | copy-start | bytes 589828
  12.8 27.6 %copy-start.1 = (f32[384,128]{1,0:T(8,128)S(1)}, f32[384,128]{1,0:T(8,128)}, u32[]{:S(2)}) copy-start(f32[384,128]{1,0:T(8,128)} %refs_1_.1) | copy-start | bytes 589828
  12.8 27.6 %copy-start.2 = (f32[384,128]{1,0:T(8,128)S(1)}, f32[384,128]{1,0:T(8,128)}, u32[]{:S(2)}) copy-start(f32[384,128]{1,0:T(8,128)} %refs_2_.1) | copy-start | bytes 589828
  12.8 6.7 %collective-permute-start.4 = (bf16[2,192,128]{2,1,0:T(8,128)(2,1)S(1)}, bf16[2,192,128]{2,1,0:T(8,128)(2,1)S(1)}, u32[]{:S(2)}, u32[]{:S(2)}) collective-permute-start(bf16[2,192,128]{2,1,0:T(8,128)(2,1)S(1)} %get-tuple-element.66), channel_id=1, source_target_pairs={{0,8},{1,9},{2,10},{3,11},{4,12},{5,13},{6,14},{7,15},{8,0},{9,1},... | collective-permute-start | bytes 294920 | tf_op jit(solution)/shard_map/ppermute | solution.py:154
  14.5 5.0 %collective-permute-start.8 = (bf16[2,192,128]{2,1,0:T(8,128)(2,1)S(1)}, bf16[2,192,128]{2,1,0:T(8,128)(2,1)S(1)}, u32[]{:S(2)}, u32[]{:S(2)}) collective-permute-start(bf16[2,192,128]{2,1,0:T(8,128)(2,1)S(1)} %get-tuple-element.65), channel_id=1, source_target_pairs={{0,4},{1,5},{2,6},{3,7},{4,0},{5,1},{6,2},{7,3},{8,12},{9,13},{10,... | collective-permute-start | bytes 294920 | tf_op jit(solution)/shard_map/ppermute | solution.py:154
  17.9 4.7 %collective-permute-start.6 = (bf16[2,192,128]{2,1,0:T(8,128)(2,1)S(1)}, bf16[2,192,128]{2,1,0:T(8,128)(2,1)S(1)}, u32[]{:S(2)}, u32[]{:S(2)}) collective-permute-start(bf16[2,192,128]{2,1,0:T(8,128)(2,1)S(1)} %fusion.4), channel_id=1, source_target_pairs={{0,1},{1,0},{2,3},{3,2},{4,5},{5,4},{6,7},{7,6},{8,9},{9,8},{10,11... | collective-permute-start | bytes 294920 | tf_op jit(solution)/shard_map/ppermute | solution.py:154
  22.7 5.3 %collective-permute-start.9 = (bf16[192,128]{1,0:T(8,128)(2,1)S(1)}, bf16[192,128]{1,0:T(8,128)(2,1)S(1)}, u32[]{:S(2)}, u32[]{:S(2)}) collective-permute-start(bf16[192,128]{1,0:T(8,128)(2,1)S(1)} %fusion.18), channel_id=1, source_target_pairs={{0,16},{16,0},{1,17},{17,1},{2,18},{18,2},{3,19},{19,3},{4,20},{20... | collective-permute-start | bytes 147464 | tf_op jit(solution)/shard_map/ppermute | solution.py:144
  28.0 5.1 %collective-permute-start.10 = (bf16[192,128]{1,0:T(8,128)(2,1)S(1)}, bf16[192,128]{1,0:T(8,128)(2,1)S(1)}, u32[]{:S(2)}, u32[]{:S(2)}) collective-permute-start(bf16[192,128]{1,0:T(8,128)(2,1)S(1)} %get-tuple-element.63), channel_id=1, source_target_pairs={{0,16},{16,0},{1,17},{17,1},{2,18},{18,2},{3,19},{19,3},{4,20},{20... | collective-permute-start | bytes 147464 | tf_op jit(solution)/shard_map/ppermute | solution.py:144
  30.8 6.0 %collective-permute-start.12 = (f32[192,128]{1,0:T(8,128)S(1)}, f32[192,128]{1,0:T(8,128)S(1)}, u32[]{:S(2)}, u32[]{:S(2)}) collective-permute-start(f32[192,128]{1,0:T(8,128)S(1)} %get-tuple-element.64), channel_id=1, source_target_pairs={{0,1},{1,0},{2,3},{3,2},{4,5},{5,4},{6,7},{7,6},{8,9},{9,8},{10,11... | collective-permute-start | bytes 294920 | tf_op jit(solution)/shard_map/ppermute | solution.py:144
  33.1 3.7 %collective-permute-start.11 = (bf16[2,192,128]{2,1,0:T(8,128)(2,1)S(1)}, bf16[2,192,128]{2,1,0:T(8,128)(2,1)S(1)}, u32[]{:S(2)}, u32[]{:S(2)}) collective-permute-start(bf16[2,192,128]{2,1,0:T(8,128)(2,1)S(1)} %get-tuple-element.76), channel_id=1, source_target_pairs={{0,2},{2,0},{1,3},{3,1},{4,6},{6,4},{5,7},{7,5},{8,10},{10,8},{9,1... | collective-permute-start | bytes 294920 | tf_op jit(solution)/shard_map/ppermute | solution.py:144
  33.2 10.0 %collective-permute-start.14 = (bf16[2,192,128]{2,1,0:T(8,128)(2,1)S(1)}, bf16[2,192,128]{2,1,0:T(8,128)(2,1)S(1)}, u32[]{:S(2)}, u32[]{:S(2)}) collective-permute-start(bf16[2,192,128]{2,1,0:T(8,128)(2,1)S(1)} %get-tuple-element.76), channel_id=1, source_target_pairs={{0,13},{1,12},{2,15},{3,14},{4,9},{5,8},{6,11},{7,10},{8,5},{9,4},... | collective-permute-start | bytes 294920 | tf_op jit(solution)/shard_map/ppermute | solution.py:154
  36.8 9.1 %collective-permute-start.13 = (bf16[2,2,192,128]{3,2,1,0:T(8,128)(2,1)S(1)}, bf16[2,2,192,128]{3,2,1,0:T(8,128)(2,1)S(1)}, u32[]{:S(2)}, u32[]{:S(2)}) collective-permute-start(bf16[2,2,192,128]{3,2,1,0:T(8,128)(2,1)S(1)} %maximum_select_fusion), channel_id=1, source_target_pairs={{0,4},{1,5},{2,11},{3,10},{4,0},{5,1},{6,15},{7,14},{8,12},{9,13},... | collective-permute-start | bytes 589832 | tf_op jit(solution)/shard_map/ppermute | solution.py:154
  38.2 7.9 %collective-permute-start.17 = (bf16[2,2,192,128]{3,2,1,0:T(8,128)(2,1)S(1)}, bf16[2,2,192,128]{3,2,1,0:T(8,128)(2,1)S(1)}, u32[]{:S(2)}, u32[]{:S(2)}) collective-permute-start(bf16[2,2,192,128]{3,2,1,0:T(8,128)(2,1)S(1)} %maximum_select_fusion), channel_id=1, source_target_pairs={{0,8},{1,9},{2,7},{3,6},{4,12},{5,13},{6,3},{7,2},{8,0},{9,1},{10,... | collective-permute-start | bytes 589832 | tf_op jit(solution)/shard_map/ppermute | solution.py:154
  38.8 8.0 %collective-permute-start.15 = (bf16[2,2,192,128]{3,2,1,0:T(8,128)(2,1)S(1)}, bf16[2,2,192,128]{3,2,1,0:T(8,128)(2,1)S(1)}, u32[]{:S(2)}, u32[]{:S(2)}) collective-permute-start(bf16[2,2,192,128]{3,2,1,0:T(8,128)(2,1)S(1)} %maximum_select_fusion), channel_id=1, source_target_pairs={{0,1},{1,0},{2,14},{3,15},{4,5},{5,4},{6,10},{7,11},{8,9},{9,8},{1... | collective-permute-start | bytes 589832 | tf_op jit(solution)/shard_map/ppermute | solution.py:154
  46.2 1.8 %collective-permute-start.18 = (bf16[4,2,192,128]{3,2,1,0:T(8,128)(2,1)S(1)}, bf16[4,2,192,128]{3,2,1,0:T(8,128)(2,1)S(1)}, u32[]{:S(2)}, u32[]{:S(2)}) collective-permute-start(bf16[4,2,192,128]{3,2,1,0:T(8,128)(2,1)S(1)} %constant_dynamic-update-slice_fusion.refs_0_), channel_id=1, source_target_pairs={{0,2},{2,0},{1,3},{3,1},{4,6},{6,4},{5,7},{7,5},{8,10},{10,8},{9,1... | collective-permute-start | bytes 1179656 | tf_op jit(solution)/shard_map/ppermute | solution.py:144
  46.9 1.7 %collective-permute-start.16 = (bf16[3,2,192,128]{3,2,1,0:T(8,128)(2,1)S(1)}, bf16[3,2,192,128]{3,2,1,0:T(8,128)(2,1)S(1)}, u32[]{:S(2)}, u32[]{:S(2)}) collective-permute-start(bf16[3,2,192,128]{3,2,1,0:T(8,128)(2,1)S(1)} %pad_maximum_fusion.refs_0_), channel_id=1, source_target_pairs={{0,2},{2,0},{1,3},{3,1},{4,6},{6,4},{5,7},{7,5},{8,10},{10,8},{9,1... | collective-permute-start | bytes 884744 | tf_op jit(solution)/shard_map/ppermute | solution.py:144

commit v21 on v17

--- a/solution.py
+++ b/solution.py
@@ -58,14 +58,16 @@
         blocks[...] = product.astype(blocks.dtype).T.reshape(blocks.shape)
         p, j = divmod(n, n_high)
         for d_rep in range(2):
-            for out, owner in ((kept, core), (away, 1 - core)):
-                slot = slot_of((LOWS[group][p], d_rep), owner)
-                out[slot - 4 * group, j] = blocks[owner, rep ^ d_rep]
+            chip = LOWS[group][p], d_rep
+            left = CHIPS.index(chip) >= 6
+            for outs, owner in ((kept, core), (away, 1 - core)):
+                outs[left][slot_of(chip, owner) - (6 if left else 4 * group), j] = blocks[owner, rep ^ d_rep]
 
 
 def first_grad_kernel(n_high, acts_ref, grad_ref, *refs):
     state_refs, refs = refs[:3], refs[3:]
-    away, kept, mine_ref, later_ref, turned_ref, columns, logit_grads, blocks, sems = refs
+    away, kept, refs = refs[:2], refs[2:4], refs[4:]
+    mine_ref, later_ref, turned_ref, columns, logit_grads, blocks, sems = refs
     _, _, _, rep = position()
     half = blocks.shape[2]
     loads = pltpu.make_async_copy(grad_ref, logit_grads, sems.at[2, 0])
@@ -92,7 +94,7 @@
 
 
 def second_grad_kernel(n_high, columns, turned_ref, away, kept, blocks):
-    sort_products(n_high, 0, turned_ref[...], columns, away, kept, blocks, lambda n: None)
+    sort_products(n_high, 0, turned_ref[...], columns, [away], [kept], blocks, lambda n: None)
 
 
 def columns_kernel(n_high, wide, acts_ref, first_ref, second_ref, sems):
@@ -187,11 +189,12 @@
             columns_shape = pltpu.VMEM((2 * n_high, tokens, 4 * half), bf16)
             blocks = pltpu.VMEM((2, 2, half, experts), bf16)
             turned = pltpu.VMEM((experts, tokens), bf16)
-            away_second, kept_second, mine, later, turned = pl.pallas_call(
+            pair = pltpu.VMEM((2, n_high, half, experts), bf16)
+            *sorted_rows, mine, later, turned = pl.pallas_call(
                 functools.partial(first_grad_kernel, n_high),
-                out_shape=[shape, shape, pltpu.VMEM((3, half, experts), f32), columns_shape, turned],
+                out_shape=[pair] * 4 + [pltpu.VMEM((3, half, experts), f32), columns_shape, turned],
                 in_specs=[anywhere] * 5,
-                out_specs=[vmem] * 5,
+                out_specs=[vmem] * 7,
                 scratch_shapes=[
                     columns_shape,
                     pltpu.VMEM((tokens, experts), bf16),
@@ -216,7 +219,7 @@
                 ),
                 compiler_params=params,
             )(*(pltpu.with_memory_space_constraint(x, pltpu.VMEM) for x in (later, turned)))
-            away, kept = (away_first, away_second), (kept_first, kept_second)
+            away, kept = (*sorted_rows[:2], away_first), (*sorted_rows[2:], kept_first)
         else:
             product = lax.dot_general(
                 acts, grad_logits, (((0,), (0,)), ((), ())), preferred_element_type=f32
@@ -232,21 +235,19 @@
                     at = (0, low ^ d_low ^ (3 * flip), owner, rep ^ d_rep ^ flip, 0, 0)
                     part = lax.dynamic_slice(product, at, (n_high, 1, 1, 1, half, experts))
                     blocks.append(part.reshape(n_high, half, experts))
-                return jnp.stack(blocks[:4]), jnp.stack(blocks[4:])
+                return jnp.stack(blocks[4:6]), jnp.stack(blocks[6:]), jnp.stack(blocks[:4])
 
             away, kept = sort_rows(1 - core), sort_rows(core)
             mine = jnp.stack([lax.dynamic_slice_in_dim(x, rep * half, half, 0) for x in state_in])
 
-        arrived = swap(away[1], "core")
-        arrived, away_first = lax.optimization_barrier((arrived, away[0]))
-        arrived = swap(away_first, "core"), arrived
-        parts = []
-        for own, theirs in zip(kept, arrived):
-            summed = own.astype(f32) + theirs.astype(f32)
-            for n in range(4):
-                slot = len(parts)
-                parts.append(summed[n] if slot == 7 else to_slot(summed[n].astype(bf16), slot))
-        parts = lax.optimization_barrier(parts)
+        arrived = swap(away[0], "core")
+        arrived, *rest = lax.optimization_barrier((arrived, *away[1:]))
+        arrived = [arrived] + [swap(x, "core") for x in rest]
+        pair, left, first = [own.astype(f32) + x.astype(f32) for own, x in zip(kept, arrived)]
+        parts = [to_slot(x.astype(bf16), 4 + n) for n, x in enumerate(pair)]
+        parts += [to_slot(left[0].astype(bf16), 6)]
+        parts += [to_slot(x.astype(bf16), n) for n, x in enumerate(first)]
+        parts = [left[1], *lax.optimization_barrier(parts)]
         total = sum(x.astype(f32) for x in parts)
 
         grad = total[0]

time: 47.8 us -> 48 us (level)
    ppermute x8 -> x9, waiting for transfers between devices: 4.63 us -> 4.28 us  [swap(): lax.ppermute(x, axis, [(i, i ^ mask) for i in range(fine.shape[axis])])]
    ppermute x8 -> x9, starting transfers between devices: 8.03 us -> 8.06 us  [swap(): lax.ppermute(x, axis, [(i, i ^ mask) for i in range(fine.shape[axis])])]
  transfers between devices with their start and end apart: 19 -> 20, of which waited for: 10 -> 10; matrix products, arithmetic and copies ran while one was open for 3% -> 3% of each run, Pallas kernels for 7% -> 7%
where the time goes in v21:
time: 48 us; the launch traced here: 47.8 us
  starting transfers between devices  25.2 us (52%)
  waiting for transfers between devices  13.1 us (27%)
  Pallas kernels  6.44 us (13%)
  between operations  1.54 us (3%)
  other arithmetic  1.35 us (3%)
    ppermute x11, starting transfers between devices, cube_swap(): return lax.ppermute(x, AXES[1:], pairs)  17.1 us
    ppermute x11, waiting for transfers between devices, cube_swap(): return lax.ppermute(x, AXES[1:], pairs)  8.84 us
    ppermute x9, starting transfers between devices, swap(): lax.ppermute(x, axis, [(i, i ^ mask) for i in range(fine.shape[axis])])  8.06 us
    ppermute x9, waiting for transfers between devices, swap(): lax.ppermute(x, axis, [(i, i ^ mask) for i in range(fine.shape[axis])])  4.28 us
    pallas_call x1, Pallas kernels, per_device(): pl.pallas_call(functools.partial(first_grad_kernel, n_high), out_shape=[p...  2.07 us
    pallas_call x1, Pallas kernels, per_device(): pl.pallas_call(functools.partial(columns_kernel, n_high, 4 * half), out_s...  1.91 us
    pallas_call x2, Pallas kernels, per_device(): pl.pallas_call(functools.partial(logits_kernel, n_high, group), out_shape...  1.89 us
  transfers between devices with their start and end apart: 20, of which 10 were waited for; matrix products, arithmetic and copies ran while one was open for 3% of the time, Pallas kernels for 7%

profile of v21, /device:TPU:0, one launch (start us, length us, event | category | flops | bytes accessed | tf_op | source)
XLA Modules:
  0.0 47.8 jit_solution(1693446273367933941)
XLA Ops:
  0.6 2.1 %shard_map.93 = (bf16[2,2,192,128]{3,2,1,0:T(8,128)(2,1)S(1)}, bf16[2,2,192,128]{3,2,1,0:T(8,128)(2,1)S(1)}, bf16[2,2,192,128]{3,2,1,0:T(8,128)(2,1)S(1)}, bf16[...) custom-call(bf16[256,6144]{1,0:T(8,128)(2,1)} %acts_ref.2, ...), custom_call_target="tpu_custom_call" | custom-call | tf_op jit(solution)/shard_map/pallas_call | solution.py:193
  4.9 3.0 %collective-permute-start.2 = (bf16[2,192,128]{2,1,0:T(8,128)(2,1)S(1)}, bf16[2,192,128]{2,1,0:T(8,128)(2,1)S(1)}, u32[]{:S(2)}, u32[]{:S(2)}) collective-permute-start(bf16[2,192,128]{2,1,0:T(8,128)(2,1)S(1)} %get-tuple-element.82), channel_id=1, source_target_pairs={{0,1},{1,0},{2,14},{3,15},{4,5},{5,4},{6,10},{7,11},{8,9},{9,8},{1... | collective-permute-start | bytes 294920 | tf_op jit(solution)/shard_map/ppermute | solution.py:161
  7.9 2.5 %collective-permute-start.3 = (bf16[2,192,128]{2,1,0:T(8,128)(2,1)S(1)}, bf16[2,192,128]{2,1,0:T(8,128)(2,1)S(1)}, u32[]{:S(2)}, u32[]{:S(2)}) collective-permute-start(bf16[2,192,128]{2,1,0:T(8,128)(2,1)S(1)} %get-tuple-element.81), channel_id=1, source_target_pairs={{0,12},{1,13},{2,3},{3,2},{4,8},{5,9},{6,7},{7,6},{8,4},{9,5},{10,... | collective-permute-start | bytes 294920 | tf_op jit(solution)/shard_map/ppermute | solution.py:161
  11.5 1.1 %collective-permute-start.6 = (bf16[2,192,128]{2,1,0:T(8,128)(2,1)S(1)}, bf16[2,192,128]{2,1,0:T(8,128)(2,1)S(1)}, u32[]{:S(2)}, u32[]{:S(2)}) collective-permute-start(bf16[2,192,128]{2,1,0:T(8,128)(2,1)S(1)} %get-tuple-element.80), channel_id=1, source_target_pairs={{0,4},{1,5},{2,11},{3,10},{4,0},{5,1},{6,15},{7,14},{8,12},{9,13},... | collective-permute-start | bytes 294920 | tf_op jit(solution)/shard_map/ppermute | solution.py:161
  12.6 2.5 %collective-permute-start.7 = (bf16[2,192,128]{2,1,0:T(8,128)(2,1)S(1)}, bf16[2,192,128]{2,1,0:T(8,128)(2,1)S(1)}, u32[]{:S(2)}, u32[]{:S(2)}) collective-permute-start(bf16[2,192,128]{2,1,0:T(8,128)(2,1)S(1)} %get-tuple-element.79), channel_id=1, source_target_pairs={{0,9},{1,8},{2,6},{3,7},{4,13},{5,12},{6,2},{7,3},{8,1},{9,0},{10,... | collective-permute-start | bytes 294920 | tf_op jit(solution)/shard_map/ppermute | solution.py:161
  15.6 0.9 %collective-permute-start.9 = (bf16[2,192,128]{2,1,0:T(8,128)(2,1)S(1)}, bf16[2,192,128]{2,1,0:T(8,128)(2,1)S(1)}, u32[]{:S(2)}, u32[]{:S(2)}) collective-permute-start(bf16[2,192,128]{2,1,0:T(8,128)(2,1)S(1)} %get-tuple-element.77), channel_id=1, source_target_pairs={{0,5},{1,4},{2,10},{3,11},{4,1},{5,0},{6,14},{7,15},{8,13},{9,12},... | collective-permute-start | bytes 294920 | tf_op jit(solution)/shard_map/ppermute | solution.py:161
  16.5 1.7 %collective-permute-done.4 = bf16[2,192,128]{2,1,0:T(8,128)(2,1)S(1)} collective-permute-done((bf16[2,192,128]{2,1,0:T(8,128)(2,1)S(1)}, bf16[2,192,128]{2,1,0:T(8,128)(2,1)S(1)}, u32[]{:S(2)}, u32[]{:S(2)}) %collective-permute-start.4) | collective-permute-done | bytes 98336 | tf_op jit(solution)/shard_map/ppermute | solution.py:161
  18.7 1.1 %collective-permute-done.8 = bf16[2,192,128]{2,1,0:T(8,128)(2,1)S(1)} collective-permute-done((bf16[2,192,128]{2,1,0:T(8,128)(2,1)S(1)}, bf16[2,192,128]{2,1,0:T(8,128)(2,1)S(1)}, u32[]{:S(2)}, u32[]{:S(2)}) %collective-permute-start.8) | collective-permute-done | bytes 98336 | tf_op jit(solution)/shard_map/ppermute | solution.py:161
  19.8 1.3 %collective-permute-done.9 = bf16[2,192,128]{2,1,0:T(8,128)(2,1)S(1)} collective-permute-done((bf16[2,192,128]{2,1,0:T(8,128)(2,1)S(1)}, bf16[2,192,128]{2,1,0:T(8,128)(2,1)S(1)}, u32[]{:S(2)}, u32[]{:S(2)}) %collective-permute-start.9) | collective-permute-done | bytes 98336 | tf_op jit(solution)/shard_map/ppermute | solution.py:161
  21.2 2.7 %collective-permute-start.10 = (bf16[192,128]{1,0:T(8,128)(2,1)S(1)}, bf16[192,128]{1,0:T(8,128)(2,1)S(1)}, u32[]{:S(2)}, u32[]{:S(2)}) collective-permute-start(bf16[192,128]{1,0:T(8,128)(2,1)S(1)} %fusion.19), channel_id=1, source_target_pairs={{0,16},{16,0},{1,17},{17,1},{2,18},{18,2},{3,19},{19,3},{4,20},{20... | collective-permute-start | bytes 147464 | tf_op jit(solution)/shard_map/ppermute | solution.py:151
  24.6 1.7 %collective-permute-done.10 = bf16[192,128]{1,0:T(8,128)(2,1)S(1)} collective-permute-done((bf16[192,128]{1,0:T(8,128)(2,1)S(1)}, bf16[192,128]{1,0:T(8,128)(2,1)S(1)}, u32[]{:S(2)}, u32[]{:S(2)}) %collective-permute-start.10) | collective-permute-done | bytes 49184 | tf_op jit(solution)/shard_map/ppermute | solution.py:151
  26.4 2.7 %collective-permute-start.11 = (bf16[192,128]{1,0:T(8,128)(2,1)S(1)}, bf16[192,128]{1,0:T(8,128)(2,1)S(1)}, u32[]{:S(2)}, u32[]{:S(2)}) collective-permute-start(bf16[192,128]{1,0:T(8,128)(2,1)S(1)} %get-tuple-element.75), channel_id=1, source_target_pairs={{0,16},{16,0},{1,17},{17,1},{2,18},{18,2},{3,19},{19,3},{4,20},{20... | collective-permute-start | bytes 147464 | tf_op jit(solution)/shard_map/ppermute | solution.py:151
  29.1 1.2 %collective-permute-start.13 = (f32[192,128]{1,0:T(8,128)S(1)}, f32[192,128]{1,0:T(8,128)S(1)}, u32[]{:S(2)}, u32[]{:S(2)}) collective-permute-start(f32[192,128]{1,0:T(8,128)S(1)} %get-tuple-element.76), channel_id=1, source_target_pairs={{0,1},{1,0},{2,3},{3,2},{4,5},{5,4},{6,7},{7,6},{8,9},{9,8},{10,11... | collective-permute-start | bytes 294920 | tf_op jit(solution)/shard_map/ppermute | solution.py:151
  30.2 1.2 %collective-permute-done.11 = bf16[192,128]{1,0:T(8,128)(2,1)S(1)} collective-permute-done((bf16[192,128]{1,0:T(8,128)(2,1)S(1)}, bf16[192,128]{1,0:T(8,128)(2,1)S(1)}, u32[]{:S(2)}, u32[]{:S(2)}) %collective-permute-start.11) | collective-permute-done | bytes 49184 | tf_op jit(solution)/shard_map/ppermute | solution.py:151
  31.5 2.3 %collective-permute-start.15 = (bf16[2,192,128]{2,1,0:T(8,128)(2,1)S(1)}, bf16[2,192,128]{2,1,0:T(8,128)(2,1)S(1)}, u32[]{:S(2)}, u32[]{:S(2)}) collective-permute-start(bf16[2,192,128]{2,1,0:T(8,128)(2,1)S(1)} %get-tuple-element.84), channel_id=1, source_target_pairs={{0,13},{1,12},{2,15},{3,14},{4,9},{5,8},{6,11},{7,10},{8,5},{9,4},... | collective-permute-start | bytes 294920 | tf_op jit(solution)/shard_map/ppermute | solution.py:161
  33.8 1.4 %collective-permute-start.14 = (bf16[2,2,192,128]{3,2,1,0:T(8,128)(2,1)S(1)}, bf16[2,2,192,128]{3,2,1,0:T(8,128)(2,1)S(1)}, u32[]{:S(2)}, u32[]{:S(2)}) collective-permute-start(bf16[2,2,192,128]{3,2,1,0:T(8,128)(2,1)S(1)} %maximum_select_fusion), channel_id=1, source_target_pairs={{0,4},{1,5},{2,11},{3,10},{4,0},{5,1},{6,15},{7,14},{8,12},{9,13},... | collective-permute-start | bytes 589832 | tf_op jit(solution)/shard_map/ppermute | solution.py:161
  35.2 1.2 %collective-permute-start.18 = (bf16[2,2,192,128]{3,2,1,0:T(8,128)(2,1)S(1)}, bf16[2,2,192,128]{3,2,1,0:T(8,128)(2,1)S(1)}, u32[]{:S(2)}, u32[]{:S(2)}) collective-permute-start(bf16[2,2,192,128]{3,2,1,0:T(8,128)(2,1)S(1)} %maximum_select_fusion), channel_id=1, source_target_pairs={{0,8},{1,9},{2,7},{3,6},{4,12},{5,13},{6,3},{7,2},{8,0},{9,1},{10,... | collective-permute-start | bytes 589832 | tf_op jit(solution)/shard_map/ppermute | solution.py:161
  36.4 1.0 %collective-permute-start.16 = (bf16[2,2,192,128]{3,2,1,0:T(8,128)(2,1)S(1)}, bf16[2,2,192,128]{3,2,1,0:T(8,128)(2,1)S(1)}, u32[]{:S(2)}, u32[]{:S(2)}) collective-permute-start(bf16[2,2,192,128]{3,2,1,0:T(8,128)(2,1)S(1)} %maximum_select_fusion), channel_id=1, source_target_pairs={{0,1},{1,0},{2,14},{3,15},{4,5},{5,4},{6,10},{7,11},{8,9},{9,8},{1... | collective-permute-start | bytes 589832 | tf_op jit(solution)/shard_map/ppermute | solution.py:161
  37.4 0.9 %multiply_subtract_fusion = (f32[384,128]{1,0:T(8,128)}, f32[384,128]{1,0:T(8,128)}, f32[384,128]{1,0:T(8,128)}) fusion(f32[384,128]{1,0:T(8,128)S(1)} %copy-done, f32[]{:T(128)} %bitcast.14, f32[]{:T(128)} %bitcast.12, f32[192,128]{1,0:T(8,128)S(1)} %get-tuple-element.76, f32[192,128]{1,0:T(8,128)S(1)} %collective-permute-done.13, pred[]{:T(512)S(6)} %eq.7, ...), kind=kLoop, calls=%fused_computation.17 | loop fusion | flops 884736 | bytes 1376265 | tf_op jit(solution)/shard_map/sub | solution.py:36
  38.3 1.9 %shard_map.95 = (bf16[256,3072]{1,0:T(8,128)(2,1)S(1)}, bf16[256,3072]{1,0:T(8,128)(2,1)S(1)}) custom-call(bf16[256,6144]{1,0:T(8,128)(2,1)} %acts_ref.2), custom_call_target="tpu_custom_call" | custom-call | tf_op jit(solution)/shard_map/pallas_call | solution.py:276
  40.2 2.9 %collective-permute-done.14 = bf16[2,2,192,128]{3,2,1,0:T(8,128)(2,1)S(1)} collective-permute-done((bf16[2,2,192,128]{3,2,1,0:T(8,128)(2,1)S(1)}, bf16[2,2,192,128]{3,2,1,0:T(8,128)(2,1)S(1)}, u32[]{:S(2)}, u32[]{:S(2)}) %collective-permute-start.14) | collective-permute-done | bytes 196640 | tf_op jit(solution)/shard_map/ppermute | solution.py:161
  43.5 1.3 %collective-permute-done.16 = bf16[2,2,192,128]{3,2,1,0:T(8,128)(2,1)S(1)} collective-permute-done((bf16[2,2,192,128]{3,2,1,0:T(8,128)(2,1)S(1)}, bf16[2,2,192,128]{3,2,1,0:T(8,128)(2,1)S(1)}, u32[]{:S(2)}, u32[]{:S(2)}) %collective-permute-start.16) | collective-permute-done | bytes 196640 | tf_op jit(solution)/shard_map/ppermute | solution.py:161
  45.6 0.9 %collective-permute-done.17.refs_1_ = bf16[3,2,192,128]{3,2,1,0:T(8,128)(2,1)S(1)} collective-permute-done((bf16[3,2,192,128]{3,2,1,0:T(8,128)(2,1)S(1)}, bf16[3,2,192,128]{3,2,1,0:T(8,128)(2,1)S(1)}, u32[]{:S(2)}, u32[]{:S(2)}) %collective-permute-start.17) | collective-permute-done | bytes 294944 | tf_op jit(solution)/shard_map/ppermute | solution.py:151
  46.5 1.3 %shard_map.97 = bf16[256,128]{1,0:T(8,128)(2,1)} custom-call(bf16[256,3072]{1,0:T(8,128)(2,1)S(1)} %get-tuple-element.68.columns_ref, bf16[3,2,192,128]{3,2,1,0:T(8,128)(2,1)S(1)} %pad_maximum_fusion.refs_0_, bf16[3,2,192,128]{3,2,1,0:T(8,128)(2,1)S(1)} %collective-permute-done.17.refs_1_, bf16[1,2,192,128]{3,2,1,0:T(8,128)(2,1)S(1)} %get-tuple-element.83.refs_2_, ...), custom_call_target="tpu_custom_call" | custom-call | tf_op jit(solution)/shard_map/pallas_call | solution.py:296
  (42 shorter events, 5.7 us)
Async XLA Ops:
  2.7 1.6 %collective-permute-start = (bf16[2,2,192,128]{3,2,1,0:T(8,128)(2,1)S(1)}, bf16[2,2,192,128]{3,2,1,0:T(8,128)(2,1)S(1)}, u32[]{:S(2)}, u32[]{:S(2)}) collective-permute-start(bf16[2,2,192,128]{3,2,1,0:T(8,128)(2,1)S(1)} %get-tuple-element.40), channel_id=1, source_target_pairs={{0,2},{2,0},{1,3},{3,1},{4,6},{6,4},{5,7},{7,5},{8,10},{10,8},{9,1... | collective-permute-start | bytes 589832 | tf_op jit(solution)/shard_map/ppermute | solution.py:151
  4.3 7.0 %collective-permute-start.5 = (bf16[4,2,192,128]{3,2,1,0:T(8,128)(2,1)S(1)}, bf16[4,2,192,128]{3,2,1,0:T(8,128)(2,1)S(1)}, u32[]{:S(2)}, u32[]{:S(2)}) collective-permute-start(bf16[4,2,192,128]{3,2,1,0:T(8,128)(2,1)S(1)} %get-tuple-element.49), channel_id=1, source_target_pairs={{0,2},{2,0},{1,3},{3,1},{4,6},{6,4},{5,7},{7,5},{8,10},{10,8},{9,1... | collective-permute-start | bytes 1179656 | tf_op jit(solution)/shard_map/ppermute | solution.py:151
  4.7 5.7 %collective-permute-start.1 = (bf16[2,2,192,128]{3,2,1,0:T(8,128)(2,1)S(1)}, bf16[2,2,192,128]{3,2,1,0:T(8,128)(2,1)S(1)}, u32[]{:S(2)}, u32[]{:S(2)}) collective-permute-start(bf16[2,2,192,128]{3,2,1,0:T(8,128)(2,1)S(1)} %get-tuple-element.45), channel_id=1, source_target_pairs={{0,2},{2,0},{1,3},{3,1},{4,6},{6,4},{5,7},{7,5},{8,10},{10,8},{9,1... | collective-permute-start | bytes 589832 | tf_op jit(solution)/shard_map/ppermute | solution.py:151
  4.9 10.2 %collective-permute-start.2 = (bf16[2,192,128]{2,1,0:T(8,128)(2,1)S(1)}, bf16[2,192,128]{2,1,0:T(8,128)(2,1)S(1)}, u32[]{:S(2)}, u32[]{:S(2)}) collective-permute-start(bf16[2,192,128]{2,1,0:T(8,128)(2,1)S(1)} %get-tuple-element.82), channel_id=1, source_target_pairs={{0,1},{1,0},{2,14},{3,15},{4,5},{5,4},{6,10},{7,11},{8,9},{9,8},{1... | collective-permute-start | bytes 294920 | tf_op jit(solution)/shard_map/ppermute | solution.py:161
  7.9 7.7 %collective-permute-start.3 = (bf16[2,192,128]{2,1,0:T(8,128)(2,1)S(1)}, bf16[2,192,128]{2,1,0:T(8,128)(2,1)S(1)}, u32[]{:S(2)}, u32[]{:S(2)}) collective-permute-start(bf16[2,192,128]{2,1,0:T(8,128)(2,1)S(1)} %get-tuple-element.81), channel_id=1, source_target_pairs={{0,12},{1,13},{2,3},{3,2},{4,8},{5,9},{6,7},{7,6},{8,4},{9,5},{10,... | collective-permute-start | bytes 294920 | tf_op jit(solution)/shard_map/ppermute | solution.py:161
  10.4 7.8 %collective-permute-start.4 = (bf16[2,192,128]{2,1,0:T(8,128)(2,1)S(1)}, bf16[2,192,128]{2,1,0:T(8,128)(2,1)S(1)}, u32[]{:S(2)}, u32[]{:S(2)}) collective-permute-start(bf16[2,192,128]{2,1,0:T(8,128)(2,1)S(1)} %fusion.14), channel_id=1, source_target_pairs={{0,13},{1,12},{2,15},{3,14},{4,9},{5,8},{6,11},{7,10},{8,5},{9,4},... | collective-permute-start | bytes 294920 | tf_op jit(solution)/shard_map/ppermute | solution.py:161
  11.4 26.0 %copy-start = (f32[384,128]{1,0:T(8,128)S(1)}, f32[384,128]{1,0:T(8,128)}, u32[]{:S(2)}) copy-start(f32[384,128]{1,0:T(8,128)} %refs_0_.1) | copy-start | bytes 589828
  11.4 26.0 %copy-start.1 = (f32[384,128]{1,0:T(8,128)S(1)}, f32[384,128]{1,0:T(8,128)}, u32[]{:S(2)}) copy-start(f32[384,128]{1,0:T(8,128)} %refs_1_.1) | copy-start | bytes 589828
  11.4 26.0 %copy-start.2 = (f32[384,128]{1,0:T(8,128)S(1)}, f32[384,128]{1,0:T(8,128)}, u32[]{:S(2)}) copy-start(f32[384,128]{1,0:T(8,128)} %refs_2_.1) | copy-start | bytes 589828
  11.5 6.7 %collective-permute-start.6 = (bf16[2,192,128]{2,1,0:T(8,128)(2,1)S(1)}, bf16[2,192,128]{2,1,0:T(8,128)(2,1)S(1)}, u32[]{:S(2)}, u32[]{:S(2)}) collective-permute-start(bf16[2,192,128]{2,1,0:T(8,128)(2,1)S(1)} %get-tuple-element.80), channel_id=1, source_target_pairs={{0,4},{1,5},{2,11},{3,10},{4,0},{5,1},{6,15},{7,14},{8,12},{9,13},... | collective-permute-start | bytes 294920 | tf_op jit(solution)/shard_map/ppermute | solution.py:161
  12.6 6.1 %collective-permute-start.7 = (bf16[2,192,128]{2,1,0:T(8,128)(2,1)S(1)}, bf16[2,192,128]{2,1,0:T(8,128)(2,1)S(1)}, u32[]{:S(2)}, u32[]{:S(2)}) collective-permute-start(bf16[2,192,128]{2,1,0:T(8,128)(2,1)S(1)} %get-tuple-element.79), channel_id=1, source_target_pairs={{0,9},{1,8},{2,6},{3,7},{4,13},{5,12},{6,2},{7,3},{8,1},{9,0},{10,... | collective-permute-start | bytes 294920 | tf_op jit(solution)/shard_map/ppermute | solution.py:161
  15.1 4.7 %collective-permute-start.8 = (bf16[2,192,128]{2,1,0:T(8,128)(2,1)S(1)}, bf16[2,192,128]{2,1,0:T(8,128)(2,1)S(1)}, u32[]{:S(2)}, u32[]{:S(2)}) collective-permute-start(bf16[2,192,128]{2,1,0:T(8,128)(2,1)S(1)} %get-tuple-element.78), channel_id=1, source_target_pairs={{0,8},{1,9},{2,7},{3,6},{4,12},{5,13},{6,3},{7,2},{8,0},{9,1},{10,... | collective-permute-start | bytes 294920 | tf_op jit(solution)/shard_map/ppermute | solution.py:161
  15.6 5.5 %collective-permute-start.9 = (bf16[2,192,128]{2,1,0:T(8,128)(2,1)S(1)}, bf16[2,192,128]{2,1,0:T(8,128)(2,1)S(1)}, u32[]{:S(2)}, u32[]{:S(2)}) collective-permute-start(bf16[2,192,128]{2,1,0:T(8,128)(2,1)S(1)} %get-tuple-element.77), channel_id=1, source_target_pairs={{0,5},{1,4},{2,10},{3,11},{4,1},{5,0},{6,14},{7,15},{8,13},{9,12},... | collective-permute-start | bytes 294920 | tf_op jit(solution)/shard_map/ppermute | solution.py:161
  21.2 5.1 %collective-permute-start.10 = (bf16[192,128]{1,0:T(8,128)(2,1)S(1)}, bf16[192,128]{1,0:T(8,128)(2,1)S(1)}, u32[]{:S(2)}, u32[]{:S(2)}) collective-permute-start(bf16[192,128]{1,0:T(8,128)(2,1)S(1)} %fusion.19), channel_id=1, source_target_pairs={{0,16},{16,0},{1,17},{17,1},{2,18},{18,2},{3,19},{19,3},{4,20},{20... | collective-permute-start | bytes 147464 | tf_op jit(solution)/shard_map/ppermute | solution.py:151
  26.4 5.1 %collective-permute-start.11 = (bf16[192,128]{1,0:T(8,128)(2,1)S(1)}, bf16[192,128]{1,0:T(8,128)(2,1)S(1)}, u32[]{:S(2)}, u32[]{:S(2)}) collective-permute-start(bf16[192,128]{1,0:T(8,128)(2,1)S(1)} %get-tuple-element.75), channel_id=1, source_target_pairs={{0,16},{16,0},{1,17},{17,1},{2,18},{18,2},{3,19},{19,3},{4,20},{20... | collective-permute-start | bytes 147464 | tf_op jit(solution)/shard_map/ppermute | solution.py:151
  29.1 4.7 %collective-permute-start.13 = (f32[192,128]{1,0:T(8,128)S(1)}, f32[192,128]{1,0:T(8,128)S(1)}, u32[]{:S(2)}, u32[]{:S(2)}) collective-permute-start(f32[192,128]{1,0:T(8,128)S(1)} %get-tuple-element.76), channel_id=1, source_target_pairs={{0,1},{1,0},{2,3},{3,2},{4,5},{5,4},{6,7},{7,6},{8,9},{9,8},{10,11... | collective-permute-start | bytes 294920 | tf_op jit(solution)/shard_map/ppermute | solution.py:151
  31.4 2.4 %collective-permute-start.12 = (bf16[2,192,128]{2,1,0:T(8,128)(2,1)S(1)}, bf16[2,192,128]{2,1,0:T(8,128)(2,1)S(1)}, u32[]{:S(2)}, u32[]{:S(2)}) collective-permute-start(bf16[2,192,128]{2,1,0:T(8,128)(2,1)S(1)} %get-tuple-element.84), channel_id=1, source_target_pairs={{0,2},{2,0},{1,3},{3,1},{4,6},{6,4},{5,7},{7,5},{8,10},{10,8},{9,1... | collective-permute-start | bytes 294920 | tf_op jit(solution)/shard_map/ppermute | solution.py:151
  31.5 8.7 %collective-permute-start.15 = (bf16[2,192,128]{2,1,0:T(8,128)(2,1)S(1)}, bf16[2,192,128]{2,1,0:T(8,128)(2,1)S(1)}, u32[]{:S(2)}, u32[]{:S(2)}) collective-permute-start(bf16[2,192,128]{2,1,0:T(8,128)(2,1)S(1)} %get-tuple-element.84), channel_id=1, source_target_pairs={{0,13},{1,12},{2,15},{3,14},{4,9},{5,8},{6,11},{7,10},{8,5},{9,4},... | collective-permute-start | bytes 294920 | tf_op jit(solution)/shard_map/ppermute | solution.py:161
  33.8 9.3 %collective-permute-start.14 = (bf16[2,2,192,128]{3,2,1,0:T(8,128)(2,1)S(1)}, bf16[2,2,192,128]{3,2,1,0:T(8,128)(2,1)S(1)}, u32[]{:S(2)}, u32[]{:S(2)}) collective-permute-start(bf16[2,2,192,128]{3,2,1,0:T(8,128)(2,1)S(1)} %maximum_select_fusion), channel_id=1, source_target_pairs={{0,4},{1,5},{2,11},{3,10},{4,0},{5,1},{6,15},{7,14},{8,12},{9,13},... | collective-permute-start | bytes 589832 | tf_op jit(solution)/shard_map/ppermute | solution.py:161
  35.2 7.9 %collective-permute-start.18 = (bf16[2,2,192,128]{3,2,1,0:T(8,128)(2,1)S(1)}, bf16[2,2,192,128]{3,2,1,0:T(8,128)(2,1)S(1)}, u32[]{:S(2)}, u32[]{:S(2)}) collective-permute-start(bf16[2,2,192,128]{3,2,1,0:T(8,128)(2,1)S(1)} %maximum_select_fusion), channel_id=1, source_target_pairs={{0,8},{1,9},{2,7},{3,6},{4,12},{5,13},{6,3},{7,2},{8,0},{9,1},{10,... | collective-permute-start | bytes 589832 | tf_op jit(solution)/shard_map/ppermute | solution.py:161
  36.4 8.5 %collective-permute-start.16 = (bf16[2,2,192,128]{3,2,1,0:T(8,128)(2,1)S(1)}, bf16[2,2,192,128]{3,2,1,0:T(8,128)(2,1)S(1)}, u32[]{:S(2)}, u32[]{:S(2)}) collective-permute-start(bf16[2,2,192,128]{3,2,1,0:T(8,128)(2,1)S(1)} %maximum_select_fusion), channel_id=1, source_target_pairs={{0,1},{1,0},{2,14},{3,15},{4,5},{5,4},{6,10},{7,11},{8,9},{9,8},{1... | collective-permute-start | bytes 589832 | tf_op jit(solution)/shard_map/ppermute | solution.py:161
  43.2 1.8 %collective-permute-start.19 = (bf16[4,2,192,128]{3,2,1,0:T(8,128)(2,1)S(1)}, bf16[4,2,192,128]{3,2,1,0:T(8,128)(2,1)S(1)}, u32[]{:S(2)}, u32[]{:S(2)}) collective-permute-start(bf16[4,2,192,128]{3,2,1,0:T(8,128)(2,1)S(1)} %constant_dynamic-update-slice_fusion.refs_0_), channel_id=1, source_target_pairs={{0,2},{2,0},{1,3},{3,1},{4,6},{6,4},{5,7},{7,5},{8,10},{10,8},{9,1... | collective-permute-start | bytes 1179656 | tf_op jit(solution)/shard_map/ppermute | solution.py:151
  44.9 1.6 %collective-permute-start.17 = (bf16[3,2,192,128]{3,2,1,0:T(8,128)(2,1)S(1)}, bf16[3,2,192,128]{3,2,1,0:T(8,128)(2,1)S(1)}, u32[]{:S(2)}, u32[]{:S(2)}) collective-permute-start(bf16[3,2,192,128]{3,2,1,0:T(8,128)(2,1)S(1)} %pad_maximum_fusion.refs_0_), channel_id=1, source_target_pairs={{0,2},{2,0},{1,3},{3,1},{4,6},{6,4},{5,7},{7,5},{8,10},{10,8},{9,1... | collective-permute-start | bytes 884744 | tf_op jit(solution)/shard_map/ppermute | solution.py:151

commit v22 on v19

--- a/solution.py
+++ b/solution.py
@@ -95,11 +95,20 @@
     sort_products(n_high, 0, turned_ref[...], columns, away, kept, blocks, lambda n: None)
 
 
-def columns_kernel(n_high, wide, acts_ref, first_ref, second_ref, sems):
-    copies = []
-    for i, (lows, out) in enumerate(zip(LOWS, (first_ref, second_ref))):
-        slices = lambda n, out=out: out.at[:, pl.ds(n * wide, wide)]
-        copies += load_columns(acts_ref, slices, sems.at[i], lows, n_high, wide)
+def columns_of(group, n_high, wide, acts_ref, out_ref, sems):
+    slices = lambda n: out_ref.at[:, pl.ds(n * wide, wide)]
+    return load_columns(acts_ref, slices, sems, LOWS[group], n_high, wide)
+
+
+def columns_kernel(n_high, wide, acts_ref, out_ref, sems):
+    for copy in columns_of(0, n_high, wide, acts_ref, out_ref, sems):
+        copy.wait()
+
+
+def first_logits_kernel(n_high, wide, acts_ref, columns_ref, *refs):
+    *pieces, out_ref, later_ref, weight, sems = refs
+    copies = columns_of(1, n_high, wide, acts_ref, later_ref, sems)
+    logits_kernel(n_high, 0, columns_ref, *pieces, out_ref, weight)
     for copy in copies:
         copy.wait()
 
@@ -247,15 +256,17 @@
 
         far = [swap(weight, "high", j) for j in range(1, n_high)]
         other = swap(grad, "rep")
-        columns = [None, None]
+        columns_shape = pltpu.VMEM((tokens, 8 * n_high * half), bf16)
+        column_sems = pltpu.SemaphoreType.DMA((2 * n_high,))
+        columns = None
         if in_kernels:
             weight, late_acts = lax.optimization_barrier((weight, acts))
             columns = pl.pallas_call(
                 functools.partial(columns_kernel, n_high, 4 * half),
-                out_shape=(pltpu.VMEM((tokens, 8 * n_high * half), bf16),) * 2,
+                out_shape=columns_shape,
                 in_specs=[anywhere],
-                out_specs=(vmem, vmem),
-                scratch_shapes=[pltpu.SemaphoreType.DMA((2, 2 * n_high))],
+                out_specs=vmem,
+                scratch_shapes=[column_sems],
                 compiler_params=params,
             )(pltpu.with_memory_space_constraint(late_acts, pltpu.HBM))
             far, columns = lax.optimization_barrier((far, columns))
@@ -279,20 +290,32 @@
         second += [column[None], across[None]]
         pieces = (first, second)
         logits = None
-        for group, (received, acts_columns) in enumerate(zip(pieces, columns)):
+        for group, received in enumerate(pieces):
             if in_kernels:
                 before = [] if logits is None else [logits]
                 operands = [
-                    pltpu.with_memory_space_constraint(x, pltpu.VMEM) for x in [acts_columns] + received + before
+                    pltpu.with_memory_space_constraint(x, pltpu.VMEM)
+                    for x in [columns] + received + before
                 ]
-                logits = pl.pallas_call(
-                    functools.partial(logits_kernel, n_high, group),
-                    out_shape=jax.ShapeDtypeStruct((tokens, experts), bf16 if before else f32),
-                    in_specs=[vmem] * len(operands),
-                    out_specs=vmem,
-                    scratch_shapes=[pltpu.VMEM((2, n_high, 2, 2, half, experts), bf16)],
-                    compiler_params=params,
-                )(*operands)
+                scratch = [pltpu.VMEM((2, n_high, 2, 2, half, experts), bf16)]
+                if before:
+                    logits = pl.pallas_call(
+                        functools.partial(logits_kernel, n_high, group),
+                        out_shape=jax.ShapeDtypeStruct((tokens, experts), bf16),
+                        in_specs=[vmem] * len(operands),
+                        out_specs=vmem,
+                        scratch_shapes=scratch,
+                        compiler_params=params,
+                    )(*operands)
+                else:
+                    logits, columns = pl.pallas_call(
+                        functools.partial(first_logits_kernel, n_high, 4 * half),
+                        out_shape=(pltpu.VMEM((tokens, experts), f32), columns_shape),
+                        in_specs=[anywhere] + [vmem] * len(operands),
+                        out_specs=(vmem, vmem),
+                        scratch_shapes=scratch + [column_sems],
+                        compiler_params=params,
+                    )(acts, *operands)
             else:
                 rows_at, values = [], []
                 for piece, blocks in zip(received, places(group, core, rep)):

time: 54.2 us -> 51.4 us (0.948)
  other arithmetic: 4.07 us -> 2.43 us
  Pallas kernels: 8.5 us -> 7.19 us
    pallas_call x2 -> x1, Pallas kernels: 3.96 us -> 1.26 us  [per_device(): pl.pallas_call(functools.partial(logits_kernel, n_high, group), out_shape...]
    pallas_call x0 -> x1, Pallas kernels: none -> 1.9 us  [per_device(): pl.pallas_call(functools.partial(first_logits_kernel, n_high, 4 * half),...]
    another operation x2, other arithmetic: 0.81 us -> 0.09 us  [per_device(): first, second = (jnp.stack([x, z, xy, yz]), jnp.stack([y, zx, xyz]))]
    broadcast_in_dim x1, other arithmetic: 0.65 us -> 0.01 us  [per_device(): second += [column[None], across[None]]]
  transfers between devices with their start and end apart: 22 -> 22, of which waited for: 10 -> 11; matrix products, arithmetic and copies ran while one was open for 7% -> 4% of each run, Pallas kernels for 8% -> 8%
where the time goes in v22:
time: 51.4 us; the launch traced here: 51.2 us
  starting transfers between devices  28.2 us (55%)
  waiting for transfers between devices  11.7 us (23%)
  Pallas kernels  7.19 us (14%)
  other arithmetic  2.43 us (5%)
  between operations  1.54 us (3%)
    ppermute x14, starting transfers between devices, cube_swap(): return lax.ppermute(x, AXES[1:], pairs)  20.2 us
    ppermute x14, waiting for transfers between devices, cube_swap(): return lax.ppermute(x, AXES[1:], pairs)  9.12 us
    ppermute x8, starting transfers between devices, swap(): lax.ppermute(x, axis, [(i, i ^ mask) for i in range(fine.shape[axis])])  8.06 us
    ppermute x8, waiting for transfers between devices, swap(): lax.ppermute(x, axis, [(i, i ^ mask) for i in range(fine.shape[axis])])  2.58 us
    pallas_call x1, Pallas kernels, per_device(): pl.pallas_call(functools.partial(first_grad_kernel, n_high), out_shape=[s...  2.06 us
    sub x1, other arithmetic, adamw(): master - 0.01 * (first_hat / (jnp.sqrt(second_hat) + 1e-08) + 0.1 * master)  1.91 us
    pallas_call x1, Pallas kernels, per_device(): pl.pallas_call(functools.partial(first_logits_kernel, n_high, 4 * half),...  1.9 us
    pallas_call x1, Pallas kernels, per_device(): pl.pallas_call(functools.partial(columns_kernel, n_high, 4 * half), out_s...  1.39 us
  transfers between devices with their start and end apart: 22, of which 11 were waited for; matrix products, arithmetic and copies ran while one was open for 4% of the time, Pallas kernels for 8%

profile of v22, /device:TPU:0, one launch (start us, length us, event | category | flops | bytes accessed | tf_op | source)
XLA Modules:
  0.0 51.2 jit_solution(10735342330397306243)
XLA Ops:
  0.6 2.1 %shard_map.93 = (bf16[4,2,192,128]{3,2,1,0:T(8,128)(2,1)S(1)}, bf16[4,2,192,128]{3,2,1,0:T(8,128)(2,1)S(1)}, f32[3,192,128]{2,1,0:T(8,128)S(1)}, bf16[4,256,768]{2,1,0:T(8,128)(2,1)S(1)}, bf16[128,256]{1,0:T(8,128)(2,1)S(1)}) custom-call(bf16[256,6144]{1,0:T(8,128)(2,1)} %acts_ref.4, bf16[256,128]{1,0:T(8,128)(2,1)} %grad_ref.1, f32[384,128]{1,0:T(8,128)} %refs_0_.1, ...), custom_call_target="tpu_custom_call" | custom-call | tf_op jit(solution)/shard_map/pallas_call | solution.py:190
  5.1 2.7 %collective-permute-start.6 = (bf16[2,192,128]{2,1,0:T(8,128)(2,1)S(1)}, bf16[2,192,128]{2,1,0:T(8,128)(2,1)S(1)}, u32[]{:S(2)}, u32[]{:S(2)}) collective-permute-start(bf16[2,192,128]{2,1,0:T(8,128)(2,1)S(1)} %get-tuple-element.67), channel_id=1, source_target_pairs={{0,1},{1,0},{2,14},{3,15},{4,5},{5,4},{6,10},{7,11},{8,9},{9,8},{1... | collective-permute-start | bytes 294920 | tf_op jit(solution)/shard_map/ppermute | solution.py:162
  7.8 2.5 %collective-permute-start.7 = (bf16[2,192,128]{2,1,0:T(8,128)(2,1)S(1)}, bf16[2,192,128]{2,1,0:T(8,128)(2,1)S(1)}, u32[]{:S(2)}, u32[]{:S(2)}) collective-permute-start(bf16[2,192,128]{2,1,0:T(8,128)(2,1)S(1)} %get-tuple-element.66), channel_id=1, source_target_pairs={{0,12},{1,13},{2,3},{3,2},{4,8},{5,9},{6,7},{7,6},{8,4},{9,5},{10,... | collective-permute-start | bytes 294920 | tf_op jit(solution)/shard_map/ppermute | solution.py:162
  10.5 1.9 %collective-permute-start.2 = (bf16[2,192,128]{2,1,0:T(8,128)(2,1)S(1)}, bf16[2,192,128]{2,1,0:T(8,128)(2,1)S(1)}, u32[]{:S(2)}, u32[]{:S(2)}) collective-permute-start(bf16[2,192,128]{2,1,0:T(8,128)(2,1)S(1)} %get-tuple-element.71), channel_id=1, source_target_pairs={{0,4},{1,5},{2,11},{3,10},{4,0},{5,1},{6,15},{7,14},{8,12},{9,13},... | collective-permute-start | bytes 294920 | tf_op jit(solution)/shard_map/ppermute | solution.py:162
  12.4 2.5 %collective-permute-start.3 = (bf16[2,192,128]{2,1,0:T(8,128)(2,1)S(1)}, bf16[2,192,128]{2,1,0:T(8,128)(2,1)S(1)}, u32[]{:S(2)}, u32[]{:S(2)}) collective-permute-start(bf16[2,192,128]{2,1,0:T(8,128)(2,1)S(1)} %get-tuple-element.70), channel_id=1, source_target_pairs={{0,9},{1,8},{2,6},{3,7},{4,13},{5,12},{6,2},{7,3},{8,1},{9,0},{10,... | collective-permute-start | bytes 294920 | tf_op jit(solution)/shard_map/ppermute | solution.py:162
  15.4 1.1 %collective-permute-start.5 = (bf16[2,192,128]{2,1,0:T(8,128)(2,1)S(1)}, bf16[2,192,128]{2,1,0:T(8,128)(2,1)S(1)}, u32[]{:S(2)}, u32[]{:S(2)}) collective-permute-start(bf16[2,192,128]{2,1,0:T(8,128)(2,1)S(1)} %get-tuple-element.68), channel_id=1, source_target_pairs={{0,5},{1,4},{2,10},{3,11},{4,1},{5,0},{6,14},{7,15},{8,13},{9,12},... | collective-permute-start | bytes 294920 | tf_op jit(solution)/shard_map/ppermute | solution.py:162
  16.6 1.9 %collective-permute-done.8 = bf16[2,192,128]{2,1,0:T(8,128)(2,1)S(1)} collective-permute-done((bf16[2,192,128]{2,1,0:T(8,128)(2,1)S(1)}, bf16[2,192,128]{2,1,0:T(8,128)(2,1)S(1)}, u32[]{:S(2)}, u32[]{:S(2)}) %collective-permute-start.8) | collective-permute-done | bytes 98336 | tf_op jit(solution)/shard_map/ppermute | solution.py:162
  18.7 1.1 %collective-permute-done.4 = bf16[2,192,128]{2,1,0:T(8,128)(2,1)S(1)} collective-permute-done((bf16[2,192,128]{2,1,0:T(8,128)(2,1)S(1)}, bf16[2,192,128]{2,1,0:T(8,128)(2,1)S(1)}, u32[]{:S(2)}, u32[]{:S(2)}) %collective-permute-start.4) | collective-permute-done | bytes 98336 | tf_op jit(solution)/shard_map/ppermute | solution.py:162
  19.9 1.1 %collective-permute-done.5 = bf16[2,192,128]{2,1,0:T(8,128)(2,1)S(1)} collective-permute-done((bf16[2,192,128]{2,1,0:T(8,128)(2,1)S(1)}, bf16[2,192,128]{2,1,0:T(8,128)(2,1)S(1)}, u32[]{:S(2)}, u32[]{:S(2)}) %collective-permute-start.5) | collective-permute-done | bytes 98336 | tf_op jit(solution)/shard_map/ppermute | solution.py:162
  21.0 2.6 %collective-permute-start.9 = (bf16[192,128]{1,0:T(8,128)(2,1)S(1)}, bf16[192,128]{1,0:T(8,128)(2,1)S(1)}, u32[]{:S(2)}, u32[]{:S(2)}) collective-permute-start(bf16[192,128]{1,0:T(8,128)(2,1)S(1)} %fusion.11), channel_id=1, source_target_pairs={{0,16},{16,0},{1,17},{17,1},{2,18},{18,2},{3,19},{19,3},{4,20},{20... | collective-permute-start | bytes 147464 | tf_op jit(solution)/shard_map/ppermute | solution.py:152
  24.4 1.7 %collective-permute-done.9 = bf16[192,128]{1,0:T(8,128)(2,1)S(1)} collective-permute-done((bf16[192,128]{1,0:T(8,128)(2,1)S(1)}, bf16[192,128]{1,0:T(8,128)(2,1)S(1)}, u32[]{:S(2)}, u32[]{:S(2)}) %collective-permute-start.9) | collective-permute-done | bytes 49184 | tf_op jit(solution)/shard_map/ppermute | solution.py:152
  26.2 2.7 %collective-permute-start.10 = (bf16[192,128]{1,0:T(8,128)(2,1)S(1)}, bf16[192,128]{1,0:T(8,128)(2,1)S(1)}, u32[]{:S(2)}, u32[]{:S(2)}) collective-permute-start(bf16[192,128]{1,0:T(8,128)(2,1)S(1)} %get-tuple-element.48), channel_id=1, source_target_pairs={{0,16},{16,0},{1,17},{17,1},{2,18},{18,2},{3,19},{19,3},{4,20},{20... | collective-permute-start | bytes 147464 | tf_op jit(solution)/shard_map/ppermute | solution.py:152
  28.9 1.4 %shard_map.95.columns_ref = bf16[256,3072]{1,0:T(8,128)(2,1)S(1)} custom-call(bf16[256,6144]{1,0:T(8,128)(2,1)} %acts_ref.4), custom_call_target="tpu_custom_call" | custom-call | tf_op jit(solution)/shard_map/pallas_call | solution.py:264
  30.3 1.2 %collective-permute-start.12 = (f32[192,128]{1,0:T(8,128)S(1)}, f32[192,128]{1,0:T(8,128)S(1)}, u32[]{:S(2)}, u32[]{:S(2)}) collective-permute-start(f32[192,128]{1,0:T(8,128)S(1)} %get-tuple-element.62), channel_id=1, source_target_pairs={{0,1},{1,0},{2,3},{3,2},{4,5},{5,4},{6,7},{7,6},{8,9},{9,8},{10,11... | collective-permute-start | bytes 294920 | tf_op jit(solution)/shard_map/ppermute | solution.py:152
  32.2 1.2 %collective-permute-start.15 = (bf16[2,192,128]{2,1,0:T(8,128)(2,1)S(1)}, bf16[2,192,128]{2,1,0:T(8,128)(2,1)S(1)}, u32[]{:S(2)}, u32[]{:S(2)}) collective-permute-start(bf16[2,192,128]{2,1,0:T(8,128)(2,1)S(1)} %get-tuple-element.56), channel_id=1, source_target_pairs={{0,1},{1,0},{2,3},{3,2},{4,5},{5,4},{6,7},{7,6},{8,9},{9,8},{10,11... | collective-permute-start | bytes 294920 | tf_op jit(solution)/shard_map/ppermute | solution.py:162
  33.4 1.7 %collective-permute-start.13 = (bf16[2,192,128]{2,1,0:T(8,128)(2,1)S(1)}, bf16[2,192,128]{2,1,0:T(8,128)(2,1)S(1)}, u32[]{:S(2)}, u32[]{:S(2)}) collective-permute-start(bf16[2,192,128]{2,1,0:T(8,128)(2,1)S(1)} %get-tuple-element.56), channel_id=1, source_target_pairs={{0,8},{1,9},{2,10},{3,11},{4,12},{5,13},{6,14},{7,15},{8,0},{9,1},... | collective-permute-start | bytes 294920 | tf_op jit(solution)/shard_map/ppermute | solution.py:162
  37.1 2.6 %collective-permute-start.16 = (bf16[2,192,128]{2,1,0:T(8,128)(2,1)S(1)}, bf16[2,192,128]{2,1,0:T(8,128)(2,1)S(1)}, u32[]{:S(2)}, u32[]{:S(2)}) collective-permute-start(bf16[2,192,128]{2,1,0:T(8,128)(2,1)S(1)} %collective-permute-done.15), channel_id=1, source_target_pairs={{0,8},{1,9},{2,10},{3,11},{4,12},{5,13},{6,14},{7,15},{8,0},{9,1},... | collective-permute-start | bytes 294920 | tf_op jit(solution)/shard_map/ppermute | solution.py:162
  39.8 1.0 %collective-permute-done.14 = bf16[2,192,128]{2,1,0:T(8,128)(2,1)S(1)} collective-permute-done((bf16[2,192,128]{2,1,0:T(8,128)(2,1)S(1)}, bf16[2,192,128]{2,1,0:T(8,128)(2,1)S(1)}, u32[]{:S(2)}, u32[]{:S(2)}) %collective-permute-start.14) | collective-permute-done | bytes 98336 | tf_op jit(solution)/shard_map/ppermute | solution.py:162
  40.8 1.7 %collective-permute-start.19 = (bf16[2,192,128]{2,1,0:T(8,128)(2,1)S(1)}, bf16[2,192,128]{2,1,0:T(8,128)(2,1)S(1)}, u32[]{:S(2)}, u32[]{:S(2)}) collective-permute-start(bf16[2,192,128]{2,1,0:T(8,128)(2,1)S(1)} %collective-permute-done.14), channel_id=1, source_target_pairs={{0,8},{1,9},{2,10},{3,11},{4,12},{5,13},{6,14},{7,15},{8,0},{9,1},... | collective-permute-start | bytes 294920 | tf_op jit(solution)/shard_map/ppermute | solution.py:162
  42.7 1.7 %collective-permute-done.18 = bf16[2,192,128]{2,1,0:T(8,128)(2,1)S(1)} collective-permute-done((bf16[2,192,128]{2,1,0:T(8,128)(2,1)S(1)}, bf16[2,192,128]{2,1,0:T(8,128)(2,1)S(1)}, u32[]{:S(2)}, u32[]{:S(2)}) %collective-permute-start.18) | collective-permute-done | bytes 98336 | tf_op jit(solution)/shard_map/ppermute | solution.py:162
  44.3 1.1 %collective-permute-done.19 = bf16[2,192,128]{2,1,0:T(8,128)(2,1)S(1)} collective-permute-done((bf16[2,192,128]{2,1,0:T(8,128)(2,1)S(1)}, bf16[2,192,128]{2,1,0:T(8,128)(2,1)S(1)}, u32[]{:S(2)}, u32[]{:S(2)}) %collective-permute-start.19) | collective-permute-done | bytes 98336 | tf_op jit(solution)/shard_map/ppermute | solution.py:162
  46.1 1.9 %multiply_subtract_fusion = (f32[384,128]{1,0:T(8,128)}, f32[384,128]{1,0:T(8,128)}, f32[384,128]{1,0:T(8,128)}) fusion(f32[384,128]{1,0:T(8,128)S(1)} %copy-done, f32[]{:T(128)} %bitcast.14, f32[]{:T(128)} %bitcast.12, f32[192,128]{1,0:T(8,128)S(1)} %get-tuple-element.62, f32[192,128]{1,0:T(8,128)} %copy-done.2, pred[]{:T(512)S(6)} %eq.3, ...), kind=kLoop, calls=%fused_computation.8 | loop fusion | flops 884736 | bytes 1376265 | tf_op jit(solution)/shard_map/sub | solution.py:36
  48.0 1.9 %shard_map.96 = (f32[256,128]{1,0:T(8,128)S(1)}, bf16[256,3072]{1,0:T(8,128)(2,1)S(1)}) custom-call(bf16[256,6144]{1,0:T(8,128)(2,1)} %acts_ref.4, bf16[256,3072]{1,0:T(8,128)(2,1)S(1)} %shard_map.95.columns_ref, bf16[4,2,192,128]{3,2,1,0:T(8,128)(2,1)S(1)} %pad_maximum_fusion.refs_0_, bf16[4,2,192,128]{3,2,1,0:T(8,128)(2,1)S(1)} %collective-permute-done.17.refs_1_), custom_call_target="tpu_custom_call" | custom-call | tf_op jit(solution)/shard_map/pallas_call | solution.py:311
  49.9 1.3 %shard_map.97 = bf16[256,128]{1,0:T(8,128)(2,1)} custom-call(bf16[256,3072]{1,0:T(8,128)(2,1)S(1)} %get-tuple-element.55.columns_ref, bf16[3,2,192,128]{3,2,1,0:T(8,128)(2,1)S(1)} %pad_maximum_fusion.1.refs_0_, bf16[3,2,192,128]{3,2,1,0:T(8,128)(2,1)S(1)} %collective-permute-done.20.refs_1_, bf16[1,2,192,128]{3,2,1,0:T(8,128)(2,1)S(1)} %get-tuple-element.72.refs_2_, ...), custom_call_target="tpu_custom_call" | custom-call | tf_op jit(solution)/shard_map/pallas_call | solution.py:302
  (45 shorter events, 7.0 us)
Async XLA Ops:
  2.7 1.9 %collective-permute-start = (bf16[4,2,192,128]{3,2,1,0:T(8,128)(2,1)S(1)}, bf16[4,2,192,128]{3,2,1,0:T(8,128)(2,1)S(1)}, u32[]{:S(2)}, u32[]{:S(2)}) collective-permute-start(bf16[4,2,192,128]{3,2,1,0:T(8,128)(2,1)S(1)} %get-tuple-element.34), channel_id=1, source_target_pairs={{0,2},{2,0},{1,3},{3,1},{4,6},{6,4},{5,7},{7,5},{8,10},{10,8},{9,1... | collective-permute-start | bytes 1179656 | tf_op jit(solution)/shard_map/ppermute | solution.py:152
  4.6 5.8 %collective-permute-start.1 = (bf16[4,2,192,128]{3,2,1,0:T(8,128)(2,1)S(1)}, bf16[4,2,192,128]{3,2,1,0:T(8,128)(2,1)S(1)}, u32[]{:S(2)}, u32[]{:S(2)}) collective-permute-start(bf16[4,2,192,128]{3,2,1,0:T(8,128)(2,1)S(1)} %get-tuple-element.36), channel_id=1, source_target_pairs={{0,2},{2,0},{1,3},{3,1},{4,6},{6,4},{5,7},{7,5},{8,10},{10,8},{9,1... | collective-permute-start | bytes 1179656 | tf_op jit(solution)/shard_map/ppermute | solution.py:152
  5.1 9.8 %collective-permute-start.6 = (bf16[2,192,128]{2,1,0:T(8,128)(2,1)S(1)}, bf16[2,192,128]{2,1,0:T(8,128)(2,1)S(1)}, u32[]{:S(2)}, u32[]{:S(2)}) collective-permute-start(bf16[2,192,128]{2,1,0:T(8,128)(2,1)S(1)} %get-tuple-element.67), channel_id=1, source_target_pairs={{0,1},{1,0},{2,14},{3,15},{4,5},{5,4},{6,10},{7,11},{8,9},{9,8},{1... | collective-permute-start | bytes 294920 | tf_op jit(solution)/shard_map/ppermute | solution.py:162
  7.8 7.6 %collective-permute-start.7 = (bf16[2,192,128]{2,1,0:T(8,128)(2,1)S(1)}, bf16[2,192,128]{2,1,0:T(8,128)(2,1)S(1)}, u32[]{:S(2)}, u32[]{:S(2)}) collective-permute-start(bf16[2,192,128]{2,1,0:T(8,128)(2,1)S(1)} %get-tuple-element.66), channel_id=1, source_target_pairs={{0,12},{1,13},{2,3},{3,2},{4,8},{5,9},{6,7},{7,6},{8,4},{9,5},{10,... | collective-permute-start | bytes 294920 | tf_op jit(solution)/shard_map/ppermute | solution.py:162
  10.3 8.1 %collective-permute-start.8 = (bf16[2,192,128]{2,1,0:T(8,128)(2,1)S(1)}, bf16[2,192,128]{2,1,0:T(8,128)(2,1)S(1)}, u32[]{:S(2)}, u32[]{:S(2)}) collective-permute-start(bf16[2,192,128]{2,1,0:T(8,128)(2,1)S(1)} %get-tuple-element.65), channel_id=1, source_target_pairs={{0,13},{1,12},{2,15},{3,14},{4,9},{5,8},{6,11},{7,10},{8,5},{9,4},... | collective-permute-start | bytes 294920 | tf_op jit(solution)/shard_map/ppermute | solution.py:162
  10.5 8.0 %collective-permute-start.2 = (bf16[2,192,128]{2,1,0:T(8,128)(2,1)S(1)}, bf16[2,192,128]{2,1,0:T(8,128)(2,1)S(1)}, u32[]{:S(2)}, u32[]{:S(2)}) collective-permute-start(bf16[2,192,128]{2,1,0:T(8,128)(2,1)S(1)} %get-tuple-element.71), channel_id=1, source_target_pairs={{0,4},{1,5},{2,11},{3,10},{4,0},{5,1},{6,15},{7,14},{8,12},{9,13},... | collective-permute-start | bytes 294920 | tf_op jit(solution)/shard_map/ppermute | solution.py:162
  12.4 6.4 %collective-permute-start.3 = (bf16[2,192,128]{2,1,0:T(8,128)(2,1)S(1)}, bf16[2,192,128]{2,1,0:T(8,128)(2,1)S(1)}, u32[]{:S(2)}, u32[]{:S(2)}) collective-permute-start(bf16[2,192,128]{2,1,0:T(8,128)(2,1)S(1)} %get-tuple-element.70), channel_id=1, source_target_pairs={{0,9},{1,8},{2,6},{3,7},{4,13},{5,12},{6,2},{7,3},{8,1},{9,0},{10,... | collective-permute-start | bytes 294920 | tf_op jit(solution)/shard_map/ppermute | solution.py:162
  14.9 4.9 %collective-permute-start.4 = (bf16[2,192,128]{2,1,0:T(8,128)(2,1)S(1)}, bf16[2,192,128]{2,1,0:T(8,128)(2,1)S(1)}, u32[]{:S(2)}, u32[]{:S(2)}) collective-permute-start(bf16[2,192,128]{2,1,0:T(8,128)(2,1)S(1)} %get-tuple-element.69), channel_id=1, source_target_pairs={{0,8},{1,9},{2,7},{3,6},{4,12},{5,13},{6,3},{7,2},{8,0},{9,1},{10,... | collective-permute-start | bytes 294920 | tf_op jit(solution)/shard_map/ppermute | solution.py:162
  15.4 5.5 %collective-permute-start.5 = (bf16[2,192,128]{2,1,0:T(8,128)(2,1)S(1)}, bf16[2,192,128]{2,1,0:T(8,128)(2,1)S(1)}, u32[]{:S(2)}, u32[]{:S(2)}) collective-permute-start(bf16[2,192,128]{2,1,0:T(8,128)(2,1)S(1)} %get-tuple-element.68), channel_id=1, source_target_pairs={{0,5},{1,4},{2,10},{3,11},{4,1},{5,0},{6,14},{7,15},{8,13},{9,12},... | collective-permute-start | bytes 294920 | tf_op jit(solution)/shard_map/ppermute | solution.py:162
  21.0 5.1 %collective-permute-start.9 = (bf16[192,128]{1,0:T(8,128)(2,1)S(1)}, bf16[192,128]{1,0:T(8,128)(2,1)S(1)}, u32[]{:S(2)}, u32[]{:S(2)}) collective-permute-start(bf16[192,128]{1,0:T(8,128)(2,1)S(1)} %fusion.11), channel_id=1, source_target_pairs={{0,16},{16,0},{1,17},{17,1},{2,18},{18,2},{3,19},{19,3},{4,20},{20... | collective-permute-start | bytes 147464 | tf_op jit(solution)/shard_map/ppermute | solution.py:152
  26.2 5.3 %collective-permute-start.10 = (bf16[192,128]{1,0:T(8,128)(2,1)S(1)}, bf16[192,128]{1,0:T(8,128)(2,1)S(1)}, u32[]{:S(2)}, u32[]{:S(2)}) collective-permute-start(bf16[192,128]{1,0:T(8,128)(2,1)S(1)} %get-tuple-element.48), channel_id=1, source_target_pairs={{0,16},{16,0},{1,17},{17,1},{2,18},{18,2},{3,19},{19,3},{4,20},{20... | collective-permute-start | bytes 147464 | tf_op jit(solution)/shard_map/ppermute | solution.py:152
  30.3 15.8 %copy-start = (f32[384,128]{1,0:T(8,128)S(1)}, f32[384,128]{1,0:T(8,128)}, u32[]{:S(2)}) copy-start(f32[384,128]{1,0:T(8,128)} %refs_0_.1) | copy-start | bytes 589828
  30.3 15.8 %copy-start.1 = (f32[384,128]{1,0:T(8,128)S(1)}, f32[384,128]{1,0:T(8,128)}, u32[]{:S(2)}) copy-start(f32[384,128]{1,0:T(8,128)} %refs_1_.1) | copy-start | bytes 589828
  30.3 4.9 %collective-permute-start.12 = (f32[192,128]{1,0:T(8,128)S(1)}, f32[192,128]{1,0:T(8,128)S(1)}, u32[]{:S(2)}, u32[]{:S(2)}) collective-permute-start(f32[192,128]{1,0:T(8,128)S(1)} %get-tuple-element.62), channel_id=1, source_target_pairs={{0,1},{1,0},{2,3},{3,2},{4,5},{5,4},{6,7},{7,6},{8,9},{9,8},{10,11... | collective-permute-start | bytes 294920 | tf_op jit(solution)/shard_map/ppermute | solution.py:152
  31.5 4.7 %collective-permute-start.11 = (bf16[2,192,128]{2,1,0:T(8,128)(2,1)S(1)}, bf16[2,192,128]{2,1,0:T(8,128)(2,1)S(1)}, u32[]{:S(2)}, u32[]{:S(2)}) collective-permute-start(bf16[2,192,128]{2,1,0:T(8,128)(2,1)S(1)} %get-tuple-element.56), channel_id=1, source_target_pairs={{0,4},{1,5},{2,6},{3,7},{4,0},{5,1},{6,2},{7,3},{8,12},{9,13},{10,... | collective-permute-start | bytes 294920 | tf_op jit(solution)/shard_map/ppermute | solution.py:162
  32.2 4.9 %collective-permute-start.15 = (bf16[2,192,128]{2,1,0:T(8,128)(2,1)S(1)}, bf16[2,192,128]{2,1,0:T(8,128)(2,1)S(1)}, u32[]{:S(2)}, u32[]{:S(2)}) collective-permute-start(bf16[2,192,128]{2,1,0:T(8,128)(2,1)S(1)} %get-tuple-element.56), channel_id=1, source_target_pairs={{0,1},{1,0},{2,3},{3,2},{4,5},{5,4},{6,7},{7,6},{8,9},{9,8},{10,11... | collective-permute-start | bytes 294920 | tf_op jit(solution)/shard_map/ppermute | solution.py:162
  33.4 6.3 %collective-permute-start.13 = (bf16[2,192,128]{2,1,0:T(8,128)(2,1)S(1)}, bf16[2,192,128]{2,1,0:T(8,128)(2,1)S(1)}, u32[]{:S(2)}, u32[]{:S(2)}) collective-permute-start(bf16[2,192,128]{2,1,0:T(8,128)(2,1)S(1)} %get-tuple-element.56), channel_id=1, source_target_pairs={{0,8},{1,9},{2,10},{3,11},{4,12},{5,13},{6,14},{7,15},{8,0},{9,1},... | collective-permute-start | bytes 294920 | tf_op jit(solution)/shard_map/ppermute | solution.py:162
  36.2 4.6 %collective-permute-start.14 = (bf16[2,192,128]{2,1,0:T(8,128)(2,1)S(1)}, bf16[2,192,128]{2,1,0:T(8,128)(2,1)S(1)}, u32[]{:S(2)}, u32[]{:S(2)}) collective-permute-start(bf16[2,192,128]{2,1,0:T(8,128)(2,1)S(1)} %collective-permute-done.11), channel_id=1, source_target_pairs={{0,1},{1,0},{2,3},{3,2},{4,5},{5,4},{6,7},{7,6},{8,9},{9,8},{10,11... | collective-permute-start | bytes 294920 | tf_op jit(solution)/shard_map/ppermute | solution.py:162
  37.1 5.4 %collective-permute-start.16 = (bf16[2,192,128]{2,1,0:T(8,128)(2,1)S(1)}, bf16[2,192,128]{2,1,0:T(8,128)(2,1)S(1)}, u32[]{:S(2)}, u32[]{:S(2)}) collective-permute-start(bf16[2,192,128]{2,1,0:T(8,128)(2,1)S(1)} %collective-permute-done.15), channel_id=1, source_target_pairs={{0,8},{1,9},{2,10},{3,11},{4,12},{5,13},{6,14},{7,15},{8,0},{9,1},... | collective-permute-start | bytes 294920 | tf_op jit(solution)/shard_map/ppermute | solution.py:162
  39.7 4.6 %collective-permute-start.18 = (bf16[2,192,128]{2,1,0:T(8,128)(2,1)S(1)}, bf16[2,192,128]{2,1,0:T(8,128)(2,1)S(1)}, u32[]{:S(2)}, u32[]{:S(2)}) collective-permute-start(bf16[2,192,128]{2,1,0:T(8,128)(2,1)S(1)} %collective-permute-done.13), channel_id=1, source_target_pairs={{0,4},{1,5},{2,6},{3,7},{4,0},{5,1},{6,2},{7,3},{8,12},{9,13},{10,... | collective-permute-start | bytes 294920 | tf_op jit(solution)/shard_map/ppermute | solution.py:162
  40.8 4.6 %collective-permute-start.19 = (bf16[2,192,128]{2,1,0:T(8,128)(2,1)S(1)}, bf16[2,192,128]{2,1,0:T(8,128)(2,1)S(1)}, u32[]{:S(2)}, u32[]{:S(2)}) collective-permute-start(bf16[2,192,128]{2,1,0:T(8,128)(2,1)S(1)} %collective-permute-done.14), channel_id=1, source_target_pairs={{0,8},{1,9},{2,10},{3,11},{4,12},{5,13},{6,14},{7,15},{8,0},{9,1},... | collective-permute-start | bytes 294920 | tf_op jit(solution)/shard_map/ppermute | solution.py:162
  42.6 5.4 %collective-permute-start.17 = (bf16[4,2,192,128]{3,2,1,0:T(8,128)(2,1)S(1)}, bf16[4,2,192,128]{3,2,1,0:T(8,128)(2,1)S(1)}, u32[]{:S(2)}, u32[]{:S(2)}) collective-permute-start(bf16[4,2,192,128]{3,2,1,0:T(8,128)(2,1)S(1)} %pad_maximum_fusion.refs_0_), channel_id=1, source_target_pairs={{0,2},{2,0},{1,3},{3,1},{4,6},{6,4},{5,7},{7,5},{8,10},{10,8},{9,1... | collective-permute-start | bytes 1179656 | tf_op jit(solution)/shard_map/ppermute | solution.py:152
  45.5 4.4 %collective-permute-start.20 = (bf16[3,2,192,128]{3,2,1,0:T(8,128)(2,1)S(1)}, bf16[3,2,192,128]{3,2,1,0:T(8,128)(2,1)S(1)}, u32[]{:S(2)}, u32[]{:S(2)}) collective-permute-start(bf16[3,2,192,128]{3,2,1,0:T(8,128)(2,1)S(1)} %pad_maximum_fusion.1.refs_0_), channel_id=1, source_target_pairs={{0,2},{2,0},{1,3},{3,1},{4,6},{6,4},{5,7},{7,5},{8,10},{10,8},{9,1... | collective-permute-start | bytes 884744 | tf_op jit(solution)/shard_map/ppermute | solution.py:152
  45.6 4.3 %collective-permute-start.21 = (bf16[2,192,128]{2,1,0:T(8,128)(2,1)}, bf16[2,192,128]{2,1,0:T(8,128)(2,1)S(1)}, u32[]{:S(2)}, u32[]{:S(2)}) collective-permute-start(bf16[2,192,128]{2,1,0:T(8,128)(2,1)} %copy-done.3), channel_id=1, source_target_pairs={{0,2},{2,0},{1,3},{3,1},{4,6},{6,4},{5,7},{7,5},{8,10},{10,8},{9,1... | collective-permute-start | bytes 294920 | tf_op jit(solution)/shard_map/ppermute | solution.py:152
  (2 other events, 15.6 us)

commit v23 on v20

--- a/solution.py
+++ b/solution.py
@@ -237,10 +237,12 @@
         (x, yz, z, xy), (y, zx, corner, home) = [
             own.astype(f32) + theirs.astype(f32) for own, theirs in zip(kept, arrived)
         ]
-        corner = to_corner(corner.astype(bf16))
-        z = z + to_neighbour(zx.astype(bf16), "x").astype(f32)
-        y = y + to_neighbour(yz.astype(bf16), "z").astype(f32)
-        x = x + to_neighbour(xy.astype(bf16), "y").astype(f32)
+        zx, yz, xy = [
+            to_neighbour(part.astype(bf16), axis) for part, axis in ((zx, "x"), (yz, "z"), (xy, "y"))
+        ]
+        yz, corner = lax.optimization_barrier((yz, corner.astype(bf16)))
+        corner = to_corner(corner)
+        z, y, x = z + zx.astype(f32), y + yz.astype(f32), x + xy.astype(f32)
         parts = [to_neighbour(part.astype(bf16), axis) for part, axis in ((z, "z"), (y, "y"), (x, "x"))]
         parts = lax.optimization_barrier((corner, *parts))
         total = home + sum(part.astype(f32) for part in parts)

time: 50 us -> 52.3 us (1.046)
  waiting for transfers between devices: 13.5 us -> 21.6 us
  starting transfers between devices: 26.9 us -> 21.1 us
    ppermute x11, starting transfers between devices: 18.8 us -> 14.5 us  [cube_swap(): return lax.ppermute(x, AXES[1:], pairs)]
    ppermute x8, waiting for transfers between devices: 4.47 us -> 8.74 us  [swap(): lax.ppermute(x, axis, [(i, i ^ mask) for i in range(fine.shape[axis])])]
    ppermute x11, waiting for transfers between devices: 9.05 us -> 12.9 us  [cube_swap(): return lax.ppermute(x, AXES[1:], pairs)]
    ppermute x8, starting transfers between devices: 8.02 us -> 6.53 us  [swap(): lax.ppermute(x, axis, [(i, i ^ mask) for i in range(fine.shape[axis])])]
  transfers between devices with their start and end apart: 19 -> 19, of which waited for: 10 -> 12; matrix products, arithmetic and copies ran while one was open for 3% -> 3% of each run, Pallas kernels for 6% -> 6%
where the time goes in v23:
time: 52.3 us; the launch traced here: 52.2 us
  waiting for transfers between devices  21.6 us (41%)
  starting transfers between devices  21.1 us (40%)
  Pallas kernels  6.43 us (12%)
  between operations  1.55 us (3%)
  other arithmetic  1.41 us (3%)
    ppermute x11, starting transfers between devices, cube_swap(): return lax.ppermute(x, AXES[1:], pairs)  14.5 us
    ppermute x11, waiting for transfers between devices, cube_swap(): return lax.ppermute(x, AXES[1:], pairs)  12.9 us
    ppermute x8, waiting for transfers between devices, swap(): lax.ppermute(x, axis, [(i, i ^ mask) for i in range(fine.shape[axis])])  8.74 us
    ppermute x8, starting transfers between devices, swap(): lax.ppermute(x, axis, [(i, i ^ mask) for i in range(fine.shape[axis])])  6.53 us
    pallas_call x1, Pallas kernels, per_device(): pl.pallas_call(functools.partial(first_grad_kernel, n_high), out_shape=[s...  2.06 us
    pallas_call x1, Pallas kernels, per_device(): pl.pallas_call(functools.partial(columns_kernel, n_high, 4 * half), out_s...  1.91 us
    pallas_call x2, Pallas kernels, per_device(): pl.pallas_call(functools.partial(logits_kernel, n_high, group), out_shape...  1.89 us
  transfers between devices with their start and end apart: 19, of which 12 were waited for; matrix products, arithmetic and copies ran while one was open for 3% of the time, Pallas kernels for 6%

profile of v23, /device:TPU:0, one launch (start us, length us, event | category | flops | bytes accessed | tf_op | source)
XLA Modules:
  0.0 52.2 jit_solution(11785152697026145157)
XLA Ops:
  0.6 2.1 %shard_map.93 = (bf16[4,2,192,128]{3,2,1,0:T(8,128)(2,1)S(1)}, bf16[4,2,192,128]{3,2,1,0:T(8,128)(2,1)S(1)}, f32[3,192,128]{2,1,0:T(8,128)S(1)}, bf16[4,256,768]{2,1,0:T(8,128)(2,1)S(1)}, bf16[128,256]{1,0:T(8,128)(2,1)S(1)}) custom-call(bf16[256,6144]{1,0:T(8,128)(2,1)} %acts_ref.2, bf16[256,128]{1,0:T(8,128)(2,1)} %grad_ref.1, f32[384,128]{1,0:T(8,128)} %refs_0_.1, ...), custom_call_target="tpu_custom_call" | custom-call | tf_op jit(solution)/shard_map/pallas_call | solution.py:186
  3.8 0.8 %collective-permute-done = bf16[4,2,192,128]{3,2,1,0:T(8,128)(2,1)S(1)} collective-permute-done((bf16[4,2,192,128]{3,2,1,0:T(8,128)(2,1)S(1)}, bf16[4,2,192,128]{3,2,1,0:T(8,128)(2,1)S(1)}, u32[]{:S(2)}, u32[]{:S(2)}) %collective-permute-start) | collective-permute-done | bytes 393248 | tf_op jit(solution)/shard_map/ppermute | solution.py:144
  5.1 2.7 %collective-permute-start.4 = (bf16[2,192,128]{2,1,0:T(8,128)(2,1)S(1)}, bf16[2,192,128]{2,1,0:T(8,128)(2,1)S(1)}, u32[]{:S(2)}, u32[]{:S(2)}) collective-permute-start(bf16[2,192,128]{2,1,0:T(8,128)(2,1)S(1)} %get-tuple-element.77), channel_id=1, source_target_pairs={{0,4},{1,5},{2,6},{3,7},{4,0},{5,1},{6,2},{7,3},{8,12},{9,13},{10,... | collective-permute-start | bytes 294920 | tf_op jit(solution)/shard_map/ppermute | solution.py:154
  7.9 1.6 %collective-permute-start.7 = (bf16[2,192,128]{2,1,0:T(8,128)(2,1)S(1)}, bf16[2,192,128]{2,1,0:T(8,128)(2,1)S(1)}, u32[]{:S(2)}, u32[]{:S(2)}) collective-permute-start(bf16[2,192,128]{2,1,0:T(8,128)(2,1)S(1)} %get-tuple-element.75), channel_id=1, source_target_pairs={{0,1},{1,0},{2,3},{3,2},{4,5},{5,4},{6,7},{7,6},{8,9},{9,8},{10,11... | collective-permute-start | bytes 294920 | tf_op jit(solution)/shard_map/ppermute | solution.py:154
  9.5 1.6 %collective-permute-start.2 = (bf16[2,192,128]{2,1,0:T(8,128)(2,1)S(1)}, bf16[2,192,128]{2,1,0:T(8,128)(2,1)S(1)}, u32[]{:S(2)}, u32[]{:S(2)}) collective-permute-start(bf16[2,192,128]{2,1,0:T(8,128)(2,1)S(1)} %get-tuple-element.76), channel_id=1, source_target_pairs={{0,8},{1,9},{2,10},{3,11},{4,12},{5,13},{6,14},{7,15},{8,0},{9,1},... | collective-permute-start | bytes 294920 | tf_op jit(solution)/shard_map/ppermute | solution.py:154
  11.1 1.7 %collective-permute-done.7 = bf16[2,192,128]{2,1,0:T(8,128)(2,1)S(1)} collective-permute-done((bf16[2,192,128]{2,1,0:T(8,128)(2,1)S(1)}, bf16[2,192,128]{2,1,0:T(8,128)(2,1)S(1)}, u32[]{:S(2)}, u32[]{:S(2)}) %collective-permute-start.7) | collective-permute-done | bytes 98336 | tf_op jit(solution)/shard_map/ppermute | solution.py:154
  12.8 1.6 %collective-permute-start.5 = (bf16[2,192,128]{2,1,0:T(8,128)(2,1)S(1)}, bf16[2,192,128]{2,1,0:T(8,128)(2,1)S(1)}, u32[]{:S(2)}, u32[]{:S(2)}) collective-permute-start(bf16[2,192,128]{2,1,0:T(8,128)(2,1)S(1)} %get-tuple-element.70), channel_id=1, source_target_pairs={{0,8},{1,9},{2,10},{3,11},{4,12},{5,13},{6,14},{7,15},{8,0},{9,1},... | collective-permute-start | bytes 294920 | tf_op jit(solution)/shard_map/ppermute | solution.py:154
  14.5 1.4 %collective-permute-start.8 = (bf16[2,192,128]{2,1,0:T(8,128)(2,1)S(1)}, bf16[2,192,128]{2,1,0:T(8,128)(2,1)S(1)}, u32[]{:S(2)}, u32[]{:S(2)}) collective-permute-start(bf16[2,192,128]{2,1,0:T(8,128)(2,1)S(1)} %get-tuple-element.69), channel_id=1, source_target_pairs={{0,4},{1,5},{2,6},{3,7},{4,0},{5,1},{6,2},{7,3},{8,12},{9,13},{10,... | collective-permute-start | bytes 294920 | tf_op jit(solution)/shard_map/ppermute | solution.py:154
  15.9 1.6 %collective-permute-start.6 = (bf16[2,192,128]{2,1,0:T(8,128)(2,1)S(1)}, bf16[2,192,128]{2,1,0:T(8,128)(2,1)S(1)}, u32[]{:S(2)}, u32[]{:S(2)}) collective-permute-start(bf16[2,192,128]{2,1,0:T(8,128)(2,1)S(1)} %fusion.4), channel_id=1, source_target_pairs={{0,1},{1,0},{2,3},{3,2},{4,5},{5,4},{6,7},{7,6},{8,9},{9,8},{10,11... | collective-permute-start | bytes 294920 | tf_op jit(solution)/shard_map/ppermute | solution.py:154
  18.1 1.0 %collective-permute-done.8 = bf16[2,192,128]{2,1,0:T(8,128)(2,1)S(1)} collective-permute-done((bf16[2,192,128]{2,1,0:T(8,128)(2,1)S(1)}, bf16[2,192,128]{2,1,0:T(8,128)(2,1)S(1)}, u32[]{:S(2)}, u32[]{:S(2)}) %collective-permute-start.8) | collective-permute-done | bytes 98336 | tf_op jit(solution)/shard_map/ppermute | solution.py:154
  19.1 2.5 %collective-permute-done.6 = bf16[2,192,128]{2,1,0:T(8,128)(2,1)S(1)} collective-permute-done((bf16[2,192,128]{2,1,0:T(8,128)(2,1)S(1)}, bf16[2,192,128]{2,1,0:T(8,128)(2,1)S(1)}, u32[]{:S(2)}, u32[]{:S(2)}) %collective-permute-start.6) | collective-permute-done | bytes 98336 | tf_op jit(solution)/shard_map/ppermute | solution.py:154
  21.7 2.3 %collective-permute-done.3 = bf16[2,192,128]{2,1,0:T(8,128)(2,1)S(1)} collective-permute-done((bf16[2,192,128]{2,1,0:T(8,128)(2,1)S(1)}, bf16[2,192,128]{2,1,0:T(8,128)(2,1)S(1)}, u32[]{:S(2)}, u32[]{:S(2)}) %collective-permute-start.3) | collective-permute-done | bytes 98336 | tf_op jit(solution)/shard_map/ppermute | solution.py:154
  24.0 3.2 %collective-permute-start.9 = (bf16[192,128]{1,0:T(8,128)(2,1)S(1)}, bf16[192,128]{1,0:T(8,128)(2,1)S(1)}, u32[]{:S(2)}, u32[]{:S(2)}) collective-permute-start(bf16[192,128]{1,0:T(8,128)(2,1)S(1)} %fusion.18), channel_id=1, source_target_pairs={{0,16},{16,0},{1,17},{17,1},{2,18},{18,2},{3,19},{19,3},{4,20},{20... | collective-permute-start | bytes 147464 | tf_op jit(solution)/shard_map/ppermute | solution.py:144
  27.9 2.5 %collective-permute-done.9 = bf16[192,128]{1,0:T(8,128)(2,1)S(1)} collective-permute-done((bf16[192,128]{1,0:T(8,128)(2,1)S(1)}, bf16[192,128]{1,0:T(8,128)(2,1)S(1)}, u32[]{:S(2)}, u32[]{:S(2)}) %collective-permute-start.9) | collective-permute-done | bytes 49184 | tf_op jit(solution)/shard_map/ppermute | solution.py:144
  30.6 2.2 %collective-permute-start.10 = (bf16[192,128]{1,0:T(8,128)(2,1)S(1)}, bf16[192,128]{1,0:T(8,128)(2,1)S(1)}, u32[]{:S(2)}, u32[]{:S(2)}) collective-permute-start(bf16[192,128]{1,0:T(8,128)(2,1)S(1)} %get-tuple-element.67), channel_id=1, source_target_pairs={{0,16},{16,0},{1,17},{17,1},{2,18},{18,2},{3,19},{19,3},{4,20},{20... | collective-permute-start | bytes 147464 | tf_op jit(solution)/shard_map/ppermute | solution.py:144
  32.8 2.8 %collective-permute-done.10 = bf16[192,128]{1,0:T(8,128)(2,1)S(1)} collective-permute-done((bf16[192,128]{1,0:T(8,128)(2,1)S(1)}, bf16[192,128]{1,0:T(8,128)(2,1)S(1)}, u32[]{:S(2)}, u32[]{:S(2)}) %collective-permute-start.10) | collective-permute-done | bytes 49184 | tf_op jit(solution)/shard_map/ppermute | solution.py:144
  35.8 1.6 %collective-permute-done.12 = f32[192,128]{1,0:T(8,128)S(1)} collective-permute-done((f32[192,128]{1,0:T(8,128)S(1)}, f32[192,128]{1,0:T(8,128)S(1)}, u32[]{:S(2)}, u32[]{:S(2)}) %collective-permute-start.12) | collective-permute-done | bytes 98336 | tf_op jit(solution)/shard_map/ppermute | solution.py:144
  37.7 1.4 %collective-permute-start.17 = (bf16[2,2,192,128]{3,2,1,0:T(8,128)(2,1)S(1)}, bf16[2,2,192,128]{3,2,1,0:T(8,128)(2,1)S(1)}, u32[]{:S(2)}, u32[]{:S(2)}) collective-permute-start(bf16[2,2,192,128]{3,2,1,0:T(8,128)(2,1)S(1)} %maximum_select_fusion), channel_id=1, source_target_pairs={{0,8},{1,9},{2,7},{3,6},{4,12},{5,13},{6,3},{7,2},{8,0},{9,1},{10,... | collective-permute-start | bytes 589832 | tf_op jit(solution)/shard_map/ppermute | solution.py:154
  39.2 1.7 %collective-permute-start.15 = (bf16[2,2,192,128]{3,2,1,0:T(8,128)(2,1)S(1)}, bf16[2,2,192,128]{3,2,1,0:T(8,128)(2,1)S(1)}, u32[]{:S(2)}, u32[]{:S(2)}) collective-permute-start(bf16[2,2,192,128]{3,2,1,0:T(8,128)(2,1)S(1)} %maximum_select_fusion), channel_id=1, source_target_pairs={{0,1},{1,0},{2,14},{3,15},{4,5},{5,4},{6,10},{7,11},{8,9},{9,8},{1... | collective-permute-start | bytes 589832 | tf_op jit(solution)/shard_map/ppermute | solution.py:154
  40.9 0.9 %multiply_subtract_fusion = (f32[384,128]{1,0:T(8,128)}, f32[384,128]{1,0:T(8,128)}, f32[384,128]{1,0:T(8,128)}) fusion(f32[384,128]{1,0:T(8,128)S(1)} %copy-done, f32[]{:T(128)} %bitcast.14, f32[]{:T(128)} %bitcast.12, f32[192,128]{1,0:T(8,128)S(1)} %get-tuple-element.68, f32[192,128]{1,0:T(8,128)S(1)} %collective-permute-done.12, pred[]{:T(512)S(6)} %eq.7, ...), kind=kLoop, calls=%fused_computation.18 | loop fusion | flops 884736 | bytes 1376265 | tf_op jit(solution)/shard_map/sub | solution.py:31
  41.8 1.9 %shard_map.95 = (bf16[256,3072]{1,0:T(8,128)(2,1)S(1)}, bf16[256,3072]{1,0:T(8,128)(2,1)S(1)}) custom-call(bf16[256,6144]{1,0:T(8,128)(2,1)} %acts_ref.2), custom_call_target="tpu_custom_call" | custom-call | tf_op jit(solution)/shard_map/pallas_call | solution.py:273
  44.0 4.4 %collective-permute-done.13 = bf16[2,2,192,128]{3,2,1,0:T(8,128)(2,1)S(1)} collective-permute-done((bf16[2,2,192,128]{3,2,1,0:T(8,128)(2,1)S(1)}, bf16[2,2,192,128]{3,2,1,0:T(8,128)(2,1)S(1)}, u32[]{:S(2)}, u32[]{:S(2)}) %collective-permute-start.13) | collective-permute-done | bytes 196640 | tf_op jit(solution)/shard_map/ppermute | solution.py:154
  49.3 1.0 %collective-permute-done.18.refs_1_ = bf16[4,2,192,128]{3,2,1,0:T(8,128)(2,1)S(1)} collective-permute-done((bf16[4,2,192,128]{3,2,1,0:T(8,128)(2,1)S(1)}, bf16[4,2,192,128]{3,2,1,0:T(8,128)(2,1)S(1)}, u32[]{:S(2)}, u32[]{:S(2)}) %collective-permute-start.18) | collective-permute-done | bytes 393248 | tf_op jit(solution)/shard_map/ppermute | solution.py:144
  50.9 1.3 %shard_map.97 = bf16[256,128]{1,0:T(8,128)(2,1)} custom-call(bf16[256,3072]{1,0:T(8,128)(2,1)S(1)} %get-tuple-element.60.columns_ref, bf16[3,2,192,128]{3,2,1,0:T(8,128)(2,1)S(1)} %pad_maximum_fusion.refs_0_, bf16[3,2,192,128]{3,2,1,0:T(8,128)(2,1)S(1)} %collective-permute-done.16.refs_1_, bf16[1,2,192,128]{3,2,1,0:T(8,128)(2,1)S(1)} %get-tuple-element.79.refs_2_, ...), custom_call_target="tpu_custom_call" | custom-call | tf_op jit(solution)/shard_map/pallas_call | solution.py:293
  (40 shorter events, 4.8 us)
Async XLA Ops:
  2.7 1.9 %collective-permute-start = (bf16[4,2,192,128]{3,2,1,0:T(8,128)(2,1)S(1)}, bf16[4,2,192,128]{3,2,1,0:T(8,128)(2,1)S(1)}, u32[]{:S(2)}, u32[]{:S(2)}) collective-permute-start(bf16[4,2,192,128]{3,2,1,0:T(8,128)(2,1)S(1)} %get-tuple-element.36), channel_id=1, source_target_pairs={{0,2},{2,0},{1,3},{3,1},{4,6},{6,4},{5,7},{7,5},{8,10},{10,8},{9,1... | collective-permute-start | bytes 1179656 | tf_op jit(solution)/shard_map/ppermute | solution.py:144
  4.6 3.2 %collective-permute-start.1 = (bf16[4,2,192,128]{3,2,1,0:T(8,128)(2,1)S(1)}, bf16[4,2,192,128]{3,2,1,0:T(8,128)(2,1)S(1)}, u32[]{:S(2)}, u32[]{:S(2)}) collective-permute-start(bf16[4,2,192,128]{3,2,1,0:T(8,128)(2,1)S(1)} %get-tuple-element.42), channel_id=1, source_target_pairs={{0,2},{2,0},{1,3},{3,1},{4,6},{6,4},{5,7},{7,5},{8,10},{10,8},{9,1... | collective-permute-start | bytes 1179656 | tf_op jit(solution)/shard_map/ppermute | solution.py:144
  5.1 6.0 %collective-permute-start.4 = (bf16[2,192,128]{2,1,0:T(8,128)(2,1)S(1)}, bf16[2,192,128]{2,1,0:T(8,128)(2,1)S(1)}, u32[]{:S(2)}, u32[]{:S(2)}) collective-permute-start(bf16[2,192,128]{2,1,0:T(8,128)(2,1)S(1)} %get-tuple-element.77), channel_id=1, source_target_pairs={{0,4},{1,5},{2,6},{3,7},{4,0},{5,1},{6,2},{7,3},{8,12},{9,13},{10,... | collective-permute-start | bytes 294920 | tf_op jit(solution)/shard_map/ppermute | solution.py:154
  7.9 4.8 %collective-permute-start.7 = (bf16[2,192,128]{2,1,0:T(8,128)(2,1)S(1)}, bf16[2,192,128]{2,1,0:T(8,128)(2,1)S(1)}, u32[]{:S(2)}, u32[]{:S(2)}) collective-permute-start(bf16[2,192,128]{2,1,0:T(8,128)(2,1)S(1)} %get-tuple-element.75), channel_id=1, source_target_pairs={{0,1},{1,0},{2,3},{3,2},{4,5},{5,4},{6,7},{7,6},{8,9},{9,8},{10,11... | collective-permute-start | bytes 294920 | tf_op jit(solution)/shard_map/ppermute | solution.py:154
  9.5 6.4 %collective-permute-start.2 = (bf16[2,192,128]{2,1,0:T(8,128)(2,1)S(1)}, bf16[2,192,128]{2,1,0:T(8,128)(2,1)S(1)}, u32[]{:S(2)}, u32[]{:S(2)}) collective-permute-start(bf16[2,192,128]{2,1,0:T(8,128)(2,1)S(1)} %get-tuple-element.76), channel_id=1, source_target_pairs={{0,8},{1,9},{2,10},{3,11},{4,12},{5,13},{6,14},{7,15},{8,0},{9,1},... | collective-permute-start | bytes 294920 | tf_op jit(solution)/shard_map/ppermute | solution.py:154
  12.8 28.1 %copy-start = (f32[384,128]{1,0:T(8,128)S(1)}, f32[384,128]{1,0:T(8,128)}, u32[]{:S(2)}) copy-start(f32[384,128]{1,0:T(8,128)} %refs_0_.1) | copy-start | bytes 589828
  12.8 28.1 %copy-start.1 = (f32[384,128]{1,0:T(8,128)S(1)}, f32[384,128]{1,0:T(8,128)}, u32[]{:S(2)}) copy-start(f32[384,128]{1,0:T(8,128)} %refs_1_.1) | copy-start | bytes 589828
  12.8 28.1 %copy-start.2 = (f32[384,128]{1,0:T(8,128)S(1)}, f32[384,128]{1,0:T(8,128)}, u32[]{:S(2)}) copy-start(f32[384,128]{1,0:T(8,128)} %refs_2_.1) | copy-start | bytes 589828
  12.8 5.2 %collective-permute-start.5 = (bf16[2,192,128]{2,1,0:T(8,128)(2,1)S(1)}, bf16[2,192,128]{2,1,0:T(8,128)(2,1)S(1)}, u32[]{:S(2)}, u32[]{:S(2)}) collective-permute-start(bf16[2,192,128]{2,1,0:T(8,128)(2,1)S(1)} %get-tuple-element.70), channel_id=1, source_target_pairs={{0,8},{1,9},{2,10},{3,11},{4,12},{5,13},{6,14},{7,15},{8,0},{9,1},... | collective-permute-start | bytes 294920 | tf_op jit(solution)/shard_map/ppermute | solution.py:154
  14.5 4.6 %collective-permute-start.8 = (bf16[2,192,128]{2,1,0:T(8,128)(2,1)S(1)}, bf16[2,192,128]{2,1,0:T(8,128)(2,1)S(1)}, u32[]{:S(2)}, u32[]{:S(2)}) collective-permute-start(bf16[2,192,128]{2,1,0:T(8,128)(2,1)S(1)} %get-tuple-element.69), channel_id=1, source_target_pairs={{0,4},{1,5},{2,6},{3,7},{4,0},{5,1},{6,2},{7,3},{8,12},{9,13},{10,... | collective-permute-start | bytes 294920 | tf_op jit(solution)/shard_map/ppermute | solution.py:154
  15.9 5.7 %collective-permute-start.6 = (bf16[2,192,128]{2,1,0:T(8,128)(2,1)S(1)}, bf16[2,192,128]{2,1,0:T(8,128)(2,1)S(1)}, u32[]{:S(2)}, u32[]{:S(2)}) collective-permute-start(bf16[2,192,128]{2,1,0:T(8,128)(2,1)S(1)} %fusion.4), channel_id=1, source_target_pairs={{0,1},{1,0},{2,3},{3,2},{4,5},{5,4},{6,7},{7,6},{8,9},{9,8},{10,11... | collective-permute-start | bytes 294920 | tf_op jit(solution)/shard_map/ppermute | solution.py:154
  17.5 6.4 %collective-permute-start.3 = (bf16[2,192,128]{2,1,0:T(8,128)(2,1)S(1)}, bf16[2,192,128]{2,1,0:T(8,128)(2,1)S(1)}, u32[]{:S(2)}, u32[]{:S(2)}) collective-permute-start(bf16[2,192,128]{2,1,0:T(8,128)(2,1)S(1)} %get-tuple-element.43), channel_id=1, source_target_pairs={{0,13},{1,12},{2,15},{3,14},{4,9},{5,8},{6,11},{7,10},{8,5},{9,4},... | collective-permute-start | bytes 294920 | tf_op jit(solution)/shard_map/ppermute | solution.py:154
  24.0 6.5 %collective-permute-start.9 = (bf16[192,128]{1,0:T(8,128)(2,1)S(1)}, bf16[192,128]{1,0:T(8,128)(2,1)S(1)}, u32[]{:S(2)}, u32[]{:S(2)}) collective-permute-start(bf16[192,128]{1,0:T(8,128)(2,1)S(1)} %fusion.18), channel_id=1, source_target_pairs={{0,16},{16,0},{1,17},{17,1},{2,18},{18,2},{3,19},{19,3},{4,20},{20... | collective-permute-start | bytes 147464 | tf_op jit(solution)/shard_map/ppermute | solution.py:144
  30.6 5.1 %collective-permute-start.10 = (bf16[192,128]{1,0:T(8,128)(2,1)S(1)}, bf16[192,128]{1,0:T(8,128)(2,1)S(1)}, u32[]{:S(2)}, u32[]{:S(2)}) collective-permute-start(bf16[192,128]{1,0:T(8,128)(2,1)S(1)} %get-tuple-element.67), channel_id=1, source_target_pairs={{0,16},{16,0},{1,17},{17,1},{2,18},{18,2},{3,19},{19,3},{4,20},{20... | collective-permute-start | bytes 147464 | tf_op jit(solution)/shard_map/ppermute | solution.py:144
  32.8 4.6 %collective-permute-start.12 = (f32[192,128]{1,0:T(8,128)S(1)}, f32[192,128]{1,0:T(8,128)S(1)}, u32[]{:S(2)}, u32[]{:S(2)}) collective-permute-start(f32[192,128]{1,0:T(8,128)S(1)} %get-tuple-element.68), channel_id=1, source_target_pairs={{0,1},{1,0},{2,3},{3,2},{4,5},{5,4},{6,7},{7,6},{8,9},{9,8},{10,11... | collective-permute-start | bytes 294920 | tf_op jit(solution)/shard_map/ppermute | solution.py:144
  35.7 1.8 %collective-permute-start.11 = (bf16[2,192,128]{2,1,0:T(8,128)(2,1)S(1)}, bf16[2,192,128]{2,1,0:T(8,128)(2,1)S(1)}, u32[]{:S(2)}, u32[]{:S(2)}) collective-permute-start(bf16[2,192,128]{2,1,0:T(8,128)(2,1)S(1)} %get-tuple-element.80), channel_id=1, source_target_pairs={{0,2},{2,0},{1,3},{3,1},{4,6},{6,4},{5,7},{7,5},{8,10},{10,8},{9,1... | collective-permute-start | bytes 294920 | tf_op jit(solution)/shard_map/ppermute | solution.py:144
  35.7 8.3 %collective-permute-start.14 = (bf16[2,192,128]{2,1,0:T(8,128)(2,1)S(1)}, bf16[2,192,128]{2,1,0:T(8,128)(2,1)S(1)}, u32[]{:S(2)}, u32[]{:S(2)}) collective-permute-start(bf16[2,192,128]{2,1,0:T(8,128)(2,1)S(1)} %get-tuple-element.80), channel_id=1, source_target_pairs={{0,13},{1,12},{2,15},{3,14},{4,9},{5,8},{6,11},{7,10},{8,5},{9,4},... | collective-permute-start | bytes 294920 | tf_op jit(solution)/shard_map/ppermute | solution.py:154
  37.5 11.0 %collective-permute-start.13 = (bf16[2,2,192,128]{3,2,1,0:T(8,128)(2,1)S(1)}, bf16[2,2,192,128]{3,2,1,0:T(8,128)(2,1)S(1)}, u32[]{:S(2)}, u32[]{:S(2)}) collective-permute-start(bf16[2,2,192,128]{3,2,1,0:T(8,128)(2,1)S(1)} %maximum_select_fusion), channel_id=1, source_target_pairs={{0,4},{1,5},{2,11},{3,10},{4,0},{5,1},{6,15},{7,14},{8,12},{9,13},... | collective-permute-start | bytes 589832 | tf_op jit(solution)/shard_map/ppermute | solution.py:154
  37.7 10.7 %collective-permute-start.17 = (bf16[2,2,192,128]{3,2,1,0:T(8,128)(2,1)S(1)}, bf16[2,2,192,128]{3,2,1,0:T(8,128)(2,1)S(1)}, u32[]{:S(2)}, u32[]{:S(2)}) collective-permute-start(bf16[2,2,192,128]{3,2,1,0:T(8,128)(2,1)S(1)} %maximum_select_fusion), channel_id=1, source_target_pairs={{0,8},{1,9},{2,7},{3,6},{4,12},{5,13},{6,3},{7,2},{8,0},{9,1},{10,... | collective-permute-start | bytes 589832 | tf_op jit(solution)/shard_map/ppermute | solution.py:154
  39.2 10.0 %collective-permute-start.15 = (bf16[2,2,192,128]{3,2,1,0:T(8,128)(2,1)S(1)}, bf16[2,2,192,128]{3,2,1,0:T(8,128)(2,1)S(1)}, u32[]{:S(2)}, u32[]{:S(2)}) collective-permute-start(bf16[2,2,192,128]{3,2,1,0:T(8,128)(2,1)S(1)} %maximum_select_fusion), channel_id=1, source_target_pairs={{0,1},{1,0},{2,14},{3,15},{4,5},{5,4},{6,10},{7,11},{8,9},{9,8},{1... | collective-permute-start | bytes 589832 | tf_op jit(solution)/shard_map/ppermute | solution.py:154
  48.5 1.8 %collective-permute-start.18 = (bf16[4,2,192,128]{3,2,1,0:T(8,128)(2,1)S(1)}, bf16[4,2,192,128]{3,2,1,0:T(8,128)(2,1)S(1)}, u32[]{:S(2)}, u32[]{:S(2)}) collective-permute-start(bf16[4,2,192,128]{3,2,1,0:T(8,128)(2,1)S(1)} %constant_dynamic-update-slice_fusion.refs_0_), channel_id=1, source_target_pairs={{0,2},{2,0},{1,3},{3,1},{4,6},{6,4},{5,7},{7,5},{8,10},{10,8},{9,1... | collective-permute-start | bytes 1179656 | tf_op jit(solution)/shard_map/ppermute | solution.py:144
  49.2 1.7 %collective-permute-start.16 = (bf16[3,2,192,128]{3,2,1,0:T(8,128)(2,1)S(1)}, bf16[3,2,192,128]{3,2,1,0:T(8,128)(2,1)S(1)}, u32[]{:S(2)}, u32[]{:S(2)}) collective-permute-start(bf16[3,2,192,128]{3,2,1,0:T(8,128)(2,1)S(1)} %pad_maximum_fusion.refs_0_), channel_id=1, source_target_pairs={{0,2},{2,0},{1,3},{3,1},{4,6},{6,4},{5,7},{7,5},{8,10},{10,8},{9,1... | collective-permute-start | bytes 884744 | tf_op jit(solution)/shard_map/ppermute | solution.py:144

commit v24 on v21

--- a/solution.py
+++ b/solution.py
@@ -134,10 +134,9 @@
         for chip in NEXT[:2] if group == 0 else NEXT[2:]:
             place = LOWS[group].index(chip[0]) ^ by
             blocks += [(place, owner, rep ^ chip[1] ^ by) for owner in range(2)]
-        if group == 1:
-            blocks.append((1, by, rep ^ 1))
         pieces.append(blocks)
     if group == 1:
+        pieces += [[(1, owner, rep ^ 1)] for owner in (core, 1 - core)]
         pieces += [[(0, owner, rep)] for owner in (core, 1 - core)]
     return pieces
 
@@ -281,11 +280,13 @@
                 scratch_shapes=[pltpu.SemaphoreType.DMA((2, 2 * n_high))],
                 compiler_params=params,
             )(pltpu.with_memory_space_constraint(late_acts, pltpu.HBM))
-        got[0], corner, state, columns = lax.optimization_barrier((got[0], corner, state, columns))
-        first, second = jnp.concatenate(got[:2]), jnp.concatenate([got[2], corner[None]])
-        first, second = [first, swap(first, "core")], [second, swap(second, "core")]
-        second += [column[None], across[None]]
-        pieces = (first, second)
+        got, corner, state, columns = lax.optimization_barrier((got, corner, state, columns))
+        first, second = jnp.concatenate([*got[:2], corner[None]]), got[2]
+        first_over, second_over = swap(first, "core"), swap(second, "core")
+        pieces = (
+            [first, first_over],
+            [second, second_over, corner[None], first_over[4:], column[None], across[None]],
+        )
         logits = None
         for group, (received, acts_columns) in enumerate(zip(pieces, columns)):
             if in_kernels:

time: 48 us -> 48.9 us (1.019)
  waiting for transfers between devices: 13.1 us -> 14 us
  transfers between devices with their start and end apart: 20 -> 20, of which waited for: 10 -> 11; matrix products, arithmetic and copies ran while one was open for 3% -> 2% of each run, Pallas kernels for 7% -> 6%
where the time goes in v24:
time: 48.9 us; the launch traced here: 48.8 us
  starting transfers between devices  25.3 us (52%)
  waiting for transfers between devices  14 us (29%)
  Pallas kernels  6.44 us (13%)
  between operations  1.54 us (3%)
  other arithmetic  1.39 us (3%)
    ppermute x11, starting transfers between devices, cube_swap(): return lax.ppermute(x, AXES[1:], pairs)  17.1 us
    ppermute x11, waiting for transfers between devices, cube_swap(): return lax.ppermute(x, AXES[1:], pairs)  9.26 us
    ppermute x9, starting transfers between devices, swap(): lax.ppermute(x, axis, [(i, i ^ mask) for i in range(fine.shape[axis])])  8.19 us
    ppermute x9, waiting for transfers between devices, swap(): lax.ppermute(x, axis, [(i, i ^ mask) for i in range(fine.shape[axis])])  4.7 us
    pallas_call x1, Pallas kernels, per_device(): pl.pallas_call(functools.partial(first_grad_kernel, n_high), out_shape=[p...  2.07 us
    pallas_call x1, Pallas kernels, per_device(): pl.pallas_call(functools.partial(columns_kernel, n_high, 4 * half), out_s...  1.91 us
    pallas_call x2, Pallas kernels, per_device(): pl.pallas_call(functools.partial(logits_kernel, n_high, group), out_shape...  1.89 us
  transfers between devices with their start and end apart: 20, of which 11 were waited for; matrix products, arithmetic and copies ran while one was open for 2% of the time, Pallas kernels for 6%

profile of v24, /device:TPU:0, one launch (start us, length us, event | category | flops | bytes accessed | tf_op | source)
XLA Modules:
  0.0 48.8 jit_solution(12541015098138241872)
XLA Ops:
  0.6 2.1 %shard_map.93 = (bf16[2,2,192,128]{3,2,1,0:T(8,128)(2,1)S(1)}, bf16[2,2,192,128]{3,2,1,0:T(8,128)(2,1)S(1)}, bf16[2,2,192,128]{3,2,1,0:T(8,128)(2,1)S(1)}, bf16[...) custom-call(bf16[256,6144]{1,0:T(8,128)(2,1)} %acts_ref.2, ...), custom_call_target="tpu_custom_call" | custom-call | tf_op jit(solution)/shard_map/pallas_call | solution.py:192
  4.9 3.0 %collective-permute-start.2 = (bf16[2,192,128]{2,1,0:T(8,128)(2,1)S(1)}, bf16[2,192,128]{2,1,0:T(8,128)(2,1)S(1)}, u32[]{:S(2)}, u32[]{:S(2)}) collective-permute-start(bf16[2,192,128]{2,1,0:T(8,128)(2,1)S(1)} %get-tuple-element.86), channel_id=1, source_target_pairs={{0,1},{1,0},{2,14},{3,15},{4,5},{5,4},{6,10},{7,11},{8,9},{9,8},{1... | collective-permute-start | bytes 294920 | tf_op jit(solution)/shard_map/ppermute | solution.py:160
  7.9 2.5 %collective-permute-start.3 = (bf16[2,192,128]{2,1,0:T(8,128)(2,1)S(1)}, bf16[2,192,128]{2,1,0:T(8,128)(2,1)S(1)}, u32[]{:S(2)}, u32[]{:S(2)}) collective-permute-start(bf16[2,192,128]{2,1,0:T(8,128)(2,1)S(1)} %get-tuple-element.85), channel_id=1, source_target_pairs={{0,12},{1,13},{2,3},{3,2},{4,8},{5,9},{6,7},{7,6},{8,4},{9,5},{10,... | collective-permute-start | bytes 294920 | tf_op jit(solution)/shard_map/ppermute | solution.py:160
  11.5 1.1 %collective-permute-start.6 = (bf16[2,192,128]{2,1,0:T(8,128)(2,1)S(1)}, bf16[2,192,128]{2,1,0:T(8,128)(2,1)S(1)}, u32[]{:S(2)}, u32[]{:S(2)}) collective-permute-start(bf16[2,192,128]{2,1,0:T(8,128)(2,1)S(1)} %get-tuple-element.84), channel_id=1, source_target_pairs={{0,4},{1,5},{2,11},{3,10},{4,0},{5,1},{6,15},{7,14},{8,12},{9,13},... | collective-permute-start | bytes 294920 | tf_op jit(solution)/shard_map/ppermute | solution.py:160
  12.6 2.5 %collective-permute-start.7 = (bf16[2,192,128]{2,1,0:T(8,128)(2,1)S(1)}, bf16[2,192,128]{2,1,0:T(8,128)(2,1)S(1)}, u32[]{:S(2)}, u32[]{:S(2)}) collective-permute-start(bf16[2,192,128]{2,1,0:T(8,128)(2,1)S(1)} %get-tuple-element.83), channel_id=1, source_target_pairs={{0,9},{1,8},{2,6},{3,7},{4,13},{5,12},{6,2},{7,3},{8,1},{9,0},{10,... | collective-permute-start | bytes 294920 | tf_op jit(solution)/shard_map/ppermute | solution.py:160
  15.6 0.9 %collective-permute-start.9 = (bf16[2,192,128]{2,1,0:T(8,128)(2,1)S(1)}, bf16[2,192,128]{2,1,0:T(8,128)(2,1)S(1)}, u32[]{:S(2)}, u32[]{:S(2)}) collective-permute-start(bf16[2,192,128]{2,1,0:T(8,128)(2,1)S(1)} %get-tuple-element.81), channel_id=1, source_target_pairs={{0,5},{1,4},{2,10},{3,11},{4,1},{5,0},{6,14},{7,15},{8,13},{9,12},... | collective-permute-start | bytes 294920 | tf_op jit(solution)/shard_map/ppermute | solution.py:160
  16.5 1.7 %collective-permute-done.4 = bf16[2,192,128]{2,1,0:T(8,128)(2,1)S(1)} collective-permute-done((bf16[2,192,128]{2,1,0:T(8,128)(2,1)S(1)}, bf16[2,192,128]{2,1,0:T(8,128)(2,1)S(1)}, u32[]{:S(2)}, u32[]{:S(2)}) %collective-permute-start.4) | collective-permute-done | bytes 98336 | tf_op jit(solution)/shard_map/ppermute | solution.py:160
  18.7 1.1 %collective-permute-done.8 = bf16[2,192,128]{2,1,0:T(8,128)(2,1)S(1)} collective-permute-done((bf16[2,192,128]{2,1,0:T(8,128)(2,1)S(1)}, bf16[2,192,128]{2,1,0:T(8,128)(2,1)S(1)}, u32[]{:S(2)}, u32[]{:S(2)}) %collective-permute-start.8) | collective-permute-done | bytes 98336 | tf_op jit(solution)/shard_map/ppermute | solution.py:160
  19.8 1.3 %collective-permute-done.9 = bf16[2,192,128]{2,1,0:T(8,128)(2,1)S(1)} collective-permute-done((bf16[2,192,128]{2,1,0:T(8,128)(2,1)S(1)}, bf16[2,192,128]{2,1,0:T(8,128)(2,1)S(1)}, u32[]{:S(2)}, u32[]{:S(2)}) %collective-permute-start.9) | collective-permute-done | bytes 98336 | tf_op jit(solution)/shard_map/ppermute | solution.py:160
  21.2 2.7 %collective-permute-start.10 = (bf16[192,128]{1,0:T(8,128)(2,1)S(1)}, bf16[192,128]{1,0:T(8,128)(2,1)S(1)}, u32[]{:S(2)}, u32[]{:S(2)}) collective-permute-start(bf16[192,128]{1,0:T(8,128)(2,1)S(1)} %fusion.19), channel_id=1, source_target_pairs={{0,16},{16,0},{1,17},{17,1},{2,18},{18,2},{3,19},{19,3},{4,20},{20... | collective-permute-start | bytes 147464 | tf_op jit(solution)/shard_map/ppermute | solution.py:150
  24.6 1.7 %collective-permute-done.10 = bf16[192,128]{1,0:T(8,128)(2,1)S(1)} collective-permute-done((bf16[192,128]{1,0:T(8,128)(2,1)S(1)}, bf16[192,128]{1,0:T(8,128)(2,1)S(1)}, u32[]{:S(2)}, u32[]{:S(2)}) %collective-permute-start.10) | collective-permute-done | bytes 49184 | tf_op jit(solution)/shard_map/ppermute | solution.py:150
  26.4 2.7 %collective-permute-start.11 = (bf16[192,128]{1,0:T(8,128)(2,1)S(1)}, bf16[192,128]{1,0:T(8,128)(2,1)S(1)}, u32[]{:S(2)}, u32[]{:S(2)}) collective-permute-start(bf16[192,128]{1,0:T(8,128)(2,1)S(1)} %get-tuple-element.79), channel_id=1, source_target_pairs={{0,16},{16,0},{1,17},{17,1},{2,18},{18,2},{3,19},{19,3},{4,20},{20... | collective-permute-start | bytes 147464 | tf_op jit(solution)/shard_map/ppermute | solution.py:150
  29.1 1.2 %collective-permute-start.13 = (f32[192,128]{1,0:T(8,128)S(1)}, f32[192,128]{1,0:T(8,128)S(1)}, u32[]{:S(2)}, u32[]{:S(2)}) collective-permute-start(f32[192,128]{1,0:T(8,128)S(1)} %get-tuple-element.80), channel_id=1, source_target_pairs={{0,1},{1,0},{2,3},{3,2},{4,5},{5,4},{6,7},{7,6},{8,9},{9,8},{10,11... | collective-permute-start | bytes 294920 | tf_op jit(solution)/shard_map/ppermute | solution.py:150
  30.2 1.2 %collective-permute-done.11 = bf16[192,128]{1,0:T(8,128)(2,1)S(1)} collective-permute-done((bf16[192,128]{1,0:T(8,128)(2,1)S(1)}, bf16[192,128]{1,0:T(8,128)(2,1)S(1)}, u32[]{:S(2)}, u32[]{:S(2)}) %collective-permute-start.11) | collective-permute-done | bytes 49184 | tf_op jit(solution)/shard_map/ppermute | solution.py:150
  31.5 2.3 %collective-permute-start.17 = (bf16[2,192,128]{2,1,0:T(8,128)(2,1)S(1)}, bf16[2,192,128]{2,1,0:T(8,128)(2,1)S(1)}, u32[]{:S(2)}, u32[]{:S(2)}) collective-permute-start(bf16[2,192,128]{2,1,0:T(8,128)(2,1)S(1)} %get-tuple-element.88), channel_id=1, source_target_pairs={{0,13},{1,12},{2,15},{3,14},{4,9},{5,8},{6,11},{7,10},{8,5},{9,4},... | collective-permute-start | bytes 294920 | tf_op jit(solution)/shard_map/ppermute | solution.py:160
  33.8 1.4 %collective-permute-start.14 = (bf16[2,2,192,128]{3,2,1,0:T(8,128)(2,1)S(1)}, bf16[2,2,192,128]{3,2,1,0:T(8,128)(2,1)S(1)}, u32[]{:S(2)}, u32[]{:S(2)}) collective-permute-start(bf16[2,2,192,128]{3,2,1,0:T(8,128)(2,1)S(1)} %maximum_select_fusion), channel_id=1, source_target_pairs={{0,4},{1,5},{2,11},{3,10},{4,0},{5,1},{6,15},{7,14},{8,12},{9,13},... | collective-permute-start | bytes 589832 | tf_op jit(solution)/shard_map/ppermute | solution.py:160
  35.2 1.2 %collective-permute-start.15 = (bf16[2,2,192,128]{3,2,1,0:T(8,128)(2,1)S(1)}, bf16[2,2,192,128]{3,2,1,0:T(8,128)(2,1)S(1)}, u32[]{:S(2)}, u32[]{:S(2)}) collective-permute-start(bf16[2,2,192,128]{3,2,1,0:T(8,128)(2,1)S(1)} %maximum_select_fusion), channel_id=1, source_target_pairs={{0,8},{1,9},{2,7},{3,6},{4,12},{5,13},{6,3},{7,2},{8,0},{9,1},{10,... | collective-permute-start | bytes 589832 | tf_op jit(solution)/shard_map/ppermute | solution.py:160
  36.4 1.0 %collective-permute-start.16 = (bf16[2,2,192,128]{3,2,1,0:T(8,128)(2,1)S(1)}, bf16[2,2,192,128]{3,2,1,0:T(8,128)(2,1)S(1)}, u32[]{:S(2)}, u32[]{:S(2)}) collective-permute-start(bf16[2,2,192,128]{3,2,1,0:T(8,128)(2,1)S(1)} %maximum_select_fusion), channel_id=1, source_target_pairs={{0,1},{1,0},{2,14},{3,15},{4,5},{5,4},{6,10},{7,11},{8,9},{9,8},{1... | collective-permute-start | bytes 589832 | tf_op jit(solution)/shard_map/ppermute | solution.py:160
  37.4 0.9 %multiply_subtract_fusion = (f32[384,128]{1,0:T(8,128)}, f32[384,128]{1,0:T(8,128)}, f32[384,128]{1,0:T(8,128)}) fusion(f32[384,128]{1,0:T(8,128)S(1)} %copy-done, f32[]{:T(128)} %bitcast.14, f32[]{:T(128)} %bitcast.12, f32[192,128]{1,0:T(8,128)S(1)} %get-tuple-element.80, f32[192,128]{1,0:T(8,128)S(1)} %collective-permute-done.13, pred[]{:T(512)S(6)} %eq.7, ...), kind=kLoop, calls=%fused_computation.17 | loop fusion | flops 884736 | bytes 1376265 | tf_op jit(solution)/shard_map/sub | solution.py:36
  38.3 1.9 %shard_map.95 = (bf16[256,3072]{1,0:T(8,128)(2,1)S(1)}, bf16[256,3072]{1,0:T(8,128)(2,1)S(1)}) custom-call(bf16[256,6144]{1,0:T(8,128)(2,1)} %acts_ref.2), custom_call_target="tpu_custom_call" | custom-call | tf_op jit(solution)/shard_map/pallas_call | solution.py:275
  40.2 2.9 %collective-permute-done.14 = bf16[2,2,192,128]{3,2,1,0:T(8,128)(2,1)S(1)} collective-permute-done((bf16[2,2,192,128]{3,2,1,0:T(8,128)(2,1)S(1)}, bf16[2,2,192,128]{3,2,1,0:T(8,128)(2,1)S(1)}, u32[]{:S(2)}, u32[]{:S(2)}) %collective-permute-start.14) | collective-permute-done | bytes 196640 | tf_op jit(solution)/shard_map/ppermute | solution.py:160
  43.2 1.7 %collective-permute-done.16.refs_0_ = bf16[2,2,192,128]{3,2,1,0:T(8,128)(2,1)S(1)} collective-permute-done((bf16[2,2,192,128]{3,2,1,0:T(8,128)(2,1)S(1)}, bf16[2,2,192,128]{3,2,1,0:T(8,128)(2,1)S(1)}, u32[]{:S(2)}, u32[]{:S(2)}) %collective-permute-start.16) | collective-permute-done | bytes 196640 | tf_op jit(solution)/shard_map/ppermute | solution.py:160
  45.5 1.4 %collective-permute-done.19.refs_1_ = bf16[5,2,192,128]{3,2,1,0:T(8,128)(2,1)S(1)} collective-permute-done((bf16[5,2,192,128]{3,2,1,0:T(8,128)(2,1)S(1)}, bf16[5,2,192,128]{3,2,1,0:T(8,128)(2,1)S(1)}, u32[]{:S(2)}, u32[]{:S(2)}) %collective-permute-start.19) | collective-permute-done | bytes 491552 | tf_op jit(solution)/shard_map/ppermute | solution.py:150
  47.5 1.3 %shard_map.97 = bf16[256,128]{1,0:T(8,128)(2,1)} custom-call(bf16[256,3072]{1,0:T(8,128)(2,1)S(1)} %get-tuple-element.70.columns_ref, bf16[2,2,192,128]{3,2,1,0:T(8,128)(2,1)S(1)} %collective-permute-done.16.refs_0_, bf16[2,2,192,128]{3,2,1,0:T(8,128)(2,1)S(1)} %collective-permute-done.18.refs_1_, bf16[1,2,192,128]{3,2,1,0:T(8,128)(2,1)S(1)} %bitcast.69, ...), custom_call_target="tpu_custom_call" | custom-call | tf_op jit(solution)/shard_map/pallas_call | solution.py:297
  (41 shorter events, 5.8 us)
Async XLA Ops:
  2.7 1.6 %collective-permute-start = (bf16[2,2,192,128]{3,2,1,0:T(8,128)(2,1)S(1)}, bf16[2,2,192,128]{3,2,1,0:T(8,128)(2,1)S(1)}, u32[]{:S(2)}, u32[]{:S(2)}) collective-permute-start(bf16[2,2,192,128]{3,2,1,0:T(8,128)(2,1)S(1)} %get-tuple-element.42), channel_id=1, source_target_pairs={{0,2},{2,0},{1,3},{3,1},{4,6},{6,4},{5,7},{7,5},{8,10},{10,8},{9,1... | collective-permute-start | bytes 589832 | tf_op jit(solution)/shard_map/ppermute | solution.py:150
  4.3 7.0 %collective-permute-start.5 = (bf16[4,2,192,128]{3,2,1,0:T(8,128)(2,1)S(1)}, bf16[4,2,192,128]{3,2,1,0:T(8,128)(2,1)S(1)}, u32[]{:S(2)}, u32[]{:S(2)}) collective-permute-start(bf16[4,2,192,128]{3,2,1,0:T(8,128)(2,1)S(1)} %get-tuple-element.51), channel_id=1, source_target_pairs={{0,2},{2,0},{1,3},{3,1},{4,6},{6,4},{5,7},{7,5},{8,10},{10,8},{9,1... | collective-permute-start | bytes 1179656 | tf_op jit(solution)/shard_map/ppermute | solution.py:150
  4.7 5.7 %collective-permute-start.1 = (bf16[2,2,192,128]{3,2,1,0:T(8,128)(2,1)S(1)}, bf16[2,2,192,128]{3,2,1,0:T(8,128)(2,1)S(1)}, u32[]{:S(2)}, u32[]{:S(2)}) collective-permute-start(bf16[2,2,192,128]{3,2,1,0:T(8,128)(2,1)S(1)} %get-tuple-element.47), channel_id=1, source_target_pairs={{0,2},{2,0},{1,3},{3,1},{4,6},{6,4},{5,7},{7,5},{8,10},{10,8},{9,1... | collective-permute-start | bytes 589832 | tf_op jit(solution)/shard_map/ppermute | solution.py:150
  4.9 10.2 %collective-permute-start.2 = (bf16[2,192,128]{2,1,0:T(8,128)(2,1)S(1)}, bf16[2,192,128]{2,1,0:T(8,128)(2,1)S(1)}, u32[]{:S(2)}, u32[]{:S(2)}) collective-permute-start(bf16[2,192,128]{2,1,0:T(8,128)(2,1)S(1)} %get-tuple-element.86), channel_id=1, source_target_pairs={{0,1},{1,0},{2,14},{3,15},{4,5},{5,4},{6,10},{7,11},{8,9},{9,8},{1... | collective-permute-start | bytes 294920 | tf_op jit(solution)/shard_map/ppermute | solution.py:160
  7.9 7.7 %collective-permute-start.3 = (bf16[2,192,128]{2,1,0:T(8,128)(2,1)S(1)}, bf16[2,192,128]{2,1,0:T(8,128)(2,1)S(1)}, u32[]{:S(2)}, u32[]{:S(2)}) collective-permute-start(bf16[2,192,128]{2,1,0:T(8,128)(2,1)S(1)} %get-tuple-element.85), channel_id=1, source_target_pairs={{0,12},{1,13},{2,3},{3,2},{4,8},{5,9},{6,7},{7,6},{8,4},{9,5},{10,... | collective-permute-start | bytes 294920 | tf_op jit(solution)/shard_map/ppermute | solution.py:160
  10.4 7.8 %collective-permute-start.4 = (bf16[2,192,128]{2,1,0:T(8,128)(2,1)S(1)}, bf16[2,192,128]{2,1,0:T(8,128)(2,1)S(1)}, u32[]{:S(2)}, u32[]{:S(2)}) collective-permute-start(bf16[2,192,128]{2,1,0:T(8,128)(2,1)S(1)} %fusion.14), channel_id=1, source_target_pairs={{0,13},{1,12},{2,15},{3,14},{4,9},{5,8},{6,11},{7,10},{8,5},{9,4},... | collective-permute-start | bytes 294920 | tf_op jit(solution)/shard_map/ppermute | solution.py:160
  11.4 26.0 %copy-start = (f32[384,128]{1,0:T(8,128)S(1)}, f32[384,128]{1,0:T(8,128)}, u32[]{:S(2)}) copy-start(f32[384,128]{1,0:T(8,128)} %refs_0_.1) | copy-start | bytes 589828
  11.4 26.0 %copy-start.1 = (f32[384,128]{1,0:T(8,128)S(1)}, f32[384,128]{1,0:T(8,128)}, u32[]{:S(2)}) copy-start(f32[384,128]{1,0:T(8,128)} %refs_1_.1) | copy-start | bytes 589828
  11.4 26.0 %copy-start.2 = (f32[384,128]{1,0:T(8,128)S(1)}, f32[384,128]{1,0:T(8,128)}, u32[]{:S(2)}) copy-start(f32[384,128]{1,0:T(8,128)} %refs_2_.1) | copy-start | bytes 589828
  11.5 6.7 %collective-permute-start.6 = (bf16[2,192,128]{2,1,0:T(8,128)(2,1)S(1)}, bf16[2,192,128]{2,1,0:T(8,128)(2,1)S(1)}, u32[]{:S(2)}, u32[]{:S(2)}) collective-permute-start(bf16[2,192,128]{2,1,0:T(8,128)(2,1)S(1)} %get-tuple-element.84), channel_id=1, source_target_pairs={{0,4},{1,5},{2,11},{3,10},{4,0},{5,1},{6,15},{7,14},{8,12},{9,13},... | collective-permute-start | bytes 294920 | tf_op jit(solution)/shard_map/ppermute | solution.py:160
  12.6 6.1 %collective-permute-start.7 = (bf16[2,192,128]{2,1,0:T(8,128)(2,1)S(1)}, bf16[2,192,128]{2,1,0:T(8,128)(2,1)S(1)}, u32[]{:S(2)}, u32[]{:S(2)}) collective-permute-start(bf16[2,192,128]{2,1,0:T(8,128)(2,1)S(1)} %get-tuple-element.83), channel_id=1, source_target_pairs={{0,9},{1,8},{2,6},{3,7},{4,13},{5,12},{6,2},{7,3},{8,1},{9,0},{10,... | collective-permute-start | bytes 294920 | tf_op jit(solution)/shard_map/ppermute | solution.py:160
  15.1 4.7 %collective-permute-start.8 = (bf16[2,192,128]{2,1,0:T(8,128)(2,1)S(1)}, bf16[2,192,128]{2,1,0:T(8,128)(2,1)S(1)}, u32[]{:S(2)}, u32[]{:S(2)}) collective-permute-start(bf16[2,192,128]{2,1,0:T(8,128)(2,1)S(1)} %get-tuple-element.82), channel_id=1, source_target_pairs={{0,8},{1,9},{2,7},{3,6},{4,12},{5,13},{6,3},{7,2},{8,0},{9,1},{10,... | collective-permute-start | bytes 294920 | tf_op jit(solution)/shard_map/ppermute | solution.py:160
  15.6 5.5 %collective-permute-start.9 = (bf16[2,192,128]{2,1,0:T(8,128)(2,1)S(1)}, bf16[2,192,128]{2,1,0:T(8,128)(2,1)S(1)}, u32[]{:S(2)}, u32[]{:S(2)}) collective-permute-start(bf16[2,192,128]{2,1,0:T(8,128)(2,1)S(1)} %get-tuple-element.81), channel_id=1, source_target_pairs={{0,5},{1,4},{2,10},{3,11},{4,1},{5,0},{6,14},{7,15},{8,13},{9,12},... | collective-permute-start | bytes 294920 | tf_op jit(solution)/shard_map/ppermute | solution.py:160
  21.2 5.1 %collective-permute-start.10 = (bf16[192,128]{1,0:T(8,128)(2,1)S(1)}, bf16[192,128]{1,0:T(8,128)(2,1)S(1)}, u32[]{:S(2)}, u32[]{:S(2)}) collective-permute-start(bf16[192,128]{1,0:T(8,128)(2,1)S(1)} %fusion.19), channel_id=1, source_target_pairs={{0,16},{16,0},{1,17},{17,1},{2,18},{18,2},{3,19},{19,3},{4,20},{20... | collective-permute-start | bytes 147464 | tf_op jit(solution)/shard_map/ppermute | solution.py:150
  26.4 5.1 %collective-permute-start.11 = (bf16[192,128]{1,0:T(8,128)(2,1)S(1)}, bf16[192,128]{1,0:T(8,128)(2,1)S(1)}, u32[]{:S(2)}, u32[]{:S(2)}) collective-permute-start(bf16[192,128]{1,0:T(8,128)(2,1)S(1)} %get-tuple-element.79), channel_id=1, source_target_pairs={{0,16},{16,0},{1,17},{17,1},{2,18},{18,2},{3,19},{19,3},{4,20},{20... | collective-permute-start | bytes 147464 | tf_op jit(solution)/shard_map/ppermute | solution.py:150
  29.1 4.7 %collective-permute-start.13 = (f32[192,128]{1,0:T(8,128)S(1)}, f32[192,128]{1,0:T(8,128)S(1)}, u32[]{:S(2)}, u32[]{:S(2)}) collective-permute-start(f32[192,128]{1,0:T(8,128)S(1)} %get-tuple-element.80), channel_id=1, source_target_pairs={{0,1},{1,0},{2,3},{3,2},{4,5},{5,4},{6,7},{7,6},{8,9},{9,8},{10,11... | collective-permute-start | bytes 294920 | tf_op jit(solution)/shard_map/ppermute | solution.py:150
  31.4 2.4 %collective-permute-start.12 = (bf16[2,192,128]{2,1,0:T(8,128)(2,1)S(1)}, bf16[2,192,128]{2,1,0:T(8,128)(2,1)S(1)}, u32[]{:S(2)}, u32[]{:S(2)}) collective-permute-start(bf16[2,192,128]{2,1,0:T(8,128)(2,1)S(1)} %get-tuple-element.88), channel_id=1, source_target_pairs={{0,2},{2,0},{1,3},{3,1},{4,6},{6,4},{5,7},{7,5},{8,10},{10,8},{9,1... | collective-permute-start | bytes 294920 | tf_op jit(solution)/shard_map/ppermute | solution.py:150
  31.5 8.7 %collective-permute-start.17 = (bf16[2,192,128]{2,1,0:T(8,128)(2,1)S(1)}, bf16[2,192,128]{2,1,0:T(8,128)(2,1)S(1)}, u32[]{:S(2)}, u32[]{:S(2)}) collective-permute-start(bf16[2,192,128]{2,1,0:T(8,128)(2,1)S(1)} %get-tuple-element.88), channel_id=1, source_target_pairs={{0,13},{1,12},{2,15},{3,14},{4,9},{5,8},{6,11},{7,10},{8,5},{9,4},... | collective-permute-start | bytes 294920 | tf_op jit(solution)/shard_map/ppermute | solution.py:160
  33.8 9.3 %collective-permute-start.14 = (bf16[2,2,192,128]{3,2,1,0:T(8,128)(2,1)S(1)}, bf16[2,2,192,128]{3,2,1,0:T(8,128)(2,1)S(1)}, u32[]{:S(2)}, u32[]{:S(2)}) collective-permute-start(bf16[2,2,192,128]{3,2,1,0:T(8,128)(2,1)S(1)} %maximum_select_fusion), channel_id=1, source_target_pairs={{0,4},{1,5},{2,11},{3,10},{4,0},{5,1},{6,15},{7,14},{8,12},{9,13},... | collective-permute-start | bytes 589832 | tf_op jit(solution)/shard_map/ppermute | solution.py:160
  35.2 7.9 %collective-permute-start.15 = (bf16[2,2,192,128]{3,2,1,0:T(8,128)(2,1)S(1)}, bf16[2,2,192,128]{3,2,1,0:T(8,128)(2,1)S(1)}, u32[]{:S(2)}, u32[]{:S(2)}) collective-permute-start(bf16[2,2,192,128]{3,2,1,0:T(8,128)(2,1)S(1)} %maximum_select_fusion), channel_id=1, source_target_pairs={{0,8},{1,9},{2,7},{3,6},{4,12},{5,13},{6,3},{7,2},{8,0},{9,1},{10,... | collective-permute-start | bytes 589832 | tf_op jit(solution)/shard_map/ppermute | solution.py:160
  36.4 8.5 %collective-permute-start.16 = (bf16[2,2,192,128]{3,2,1,0:T(8,128)(2,1)S(1)}, bf16[2,2,192,128]{3,2,1,0:T(8,128)(2,1)S(1)}, u32[]{:S(2)}, u32[]{:S(2)}) collective-permute-start(bf16[2,2,192,128]{3,2,1,0:T(8,128)(2,1)S(1)} %maximum_select_fusion), channel_id=1, source_target_pairs={{0,1},{1,0},{2,14},{3,15},{4,5},{5,4},{6,10},{7,11},{8,9},{9,8},{1... | collective-permute-start | bytes 589832 | tf_op jit(solution)/shard_map/ppermute | solution.py:160
  44.9 1.9 %collective-permute-start.19 = (bf16[5,2,192,128]{3,2,1,0:T(8,128)(2,1)S(1)}, bf16[5,2,192,128]{3,2,1,0:T(8,128)(2,1)S(1)}, u32[]{:S(2)}, u32[]{:S(2)}) collective-permute-start(bf16[5,2,192,128]{3,2,1,0:T(8,128)(2,1)S(1)} %pad_maximum_fusion.refs_0_), channel_id=1, source_target_pairs={{0,2},{2,0},{1,3},{3,1},{4,6},{6,4},{5,7},{7,5},{8,10},{10,8},{9,1... | collective-permute-start | bytes 1474568 | tf_op jit(solution)/shard_map/ppermute | solution.py:150
  45.0 2.5 %collective-permute-start.18 = (bf16[2,2,192,128]{3,2,1,0:T(8,128)(2,1)S(1)}, bf16[2,2,192,128]{3,2,1,0:T(8,128)(2,1)S(1)}, u32[]{:S(2)}, u32[]{:S(2)}) collective-permute-start(bf16[2,2,192,128]{3,2,1,0:T(8,128)(2,1)S(1)} %collective-permute-done.16.refs_0_), channel_id=1, source_target_pairs={{0,2},{2,0},{1,3},{3,1},{4,6},{6,4},{5,7},{7,5},{8,10},{10,8},{9,1... | collective-permute-start | bytes 589832 | tf_op jit(solution)/shard_map/ppermute | solution.py:150

commit v25 on v21

--- a/solution.py
+++ b/solution.py
@@ -240,13 +240,16 @@
             away, kept = sort_rows(1 - core), sort_rows(core)
             mine = jnp.stack([lax.dynamic_slice_in_dim(x, rep * half, half, 0) for x in state_in])
 
-        arrived = swap(away[0], "core")
-        arrived, *rest = lax.optimization_barrier((arrived, *away[1:]))
-        arrived = [arrived] + [swap(x, "core") for x in rest]
+        arrived = swap(away[1], "core")
+        arrived, *rest = lax.optimization_barrier((arrived, away[0], away[2]))
+        arrived = [swap(rest[0], "core"), arrived, swap(rest[1], "core")]
         pair, left, first = [own.astype(f32) + x.astype(f32) for own, x in zip(kept, arrived)]
+        corner = cube_swap(left[0].astype(bf16), lambda core: (1, 0)).astype(f32)
         parts = [to_slot(x.astype(bf16), 4 + n) for n, x in enumerate(pair)]
-        parts += [to_slot(left[0].astype(bf16), 6)]
-        parts += [to_slot(x.astype(bf16), n) for n, x in enumerate(first)]
+        parts += [to_slot(first[n].astype(bf16), n) for n in (2, 3)]
+        for n in range(2):
+            part = first[n] + jnp.where(core == 1 - n, corner, 0.0)
+            parts.append(to_slot(part.astype(bf16), n))
         parts = [left[1], *lax.optimization_barrier(parts)]
         total = sum(x.astype(f32) for x in parts)
 

time: 48 us -> 48.6 us (1.012)
  waiting for transfers between devices: 13.1 us -> 13.9 us
  starting transfers between devices: 25.2 us -> 24.7 us
    ppermute x9, waiting for transfers between devices: 4.28 us -> 5.1 us  [swap(): lax.ppermute(x, axis, [(i, i ^ mask) for i in range(fine.shape[axis])])]
    ppermute x9, starting transfers between devices: 8.06 us -> 7.57 us  [swap(): lax.ppermute(x, axis, [(i, i ^ mask) for i in range(fine.shape[axis])])]
  transfers between devices with their start and end apart: 20 -> 20, of which waited for: 10 -> 14; matrix products, arithmetic and copies ran while one was open for 3% -> 3% of each run, Pallas kernels for 7% -> 6%
where the time goes in v25:
time: 48.6 us; the launch traced here: 48 us
  starting transfers between devices  24.7 us (51%)
  waiting for transfers between devices  13.9 us (29%)
  Pallas kernels  6.44 us (13%)
  between operations  1.54 us (3%)
  other arithmetic  1.4 us (3%)
    ppermute x11, starting transfers between devices, cube_swap(): return lax.ppermute(x, AXES[1:], pairs)  17.1 us
    ppermute x11, waiting for transfers between devices, cube_swap(): return lax.ppermute(x, AXES[1:], pairs)  8.76 us
    ppermute x9, starting transfers between devices, swap(): lax.ppermute(x, axis, [(i, i ^ mask) for i in range(fine.shape[axis])])  7.57 us
    ppermute x9, waiting for transfers between devices, swap(): lax.ppermute(x, axis, [(i, i ^ mask) for i in range(fine.shape[axis])])  5.1 us
    pallas_call x1, Pallas kernels, per_device(): pl.pallas_call(functools.partial(first_grad_kernel, n_high), out_shape=[p...  2.07 us
    pallas_call x1, Pallas kernels, per_device(): pl.pallas_call(functools.partial(columns_kernel, n_high, 4 * half), out_s...  1.91 us
    pallas_call x2, Pallas kernels, per_device(): pl.pallas_call(functools.partial(logits_kernel, n_high, group), out_shape...  1.89 us
  transfers between devices with their start and end apart: 20, of which 14 were waited for; matrix products, arithmetic and copies ran while one was open for 3% of the time, Pallas kernels for 6%

profile of v25, /device:TPU:0, one launch (start us, length us, event | category | flops | bytes accessed | tf_op | source)
XLA Modules:
  0.0 48.0 jit_solution(1790529786745930094)
XLA Ops:
  0.6 2.1 %shard_map.93 = (bf16[2,2,192,128]{3,2,1,0:T(8,128)(2,1)S(1)}, bf16[2,2,192,128]{3,2,1,0:T(8,128)(2,1)S(1)}, bf16[2,2,192,128]{3,2,1,0:T(8,128)(2,1)S(1)}, bf16[...) custom-call(bf16[256,6144]{1,0:T(8,128)(2,1)} %acts_ref.2, ...), custom_call_target="tpu_custom_call" | custom-call | tf_op jit(solution)/shard_map/pallas_call | solution.py:193
  4.9 2.9 %collective-permute-start.7 = (bf16[2,192,128]{2,1,0:T(8,128)(2,1)S(1)}, bf16[2,192,128]{2,1,0:T(8,128)(2,1)S(1)}, u32[]{:S(2)}, u32[]{:S(2)}) collective-permute-start(bf16[2,192,128]{2,1,0:T(8,128)(2,1)S(1)} %fusion.17), channel_id=1, source_target_pairs={{0,4},{1,5},{2,6},{3,7},{4,0},{5,1},{6,2},{7,3},{8,12},{9,13},{10,... | collective-permute-start | bytes 294920 | tf_op jit(solution)/shard_map/ppermute | solution.py:161
  7.9 1.6 %collective-permute-start.2 = (bf16[2,192,128]{2,1,0:T(8,128)(2,1)S(1)}, bf16[2,192,128]{2,1,0:T(8,128)(2,1)S(1)}, u32[]{:S(2)}, u32[]{:S(2)}) collective-permute-start(bf16[2,192,128]{2,1,0:T(8,128)(2,1)S(1)} %get-tuple-element.82), channel_id=1, source_target_pairs={{0,1},{1,0},{2,14},{3,15},{4,5},{5,4},{6,10},{7,11},{8,9},{9,8},{1... | collective-permute-start | bytes 294920 | tf_op jit(solution)/shard_map/ppermute | solution.py:161
  9.5 2.4 %collective-permute-start.3 = (bf16[2,192,128]{2,1,0:T(8,128)(2,1)S(1)}, bf16[2,192,128]{2,1,0:T(8,128)(2,1)S(1)}, u32[]{:S(2)}, u32[]{:S(2)}) collective-permute-start(bf16[2,192,128]{2,1,0:T(8,128)(2,1)S(1)} %get-tuple-element.81), channel_id=1, source_target_pairs={{0,12},{1,13},{2,3},{3,2},{4,8},{5,9},{6,7},{7,6},{8,4},{9,5},{10,... | collective-permute-start | bytes 294920 | tf_op jit(solution)/shard_map/ppermute | solution.py:161
  12.1 0.7 %collective-permute-start.8 = (bf16[2,192,128]{2,1,0:T(8,128)(2,1)S(1)}, bf16[2,192,128]{2,1,0:T(8,128)(2,1)S(1)}, u32[]{:S(2)}, u32[]{:S(2)}) collective-permute-start(bf16[2,192,128]{2,1,0:T(8,128)(2,1)S(1)} %get-tuple-element.76), channel_id=1, source_target_pairs={{0,4},{1,5},{2,11},{3,10},{4,0},{5,1},{6,15},{7,14},{8,12},{9,13},... | collective-permute-start | bytes 294920 | tf_op jit(solution)/shard_map/ppermute | solution.py:161
  12.8 2.5 %collective-permute-start.9 = (bf16[2,192,128]{2,1,0:T(8,128)(2,1)S(1)}, bf16[2,192,128]{2,1,0:T(8,128)(2,1)S(1)}, u32[]{:S(2)}, u32[]{:S(2)}) collective-permute-start(bf16[2,192,128]{2,1,0:T(8,128)(2,1)S(1)} %get-tuple-element.75), channel_id=1, source_target_pairs={{0,9},{1,8},{2,6},{3,7},{4,13},{5,12},{6,2},{7,3},{8,1},{9,0},{10,... | collective-permute-start | bytes 294920 | tf_op jit(solution)/shard_map/ppermute | solution.py:161
  15.8 1.3 %collective-permute-start.6 = (bf16[2,192,128]{2,1,0:T(8,128)(2,1)S(1)}, bf16[2,192,128]{2,1,0:T(8,128)(2,1)S(1)}, u32[]{:S(2)}, u32[]{:S(2)}) collective-permute-start(bf16[2,192,128]{2,1,0:T(8,128)(2,1)S(1)} %get-tuple-element.79), channel_id=1, source_target_pairs={{0,5},{1,4},{2,10},{3,11},{4,1},{5,0},{6,14},{7,15},{8,13},{9,12},... | collective-permute-start | bytes 294920 | tf_op jit(solution)/shard_map/ppermute | solution.py:161
  17.8 1.6 %collective-permute-done.9 = bf16[2,192,128]{2,1,0:T(8,128)(2,1)S(1)} collective-permute-done((bf16[2,192,128]{2,1,0:T(8,128)(2,1)S(1)}, bf16[2,192,128]{2,1,0:T(8,128)(2,1)S(1)}, u32[]{:S(2)}, u32[]{:S(2)}) %collective-permute-start.9) | collective-permute-done | bytes 98336 | tf_op jit(solution)/shard_map/ppermute | solution.py:161
  19.4 0.7 %collective-permute-done.5 = bf16[2,192,128]{2,1,0:T(8,128)(2,1)S(1)} collective-permute-done((bf16[2,192,128]{2,1,0:T(8,128)(2,1)S(1)}, bf16[2,192,128]{2,1,0:T(8,128)(2,1)S(1)}, u32[]{:S(2)}, u32[]{:S(2)}) %collective-permute-start.5) | collective-permute-done | bytes 98336 | tf_op jit(solution)/shard_map/ppermute | solution.py:161
  20.1 1.3 %collective-permute-done.6 = bf16[2,192,128]{2,1,0:T(8,128)(2,1)S(1)} collective-permute-done((bf16[2,192,128]{2,1,0:T(8,128)(2,1)S(1)}, bf16[2,192,128]{2,1,0:T(8,128)(2,1)S(1)}, u32[]{:S(2)}, u32[]{:S(2)}) %collective-permute-start.6) | collective-permute-done | bytes 98336 | tf_op jit(solution)/shard_map/ppermute | solution.py:161
  21.5 2.7 %collective-permute-start.10 = (bf16[192,128]{1,0:T(8,128)(2,1)S(1)}, bf16[192,128]{1,0:T(8,128)(2,1)S(1)}, u32[]{:S(2)}, u32[]{:S(2)}) collective-permute-start(bf16[192,128]{1,0:T(8,128)(2,1)S(1)} %fusion.22), channel_id=1, source_target_pairs={{0,16},{16,0},{1,17},{17,1},{2,18},{18,2},{3,19},{19,3},{4,20},{20... | collective-permute-start | bytes 147464 | tf_op jit(solution)/shard_map/ppermute | solution.py:151
  24.8 1.7 %collective-permute-done.10 = bf16[192,128]{1,0:T(8,128)(2,1)S(1)} collective-permute-done((bf16[192,128]{1,0:T(8,128)(2,1)S(1)}, bf16[192,128]{1,0:T(8,128)(2,1)S(1)}, u32[]{:S(2)}, u32[]{:S(2)}) %collective-permute-start.10) | collective-permute-done | bytes 49184 | tf_op jit(solution)/shard_map/ppermute | solution.py:151
  26.6 2.7 %collective-permute-start.11 = (bf16[192,128]{1,0:T(8,128)(2,1)S(1)}, bf16[192,128]{1,0:T(8,128)(2,1)S(1)}, u32[]{:S(2)}, u32[]{:S(2)}) collective-permute-start(bf16[192,128]{1,0:T(8,128)(2,1)S(1)} %get-tuple-element.73), channel_id=1, source_target_pairs={{0,16},{16,0},{1,17},{17,1},{2,18},{18,2},{3,19},{19,3},{4,20},{20... | collective-permute-start | bytes 147464 | tf_op jit(solution)/shard_map/ppermute | solution.py:151
  29.9 1.8 %collective-permute-done.11 = bf16[192,128]{1,0:T(8,128)(2,1)S(1)} collective-permute-done((bf16[192,128]{1,0:T(8,128)(2,1)S(1)}, bf16[192,128]{1,0:T(8,128)(2,1)S(1)}, u32[]{:S(2)}, u32[]{:S(2)}) %collective-permute-start.11) | collective-permute-done | bytes 49184 | tf_op jit(solution)/shard_map/ppermute | solution.py:151
  31.8 1.9 %collective-permute-start.15 = (bf16[2,192,128]{2,1,0:T(8,128)(2,1)S(1)}, bf16[2,192,128]{2,1,0:T(8,128)(2,1)S(1)}, u32[]{:S(2)}, u32[]{:S(2)}) collective-permute-start(bf16[2,192,128]{2,1,0:T(8,128)(2,1)S(1)} %get-tuple-element.84), channel_id=1, source_target_pairs={{0,13},{1,12},{2,15},{3,14},{4,9},{5,8},{6,11},{7,10},{8,5},{9,4},... | collective-permute-start | bytes 294920 | tf_op jit(solution)/shard_map/ppermute | solution.py:161
  34.0 1.1 %collective-permute-start.14 = (bf16[2,2,192,128]{3,2,1,0:T(8,128)(2,1)S(1)}, bf16[2,2,192,128]{3,2,1,0:T(8,128)(2,1)S(1)}, u32[]{:S(2)}, u32[]{:S(2)}) collective-permute-start(bf16[2,2,192,128]{3,2,1,0:T(8,128)(2,1)S(1)} %maximum_select_fusion), channel_id=1, source_target_pairs={{0,4},{1,5},{2,11},{3,10},{4,0},{5,1},{6,15},{7,14},{8,12},{9,13},... | collective-permute-start | bytes 589832 | tf_op jit(solution)/shard_map/ppermute | solution.py:161
  35.1 1.6 %collective-permute-start.18 = (bf16[2,2,192,128]{3,2,1,0:T(8,128)(2,1)S(1)}, bf16[2,2,192,128]{3,2,1,0:T(8,128)(2,1)S(1)}, u32[]{:S(2)}, u32[]{:S(2)}) collective-permute-start(bf16[2,2,192,128]{3,2,1,0:T(8,128)(2,1)S(1)} %maximum_select_fusion), channel_id=1, source_target_pairs={{0,8},{1,9},{2,7},{3,6},{4,12},{5,13},{6,3},{7,2},{8,0},{9,1},{10,... | collective-permute-start | bytes 589832 | tf_op jit(solution)/shard_map/ppermute | solution.py:161
  37.2 0.9 %multiply_subtract_fusion = (f32[384,128]{1,0:T(8,128)}, f32[384,128]{1,0:T(8,128)}, f32[384,128]{1,0:T(8,128)}) fusion(f32[384,128]{1,0:T(8,128)S(1)} %copy-done, f32[]{:T(128)} %bitcast.14, f32[]{:T(128)} %bitcast.12, f32[192,128]{1,0:T(8,128)S(1)} %get-tuple-element.74, f32[192,128]{1,0:T(8,128)S(1)} %collective-permute-done.13, pred[]{:T(512)S(6)} %eq.12, ...), kind=kLoop, calls=%fused_computation.24 | loop fusion | flops 884736 | bytes 1376265 | tf_op jit(solution)/shard_map/sub | solution.py:36
  38.1 1.9 %shard_map.95 = (bf16[256,3072]{1,0:T(8,128)(2,1)S(1)}, bf16[256,3072]{1,0:T(8,128)(2,1)S(1)}) custom-call(bf16[256,6144]{1,0:T(8,128)(2,1)} %acts_ref.2), custom_call_target="tpu_custom_call" | custom-call | tf_op jit(solution)/shard_map/pallas_call | solution.py:279
  40.2 1.6 %collective-permute-done.14 = bf16[2,2,192,128]{3,2,1,0:T(8,128)(2,1)S(1)} collective-permute-done((bf16[2,2,192,128]{3,2,1,0:T(8,128)(2,1)S(1)}, bf16[2,2,192,128]{3,2,1,0:T(8,128)(2,1)S(1)}, u32[]{:S(2)}, u32[]{:S(2)}) %collective-permute-start.14) | collective-permute-done | bytes 196640 | tf_op jit(solution)/shard_map/ppermute | solution.py:161
  41.8 1.6 %collective-permute-done.18 = bf16[2,2,192,128]{3,2,1,0:T(8,128)(2,1)S(1)} collective-permute-done((bf16[2,2,192,128]{3,2,1,0:T(8,128)(2,1)S(1)}, bf16[2,2,192,128]{3,2,1,0:T(8,128)(2,1)S(1)}, u32[]{:S(2)}, u32[]{:S(2)}) %collective-permute-start.18) | collective-permute-done | bytes 196640 | tf_op jit(solution)/shard_map/ppermute | solution.py:161
  44.0 1.1 %collective-permute-done.16 = bf16[2,2,192,128]{3,2,1,0:T(8,128)(2,1)S(1)} collective-permute-done((bf16[2,2,192,128]{3,2,1,0:T(8,128)(2,1)S(1)}, bf16[2,2,192,128]{3,2,1,0:T(8,128)(2,1)S(1)}, u32[]{:S(2)}, u32[]{:S(2)}) %collective-permute-start.16) | collective-permute-done | bytes 196640 | tf_op jit(solution)/shard_map/ppermute | solution.py:161
  45.9 0.8 %collective-permute-done.17.refs_1_ = bf16[3,2,192,128]{3,2,1,0:T(8,128)(2,1)S(1)} collective-permute-done((bf16[3,2,192,128]{3,2,1,0:T(8,128)(2,1)S(1)}, bf16[3,2,192,128]{3,2,1,0:T(8,128)(2,1)S(1)}, u32[]{:S(2)}, u32[]{:S(2)}) %collective-permute-start.17) | collective-permute-done | bytes 294944 | tf_op jit(solution)/shard_map/ppermute | solution.py:151
  46.8 1.3 %shard_map.97 = bf16[256,128]{1,0:T(8,128)(2,1)} custom-call(bf16[256,3072]{1,0:T(8,128)(2,1)S(1)} %get-tuple-element.66.columns_ref, bf16[3,2,192,128]{3,2,1,0:T(8,128)(2,1)S(1)} %pad_maximum_fusion.refs_0_, bf16[3,2,192,128]{3,2,1,0:T(8,128)(2,1)S(1)} %collective-permute-done.17.refs_1_, bf16[1,2,192,128]{3,2,1,0:T(8,128)(2,1)S(1)} %get-tuple-element.83.refs_2_, ...), custom_call_target="tpu_custom_call" | custom-call | tf_op jit(solution)/shard_map/pallas_call | solution.py:299
  (43 shorter events, 6.7 us)
Async XLA Ops:
  2.7 1.6 %collective-permute-start = (bf16[2,2,192,128]{3,2,1,0:T(8,128)(2,1)S(1)}, bf16[2,2,192,128]{3,2,1,0:T(8,128)(2,1)S(1)}, u32[]{:S(2)}, u32[]{:S(2)}) collective-permute-start(bf16[2,2,192,128]{3,2,1,0:T(8,128)(2,1)S(1)} %get-tuple-element.39), channel_id=1, source_target_pairs={{0,2},{2,0},{1,3},{3,1},{4,6},{6,4},{5,7},{7,5},{8,10},{10,8},{9,1... | collective-permute-start | bytes 589832 | tf_op jit(solution)/shard_map/ppermute | solution.py:151
  4.3 7.5 %collective-permute-start.4 = (bf16[4,2,192,128]{3,2,1,0:T(8,128)(2,1)S(1)}, bf16[4,2,192,128]{3,2,1,0:T(8,128)(2,1)S(1)}, u32[]{:S(2)}, u32[]{:S(2)}) collective-permute-start(bf16[4,2,192,128]{3,2,1,0:T(8,128)(2,1)S(1)} %get-tuple-element.48), channel_id=1, source_target_pairs={{0,2},{2,0},{1,3},{3,1},{4,6},{6,4},{5,7},{7,5},{8,10},{10,8},{9,1... | collective-permute-start | bytes 1179656 | tf_op jit(solution)/shard_map/ppermute | solution.py:151
  4.7 3.1 %collective-permute-start.1 = (bf16[2,2,192,128]{3,2,1,0:T(8,128)(2,1)S(1)}, bf16[2,2,192,128]{3,2,1,0:T(8,128)(2,1)S(1)}, u32[]{:S(2)}, u32[]{:S(2)}) collective-permute-start(bf16[2,2,192,128]{3,2,1,0:T(8,128)(2,1)S(1)} %get-tuple-element.46), channel_id=1, source_target_pairs={{0,2},{2,0},{1,3},{3,1},{4,6},{6,4},{5,7},{7,5},{8,10},{10,8},{9,1... | collective-permute-start | bytes 589832 | tf_op jit(solution)/shard_map/ppermute | solution.py:151
  4.9 7.1 %collective-permute-start.7 = (bf16[2,192,128]{2,1,0:T(8,128)(2,1)S(1)}, bf16[2,192,128]{2,1,0:T(8,128)(2,1)S(1)}, u32[]{:S(2)}, u32[]{:S(2)}) collective-permute-start(bf16[2,192,128]{2,1,0:T(8,128)(2,1)S(1)} %fusion.17), channel_id=1, source_target_pairs={{0,4},{1,5},{2,6},{3,7},{4,0},{5,1},{6,2},{7,3},{8,12},{9,13},{10,... | collective-permute-start | bytes 294920 | tf_op jit(solution)/shard_map/ppermute | solution.py:161
  7.9 8.0 %collective-permute-start.2 = (bf16[2,192,128]{2,1,0:T(8,128)(2,1)S(1)}, bf16[2,192,128]{2,1,0:T(8,128)(2,1)S(1)}, u32[]{:S(2)}, u32[]{:S(2)}) collective-permute-start(bf16[2,192,128]{2,1,0:T(8,128)(2,1)S(1)} %get-tuple-element.82), channel_id=1, source_target_pairs={{0,1},{1,0},{2,14},{3,15},{4,5},{5,4},{6,10},{7,11},{8,9},{9,8},{1... | collective-permute-start | bytes 294920 | tf_op jit(solution)/shard_map/ppermute | solution.py:161
  9.5 7.7 %collective-permute-start.3 = (bf16[2,192,128]{2,1,0:T(8,128)(2,1)S(1)}, bf16[2,192,128]{2,1,0:T(8,128)(2,1)S(1)}, u32[]{:S(2)}, u32[]{:S(2)}) collective-permute-start(bf16[2,192,128]{2,1,0:T(8,128)(2,1)S(1)} %get-tuple-element.81), channel_id=1, source_target_pairs={{0,12},{1,13},{2,3},{3,2},{4,8},{5,9},{6,7},{7,6},{8,4},{9,5},{10,... | collective-permute-start | bytes 294920 | tf_op jit(solution)/shard_map/ppermute | solution.py:161
  12.0 25.2 %copy-start = (f32[384,128]{1,0:T(8,128)S(1)}, f32[384,128]{1,0:T(8,128)}, u32[]{:S(2)}) copy-start(f32[384,128]{1,0:T(8,128)} %refs_0_.1) | copy-start | bytes 589828
  12.0 25.2 %copy-start.1 = (f32[384,128]{1,0:T(8,128)S(1)}, f32[384,128]{1,0:T(8,128)}, u32[]{:S(2)}) copy-start(f32[384,128]{1,0:T(8,128)} %refs_1_.1) | copy-start | bytes 589828
  12.0 25.2 %copy-start.2 = (f32[384,128]{1,0:T(8,128)S(1)}, f32[384,128]{1,0:T(8,128)}, u32[]{:S(2)}) copy-start(f32[384,128]{1,0:T(8,128)} %refs_2_.1) | copy-start | bytes 589828
  12.1 5.7 %collective-permute-start.8 = (bf16[2,192,128]{2,1,0:T(8,128)(2,1)S(1)}, bf16[2,192,128]{2,1,0:T(8,128)(2,1)S(1)}, u32[]{:S(2)}, u32[]{:S(2)}) collective-permute-start(bf16[2,192,128]{2,1,0:T(8,128)(2,1)S(1)} %get-tuple-element.76), channel_id=1, source_target_pairs={{0,4},{1,5},{2,11},{3,10},{4,0},{5,1},{6,15},{7,14},{8,12},{9,13},... | collective-permute-start | bytes 294920 | tf_op jit(solution)/shard_map/ppermute | solution.py:161
  12.8 6.6 %collective-permute-start.9 = (bf16[2,192,128]{2,1,0:T(8,128)(2,1)S(1)}, bf16[2,192,128]{2,1,0:T(8,128)(2,1)S(1)}, u32[]{:S(2)}, u32[]{:S(2)}) collective-permute-start(bf16[2,192,128]{2,1,0:T(8,128)(2,1)S(1)} %get-tuple-element.75), channel_id=1, source_target_pairs={{0,9},{1,8},{2,6},{3,7},{4,13},{5,12},{6,2},{7,3},{8,1},{9,0},{10,... | collective-permute-start | bytes 294920 | tf_op jit(solution)/shard_map/ppermute | solution.py:161
  15.3 4.8 %collective-permute-start.5 = (bf16[2,192,128]{2,1,0:T(8,128)(2,1)S(1)}, bf16[2,192,128]{2,1,0:T(8,128)(2,1)S(1)}, u32[]{:S(2)}, u32[]{:S(2)}) collective-permute-start(bf16[2,192,128]{2,1,0:T(8,128)(2,1)S(1)} %get-tuple-element.80), channel_id=1, source_target_pairs={{0,8},{1,9},{2,7},{3,6},{4,12},{5,13},{6,3},{7,2},{8,0},{9,1},{10,... | collective-permute-start | bytes 294920 | tf_op jit(solution)/shard_map/ppermute | solution.py:161
  15.8 5.5 %collective-permute-start.6 = (bf16[2,192,128]{2,1,0:T(8,128)(2,1)S(1)}, bf16[2,192,128]{2,1,0:T(8,128)(2,1)S(1)}, u32[]{:S(2)}, u32[]{:S(2)}) collective-permute-start(bf16[2,192,128]{2,1,0:T(8,128)(2,1)S(1)} %get-tuple-element.79), channel_id=1, source_target_pairs={{0,5},{1,4},{2,10},{3,11},{4,1},{5,0},{6,14},{7,15},{8,13},{9,12},... | collective-permute-start | bytes 294920 | tf_op jit(solution)/shard_map/ppermute | solution.py:161
  21.5 5.1 %collective-permute-start.10 = (bf16[192,128]{1,0:T(8,128)(2,1)S(1)}, bf16[192,128]{1,0:T(8,128)(2,1)S(1)}, u32[]{:S(2)}, u32[]{:S(2)}) collective-permute-start(bf16[192,128]{1,0:T(8,128)(2,1)S(1)} %fusion.22), channel_id=1, source_target_pairs={{0,16},{16,0},{1,17},{17,1},{2,18},{18,2},{3,19},{19,3},{4,20},{20... | collective-permute-start | bytes 147464 | tf_op jit(solution)/shard_map/ppermute | solution.py:151
  26.6 5.1 %collective-permute-start.11 = (bf16[192,128]{1,0:T(8,128)(2,1)S(1)}, bf16[192,128]{1,0:T(8,128)(2,1)S(1)}, u32[]{:S(2)}, u32[]{:S(2)}) collective-permute-start(bf16[192,128]{1,0:T(8,128)(2,1)S(1)} %get-tuple-element.73), channel_id=1, source_target_pairs={{0,16},{16,0},{1,17},{17,1},{2,18},{18,2},{3,19},{19,3},{4,20},{20... | collective-permute-start | bytes 147464 | tf_op jit(solution)/shard_map/ppermute | solution.py:151
  29.3 4.6 %collective-permute-start.13 = (f32[192,128]{1,0:T(8,128)S(1)}, f32[192,128]{1,0:T(8,128)S(1)}, u32[]{:S(2)}, u32[]{:S(2)}) collective-permute-start(f32[192,128]{1,0:T(8,128)S(1)} %get-tuple-element.74), channel_id=1, source_target_pairs={{0,1},{1,0},{2,3},{3,2},{4,5},{5,4},{6,7},{7,6},{8,9},{9,8},{10,11... | collective-permute-start | bytes 294920 | tf_op jit(solution)/shard_map/ppermute | solution.py:151
  31.7 2.2 %collective-permute-start.12 = (bf16[2,192,128]{2,1,0:T(8,128)(2,1)S(1)}, bf16[2,192,128]{2,1,0:T(8,128)(2,1)S(1)}, u32[]{:S(2)}, u32[]{:S(2)}) collective-permute-start(bf16[2,192,128]{2,1,0:T(8,128)(2,1)S(1)} %get-tuple-element.84), channel_id=1, source_target_pairs={{0,2},{2,0},{1,3},{3,1},{4,6},{6,4},{5,7},{7,5},{8,10},{10,8},{9,1... | collective-permute-start | bytes 294920 | tf_op jit(solution)/shard_map/ppermute | solution.py:151
  31.8 8.5 %collective-permute-start.15 = (bf16[2,192,128]{2,1,0:T(8,128)(2,1)S(1)}, bf16[2,192,128]{2,1,0:T(8,128)(2,1)S(1)}, u32[]{:S(2)}, u32[]{:S(2)}) collective-permute-start(bf16[2,192,128]{2,1,0:T(8,128)(2,1)S(1)} %get-tuple-element.84), channel_id=1, source_target_pairs={{0,13},{1,12},{2,15},{3,14},{4,9},{5,8},{6,11},{7,10},{8,5},{9,4},... | collective-permute-start | bytes 294920 | tf_op jit(solution)/shard_map/ppermute | solution.py:161
  34.0 7.9 %collective-permute-start.14 = (bf16[2,2,192,128]{3,2,1,0:T(8,128)(2,1)S(1)}, bf16[2,2,192,128]{3,2,1,0:T(8,128)(2,1)S(1)}, u32[]{:S(2)}, u32[]{:S(2)}) collective-permute-start(bf16[2,2,192,128]{3,2,1,0:T(8,128)(2,1)S(1)} %maximum_select_fusion), channel_id=1, source_target_pairs={{0,4},{1,5},{2,11},{3,10},{4,0},{5,1},{6,15},{7,14},{8,12},{9,13},... | collective-permute-start | bytes 589832 | tf_op jit(solution)/shard_map/ppermute | solution.py:161
  35.1 8.4 %collective-permute-start.18 = (bf16[2,2,192,128]{3,2,1,0:T(8,128)(2,1)S(1)}, bf16[2,2,192,128]{3,2,1,0:T(8,128)(2,1)S(1)}, u32[]{:S(2)}, u32[]{:S(2)}) collective-permute-start(bf16[2,2,192,128]{3,2,1,0:T(8,128)(2,1)S(1)} %maximum_select_fusion), channel_id=1, source_target_pairs={{0,8},{1,9},{2,7},{3,6},{4,12},{5,13},{6,3},{7,2},{8,0},{9,1},{10,... | collective-permute-start | bytes 589832 | tf_op jit(solution)/shard_map/ppermute | solution.py:161
  36.7 8.4 %collective-permute-start.16 = (bf16[2,2,192,128]{3,2,1,0:T(8,128)(2,1)S(1)}, bf16[2,2,192,128]{3,2,1,0:T(8,128)(2,1)S(1)}, u32[]{:S(2)}, u32[]{:S(2)}) collective-permute-start(bf16[2,2,192,128]{3,2,1,0:T(8,128)(2,1)S(1)} %maximum_select_fusion), channel_id=1, source_target_pairs={{0,1},{1,0},{2,14},{3,15},{4,5},{5,4},{6,10},{7,11},{8,9},{9,8},{1... | collective-permute-start | bytes 589832 | tf_op jit(solution)/shard_map/ppermute | solution.py:161
  43.5 1.8 %collective-permute-start.19 = (bf16[4,2,192,128]{3,2,1,0:T(8,128)(2,1)S(1)}, bf16[4,2,192,128]{3,2,1,0:T(8,128)(2,1)S(1)}, u32[]{:S(2)}, u32[]{:S(2)}) collective-permute-start(bf16[4,2,192,128]{3,2,1,0:T(8,128)(2,1)S(1)} %constant_dynamic-update-slice_fusion.refs_0_), channel_id=1, source_target_pairs={{0,2},{2,0},{1,3},{3,1},{4,6},{6,4},{5,7},{7,5},{8,10},{10,8},{9,1... | collective-permute-start | bytes 1179656 | tf_op jit(solution)/shard_map/ppermute | solution.py:151
  45.1 1.6 %collective-permute-start.17 = (bf16[3,2,192,128]{3,2,1,0:T(8,128)(2,1)S(1)}, bf16[3,2,192,128]{3,2,1,0:T(8,128)(2,1)S(1)}, u32[]{:S(2)}, u32[]{:S(2)}) collective-permute-start(bf16[3,2,192,128]{3,2,1,0:T(8,128)(2,1)S(1)} %pad_maximum_fusion.refs_0_), channel_id=1, source_target_pairs={{0,2},{2,0},{1,3},{3,1},{4,6},{6,4},{5,7},{7,5},{8,10},{10,8},{9,1... | collective-permute-start | bytes 884744 | tf_op jit(solution)/shard_map/ppermute | solution.py:151

commit v26 on v25

--- a/solution.py
+++ b/solution.py
@@ -244,12 +244,11 @@
         arrived, *rest = lax.optimization_barrier((arrived, away[0], away[2]))
         arrived = [swap(rest[0], "core"), arrived, swap(rest[1], "core")]
         pair, left, first = [own.astype(f32) + x.astype(f32) for own, x in zip(kept, arrived)]
-        corner = cube_swap(left[0].astype(bf16), lambda core: (1, 0)).astype(f32)
-        parts = [to_slot(x.astype(bf16), 4 + n) for n, x in enumerate(pair)]
-        parts += [to_slot(first[n].astype(bf16), n) for n in (2, 3)]
-        for n in range(2):
-            part = first[n] + jnp.where(core == 1 - n, corner, 0.0)
-            parts.append(to_slot(part.astype(bf16), n))
+        corner = cube_swap(left[0].astype(bf16), lambda core: (1 - core, core)).astype(f32)
+        sums = [first[0], first[2], first[3], pair[1]]
+        parts = [to_slot(x.astype(bf16), slot) for x, slot in zip(sums, (0, 2, 3, 5))]
+        for part, slot, of_core in ((pair[0], 4, 1), (first[1], 1, 0)):
+            parts.append(to_slot((part + jnp.where(core == of_core, corner, 0.0)).astype(bf16), slot))
         parts = [left[1], *lax.optimization_barrier(parts)]
         total = sum(x.astype(f32) for x in parts)
 

time: 48.6 us -> 50.2 us (1.033)
  starting transfers between devices: 24.7 us -> 28 us
  waiting for transfers between devices: 13.9 us -> 12.1 us
    ppermute x11, starting transfers between devices: 17.1 us -> 19.1 us  [cube_swap(): return lax.ppermute(x, AXES[1:], pairs)]
    ppermute x9, starting transfers between devices: 7.57 us -> 8.86 us  [swap(): lax.ppermute(x, axis, [(i, i ^ mask) for i in range(fine.shape[axis])])]
    ppermute x9, waiting for transfers between devices: 5.1 us -> 3.85 us  [swap(): lax.ppermute(x, axis, [(i, i ^ mask) for i in range(fine.shape[axis])])]
  transfers between devices with their start and end apart: 20 -> 20, of which waited for: 14 -> 8; matrix products, arithmetic and copies ran while one was open for 3% -> 3% of each run, Pallas kernels for 6% -> 6%
where the time goes in v26:
time: 50.2 us; the launch traced here: 49.7 us
  starting transfers between devices  28 us (56%)
  waiting for transfers between devices  12.1 us (24%)
  Pallas kernels  6.44 us (13%)
  between operations  1.58 us (3%)
  other arithmetic  1.39 us (3%)
    ppermute x11, starting transfers between devices, cube_swap(): return lax.ppermute(x, AXES[1:], pairs)  19.1 us
    ppermute x9, starting transfers between devices, swap(): lax.ppermute(x, axis, [(i, i ^ mask) for i in range(fine.shape[axis])])  8.86 us
    ppermute x11, waiting for transfers between devices, cube_swap(): return lax.ppermute(x, AXES[1:], pairs)  8.29 us
    ppermute x9, waiting for transfers between devices, swap(): lax.ppermute(x, axis, [(i, i ^ mask) for i in range(fine.shape[axis])])  3.85 us
    pallas_call x1, Pallas kernels, per_device(): pl.pallas_call(functools.partial(first_grad_kernel, n_high), out_shape=[p...  2.07 us
    pallas_call x1, Pallas kernels, per_device(): pl.pallas_call(functools.partial(columns_kernel, n_high, 4 * half), out_s...  1.91 us
    pallas_call x2, Pallas kernels, per_device(): pl.pallas_call(functools.partial(logits_kernel, n_high, group), out_shape...  1.89 us
  transfers between devices with their start and end apart: 20, of which 8 were waited for; matrix products, arithmetic and copies ran while one was open for 3% of the time, Pallas kernels for 6%

profile of v26, /device:TPU:0, one launch (start us, length us, event | category | flops | bytes accessed | tf_op | source)
XLA Modules:
  0.0 49.7 jit_solution(9717608167518114783)
XLA Ops:
  0.6 2.1 %shard_map.93 = (bf16[2,2,192,128]{3,2,1,0:T(8,128)(2,1)S(1)}, bf16[2,2,192,128]{3,2,1,0:T(8,128)(2,1)S(1)}, bf16[2,2,192,128]{3,2,1,0:T(8,128)(2,1)S(1)}, bf16[...) custom-call(bf16[256,6144]{1,0:T(8,128)(2,1)} %acts_ref.2, ...), custom_call_target="tpu_custom_call" | custom-call | tf_op jit(solution)/shard_map/pallas_call | solution.py:193
  3.2 0.6 %shard_map.94 = (bf16[4,2,192,128]{3,2,1,0:T(8,128)(2,1)S(1)}, bf16[4,2,192,128]{3,2,1,0:T(8,128)(2,1)S(1)}) custom-call(bf16[4,256,768]{2,1,0:T(8,128)(2,1)S(1)} %get-tuple-element.41.columns, bf16[128,256]{1,0:T(8,128)(2,1)S(1)} %get-tuple-element.42.turned_ref), custom_call_target="tpu_custom_call" | custom-call | flops 201326592 | bytes 1572864 | tf_op jit(solution)/shard_map/pallas_call | solution.py:209
  4.9 2.9 %collective-permute-start.7 = (bf16[2,192,128]{2,1,0:T(8,128)(2,1)S(1)}, bf16[2,192,128]{2,1,0:T(8,128)(2,1)S(1)}, u32[]{:S(2)}, u32[]{:S(2)}) collective-permute-start(bf16[2,192,128]{2,1,0:T(8,128)(2,1)S(1)} %fusion.18), channel_id=1, source_target_pairs={{0,4},{1,5},{2,3},{3,2},{4,0},{5,1},{6,7},{7,6},{8,12},{9,13},{10,... | collective-permute-start | bytes 294920 | tf_op jit(solution)/shard_map/ppermute | solution.py:161
  7.9 2.4 %collective-permute-start.6 = (bf16[2,192,128]{2,1,0:T(8,128)(2,1)S(1)}, bf16[2,192,128]{2,1,0:T(8,128)(2,1)S(1)}, u32[]{:S(2)}, u32[]{:S(2)}) collective-permute-start(bf16[2,192,128]{2,1,0:T(8,128)(2,1)S(1)} %fusion.17), channel_id=1, source_target_pairs={{0,12},{1,13},{2,3},{3,2},{4,8},{5,9},{6,7},{7,6},{8,4},{9,5},{10,... | collective-permute-start | bytes 294920 | tf_op jit(solution)/shard_map/ppermute | solution.py:161
  10.5 2.1 %collective-permute-start.8 = (bf16[2,192,128]{2,1,0:T(8,128)(2,1)S(1)}, bf16[2,192,128]{2,1,0:T(8,128)(2,1)S(1)}, u32[]{:S(2)}, u32[]{:S(2)}) collective-permute-start(bf16[2,192,128]{2,1,0:T(8,128)(2,1)S(1)} %get-tuple-element.83), channel_id=1, source_target_pairs={{0,1},{1,0},{2,14},{3,15},{4,5},{5,4},{6,10},{7,11},{8,9},{9,8},{1... | collective-permute-start | bytes 294920 | tf_op jit(solution)/shard_map/ppermute | solution.py:161
  12.6 1.5 %collective-permute-start.9 = (bf16[2,192,128]{2,1,0:T(8,128)(2,1)S(1)}, bf16[2,192,128]{2,1,0:T(8,128)(2,1)S(1)}, u32[]{:S(2)}, u32[]{:S(2)}) collective-permute-start(bf16[2,192,128]{2,1,0:T(8,128)(2,1)S(1)} %get-tuple-element.82), channel_id=1, source_target_pairs={{0,9},{1,8},{2,6},{3,7},{4,13},{5,12},{6,2},{7,3},{8,1},{9,0},{10,... | collective-permute-start | bytes 294920 | tf_op jit(solution)/shard_map/ppermute | solution.py:161
  14.1 1.6 %collective-permute-start.2 = (bf16[2,192,128]{2,1,0:T(8,128)(2,1)S(1)}, bf16[2,192,128]{2,1,0:T(8,128)(2,1)S(1)}, u32[]{:S(2)}, u32[]{:S(2)}) collective-permute-start(bf16[2,192,128]{2,1,0:T(8,128)(2,1)S(1)} %get-tuple-element.79), channel_id=1, source_target_pairs={{0,4},{1,5},{2,11},{3,10},{4,0},{5,1},{6,15},{7,14},{8,12},{9,13},... | collective-permute-start | bytes 294920 | tf_op jit(solution)/shard_map/ppermute | solution.py:161
  16.1 1.5 %collective-permute-start.4 = (bf16[2,192,128]{2,1,0:T(8,128)(2,1)S(1)}, bf16[2,192,128]{2,1,0:T(8,128)(2,1)S(1)}, u32[]{:S(2)}, u32[]{:S(2)}) collective-permute-start(bf16[2,192,128]{2,1,0:T(8,128)(2,1)S(1)} %get-tuple-element.77), channel_id=1, source_target_pairs={{0,5},{1,4},{2,10},{3,11},{4,1},{5,0},{6,14},{7,15},{8,13},{9,12},... | collective-permute-start | bytes 294920 | tf_op jit(solution)/shard_map/ppermute | solution.py:161
  17.7 1.8 %collective-permute-done.9 = bf16[2,192,128]{2,1,0:T(8,128)(2,1)S(1)} collective-permute-done((bf16[2,192,128]{2,1,0:T(8,128)(2,1)S(1)}, bf16[2,192,128]{2,1,0:T(8,128)(2,1)S(1)}, u32[]{:S(2)}, u32[]{:S(2)}) %collective-permute-start.9) | collective-permute-done | bytes 98336 | tf_op jit(solution)/shard_map/ppermute | solution.py:161
  19.5 0.8 %collective-permute-done.3 = bf16[2,192,128]{2,1,0:T(8,128)(2,1)S(1)} collective-permute-done((bf16[2,192,128]{2,1,0:T(8,128)(2,1)S(1)}, bf16[2,192,128]{2,1,0:T(8,128)(2,1)S(1)}, u32[]{:S(2)}, u32[]{:S(2)}) %collective-permute-start.3) | collective-permute-done | bytes 98336 | tf_op jit(solution)/shard_map/ppermute | solution.py:161
  20.3 1.4 %collective-permute-done.4 = bf16[2,192,128]{2,1,0:T(8,128)(2,1)S(1)} collective-permute-done((bf16[2,192,128]{2,1,0:T(8,128)(2,1)S(1)}, bf16[2,192,128]{2,1,0:T(8,128)(2,1)S(1)}, u32[]{:S(2)}, u32[]{:S(2)}) %collective-permute-start.4) | collective-permute-done | bytes 98336 | tf_op jit(solution)/shard_map/ppermute | solution.py:161
  21.8 2.7 %collective-permute-start.10 = (bf16[192,128]{1,0:T(8,128)(2,1)S(1)}, bf16[192,128]{1,0:T(8,128)(2,1)S(1)}, u32[]{:S(2)}, u32[]{:S(2)}) collective-permute-start(bf16[192,128]{1,0:T(8,128)(2,1)S(1)} %fusion.23), channel_id=1, source_target_pairs={{0,16},{16,0},{1,17},{17,1},{2,18},{18,2},{3,19},{19,3},{4,20},{20... | collective-permute-start | bytes 147464 | tf_op jit(solution)/shard_map/ppermute | solution.py:151
  25.2 1.7 %collective-permute-done.10 = bf16[192,128]{1,0:T(8,128)(2,1)S(1)} collective-permute-done((bf16[192,128]{1,0:T(8,128)(2,1)S(1)}, bf16[192,128]{1,0:T(8,128)(2,1)S(1)}, u32[]{:S(2)}, u32[]{:S(2)}) %collective-permute-start.10) | collective-permute-done | bytes 49184 | tf_op jit(solution)/shard_map/ppermute | solution.py:151
  26.9 2.7 %collective-permute-start.11 = (bf16[192,128]{1,0:T(8,128)(2,1)S(1)}, bf16[192,128]{1,0:T(8,128)(2,1)S(1)}, u32[]{:S(2)}, u32[]{:S(2)}) collective-permute-start(bf16[192,128]{1,0:T(8,128)(2,1)S(1)} %get-tuple-element.73), channel_id=1, source_target_pairs={{0,16},{16,0},{1,17},{17,1},{2,18},{18,2},{3,19},{19,3},{4,20},{20... | collective-permute-start | bytes 147464 | tf_op jit(solution)/shard_map/ppermute | solution.py:151
  29.6 1.8 %collective-permute-start.13 = (f32[192,128]{1,0:T(8,128)S(1)}, f32[192,128]{1,0:T(8,128)S(1)}, u32[]{:S(2)}, u32[]{:S(2)}) collective-permute-start(f32[192,128]{1,0:T(8,128)S(1)} %get-tuple-element.74), channel_id=1, source_target_pairs={{0,1},{1,0},{2,3},{3,2},{4,5},{5,4},{6,7},{7,6},{8,9},{9,8},{10,11... | collective-permute-start | bytes 294920 | tf_op jit(solution)/shard_map/ppermute | solution.py:151
  32.1 2.7 %collective-permute-start.15 = (bf16[2,192,128]{2,1,0:T(8,128)(2,1)S(1)}, bf16[2,192,128]{2,1,0:T(8,128)(2,1)S(1)}, u32[]{:S(2)}, u32[]{:S(2)}) collective-permute-start(bf16[2,192,128]{2,1,0:T(8,128)(2,1)S(1)} %get-tuple-element.81), channel_id=1, source_target_pairs={{0,13},{1,12},{2,15},{3,14},{4,9},{5,8},{6,11},{7,10},{8,5},{9,4},... | collective-permute-start | bytes 294920 | tf_op jit(solution)/shard_map/ppermute | solution.py:161
  34.8 2.5 %collective-permute-start.14 = (bf16[2,2,192,128]{3,2,1,0:T(8,128)(2,1)S(1)}, bf16[2,2,192,128]{3,2,1,0:T(8,128)(2,1)S(1)}, u32[]{:S(2)}, u32[]{:S(2)}) collective-permute-start(bf16[2,2,192,128]{3,2,1,0:T(8,128)(2,1)S(1)} %maximum_select_fusion), channel_id=1, source_target_pairs={{0,4},{1,5},{2,11},{3,10},{4,0},{5,1},{6,15},{7,14},{8,12},{9,13},... | collective-permute-start | bytes 589832 | tf_op jit(solution)/shard_map/ppermute | solution.py:161
  37.3 1.6 %collective-permute-start.16 = (bf16[2,2,192,128]{3,2,1,0:T(8,128)(2,1)S(1)}, bf16[2,2,192,128]{3,2,1,0:T(8,128)(2,1)S(1)}, u32[]{:S(2)}, u32[]{:S(2)}) collective-permute-start(bf16[2,2,192,128]{3,2,1,0:T(8,128)(2,1)S(1)} %maximum_select_fusion), channel_id=1, source_target_pairs={{0,1},{1,0},{2,14},{3,15},{4,5},{5,4},{6,10},{7,11},{8,9},{9,8},{1... | collective-permute-start | bytes 589832 | tf_op jit(solution)/shard_map/ppermute | solution.py:161
  38.8 0.9 %multiply_subtract_fusion = (f32[384,128]{1,0:T(8,128)}, f32[384,128]{1,0:T(8,128)}, f32[384,128]{1,0:T(8,128)}) fusion(f32[384,128]{1,0:T(8,128)S(1)} %copy-done, f32[]{:T(128)} %bitcast.14, f32[]{:T(128)} %bitcast.12, f32[192,128]{1,0:T(8,128)S(1)} %get-tuple-element.74, f32[192,128]{1,0:T(8,128)S(1)} %collective-permute-done.13, pred[]{:T(512)S(6)} %eq.12, ...), kind=kLoop, calls=%fused_computation.25 | loop fusion | flops 884736 | bytes 1376265 | tf_op jit(solution)/shard_map/sub | solution.py:36
  39.7 1.9 %shard_map.95 = (bf16[256,3072]{1,0:T(8,128)(2,1)S(1)}, bf16[256,3072]{1,0:T(8,128)(2,1)S(1)}) custom-call(bf16[256,6144]{1,0:T(8,128)(2,1)} %acts_ref.2), custom_call_target="tpu_custom_call" | custom-call | tf_op jit(solution)/shard_map/pallas_call | solution.py:278
  41.7 4.3 %collective-permute-done.14 = bf16[2,2,192,128]{3,2,1,0:T(8,128)(2,1)S(1)} collective-permute-done((bf16[2,2,192,128]{3,2,1,0:T(8,128)(2,1)S(1)}, bf16[2,2,192,128]{3,2,1,0:T(8,128)(2,1)S(1)}, u32[]{:S(2)}, u32[]{:S(2)}) %collective-permute-start.14) | collective-permute-done | bytes 196640 | tf_op jit(solution)/shard_map/ppermute | solution.py:161
  46.7 1.1 %collective-permute-done.19.refs_1_ = bf16[4,2,192,128]{3,2,1,0:T(8,128)(2,1)S(1)} collective-permute-done((bf16[4,2,192,128]{3,2,1,0:T(8,128)(2,1)S(1)}, bf16[4,2,192,128]{3,2,1,0:T(8,128)(2,1)S(1)}, u32[]{:S(2)}, u32[]{:S(2)}) %collective-permute-start.19) | collective-permute-done | bytes 393248 | tf_op jit(solution)/shard_map/ppermute | solution.py:151
  47.8 0.6 %shard_map.96.refs_4_ = f32[256,128]{1,0:T(8,128)S(1)} custom-call(bf16[256,3072]{1,0:T(8,128)(2,1)S(1)} %get-tuple-element.68.columns_ref, bf16[4,2,192,128]{3,2,1,0:T(8,128)(2,1)S(1)} %constant_dynamic-update-slice_fusion.refs_0_, bf16[4,2,192,128]{3,2,1,0:T(8,128)(2,1)S(1)} %collective-permute-done.19.refs_1_), custom_call_target="tpu_custom_call" | custom-call | tf_op jit(solution)/shard_map/pallas_call | solution.py:298
  48.4 1.3 %shard_map.97 = bf16[256,128]{1,0:T(8,128)(2,1)} custom-call(bf16[256,3072]{1,0:T(8,128)(2,1)S(1)} %get-tuple-element.66.columns_ref, bf16[3,2,192,128]{3,2,1,0:T(8,128)(2,1)S(1)} %pad_maximum_fusion.refs_0_, bf16[3,2,192,128]{3,2,1,0:T(8,128)(2,1)S(1)} %collective-permute-done.17.refs_1_, bf16[1,2,192,128]{3,2,1,0:T(8,128)(2,1)S(1)} %get-tuple-element.80.refs_2_, ...), custom_call_target="tpu_custom_call" | custom-call | tf_op jit(solution)/shard_map/pallas_call | solution.py:298
  (43 shorter events, 3.9 us)
Async XLA Ops:
  2.7 1.6 %collective-permute-start = (bf16[2,2,192,128]{3,2,1,0:T(8,128)(2,1)S(1)}, bf16[2,2,192,128]{3,2,1,0:T(8,128)(2,1)S(1)}, u32[]{:S(2)}, u32[]{:S(2)}) collective-permute-start(bf16[2,2,192,128]{3,2,1,0:T(8,128)(2,1)S(1)} %get-tuple-element.39), channel_id=1, source_target_pairs={{0,2},{2,0},{1,3},{3,1},{4,6},{6,4},{5,7},{7,5},{8,10},{10,8},{9,1... | collective-permute-start | bytes 589832 | tf_op jit(solution)/shard_map/ppermute | solution.py:151
  4.3 6.0 %collective-permute-start.1 = (bf16[4,2,192,128]{3,2,1,0:T(8,128)(2,1)S(1)}, bf16[4,2,192,128]{3,2,1,0:T(8,128)(2,1)S(1)}, u32[]{:S(2)}, u32[]{:S(2)}) collective-permute-start(bf16[4,2,192,128]{3,2,1,0:T(8,128)(2,1)S(1)} %get-tuple-element.46), channel_id=1, source_target_pairs={{0,2},{2,0},{1,3},{3,1},{4,6},{6,4},{5,7},{7,5},{8,10},{10,8},{9,1... | collective-permute-start | bytes 1179656 | tf_op jit(solution)/shard_map/ppermute | solution.py:151
  4.7 3.1 %collective-permute-start.5 = (bf16[2,2,192,128]{3,2,1,0:T(8,128)(2,1)S(1)}, bf16[2,2,192,128]{3,2,1,0:T(8,128)(2,1)S(1)}, u32[]{:S(2)}, u32[]{:S(2)}) collective-permute-start(bf16[2,2,192,128]{3,2,1,0:T(8,128)(2,1)S(1)} %get-tuple-element.48), channel_id=1, source_target_pairs={{0,2},{2,0},{1,3},{3,1},{4,6},{6,4},{5,7},{7,5},{8,10},{10,8},{9,1... | collective-permute-start | bytes 589832 | tf_op jit(solution)/shard_map/ppermute | solution.py:151
  4.9 5.6 %collective-permute-start.7 = (bf16[2,192,128]{2,1,0:T(8,128)(2,1)S(1)}, bf16[2,192,128]{2,1,0:T(8,128)(2,1)S(1)}, u32[]{:S(2)}, u32[]{:S(2)}) collective-permute-start(bf16[2,192,128]{2,1,0:T(8,128)(2,1)S(1)} %fusion.18), channel_id=1, source_target_pairs={{0,4},{1,5},{2,3},{3,2},{4,0},{5,1},{6,7},{7,6},{8,12},{9,13},{10,... | collective-permute-start | bytes 294920 | tf_op jit(solution)/shard_map/ppermute | solution.py:161
  7.9 8.3 %collective-permute-start.6 = (bf16[2,192,128]{2,1,0:T(8,128)(2,1)S(1)}, bf16[2,192,128]{2,1,0:T(8,128)(2,1)S(1)}, u32[]{:S(2)}, u32[]{:S(2)}) collective-permute-start(bf16[2,192,128]{2,1,0:T(8,128)(2,1)S(1)} %fusion.17), channel_id=1, source_target_pairs={{0,12},{1,13},{2,3},{3,2},{4,8},{5,9},{6,7},{7,6},{8,4},{9,5},{10,... | collective-permute-start | bytes 294920 | tf_op jit(solution)/shard_map/ppermute | solution.py:161
  10.5 28.3 %copy-start = (f32[384,128]{1,0:T(8,128)S(1)}, f32[384,128]{1,0:T(8,128)}, u32[]{:S(2)}) copy-start(f32[384,128]{1,0:T(8,128)} %refs_0_.1) | copy-start | bytes 589828
  10.5 28.3 %copy-start.1 = (f32[384,128]{1,0:T(8,128)S(1)}, f32[384,128]{1,0:T(8,128)}, u32[]{:S(2)}) copy-start(f32[384,128]{1,0:T(8,128)} %refs_1_.1) | copy-start | bytes 589828
  10.5 28.3 %copy-start.2 = (f32[384,128]{1,0:T(8,128)S(1)}, f32[384,128]{1,0:T(8,128)}, u32[]{:S(2)}) copy-start(f32[384,128]{1,0:T(8,128)} %refs_2_.1) | copy-start | bytes 589828
  10.5 7.1 %collective-permute-start.8 = (bf16[2,192,128]{2,1,0:T(8,128)(2,1)S(1)}, bf16[2,192,128]{2,1,0:T(8,128)(2,1)S(1)}, u32[]{:S(2)}, u32[]{:S(2)}) collective-permute-start(bf16[2,192,128]{2,1,0:T(8,128)(2,1)S(1)} %get-tuple-element.83), channel_id=1, source_target_pairs={{0,1},{1,0},{2,14},{3,15},{4,5},{5,4},{6,10},{7,11},{8,9},{9,8},{1... | collective-permute-start | bytes 294920 | tf_op jit(solution)/shard_map/ppermute | solution.py:161
  12.6 6.9 %collective-permute-start.9 = (bf16[2,192,128]{2,1,0:T(8,128)(2,1)S(1)}, bf16[2,192,128]{2,1,0:T(8,128)(2,1)S(1)}, u32[]{:S(2)}, u32[]{:S(2)}) collective-permute-start(bf16[2,192,128]{2,1,0:T(8,128)(2,1)S(1)} %get-tuple-element.82), channel_id=1, source_target_pairs={{0,9},{1,8},{2,6},{3,7},{4,13},{5,12},{6,2},{7,3},{8,1},{9,0},{10,... | collective-permute-start | bytes 294920 | tf_op jit(solution)/shard_map/ppermute | solution.py:161
  14.1 5.4 %collective-permute-start.2 = (bf16[2,192,128]{2,1,0:T(8,128)(2,1)S(1)}, bf16[2,192,128]{2,1,0:T(8,128)(2,1)S(1)}, u32[]{:S(2)}, u32[]{:S(2)}) collective-permute-start(bf16[2,192,128]{2,1,0:T(8,128)(2,1)S(1)} %get-tuple-element.79), channel_id=1, source_target_pairs={{0,4},{1,5},{2,11},{3,10},{4,0},{5,1},{6,15},{7,14},{8,12},{9,13},... | collective-permute-start | bytes 294920 | tf_op jit(solution)/shard_map/ppermute | solution.py:161
  15.7 4.6 %collective-permute-start.3 = (bf16[2,192,128]{2,1,0:T(8,128)(2,1)S(1)}, bf16[2,192,128]{2,1,0:T(8,128)(2,1)S(1)}, u32[]{:S(2)}, u32[]{:S(2)}) collective-permute-start(bf16[2,192,128]{2,1,0:T(8,128)(2,1)S(1)} %get-tuple-element.78), channel_id=1, source_target_pairs={{0,8},{1,9},{2,7},{3,6},{4,12},{5,13},{6,3},{7,2},{8,0},{9,1},{10,... | collective-permute-start | bytes 294920 | tf_op jit(solution)/shard_map/ppermute | solution.py:161
  16.1 5.5 %collective-permute-start.4 = (bf16[2,192,128]{2,1,0:T(8,128)(2,1)S(1)}, bf16[2,192,128]{2,1,0:T(8,128)(2,1)S(1)}, u32[]{:S(2)}, u32[]{:S(2)}) collective-permute-start(bf16[2,192,128]{2,1,0:T(8,128)(2,1)S(1)} %get-tuple-element.77), channel_id=1, source_target_pairs={{0,5},{1,4},{2,10},{3,11},{4,1},{5,0},{6,14},{7,15},{8,13},{9,12},... | collective-permute-start | bytes 294920 | tf_op jit(solution)/shard_map/ppermute | solution.py:161
  21.8 5.1 %collective-permute-start.10 = (bf16[192,128]{1,0:T(8,128)(2,1)S(1)}, bf16[192,128]{1,0:T(8,128)(2,1)S(1)}, u32[]{:S(2)}, u32[]{:S(2)}) collective-permute-start(bf16[192,128]{1,0:T(8,128)(2,1)S(1)} %fusion.23), channel_id=1, source_target_pairs={{0,16},{16,0},{1,17},{17,1},{2,18},{18,2},{3,19},{19,3},{4,20},{20... | collective-permute-start | bytes 147464 | tf_op jit(solution)/shard_map/ppermute | solution.py:151
  26.9 5.1 %collective-permute-start.11 = (bf16[192,128]{1,0:T(8,128)(2,1)S(1)}, bf16[192,128]{1,0:T(8,128)(2,1)S(1)}, u32[]{:S(2)}, u32[]{:S(2)}) collective-permute-start(bf16[192,128]{1,0:T(8,128)(2,1)S(1)} %get-tuple-element.73), channel_id=1, source_target_pairs={{0,16},{16,0},{1,17},{17,1},{2,18},{18,2},{3,19},{19,3},{4,20},{20... | collective-permute-start | bytes 147464 | tf_op jit(solution)/shard_map/ppermute | solution.py:151
  29.6 5.1 %collective-permute-start.13 = (f32[192,128]{1,0:T(8,128)S(1)}, f32[192,128]{1,0:T(8,128)S(1)}, u32[]{:S(2)}, u32[]{:S(2)}) collective-permute-start(f32[192,128]{1,0:T(8,128)S(1)} %get-tuple-element.74), channel_id=1, source_target_pairs={{0,1},{1,0},{2,3},{3,2},{4,5},{5,4},{6,7},{7,6},{8,9},{9,8},{10,11... | collective-permute-start | bytes 294920 | tf_op jit(solution)/shard_map/ppermute | solution.py:151
  32.0 2.8 %collective-permute-start.12 = (bf16[2,192,128]{2,1,0:T(8,128)(2,1)S(1)}, bf16[2,192,128]{2,1,0:T(8,128)(2,1)S(1)}, u32[]{:S(2)}, u32[]{:S(2)}) collective-permute-start(bf16[2,192,128]{2,1,0:T(8,128)(2,1)S(1)} %get-tuple-element.81), channel_id=1, source_target_pairs={{0,2},{2,0},{1,3},{3,1},{4,6},{6,4},{5,7},{7,5},{8,10},{10,8},{9,1... | collective-permute-start | bytes 294920 | tf_op jit(solution)/shard_map/ppermute | solution.py:151
  32.1 9.6 %collective-permute-start.15 = (bf16[2,192,128]{2,1,0:T(8,128)(2,1)S(1)}, bf16[2,192,128]{2,1,0:T(8,128)(2,1)S(1)}, u32[]{:S(2)}, u32[]{:S(2)}) collective-permute-start(bf16[2,192,128]{2,1,0:T(8,128)(2,1)S(1)} %get-tuple-element.81), channel_id=1, source_target_pairs={{0,13},{1,12},{2,15},{3,14},{4,9},{5,8},{6,11},{7,10},{8,5},{9,4},... | collective-permute-start | bytes 294920 | tf_op jit(solution)/shard_map/ppermute | solution.py:161
  34.8 11.1 %collective-permute-start.14 = (bf16[2,2,192,128]{3,2,1,0:T(8,128)(2,1)S(1)}, bf16[2,2,192,128]{3,2,1,0:T(8,128)(2,1)S(1)}, u32[]{:S(2)}, u32[]{:S(2)}) collective-permute-start(bf16[2,2,192,128]{3,2,1,0:T(8,128)(2,1)S(1)} %maximum_select_fusion), channel_id=1, source_target_pairs={{0,4},{1,5},{2,11},{3,10},{4,0},{5,1},{6,15},{7,14},{8,12},{9,13},... | collective-permute-start | bytes 589832 | tf_op jit(solution)/shard_map/ppermute | solution.py:161
  37.3 8.7 %collective-permute-start.18 = (bf16[2,2,192,128]{3,2,1,0:T(8,128)(2,1)S(1)}, bf16[2,2,192,128]{3,2,1,0:T(8,128)(2,1)S(1)}, u32[]{:S(2)}, u32[]{:S(2)}) collective-permute-start(bf16[2,2,192,128]{3,2,1,0:T(8,128)(2,1)S(1)} %maximum_select_fusion), channel_id=1, source_target_pairs={{0,8},{1,9},{2,7},{3,6},{4,12},{5,13},{6,3},{7,2},{8,0},{9,1},{10,... | collective-permute-start | bytes 589832 | tf_op jit(solution)/shard_map/ppermute | solution.py:161
  37.3 8.8 %collective-permute-start.16 = (bf16[2,2,192,128]{3,2,1,0:T(8,128)(2,1)S(1)}, bf16[2,2,192,128]{3,2,1,0:T(8,128)(2,1)S(1)}, u32[]{:S(2)}, u32[]{:S(2)}) collective-permute-start(bf16[2,2,192,128]{3,2,1,0:T(8,128)(2,1)S(1)} %maximum_select_fusion), channel_id=1, source_target_pairs={{0,1},{1,0},{2,14},{3,15},{4,5},{5,4},{6,10},{7,11},{8,9},{9,8},{1... | collective-permute-start | bytes 589832 | tf_op jit(solution)/shard_map/ppermute | solution.py:161
  46.0 1.8 %collective-permute-start.19 = (bf16[4,2,192,128]{3,2,1,0:T(8,128)(2,1)S(1)}, bf16[4,2,192,128]{3,2,1,0:T(8,128)(2,1)S(1)}, u32[]{:S(2)}, u32[]{:S(2)}) collective-permute-start(bf16[4,2,192,128]{3,2,1,0:T(8,128)(2,1)S(1)} %constant_dynamic-update-slice_fusion.refs_0_), channel_id=1, source_target_pairs={{0,2},{2,0},{1,3},{3,1},{4,6},{6,4},{5,7},{7,5},{8,10},{10,8},{9,1... | collective-permute-start | bytes 1179656 | tf_op jit(solution)/shard_map/ppermute | solution.py:151
  46.1 2.3 %collective-permute-start.17 = (bf16[3,2,192,128]{3,2,1,0:T(8,128)(2,1)S(1)}, bf16[3,2,192,128]{3,2,1,0:T(8,128)(2,1)S(1)}, u32[]{:S(2)}, u32[]{:S(2)}) collective-permute-start(bf16[3,2,192,128]{3,2,1,0:T(8,128)(2,1)S(1)} %pad_maximum_fusion.refs_0_), channel_id=1, source_target_pairs={{0,2},{2,0},{1,3},{3,1},{4,6},{6,4},{5,7},{7,5},{8,10},{10,8},{9,1... | collective-permute-start | bytes 884744 | tf_op jit(solution)/shard_map/ppermute | solution.py:151
